TPU v7x, 32 devices: a whole 2x2x4 slice. The times are simulated.
32 devices in a mesh: dp: 4 (over y, core), tok: 8 (over z, x).
Axes of the slice: x: 2, y: 2, z: 4, core: 2. Of those that a mesh axis runs over, the one named last changes fastest.
Arguments:
- query_in: bfloat16 [4, 2048, 640], P('dp', 'tok'), may hold values from -6 to 6
- key_in: bfloat16 [4, 2048, 640], P('dp', 'tok'), may hold values from -6 to 6
- value_in: bfloat16 [4, 2048, 640], P('dp', 'tok'), may hold values from -6 to 6
- out_grad: bfloat16 [4, 2048, 640], P('dp', 'tok'), may hold values from -6 to 6
- bias: bfloat16 [3, 640], replicated, may hold values from -3 to 3
- lengths: int32 [4, 4], P('dp'), may hold values from 0 to 4, as said below
- widths: int32 [4, 4], P('dp'), may hold values from 64 to 256, as said below
Outputs:
- attn_out: bfloat16 [4, 2048, 640], P('dp', 'tok')
- query_grad: bfloat16 [4, 2048, 640], P('dp', 'tok')
- key_grad: bfloat16 [4, 2048, 640], P('dp', 'tok')
- value_grad: bfloat16 [4, 2048, 640], P('dp', 'tok')
- bias_grad: float32 [3, 640], replicated
Inputs may be any that keep to these rules, and one draw needn't show every extreme that they name: Each replica's lengths sum to 8; the nonzero ones come first and zeros follow; the first is 4; every nonzero length but the last nonzero one is at least 3. `widths`: each width is 256 divided by 1, 2 or 4; the first image of every replica has width 256.
All inputs are finite; a program needn't handle non-finite values.
Results may differ from a plain program's by a relative error of at most 0.025.
Values may be sent and summed in bfloat16 or wider, within the bound.
No kernel may reach another device: no remote copies, remote signals or barrier semaphores. Data moves between devices by JAX's collectives and lax.ppermute only.
A program may use at most 64 MiB of HBM per device.

v0:
```python
import jax
import jax.numpy as jnp
from jax import lax
from jax.sharding import PartitionSpec as P

HEADS = 8
HEAD_DIM = 80
SPAN = 4


rope_base = 10000.0


def from_behind(value, axis, steps):
    count = lax.axis_size(axis)
    initial, last = (max(0, -steps), min(count, count - steps))
    return lax.ppermute(value, axis, [(source, source + steps) for source in range(initial, last)])


def image_ids(spots, ends):
    return jnp.sum((spots[:, None] >= ends[None, :]).astype(jnp.int32), axis=1)


def rotary(spots, lengths_row, widths_row, tokd):
    ends = jnp.cumsum(lengths_row) * tokd
    ids = image_ids(spots, ends)
    starts = ends - lengths_row * tokd
    onehot = ids[:, None] == jnp.arange(lengths_row.shape[0], dtype=jnp.int32)[None, :]
    start = jnp.sum(jnp.where(onehot, starts[None, :], 0), axis=1)
    width = jnp.sum(jnp.where(onehot, widths_row[None, :], 1), axis=1)
    width = jnp.maximum(width - (lengths_row.shape[0] - 1), 1)
    local = spots - start
    rowpos = local // width
    colpos = local % width
    quarter = HEAD_DIM // 4
    inverse = rope_base ** (-jnp.arange(quarter, dtype=jnp.float32) / quarter)
    angles = jnp.concatenate(
        [
            rowpos.astype(jnp.float32)[:, None] * inverse,
            colpos.astype(jnp.float32)[:, None] * inverse,
        ],
        axis=1,
    )
    angles = jnp.concatenate([angles, angles], axis=1)
    return (jnp.cos(angles), jnp.sin(angles))


def rotate(values, cosv, sinv):
    half = values.shape[-1] // 2
    turned = jnp.concatenate([-values[..., half:], values[..., :half]], axis=-1)
    return values * cosv + turned * sinv


def unrotate(values, cosv, sinv):
    half = values.shape[-1] // 2
    scaled = values * sinv
    return values * cosv + jnp.concatenate([scaled[..., half:], -scaled[..., :half]], axis=-1)


def block_of(array, number, tokd):
    return array[:, number * tokd : (number + 1) * tokd]


def on_device(query_in, key_in, value_in, out_grad, bias, lengths, widths):
    tokd = query_in.shape[1]
    model = query_in.shape[2]
    index = lax.axis_index("tok")
    count = lax.axis_size("tok")
    lengths_row = lengths[0]
    widths_row = widths[0]
    spots = index * tokd + jnp.arange(tokd, dtype=jnp.int32)
    cosv, sinv = rotary(spots, lengths_row, widths_row, tokd)
    cosv = cosv[:, None, :]
    sinv = sinv[:, None, :]
    bias_f = bias.astype(jnp.float32).reshape(3, HEADS, HEAD_DIM)
    query_rot = rotate(
        query_in[0].astype(jnp.float32).reshape(tokd, HEADS, HEAD_DIM) + bias_f[0], cosv, sinv
    ).astype(jnp.bfloat16)
    key_rot = rotate(
        key_in[0].astype(jnp.float32).reshape(tokd, HEADS, HEAD_DIM) + bias_f[1], cosv, sinv
    ).astype(jnp.bfloat16)
    value_b = (value_in[0].astype(jnp.float32).reshape(tokd, HEADS, HEAD_DIM) + bias_f[2]).astype(
        jnp.bfloat16
    )
    pair = jnp.stack([key_rot.reshape(tokd, model), value_b.reshape(tokd, model)])
    left_parts = []
    moving = pair
    for stride in range(SPAN - 1):
        moving = from_behind(moving, "tok", 1)
        left_parts.insert(0, moving)
    right_parts = []
    moving = pair
    for stride in range(SPAN - 1):
        moving = from_behind(moving, "tok", -1)
        right_parts.append(moving)
    window = jnp.concatenate(left_parts + [pair] + right_parts, axis=1)
    span_rows = window.shape[1]
    nblocks = 2 * SPAN - 1
    win_spots = (index - (SPAN - 1)) * tokd + jnp.arange(span_rows, dtype=jnp.int32)
    valid = (win_spots >= 0) & (win_spots < count * tokd)
    ends = jnp.cumsum(lengths_row) * tokd
    win_ids = jnp.where(valid, image_ids(win_spots, ends), -1)
    own_ids = image_ids(spots, ends)
    mask = own_ids[:, None] == win_ids[None, :]
    active = [jnp.any(mask[:, number * tokd : (number + 1) * tokd]) for number in range(nblocks)]
    scale = HEAD_DIM ** (-0.5)
    query_heads = query_rot.transpose(1, 0, 2)
    key_heads = window[0].reshape(span_rows, HEADS, HEAD_DIM).transpose(1, 0, 2)
    value_heads = window[1].reshape(span_rows, HEADS, HEAD_DIM).transpose(1, 0, 2)
    grad_heads = out_grad[0].reshape(tokd, HEADS, HEAD_DIM).transpose(1, 0, 2)
    hdim = query_heads.shape[2]

    def one_head(items):
        query_h, key_h, value_h, grad_h = items
        key_parts = [key_h[number * tokd : (number + 1) * tokd] for number in range(nblocks)]
        value_parts = [value_h[number * tokd : (number + 1) * tokd] for number in range(nblocks)]
        score_parts = []
        for number in range(nblocks):
            score_parts.append(
                lax.cond(
                    active[number],
                    lambda keys=key_parts[number]: jnp.einsum(
                        "qd,kd->qk", query_h, keys, preferred_element_type=jnp.float32
                    )
                    * scale,
                    lambda: jnp.full((tokd, tokd), -1e30, jnp.float32),
                )
            )
        scores = jnp.concatenate(score_parts, axis=1)
        scores = jnp.where(mask, scores, -1e30)
        top = jnp.max(scores, axis=-1, keepdims=True)
        expo = jnp.exp(scores - top)
        probs = expo / jnp.sum(expo, axis=-1, keepdims=True)
        probs_b = probs.astype(jnp.bfloat16)
        out_acc = jnp.zeros((tokd, hdim), jnp.float32)
        for number in range(nblocks):
            out_acc = out_acc + lax.cond(
                active[number],
                lambda weights=probs_b[:, number * tokd : (number + 1) * tokd], vals=value_parts[
                    number
                ]: jnp.einsum("qk,kd->qd", weights, vals, preferred_element_type=jnp.float32),
                lambda: jnp.zeros((tokd, hdim), jnp.float32),
            )
        out_b = out_acc.astype(jnp.bfloat16)
        delta = jnp.sum(grad_h.astype(jnp.float32) * out_b.astype(jnp.float32), axis=-1)
        dquery = jnp.zeros((tokd, hdim), jnp.float32)
        dkey_parts = []
        dvalue_parts = []
        for number in range(nblocks):
            block_probs = probs[:, number * tokd : (number + 1) * tokd]
            block_probs_b = probs_b[:, number * tokd : (number + 1) * tokd]

            def compute(
                block_probs=block_probs,
                block_probs_b=block_probs_b,
                keys=key_parts[number],
                vals=value_parts[number],
            ):
                dprobs = jnp.einsum("qd,kd->qk", grad_h, vals, preferred_element_type=jnp.float32)
                dscore_b = (block_probs * (dprobs - delta[:, None]) * scale).astype(jnp.bfloat16)
                part_q = jnp.einsum("qk,kd->qd", dscore_b, keys, preferred_element_type=jnp.float32)
                part_k = jnp.einsum(
                    "qk,qd->kd", dscore_b, query_h, preferred_element_type=jnp.float32
                )
                part_v = jnp.einsum(
                    "qk,qd->kd", block_probs_b, grad_h, preferred_element_type=jnp.float32
                )
                return (part_q, part_k, part_v)

            def skipped():
                zeros = jnp.zeros((tokd, hdim), jnp.float32)
                return (zeros, zeros, zeros)

            part_q, part_k, part_v = lax.cond(active[number], compute, skipped)
            dquery = dquery + part_q
            dkey_parts.append(part_k)
            dvalue_parts.append(part_v)
        return (
            out_b,
            dquery,
            jnp.concatenate(dkey_parts, axis=0),
            jnp.concatenate(dvalue_parts, axis=0),
        )

    outs, dquery, dkey, dvalue = lax.map(
        one_head, (query_heads, key_heads, value_heads, grad_heads)
    )
    attn_rows = outs.transpose(1, 0, 2).reshape(tokd, model)
    dquery_f = unrotate(dquery.transpose(1, 0, 2), cosv, sinv).reshape(tokd, model)
    terms = jnp.stack(
        [
            dkey.transpose(1, 0, 2).reshape(span_rows, model),
            dvalue.transpose(1, 0, 2).reshape(span_rows, model),
        ]
    )
    left_terms = terms[:, : SPAN * tokd]
    right_terms = terms[:, SPAN * tokd :]
    left_acc = block_of(left_terms, 0, tokd)
    for number in range(1, SPAN):
        left_acc = from_behind(left_acc, "tok", -1) + block_of(left_terms, number, tokd)
    right_acc = block_of(right_terms, SPAN - 2, tokd)
    for number in range(SPAN - 2, -1, -1):
        moved = from_behind(right_acc, "tok", 1)
        right_acc = moved + block_of(right_terms, number - 1, tokd) if number > 0 else moved
    owned = left_acc + right_acc
    dkey_f = unrotate(owned[0].reshape(tokd, HEADS, HEAD_DIM), cosv, sinv).reshape(tokd, model)
    dvalue_f = owned[1]
    local_sums = jnp.stack(
        [jnp.sum(dquery_f, axis=0), jnp.sum(dkey_f, axis=0), jnp.sum(dvalue_f, axis=0)]
    )
    summed = lax.psum(local_sums, ("dp", "tok"))
    tokens_all = lax.axis_size("dp") * count * tokd
    bias_grad = summed * (1.0 / tokens_all**0.5)
    return (
        attn_rows[None],
        dquery_f.astype(jnp.bfloat16)[None],
        dkey_f.astype(jnp.bfloat16)[None],
        dvalue_f.astype(jnp.bfloat16)[None],
        bias_grad,
    )


def solution(mesh):
    in_specs = (
        P("dp", "tok", None),
        P("dp", "tok", None),
        P("dp", "tok", None),
        P("dp", "tok", None),
        P(),
        P("dp", None),
        P("dp", None),
    )
    out_specs = (
        P("dp", "tok", None),
        P("dp", "tok", None),
        P("dp", "tok", None),
        P("dp", "tok", None),
        P(),
    )
    return jax.shard_map(
        on_device, mesh=mesh, in_specs=in_specs, out_specs=out_specs, check_vma=False
    )
```

profile of v0, /device:TPU:0, one launch (start us, length us, event | category | flops | bytes accessed | tf_op | source)
XLA Modules:
  0.0 645.0 jit_solution(8118299379559791348)
XLA Ops:
  8.9 4.9 collective-permute-start
  15.1 26.7 %collective-permute-done = bf16[2,256,640]{1,2,0:T(8,128)(2,1)S(1)} collective-permute-done((bf16[2,256,640]{1,2,0:T(8,128)(2,1)S(1)}, bf16[2,256,640]{1,2,0:T(8,128)(2,1)S(1)}, u32[]{:S(2)}, u32[]{:S(2)}) %collective-permute-start) | collective-permute-done | bytes 655392 | tf_op jit(solution)/shard_map/ppermute | solution.py:17
  41.7 5.2 collective-permute-start.1
  48.4 24.9 %collective-permute-done.1 = bf16[2,256,640]{1,2,0:T(8,128)(2,1)} collective-permute-done((bf16[2,256,640]{1,2,0:T(8,128)(2,1)S(1)}, bf16[2,256,640]{1,2,0:T(8,128)(2,1)}, u32[]{:S(2)}, u32[]{:S(2)}) %collective-permute-start.1) | collective-permute-done | bytes 655392 | tf_op jit(solution)/shard_map/ppermute | solution.py:17
  73.3 5.3 collective-permute-start.2
  82.0 22.3 %collective-permute-done.2 = bf16[2,256,640]{1,2,0:T(8,128)(2,1)} collective-permute-done((bf16[2,256,640]{1,2,0:T(8,128)(2,1)}, bf16[2,256,640]{1,2,0:T(8,128)(2,1)}, u32[]{:S(2)}, u32[]{:S(2)}) %collective-permute-start.2) | collective-permute-done | bytes 655392 | tf_op jit(solution)/shard_map/ppermute | solution.py:17
  107.9 2.5 fusion.56
  110.4 289.0 %while.17 = (s32[]{:T(128)}, bf16[8,256,80]{1,2,0:T(8,128)(2,1)}, f32[8,256,80]{1,2,0:T(8,128)}, f32[8,1792,80]{1,2,0:T(8,128)}, f32[8,1792,80]{1,2,0:T(8,128)},...) while((s32[]{:T(128)}, bf16[8,256,80]{1,2,0:T(8,128)(2,1)}, ...), condition=%wide.region_58.59_spmd.clone, body=%wide.region_12.58_spmd.clone.sunk | while | flops 448548096 | bytes 45132880 | solution.py:185
  128.7 1.8 multiply_reduce_fusion.2
  132.6 1.6 conditional.80
  137.9 1.5 conditional.77
  164.8 1.8 multiply_reduce_fusion.2
  168.8 1.6 conditional.80
  174.0 1.5 conditional.77
  200.9 1.8 multiply_reduce_fusion.2
  204.9 1.6 conditional.80
  210.1 1.5 conditional.77
  237.0 1.8 multiply_reduce_fusion.2
  241.0 1.6 conditional.80
  246.2 1.5 conditional.77
  273.2 1.8 multiply_reduce_fusion.2
  277.1 1.6 conditional.80
  282.4 1.5 conditional.77
  309.3 1.8 multiply_reduce_fusion.2
  313.2 1.6 conditional.80
  318.5 1.5 conditional.77
  345.4 1.8 multiply_reduce_fusion.2
  349.4 1.6 conditional.80
  354.6 1.5 conditional.77
  381.5 1.8 multiply_reduce_fusion.2
  385.5 1.6 conditional.80
  390.7 1.5 conditional.77
  399.4 1.5 fusion.28
  400.9 1.6 collective-permute-start.6
  402.5 37.2 %collective-permute-done.6 = f32[2,256,640]{1,2,0:T(8,128)S(1)} collective-permute-done((f32[2,256,640]{1,2,0:T(8,128)S(1)}, f32[2,256,640]{1,2,0:T(8,128)S(1)}, u32[]{:S(2)}, u32[]{:S(2)}) %collective-permute-start.6) | collective-permute-done | bytes 1310752 | tf_op jit(solution)/shard_map/ppermute | solution.py:17
  440.0 1.5 collective-permute-start.7
  441.5 33.1 %collective-permute-done.7 = f32[2,256,640]{1,2,0:T(8,128)S(1)} collective-permute-done((f32[2,256,640]{1,2,0:T(8,128)S(1)}, f32[2,256,640]{1,2,0:T(8,128)S(1)}, u32[]{:S(2)}, u32[]{:S(2)}) %collective-permute-start.7) | collective-permute-done | bytes 1310752 | tf_op jit(solution)/shard_map/ppermute | solution.py:17
  474.9 11.2 %collective-permute-start.9 = (f32[2,256,640]{1,2,0:T(8,128)S(1)}, f32[2,256,640]{1,2,0:T(8,128)S(1)}, u32[]{:S(2)}, u32[]{:S(2)}) collective-permute-start(f32[2,256,640]{1,2,0:T(8,128)S(1)} %get-tuple-element.658), channel_id=1, source_target_pairs={{0,1},{1,2},{2,3},{3,4},{4,5},{5,6},{6,7},{8,9},{9,10},{10,11},{11... | collective-permute-start | bytes 3932168 | tf_op jit(solution)/shard_map/ppermute | solution.py:17
  486.1 24.3 %collective-permute-done.9 = f32[2,256,640]{1,2,0:T(8,128)S(1)} collective-permute-done((f32[2,256,640]{1,2,0:T(8,128)S(1)}, f32[2,256,640]{1,2,0:T(8,128)S(1)}, u32[]{:S(2)}, u32[]{:S(2)}) %collective-permute-start.9) | collective-permute-done | bytes 1310752 | tf_op jit(solution)/shard_map/ppermute | solution.py:17
  510.6 4.5 collective-permute-start.10
  515.1 1.4 collective-permute-start.8
  516.5 49.7 %collective-permute-done.10 = f32[2,256,640]{1,2,0:T(8,128)S(1)} collective-permute-done((f32[2,256,640]{1,2,0:T(8,128)S(1)}, f32[2,256,640]{1,2,0:T(8,128)S(1)}, u32[]{:S(2)}, u32[]{:S(2)}) %collective-permute-start.10) | collective-permute-done | bytes 1310752 | tf_op jit(solution)/shard_map/ppermute | solution.py:17
  567.5 5.6 collective-permute-start.11
  573.1 1.9 copy.86
  576.0 1.9 copy.87
  577.8 17.7 %collective-permute-done.11 = f32[2,256,640]{1,2,0:T(8,128)} collective-permute-done((f32[2,256,640]{1,2,0:T(8,128)}, f32[2,256,640]{1,2,0:T(8,128)}, u32[]{:S(2)}, u32[]{:S(2)}) %collective-permute-start.11) | collective-permute-done | bytes 1310752 | tf_op jit(solution)/shard_map/ppermute | solution.py:17
  595.5 1.9 fusion.35
  598.9 44.6 %psum.7 = f32[3,640]{1,0:T(4,128)S(1)} all-reduce(f32[3,640]{1,0:T(4,128)S(1)} %pad_maximum_fusion.4), channel_id=1, replica_groups=mesh['dp'=4,'tok'=8] {'dp','tok'}, use_global_device_ids=true, to_apply=%region_62.63 | all-reduce | flops 1920 | bytes 15360 | tf_op jit(solution)/shard_map/psum | solution.py:211
  (1385 shorter events, 325.1 us)
Async XLA Ops:
  8.2 70.4 %copy-start.35 = (bf16[1,256,640]{2,1,0:T(8,128)(2,1)S(1)}, bf16[1,256,640]{2,1,0:T(8,128)(2,1)}, u32[]{:S(2)}) copy-start(bf16[1,256,640]{2,1,0:T(8,128)(2,1)} %param.54) | copy-start | bytes 983044
  8.9 32.9 %collective-permute-start = (bf16[2,256,640]{1,2,0:T(8,128)(2,1)S(1)}, bf16[2,256,640]{1,2,0:T(8,128)(2,1)S(1)}, u32[]{:S(2)}, u32[]{:S(2)}) collective-permute-start(bf16[2,256,640]{1,2,0:T(8,128)(2,1)S(1)} %pad_maximum_fusion.1), channel_id=1, source_target_pairs={{0,1},{1,2},{2,3},{3,4},{4,5},{5,6},{6,7},{8,9},{9,10},{10,11},{11... | collective-permute-start | bytes 1966088 | tf_op jit(solution)/shard_map/ppermute | solution.py:17
  13.8 33.3 %collective-permute-start.3 = (bf16[2,256,640]{1,2,0:T(8,128)(2,1)S(1)}, bf16[2,256,640]{1,2,0:T(8,128)(2,1)S(1)}, u32[]{:S(2)}, u32[]{:S(2)}) collective-permute-start(bf16[2,256,640]{1,2,0:T(8,128)(2,1)S(1)} %pad_maximum_fusion.1), channel_id=1, source_target_pairs={{1,0},{2,1},{3,2},{4,3},{5,4},{6,5},{7,6},{9,8},{10,9},{11,10},{12... | collective-permute-start | bytes 1966088 | tf_op jit(solution)/shard_map/ppermute | solution.py:17
  41.7 31.5 %collective-permute-start.1 = (bf16[2,256,640]{1,2,0:T(8,128)(2,1)S(1)}, bf16[2,256,640]{1,2,0:T(8,128)(2,1)}, u32[]{:S(2)}, u32[]{:S(2)}) collective-permute-start(bf16[2,256,640]{1,2,0:T(8,128)(2,1)S(1)} %collective-permute-done), channel_id=1, source_target_pairs={{0,1},{1,2},{2,3},{3,4},{4,5},{5,6},{6,7},{8,9},{9,10},{10,11},{11... | collective-permute-start | bytes 1966088 | tf_op jit(solution)/shard_map/ppermute | solution.py:17
  47.1 33.6 %collective-permute-start.4 = (bf16[2,256,640]{1,2,0:T(8,128)(2,1)S(1)}, bf16[2,256,640]{1,2,0:T(8,128)(2,1)}, u32[]{:S(2)}, u32[]{:S(2)}) collective-permute-start(bf16[2,256,640]{1,2,0:T(8,128)(2,1)S(1)} %collective-permute-done.3), channel_id=1, source_target_pairs={{1,0},{2,1},{3,2},{4,3},{5,4},{6,5},{7,6},{9,8},{10,9},{11,10},{12... | collective-permute-start | bytes 1966088 | tf_op jit(solution)/shard_map/ppermute | solution.py:17
  73.3 31.0 %collective-permute-start.2 = (bf16[2,256,640]{1,2,0:T(8,128)(2,1)}, bf16[2,256,640]{1,2,0:T(8,128)(2,1)}, u32[]{:S(2)}, u32[]{:S(2)}) collective-permute-start(bf16[2,256,640]{1,2,0:T(8,128)(2,1)} %collective-permute-done.1), channel_id=1, source_target_pairs={{0,1},{1,2},{2,3},{3,4},{4,5},{5,6},{6,7},{8,9},{9,10},{10,11},{11... | collective-permute-start | bytes 1966088 | tf_op jit(solution)/shard_map/ppermute | solution.py:17
  80.7 27.1 %collective-permute-start.5 = (bf16[2,256,640]{1,2,0:T(8,128)(2,1)}, bf16[2,256,640]{1,2,0:T(8,128)(2,1)S(1)}, u32[]{:S(2)}, u32[]{:S(2)}) collective-permute-start(bf16[2,256,640]{1,2,0:T(8,128)(2,1)} %collective-permute-done.4), channel_id=1, source_target_pairs={{1,0},{2,1},{3,2},{4,3},{5,4},{6,5},{7,6},{9,8},{10,9},{11,10},{12... | collective-permute-start | bytes 1966088 | tf_op jit(solution)/shard_map/ppermute | solution.py:17
  110.4 9.4 %copy-start.31 = (bf16[8,256,80]{1,2,0:T(8,128)(2,1)}, bf16[8,256,80]{1,2,0:T(8,128)(2,1)S(1)}, u32[]{:S(2)}) copy-start(bf16[8,256,80]{1,2,0:T(8,128)(2,1)S(1)} %get-tuple-element.989) | copy-start | bytes 983044 | tf_op jit(solution)/shard_map/while
  110.4 12.4 %copy-start.33 = (s32[256]{0:T(256)}, s32[256]{0:T(256)S(1)}, u32[]{:S(2)}) copy-start(s32[256]{0:T(256)S(1)} %get-tuple-element.1000) | copy-start | bytes 3076 | tf_op jit(solution)/shard_map/while
  137.2 8.0 %copy-start.8 = (f32[256,80]{0,1:T(8,128)S(1)}, f32[256,80]{0,1:T(8,128)}, u32[]{:S(2)}) copy-start(f32[256,80]{0,1:T(8,128)} %copy-done.7) | copy-start | bytes 245764 | tf_op jit(solution)/shard_map/while
  146.5 9.4 %copy-start.31 = (bf16[8,256,80]{1,2,0:T(8,128)(2,1)}, bf16[8,256,80]{1,2,0:T(8,128)(2,1)S(1)}, u32[]{:S(2)}) copy-start(bf16[8,256,80]{1,2,0:T(8,128)(2,1)S(1)} %get-tuple-element.989) | copy-start | bytes 983044 | tf_op jit(solution)/shard_map/while
  146.5 12.4 %copy-start.33 = (s32[256]{0:T(256)}, s32[256]{0:T(256)S(1)}, u32[]{:S(2)}) copy-start(s32[256]{0:T(256)S(1)} %get-tuple-element.1000) | copy-start | bytes 3076 | tf_op jit(solution)/shard_map/while
  173.4 8.0 %copy-start.8 = (f32[256,80]{0,1:T(8,128)S(1)}, f32[256,80]{0,1:T(8,128)}, u32[]{:S(2)}) copy-start(f32[256,80]{0,1:T(8,128)} %copy-done.7) | copy-start | bytes 245764 | tf_op jit(solution)/shard_map/while
  182.6 9.4 %copy-start.31 = (bf16[8,256,80]{1,2,0:T(8,128)(2,1)}, bf16[8,256,80]{1,2,0:T(8,128)(2,1)S(1)}, u32[]{:S(2)}) copy-start(bf16[8,256,80]{1,2,0:T(8,128)(2,1)S(1)} %get-tuple-element.989) | copy-start | bytes 983044 | tf_op jit(solution)/shard_map/while
  182.6 12.4 %copy-start.33 = (s32[256]{0:T(256)}, s32[256]{0:T(256)S(1)}, u32[]{:S(2)}) copy-start(s32[256]{0:T(256)S(1)} %get-tuple-element.1000) | copy-start | bytes 3076 | tf_op jit(solution)/shard_map/while
  209.5 8.0 %copy-start.8 = (f32[256,80]{0,1:T(8,128)S(1)}, f32[256,80]{0,1:T(8,128)}, u32[]{:S(2)}) copy-start(f32[256,80]{0,1:T(8,128)} %copy-done.7) | copy-start | bytes 245764 | tf_op jit(solution)/shard_map/while
  211.6 6.0 copy-start.20
  211.6 6.0 copy-start.23
  218.7 9.4 %copy-start.31 = (bf16[8,256,80]{1,2,0:T(8,128)(2,1)}, bf16[8,256,80]{1,2,0:T(8,128)(2,1)S(1)}, u32[]{:S(2)}) copy-start(bf16[8,256,80]{1,2,0:T(8,128)(2,1)S(1)} %get-tuple-element.989) | copy-start | bytes 983044 | tf_op jit(solution)/shard_map/while
  218.7 12.4 %copy-start.33 = (s32[256]{0:T(256)}, s32[256]{0:T(256)S(1)}, u32[]{:S(2)}) copy-start(s32[256]{0:T(256)S(1)} %get-tuple-element.1000) | copy-start | bytes 3076 | tf_op jit(solution)/shard_map/while
  245.6 8.0 %copy-start.8 = (f32[256,80]{0,1:T(8,128)S(1)}, f32[256,80]{0,1:T(8,128)}, u32[]{:S(2)}) copy-start(f32[256,80]{0,1:T(8,128)} %copy-done.7) | copy-start | bytes 245764 | tf_op jit(solution)/shard_map/while
  247.7 6.0 copy-start.23
  254.9 9.4 %copy-start.31 = (bf16[8,256,80]{1,2,0:T(8,128)(2,1)}, bf16[8,256,80]{1,2,0:T(8,128)(2,1)S(1)}, u32[]{:S(2)}) copy-start(bf16[8,256,80]{1,2,0:T(8,128)(2,1)S(1)} %get-tuple-element.989) | copy-start | bytes 983044 | tf_op jit(solution)/shard_map/while
  254.9 12.4 %copy-start.33 = (s32[256]{0:T(256)}, s32[256]{0:T(256)S(1)}, u32[]{:S(2)}) copy-start(s32[256]{0:T(256)S(1)} %get-tuple-element.1000) | copy-start | bytes 3076 | tf_op jit(solution)/shard_map/while
  281.7 8.0 %copy-start.8 = (f32[256,80]{0,1:T(8,128)S(1)}, f32[256,80]{0,1:T(8,128)}, u32[]{:S(2)}) copy-start(f32[256,80]{0,1:T(8,128)} %copy-done.7) | copy-start | bytes 245764 | tf_op jit(solution)/shard_map/while
  291.0 9.4 %copy-start.31 = (bf16[8,256,80]{1,2,0:T(8,128)(2,1)}, bf16[8,256,80]{1,2,0:T(8,128)(2,1)S(1)}, u32[]{:S(2)}) copy-start(bf16[8,256,80]{1,2,0:T(8,128)(2,1)S(1)} %get-tuple-element.989) | copy-start | bytes 983044 | tf_op jit(solution)/shard_map/while
  291.0 12.4 %copy-start.33 = (s32[256]{0:T(256)}, s32[256]{0:T(256)S(1)}, u32[]{:S(2)}) copy-start(s32[256]{0:T(256)S(1)} %get-tuple-element.1000) | copy-start | bytes 3076 | tf_op jit(solution)/shard_map/while
  317.8 8.0 %copy-start.8 = (f32[256,80]{0,1:T(8,128)S(1)}, f32[256,80]{0,1:T(8,128)}, u32[]{:S(2)}) copy-start(f32[256,80]{0,1:T(8,128)} %copy-done.7) | copy-start | bytes 245764 | tf_op jit(solution)/shard_map/while
  320.0 6.0 copy-start.23
  327.1 9.4 %copy-start.31 = (bf16[8,256,80]{1,2,0:T(8,128)(2,1)}, bf16[8,256,80]{1,2,0:T(8,128)(2,1)S(1)}, u32[]{:S(2)}) copy-start(bf16[8,256,80]{1,2,0:T(8,128)(2,1)S(1)} %get-tuple-element.989) | copy-start | bytes 983044 | tf_op jit(solution)/shard_map/while
  327.1 12.4 %copy-start.33 = (s32[256]{0:T(256)}, s32[256]{0:T(256)S(1)}, u32[]{:S(2)}) copy-start(s32[256]{0:T(256)S(1)} %get-tuple-element.1000) | copy-start | bytes 3076 | tf_op jit(solution)/shard_map/while
  353.9 8.0 %copy-start.8 = (f32[256,80]{0,1:T(8,128)S(1)}, f32[256,80]{0,1:T(8,128)}, u32[]{:S(2)}) copy-start(f32[256,80]{0,1:T(8,128)} %copy-done.7) | copy-start | bytes 245764 | tf_op jit(solution)/shard_map/while
  356.1 6.0 copy-start.23
  363.3 9.4 %copy-start.31 = (bf16[8,256,80]{1,2,0:T(8,128)(2,1)}, bf16[8,256,80]{1,2,0:T(8,128)(2,1)S(1)}, u32[]{:S(2)}) copy-start(bf16[8,256,80]{1,2,0:T(8,128)(2,1)S(1)} %get-tuple-element.989) | copy-start | bytes 983044 | tf_op jit(solution)/shard_map/while
  363.3 12.4 %copy-start.33 = (s32[256]{0:T(256)}, s32[256]{0:T(256)S(1)}, u32[]{:S(2)}) copy-start(s32[256]{0:T(256)S(1)} %get-tuple-element.1000) | copy-start | bytes 3076 | tf_op jit(solution)/shard_map/while
  390.1 8.0 %copy-start.8 = (f32[256,80]{0,1:T(8,128)S(1)}, f32[256,80]{0,1:T(8,128)}, u32[]{:S(2)}) copy-start(f32[256,80]{0,1:T(8,128)} %copy-done.7) | copy-start | bytes 245764 | tf_op jit(solution)/shard_map/while
  399.4 40.4 %slice-start = ((s8[4587520]{0:T(1024)(128)(4,1)}), s8[4194304]{0:T(1024)(128)(4,1)S(1)}, s32[]{:S(2)}) async-start(s8[4587520]{0:T(1024)(128)(4,1)} %bitcast.227), calls=%async_computation | async-start | bytes 8388608
  399.4 40.3 %slice-start.1 = ((s8[4587520]{0:T(1024)(128)(4,1)}), s8[393216]{0:T(1024)(128)(4,1)S(1)}, s32[]{:S(2)}) async-start(s8[4587520]{0:T(1024)(128)(4,1)} %bitcast.227), calls=%async_computation.1 | async-start | bytes 786432
  399.4 40.3 %copy-start = (f32[8,1792,80]{1,2,0:T(8,128)S(1)}, f32[8,1792,80]{1,2,0:T(8,128)}, u32[]{:S(2)}) copy-start(f32[8,1792,80]{1,2,0:T(8,128)} %get-tuple-element.398) | copy-start | bytes 13762564
  400.9 38.8 %collective-permute-start.6 = (f32[2,256,640]{1,2,0:T(8,128)S(1)}, f32[2,256,640]{1,2,0:T(8,128)S(1)}, u32[]{:S(2)}, u32[]{:S(2)}) collective-permute-start(f32[2,256,640]{1,2,0:T(8,128)S(1)} %fusion.28), channel_id=1, source_target_pairs={{1,0},{2,1},{3,2},{4,3},{5,4},{6,5},{7,6},{9,8},{10,9},{11,10},{12... | collective-permute-start | bytes 3932168 | tf_op jit(solution)/shard_map/ppermute | solution.py:17
  440.0 34.6 %collective-permute-start.7 = (f32[2,256,640]{1,2,0:T(8,128)S(1)}, f32[2,256,640]{1,2,0:T(8,128)S(1)}, u32[]{:S(2)}, u32[]{:S(2)}) collective-permute-start(f32[2,256,640]{1,2,0:T(8,128)S(1)} %fusion.30), channel_id=1, source_target_pairs={{1,0},{2,1},{3,2},{4,3},{5,4},{6,5},{7,6},{9,8},{10,9},{11,10},{12... | collective-permute-start | bytes 3932168 | tf_op jit(solution)/shard_map/ppermute | solution.py:17
  474.9 35.5 %collective-permute-start.9 = (f32[2,256,640]{1,2,0:T(8,128)S(1)}, f32[2,256,640]{1,2,0:T(8,128)S(1)}, u32[]{:S(2)}, u32[]{:S(2)}) collective-permute-start(f32[2,256,640]{1,2,0:T(8,128)S(1)} %get-tuple-element.658), channel_id=1, source_target_pairs={{0,1},{1,2},{2,3},{3,4},{4,5},{5,6},{6,7},{8,9},{9,10},{10,11},{11... | collective-permute-start | bytes 3932168 | tf_op jit(solution)/shard_map/ppermute | solution.py:17
  510.6 55.7 %collective-permute-start.10 = (f32[2,256,640]{1,2,0:T(8,128)S(1)}, f32[2,256,640]{1,2,0:T(8,128)S(1)}, u32[]{:S(2)}, u32[]{:S(2)}) collective-permute-start(f32[2,256,640]{1,2,0:T(8,128)S(1)} %fusion.27), channel_id=1, source_target_pairs={{0,1},{1,2},{2,3},{3,4},{4,5},{5,6},{6,7},{8,9},{9,10},{10,11},{11... | collective-permute-start | bytes 3932168 | tf_op jit(solution)/shard_map/ppermute | solution.py:17
  515.1 59.9 %copy-start.25 = (f32[8,256,80]{1,2,0:T(8,128)S(1)}, f32[8,256,80]{1,2,0:T(8,128)}, u32[]{:S(2)}) copy-start(f32[8,256,80]{1,2,0:T(8,128)} %get-tuple-element.397) | copy-start | bytes 1966084
  515.1 59.9 %copy-start.30 = (f32[256,80]{0,1:T(8,128)S(1)}, f32[256,80]{0,1:T(8,128)}, u32[]{:S(2)}) copy-start(f32[256,80]{0,1:T(8,128)} %copy-done.29) | copy-start | bytes 245764
  515.1 62.7 %collective-permute-start.8 = (f32[2,256,640]{1,2,0:T(8,128)S(1)}, f32[2,256,640]{1,2,0:T(8,128)S(1)}, u32[]{:S(2)}, u32[]{:S(2)}) collective-permute-start(f32[2,256,640]{1,2,0:T(8,128)S(1)} %get-tuple-element.657), channel_id=1, source_target_pairs={{1,0},{2,1},{3,2},{4,3},{5,4},{6,5},{7,6},{9,8},{10,9},{11,10},{12... | collective-permute-start | bytes 3932168 | tf_op jit(solution)/shard_map/ppermute | solution.py:17
  567.5 7.6 %copy-start.27 = (f32[256,80]{0,1:T(8,128)S(1)}, f32[256,80]{0,1:T(8,128)}, u32[]{:S(2)}) copy-start(f32[256,80]{0,1:T(8,128)} %copy-done.26) | copy-start | bytes 245764
  567.5 28.0 %collective-permute-start.11 = (f32[2,256,640]{1,2,0:T(8,128)}, f32[2,256,640]{1,2,0:T(8,128)}, u32[]{:S(2)}, u32[]{:S(2)}) collective-permute-start(f32[2,256,640]{1,2,0:T(8,128)} %fusion.37), channel_id=1, source_target_pairs={{0,1},{1,2},{2,3},{3,4},{4,5},{5,6},{6,7},{8,9},{9,10},{10,11},{11... | collective-permute-start | bytes 3932168 | tf_op jit(solution)/shard_map/ppermute | solution.py:17
  (206 other events, 486.3 us)
where the time goes:
time: 652 us; the launch traced here: 645 us
  waiting for transfers between devices  236 us (36%)
  local copies, waits for them, and re-layouts  155 us (24%)
  matrix products  76.3 us (12%)
  starting transfers between devices  45 us (7%)
  blocking collectives  44.6 us (7%)
  other arithmetic  43.5 us (7%)
  loops' own time  43.3 us (7%)
    ppermute x12, waiting for transfers between devices, from_behind(): lax.ppermute(value, axis, [(source, source + steps) for source in range(i...  236 us
    while x720, local copies, waits for them, and re-layouts  91.6 us
    ppermute x12, starting transfers between devices, from_behind(): lax.ppermute(value, axis, [(source, source + steps) for source in range(i...  45 us
    psum x1, blocking collectives, on_device(): summed = lax.psum(local_sums, ('dp', 'tok'))  44.6 us
    another operation x1, loops' own time, on_device(): lax.map(one_head, (query_heads, key_heads, value_heads, grad_heads))  40.9 us
    dot_general x32, matrix products, one_head(): jnp.einsum('qk,kd->qd', weights, vals, preferred_element_type=jnp.float32)  26.8 us
    another operation x120, local copies, waits for them, and re-layouts  16.2 us
    reduce_sum x8, other arithmetic, one_head(): jnp.sum(grad_h.astype(jnp.float32) * out_b.astype(jnp.float32), axis=-1)  14.4 us
  transfers between devices with their start and end apart: 12, of which 8 were waited for; matrix products, arithmetic and copies ran while one was open for 2% of the time, Pallas kernels for 0%

commit v1 on v0

v1 whole, which is shorter than its diff:
```python
import functools

import jax
import jax.numpy as jnp
import numpy as np
from jax import lax
from jax.experimental import pallas as pl
from jax.experimental.pallas import tpu as pltpu
from jax.sharding import PartitionSpec as P

HEADS = 8
HEAD_DIM = 80
SPAN = 4
OWN_HEADS = HEADS // SPAN
PART = OWN_HEADS * HEAD_DIM
SCALE = HEAD_DIM**-0.5
LOG2E = 1.4426950408889634
NEG = -1e30

rope_base = 10000.0


def trade_rounds(count):
    def pairs_of(shift):
        found = []
        for source in range(count):
            target = source + shift
            if 0 <= target < count and (source < SPAN) == (target < SPAN):
                found.append((source, target))
        return found

    rounds = []
    for shift in range(1, SPAN):
        ahead, back = pairs_of(shift), pairs_of(shift - SPAN)
        both = ahead + back
        if len({s for s, _ in both}) == len(both) and len({t for _, t in both}) == len(both):
            rounds.append((shift, both))
        else:
            rounds.append((shift, ahead))
            rounds.append((shift - SPAN, back))
    return rounds


def source_table(rounds, count):
    table = np.full((len(rounds), count), -1, np.int32)
    for number, (_, pairs) in enumerate(rounds):
        for source, target in pairs:
            table[number, target] = source
    return table


def target_table(rounds, count):
    table = np.full((len(rounds), count), -1, np.int32)
    for number, (_, pairs) in enumerate(rounds):
        for source, target in pairs:
            table[number, source] = target
    return table


def image_of(block, lengths, images):
    image = jnp.int32(0)
    start = jnp.int32(0)
    begin = jnp.int32(0)
    for number in range(images):
        size = lengths[0, number]
        inside = (block >= begin) & (block < begin + size)
        image = jnp.where(inside, number, image)
        start = jnp.where(inside, begin, start)
        begin = begin + size
    return image, start


def handler_of(start, residue, count):
    device = start + lax.rem(residue - lax.rem(start, SPAN) + SPAN, SPAN)
    return jnp.where(device >= count, device - SPAN, device)


def swap_halves(values):
    half = HEAD_DIM // 2
    return jnp.concatenate([values[:, half:], values[:, :half]], axis=1)


def pack_kernel(shifts, query, key, value, grad, *outs):
    me = lax.axis_index("tok")
    for residue in range(SPAN):
        lanes = slice(residue * PART, (residue + 1) * PART)
        piece = jnp.concatenate([ref[:, lanes] for ref in (query, key, value, grad)], axis=1)
        for shift, out in zip(shifts, outs):

            @pl.when(lax.rem(me + shift + SPAN, SPAN) == residue)
            def _(out=out, piece=piece):
                out[...] = piece


def angles_kernel(images, tokd, lengths, widths, table, inverse, cos_out, sin_out):
    me = lax.axis_index("tok")
    slots = table.shape[0] + 1
    lane = lax.broadcasted_iota(jnp.int32, (tokd, HEAD_DIM), 1)
    spot = lax.broadcasted_iota(jnp.int32, (tokd, HEAD_DIM), 0)
    quarter = HEAD_DIM // 4
    by_row = lax.rem(lane, 2 * quarter) < quarter
    sign = jnp.where(lane < 2 * quarter, -1.0, 1.0)

    def one(slot, carry):
        block = jnp.where(slot == 0, me, table[jnp.maximum(slot - 1, 0), me])
        image, start = image_of(block, lengths, images)
        width = widths[0, image]
        bits = jnp.where(width == tokd, 0, jnp.where(width * 2 == tokd, 1, 2))
        full = tokd.bit_length() - 1
        local = spot + (block - start) * tokd
        shift = full - bits
        rowpos = lax.shift_right_logical(local, jnp.broadcast_to(shift, local.shape))
        colpos = local & (width - 1)
        angle = jnp.where(by_row, rowpos, colpos).astype(jnp.float32) * inverse[0:1, :]
        rows = pl.ds(pl.multiple_of(slot * tokd, tokd), tokd)
        cos_out[rows, :] = jnp.cos(angle)
        sin_out[rows, :] = jnp.sin(angle) * sign
        return carry

    lax.fori_loop(0, slots, one, 0)


def attend_kernel(slots, count, images, tokd, lengths, table, cosv, sinv, bias, *refs):
    msgs, outs, sums = refs[:slots], refs[slots : 2 * slots], refs[2 * slots]
    q_all, k_all, v_all, dk_acc, dv_acc = refs[2 * slots + 1 :]
    me = lax.axis_index("tok")
    residue = lax.rem(me, SPAN)
    ids = []
    for slot in range(slots):
        block = me if slot == 0 else table[slot - 1, me]
        image, start = image_of(block, lengths, images)
        handled = (block >= 0) & (handler_of(start, residue, count) == me)
        ids.append(jnp.where(handled, image, -1 - slot))
    own_bias = jnp.zeros((3, PART), jnp.float32)
    for number in range(SPAN):
        piece = bias[:, number * PART : (number + 1) * PART].astype(jnp.float32)
        own_bias = jnp.where(residue == number, piece, own_bias)
    transposed = (((1,), (1,)), ((), ()))

    def cut(slot, tensor, head):
        begin = tensor * PART + head * HEAD_DIM
        return slice(begin, begin + HEAD_DIM)

    def block_rows(slot):
        return slice(slot * tokd, (slot + 1) * tokd)

    sums[...] = jnp.zeros_like(sums)
    for head in range(OWN_HEADS):
        lanes = slice(head * HEAD_DIM, (head + 1) * HEAD_DIM)
        for slot in range(slots):
            rows = block_rows(slot)
            cos_b, sin_b = cosv[rows, :], sinv[rows, :]
            for tensor, store in ((0, q_all), (1, k_all)):
                plain = msgs[slot][:, cut(slot, tensor, head)].astype(jnp.float32)
                plain = plain + own_bias[tensor : tensor + 1, lanes]
                turned = plain * cos_b + swap_halves(plain) * sin_b
                store[rows, :] = turned.astype(jnp.bfloat16)
            plain = msgs[slot][:, cut(slot, 2, head)].astype(jnp.float32)
            v_all[rows, :] = (plain + own_bias[2:3, lanes]).astype(jnp.bfloat16)
        dq_total = jnp.zeros((1, HEAD_DIM), jnp.float32)
        for slot in range(slots):
            rows = block_rows(slot)
            query_b = q_all[rows, :]
            grad_b = msgs[slot][:, cut(slot, 3, head)]
            scores = lax.dot_general(
                query_b, k_all[...], transposed, preferred_element_type=jnp.float32
            )
            offs = [jnp.where(ids[slot] == ids[other], 0.0, NEG) for other in range(slots)]
            tops = [
                jnp.max(scores[:, block_rows(other)], axis=1, keepdims=True) + offs[other]
                for other in range(slots)
            ]
            top = functools.reduce(jnp.maximum, tops)
            expo = jnp.concatenate(
                [
                    jnp.exp2(
                        (scores[:, block_rows(other)] - (top - offs[other])) * (SCALE * LOG2E)
                    )
                    for other in range(slots)
                ],
                axis=1,
            )
            probs = expo * (1.0 / jnp.sum(expo, axis=1, keepdims=True))
            probs_b = probs.astype(jnp.bfloat16)
            out_b = jnp.dot(probs_b, v_all[...], preferred_element_type=jnp.float32).astype(
                jnp.bfloat16
            )
            delta = jnp.sum(
                grad_b.astype(jnp.float32) * out_b.astype(jnp.float32), axis=1, keepdims=True
            )
            dprobs = lax.dot_general(
                grad_b, v_all[...], transposed, preferred_element_type=jnp.float32
            )
            dscore_b = (probs * (dprobs - delta)).astype(jnp.bfloat16)
            dquery = jnp.dot(dscore_b, k_all[...], preferred_element_type=jnp.float32) * SCALE
            part_k = jnp.dot(query_b.T, dscore_b, preferred_element_type=jnp.float32)
            part_v = jnp.dot(grad_b.T, probs_b, preferred_element_type=jnp.float32)
            if slot == 0:
                dk_acc[...] = part_k
                dv_acc[...] = part_v
            else:
                dk_acc[...] += part_k
                dv_acc[...] += part_v
            outs[slot][:, cut(slot, 0, head)] = out_b
            dquery = dquery * cosv[rows, :] - swap_halves(dquery) * sinv[rows, :]
            dq_total = dq_total + jnp.where(
                ids[slot] >= 0, jnp.sum(dquery, axis=0, keepdims=True), 0.0
            )
            outs[slot][:, cut(slot, 1, head)] = dquery.astype(jnp.bfloat16)
        dk_total = jnp.zeros((1, HEAD_DIM), jnp.float32)
        dv_total = jnp.zeros((1, HEAD_DIM), jnp.float32)
        for slot in range(slots):
            rows = block_rows(slot)
            dkey = dk_acc[:, rows].T * SCALE
            dkey = dkey * cosv[rows, :] - swap_halves(dkey) * sinv[rows, :]
            dvalue = dv_acc[:, rows].T
            outs[slot][:, cut(slot, 2, head)] = dkey.astype(jnp.bfloat16)
            outs[slot][:, cut(slot, 3, head)] = dvalue.astype(jnp.bfloat16)
            live = ids[slot] >= 0
            dk_total = dk_total + jnp.where(live, jnp.sum(dkey, axis=0, keepdims=True), 0.0)
            dv_total = dv_total + jnp.where(live, jnp.sum(dvalue, axis=0, keepdims=True), 0.0)
        for number, total in enumerate((dq_total, dk_total, dv_total)):
            at = number * OWN_HEADS + head
            sums[at : at + 1, :HEAD_DIM] = total


def unpack_kernel(slots, count, images, lengths, table, *refs):
    msgs, outs = refs[:slots], refs[slots:]
    me = lax.axis_index("tok")
    _, start = image_of(me, lengths, images)
    for residue in range(SPAN):
        lanes = slice(residue * PART, (residue + 1) * PART)
        handler = handler_of(start, residue, count)
        for slot in range(slots):
            source = me if slot == 0 else table[slot - 1, me]

            @pl.when(source == handler)
            def _(slot=slot, lanes=lanes):
                for number, out in enumerate(outs):
                    out[:, lanes] = msgs[slot][:, number * PART : (number + 1) * PART]


def on_device(query_in, key_in, value_in, out_grad, bias, lengths, widths):
    tokd = query_in.shape[1]
    model = query_in.shape[2]
    images = lengths.shape[1]
    count = lax.axis_size("tok")
    rounds = trade_rounds(count)
    shifts = [0] + [shift for shift, _ in rounds]
    slots = len(shifts)
    table = jnp.asarray(source_table(rounds, count))
    quarter = HEAD_DIM // 4
    inverse = rope_base ** (-np.arange(quarter, dtype=np.float64) / quarter)
    inverse = jnp.asarray(np.tile(inverse, 4)[None], jnp.float32)
    smem = pl.BlockSpec(memory_space=pltpu.SMEM)
    vmem = pl.BlockSpec(memory_space=pltpu.VMEM)
    message = jax.ShapeDtypeStruct((tokd, model), jnp.bfloat16)

    def params(mib):
        return pltpu.CompilerParams(vmem_limit_bytes=mib * 1024 * 1024)

    sends = pl.pallas_call(
        functools.partial(pack_kernel, shifts),
        out_shape=[message] * slots,
        in_specs=[vmem] * 4,
        out_specs=[vmem] * slots,
        compiler_params=params(16),
        name="pack_heads",
    )(query_in[0], key_in[0], value_in[0], out_grad[0])
    got = [sends[0]] + [
        lax.ppermute(send, "tok", pairs) for send, (_, pairs) in zip(sends[1:], rounds)
    ]
    table_shape = jax.ShapeDtypeStruct((slots * tokd, HEAD_DIM), jnp.float32)
    cosv, sinv = pl.pallas_call(
        functools.partial(angles_kernel, images, tokd),
        out_shape=[table_shape] * 2,
        in_specs=[smem, smem, smem, vmem],
        out_specs=[vmem] * 2,
        compiler_params=params(16),
        cost_estimate=pl.CostEstimate(
            flops=slots * tokd * HEAD_DIM * 200, bytes_accessed=0, transcendentals=0
        ),
        name="rotary_angles",
    )(lengths, widths, table, inverse)
    span = slots * tokd
    results = pl.pallas_call(
        functools.partial(attend_kernel, slots, count, images, tokd),
        out_shape=[message] * slots + [jax.ShapeDtypeStruct((8, 128), jnp.float32)],
        in_specs=[smem, smem] + [vmem] * (3 + slots),
        out_specs=[vmem] * (slots + 1),
        scratch_shapes=[pltpu.VMEM((span, HEAD_DIM), jnp.bfloat16)] * 3
        + [pltpu.VMEM((HEAD_DIM, span), jnp.float32)] * 2,
        compiler_params=params(40),
        cost_estimate=pl.CostEstimate(
            flops=12 * span * span * PART, bytes_accessed=0, transcendentals=0
        ),
        name="attend",
    )(lengths, table, cosv, sinv, bias, *got)
    sums = results[slots]
    back = [results[0]] + [
        lax.ppermute(result, "tok", [(target, source) for source, target in pairs])
        for result, (_, pairs) in zip(results[1:slots], rounds)
    ]
    every = lax.all_gather(sums, ("dp", "tok"))
    n_dp = lax.axis_size("dp")
    every = jnp.sum(every.reshape(n_dp * (count // SPAN), SPAN, 8, 128), axis=0)
    parts = every[:, : 3 * OWN_HEADS, :HEAD_DIM].reshape(SPAN, 3, PART)
    tokens_all = n_dp * count * tokd
    bias_grad = parts.transpose(1, 0, 2).reshape(3, model) * (1.0 / tokens_all**0.5)
    outs = pl.pallas_call(
        functools.partial(unpack_kernel, slots, count, images),
        out_shape=[message] * 4,
        in_specs=[smem, smem] + [vmem] * slots,
        out_specs=[vmem] * 4,
        compiler_params=params(16),
        name="unpack_heads",
    )(lengths, jnp.asarray(target_table(rounds, count)), *back)
    return tuple(out[None] for out in outs) + (bias_grad,)


def solution(mesh):
    in_specs = (
        P("dp", "tok", None),
        P("dp", "tok", None),
        P("dp", "tok", None),
        P("dp", "tok", None),
        P(),
        P("dp", None),
        P("dp", None),
    )
    out_specs = (
        P("dp", "tok", None),
        P("dp", "tok", None),
        P("dp", "tok", None),
        P("dp", "tok", None),
        P(),
    )
    return jax.shard_map(
        on_device, mesh=mesh, in_specs=in_specs, out_specs=out_specs, check_vma=False
    )
```

time: 652 us -> 124 us (0.19); the launches traced: 645 us -> 124 us
  waiting for transfers between devices: 236 us -> 10.1 us
  local copies, waits for them, and re-layouts: 155 us -> 4.68 us
  matrix products: 76.3 us -> 0 us
  other arithmetic: 43.5 us -> 0.02 us
  loops' own time: 43.3 us -> 0 us
  starting transfers between devices: 45 us -> 9.8 us
  blocking collectives: 44.6 us -> 74.8 us
  Pallas kernels: 0 us -> 23.9 us
    ppermute x12 -> x6, waiting for transfers between devices: 236 us -> 10.1 us  [the longest x3 10.1 us: on_device(): lax.ppermute(send, 'tok', pairs)]
    while x720 -> x0, local copies, waits for them, and re-layouts: 91.6 us -> none
    dot_general x192 -> x0, matrix products: 76.3 us -> none  [the longest x32 26.8 us: one_head(): jnp.einsum('qk,kd->qd', weights, vals, preferred_element_type=jnp.float32)]
    all_gather x0 -> x1, blocking collectives: none -> 74.8 us  [on_device(): every = lax.all_gather(sums, ('dp', 'tok'))]
    psum x1 -> x0, blocking collectives: 44.6 us -> none  [on_device(): summed = lax.psum(local_sums, ('dp', 'tok'))]
    another operation x169 -> x0, loops' own time: 43.3 us -> none  [the longest x1 40.9 us: on_device(): lax.map(one_head, (query_heads, key_heads, value_heads, grad_heads))]
    ppermute x12 -> x6, starting transfers between devices: 45 us -> 9.8 us  [the longest x3 6.01 us: on_device(): lax.ppermute(send, 'tok', pairs)]
    pallas_call x0 -> x4, Pallas kernels: none -> 23.9 us  [the longest x1 18 us: on_device(): pl.pallas_call(functools.partial(attend_kernel, slots, count, images, tok...]
  transfers between devices with their start and end apart: 12 -> 6, of which waited for: 8 -> 3; matrix products, arithmetic and copies ran while one was open for 2% -> 1% of each run, Pallas kernels for 0% -> 2%
where the time goes in v1:
time: 124 us
  blocking collectives  74.8 us (60%)
  Pallas kernels  23.9 us (19%)
  waiting for transfers between devices  10.1 us (8%)
  starting transfers between devices  9.8 us (8%)
  local copies, waits for them, and re-layouts  4.68 us (4%)
    all_gather x1, blocking collectives, on_device(): every = lax.all_gather(sums, ('dp', 'tok'))  74.8 us
    pallas_call x1, Pallas kernels, on_device(): pl.pallas_call(functools.partial(attend_kernel, slots, count, images, tok...  18 us
    ppermute x3, waiting for transfers between devices, on_device(): lax.ppermute(send, 'tok', pairs)  10.1 us
    ppermute x3, starting transfers between devices, on_device(): lax.ppermute(send, 'tok', pairs)  6.01 us
    unnamed x20, local copies, waits for them, and re-layouts  3.91 us
    ppermute x3, starting transfers between devices, on_device(): lax.ppermute(result, 'tok', [(target, source) for source, target in pairs])  3.79 us
    pallas_call x1, Pallas kernels, on_device(): pl.pallas_call(functools.partial(angles_kernel, images, tokd), out_shape=...  2.63 us
  transfers between devices with their start and end apart: 6, of which 3 were waited for; matrix products, arithmetic and copies ran while one was open for 1% of the time, Pallas kernels for 2%

profile of v1, /device:TPU:0, one launch (start us, length us, event | category | flops | bytes accessed | tf_op | source)
XLA Modules:
  0.0 124.0 jit_solution(5106793675050421396)
XLA Ops:
  0.6 0.0 copy-start
  0.6 1.0 copy-done
  1.6 0.0 copy-start.1
  1.6 1.0 copy-done.1
  2.6 0.0 copy-start.2
  2.6 1.0 copy-done.2
  3.6 0.0 copy-start.3
  3.6 1.0 copy-done.3
  4.5 0.8 pack_heads.1
  5.3 0.0 copy-start.8
  5.4 3.0 %collective-permute-start = (bf16[256,640]{1,0:T(8,128)(2,1)S(1)}, bf16[256,640]{1,0:T(8,128)(2,1)S(1)}, u32[]{:S(2)}, u32[]{:S(2)}) collective-permute-start(bf16[256,640]{1,0:T(8,128)(2,1)S(1)} %get-tuple-element.23), channel_id=1, source_target_pairs={{0,1},{1,2},{2,3},{4,5},{5,6},{6,7},{3,0},{7,4},{8,9},{9,10},{10,1... | collective-permute-start | bytes 983048 | tf_op jit(solution)/shard_map/ppermute | solution.py:271
  8.3 0.0 copy-start.5
  8.3 0.0 copy-start.7
  8.3 0.0 copy-start.9
  8.4 1.6 %collective-permute-start.1 = (bf16[256,640]{1,0:T(8,128)(2,1)S(1)}, bf16[256,640]{1,0:T(8,128)(2,1)S(1)}, u32[]{:S(2)}, u32[]{:S(2)}) collective-permute-start(bf16[256,640]{1,0:T(8,128)(2,1)S(1)} %get-tuple-element.24), channel_id=1, source_target_pairs={{0,2},{1,3},{4,6},{5,7},{2,0},{3,1},{6,4},{7,5},{8,10},{9,11},{12,... | collective-permute-start | bytes 983048 | tf_op jit(solution)/shard_map/ppermute | solution.py:271
  9.9 1.4 %collective-permute-start.2 = (bf16[256,640]{1,0:T(8,128)(2,1)S(1)}, bf16[256,640]{1,0:T(8,128)(2,1)S(1)}, u32[]{:S(2)}, u32[]{:S(2)}) collective-permute-start(bf16[256,640]{1,0:T(8,128)(2,1)S(1)} %get-tuple-element.25), channel_id=1, source_target_pairs={{0,3},{4,7},{1,0},{2,1},{3,2},{5,4},{6,5},{7,6},{8,11},{12,15},{9,... | collective-permute-start | bytes 983048 | tf_op jit(solution)/shard_map/ppermute | solution.py:271
  11.4 0.0 copy-done.8
  11.4 0.0 copy-done.5
  11.4 0.0 copy-done.7
  11.4 0.0 copy-done.9
  11.4 2.6 %rotary_angles.1 = (f32[1024,80]{1,0:T(8,128)S(1)}, f32[1024,80]{1,0:T(8,128)S(1)}) custom-call(s32[1,4]{1,0:T(1,128)S(1)} %copy-done.5, s32[1,4]{1,0:T(1,128)S(1)} %copy-done.7, s32[3,8]{1,0:T(4,128)S(1)} %copy-done.8, f32[1,80]{1,0:T(1,128)S(1)} %copy-done.9), custom_call_target="tpu_custom_call" | custom-call | flops 16384000 | tf_op jit(solution)/shard_map/rotary_angles/pallas_call | solution.py:274
  14.0 0.0 copy-start.6
  14.0 3.9 %collective-permute-done.refs_1_ = bf16[256,640]{1,0:T(8,128)(2,1)S(1)} collective-permute-done((bf16[256,640]{1,0:T(8,128)(2,1)S(1)}, bf16[256,640]{1,0:T(8,128)(2,1)S(1)}, u32[]{:S(2)}, u32[]{:S(2)}) %collective-permute-start) | collective-permute-done | bytes 327712 | tf_op jit(solution)/shard_map/ppermute | solution.py:271
  17.9 1.0 collective-permute-done.1.refs_2_
  19.0 5.1 %collective-permute-done.2.refs_3_ = bf16[256,640]{1,0:T(8,128)(2,1)S(1)} collective-permute-done((bf16[256,640]{1,0:T(8,128)(2,1)S(1)}, bf16[256,640]{1,0:T(8,128)(2,1)S(1)}, u32[]{:S(2)}, u32[]{:S(2)}) %collective-permute-start.2) | collective-permute-done | bytes 327712 | tf_op jit(solution)/shard_map/ppermute | solution.py:271
  24.1 0.0 copy-done.6
  24.1 18.0 %attend.1 = (bf16[256,640]{1,0:T(8,128)(2,1)S(1)}, bf16[256,640]{1,0:T(8,128)(2,1)S(1)}, bf16[256,640]{1,0:T(8,128)(2,1)S(1)}, bf16[256,640]{1,0:T(8,128)(2,1)S(1)}, f32[8,128]{1,0:T(8,128)S(1)}) custom-call(s32[1,4]{1,0:T(1,128)S(1)} %copy-done.5, s32[3,8]{1,0:T(4,128)S(1)} %copy-done.8, f32[1024,80]{1,0:T(8,128)S(1)} %get-tuple-element.20.cosv, ...), custom_call_target="tpu_custom_call" | custom-call | flops 2013265920 | tf_op jit(solution)/shard_map/attend/pallas_call | solution.py:286
  42.1 3.0 %collective-permute-start.3 = (bf16[256,640]{1,0:T(8,128)(2,1)S(1)}, bf16[256,640]{1,0:T(8,128)(2,1)S(1)}, u32[]{:S(2)}, u32[]{:S(2)}) collective-permute-start(bf16[256,640]{1,0:T(8,128)(2,1)S(1)} %get-tuple-element.27), channel_id=1, source_target_pairs={{1,0},{2,1},{3,2},{5,4},{6,5},{7,6},{0,3},{4,7},{9,8},{10,9},{11,1... | collective-permute-start | bytes 983048 | tf_op jit(solution)/shard_map/ppermute | solution.py:301
  45.1 0.4 collective-permute-start.4
  45.5 0.4 collective-permute-start.5
  45.9 74.8 %all-gather = f32[256,128]{1,0:T(8,128)S(1)} all-gather(f32[8,128]{1,0:T(8,128)S(1)} %get-tuple-element.34), channel_id=2, replica_groups=mesh['dp'=4,'tok'=8] {'dp','tok'}, dimensions={0}, use_global_device_ids=true | all-gather | bytes 135168 | tf_op jit(solution)/shard_map/all_gather | solution.py:304
  120.8 0.1 mul.17
  120.9 0.0 copy-start.4
  120.9 0.7 mul.19
  121.6 0.0 collective-permute-done.3.refs_1_
  121.6 0.0 collective-permute-done.4.refs_2_
  121.6 0.0 collective-permute-done.5.refs_3_
  121.6 0.0 copy-done.4
  121.6 2.4 %unpack_heads.1 = (bf16[256,640]{1,0:T(8,128)(2,1)}, bf16[256,640]{1,0:T(8,128)(2,1)}, bf16[256,640]{1,0:T(8,128)(2,1)}, bf16[256,640]{1,0:T(8,128)(2,1)}) custom-call(s32[1,4]{1,0:T(1,128)S(1)} %copy-done.5, s32[3,8]{1,0:T(4,128)S(1)} %copy-done.4, bf16[256,640]{1,0:T(8,128)(2,1)S(1)} %get-tuple-element.26.refs_0_, ...), custom_call_target="tpu_custom_call" | custom-call | tf_op jit(solution)/shard_map/unpack_heads/pallas_call | solution.py:310
  (3 shorter events, 0.0 us)
Async XLA Ops:
  0.6 1.0 copy-start
  1.6 1.0 copy-start.1
  2.6 1.0 copy-start.2
  3.6 1.0 copy-start.3
  5.3 6.0 %copy-start.8 = (s32[3,8]{1,0:T(4,128)S(1)}, s32[3,8]{1,0:T(4,128)}, u32[]{:S(2)}) copy-start(s32[3,8]{1,0:T(4,128)} %constant.10.clone.table) | copy-start | bytes 292
  5.4 12.6 %collective-permute-start = (bf16[256,640]{1,0:T(8,128)(2,1)S(1)}, bf16[256,640]{1,0:T(8,128)(2,1)S(1)}, u32[]{:S(2)}, u32[]{:S(2)}) collective-permute-start(bf16[256,640]{1,0:T(8,128)(2,1)S(1)} %get-tuple-element.23), channel_id=1, source_target_pairs={{0,1},{1,2},{2,3},{4,5},{5,6},{6,7},{3,0},{7,4},{8,9},{9,10},{10,1... | collective-permute-start | bytes 983048 | tf_op jit(solution)/shard_map/ppermute | solution.py:271
  8.3 3.0 %copy-start.5 = (s32[1,4]{1,0:T(1,128)S(1)}, s32[1,4]{1,0:T(1,128)}, u32[]{:S(2)}) copy-start(s32[1,4]{1,0:T(1,128)} %lengths.5) | copy-start | bytes 52
  8.3 3.0 %copy-start.7 = (s32[1,4]{1,0:T(1,128)S(1)}, s32[1,4]{1,0:T(1,128)}, u32[]{:S(2)}) copy-start(s32[1,4]{1,0:T(1,128)} %widths.1) | copy-start | bytes 52
  8.3 3.0 %copy-start.9 = (f32[1,80]{1,0:T(1,128)S(1)}, f32[1,80]{1,0:T(1,128)}, u32[]{:S(2)}) copy-start(f32[1,80]{1,0:T(1,128)} %constant.11.clone.inverse) | copy-start | bytes 964
  8.4 10.6 %collective-permute-start.1 = (bf16[256,640]{1,0:T(8,128)(2,1)S(1)}, bf16[256,640]{1,0:T(8,128)(2,1)S(1)}, u32[]{:S(2)}, u32[]{:S(2)}) collective-permute-start(bf16[256,640]{1,0:T(8,128)(2,1)S(1)} %get-tuple-element.24), channel_id=1, source_target_pairs={{0,2},{1,3},{4,6},{5,7},{2,0},{3,1},{6,4},{7,5},{8,10},{9,11},{12,... | collective-permute-start | bytes 983048 | tf_op jit(solution)/shard_map/ppermute | solution.py:271
  9.9 14.2 %collective-permute-start.2 = (bf16[256,640]{1,0:T(8,128)(2,1)S(1)}, bf16[256,640]{1,0:T(8,128)(2,1)S(1)}, u32[]{:S(2)}, u32[]{:S(2)}) collective-permute-start(bf16[256,640]{1,0:T(8,128)(2,1)S(1)} %get-tuple-element.25), channel_id=1, source_target_pairs={{0,3},{4,7},{1,0},{2,1},{3,2},{5,4},{6,5},{7,6},{8,11},{12,15},{9,... | collective-permute-start | bytes 983048 | tf_op jit(solution)/shard_map/ppermute | solution.py:271
  14.0 10.1 %copy-start.6 = (bf16[3,640]{1,0:T(4,128)(2,1)S(1)}, bf16[3,640]{1,0:T(4,128)(2,1)}, u32[]{:S(2)}) copy-start(bf16[3,640]{1,0:T(4,128)(2,1)} %bias.1) | copy-start | bytes 11524
  42.1 79.5 %collective-permute-start.3 = (bf16[256,640]{1,0:T(8,128)(2,1)S(1)}, bf16[256,640]{1,0:T(8,128)(2,1)S(1)}, u32[]{:S(2)}, u32[]{:S(2)}) collective-permute-start(bf16[256,640]{1,0:T(8,128)(2,1)S(1)} %get-tuple-element.27), channel_id=1, source_target_pairs={{1,0},{2,1},{3,2},{5,4},{6,5},{7,6},{0,3},{4,7},{9,8},{10,9},{11,1... | collective-permute-start | bytes 983048 | tf_op jit(solution)/shard_map/ppermute | solution.py:301
  45.1 76.5 %collective-permute-start.4 = (bf16[256,640]{1,0:T(8,128)(2,1)S(1)}, bf16[256,640]{1,0:T(8,128)(2,1)S(1)}, u32[]{:S(2)}, u32[]{:S(2)}) collective-permute-start(bf16[256,640]{1,0:T(8,128)(2,1)S(1)} %get-tuple-element.28), channel_id=1, source_target_pairs={{2,0},{3,1},{6,4},{7,5},{0,2},{1,3},{4,6},{5,7},{10,8},{11,9},{14,... | collective-permute-start | bytes 983048 | tf_op jit(solution)/shard_map/ppermute | solution.py:301
  45.5 76.0 %collective-permute-start.5 = (bf16[256,640]{1,0:T(8,128)(2,1)S(1)}, bf16[256,640]{1,0:T(8,128)(2,1)S(1)}, u32[]{:S(2)}, u32[]{:S(2)}) collective-permute-start(bf16[256,640]{1,0:T(8,128)(2,1)S(1)} %get-tuple-element.29), channel_id=1, source_target_pairs={{3,0},{7,4},{0,1},{1,2},{2,3},{4,5},{5,6},{6,7},{11,8},{15,12},{8,... | collective-permute-start | bytes 983048 | tf_op jit(solution)/shard_map/ppermute | solution.py:301
  120.9 0.7 copy-start.4

commit v2 on v1

v2 whole, which is shorter than its diff:
```python
import functools

import jax
import jax.numpy as jnp
import numpy as np
from jax import lax
from jax.experimental import pallas as pl
from jax.experimental.pallas import tpu as pltpu
from jax.sharding import PartitionSpec as P

HEADS = 8
HEAD_DIM = 80
SPAN = 4
OWN_HEADS = HEADS // SPAN
PART = OWN_HEADS * HEAD_DIM
SCALE = HEAD_DIM**-0.5
LOG2E = 1.4426950408889634
NEG = -1e30
LANES = 128

rope_base = 10000.0


def trade_rounds(count):
    def pairs_of(shift):
        found = []
        for source in range(count):
            target = source + shift
            if 0 <= target < count and (source < SPAN) == (target < SPAN):
                found.append((source, target))
        return found

    rounds = []
    for shift in range(1, SPAN):
        ahead, back = pairs_of(shift), pairs_of(shift - SPAN)
        both = ahead + back
        if len({s for s, _ in both}) == len(both) and len({t for _, t in both}) == len(both):
            rounds.append((shift, both))
        else:
            rounds.append((shift, ahead))
            rounds.append((shift - SPAN, back))
    return rounds


def source_table(rounds, count):
    table = np.full((len(rounds), count), -1, np.int32)
    for number, (_, pairs) in enumerate(rounds):
        for source, target in pairs:
            table[number, target] = source
    return table


def target_table(rounds, count):
    table = np.full((len(rounds), count), -1, np.int32)
    for number, (_, pairs) in enumerate(rounds):
        for source, target in pairs:
            table[number, source] = target
    return table


def image_of(block, lengths, images):
    image = jnp.int32(0)
    start = jnp.int32(0)
    begin = jnp.int32(0)
    for number in range(images):
        size = lengths[0, number]
        inside = (block >= begin) & (block < begin + size)
        image = jnp.where(inside, number, image)
        start = jnp.where(inside, begin, start)
        begin = begin + size
    return image, start


def handler_of(start, residue, count):
    device = start + lax.rem(residue - lax.rem(start, SPAN) + SPAN, SPAN)
    return jnp.where(device >= count, device - SPAN, device)


def swap_halves(values):
    half = HEAD_DIM // 2
    zeros = jnp.zeros((values.shape[0], LANES - HEAD_DIM), values.dtype)
    return jnp.concatenate([values[:, half:HEAD_DIM], values[:, :half], zeros], axis=1)


def padded(values):
    zeros = jnp.zeros((values.shape[0], LANES - values.shape[1]), values.dtype)
    return jnp.concatenate([values, zeros], axis=1)


def message_lanes(half, tensor):
    begin = (half * 4 + tensor) * HEAD_DIM
    return slice(begin, begin + HEAD_DIM)


def pack_kernel(shifts, *refs):
    inputs, outs, held, sems = refs[:4], refs[4:-5], refs[-5:-1], refs[-1]
    slots = len(shifts)
    me = lax.axis_index("tok")
    copies = [
        pltpu.make_async_copy(source, target, sems.at[number])
        for number, (source, target) in enumerate(zip(inputs, held))
    ]
    for copy in copies:
        copy.start()
    for copy in copies:
        copy.wait()
    rows = held[0].shape[0] // 2
    for head in range(OWN_HEADS):
        for residue in range(SPAN):
            begin = (residue * OWN_HEADS + head) * HEAD_DIM
            piece = jnp.concatenate(
                [
                    ref[half * rows : (half + 1) * rows, begin : begin + HEAD_DIM]
                    for half in range(2)
                    for ref in held
                ],
                axis=1,
            )
            for slot, shift in enumerate(shifts):

                @pl.when(lax.rem(me + shift + SPAN, SPAN) == residue)
                def _(out=outs[head * slots + slot], piece=piece):
                    out[...] = piece


def angles_kernel(images, tokd, lengths, widths, table, inverse, cos_out, sin_out):
    me = lax.axis_index("tok")
    slots = table.shape[0] + 1
    lane = lax.broadcasted_iota(jnp.int32, (tokd, LANES), 1)
    spot = lax.broadcasted_iota(jnp.int32, (tokd, LANES), 0)
    quarter = HEAD_DIM // 4
    by_row = lax.rem(lane, 2 * quarter) < quarter
    sign = jnp.where(lane < 2 * quarter, -1.0, 1.0)
    keep = jnp.where(lane < HEAD_DIM, 1.0, 0.0)

    def one(slot, carry):
        block = jnp.where(slot == 0, me, table[jnp.maximum(slot - 1, 0), me])
        image, start = image_of(block, lengths, images)
        width = widths[0, image]
        bits = jnp.where(width == tokd, 0, jnp.where(width * 2 == tokd, 1, 2))
        full = tokd.bit_length() - 1
        local = spot + (block - start) * tokd
        shift = full - bits
        rowpos = lax.shift_right_logical(local, jnp.broadcast_to(shift, local.shape))
        colpos = local & (width - 1)
        angle = jnp.where(by_row, rowpos, colpos).astype(jnp.float32) * inverse[0:1, :]
        rows = pl.ds(pl.multiple_of(slot * tokd, tokd), tokd)
        cos_out[rows, :] = jnp.cos(angle) * keep
        sin_out[rows, :] = jnp.sin(angle) * sign
        return carry

    lax.fori_loop(0, slots, one, 0)


def attend_kernel(slots, count, images, tokd, head, factor, lengths, table, cosv, sinv, bias, *refs):
    msgs, refs = refs[:slots], refs[slots:]
    if head > 0:
        before, refs = refs[0], refs[1:]
    outs, sums = refs[:slots], refs[slots]
    q_all, k_all, v_all, dk_acc, dv_acc = refs[slots + 1 :]
    me = lax.axis_index("tok")
    residue = lax.rem(me, SPAN)
    ids = []
    for slot in range(slots):
        block = me if slot == 0 else table[slot - 1, me]
        image, start = image_of(block, lengths, images)
        handled = (block >= 0) & (handler_of(start, residue, count) == me)
        ids.append(jnp.where(handled, image, -1 - slot))
    own_bias = jnp.zeros((3, HEAD_DIM), jnp.float32)
    for number in range(SPAN):
        begin = (number * OWN_HEADS + head) * HEAD_DIM
        piece = bias[:, begin : begin + HEAD_DIM].astype(jnp.float32)
        own_bias = jnp.where(residue == number, piece, own_bias)
    own_bias = padded(own_bias)
    transposed = (((1,), (1,)), ((), ()))
    part = tokd // 2
    lane = lax.broadcasted_iota(jnp.int32, (1, LANES), 1)
    ones = jnp.where((lane == HEAD_DIM) | (lane == HEAD_DIM + 1), 1.0, 0.0)

    def block_rows(slot):
        return slice(slot * tokd, (slot + 1) * tokd)

    for slot in range(slots):
        for half in range(2):
            begin = slot * tokd + half * part
            rows = slice(begin, begin + part)
            cos_b, sin_b = cosv[rows, :], sinv[rows, :]
            for tensor, store in ((0, q_all), (1, k_all)):
                plain = msgs[slot][:, message_lanes(half, tensor)].astype(jnp.float32)
                plain = padded(plain) + own_bias[tensor : tensor + 1, :]
                turned = plain * cos_b + swap_halves(plain) * sin_b
                store[rows, :] = turned.astype(jnp.bfloat16)
            plain = msgs[slot][:, message_lanes(half, 2)].astype(jnp.float32)
            plain = padded(plain) + own_bias[2:3, :] + ones
            v_all[rows, :] = plain.astype(jnp.bfloat16)
    dq_total = jnp.zeros((1, LANES), jnp.float32)
    for slot in range(slots):
        rows = block_rows(slot)
        query_b = q_all[rows, :]
        scores = lax.dot_general(
            query_b, k_all[...], transposed, preferred_element_type=jnp.float32
        )
        offs = [jnp.where(ids[slot] == ids[other], 0.0, NEG) for other in range(slots)]
        tops = [
            jnp.max(scores[:, block_rows(other)], axis=1, keepdims=True) + offs[other]
            for other in range(slots)
        ]
        top = functools.reduce(jnp.maximum, tops)
        expo_b = jnp.concatenate(
            [
                jnp.exp2(
                    (scores[:, block_rows(other)] - (top - offs[other])) * (SCALE * LOG2E)
                ).astype(jnp.bfloat16)
                for other in range(slots)
            ],
            axis=1,
        )
        mixed = jnp.dot(expo_b, v_all[...], preferred_element_type=jnp.float32)
        inv = 1.0 / mixed[:, HEAD_DIM : HEAD_DIM + 1]
        out_b = (mixed * inv).astype(jnp.bfloat16)
        grad = jnp.concatenate(
            [msgs[slot][:, message_lanes(half, 3)] for half in range(2)], axis=0
        ).astype(jnp.float32)
        grad = padded(grad)
        delta = jnp.sum(grad * out_b.astype(jnp.float32), axis=1, keepdims=True) * inv
        coarse = delta.astype(jnp.bfloat16).astype(jnp.float32)
        grad_b = jnp.where(
            lane == HEAD_DIM,
            -coarse,
            jnp.where(lane == HEAD_DIM + 1, coarse - delta, grad * inv),
        ).astype(jnp.bfloat16)
        dprobs = lax.dot_general(
            grad_b, v_all[...], transposed, preferred_element_type=jnp.float32
        )
        dscore_b = (expo_b.astype(jnp.float32) * dprobs).astype(jnp.bfloat16)
        dquery = jnp.dot(dscore_b, k_all[...], preferred_element_type=jnp.float32) * SCALE
        part_k = jnp.dot(query_b.T, dscore_b, preferred_element_type=jnp.float32)
        part_v = jnp.dot(grad_b.T, expo_b, preferred_element_type=jnp.float32)
        if slot == 0:
            dk_acc[...] = part_k
            dv_acc[...] = part_v
        else:
            dk_acc[...] += part_k
            dv_acc[...] += part_v
        dquery = dquery * cosv[rows, :] - swap_halves(dquery) * sinv[rows, :]
        dq_total = dq_total + jnp.where(
            ids[slot] >= 0, jnp.sum(dquery, axis=0, keepdims=True), 0.0
        )
        dquery_b = dquery.astype(jnp.bfloat16)
        for half in range(2):
            inner = slice(half * part, (half + 1) * part)
            outs[slot][:, message_lanes(half, 0)] = out_b[inner, :HEAD_DIM]
            outs[slot][:, message_lanes(half, 1)] = dquery_b[inner, :HEAD_DIM]
    dk_total = jnp.zeros((1, LANES), jnp.float32)
    dv_total = jnp.zeros((1, LANES), jnp.float32)
    for slot in range(slots):
        rows = block_rows(slot)
        dkey = dk_acc[:, rows].T * SCALE
        dkey = dkey * cosv[rows, :] - swap_halves(dkey) * sinv[rows, :]
        dvalue = dv_acc[:, rows].T
        dkey_b, dvalue_b = dkey.astype(jnp.bfloat16), dvalue.astype(jnp.bfloat16)
        for half in range(2):
            inner = slice(half * part, (half + 1) * part)
            outs[slot][:, message_lanes(half, 2)] = dkey_b[inner, :HEAD_DIM]
            outs[slot][:, message_lanes(half, 3)] = dvalue_b[inner, :HEAD_DIM]
        live = ids[slot] >= 0
        dk_total = dk_total + jnp.where(live, jnp.sum(dkey, axis=0, keepdims=True), 0.0)
        dv_total = dv_total + jnp.where(live, jnp.sum(dvalue, axis=0, keepdims=True), 0.0)
    sums[...] = jnp.zeros_like(sums) if head == 0 else before[...]
    for number in range(SPAN):
        begin = (number * OWN_HEADS + head) * HEAD_DIM

        @pl.when(residue == number)
        def _(begin=begin):
            for at, total in enumerate((dq_total, dk_total, dv_total)):
                sums[at : at + 1, begin : begin + HEAD_DIM] = total[:, :HEAD_DIM] * factor


def unpack_kernel(slots, count, images, lengths, table, *refs):
    msgs, outs = refs[: OWN_HEADS * slots], refs[OWN_HEADS * slots :]
    me = lax.axis_index("tok")
    _, start = image_of(me, lengths, images)
    part = outs[0].shape[0] // 2
    for residue in range(SPAN):
        handler = handler_of(start, residue, count)
        for slot in range(slots):
            source = me if slot == 0 else table[slot - 1, me]

            @pl.when(source == handler)
            def _(slot=slot, residue=residue):
                for number, out in enumerate(outs):
                    for half in range(2):
                        lanes = message_lanes(half, number)
                        piece = jnp.concatenate(
                            [msgs[head * slots + slot][:, lanes] for head in range(OWN_HEADS)],
                            axis=1,
                        )
                        out[half * part : (half + 1) * part, residue * PART : (residue + 1) * PART] = piece


def sum_over(value, axis):
    size = lax.axis_size(axis)
    if size & (size - 1):
        return lax.psum(value, axis)
    step = 1
    while step < size:
        value = value + lax.ppermute(value, axis, [(one, one ^ step) for one in range(size)])
        step *= 2
    return value


def on_device(query_in, key_in, value_in, out_grad, bias, lengths, widths):
    tokd = query_in.shape[1]
    model = query_in.shape[2]
    images = lengths.shape[1]
    count = lax.axis_size("tok")
    rounds = trade_rounds(count)
    shifts = [0] + [shift for shift, _ in rounds]
    slots = len(shifts)
    table = jnp.asarray(source_table(rounds, count))
    quarter = HEAD_DIM // 4
    inverse = rope_base ** (-np.arange(quarter, dtype=np.float64) / quarter)
    inverse = np.concatenate([np.tile(inverse, 4), np.zeros(LANES - HEAD_DIM)])
    inverse = jnp.asarray(inverse[None], jnp.float32)
    smem = pl.BlockSpec(memory_space=pltpu.SMEM)
    vmem = pl.BlockSpec(memory_space=pltpu.VMEM)
    hbm = pl.BlockSpec(memory_space=pltpu.HBM)
    whole = jax.ShapeDtypeStruct((tokd, model), jnp.bfloat16)
    message = jax.ShapeDtypeStruct((tokd // 2, model), jnp.bfloat16)
    sums_shape = jax.ShapeDtypeStruct((8, model), jnp.float32)
    tokens_all = lax.axis_size("dp") * count * tokd

    def params(mib):
        return pltpu.CompilerParams(vmem_limit_bytes=mib * 1024 * 1024)

    sends = pl.pallas_call(
        functools.partial(pack_kernel, shifts),
        out_shape=[message] * (OWN_HEADS * slots),
        in_specs=[hbm] * 4,
        out_specs=[vmem] * (OWN_HEADS * slots),
        scratch_shapes=[pltpu.VMEM((tokd, model), jnp.bfloat16)] * 4
        + [pltpu.SemaphoreType.DMA((4,))],
        compiler_params=params(16),
        name="pack_heads",
    )(query_in[0], key_in[0], value_in[0], out_grad[0])
    got = []
    for head in range(OWN_HEADS):
        mine = sends[head * slots : (head + 1) * slots]
        got.append(
            [mine[0]]
            + [lax.ppermute(send, "tok", pairs) for send, (_, pairs) in zip(mine[1:], rounds)]
        )
    span = slots * tokd
    table_shape = jax.ShapeDtypeStruct((span, LANES), jnp.float32)
    cosv, sinv = pl.pallas_call(
        functools.partial(angles_kernel, images, tokd),
        out_shape=[table_shape] * 2,
        in_specs=[smem, smem, smem, vmem],
        out_specs=[vmem] * 2,
        compiler_params=params(16),
        cost_estimate=pl.CostEstimate(
            flops=span * LANES * 200, bytes_accessed=0, transcendentals=0
        ),
        name="rotary_angles",
    )(lengths, widths, table, inverse)
    back = []
    sums = None
    for head in range(OWN_HEADS):
        operands = [lengths, table, cosv, sinv, bias] + got[head]
        if head > 0:
            operands.append(sums)
        results = pl.pallas_call(
            functools.partial(
                attend_kernel, slots, count, images, tokd, head, 1.0 / tokens_all**0.5
            ),
            out_shape=[message] * slots + [sums_shape],
            in_specs=[smem, smem] + [vmem] * (len(operands) - 2),
            out_specs=[vmem] * (slots + 1),
            scratch_shapes=[pltpu.VMEM((span, LANES), jnp.bfloat16)] * 3
            + [pltpu.VMEM((LANES, span), jnp.float32)] * 2,
            compiler_params=params(32),
            cost_estimate=pl.CostEstimate(
                flops=12 * span * span * 256, bytes_accessed=0, transcendentals=0
            ),
            name="attend_head",
        )(*operands)
        sums = results[slots]
        back.append(results[0])
        back += [
            lax.ppermute(result, "tok", [(target, source) for source, target in pairs])
            for result, (_, pairs) in zip(results[1:slots], rounds)
        ]
    sums = sum_over(sum_over(sums, "dp"), "tok")
    outs = pl.pallas_call(
        functools.partial(unpack_kernel, slots, count, images),
        out_shape=[whole] * 4,
        in_specs=[smem, smem] + [vmem] * (OWN_HEADS * slots),
        out_specs=[vmem] * 4,
        compiler_params=params(16),
        name="unpack_heads",
    )(lengths, jnp.asarray(target_table(rounds, count)), *back)
    return tuple(out[None] for out in outs) + (sums[:3],)


def solution(mesh):
    in_specs = (
        P("dp", "tok", None),
        P("dp", "tok", None),
        P("dp", "tok", None),
        P("dp", "tok", None),
        P(),
        P("dp", None),
        P("dp", None),
    )
    out_specs = (
        P("dp", "tok", None),
        P("dp", "tok", None),
        P("dp", "tok", None),
        P("dp", "tok", None),
        P(),
    )
    return jax.shard_map(
        on_device, mesh=mesh, in_specs=in_specs, out_specs=out_specs, check_vma=False
    )
```

time: 124 us -> 74.7 us (0.60)
  blocking collectives: 74.8 us -> 0 us
  starting transfers between devices: 9.8 us -> 22 us
  waiting for transfers between devices: 10.1 us -> 20.1 us
  Pallas kernels: 23.9 us -> 27.1 us
    all_gather x1 -> x0, blocking collectives: 74.8 us -> none  [on_device(): every = lax.all_gather(sums, ('dp', 'tok'))]
    ppermute x0 -> x5, waiting for transfers between devices: none -> 9.42 us  [sum_over(): lax.ppermute(value, axis, [(one, one ^ step) for one in range(size)])]
    ppermute x3 -> x6, waiting for transfers between devices: 0.01 us -> 7.98 us  [on_device(): lax.ppermute(result, 'tok', [(target, source) for source, target in pairs])]
    ppermute x3 -> x6, waiting for transfers between devices: 10.1 us -> 2.73 us  [on_device(): lax.ppermute(send, 'tok', pairs)]
    ppermute x0 -> x5, starting transfers between devices: none -> 5.87 us  [sum_over(): lax.ppermute(value, axis, [(one, one ^ step) for one in range(size)])]
    ppermute x3 -> x6, starting transfers between devices: 6.01 us -> 9.79 us  [on_device(): lax.ppermute(send, 'tok', pairs)]
    ppermute x3 -> x6, starting transfers between devices: 3.79 us -> 6.3 us  [on_device(): lax.ppermute(result, 'tok', [(target, source) for source, target in pairs])]
    pallas_call x1, Pallas kernels: 2.41 us -> 4.03 us  [on_device(): pl.pallas_call(functools.partial(unpack_kernel, slots, count, images), ou...]
  transfers between devices with their start and end apart: 6 -> 17, of which waited for: 3 -> 8; matrix products, arithmetic and copies ran while one was open for 1% -> 1% of each run, Pallas kernels for 2% -> 29%
where the time goes in v2:
time: 74.7 us; the launch traced here: 74.4 us
  Pallas kernels  27.1 us (36%)
  starting transfers between devices  22 us (29%)
  waiting for transfers between devices  20.1 us (27%)
  local copies, waits for them, and re-layouts  3.91 us (5%)
    pallas_call x2, Pallas kernels, on_device(): pl.pallas_call(functools.partial(attend_kernel, slots, count, images, tok...  18.6 us
    ppermute x6, starting transfers between devices, on_device(): lax.ppermute(send, 'tok', pairs)  9.79 us
    ppermute x5, waiting for transfers between devices, sum_over(): lax.ppermute(value, axis, [(one, one ^ step) for one in range(size)])  9.42 us
    ppermute x6, waiting for transfers between devices, on_device(): lax.ppermute(result, 'tok', [(target, source) for source, target in pairs])  7.98 us
    ppermute x6, starting transfers between devices, on_device(): lax.ppermute(result, 'tok', [(target, source) for source, target in pairs])  6.3 us
    ppermute x5, starting transfers between devices, sum_over(): lax.ppermute(value, axis, [(one, one ^ step) for one in range(size)])  5.87 us
    pallas_call x1, Pallas kernels, on_device(): pl.pallas_call(functools.partial(unpack_kernel, slots, count, images), ou...  4.03 us
    unnamed x20, local copies, waits for them, and re-layouts  3.91 us
  transfers between devices with their start and end apart: 17, of which 8 were waited for; matrix products, arithmetic and copies ran while one was open for 1% of the time, Pallas kernels for 29%

profile of v2, /device:TPU:0, one launch (start us, length us, event | category | flops | bytes accessed | tf_op | source)
XLA Modules:
  0.0 74.4 jit_solution(13848714028857884377)
XLA Ops:
  0.6 0.0 copy-start
  0.6 1.0 %copy-done = bf16[1,256,640]{2,1,0:T(8,128)(2,1)S(1)} copy-done((bf16[1,256,640]{2,1,0:T(8,128)(2,1)S(1)}, bf16[1,256,640]{2,1,0:T(8,128)(2,1)}, u32[]{:S(2)}) %copy-start) | copy-done | bytes 327704
  1.6 1.0 %copy-done.1 = bf16[1,256,640]{2,1,0:T(8,128)(2,1)S(1)} copy-done((bf16[1,256,640]{2,1,0:T(8,128)(2,1)S(1)}, bf16[1,256,640]{2,1,0:T(8,128)(2,1)}, u32[]{:S(2)}) %copy-start.1) | copy-done | bytes 327704
  2.6 1.0 %copy-done.2 = bf16[1,256,640]{2,1,0:T(8,128)(2,1)S(1)} copy-done((bf16[1,256,640]{2,1,0:T(8,128)(2,1)S(1)}, bf16[1,256,640]{2,1,0:T(8,128)(2,1)}, u32[]{:S(2)}) %copy-start.2) | copy-done | bytes 327704
  3.6 1.0 %copy-done.3 = bf16[1,256,640]{2,1,0:T(8,128)(2,1)S(1)} copy-done((bf16[1,256,640]{2,1,0:T(8,128)(2,1)S(1)}, bf16[1,256,640]{2,1,0:T(8,128)(2,1)}, u32[]{:S(2)}) %copy-start.3) | copy-done | bytes 327704
  4.5 1.8 %pack_heads.1 = (bf16[128,640]{1,0:T(8,128)(2,1)S(1)}, bf16[128,640]{1,0:T(8,128)(2,1)S(1)}, bf16[128,640]{1,0:T(8,128)(2,1)S(1)}, bf16[128,640]{1,0:T(8,128)(2,...) custom-call(bf16[256,640]{1,0:T(8,128)(2,1)S(1)} %bitcast.8, ...), custom_call_target="tpu_custom_call" | custom-call | tf_op jit(solution)/shard_map/pack_heads/pallas_call | solution.py:336
  6.3 3.0 %collective-permute-start = (bf16[128,640]{1,0:T(8,128)(2,1)S(1)}, bf16[128,640]{1,0:T(8,128)(2,1)S(1)}, u32[]{:S(2)}, u32[]{:S(2)}) collective-permute-start(bf16[128,640]{1,0:T(8,128)(2,1)S(1)} %get-tuple-element.32), channel_id=1, source_target_pairs={{0,1},{1,2},{2,3},{4,5},{5,6},{6,7},{3,0},{7,4},{8,9},{9,10},{10,1... | collective-permute-start | bytes 491528 | tf_op jit(solution)/shard_map/ppermute | solution.py:351
  9.3 1.6 %collective-permute-start.1 = (bf16[128,640]{1,0:T(8,128)(2,1)S(1)}, bf16[128,640]{1,0:T(8,128)(2,1)S(1)}, u32[]{:S(2)}, u32[]{:S(2)}) collective-permute-start(bf16[128,640]{1,0:T(8,128)(2,1)S(1)} %get-tuple-element.33), channel_id=1, source_target_pairs={{0,2},{1,3},{4,6},{5,7},{2,0},{3,1},{6,4},{7,5},{8,10},{9,11},{12,... | collective-permute-start | bytes 491528 | tf_op jit(solution)/shard_map/ppermute | solution.py:351
  10.9 1.4 %collective-permute-start.2 = (bf16[128,640]{1,0:T(8,128)(2,1)S(1)}, bf16[128,640]{1,0:T(8,128)(2,1)S(1)}, u32[]{:S(2)}, u32[]{:S(2)}) collective-permute-start(bf16[128,640]{1,0:T(8,128)(2,1)S(1)} %get-tuple-element.34), channel_id=1, source_target_pairs={{0,3},{4,7},{1,0},{2,1},{3,2},{5,4},{6,5},{7,6},{8,11},{12,15},{9,... | collective-permute-start | bytes 491528 | tf_op jit(solution)/shard_map/ppermute | solution.py:351
  12.4 0.6 collective-permute-start.6
  13.0 0.5 collective-permute-start.7
  13.4 0.0 copy-done.7
  13.4 2.7 %rotary_angles.1 = (f32[1024,128]{1,0:T(8,128)S(1)}, f32[1024,128]{1,0:T(8,128)S(1)}) custom-call(s32[1,4]{1,0:T(1,128)S(1)} %copy-done.5, s32[1,4]{1,0:T(1,128)S(1)} %copy-done.7, s32[3,8]{1,0:T(4,128)S(1)} %copy-done.8, f32[1,128]{1,0:T(1,128)S(1)} %copy-done.9), custom_call_target="tpu_custom_call" | custom-call | flops 26214400 | tf_op jit(solution)/shard_map/rotary_angles/pallas_call | solution.py:355
  16.1 0.0 copy-start.6
  16.1 0.0 collective-permute-done.refs_1_
  16.1 2.7 %collective-permute-start.8 = (bf16[128,640]{1,0:T(8,128)(2,1)S(1)}, bf16[128,640]{1,0:T(8,128)(2,1)S(1)}, u32[]{:S(2)}, u32[]{:S(2)}) collective-permute-start(bf16[128,640]{1,0:T(8,128)(2,1)S(1)} %get-tuple-element.42), channel_id=1, source_target_pairs={{0,3},{4,7},{1,0},{2,1},{3,2},{5,4},{6,5},{7,6},{8,11},{12,15},{9,... | collective-permute-start | bytes 491528 | tf_op jit(solution)/shard_map/ppermute | solution.py:351
  18.9 0.0 collective-permute-done.1.refs_2_
  18.9 2.7 %collective-permute-done.2.refs_3_ = bf16[128,640]{1,0:T(8,128)(2,1)S(1)} collective-permute-done((bf16[128,640]{1,0:T(8,128)(2,1)S(1)}, bf16[128,640]{1,0:T(8,128)(2,1)S(1)}, u32[]{:S(2)}, u32[]{:S(2)}) %collective-permute-start.2) | collective-permute-done | bytes 163872 | tf_op jit(solution)/shard_map/ppermute | solution.py:351
  21.6 0.0 copy-done.6
  21.6 9.3 %attend_head.2 = (bf16[128,640]{1,0:T(8,128)(2,1)S(1)}, bf16[128,640]{1,0:T(8,128)(2,1)S(1)}, bf16[128,640]{1,0:T(8,128)(2,1)S(1)}, bf16[128,640]{1,0:T(8,128)(2,1)S(1)}, f32[8,640]{1,0:T(8,128)S(1)}) custom-call(s32[1,4]{1,0:T(1,128)S(1)} %copy-done.5, s32[3,8]{1,0:T(4,128)S(1)} %copy-done.8, f32[1024,128]{1,0:T(8,128)S(1)} %get-tuple-element.29.cosv, ...), custom_call_target="tpu_custom_call" | custom-call | flops 3221225472 | tf_op jit(solution)/shard_map/attend_head/pallas_call | solution.py:372
  30.9 1.1 %collective-permute-start.3 = (bf16[128,640]{1,0:T(8,128)(2,1)S(1)}, bf16[128,640]{1,0:T(8,128)(2,1)S(1)}, u32[]{:S(2)}, u32[]{:S(2)}) collective-permute-start(bf16[128,640]{1,0:T(8,128)(2,1)S(1)} %get-tuple-element.36), channel_id=1, source_target_pairs={{1,0},{2,1},{3,2},{5,4},{6,5},{7,6},{0,3},{4,7},{9,8},{10,9},{11,1... | collective-permute-start | bytes 491528 | tf_op jit(solution)/shard_map/ppermute | solution.py:390
  32.0 0.0 collective-permute-done.6.refs_1_
  32.0 0.0 collective-permute-done.7.refs_2_
  32.0 0.0 collective-permute-done.8.refs_3_
  32.0 9.3 %attend_head.3 = (bf16[128,640]{1,0:T(8,128)(2,1)S(1)}, bf16[128,640]{1,0:T(8,128)(2,1)S(1)}, bf16[128,640]{1,0:T(8,128)(2,1)S(1)}, bf16[128,640]{1,0:T(8,128)(2,1)S(1)}, f32[8,640]{1,0:T(8,128)S(1)}) custom-call(s32[1,4]{1,0:T(1,128)S(1)} %copy-done.5, s32[3,8]{1,0:T(4,128)S(1)} %copy-done.8, f32[1024,128]{1,0:T(8,128)S(1)} %get-tuple-element.29.cosv, ...), custom_call_target="tpu_custom_call" | custom-call | flops 3221225472 | tf_op jit(solution)/shard_map/attend_head/pallas_call | solution.py:372
  41.3 0.0 collective-permute-start.12
  41.3 1.2 %collective-permute-done.12 = f32[8,640]{1,0:T(8,128)S(1)} collective-permute-done((f32[8,640]{1,0:T(8,128)S(1)}, f32[8,640]{1,0:T(8,128)S(1)}, u32[]{:S(2)}, u32[]{:S(2)}) %collective-permute-start.12) | collective-permute-done | bytes 20512 | tf_op jit(solution)/shard_map/ppermute | solution.py:307
  42.5 1.5 %collective-permute-start.13 = (f32[8,640]{1,0:T(8,128)S(1)}, f32[8,640]{1,0:T(8,128)S(1)}, u32[]{:S(2)}, u32[]{:S(2)}) collective-permute-start(f32[8,640]{1,0:T(8,128)S(1)} %add.15), channel_id=1, source_target_pairs={{0,16},{8,24},{16,0},{24,8},{1,17},{9,25},{17,1},{25,9},{2,18},{10... | collective-permute-start | bytes 61448 | tf_op jit(solution)/shard_map/ppermute | solution.py:307
  44.0 2.3 %collective-permute-done.13 = f32[8,640]{1,0:T(8,128)S(1)} collective-permute-done((f32[8,640]{1,0:T(8,128)S(1)}, f32[8,640]{1,0:T(8,128)S(1)}, u32[]{:S(2)}, u32[]{:S(2)}) %collective-permute-start.13) | collective-permute-done | bytes 20512 | tf_op jit(solution)/shard_map/ppermute | solution.py:307
  46.3 1.2 %collective-permute-start.14 = (f32[8,640]{1,0:T(8,128)S(1)}, f32[8,640]{1,0:T(8,128)S(1)}, u32[]{:S(2)}, u32[]{:S(2)}) collective-permute-start(f32[8,640]{1,0:T(8,128)S(1)} %add.16), channel_id=1, source_target_pairs={{0,1},{1,0},{2,3},{3,2},{4,5},{5,4},{6,7},{7,6},{8,9},{9,8},{10,11... | collective-permute-start | bytes 61448 | tf_op jit(solution)/shard_map/ppermute | solution.py:307
  47.4 2.6 %collective-permute-done.14 = f32[8,640]{1,0:T(8,128)S(1)} collective-permute-done((f32[8,640]{1,0:T(8,128)S(1)}, f32[8,640]{1,0:T(8,128)S(1)}, u32[]{:S(2)}, u32[]{:S(2)}) %collective-permute-start.14) | collective-permute-done | bytes 20512 | tf_op jit(solution)/shard_map/ppermute | solution.py:307
  50.1 0.4 collective-permute-start.15
  50.5 3.3 %collective-permute-done.15 = f32[8,640]{1,0:T(8,128)S(1)} collective-permute-done((f32[8,640]{1,0:T(8,128)S(1)}, f32[8,640]{1,0:T(8,128)S(1)}, u32[]{:S(2)}, u32[]{:S(2)}) %collective-permute-start.15) | collective-permute-done | bytes 20512 | tf_op jit(solution)/shard_map/ppermute | solution.py:307
  53.9 2.7 %collective-permute-start.16 = (f32[8,640]{1,0:T(8,128)S(1)}, f32[8,640]{1,0:T(8,128)S(1)}, u32[]{:S(2)}, u32[]{:S(2)}) collective-permute-start(f32[8,640]{1,0:T(8,128)S(1)} %add.18), channel_id=1, source_target_pairs={{0,4},{1,5},{2,6},{3,7},{4,0},{5,1},{6,2},{7,3},{8,12},{9,13},{10,... | collective-permute-start | bytes 61448 | tf_op jit(solution)/shard_map/ppermute | solution.py:307
  56.6 0.5 collective-permute-start.4
  57.0 0.8 %collective-permute-start.5 = (bf16[128,640]{1,0:T(8,128)(2,1)S(1)}, bf16[128,640]{1,0:T(8,128)(2,1)S(1)}, u32[]{:S(2)}, u32[]{:S(2)}) collective-permute-start(bf16[128,640]{1,0:T(8,128)(2,1)S(1)} %get-tuple-element.38), channel_id=1, source_target_pairs={{3,0},{7,4},{0,1},{1,2},{2,3},{4,5},{5,6},{6,7},{11,8},{15,12},{8,... | collective-permute-start | bytes 491528 | tf_op jit(solution)/shard_map/ppermute | solution.py:390
  57.8 2.1 %collective-permute-start.9 = (bf16[128,640]{1,0:T(8,128)(2,1)S(1)}, bf16[128,640]{1,0:T(8,128)(2,1)S(1)}, u32[]{:S(2)}, u32[]{:S(2)}) collective-permute-start(bf16[128,640]{1,0:T(8,128)(2,1)S(1)} %get-tuple-element.45), channel_id=1, source_target_pairs={{1,0},{2,1},{3,2},{5,4},{6,5},{7,6},{0,3},{4,7},{9,8},{10,9},{11,1... | collective-permute-start | bytes 491528 | tf_op jit(solution)/shard_map/ppermute | solution.py:390
  60.0 0.0 collective-permute-done.16
  60.0 1.6 %collective-permute-start.10 = (bf16[128,640]{1,0:T(8,128)(2,1)S(1)}, bf16[128,640]{1,0:T(8,128)(2,1)S(1)}, u32[]{:S(2)}, u32[]{:S(2)}) collective-permute-start(bf16[128,640]{1,0:T(8,128)(2,1)S(1)} %get-tuple-element.46), channel_id=1, source_target_pairs={{2,0},{3,1},{6,4},{7,5},{0,2},{1,3},{4,6},{5,7},{10,8},{11,9},{14,... | collective-permute-start | bytes 491528 | tf_op jit(solution)/shard_map/ppermute | solution.py:390
  61.5 0.0 collective-permute-done.3.refs_1_
  61.5 0.2 collective-permute-start.11
  61.8 0.6 slice_add_fusion
  62.4 0.9 %collective-permute-done.4.refs_2_ = bf16[128,640]{1,0:T(8,128)(2,1)S(1)} collective-permute-done((bf16[128,640]{1,0:T(8,128)(2,1)S(1)}, bf16[128,640]{1,0:T(8,128)(2,1)S(1)}, u32[]{:S(2)}, u32[]{:S(2)}) %collective-permute-start.4) | collective-permute-done | bytes 163872 | tf_op jit(solution)/shard_map/ppermute | solution.py:390
  63.3 3.5 %collective-permute-done.5.refs_3_ = bf16[128,640]{1,0:T(8,128)(2,1)S(1)} collective-permute-done((bf16[128,640]{1,0:T(8,128)(2,1)S(1)}, bf16[128,640]{1,0:T(8,128)(2,1)S(1)}, u32[]{:S(2)}, u32[]{:S(2)}) %collective-permute-start.5) | collective-permute-done | bytes 163872 | tf_op jit(solution)/shard_map/ppermute | solution.py:390
  66.9 0.0 collective-permute-done.9.refs_5_
  66.9 0.0 collective-permute-done.10.refs_6_
  66.9 3.5 %collective-permute-done.11.refs_7_ = bf16[128,640]{1,0:T(8,128)(2,1)S(1)} collective-permute-done((bf16[128,640]{1,0:T(8,128)(2,1)S(1)}, bf16[128,640]{1,0:T(8,128)(2,1)S(1)}, u32[]{:S(2)}, u32[]{:S(2)}) %collective-permute-start.11) | collective-permute-done | bytes 163872 | tf_op jit(solution)/shard_map/ppermute | solution.py:390
  70.4 4.0 %unpack_heads.1 = (bf16[256,640]{1,0:T(8,128)(2,1)}, bf16[256,640]{1,0:T(8,128)(2,1)}, bf16[256,640]{1,0:T(8,128)(2,1)}, bf16[256,640]{1,0:T(8,128)(2,1)}) custom-call(s32[1,4]{1,0:T(1,128)S(1)} %copy-done.5, s32[3,8]{1,0:T(4,128)S(1)} %copy-done.4, bf16[128,640]{1,0:T(8,128)(2,1)S(1)} %get-tuple-element.35.refs_0_, ...), custom_call_target="tpu_custom_call" | custom-call | tf_op jit(solution)/shard_map/unpack_heads/pallas_call | solution.py:394
  (16 shorter events, 0.0 us)
Async XLA Ops:
  0.6 1.0 %copy-start = (bf16[1,256,640]{2,1,0:T(8,128)(2,1)S(1)}, bf16[1,256,640]{2,1,0:T(8,128)(2,1)}, u32[]{:S(2)}) copy-start(bf16[1,256,640]{2,1,0:T(8,128)(2,1)} %param.10) | copy-start | bytes 983044
  1.6 1.0 %copy-start.1 = (bf16[1,256,640]{2,1,0:T(8,128)(2,1)S(1)}, bf16[1,256,640]{2,1,0:T(8,128)(2,1)}, u32[]{:S(2)}) copy-start(bf16[1,256,640]{2,1,0:T(8,128)(2,1)} %param.11) | copy-start | bytes 983044
  2.6 1.0 %copy-start.2 = (bf16[1,256,640]{2,1,0:T(8,128)(2,1)S(1)}, bf16[1,256,640]{2,1,0:T(8,128)(2,1)}, u32[]{:S(2)}) copy-start(bf16[1,256,640]{2,1,0:T(8,128)(2,1)} %param.12) | copy-start | bytes 983044
  3.6 1.0 %copy-start.3 = (bf16[1,256,640]{2,1,0:T(8,128)(2,1)S(1)}, bf16[1,256,640]{2,1,0:T(8,128)(2,1)}, u32[]{:S(2)}) copy-start(bf16[1,256,640]{2,1,0:T(8,128)(2,1)} %param.13) | copy-start | bytes 983044
  6.3 9.8 %collective-permute-start = (bf16[128,640]{1,0:T(8,128)(2,1)S(1)}, bf16[128,640]{1,0:T(8,128)(2,1)S(1)}, u32[]{:S(2)}, u32[]{:S(2)}) collective-permute-start(bf16[128,640]{1,0:T(8,128)(2,1)S(1)} %get-tuple-element.32), channel_id=1, source_target_pairs={{0,1},{1,2},{2,3},{4,5},{5,6},{6,7},{3,0},{7,4},{8,9},{9,10},{10,1... | collective-permute-start | bytes 491528 | tf_op jit(solution)/shard_map/ppermute | solution.py:351
  9.3 9.5 %collective-permute-start.1 = (bf16[128,640]{1,0:T(8,128)(2,1)S(1)}, bf16[128,640]{1,0:T(8,128)(2,1)S(1)}, u32[]{:S(2)}, u32[]{:S(2)}) collective-permute-start(bf16[128,640]{1,0:T(8,128)(2,1)S(1)} %get-tuple-element.33), channel_id=1, source_target_pairs={{0,2},{1,3},{4,6},{5,7},{2,0},{3,1},{6,4},{7,5},{8,10},{9,11},{12,... | collective-permute-start | bytes 491528 | tf_op jit(solution)/shard_map/ppermute | solution.py:351
  10.9 2.5 %copy-start.8 = (s32[3,8]{1,0:T(4,128)S(1)}, s32[3,8]{1,0:T(4,128)}, u32[]{:S(2)}) copy-start(s32[3,8]{1,0:T(4,128)} %constant.6.clone.table) | copy-start | bytes 292
  10.9 10.7 %collective-permute-start.2 = (bf16[128,640]{1,0:T(8,128)(2,1)S(1)}, bf16[128,640]{1,0:T(8,128)(2,1)S(1)}, u32[]{:S(2)}, u32[]{:S(2)}) collective-permute-start(bf16[128,640]{1,0:T(8,128)(2,1)S(1)} %get-tuple-element.34), channel_id=1, source_target_pairs={{0,3},{4,7},{1,0},{2,1},{3,2},{5,4},{6,5},{7,6},{8,11},{12,15},{9,... | collective-permute-start | bytes 491528 | tf_op jit(solution)/shard_map/ppermute | solution.py:351
  12.4 1.1 %copy-start.5 = (s32[1,4]{1,0:T(1,128)S(1)}, s32[1,4]{1,0:T(1,128)}, u32[]{:S(2)}) copy-start(s32[1,4]{1,0:T(1,128)} %lengths.7) | copy-start | bytes 52
  12.4 1.1 %copy-start.7 = (s32[1,4]{1,0:T(1,128)S(1)}, s32[1,4]{1,0:T(1,128)}, u32[]{:S(2)}) copy-start(s32[1,4]{1,0:T(1,128)} %widths.1) | copy-start | bytes 52
  12.4 1.1 %copy-start.9 = (f32[1,128]{1,0:T(1,128)S(1)}, f32[1,128]{1,0:T(1,128)}, u32[]{:S(2)}) copy-start(f32[1,128]{1,0:T(1,128)} %constant.7.clone.inverse) | copy-start | bytes 1540
  12.4 19.6 %collective-permute-start.6 = (bf16[128,640]{1,0:T(8,128)(2,1)S(1)}, bf16[128,640]{1,0:T(8,128)(2,1)S(1)}, u32[]{:S(2)}, u32[]{:S(2)}) collective-permute-start(bf16[128,640]{1,0:T(8,128)(2,1)S(1)} %get-tuple-element.40), channel_id=1, source_target_pairs={{0,1},{1,2},{2,3},{4,5},{5,6},{6,7},{3,0},{7,4},{8,9},{9,10},{10,1... | collective-permute-start | bytes 491528 | tf_op jit(solution)/shard_map/ppermute | solution.py:351
  13.0 19.0 %collective-permute-start.7 = (bf16[128,640]{1,0:T(8,128)(2,1)S(1)}, bf16[128,640]{1,0:T(8,128)(2,1)S(1)}, u32[]{:S(2)}, u32[]{:S(2)}) collective-permute-start(bf16[128,640]{1,0:T(8,128)(2,1)S(1)} %get-tuple-element.41), channel_id=1, source_target_pairs={{0,2},{1,3},{4,6},{5,7},{2,0},{3,1},{6,4},{7,5},{8,10},{9,11},{12,... | collective-permute-start | bytes 491528 | tf_op jit(solution)/shard_map/ppermute | solution.py:351
  16.1 5.5 %copy-start.6 = (bf16[3,640]{1,0:T(4,128)(2,1)S(1)}, bf16[3,640]{1,0:T(4,128)(2,1)}, u32[]{:S(2)}) copy-start(bf16[3,640]{1,0:T(4,128)(2,1)} %bias.3) | copy-start | bytes 11524
  16.1 15.9 %collective-permute-start.8 = (bf16[128,640]{1,0:T(8,128)(2,1)S(1)}, bf16[128,640]{1,0:T(8,128)(2,1)S(1)}, u32[]{:S(2)}, u32[]{:S(2)}) collective-permute-start(bf16[128,640]{1,0:T(8,128)(2,1)S(1)} %get-tuple-element.42), channel_id=1, source_target_pairs={{0,3},{4,7},{1,0},{2,1},{3,2},{5,4},{6,5},{7,6},{8,11},{12,15},{9,... | collective-permute-start | bytes 491528 | tf_op jit(solution)/shard_map/ppermute | solution.py:351
  30.9 30.7 %collective-permute-start.3 = (bf16[128,640]{1,0:T(8,128)(2,1)S(1)}, bf16[128,640]{1,0:T(8,128)(2,1)S(1)}, u32[]{:S(2)}, u32[]{:S(2)}) collective-permute-start(bf16[128,640]{1,0:T(8,128)(2,1)S(1)} %get-tuple-element.36), channel_id=1, source_target_pairs={{1,0},{2,1},{3,2},{5,4},{6,5},{7,6},{0,3},{4,7},{9,8},{10,9},{11,1... | collective-permute-start | bytes 491528 | tf_op jit(solution)/shard_map/ppermute | solution.py:390
  41.3 1.2 %collective-permute-start.12 = (f32[8,640]{1,0:T(8,128)S(1)}, f32[8,640]{1,0:T(8,128)S(1)}, u32[]{:S(2)}, u32[]{:S(2)}) collective-permute-start(f32[8,640]{1,0:T(8,128)S(1)} %get-tuple-element.52), channel_id=1, source_target_pairs={{0,8},{8,0},{16,24},{24,16},{1,9},{9,1},{17,25},{25,17},{2,10},{10... | collective-permute-start | bytes 61448 | tf_op jit(solution)/shard_map/ppermute | solution.py:307
  42.5 3.8 %collective-permute-start.13 = (f32[8,640]{1,0:T(8,128)S(1)}, f32[8,640]{1,0:T(8,128)S(1)}, u32[]{:S(2)}, u32[]{:S(2)}) collective-permute-start(f32[8,640]{1,0:T(8,128)S(1)} %add.15), channel_id=1, source_target_pairs={{0,16},{8,24},{16,0},{24,8},{1,17},{9,25},{17,1},{25,9},{2,18},{10... | collective-permute-start | bytes 61448 | tf_op jit(solution)/shard_map/ppermute | solution.py:307
  46.3 3.8 %collective-permute-start.14 = (f32[8,640]{1,0:T(8,128)S(1)}, f32[8,640]{1,0:T(8,128)S(1)}, u32[]{:S(2)}, u32[]{:S(2)}) collective-permute-start(f32[8,640]{1,0:T(8,128)S(1)} %add.16), channel_id=1, source_target_pairs={{0,1},{1,0},{2,3},{3,2},{4,5},{5,4},{6,7},{7,6},{8,9},{9,8},{10,11... | collective-permute-start | bytes 61448 | tf_op jit(solution)/shard_map/ppermute | solution.py:307
  50.1 3.8 %collective-permute-start.15 = (f32[8,640]{1,0:T(8,128)S(1)}, f32[8,640]{1,0:T(8,128)S(1)}, u32[]{:S(2)}, u32[]{:S(2)}) collective-permute-start(f32[8,640]{1,0:T(8,128)S(1)} %add.17), channel_id=1, source_target_pairs={{0,2},{1,3},{2,0},{3,1},{4,6},{5,7},{6,4},{7,5},{8,10},{9,11},{10,... | collective-permute-start | bytes 61448 | tf_op jit(solution)/shard_map/ppermute | solution.py:307
  53.9 6.1 %collective-permute-start.16 = (f32[8,640]{1,0:T(8,128)S(1)}, f32[8,640]{1,0:T(8,128)S(1)}, u32[]{:S(2)}, u32[]{:S(2)}) collective-permute-start(f32[8,640]{1,0:T(8,128)S(1)} %add.18), channel_id=1, source_target_pairs={{0,4},{1,5},{2,6},{3,7},{4,0},{5,1},{6,2},{7,3},{8,12},{9,13},{10,... | collective-permute-start | bytes 61448 | tf_op jit(solution)/shard_map/ppermute | solution.py:307
  56.6 6.8 %collective-permute-start.4 = (bf16[128,640]{1,0:T(8,128)(2,1)S(1)}, bf16[128,640]{1,0:T(8,128)(2,1)S(1)}, u32[]{:S(2)}, u32[]{:S(2)}) collective-permute-start(bf16[128,640]{1,0:T(8,128)(2,1)S(1)} %get-tuple-element.37), channel_id=1, source_target_pairs={{2,0},{3,1},{6,4},{7,5},{0,2},{1,3},{4,6},{5,7},{10,8},{11,9},{14,... | collective-permute-start | bytes 491528 | tf_op jit(solution)/shard_map/ppermute | solution.py:390
  57.0 9.8 %collective-permute-start.5 = (bf16[128,640]{1,0:T(8,128)(2,1)S(1)}, bf16[128,640]{1,0:T(8,128)(2,1)S(1)}, u32[]{:S(2)}, u32[]{:S(2)}) collective-permute-start(bf16[128,640]{1,0:T(8,128)(2,1)S(1)} %get-tuple-element.38), channel_id=1, source_target_pairs={{3,0},{7,4},{0,1},{1,2},{2,3},{4,5},{5,6},{6,7},{11,8},{15,12},{8,... | collective-permute-start | bytes 491528 | tf_op jit(solution)/shard_map/ppermute | solution.py:390
  57.8 9.1 %collective-permute-start.9 = (bf16[128,640]{1,0:T(8,128)(2,1)S(1)}, bf16[128,640]{1,0:T(8,128)(2,1)S(1)}, u32[]{:S(2)}, u32[]{:S(2)}) collective-permute-start(bf16[128,640]{1,0:T(8,128)(2,1)S(1)} %get-tuple-element.45), channel_id=1, source_target_pairs={{1,0},{2,1},{3,2},{5,4},{6,5},{7,6},{0,3},{4,7},{9,8},{10,9},{11,1... | collective-permute-start | bytes 491528 | tf_op jit(solution)/shard_map/ppermute | solution.py:390
  60.0 6.9 %collective-permute-start.10 = (bf16[128,640]{1,0:T(8,128)(2,1)S(1)}, bf16[128,640]{1,0:T(8,128)(2,1)S(1)}, u32[]{:S(2)}, u32[]{:S(2)}) collective-permute-start(bf16[128,640]{1,0:T(8,128)(2,1)S(1)} %get-tuple-element.46), channel_id=1, source_target_pairs={{2,0},{3,1},{6,4},{7,5},{0,2},{1,3},{4,6},{5,7},{10,8},{11,9},{14,... | collective-permute-start | bytes 491528 | tf_op jit(solution)/shard_map/ppermute | solution.py:390
  61.5 8.8 %collective-permute-start.11 = (bf16[128,640]{1,0:T(8,128)(2,1)S(1)}, bf16[128,640]{1,0:T(8,128)(2,1)S(1)}, u32[]{:S(2)}, u32[]{:S(2)}) collective-permute-start(bf16[128,640]{1,0:T(8,128)(2,1)S(1)} %get-tuple-element.47), channel_id=1, source_target_pairs={{3,0},{7,4},{0,1},{1,2},{2,3},{4,5},{5,6},{6,7},{11,8},{15,12},{8,... | collective-permute-start | bytes 491528 | tf_op jit(solution)/shard_map/ppermute | solution.py:390
  62.4 8.0 %copy-start.4 = (s32[3,8]{1,0:T(4,128)S(1)}, s32[3,8]{1,0:T(4,128)}, u32[]{:S(2)}) copy-start(s32[3,8]{1,0:T(4,128)} %constant.8.clone.table) | copy-start | bytes 292

commit v3 on v2

v3 whole, which is shorter than its diff:
```python
import functools

import jax
import jax.numpy as jnp
import numpy as np
from jax import lax
from jax.experimental import pallas as pl
from jax.experimental.pallas import tpu as pltpu
from jax.sharding import PartitionSpec as P

HEADS = 8
HEAD_DIM = 80
SPAN = 4
OWN_HEADS = HEADS // SPAN
PART = OWN_HEADS * HEAD_DIM
SCALE = HEAD_DIM**-0.5
LOG2E = 1.4426950408889634
NEG = -1e30
LANES = 128
HALF = HEAD_DIM // 2
PACK_MIB = 60

rope_base = 10000.0


def trade_rounds(count):
    def pairs_of(shift):
        found = []
        for source in range(count):
            target = source + shift
            if 0 <= target < count and (source < SPAN) == (target < SPAN):
                found.append((source, target))
        return found

    rounds = []
    for shift in range(1, SPAN):
        ahead, back = pairs_of(shift), pairs_of(shift - SPAN)
        both = ahead + back
        if len({s for s, _ in both}) == len(both) and len({t for _, t in both}) == len(both):
            rounds.append((shift, both))
        else:
            rounds.append((shift, ahead))
            rounds.append((shift - SPAN, back))
    return rounds


def source_table(rounds, count):
    table = np.full((len(rounds), count), -1, np.int32)
    for number, (_, pairs) in enumerate(rounds):
        for source, target in pairs:
            table[number, target] = source
    return table


def target_table(rounds, count):
    table = np.full((len(rounds), count), -1, np.int32)
    for number, (_, pairs) in enumerate(rounds):
        for source, target in pairs:
            table[number, source] = target
    return table


def image_of(block, lengths, images):
    image = jnp.int32(0)
    start = jnp.int32(0)
    begin = jnp.int32(0)
    for number in range(images):
        size = lengths[0, number]
        inside = (block >= begin) & (block < begin + size)
        image = jnp.where(inside, number, image)
        start = jnp.where(inside, begin, start)
        begin = begin + size
    return image, start


def handler_of(start, residue, count):
    device = start + lax.rem(residue - lax.rem(start, SPAN) + SPAN, SPAN)
    return jnp.where(device >= count, device - SPAN, device)


def message_rows(tensor):
    return slice(tensor * HEAD_DIM, (tensor + 1) * HEAD_DIM)


def head_rows(residue, head):
    begin = (residue * OWN_HEADS + head) * HEAD_DIM
    return pl.ds(pl.multiple_of(begin, 16), HEAD_DIM)


def rotate(values, cosv, sinv):
    first, second = values[:HALF], values[HALF:]
    return jnp.concatenate([first * cosv - second * sinv, second * cosv + first * sinv], axis=0)


def unrotate(values, cosv, sinv):
    first, second = values[:HALF], values[HALF:]
    return jnp.concatenate([first * cosv + second * sinv, second * cosv - first * sinv], axis=0)


def pack_kernel(shifts, *refs):
    inputs, outs, held, turned, sems = refs[:4], refs[4:-9], refs[-9:-5], refs[-5:-1], refs[-1]
    slots = len(shifts)
    me = lax.axis_index("tok")
    copies = [
        pltpu.make_async_copy(source, target, sems.at[number])
        for number, (source, target) in enumerate(zip(inputs, held))
    ]
    for copy in copies:
        copy.start()
    for copy, source, target in zip(copies, held, turned):
        copy.wait()
        target[...] = source[...].T
    for head in range(OWN_HEADS):
        for slot, shift in enumerate(shifts):
            residue = lax.rem(me + shift + SPAN, SPAN)
            for number, source in enumerate(turned):
                outs[head * slots + slot][message_rows(number), :] = source[
                    head_rows(residue, head), :
                ]


def tables_kernel(images, tokd, lengths, widths, table, inverse, bias, cos_out, sin_out, bias_out):
    me = lax.axis_index("tok")
    slots = table.shape[0] + 1
    spot = lax.broadcasted_iota(jnp.int32, (HALF, tokd), 1)
    by_row = lax.broadcasted_iota(jnp.int32, (HALF, tokd), 0) < HALF // 2
    for slot in range(slots):
        block = me if slot == 0 else table[slot - 1, me]
        image, start = image_of(block, lengths, images)
        width = widths[0, image]
        bits = jnp.where(width == tokd, 0, jnp.where(width * 2 == tokd, 1, 2))
        shift = tokd.bit_length() - 1 - bits
        local = spot + (block - start) * tokd
        rowpos = lax.shift_right_logical(local, jnp.broadcast_to(shift, local.shape))
        colpos = local & (width - 1)
        angle = jnp.where(by_row, rowpos, colpos).astype(jnp.float32) * inverse[:, 0:1]
        cos_out[:, slot * tokd : (slot + 1) * tokd] = jnp.cos(angle)
        sin_out[:, slot * tokd : (slot + 1) * tokd] = jnp.sin(angle)
    plain = bias[...].astype(jnp.float32)
    rest = jnp.zeros((LANES - plain.shape[0], plain.shape[1]), jnp.float32)
    bias_out[...] = jnp.concatenate([plain, rest], axis=0).T


def attend_kernel(slots, count, images, tokd, head, factor, lengths, table, cosv, sinv, bias, *refs):
    msgs, refs = refs[:slots], refs[slots:]
    if head > 0:
        before, refs = refs[0], refs[1:]
    outs, sums = refs[:slots], refs[slots]
    qt_all, kt_all, vt_all, q_all, k_all, v_all, g_all, s_buf, e_buf, d_buf = refs[slots + 1 :]
    me = lax.axis_index("tok")
    residue = lax.rem(me, SPAN)
    ids = []
    for slot in range(slots):
        block = me if slot == 0 else table[slot - 1, me]
        image, start = image_of(block, lengths, images)
        handled = (block >= 0) & (handler_of(start, residue, count) == me)
        ids.append(jnp.where(handled, image, -1 - slot))
    own_bias = bias[head_rows(residue, head), :]
    rest_row = lax.broadcasted_iota(jnp.int32, (LANES - HEAD_DIM, tokd), 0)
    zeros = jnp.zeros((LANES - HEAD_DIM, tokd), jnp.float32)
    ones = jnp.where(rest_row < 2, 1.0, 0.0)

    def block_of(slot):
        return slice(slot * tokd, (slot + 1) * tokd)

    def stage(slot):
        at = block_of(slot)
        cos_b, sin_b = cosv[:, at], sinv[:, at]
        query, key, value = (
            msgs[slot][message_rows(tensor), :].astype(jnp.float32)
            + own_bias[:, tensor : tensor + 1]
            for tensor in range(3)
        )
        query = rotate(query, cos_b, sin_b) * (SCALE * LOG2E)
        for values, rest, turned, plain in (
            (query, zeros, qt_all, q_all),
            (rotate(key, cos_b, sin_b), zeros, kt_all, k_all),
            (value, ones, vt_all, v_all),
        ):
            values = jnp.concatenate([values, rest], axis=0).astype(jnp.bfloat16)
            turned[:, at] = values
            plain[at, :] = values.T

    def scores(slot, other):
        part = jnp.dot(
            k_all[block_of(other), :], qt_all[:, block_of(slot)], preferred_element_type=jnp.float32
        )
        s_buf[block_of(other), :] = part
        return jnp.max(part, axis=0, keepdims=True)

    def exponentials(slot, other, top):
        part = jnp.exp2(s_buf[block_of(other), :] - top)
        e_buf[block_of(other), block_of(slot)] = part.astype(jnp.bfloat16)

    def output(slot):
        mixed = jnp.dot(
            vt_all[...], e_buf[:, block_of(slot)], preferred_element_type=jnp.float32
        )
        inv = 1.0 / mixed[HEAD_DIM : HEAD_DIM + 1]
        out_b = (mixed[:HEAD_DIM] * inv).astype(jnp.bfloat16)
        outs[slot][message_rows(0), :] = out_b
        grad = msgs[slot][message_rows(3), :].astype(jnp.float32)
        delta = jnp.sum(grad * out_b.astype(jnp.float32), axis=0, keepdims=True) * inv
        coarse = delta.astype(jnp.bfloat16).astype(jnp.float32)
        rest = jnp.where(rest_row == 0, -coarse, jnp.where(rest_row == 1, coarse - delta, 0.0))
        grad = jnp.concatenate([grad * inv, rest], axis=0).astype(jnp.bfloat16)
        g_all[block_of(slot), :] = grad.T
        return grad

    def dscores(slot, other, grad):
        part = jnp.dot(v_all[block_of(other), :], grad, preferred_element_type=jnp.float32)
        d_buf[block_of(other), block_of(slot)] = (
            e_buf[block_of(other), block_of(slot)] * part.astype(jnp.bfloat16)
        )

    def query_part(slot):
        at = block_of(slot)
        dquery = jnp.dot(kt_all[:HEAD_DIM, :], d_buf[:, at], preferred_element_type=jnp.float32)
        dquery = unrotate(dquery * SCALE, cosv[:, at], sinv[:, at])
        outs[slot][message_rows(1), :] = dquery.astype(jnp.bfloat16)
        return jnp.where(ids[slot] >= 0, dquery, 0.0)

    for slot in range(slots):
        stage(slot)
    dq_total = jnp.zeros((HEAD_DIM, tokd), jnp.float32)
    grad = None
    for slot in range(slots + 1):
        if slot < slots:
            offs = [jnp.where(ids[slot] == ids[other], 0.0, NEG) for other in range(slots)]
            tops = [scores(slot, other) + offs[other] for other in range(slots)]
            top = functools.reduce(jnp.maximum, tops)
        for other in range(slots):
            if slot > 0:
                dscores(slot - 1, other, grad)
            if slot < slots:
                exponentials(slot, other, top - offs[other])
        if slot > 0:
            dq_total = dq_total + query_part(slot - 1)
        if slot < slots:
            grad = output(slot)
    dk_total = jnp.zeros((HEAD_DIM, tokd), jnp.float32)
    dv_total = jnp.zeros((1, LANES), jnp.float32)
    for slot in range(slots):
        at = block_of(slot)
        live = ids[slot] >= 0
        dvalue = jnp.dot(e_buf[at, :], g_all[...], preferred_element_type=jnp.float32)
        dv_total = dv_total + jnp.where(live, jnp.sum(dvalue, axis=0, keepdims=True), 0.0)
        outs[slot][message_rows(3), :] = dvalue.astype(jnp.bfloat16).T[:HEAD_DIM]
        dkey = jnp.dot(d_buf[at, :], q_all[...], preferred_element_type=jnp.float32)
        dkey = unrotate(dkey.T[:HEAD_DIM] * (1.0 / LOG2E), cosv[:, at], sinv[:, at])
        outs[slot][message_rows(2), :] = dkey.astype(jnp.bfloat16)
        dk_total = dk_total + jnp.where(live, dkey, 0.0)
    lane = lax.broadcasted_iota(jnp.int32, (HEAD_DIM, LANES), 1)
    columns = jnp.where(
        lane == 0,
        jnp.sum(dq_total, axis=1, keepdims=True),
        jnp.where(lane == 1, jnp.sum(dk_total, axis=1, keepdims=True), 0.0),
    )
    columns = jnp.concatenate([columns, jnp.zeros((LANES - HEAD_DIM, LANES), jnp.float32)], axis=0)
    lines = columns.T
    sums[...] = jnp.zeros_like(sums) if head == 0 else before[...]
    for number, total in enumerate((lines[0:1], lines[1:2], dv_total)):
        at = number * OWN_HEADS + head
        sums[at : at + 1, :] = total * factor


def unpack_kernel(slots, count, images, lengths, table, *refs):
    msgs, tiles = refs[: OWN_HEADS * slots], refs[OWN_HEADS * slots]
    outs, bias_out = refs[OWN_HEADS * slots + 1 : -2], refs[-2]
    held = refs[-1]
    me = lax.axis_index("tok")
    _, start = image_of(me, lengths, images)
    for slot in range(slots):
        source = me if slot == 0 else table[slot - 1, me]
        residue = lax.rem(source + SPAN, SPAN)

        @pl.when((source >= 0) & (source == handler_of(start, residue, count)))
        def _(slot=slot, residue=residue):
            for head in range(OWN_HEADS):
                for number in range(4):
                    held[number, head_rows(residue, head), :] = msgs[head * slots + slot][
                        message_rows(number), :
                    ]

    for number, out in enumerate(outs):
        out[...] = held[number].T

    def add(group, totals):
        return tuple(
            total + tiles[group * SPAN + residue] for residue, total in enumerate(totals)
        )

    groups = tiles.shape[0] // SPAN
    zero = jnp.zeros(tiles.shape[1:], jnp.float32)
    totals = lax.fori_loop(0, groups, add, (zero,) * SPAN, unroll=groups <= 8)
    for residue, total in enumerate(totals):
        for head in range(OWN_HEADS):
            begin = (residue * OWN_HEADS + head) * HEAD_DIM
            for tensor in range(3):
                at = tensor * OWN_HEADS + head
                bias_out[tensor : tensor + 1, begin : begin + HEAD_DIM] = total[
                    at : at + 1, :HEAD_DIM
                ]


def on_device(query_in, key_in, value_in, out_grad, bias, lengths, widths):
    tokd = query_in.shape[1]
    model = query_in.shape[2]
    images = lengths.shape[1]
    count = lax.axis_size("tok")
    rounds = trade_rounds(count)
    shifts = [0] + [shift for shift, _ in rounds]
    slots = len(shifts)
    table = jnp.asarray(source_table(rounds, count))
    quarter = HEAD_DIM // 4
    inverse = rope_base ** (-np.arange(quarter, dtype=np.float64) / quarter)
    inverse = jnp.asarray(np.tile(np.tile(inverse, 2)[:, None], (1, LANES)), jnp.float32)
    smem = pl.BlockSpec(memory_space=pltpu.SMEM)
    vmem = pl.BlockSpec(memory_space=pltpu.VMEM)
    hbm = pl.BlockSpec(memory_space=pltpu.HBM)
    whole = jax.ShapeDtypeStruct((tokd, model), jnp.bfloat16)
    message = jax.ShapeDtypeStruct((4 * HEAD_DIM, tokd), jnp.bfloat16)
    sums_shape = jax.ShapeDtypeStruct((8, LANES), jnp.float32)
    devices = lax.axis_size("dp") * count
    tokens_all = devices * tokd

    def params(mib):
        return pltpu.CompilerParams(vmem_limit_bytes=mib * 1024 * 1024)

    sends = pl.pallas_call(
        functools.partial(pack_kernel, shifts),
        out_shape=[message] * (OWN_HEADS * slots),
        in_specs=[hbm] * 4,
        out_specs=[vmem] * (OWN_HEADS * slots),
        scratch_shapes=[pltpu.VMEM((tokd, model), jnp.bfloat16)] * 4
        + [pltpu.VMEM((model, tokd), jnp.bfloat16)] * 4
        + [pltpu.SemaphoreType.DMA((4,))],
        compiler_params=params(PACK_MIB),
        name="pack_heads",
    )(query_in[0], key_in[0], value_in[0], out_grad[0])
    got = []
    for head in range(OWN_HEADS):
        mine = sends[head * slots : (head + 1) * slots]
        got.append(
            [mine[0]]
            + [lax.ppermute(send, "tok", pairs) for send, (_, pairs) in zip(mine[1:], rounds)]
        )
    span = slots * tokd
    table_shape = jax.ShapeDtypeStruct((HALF, span), jnp.float32)
    cosv, sinv, bias_cols = pl.pallas_call(
        functools.partial(tables_kernel, images, tokd),
        out_shape=[table_shape] * 2 + [jax.ShapeDtypeStruct((model, LANES), jnp.float32)],
        in_specs=[smem, smem, smem, vmem, vmem],
        out_specs=[vmem] * 3,
        compiler_params=params(16),
        cost_estimate=pl.CostEstimate(
            flops=span * LANES * 200, bytes_accessed=0, transcendentals=0
        ),
        name="rotary_tables",
    )(lengths, widths, table, inverse, bias)
    back = []
    sums = None
    for head in range(OWN_HEADS):
        operands = [lengths, table, cosv, sinv, bias_cols] + got[head]
        if head > 0:
            operands.append(sums)
        results = pl.pallas_call(
            functools.partial(
                attend_kernel, slots, count, images, tokd, head, 1.0 / tokens_all**0.5
            ),
            out_shape=[message] * slots + [sums_shape],
            in_specs=[smem, smem] + [vmem] * (len(operands) - 2),
            out_specs=[vmem] * (slots + 1),
            scratch_shapes=[pltpu.VMEM((LANES, span), jnp.bfloat16)] * 3
            + [pltpu.VMEM((span, LANES), jnp.bfloat16)] * 4
            + [pltpu.VMEM((span, tokd), jnp.float32)]
            + [pltpu.VMEM((span, span), jnp.bfloat16)] * 2,
            compiler_params=params(32),
            cost_estimate=pl.CostEstimate(
                flops=12 * span * span * 256, bytes_accessed=0, transcendentals=0
            ),
            name="attend_head",
        )(*operands)
        sums = results[slots]
        if head + 1 < OWN_HEADS:
            results, got[head + 1] = lax.optimization_barrier((results, got[head + 1]))
            sums = results[slots]
        back.append(results[0])
        back += [
            lax.ppermute(result, "tok", [(target, source) for source, target in pairs])
            for result, (_, pairs) in zip(results[1:slots], rounds)
        ]
    early = back[: slots * (OWN_HEADS - 1)]
    sums, early = lax.optimization_barrier((sums, early))
    back[: slots * (OWN_HEADS - 1)] = early
    tiles = lax.all_to_all(
        jnp.broadcast_to(sums[None], (devices,) + sums.shape), ("dp", "tok"), 0, 0, tiled=True
    )
    *outs, bias_grad = pl.pallas_call(
        functools.partial(unpack_kernel, slots, count, images),
        out_shape=[whole] * 4 + [jax.ShapeDtypeStruct((3, model), jnp.float32)],
        in_specs=[smem, smem] + [vmem] * (OWN_HEADS * slots + 1),
        out_specs=[vmem] * 5,
        scratch_shapes=[pltpu.VMEM((4, model, tokd), jnp.bfloat16)],
        compiler_params=params(16),
        name="unpack_heads",
    )(lengths, jnp.asarray(target_table(rounds, count)), *back, tiles)
    return tuple(out[None] for out in outs) + (bias_grad,)


def solution(mesh):
    in_specs = (
        P("dp", "tok", None),
        P("dp", "tok", None),
        P("dp", "tok", None),
        P("dp", "tok", None),
        P(),
        P("dp", None),
        P("dp", None),
    )
    out_specs = (
        P("dp", "tok", None),
        P("dp", "tok", None),
        P("dp", "tok", None),
        P("dp", "tok", None),
        P(),
    )
    return jax.shard_map(
        on_device, mesh=mesh, in_specs=in_specs, out_specs=out_specs, check_vma=False
    )
```

time: 74.7 us -> 53.8 us (0.72)
  Pallas kernels: 27.1 us -> 15.7 us
  waiting for transfers between devices: 20.1 us -> 14.3 us
  local copies, waits for them, and re-layouts: 3.91 us -> 1.61 us
    ppermute x5 -> x0, waiting for transfers between devices: 9.42 us -> none  [sum_over(): lax.ppermute(value, axis, [(one, one ^ step) for one in range(size)])]
    pallas_call x2, Pallas kernels: 18.6 us -> 9.86 us  [on_device(): pl.pallas_call(functools.partial(attend_kernel, slots, count, images, tok...]
    ppermute x5 -> x0, starting transfers between devices: 5.87 us -> none  [sum_over(): lax.ppermute(value, axis, [(one, one ^ step) for one in range(size)])]
    all_to_all x0 -> x1, starting transfers between devices: none -> 4.82 us  [on_device(): lax.all_to_all(jnp.broadcast_to(sums[None], (devices,) + sums.shape), ('d...]
    unnamed x20 -> x16, local copies, waits for them, and re-layouts: 3.91 us -> 0.95 us
    ppermute x6, waiting for transfers between devices: 7.98 us -> 10.6 us  [on_device(): lax.ppermute(result, 'tok', [(target, source) for source, target in pairs])]
    pallas_call x1, Pallas kernels: 4.03 us -> 2 us  [on_device(): pl.pallas_call(functools.partial(unpack_kernel, slots, count, images), ou...]
    pallas_call x1, Pallas kernels: 2.67 us -> 1.23 us  [on_device(): pl.pallas_call(functools.partial(tables_kernel, images, tokd), out_shape=...]
  transfers between devices with their start and end apart: 17 -> 13, of which waited for: 8 -> 7; matrix products, arithmetic and copies ran while one was open for 1% -> 0% of each run, Pallas kernels for 29% -> 21%
where the time goes in v3:
time: 53.8 us; the launch traced here: 53.6 us
  starting transfers between devices  21.3 us (40%)
  Pallas kernels  15.7 us (29%)
  waiting for transfers between devices  14.3 us (27%)
  local copies, waits for them, and re-layouts  1.61 us (3%)
  between operations  0.71 us (1%)
    ppermute x6, waiting for transfers between devices, on_device(): lax.ppermute(result, 'tok', [(target, source) for source, target in pairs])  10.6 us
    ppermute x6, starting transfers between devices, on_device(): lax.ppermute(send, 'tok', pairs)  10.5 us
    pallas_call x2, Pallas kernels, on_device(): pl.pallas_call(functools.partial(attend_kernel, slots, count, images, tok...  9.86 us
    ppermute x6, starting transfers between devices, on_device(): lax.ppermute(result, 'tok', [(target, source) for source, target in pairs])  5.93 us
    all_to_all x1, starting transfers between devices, on_device(): lax.all_to_all(jnp.broadcast_to(sums[None], (devices,) + sums.shape), ('d...  4.82 us
    ppermute x6, waiting for transfers between devices, on_device(): lax.ppermute(send, 'tok', pairs)  3.66 us
    pallas_call x1, Pallas kernels, on_device(): pl.pallas_call(functools.partial(pack_kernel, shifts), out_shape=[message...  2.65 us
    pallas_call x1, Pallas kernels, on_device(): pl.pallas_call(functools.partial(unpack_kernel, slots, count, images), ou...  2 us
  transfers between devices with their start and end apart: 13, of which 7 were waited for; matrix products, arithmetic and copies ran while one was open for 0% of the time, Pallas kernels for 21%

profile of v3, /device:TPU:0, one launch (start us, length us, event | category | flops | bytes accessed | tf_op | source)
XLA Modules:
  0.0 53.6 jit_solution(14361799363827821292)
XLA Ops:
  0.6 0.0 copy-start.6
  0.6 2.7 %pack_heads.1 = (bf16[320,256]{1,0:T(8,128)(2,1)}, bf16[320,256]{1,0:T(8,128)(2,1)}, bf16[320,256]{1,0:T(8,128)(2,1)}, bf16[320,256]{1,0:T(8,128)(2,1)}, bf16[32...) custom-call(bf16[256,640]{1,0:T(8,128)(2,1)} %bitcast.8, ...), custom_call_target="tpu_custom_call" | custom-call | tf_op jit(solution)/shard_map/pack_heads/pallas_call | solution.py:330
  3.3 0.0 copy-start.4
  3.3 3.0 %collective-permute-start = (bf16[320,256]{1,0:T(8,128)(2,1)}, bf16[320,256]{1,0:T(8,128)(2,1)S(1)}, u32[]{:S(2)}, u32[]{:S(2)}) collective-permute-start(bf16[320,256]{1,0:T(8,128)(2,1)} %get-tuple-element.49), channel_id=1, source_target_pairs={{0,1},{1,2},{2,3},{4,5},{5,6},{6,7},{3,0},{7,4},{8,9},{9,10},{10,1... | collective-permute-start | bytes 491528 | tf_op jit(solution)/shard_map/ppermute | solution.py:346
  6.3 1.6 %collective-permute-start.1 = (bf16[320,256]{1,0:T(8,128)(2,1)}, bf16[320,256]{1,0:T(8,128)(2,1)S(1)}, u32[]{:S(2)}, u32[]{:S(2)}) collective-permute-start(bf16[320,256]{1,0:T(8,128)(2,1)} %get-tuple-element.50), channel_id=1, source_target_pairs={{0,2},{1,3},{4,6},{5,7},{2,0},{3,1},{6,4},{7,5},{8,10},{9,11},{12,... | collective-permute-start | bytes 491528 | tf_op jit(solution)/shard_map/ppermute | solution.py:346
  7.9 0.0 copy-start.7
  7.9 1.4 %collective-permute-start.2 = (bf16[320,256]{1,0:T(8,128)(2,1)}, bf16[320,256]{1,0:T(8,128)(2,1)S(1)}, u32[]{:S(2)}, u32[]{:S(2)}) collective-permute-start(bf16[320,256]{1,0:T(8,128)(2,1)} %get-tuple-element.51), channel_id=1, source_target_pairs={{0,3},{4,7},{1,0},{2,1},{3,2},{5,4},{6,5},{7,6},{8,11},{12,15},{9,... | collective-permute-start | bytes 491528 | tf_op jit(solution)/shard_map/ppermute | solution.py:346
  9.3 0.0 copy-start.1
  9.3 0.0 copy-start.5
  9.3 0.6 %collective-permute-start.3 = (bf16[320,256]{1,0:T(8,128)(2,1)}, bf16[320,256]{1,0:T(8,128)(2,1)S(1)}, u32[]{:S(2)}, u32[]{:S(2)}) collective-permute-start(bf16[320,256]{1,0:T(8,128)(2,1)} %get-tuple-element.58), channel_id=1, source_target_pairs={{0,1},{1,2},{2,3},{4,5},{5,6},{6,7},{3,0},{7,4},{8,9},{9,10},{10,1... | collective-permute-start | bytes 491528 | tf_op jit(solution)/shard_map/ppermute | solution.py:346
  9.9 0.4 collective-permute-start.4
  10.4 0.0 copy-done.6
  10.4 0.0 copy-done.4
  10.4 0.0 copy-done.7
  10.4 0.0 copy-done.1
  10.4 0.0 copy-done.5
  10.4 1.2 %rotary_tables.1 = (f32[40,1024]{1,0:T(8,128)S(1)}, f32[40,1024]{1,0:T(8,128)S(1)}, f32[640,128]{1,0:T(8,128)S(1)}) custom-call(s32[1,4]{1,0:T(1,128)S(1)} %copy-done.1, s32[1,4]{1,0:T(1,128)S(1)} %copy-done.5, s32[3,8]{1,0:T(4,128)S(1)} %copy-done.7, f32[40,128]{1,0:T(8,128)S(1)} %copy-done.6, bf16[3,640]{1,0:T(4,128)(2,1)S(1)} %copy-done.4), custom_call_target="tpu_custom_call" | custom-call | flops 26214400 | tf_op jit(solution)/shard_map/rotary_tables/pallas_call | solution.py:350
  11.6 0.9 %collective-permute-done.refs_1_ = bf16[320,256]{1,0:T(8,128)(2,1)S(1)} collective-permute-done((bf16[320,256]{1,0:T(8,128)(2,1)}, bf16[320,256]{1,0:T(8,128)(2,1)S(1)}, u32[]{:S(2)}, u32[]{:S(2)}) %collective-permute-start) | collective-permute-done | bytes 163872 | tf_op jit(solution)/shard_map/ppermute | solution.py:346
  12.6 3.5 %collective-permute-start.5 = (bf16[320,256]{1,0:T(8,128)(2,1)}, bf16[320,256]{1,0:T(8,128)(2,1)S(1)}, u32[]{:S(2)}, u32[]{:S(2)}) collective-permute-start(bf16[320,256]{1,0:T(8,128)(2,1)} %get-tuple-element.60), channel_id=1, source_target_pairs={{0,3},{4,7},{1,0},{2,1},{3,2},{5,4},{6,5},{7,6},{8,11},{12,15},{9,... | collective-permute-start | bytes 491528 | tf_op jit(solution)/shard_map/ppermute | solution.py:346
  16.0 0.0 collective-permute-done.1.refs_2_
  16.0 2.7 %collective-permute-done.2.refs_3_ = bf16[320,256]{1,0:T(8,128)(2,1)S(1)} collective-permute-done((bf16[320,256]{1,0:T(8,128)(2,1)}, bf16[320,256]{1,0:T(8,128)(2,1)S(1)}, u32[]{:S(2)}, u32[]{:S(2)}) %collective-permute-start.2) | collective-permute-done | bytes 163872 | tf_op jit(solution)/shard_map/ppermute | solution.py:346
  18.8 0.0 copy-start.3
  18.8 0.9 %copy-done.3 = bf16[320,256]{1,0:T(8,128)(2,1)S(1)} copy-done((bf16[320,256]{1,0:T(8,128)(2,1)S(1)}, bf16[320,256]{1,0:T(8,128)(2,1)}, u32[]{:S(2)}) %copy-start.3) | copy-done | bytes 163864
  19.7 0.0 copy-start.2
  19.7 4.9 %attend_head.2 = (bf16[320,256]{1,0:T(8,128)(2,1)S(1)}, bf16[320,256]{1,0:T(8,128)(2,1)S(1)}, bf16[320,256]{1,0:T(8,128)(2,1)S(1)}, bf16[320,256]{1,0:T(8,128)(2,1)S(1)}, f32[8,128]{1,0:T(8,128)S(1)}) custom-call(s32[1,4]{1,0:T(1,128)S(1)} %copy-done.1, s32[3,8]{1,0:T(4,128)S(1)} %copy-done.7, f32[40,1024]{1,0:T(8,128)S(1)} %get-tuple-element.45.cosv, ...), custom_call_target="tpu_custom_call" | custom-call | flops 3221225472 | tf_op jit(solution)/shard_map/attend_head/pallas_call | solution.py:367
  24.6 0.0 collective-permute-done.3.refs_1_
  24.6 0.0 collective-permute-done.4.refs_2_
  24.6 0.0 collective-permute-done.5.refs_3_
  24.6 0.9 %collective-permute-start.6 = (bf16[320,256]{1,0:T(8,128)(2,1)S(1)}, bf16[320,256]{1,0:T(8,128)(2,1)S(1)}, u32[]{:S(2)}, u32[]{:S(2)}) collective-permute-start(bf16[320,256]{1,0:T(8,128)(2,1)S(1)} %get-tuple-element.68), channel_id=1, source_target_pairs={{1,0},{2,1},{3,2},{5,4},{6,5},{7,6},{0,3},{4,7},{9,8},{10,9},{11,1... | collective-permute-start | bytes 491528 | tf_op jit(solution)/shard_map/ppermute | solution.py:390
  25.6 0.4 collective-permute-start.7
  26.0 0.7 %collective-permute-start.8 = (bf16[320,256]{1,0:T(8,128)(2,1)S(1)}, bf16[320,256]{1,0:T(8,128)(2,1)S(1)}, u32[]{:S(2)}, u32[]{:S(2)}) collective-permute-start(bf16[320,256]{1,0:T(8,128)(2,1)S(1)} %get-tuple-element.70), channel_id=1, source_target_pairs={{3,0},{7,4},{0,1},{1,2},{2,3},{4,5},{5,6},{6,7},{11,8},{15,12},{8,... | collective-permute-start | bytes 491528 | tf_op jit(solution)/shard_map/ppermute | solution.py:390
  26.7 0.0 copy-done.2
  26.7 4.9 %attend_head.3 = (bf16[320,256]{1,0:T(8,128)(2,1)S(1)}, bf16[320,256]{1,0:T(8,128)(2,1)S(1)}, bf16[320,256]{1,0:T(8,128)(2,1)S(1)}, bf16[320,256]{1,0:T(8,128)(2,1)S(1)}, f32[8,128]{1,0:T(8,128)S(1)}) custom-call(s32[1,4]{1,0:T(1,128)S(1)} %copy-done.1, s32[3,8]{1,0:T(4,128)S(1)} %copy-done.7, f32[40,1024]{1,0:T(8,128)S(1)} %get-tuple-element.45.cosv, ...), custom_call_target="tpu_custom_call" | custom-call | flops 3221225472 | tf_op jit(solution)/shard_map/attend_head/pallas_call | solution.py:367
  31.6 0.0 collective-permute-done.6.refs_1_
  31.6 0.3 collective-permute-done.7.refs_2_
  31.9 1.3 %collective-permute-done.8.refs_3_ = bf16[320,256]{1,0:T(8,128)(2,1)S(1)} collective-permute-done((bf16[320,256]{1,0:T(8,128)(2,1)S(1)}, bf16[320,256]{1,0:T(8,128)(2,1)S(1)}, u32[]{:S(2)}, u32[]{:S(2)}) %collective-permute-start.8) | collective-permute-done | bytes 163872 | tf_op jit(solution)/shard_map/ppermute | solution.py:390
  33.2 0.7 %broadcast_in_dim.18 = f32[32,8,128]{2,1,0:T(8,128)} broadcast(f32[8,128]{1,0:T(8,128)S(1)} %get-tuple-element.79), dimensions={1,2} | broadcast | bytes 135168 | tf_op jit(solution)/shard_map/broadcast_in_dim | solution.py:397
  33.9 4.8 %all-to-all-start = ((f32[32,8,128]{2,1,0:T(8,128)}), f32[32,8,128]{2,1,0:T(8,128)S(1)}, u32[]{:S(2)}, u32[]{:S(2)}) async-start(f32[32,8,128]{2,1,0:T(8,128)} %broadcast_in_dim.18), calls=%async_computation | async-start | bytes 262144 | tf_op jit(solution)/shard_map/all_to_all | solution.py:396
  38.7 2.7 %collective-permute-start.9 = (bf16[320,256]{1,0:T(8,128)(2,1)S(1)}, bf16[320,256]{1,0:T(8,128)(2,1)S(1)}, u32[]{:S(2)}, u32[]{:S(2)}) collective-permute-start(bf16[320,256]{1,0:T(8,128)(2,1)S(1)} %get-tuple-element.76), channel_id=1, source_target_pairs={{1,0},{2,1},{3,2},{5,4},{6,5},{7,6},{0,3},{4,7},{9,8},{10,9},{11,1... | collective-permute-start | bytes 491528 | tf_op jit(solution)/shard_map/ppermute | solution.py:390
  41.4 0.0 copy-start
  41.4 0.6 %collective-permute-start.10 = (bf16[320,256]{1,0:T(8,128)(2,1)S(1)}, bf16[320,256]{1,0:T(8,128)(2,1)S(1)}, u32[]{:S(2)}, u32[]{:S(2)}) collective-permute-start(bf16[320,256]{1,0:T(8,128)(2,1)S(1)} %get-tuple-element.77), channel_id=1, source_target_pairs={{2,0},{3,1},{6,4},{7,5},{0,2},{1,3},{4,6},{5,7},{10,8},{11,9},{14,... | collective-permute-start | bytes 491528 | tf_op jit(solution)/shard_map/ppermute | solution.py:390
  42.0 0.6 %collective-permute-start.11 = (bf16[320,256]{1,0:T(8,128)(2,1)S(1)}, bf16[320,256]{1,0:T(8,128)(2,1)S(1)}, u32[]{:S(2)}, u32[]{:S(2)}) collective-permute-start(bf16[320,256]{1,0:T(8,128)(2,1)S(1)} %get-tuple-element.78), channel_id=1, source_target_pairs={{3,0},{7,4},{0,1},{1,2},{2,3},{4,5},{5,6},{6,7},{11,8},{15,12},{8,... | collective-permute-start | bytes 491528 | tf_op jit(solution)/shard_map/ppermute | solution.py:390
  42.6 3.9 %collective-permute-done.9.refs_5_ = bf16[320,256]{1,0:T(8,128)(2,1)S(1)} collective-permute-done((bf16[320,256]{1,0:T(8,128)(2,1)S(1)}, bf16[320,256]{1,0:T(8,128)(2,1)S(1)}, u32[]{:S(2)}, u32[]{:S(2)}) %collective-permute-start.9) | collective-permute-done | bytes 163872 | tf_op jit(solution)/shard_map/ppermute | solution.py:390
  46.5 4.6 %collective-permute-done.10.refs_6_ = bf16[320,256]{1,0:T(8,128)(2,1)S(1)} collective-permute-done((bf16[320,256]{1,0:T(8,128)(2,1)S(1)}, bf16[320,256]{1,0:T(8,128)(2,1)S(1)}, u32[]{:S(2)}, u32[]{:S(2)}) %collective-permute-start.10) | collective-permute-done | bytes 163872 | tf_op jit(solution)/shard_map/ppermute | solution.py:390
  51.1 0.6 %collective-permute-done.11.refs_7_ = bf16[320,256]{1,0:T(8,128)(2,1)S(1)} collective-permute-done((bf16[320,256]{1,0:T(8,128)(2,1)S(1)}, bf16[320,256]{1,0:T(8,128)(2,1)S(1)}, u32[]{:S(2)}, u32[]{:S(2)}) %collective-permute-start.11) | collective-permute-done | bytes 163872 | tf_op jit(solution)/shard_map/ppermute | solution.py:390
  51.6 0.0 all-to-all-done.refs_8_
  51.6 0.0 copy-done
  51.6 2.0 %unpack_heads.1 = (bf16[256,640]{1,0:T(8,128)(2,1)}, bf16[256,640]{1,0:T(8,128)(2,1)}, bf16[256,640]{1,0:T(8,128)(2,1)}, bf16[256,640]{1,0:T(8,128)(2,1)}, f32[3,640]{1,0:T(4,128)}) custom-call(s32[1,4]{1,0:T(1,128)S(1)} %copy-done.1, s32[3,8]{1,0:T(4,128)S(1)} %copy-done, bf16[320,256]{1,0:T(8,128)(2,1)S(1)} %get-tuple-element.71.refs_0_, ...), custom_call_target="tpu_custom_call" | custom-call | tf_op jit(solution)/shard_map/unpack_heads/pallas_call | solution.py:399
Async XLA Ops:
  0.6 9.7 %copy-start.6 = (f32[40,128]{1,0:T(8,128)S(1)}, f32[40,128]{1,0:T(8,128)}, u32[]{:S(2)}) copy-start(f32[40,128]{1,0:T(8,128)} %constant.7.clone.inverse) | copy-start | bytes 61444
  3.3 7.1 %copy-start.4 = (bf16[3,640]{1,0:T(4,128)(2,1)S(1)}, bf16[3,640]{1,0:T(4,128)(2,1)}, u32[]{:S(2)}) copy-start(bf16[3,640]{1,0:T(4,128)(2,1)} %bias.1) | copy-start | bytes 11524
  3.3 9.2 %collective-permute-start = (bf16[320,256]{1,0:T(8,128)(2,1)}, bf16[320,256]{1,0:T(8,128)(2,1)S(1)}, u32[]{:S(2)}, u32[]{:S(2)}) collective-permute-start(bf16[320,256]{1,0:T(8,128)(2,1)} %get-tuple-element.49), channel_id=1, source_target_pairs={{0,1},{1,2},{2,3},{4,5},{5,6},{6,7},{3,0},{7,4},{8,9},{9,10},{10,1... | collective-permute-start | bytes 491528 | tf_op jit(solution)/shard_map/ppermute | solution.py:346
  6.3 9.7 %collective-permute-start.1 = (bf16[320,256]{1,0:T(8,128)(2,1)}, bf16[320,256]{1,0:T(8,128)(2,1)S(1)}, u32[]{:S(2)}, u32[]{:S(2)}) collective-permute-start(bf16[320,256]{1,0:T(8,128)(2,1)} %get-tuple-element.50), channel_id=1, source_target_pairs={{0,2},{1,3},{4,6},{5,7},{2,0},{3,1},{6,4},{7,5},{8,10},{9,11},{12,... | collective-permute-start | bytes 491528 | tf_op jit(solution)/shard_map/ppermute | solution.py:346
  7.9 2.5 %copy-start.7 = (s32[3,8]{1,0:T(4,128)S(1)}, s32[3,8]{1,0:T(4,128)}, u32[]{:S(2)}) copy-start(s32[3,8]{1,0:T(4,128)} %constant.6.clone.table) | copy-start | bytes 292
  7.9 10.9 %collective-permute-start.2 = (bf16[320,256]{1,0:T(8,128)(2,1)}, bf16[320,256]{1,0:T(8,128)(2,1)S(1)}, u32[]{:S(2)}, u32[]{:S(2)}) collective-permute-start(bf16[320,256]{1,0:T(8,128)(2,1)} %get-tuple-element.51), channel_id=1, source_target_pairs={{0,3},{4,7},{1,0},{2,1},{3,2},{5,4},{6,5},{7,6},{8,11},{12,15},{9,... | collective-permute-start | bytes 491528 | tf_op jit(solution)/shard_map/ppermute | solution.py:346
  9.3 1.1 %copy-start.1 = (s32[1,4]{1,0:T(1,128)S(1)}, s32[1,4]{1,0:T(1,128)}, u32[]{:S(2)}) copy-start(s32[1,4]{1,0:T(1,128)} %lengths.7) | copy-start | bytes 52
  9.3 1.1 %copy-start.5 = (s32[1,4]{1,0:T(1,128)S(1)}, s32[1,4]{1,0:T(1,128)}, u32[]{:S(2)}) copy-start(s32[1,4]{1,0:T(1,128)} %widths.1) | copy-start | bytes 52
  9.3 15.3 %collective-permute-start.3 = (bf16[320,256]{1,0:T(8,128)(2,1)}, bf16[320,256]{1,0:T(8,128)(2,1)S(1)}, u32[]{:S(2)}, u32[]{:S(2)}) collective-permute-start(bf16[320,256]{1,0:T(8,128)(2,1)} %get-tuple-element.58), channel_id=1, source_target_pairs={{0,1},{1,2},{2,3},{4,5},{5,6},{6,7},{3,0},{7,4},{8,9},{9,10},{10,1... | collective-permute-start | bytes 491528 | tf_op jit(solution)/shard_map/ppermute | solution.py:346
  9.9 14.7 %collective-permute-start.4 = (bf16[320,256]{1,0:T(8,128)(2,1)}, bf16[320,256]{1,0:T(8,128)(2,1)S(1)}, u32[]{:S(2)}, u32[]{:S(2)}) collective-permute-start(bf16[320,256]{1,0:T(8,128)(2,1)} %get-tuple-element.59), channel_id=1, source_target_pairs={{0,2},{1,3},{4,6},{5,7},{2,0},{3,1},{6,4},{7,5},{8,10},{9,11},{12,... | collective-permute-start | bytes 491528 | tf_op jit(solution)/shard_map/ppermute | solution.py:346
  12.6 12.1 %collective-permute-start.5 = (bf16[320,256]{1,0:T(8,128)(2,1)}, bf16[320,256]{1,0:T(8,128)(2,1)S(1)}, u32[]{:S(2)}, u32[]{:S(2)}) collective-permute-start(bf16[320,256]{1,0:T(8,128)(2,1)} %get-tuple-element.60), channel_id=1, source_target_pairs={{0,3},{4,7},{1,0},{2,1},{3,2},{5,4},{6,5},{7,6},{8,11},{12,15},{9,... | collective-permute-start | bytes 491528 | tf_op jit(solution)/shard_map/ppermute | solution.py:346
  18.8 0.9 %copy-start.3 = (bf16[320,256]{1,0:T(8,128)(2,1)S(1)}, bf16[320,256]{1,0:T(8,128)(2,1)}, u32[]{:S(2)}) copy-start(bf16[320,256]{1,0:T(8,128)(2,1)} %get-tuple-element.48.refs_0_) | copy-start | bytes 491524
  19.7 7.0 %copy-start.2 = (bf16[320,256]{1,0:T(8,128)(2,1)S(1)}, bf16[320,256]{1,0:T(8,128)(2,1)}, u32[]{:S(2)}) copy-start(bf16[320,256]{1,0:T(8,128)(2,1)} %get-tuple-element.61.refs_0_) | copy-start | bytes 491524
  24.6 7.0 %collective-permute-start.6 = (bf16[320,256]{1,0:T(8,128)(2,1)S(1)}, bf16[320,256]{1,0:T(8,128)(2,1)S(1)}, u32[]{:S(2)}, u32[]{:S(2)}) collective-permute-start(bf16[320,256]{1,0:T(8,128)(2,1)S(1)} %get-tuple-element.68), channel_id=1, source_target_pairs={{1,0},{2,1},{3,2},{5,4},{6,5},{7,6},{0,3},{4,7},{9,8},{10,9},{11,1... | collective-permute-start | bytes 491528 | tf_op jit(solution)/shard_map/ppermute | solution.py:390
  25.6 6.4 %collective-permute-start.7 = (bf16[320,256]{1,0:T(8,128)(2,1)S(1)}, bf16[320,256]{1,0:T(8,128)(2,1)S(1)}, u32[]{:S(2)}, u32[]{:S(2)}) collective-permute-start(bf16[320,256]{1,0:T(8,128)(2,1)S(1)} %get-tuple-element.69), channel_id=1, source_target_pairs={{2,0},{3,1},{6,4},{7,5},{0,2},{1,3},{4,6},{5,7},{10,8},{11,9},{14,... | collective-permute-start | bytes 491528 | tf_op jit(solution)/shard_map/ppermute | solution.py:390
  26.0 7.2 %collective-permute-start.8 = (bf16[320,256]{1,0:T(8,128)(2,1)S(1)}, bf16[320,256]{1,0:T(8,128)(2,1)S(1)}, u32[]{:S(2)}, u32[]{:S(2)}) collective-permute-start(bf16[320,256]{1,0:T(8,128)(2,1)S(1)} %get-tuple-element.70), channel_id=1, source_target_pairs={{3,0},{7,4},{0,1},{1,2},{2,3},{4,5},{5,6},{6,7},{11,8},{15,12},{8,... | collective-permute-start | bytes 491528 | tf_op jit(solution)/shard_map/ppermute | solution.py:390
  33.9 17.7 %all-to-all-start = ((f32[32,8,128]{2,1,0:T(8,128)}), f32[32,8,128]{2,1,0:T(8,128)S(1)}, u32[]{:S(2)}, u32[]{:S(2)}) async-start(f32[32,8,128]{2,1,0:T(8,128)} %broadcast_in_dim.18), calls=%async_computation | async-start | bytes 262144 | tf_op jit(solution)/shard_map/all_to_all | solution.py:396
  38.7 7.8 %collective-permute-start.9 = (bf16[320,256]{1,0:T(8,128)(2,1)S(1)}, bf16[320,256]{1,0:T(8,128)(2,1)S(1)}, u32[]{:S(2)}, u32[]{:S(2)}) collective-permute-start(bf16[320,256]{1,0:T(8,128)(2,1)S(1)} %get-tuple-element.76), channel_id=1, source_target_pairs={{1,0},{2,1},{3,2},{5,4},{6,5},{7,6},{0,3},{4,7},{9,8},{10,9},{11,1... | collective-permute-start | bytes 491528 | tf_op jit(solution)/shard_map/ppermute | solution.py:390
  41.4 10.2 %copy-start = (s32[3,8]{1,0:T(4,128)S(1)}, s32[3,8]{1,0:T(4,128)}, u32[]{:S(2)}) copy-start(s32[3,8]{1,0:T(4,128)} %constant.8.clone.table) | copy-start | bytes 292
  41.4 9.6 %collective-permute-start.10 = (bf16[320,256]{1,0:T(8,128)(2,1)S(1)}, bf16[320,256]{1,0:T(8,128)(2,1)S(1)}, u32[]{:S(2)}, u32[]{:S(2)}) collective-permute-start(bf16[320,256]{1,0:T(8,128)(2,1)S(1)} %get-tuple-element.77), channel_id=1, source_target_pairs={{2,0},{3,1},{6,4},{7,5},{0,2},{1,3},{4,6},{5,7},{10,8},{11,9},{14,... | collective-permute-start | bytes 491528 | tf_op jit(solution)/shard_map/ppermute | solution.py:390
  42.0 9.6 %collective-permute-start.11 = (bf16[320,256]{1,0:T(8,128)(2,1)S(1)}, bf16[320,256]{1,0:T(8,128)(2,1)S(1)}, u32[]{:S(2)}, u32[]{:S(2)}) collective-permute-start(bf16[320,256]{1,0:T(8,128)(2,1)S(1)} %get-tuple-element.78), channel_id=1, source_target_pairs={{3,0},{7,4},{0,1},{1,2},{2,3},{4,5},{5,6},{6,7},{11,8},{15,12},{8,... | collective-permute-start | bytes 491528 | tf_op jit(solution)/shard_map/ppermute | solution.py:390

commit v4 on v3

v4 whole, which is shorter than its diff:
```python
import functools

import jax
import jax.numpy as jnp
import numpy as np
from jax import lax
from jax.experimental import pallas as pl
from jax.experimental.pallas import tpu as pltpu
from jax.sharding import PartitionSpec as P

HEADS = 8
HEAD_DIM = 80
SPAN = 4
OWN_HEADS = HEADS // SPAN
PART = OWN_HEADS * HEAD_DIM
SCALE = HEAD_DIM**-0.5
LOG2E = 1.4426950408889634
NEG = -1e30
LANES = 128
HALF = HEAD_DIM // 2
PACK_MIB = 60

rope_base = 10000.0


def is_closed(count):
    return count in (SPAN, 2 * SPAN)


def trade_rounds(count):
    rounds = []
    for shift in [*range(1, SPAN), *range(-1, -SPAN, -1)]:
        pairs = [
            (source, source + shift)
            for source in range(max(0, -shift), min(count, count - shift))
            if (source < SPAN) == (source + shift < SPAN)
        ]
        rounds.append((shift, pairs))
    return rounds


def trade_tables(count):
    device = np.arange(count, dtype=np.int32)
    if is_closed(count):
        table = device // SPAN * SPAN + np.arange(SPAN, dtype=np.int32)[:, None]
        return table, table
    rounds = trade_rounds(count)
    sources = np.full((1 + len(rounds), count), -1, np.int32)
    targets = sources.copy()
    sources[0] = targets[0] = device
    for slot, (_, pairs) in enumerate(rounds, 1):
        for source, target in pairs:
            sources[slot, target] = source
            targets[slot, source] = target
    return sources, targets


def trade(slices, back=False):
    count = lax.axis_size("tok")
    if is_closed(count):
        groups = [list(range(begin, begin + SPAN)) for begin in range(0, count, SPAN)]
        return lax.all_to_all(slices, "tok", 0, 0, axis_index_groups=groups, tiled=True)
    moved = [slices[0]]
    for slot, (_, pairs) in enumerate(trade_rounds(count), 1):
        if back:
            pairs = [(target, source) for source, target in pairs]
        moved.append(lax.ppermute(slices[slot], "tok", pairs))
    return jnp.stack(moved)


def image_of(block, lengths, images):
    image = jnp.int32(0)
    start = jnp.int32(0)
    begin = jnp.int32(0)
    for number in range(images):
        size = lengths[0, number]
        inside = (block >= begin) & (block < begin + size)
        image = jnp.where(inside, number, image)
        start = jnp.where(inside, begin, start)
        begin = begin + size
    return image, start


def handler_of(start, residue, count):
    device = start + lax.rem(residue - lax.rem(start, SPAN) + SPAN, SPAN)
    return jnp.where(device >= count, device - SPAN, device)


def message_rows(tensor):
    return slice(tensor * HEAD_DIM, (tensor + 1) * HEAD_DIM)


def rotate(values, cosv, sinv):
    first, second = values[:HALF], values[HALF:]
    return jnp.concatenate([first * cosv - second * sinv, second * cosv + first * sinv], axis=0)


def unrotate(values, cosv, sinv):
    first, second = values[:HALF], values[HALF:]
    return jnp.concatenate([first * cosv + second * sinv, second * cosv - first * sinv], axis=0)


def phase_lanes(phase, model):
    size = SPAN * HEAD_DIM
    begin = phase * size // LANES * LANES
    end = -(-(phase + 1) * size // LANES) * LANES
    return begin, min(end, model)


def pack_kernel(phase, shifts, *refs):
    inputs, out, held, turned, sems = refs[:4], refs[4], refs[5], refs[6], refs[7]
    begin, end = phase_lanes(phase, inputs[0].shape[1])
    copies = [
        pltpu.make_async_copy(source.at[:, begin:end], held.at[number], sems.at[number])
        for number, source in enumerate(inputs)
    ]
    for copy in copies:
        copy.start()
    me = lax.axis_index("tok")
    inner = phase * SPAN * HEAD_DIM - begin
    for number, copy in enumerate(copies):
        copy.wait()
        turned[number] = held[number].T
        for slot in range(out.shape[0]):
            if shifts is None:
                rows = slice(inner + slot * HEAD_DIM, inner + (slot + 1) * HEAD_DIM)
            else:
                residue = lax.rem(me + shifts[slot] + SPAN, SPAN)
                rows = pl.ds(pl.multiple_of(inner + residue * HEAD_DIM, 16), HEAD_DIM)
            out[slot, message_rows(number), :] = turned[number, rows, :]


def tables_kernel(images, tokd, lengths, widths, table, inverse, bias, cos_out, sin_out, bias_out):
    me = lax.axis_index("tok")
    slots = table.shape[0]
    spot = lax.broadcasted_iota(jnp.int32, (HALF, tokd), 1)
    by_row = lax.broadcasted_iota(jnp.int32, (HALF, tokd), 0) < HALF // 2
    for slot in range(slots):
        block = table[slot, me]
        image, start = image_of(block, lengths, images)
        width = widths[0, image]
        bits = jnp.where(width == tokd, 0, jnp.where(width * 2 == tokd, 1, 2))
        shift = tokd.bit_length() - 1 - bits
        local = spot + (block - start) * tokd
        rowpos = lax.shift_right_logical(local, jnp.broadcast_to(shift, local.shape))
        colpos = local & (width - 1)
        angle = jnp.where(by_row, rowpos, colpos).astype(jnp.float32) * inverse[:, 0:1]
        cos_out[:, slot * tokd : (slot + 1) * tokd] = jnp.cos(angle)
        sin_out[:, slot * tokd : (slot + 1) * tokd] = jnp.sin(angle)
    plain = bias[...].astype(jnp.float32)
    rest = jnp.zeros((LANES - plain.shape[0], plain.shape[1]), jnp.float32)
    bias_out[...] = jnp.concatenate([plain, rest], axis=0).T


def attend_kernel(slots, count, images, tokd, head, factor, lengths, table, cosv, sinv, bias, *refs):
    if head > 0:
        before, refs = refs[0], refs[1:]
    msgs, outs, sums = refs[:3]
    qt_all, kt_all, vt_all, q_all, k_all, v_all, g_all, s_buf, e_buf, d_buf = refs[3:]
    me = lax.axis_index("tok")
    residue = lax.rem(me, SPAN)
    ids = []
    for slot in range(slots):
        block = table[slot, me]
        image, start = image_of(block, lengths, images)
        handled = (block >= 0) & (handler_of(start, residue, count) == me)
        ids.append(jnp.where(handled, image, -1 - slot))
    begin = pl.multiple_of((head * SPAN + residue) * HEAD_DIM, 16)
    own_bias = bias[pl.ds(begin, HEAD_DIM), :]
    rest_row = lax.broadcasted_iota(jnp.int32, (LANES - HEAD_DIM, tokd), 0)
    zeros = jnp.zeros((LANES - HEAD_DIM, tokd), jnp.float32)
    ones = jnp.where(rest_row < 2, 1.0, 0.0)

    def block_of(slot):
        return slice(slot * tokd, (slot + 1) * tokd)

    def stage(slot):
        at = block_of(slot)
        cos_b, sin_b = cosv[:, at], sinv[:, at]
        query, key, value = (
            msgs[slot, message_rows(tensor), :].astype(jnp.float32)
            + own_bias[:, tensor : tensor + 1]
            for tensor in range(3)
        )
        query = rotate(query, cos_b, sin_b) * (SCALE * LOG2E)
        for values, rest, turned, plain in (
            (query, zeros, qt_all, q_all),
            (rotate(key, cos_b, sin_b), zeros, kt_all, k_all),
            (value, ones, vt_all, v_all),
        ):
            values = jnp.concatenate([values, rest], axis=0).astype(jnp.bfloat16)
            turned[:, at] = values
            plain[at, :] = values.T

    def scores(slot, other):
        part = jnp.dot(
            k_all[block_of(other), :], qt_all[:, block_of(slot)], preferred_element_type=jnp.float32
        )
        s_buf[block_of(other), :] = part
        return jnp.max(part, axis=0, keepdims=True)

    def exponentials(slot, other, top):
        part = jnp.exp2(s_buf[block_of(other), :] - top)
        e_buf[block_of(other), block_of(slot)] = part.astype(jnp.bfloat16)

    def output(slot):
        mixed = jnp.dot(
            vt_all[...], e_buf[:, block_of(slot)], preferred_element_type=jnp.float32
        )
        inv = 1.0 / mixed[HEAD_DIM : HEAD_DIM + 1]
        out_b = (mixed[:HEAD_DIM] * inv).astype(jnp.bfloat16)
        outs[slot, message_rows(0), :] = out_b
        grad = msgs[slot, message_rows(3), :].astype(jnp.float32)
        delta = jnp.sum(grad * out_b.astype(jnp.float32), axis=0, keepdims=True) * inv
        coarse = delta.astype(jnp.bfloat16).astype(jnp.float32)
        rest = jnp.where(rest_row == 0, -coarse, jnp.where(rest_row == 1, coarse - delta, 0.0))
        grad = jnp.concatenate([grad * inv, rest], axis=0).astype(jnp.bfloat16)
        g_all[block_of(slot), :] = grad.T
        return grad

    def dscores(slot, other, grad):
        part = jnp.dot(v_all[block_of(other), :], grad, preferred_element_type=jnp.float32)
        d_buf[block_of(other), block_of(slot)] = (
            e_buf[block_of(other), block_of(slot)] * part.astype(jnp.bfloat16)
        )

    def query_part(slot):
        at = block_of(slot)
        dquery = jnp.dot(kt_all[:HEAD_DIM, :], d_buf[:, at], preferred_element_type=jnp.float32)
        dquery = unrotate(dquery * SCALE, cosv[:, at], sinv[:, at])
        outs[slot, message_rows(1), :] = dquery.astype(jnp.bfloat16)
        return jnp.where(ids[slot] >= 0, dquery, 0.0)

    for slot in range(slots):
        stage(slot)
    dq_total = jnp.zeros((HEAD_DIM, tokd), jnp.float32)
    grad = None
    for slot in range(slots + 1):
        if slot < slots:
            offs = [jnp.where(ids[slot] == ids[other], 0.0, NEG) for other in range(slots)]
            tops = [scores(slot, other) + offs[other] for other in range(slots)]
            top = functools.reduce(jnp.maximum, tops)
        for other in range(slots):
            if slot > 0:
                dscores(slot - 1, other, grad)
            if slot < slots:
                exponentials(slot, other, top - offs[other])
        if slot > 0:
            dq_total = dq_total + query_part(slot - 1)
        if slot < slots:
            grad = output(slot)
    dk_total = jnp.zeros((HEAD_DIM, tokd), jnp.float32)
    dv_total = jnp.zeros((1, LANES), jnp.float32)
    for slot in range(slots):
        at = block_of(slot)
        live = ids[slot] >= 0
        dvalue = jnp.dot(e_buf[at, :], g_all[...], preferred_element_type=jnp.float32)
        dv_total = dv_total + jnp.where(live, jnp.sum(dvalue, axis=0, keepdims=True), 0.0)
        outs[slot, message_rows(3), :] = dvalue.astype(jnp.bfloat16).T[:HEAD_DIM]
        dkey = jnp.dot(d_buf[at, :], q_all[...], preferred_element_type=jnp.float32)
        dkey = unrotate(dkey.T[:HEAD_DIM] * (1.0 / LOG2E), cosv[:, at], sinv[:, at])
        outs[slot, message_rows(2), :] = dkey.astype(jnp.bfloat16)
        dk_total = dk_total + jnp.where(live, dkey, 0.0)
    lane = lax.broadcasted_iota(jnp.int32, (HEAD_DIM, LANES), 1)
    columns = jnp.where(
        lane == 0,
        jnp.sum(dq_total, axis=1, keepdims=True),
        jnp.where(lane == 1, jnp.sum(dk_total, axis=1, keepdims=True), 0.0),
    )
    columns = jnp.concatenate([columns, jnp.zeros((LANES - HEAD_DIM, LANES), jnp.float32)], axis=0)
    lines = columns.T
    sums[...] = jnp.zeros_like(sums) if head == 0 else before[...]
    for number, total in enumerate((lines[0:1], lines[1:2], dv_total)):
        at = number * OWN_HEADS + head
        sums[at : at + 1, :] = total * factor


def unpack_kernel(closed, count, images, lengths, table, *refs):
    msgs, tiles = refs[:OWN_HEADS], refs[OWN_HEADS]
    outs, bias_out, held = refs[OWN_HEADS + 1 : -2], refs[-2], refs[-1]
    me = lax.axis_index("tok")
    if closed:
        for slot in range(SPAN):
            for phase in range(OWN_HEADS):
                begin = (phase * SPAN + slot) * HEAD_DIM
                for number in range(4):
                    held[number, begin : begin + HEAD_DIM, :] = msgs[phase][
                        slot, message_rows(number), :
                    ]
    else:
        _, start = image_of(me, lengths, images)
        for slot in range(table.shape[0]):
            source = table[slot, me]
            residue = lax.rem(source + SPAN, SPAN)

            @pl.when((source >= 0) & (source == handler_of(start, residue, count)))
            def _(slot=slot, residue=residue):
                for phase in range(OWN_HEADS):
                    begin = pl.multiple_of((phase * SPAN + residue) * HEAD_DIM, 16)
                    for number in range(4):
                        held[number, pl.ds(begin, HEAD_DIM), :] = msgs[phase][
                            slot, message_rows(number), :
                        ]

    for number, out in enumerate(outs):
        out[...] = held[number].T

    def add(group, totals):
        return tuple(
            total + tiles[group * SPAN + residue] for residue, total in enumerate(totals)
        )

    groups = tiles.shape[0] // SPAN
    zero = jnp.zeros(tiles.shape[1:], jnp.float32)
    totals = lax.fori_loop(0, groups, add, (zero,) * SPAN, unroll=groups <= 8)
    for residue, total in enumerate(totals):
        for phase in range(OWN_HEADS):
            begin = (phase * SPAN + residue) * HEAD_DIM
            for tensor in range(3):
                at = tensor * OWN_HEADS + phase
                bias_out[tensor : tensor + 1, begin : begin + HEAD_DIM] = total[
                    at : at + 1, :HEAD_DIM
                ]


def on_device(query_in, key_in, value_in, out_grad, bias, lengths, widths):
    tokd = query_in.shape[1]
    model = query_in.shape[2]
    images = lengths.shape[1]
    count = lax.axis_size("tok")
    dp_size = lax.axis_size("dp")
    closed = is_closed(count)
    sources, targets = trade_tables(count)
    slots = sources.shape[0]
    span = slots * tokd
    table = jnp.asarray(sources)
    shifts = None if closed else [0] + [shift for shift, _ in trade_rounds(count)]
    quarter = HEAD_DIM // 4
    inverse = rope_base ** (-np.arange(quarter, dtype=np.float64) / quarter)
    inverse = jnp.asarray(np.tile(np.tile(inverse, 2)[:, None], (1, LANES)), jnp.float32)
    smem = pl.BlockSpec(memory_space=pltpu.SMEM)
    vmem = pl.BlockSpec(memory_space=pltpu.VMEM)
    hbm = pl.BlockSpec(memory_space=pltpu.HBM)
    whole = jax.ShapeDtypeStruct((tokd, model), jnp.bfloat16)
    messages = jax.ShapeDtypeStruct((slots, 4 * HEAD_DIM, tokd), jnp.bfloat16)
    sums_shape = jax.ShapeDtypeStruct((8, LANES), jnp.float32)
    tokens_all = dp_size * count * tokd

    def params(mib):
        return pltpu.CompilerParams(vmem_limit_bytes=mib * 1024 * 1024)

    def pack(phase, inputs):
        begin, end = phase_lanes(phase, model)
        return pl.pallas_call(
            functools.partial(pack_kernel, phase, shifts),
            out_shape=messages,
            in_specs=[hbm] * 4,
            out_specs=vmem,
            scratch_shapes=[
                pltpu.VMEM((4, tokd, end - begin), jnp.bfloat16),
                pltpu.VMEM((4, end - begin, tokd), jnp.bfloat16),
                pltpu.SemaphoreType.DMA((4,)),
            ],
            compiler_params=params(PACK_MIB),
            name="pack_heads",
        )(*inputs)

    inputs = (query_in[0], key_in[0], value_in[0], out_grad[0])
    got = [trade(pack(0, inputs))]
    table_shape = jax.ShapeDtypeStruct((HALF, span), jnp.float32)
    tables = pl.pallas_call(
        functools.partial(tables_kernel, images, tokd),
        out_shape=[table_shape] * 2 + [jax.ShapeDtypeStruct((model, LANES), jnp.float32)],
        in_specs=[smem, smem, smem, vmem, vmem],
        out_specs=[vmem] * 3,
        compiler_params=params(16),
        cost_estimate=pl.CostEstimate(
            flops=span * LANES * 200, bytes_accessed=0, transcendentals=0
        ),
        name="rotary_tables",
    )(lengths, widths, table, inverse, bias)
    for phase in range(1, OWN_HEADS):
        tables, inputs = lax.optimization_barrier((tables, inputs))
        packed = pack(phase, inputs)
        got[0], packed = lax.optimization_barrier((got[0], packed))
        got.append(trade(packed))
    back = []
    sums = []
    for phase in range(OWN_HEADS):
        results, total = pl.pallas_call(
            functools.partial(
                attend_kernel, slots, count, images, tokd, phase, 1.0 / tokens_all**0.5
            ),
            out_shape=[messages, sums_shape],
            in_specs=[smem, smem] + [vmem] * (4 + len(sums)),
            out_specs=[vmem] * 2,
            scratch_shapes=[pltpu.VMEM((LANES, span), jnp.bfloat16)] * 3
            + [pltpu.VMEM((span, LANES), jnp.bfloat16)] * 4
            + [pltpu.VMEM((span, tokd), jnp.float32)]
            + [pltpu.VMEM((span, span), jnp.bfloat16)] * 2,
            compiler_params=params(32),
            cost_estimate=pl.CostEstimate(
                flops=12 * span * span * 256, bytes_accessed=0, transcendentals=0
            ),
            name="attend_head",
        )(lengths, table, *tables, *sums, got[phase])
        sums = [total]
        back.append(trade(results, back=True))
    total, early = lax.optimization_barrier((sums[0], back[:-1]))
    back[:-1] = early
    tiles = total[None]
    for axis, size in (("dp", dp_size), ("tok", count)):
        tiles = jnp.sum(tiles, axis=0)
        tiles = jnp.broadcast_to(tiles[None], (size,) + total.shape)
        tiles = lax.all_to_all(tiles, axis, 0, 0, tiled=True)
    *outs, bias_grad = pl.pallas_call(
        functools.partial(unpack_kernel, closed, count, images),
        out_shape=[whole] * 4 + [jax.ShapeDtypeStruct((3, model), jnp.float32)],
        in_specs=[smem, smem] + [vmem] * (OWN_HEADS + 1),
        out_specs=[vmem] * 5,
        scratch_shapes=[pltpu.VMEM((4, model, tokd), jnp.bfloat16)],
        compiler_params=params(16),
        name="unpack_heads",
    )(lengths, jnp.asarray(targets), *back, tiles)
    return tuple(out[None] for out in outs) + (bias_grad,)


def solution(mesh):
    in_specs = (
        P("dp", "tok", None),
        P("dp", "tok", None),
        P("dp", "tok", None),
        P("dp", "tok", None),
        P(),
        P("dp", None),
        P("dp", None),
    )
    out_specs = (
        P("dp", "tok", None),
        P("dp", "tok", None),
        P("dp", "tok", None),
        P("dp", "tok", None),
        P(),
    )
    return jax.shard_map(
        on_device, mesh=mesh, in_specs=in_specs, out_specs=out_specs, check_vma=False
    )
```

time: 53.8 us -> 74.1 us (1.38)
  blocking collectives: 0 us -> 28.7 us
  starting transfers between devices: 21.3 us -> 12.3 us
  Pallas kernels: 15.7 us -> 18.2 us
  local copies, waits for them, and re-layouts: 1.61 us -> 0.04 us
  waiting for transfers between devices: 14.3 us -> 13.5 us
    all_to_all x0 -> x3, blocking collectives: none -> 28.7 us  [the longest x2 17.6 us: on_device(): tiles = lax.all_to_all(tiles, axis, 0, 0, tiled=True)]
    ppermute x12 -> x0, starting transfers between devices: 16.5 us -> none  [the longest x6 10.5 us: on_device(): lax.ppermute(send, 'tok', pairs)]
    ppermute x12 -> x0, waiting for transfers between devices: 14.3 us -> none  [the longest x6 10.6 us: on_device(): lax.ppermute(result, 'tok', [(target, source) for source, target in pairs])]
    all_to_all x1 -> x3, waiting for transfers between devices: 0.01 us -> 13.5 us  [trade(): lax.all_to_all(slices, 'tok', 0, 0, axis_index_groups=groups, tiled=True)]
    all_to_all x1 -> x3, starting transfers between devices: 4.82 us -> 12.3 us  [trade(): lax.all_to_all(slices, 'tok', 0, 0, axis_index_groups=groups, tiled=True)]
    pallas_call x2 -> x3, Pallas kernels: 4.66 us -> 6.31 us  [the longest x2 4.48 us: pack(): pl.pallas_call(functools.partial(pack_kernel, phase, shifts), out_shape=m...]
    unnamed x16 -> x10, local copies, waits for them, and re-layouts: 0.95 us -> 0.03 us
    pallas_call x2, Pallas kernels: 9.86 us -> 10.7 us  [on_device(): pl.pallas_call(functools.partial(attend_kernel, slots, count, images, tok...]
  transfers between devices with their start and end apart: 13 -> 3, of which waited for: 7 -> 3; matrix products, arithmetic and copies ran while one was open for 0% -> 0% of each run, Pallas kernels for 21% -> 19%
where the time goes in v4:
time: 74.1 us; the launch traced here: 73.6 us
  blocking collectives  28.7 us (39%)
  Pallas kernels  18.2 us (25%)
  waiting for transfers between devices  13.5 us (18%)
  starting transfers between devices  12.3 us (17%)
    all_to_all x2, blocking collectives, on_device(): tiles = lax.all_to_all(tiles, axis, 0, 0, tiled=True)  17.6 us
    all_to_all x3, waiting for transfers between devices, trade(): lax.all_to_all(slices, 'tok', 0, 0, axis_index_groups=groups, tiled=True)  13.5 us
    all_to_all x3, starting transfers between devices, trade(): lax.all_to_all(slices, 'tok', 0, 0, axis_index_groups=groups, tiled=True)  12.3 us
    all_to_all x1, blocking collectives, trade(): lax.all_to_all(slices, 'tok', 0, 0, axis_index_groups=groups, tiled=True)  11.1 us
    pallas_call x2, Pallas kernels, on_device(): pl.pallas_call(functools.partial(attend_kernel, slots, count, images, tok...  10.7 us
    pallas_call x2, Pallas kernels, pack(): pl.pallas_call(functools.partial(pack_kernel, phase, shifts), out_shape=m...  4.48 us
    pallas_call x1, Pallas kernels, on_device(): pl.pallas_call(functools.partial(unpack_kernel, closed, count, images), o...  1.84 us
  transfers between devices with their start and end apart: 3, of which 3 were waited for; matrix products, arithmetic and copies ran while one was open for 0% of the time, Pallas kernels for 19%

profile of v4, /device:TPU:0, one launch (start us, length us, event | category | flops | bytes accessed | tf_op | source)
XLA Modules:
  0.0 73.6 jit_solution(12169048519617179927)
XLA Ops:
  0.6 2.2 %pack_heads.2 = bf16[4,320,256]{2,1,0:T(8,128)(2,1)} custom-call(bf16[256,640]{1,0:T(8,128)(2,1)} %bitcast.8, bf16[256,640]{1,0:T(8,128)(2,1)} %bitcast.10, bf16[256,640]{1,0:T(8,128)(2,1)} %bitcast.12, bf16[256,640]{1,0:T(8,128)(2,1)} %bitcast.14), custom_call_target="tpu_custom_call" | custom-call | tf_op jit(solution)/shard_map/pack_heads/pallas_call | solution.py:354
  2.9 0.0 copy-start
  2.9 0.0 copy-start.1
  2.9 0.0 copy-start.2
  2.9 0.0 copy-start.3
  2.9 0.0 copy-start.4
  2.9 5.4 %all-to-all-start = ((bf16[4,320,256]{2,1,0:T(8,128)(2,1)}), bf16[4,320,256]{2,1,0:T(8,128)(2,1)S(1)}, u32[]{:S(2)}, u32[]{:S(2)}) async-start(bf16[4,320,256]{2,1,0:T(8,128)(2,1)} %pack_heads.2), calls=%async_computation | async-start | bytes 1310720 | tf_op jit(solution)/shard_map/all_to_all | solution.py:62
  8.3 0.0 copy-done
  8.3 0.0 copy-done.1
  8.3 0.0 copy-done.2
  8.3 0.0 copy-done.3
  8.3 0.0 copy-done.4
  8.3 1.2 %rotary_tables.1 = (f32[40,1024]{1,0:T(8,128)S(1)}, f32[40,1024]{1,0:T(8,128)S(1)}, f32[640,128]{1,0:T(8,128)S(1)}) custom-call(s32[1,4]{1,0:T(1,128)S(1)} %copy-done.1, s32[1,4]{1,0:T(1,128)S(1)} %copy-done.3, s32[4,8]{1,0:T(4,128)S(1)} %copy-done, f32[40,128]{1,0:T(8,128)S(1)} %copy-done.4, bf16[3,640]{1,0:T(4,128)(2,1)S(1)} %copy-done.2), custom_call_target="tpu_custom_call" | custom-call | flops 26214400 | tf_op jit(solution)/shard_map/rotary_tables/pallas_call | solution.py:371
  9.6 2.2 %pack_heads.3 = bf16[4,320,256]{2,1,0:T(8,128)(2,1)} custom-call(bf16[256,640]{1,0:T(8,128)(2,1)} %bitcast.9, bf16[256,640]{1,0:T(8,128)(2,1)} %bitcast.11, bf16[256,640]{1,0:T(8,128)(2,1)} %bitcast.13, bf16[256,640]{1,0:T(8,128)(2,1)} %bitcast.15), custom_call_target="tpu_custom_call" | custom-call | tf_op jit(solution)/shard_map/pack_heads/pallas_call | solution.py:354
  11.8 5.9 %all-to-all-done.refs_0_ = bf16[4,320,256]{2,1,0:T(8,128)(2,1)S(1)} async-done(((bf16[4,320,256]{2,1,0:T(8,128)(2,1)}), bf16[4,320,256]{2,1,0:T(8,128)(2,1)S(1)}, u32[]{:S(2)}, u32[]{:S(2)}) %all-to-all-start) | async-done | bytes 655392 | tf_op jit(solution)/shard_map/all_to_all | solution.py:62
  17.7 3.5 %all-to-all-start.1 = ((bf16[4,320,256]{2,1,0:T(8,128)(2,1)}), bf16[4,320,256]{2,1,0:T(8,128)(2,1)S(1)}, u32[]{:S(2)}, u32[]{:S(2)}) async-start(bf16[4,320,256]{2,1,0:T(8,128)(2,1)} %pack_heads.3), calls=%async_computation.1 | async-start | bytes 1310720 | tf_op jit(solution)/shard_map/all_to_all | solution.py:62
  21.2 5.7 %attend_head.2 = (bf16[4,320,256]{2,1,0:T(8,128)(2,1)}, f32[8,128]{1,0:T(8,128)S(1)}) custom-call(s32[1,4]{1,0:T(1,128)S(1)} %copy-done.1, s32[4,8]{1,0:T(4,128)S(1)} %copy-done, f32[40,1024]{1,0:T(8,128)S(1)} %get-tuple-element.31.cosv, f32[40,1024]{1,0:T(8,128)S(1)} %get-tuple-element.32.sinv, f32[640,128]{1,0:T(8,128)S(1)} %get-tuple-element.33.bias, ...), custom_call_target="tpu_custom_call" | custom-call | flops 3221225472 | tf_op jit(solution)/shard_map/attend_head/pallas_call | solution.py:390
  27.0 3.8 %all-to-all-done.1.refs_1_ = bf16[4,320,256]{2,1,0:T(8,128)(2,1)S(1)} async-done(((bf16[4,320,256]{2,1,0:T(8,128)(2,1)}), bf16[4,320,256]{2,1,0:T(8,128)(2,1)S(1)}, u32[]{:S(2)}, u32[]{:S(2)}) %all-to-all-start.1) | async-done | bytes 655392 | tf_op jit(solution)/shard_map/all_to_all | solution.py:62
  30.8 3.5 %all-to-all-start.2 = ((bf16[4,320,256]{2,1,0:T(8,128)(2,1)}), bf16[4,320,256]{2,1,0:T(8,128)(2,1)S(1)}, u32[]{:S(2)}, u32[]{:S(2)}) async-start(bf16[4,320,256]{2,1,0:T(8,128)(2,1)} %get-tuple-element.42), calls=%async_computation.2 | async-start | bytes 1310720 | tf_op jit(solution)/shard_map/all_to_all | solution.py:62
  34.2 4.9 %attend_head.3 = (bf16[4,320,256]{2,1,0:T(8,128)(2,1)S(1)}, f32[8,128]{1,0:T(8,128)S(1)}) custom-call(s32[1,4]{1,0:T(1,128)S(1)} %copy-done.1, s32[4,8]{1,0:T(4,128)S(1)} %copy-done, f32[40,1024]{1,0:T(8,128)S(1)} %get-tuple-element.31.cosv, f32[40,1024]{1,0:T(8,128)S(1)} %get-tuple-element.32.sinv, f32[640,128]{1,0:T(8,128)S(1)} %get-tuple-element.33.bias, ...), custom_call_target="tpu_custom_call" | custom-call | flops 3221225472 | tf_op jit(solution)/shard_map/attend_head/pallas_call | solution.py:390
  39.2 3.8 %all-to-all-done.2.refs_0_ = bf16[4,320,256]{2,1,0:T(8,128)(2,1)S(1)} async-done(((bf16[4,320,256]{2,1,0:T(8,128)(2,1)}), bf16[4,320,256]{2,1,0:T(8,128)(2,1)S(1)}, u32[]{:S(2)}, u32[]{:S(2)}) %all-to-all-start.2) | async-done | bytes 655392 | tf_op jit(solution)/shard_map/all_to_all | solution.py:62
  43.0 6.4 %all_to_all.30 = f32[4,8,128]{2,1,0:T(8,128)S(1)} all-to-all(f32[4,8,128]{2,1,0:T(8,128)S(1)} %broadcast_in_dim.12), channel_id=1, replica_groups=mesh['dp'=4,'tok'=8] {'dp'}, dimensions={0} | all-to-all | bytes 32768 | tf_op jit(solution)/shard_map/all_to_all | solution.py:415
  49.4 11.2 %all_to_all.31.refs_2_ = f32[8,8,128]{2,1,0:T(8,128)S(1)} all-to-all(f32[8,8,128]{2,1,0:T(8,128)S(1)} %broadcast_in_dim.26), channel_id=1, replica_groups=mesh['dp'=4,'tok'=8] {'tok'}, dimensions={0} | all-to-all | bytes 65536 | tf_op jit(solution)/shard_map/all_to_all | solution.py:415
  60.6 11.1 %all_to_all.32.refs_1_ = bf16[4,320,256]{2,1,0:T(8,128)(2,1)S(1)} all-to-all(bf16[4,320,256]{2,1,0:T(8,128)(2,1)S(1)} %get-tuple-element.44), channel_id=1, replica_groups={{0,1,2,3},{4,5,6,7},{8,9,10,11},{12,13,14,15},{16,17,18,19},{20,21,22,2..., dimensions={0} | all-to-all | bytes 1310720 | tf_op jit(solution)/shard_map/all_to_all | solution.py:62
  71.7 1.8 %unpack_heads.1 = (bf16[256,640]{1,0:T(8,128)(2,1)}, bf16[256,640]{1,0:T(8,128)(2,1)}, bf16[256,640]{1,0:T(8,128)(2,1)}, bf16[256,640]{1,0:T(8,128)(2,1)}, f32[3,640]{1,0:T(4,128)}) custom-call(s32[1,4]{1,0:T(1,128)S(1)} %copy-done.1, s32[4,8]{1,0:T(4,128)S(1)} %copy-done, bf16[4,320,256]{2,1,0:T(8,128)(2,1)S(1)} %all-to-all-done.2.refs_0_, ...), custom_call_target="tpu_custom_call" | custom-call | tf_op jit(solution)/shard_map/unpack_heads/pallas_call | solution.py:416
  (3 shorter events, 0.0 us)
Async XLA Ops:
  2.9 5.4 %copy-start = (s32[4,8]{1,0:T(4,128)S(1)}, s32[4,8]{1,0:T(4,128)}, u32[]{:S(2)}) copy-start(s32[4,8]{1,0:T(4,128)} %constant.6.clone.table) | copy-start | bytes 388
  2.9 5.4 %copy-start.1 = (s32[1,4]{1,0:T(1,128)S(1)}, s32[1,4]{1,0:T(1,128)}, u32[]{:S(2)}) copy-start(s32[1,4]{1,0:T(1,128)} %lengths.7) | copy-start | bytes 52
  2.9 5.4 %copy-start.2 = (bf16[3,640]{1,0:T(4,128)(2,1)S(1)}, bf16[3,640]{1,0:T(4,128)(2,1)}, u32[]{:S(2)}) copy-start(bf16[3,640]{1,0:T(4,128)(2,1)} %bias.1) | copy-start | bytes 11524
  2.9 5.4 %copy-start.3 = (s32[1,4]{1,0:T(1,128)S(1)}, s32[1,4]{1,0:T(1,128)}, u32[]{:S(2)}) copy-start(s32[1,4]{1,0:T(1,128)} %widths.1) | copy-start | bytes 52
  2.9 5.4 %copy-start.4 = (f32[40,128]{1,0:T(8,128)S(1)}, f32[40,128]{1,0:T(8,128)}, u32[]{:S(2)}) copy-start(f32[40,128]{1,0:T(8,128)} %constant.7.clone.inverse) | copy-start | bytes 61444
  2.9 14.8 %all-to-all-start = ((bf16[4,320,256]{2,1,0:T(8,128)(2,1)}), bf16[4,320,256]{2,1,0:T(8,128)(2,1)S(1)}, u32[]{:S(2)}, u32[]{:S(2)}) async-start(bf16[4,320,256]{2,1,0:T(8,128)(2,1)} %pack_heads.2), calls=%async_computation | async-start | bytes 1310720 | tf_op jit(solution)/shard_map/all_to_all | solution.py:62
  17.7 13.0 %all-to-all-start.1 = ((bf16[4,320,256]{2,1,0:T(8,128)(2,1)}), bf16[4,320,256]{2,1,0:T(8,128)(2,1)S(1)}, u32[]{:S(2)}, u32[]{:S(2)}) async-start(bf16[4,320,256]{2,1,0:T(8,128)(2,1)} %pack_heads.3), calls=%async_computation.1 | async-start | bytes 1310720 | tf_op jit(solution)/shard_map/all_to_all | solution.py:62
  30.8 12.2 %all-to-all-start.2 = ((bf16[4,320,256]{2,1,0:T(8,128)(2,1)}), bf16[4,320,256]{2,1,0:T(8,128)(2,1)S(1)}, u32[]{:S(2)}, u32[]{:S(2)}) async-start(bf16[4,320,256]{2,1,0:T(8,128)(2,1)} %get-tuple-element.42), calls=%async_computation.2 | async-start | bytes 1310720 | tf_op jit(solution)/shard_map/all_to_all | solution.py:62

commit v5 on v4

--- a/solution.py
+++ b/solution.py
@@ -19,6 +19,7 @@
 LANES = 128
 HALF = HEAD_DIM // 2
 PACK_MIB = 60
+UNPACK_FLOPS = 20_000_000_000
 
 rope_base = 10000.0
 
@@ -28,27 +29,26 @@
 
 
 def trade_rounds(count):
+    if is_closed(count):
+        return [[(one, one ^ step) for one in range(count)] for step in range(SPAN - 1, 0, -1)]
     rounds = []
     for shift in [*range(1, SPAN), *range(-1, -SPAN, -1)]:
-        pairs = [
-            (source, source + shift)
-            for source in range(max(0, -shift), min(count, count - shift))
-            if (source < SPAN) == (source + shift < SPAN)
-        ]
-        rounds.append((shift, pairs))
+        rounds.append(
+            [
+                (source, source + shift)
+                for source in range(max(0, -shift), min(count, count - shift))
+                if (source < SPAN) == (source + shift < SPAN)
+            ]
+        )
     return rounds
 
 
 def trade_tables(count):
-    device = np.arange(count, dtype=np.int32)
-    if is_closed(count):
-        table = device // SPAN * SPAN + np.arange(SPAN, dtype=np.int32)[:, None]
-        return table, table
     rounds = trade_rounds(count)
     sources = np.full((1 + len(rounds), count), -1, np.int32)
     targets = sources.copy()
-    sources[0] = targets[0] = device
-    for slot, (_, pairs) in enumerate(rounds, 1):
+    sources[0] = targets[0] = np.arange(count)
+    for slot, pairs in enumerate(rounds, 1):
         for source, target in pairs:
             sources[slot, target] = source
             targets[slot, source] = target
@@ -56,16 +56,12 @@
 
 
 def trade(slices, back=False):
-    count = lax.axis_size("tok")
-    if is_closed(count):
-        groups = [list(range(begin, begin + SPAN)) for begin in range(0, count, SPAN)]
-        return lax.all_to_all(slices, "tok", 0, 0, axis_index_groups=groups, tiled=True)
     moved = [slices[0]]
-    for slot, (_, pairs) in enumerate(trade_rounds(count), 1):
+    for slot, pairs in enumerate(trade_rounds(lax.axis_size("tok")), 1):
         if back:
             pairs = [(target, source) for source, target in pairs]
         moved.append(lax.ppermute(slices[slot], "tok", pairs))
-    return jnp.stack(moved)
+    return moved
 
 
 def image_of(block, lengths, images):
@@ -107,8 +103,8 @@
     return begin, min(end, model)
 
 
-def pack_kernel(phase, shifts, *refs):
-    inputs, out, held, turned, sems = refs[:4], refs[4], refs[5], refs[6], refs[7]
+def pack_kernel(phase, closed, *refs):
+    inputs, outs, held, turned, sems = refs[:4], refs[4:-3], refs[-3], refs[-2], refs[-1]
     begin, end = phase_lanes(phase, inputs[0].shape[1])
     copies = [
         pltpu.make_async_copy(source.at[:, begin:end], held.at[number], sems.at[number])
@@ -116,18 +112,18 @@
     ]
     for copy in copies:
         copy.start()
-    me = lax.axis_index("tok")
+    me = lax.rem(lax.axis_index("tok"), SPAN)
     inner = phase * SPAN * HEAD_DIM - begin
+    steps = [0] + (
+        [*range(SPAN - 1, 0, -1)] if closed else [*range(1, SPAN), *range(SPAN - 1, 0, -1)]
+    )
     for number, copy in enumerate(copies):
         copy.wait()
         turned[number] = held[number].T
-        for slot in range(out.shape[0]):
-            if shifts is None:
-                rows = slice(inner + slot * HEAD_DIM, inner + (slot + 1) * HEAD_DIM)
-            else:
-                residue = lax.rem(me + shifts[slot] + SPAN, SPAN)
-                rows = pl.ds(pl.multiple_of(inner + residue * HEAD_DIM, 16), HEAD_DIM)
-            out[slot, message_rows(number), :] = turned[number, rows, :]
+        for out, step in zip(outs, steps):
+            residue = me ^ step if closed else lax.rem(me + step, SPAN)
+            rows = pl.ds(pl.multiple_of(inner + residue * HEAD_DIM, 16), HEAD_DIM)
+            out[message_rows(number), :] = turned[number, rows, :]
 
 
 def tables_kernel(images, tokd, lengths, widths, table, inverse, bias, cos_out, sin_out, bias_out):
@@ -155,8 +151,8 @@
 def attend_kernel(slots, count, images, tokd, head, factor, lengths, table, cosv, sinv, bias, *refs):
     if head > 0:
         before, refs = refs[0], refs[1:]
-    msgs, outs, sums = refs[:3]
-    qt_all, kt_all, vt_all, q_all, k_all, v_all, g_all, s_buf, e_buf, d_buf = refs[3:]
+    msgs, outs, sums = refs[:slots], refs[slots : 2 * slots], refs[2 * slots]
+    qt_all, kt_all, vt_all, q_all, k_all, v_all, g_all, s_buf, e_buf, d_buf = refs[2 * slots + 1 :]
     me = lax.axis_index("tok")
     residue = lax.rem(me, SPAN)
     ids = []
@@ -178,7 +174,7 @@
         at = block_of(slot)
         cos_b, sin_b = cosv[:, at], sinv[:, at]
         query, key, value = (
-            msgs[slot, message_rows(tensor), :].astype(jnp.float32)
+            msgs[slot][message_rows(tensor), :].astype(jnp.float32)
             + own_bias[:, tensor : tensor + 1]
             for tensor in range(3)
         )
@@ -209,8 +205,8 @@
         )
         inv = 1.0 / mixed[HEAD_DIM : HEAD_DIM + 1]
         out_b = (mixed[:HEAD_DIM] * inv).astype(jnp.bfloat16)
-        outs[slot, message_rows(0), :] = out_b
-        grad = msgs[slot, message_rows(3), :].astype(jnp.float32)
+        outs[slot][message_rows(0), :] = out_b
+        grad = msgs[slot][message_rows(3), :].astype(jnp.float32)
         delta = jnp.sum(grad * out_b.astype(jnp.float32), axis=0, keepdims=True) * inv
         coarse = delta.astype(jnp.bfloat16).astype(jnp.float32)
         rest = jnp.where(rest_row == 0, -coarse, jnp.where(rest_row == 1, coarse - delta, 0.0))
@@ -228,7 +224,7 @@
         at = block_of(slot)
         dquery = jnp.dot(kt_all[:HEAD_DIM, :], d_buf[:, at], preferred_element_type=jnp.float32)
         dquery = unrotate(dquery * SCALE, cosv[:, at], sinv[:, at])
-        outs[slot, message_rows(1), :] = dquery.astype(jnp.bfloat16)
+        outs[slot][message_rows(1), :] = dquery.astype(jnp.bfloat16)
         return jnp.where(ids[slot] >= 0, dquery, 0.0)
 
     for slot in range(slots):
@@ -256,10 +252,10 @@
         live = ids[slot] >= 0
         dvalue = jnp.dot(e_buf[at, :], g_all[...], preferred_element_type=jnp.float32)
         dv_total = dv_total + jnp.where(live, jnp.sum(dvalue, axis=0, keepdims=True), 0.0)
-        outs[slot, message_rows(3), :] = dvalue.astype(jnp.bfloat16).T[:HEAD_DIM]
+        outs[slot][message_rows(3), :] = dvalue.astype(jnp.bfloat16).T[:HEAD_DIM]
         dkey = jnp.dot(d_buf[at, :], q_all[...], preferred_element_type=jnp.float32)
         dkey = unrotate(dkey.T[:HEAD_DIM] * (1.0 / LOG2E), cosv[:, at], sinv[:, at])
-        outs[slot, message_rows(2), :] = dkey.astype(jnp.bfloat16)
+        outs[slot][message_rows(2), :] = dkey.astype(jnp.bfloat16)
         dk_total = dk_total + jnp.where(live, dkey, 0.0)
     lane = lax.broadcasted_iota(jnp.int32, (HEAD_DIM, LANES), 1)
     columns = jnp.where(
@@ -275,36 +271,31 @@
         sums[at : at + 1, :] = total * factor
 
 
-def unpack_kernel(closed, count, images, lengths, table, *refs):
-    msgs, tiles = refs[:OWN_HEADS], refs[OWN_HEADS]
-    outs, bias_out, held = refs[OWN_HEADS + 1 : -2], refs[-2], refs[-1]
+def unpack_kernel(slots, count, images, lengths, table, *refs):
+    msgs, outs, held = refs[: OWN_HEADS * slots], refs[OWN_HEADS * slots : -1], refs[-1]
     me = lax.axis_index("tok")
-    if closed:
-        for slot in range(SPAN):
+    _, start = image_of(me, lengths, images)
+    for slot in range(slots):
+        source = table[slot, me]
+        residue = lax.rem(source + SPAN, SPAN)
+
+        def place(slot=slot, residue=residue):
             for phase in range(OWN_HEADS):
-                begin = (phase * SPAN + slot) * HEAD_DIM
+                begin = pl.multiple_of((phase * SPAN + residue) * HEAD_DIM, 16)
                 for number in range(4):
-                    held[number, begin : begin + HEAD_DIM, :] = msgs[phase][
-                        slot, message_rows(number), :
+                    held[number, pl.ds(begin, HEAD_DIM), :] = msgs[phase * slots + slot][
+                        message_rows(number), :
                     ]
-    else:
-        _, start = image_of(me, lengths, images)
-        for slot in range(table.shape[0]):
-            source = table[slot, me]
-            residue = lax.rem(source + SPAN, SPAN)
-
-            @pl.when((source >= 0) & (source == handler_of(start, residue, count)))
-            def _(slot=slot, residue=residue):
-                for phase in range(OWN_HEADS):
-                    begin = pl.multiple_of((phase * SPAN + residue) * HEAD_DIM, 16)
-                    for number in range(4):
-                        held[number, pl.ds(begin, HEAD_DIM), :] = msgs[phase][
-                            slot, message_rows(number), :
-                        ]
-
+
+        if is_closed(count):
+            place()
+        else:
+            pl.when((source >= 0) & (source == handler_of(start, residue, count)))(place)
     for number, out in enumerate(outs):
         out[...] = held[number].T
 
+
+def bias_kernel(tiles, bias_out):
     def add(group, totals):
         return tuple(
             total + tiles[group * SPAN + residue] for residue, total in enumerate(totals)
@@ -334,7 +325,6 @@
     slots = sources.shape[0]
     span = slots * tokd
     table = jnp.asarray(sources)
-    shifts = None if closed else [0] + [shift for shift, _ in trade_rounds(count)]
     quarter = HEAD_DIM // 4
     inverse = rope_base ** (-np.arange(quarter, dtype=np.float64) / quarter)
     inverse = jnp.asarray(np.tile(np.tile(inverse, 2)[:, None], (1, LANES)), jnp.float32)
@@ -342,7 +332,7 @@
     vmem = pl.BlockSpec(memory_space=pltpu.VMEM)
     hbm = pl.BlockSpec(memory_space=pltpu.HBM)
     whole = jax.ShapeDtypeStruct((tokd, model), jnp.bfloat16)
-    messages = jax.ShapeDtypeStruct((slots, 4 * HEAD_DIM, tokd), jnp.bfloat16)
+    messages = [jax.ShapeDtypeStruct((4 * HEAD_DIM, tokd), jnp.bfloat16)] * slots
     sums_shape = jax.ShapeDtypeStruct((8, LANES), jnp.float32)
     tokens_all = dp_size * count * tokd
 
@@ -352,10 +342,10 @@
     def pack(phase, inputs):
         begin, end = phase_lanes(phase, model)
         return pl.pallas_call(
-            functools.partial(pack_kernel, phase, shifts),
+            functools.partial(pack_kernel, phase, closed),
             out_shape=messages,
             in_specs=[hbm] * 4,
-            out_specs=vmem,
+            out_specs=[vmem] * slots,
             scratch_shapes=[
                 pltpu.VMEM((4, tokd, end - begin), jnp.bfloat16),
                 pltpu.VMEM((4, end - begin, tokd), jnp.bfloat16),
@@ -382,18 +372,18 @@
     for phase in range(1, OWN_HEADS):
         tables, inputs = lax.optimization_barrier((tables, inputs))
         packed = pack(phase, inputs)
-        got[0], packed = lax.optimization_barrier((got[0], packed))
+        tables, packed = lax.optimization_barrier((tables, packed))
         got.append(trade(packed))
     back = []
     sums = []
     for phase in range(OWN_HEADS):
-        results, total = pl.pallas_call(
+        *results, total = pl.pallas_call(
             functools.partial(
                 attend_kernel, slots, count, images, tokd, phase, 1.0 / tokens_all**0.5
             ),
-            out_shape=[messages, sums_shape],
-            in_specs=[smem, smem] + [vmem] * (4 + len(sums)),
-            out_specs=[vmem] * 2,
+            out_shape=messages + [sums_shape],
+            in_specs=[smem, smem] + [vmem] * (3 + len(sums) + slots),
+            out_specs=[vmem] * (slots + 1),
             scratch_shapes=[pltpu.VMEM((LANES, span), jnp.bfloat16)] * 3
             + [pltpu.VMEM((span, LANES), jnp.bfloat16)] * 4
             + [pltpu.VMEM((span, tokd), jnp.float32)]
@@ -403,25 +393,35 @@
                 flops=12 * span * span * 256, bytes_accessed=0, transcendentals=0
             ),
             name="attend_head",
-        )(lengths, table, *tables, *sums, got[phase])
+        )(lengths, table, *tables, *sums, *got[phase])
         sums = [total]
+        if phase + 1 < OWN_HEADS:
+            results, got[phase + 1] = lax.optimization_barrier((results, got[phase + 1]))
         back.append(trade(results, back=True))
     total, early = lax.optimization_barrier((sums[0], back[:-1]))
     back[:-1] = early
-    tiles = total[None]
-    for axis, size in (("dp", dp_size), ("tok", count)):
-        tiles = jnp.sum(tiles, axis=0)
-        tiles = jnp.broadcast_to(tiles[None], (size,) + total.shape)
-        tiles = lax.all_to_all(tiles, axis, 0, 0, tiled=True)
-    *outs, bias_grad = pl.pallas_call(
-        functools.partial(unpack_kernel, closed, count, images),
-        out_shape=[whole] * 4 + [jax.ShapeDtypeStruct((3, model), jnp.float32)],
-        in_specs=[smem, smem] + [vmem] * (OWN_HEADS + 1),
-        out_specs=[vmem] * 5,
+    devices = dp_size * count
+    tiles = jnp.broadcast_to(total[None], (devices,) + total.shape)
+    tiles = lax.all_to_all(tiles, ("dp", "tok"), 0, 0, tiled=True)
+    outs = pl.pallas_call(
+        functools.partial(unpack_kernel, slots, count, images),
+        out_shape=[whole] * 4,
+        in_specs=[smem, smem] + [vmem] * (OWN_HEADS * slots),
+        out_specs=[vmem] * 4,
         scratch_shapes=[pltpu.VMEM((4, model, tokd), jnp.bfloat16)],
         compiler_params=params(16),
+        cost_estimate=pl.CostEstimate(flops=UNPACK_FLOPS, bytes_accessed=0, transcendentals=0),
         name="unpack_heads",
-    )(lengths, jnp.asarray(targets), *back, tiles)
+    )(lengths, jnp.asarray(targets), *(result for results in back for result in results))
+    outs, tiles = lax.optimization_barrier((outs, tiles))
+    bias_grad = pl.pallas_call(
+        bias_kernel,
+        out_shape=jax.ShapeDtypeStruct((3, model), jnp.float32),
+        in_specs=[vmem],
+        out_specs=vmem,
+        compiler_params=params(16),
+        name="bias_sums",
+    )(tiles)
     return tuple(out[None] for out in outs) + (bias_grad,)
 
 

time: 74.1 us -> 49.2 us (0.66)
  blocking collectives: 28.7 us -> 0 us
  starting transfers between devices: 12.3 us -> 21 us
  waiting for transfers between devices: 13.5 us -> 8.29 us
    all_to_all x3 -> x0, blocking collectives: 28.7 us -> none  [the longest x2 17.6 us: on_device(): tiles = lax.all_to_all(tiles, axis, 0, 0, tiled=True)]
    ppermute x0 -> x12, starting transfers between devices: none -> 15.2 us  [trade(): moved.append(lax.ppermute(slices[slot], 'tok', pairs))]
    all_to_all x3 -> x1, waiting for transfers between devices: 13.5 us -> 5.85 us  [on_device(): tiles = lax.all_to_all(tiles, ('dp', 'tok'), 0, 0, tiled=True)]
    all_to_all x3 -> x1, starting transfers between devices: 12.3 us -> 5.73 us  [on_device(): tiles = lax.all_to_all(tiles, ('dp', 'tok'), 0, 0, tiled=True)]
    ppermute x0 -> x12, waiting for transfers between devices: none -> 2.44 us  [trade(): moved.append(lax.ppermute(slices[slot], 'tok', pairs))]
    pallas_call x3 -> x4, Pallas kernels: 6.31 us -> 7.19 us  [the longest x2 4.63 us: pack(): pl.pallas_call(functools.partial(pack_kernel, phase, closed), out_shape=m...]
    pallas_call x2, Pallas kernels: 10.7 us -> 9.82 us  [on_device(): pl.pallas_call(functools.partial(attend_kernel, slots, count, images, tok...]
  transfers between devices with their start and end apart: 3 -> 13, of which waited for: 3 -> 3; matrix products, arithmetic and copies ran while one was open for 0% -> 1% of each run, Pallas kernels for 19% -> 31%
where the time goes in v5:
time: 49.2 us; the launch traced here: 49 us
  starting transfers between devices  21 us (43%)
  Pallas kernels  18.2 us (37%)
  waiting for transfers between devices  8.29 us (17%)
  between operations  0.76 us (2%)
  local copies, waits for them, and re-layouts  0.7 us (1%)
    ppermute x12, starting transfers between devices, trade(): moved.append(lax.ppermute(slices[slot], 'tok', pairs))  15.2 us
    pallas_call x2, Pallas kernels, on_device(): pl.pallas_call(functools.partial(attend_kernel, slots, count, images, tok...  9.82 us
    all_to_all x1, waiting for transfers between devices, on_device(): tiles = lax.all_to_all(tiles, ('dp', 'tok'), 0, 0, tiled=True)  5.85 us
    all_to_all x1, starting transfers between devices, on_device(): tiles = lax.all_to_all(tiles, ('dp', 'tok'), 0, 0, tiled=True)  5.73 us
    pallas_call x2, Pallas kernels, pack(): pl.pallas_call(functools.partial(pack_kernel, phase, closed), out_shape=m...  4.63 us
    ppermute x12, waiting for transfers between devices, trade(): moved.append(lax.ppermute(slices[slot], 'tok', pairs))  2.44 us
    pallas_call x1, Pallas kernels, on_device(): pl.pallas_call(functools.partial(unpack_kernel, slots, count, images), ou...  1.86 us
    pallas_call x1, Pallas kernels, on_device(): pl.pallas_call(functools.partial(tables_kernel, images, tokd), out_shape=...  1.23 us
  transfers between devices with their start and end apart: 13, of which 3 were waited for; matrix products, arithmetic and copies ran while one was open for 1% of the time, Pallas kernels for 31%

profile of v5, /device:TPU:0, one launch (start us, length us, event | category | flops | bytes accessed | tf_op | source)
XLA Modules:
  0.0 49.0 jit_solution(5073128227197482005)
XLA Ops:
  0.6 0.0 copy-start.4
  0.6 0.0 copy-start.5
  0.7 0.0 copy-start.6
  0.7 2.3 %pack_heads.3 = (bf16[320,256]{1,0:T(8,128)(2,1)}, bf16[320,256]{1,0:T(8,128)(2,1)}, bf16[320,256]{1,0:T(8,128)(2,1)}, bf16[320,256]{1,0:T(8,128)(2,1)}) custom-call(bf16[256,640]{1,0:T(8,128)(2,1)} %bitcast.8, bf16[256,640]{1,0:T(8,128)(2,1)} %bitcast.10, bf16[256,640]{1,0:T(8,128)(2,1)} %bitcast.12, bf16[256,640]{1,0:T(8,128)(2,1)} %bitcast.14), custom_call_target="tpu_custom_call" | custom-call | tf_op jit(solution)/shard_map/pack_heads/pallas_call | solution.py:344
  3.0 0.0 copy-start.2
  3.0 4.0 %collective-permute-start = (bf16[320,256]{1,0:T(8,128)(2,1)}, bf16[320,256]{1,0:T(8,128)(2,1)S(1)}, u32[]{:S(2)}, u32[]{:S(2)}) collective-permute-start(bf16[320,256]{1,0:T(8,128)(2,1)} %get-tuple-element.80), channel_id=1, source_target_pairs={{0,3},{1,2},{2,1},{3,0},{4,7},{5,6},{6,5},{7,4},{8,11},{9,10},{10,... | collective-permute-start | bytes 491528 | tf_op jit(solution)/shard_map/ppermute | solution.py:63
  7.0 0.0 copy-start.3
  7.0 0.4 collective-permute-start.1
  7.4 0.2 collective-permute-start.2
  7.6 0.0 copy-done.4
  7.7 0.0 copy-done.5
  7.7 0.0 copy-done.6
  7.7 0.0 copy-done.2
  7.7 0.0 copy-done.3
  7.7 1.2 %rotary_tables.1 = (f32[40,1024]{1,0:T(8,128)S(1)}, f32[40,1024]{1,0:T(8,128)S(1)}, f32[640,128]{1,0:T(8,128)S(1)}) custom-call(s32[1,4]{1,0:T(1,128)S(1)} %copy-done.4, s32[1,4]{1,0:T(1,128)S(1)} %copy-done.3, s32[4,8]{1,0:T(4,128)S(1)} %copy-done.6, f32[40,128]{1,0:T(8,128)S(1)} %copy-done.5, bf16[3,640]{1,0:T(4,128)(2,1)S(1)} %copy-done.2), custom_call_target="tpu_custom_call" | custom-call | flops 26214400 | tf_op jit(solution)/shard_map/rotary_tables/pallas_call | solution.py:361
  8.9 0.0 copy-start.1
  8.9 2.3 %pack_heads.2 = (bf16[320,256]{1,0:T(8,128)(2,1)}, bf16[320,256]{1,0:T(8,128)(2,1)}, bf16[320,256]{1,0:T(8,128)(2,1)}, bf16[320,256]{1,0:T(8,128)(2,1)}) custom-call(bf16[256,640]{1,0:T(8,128)(2,1)} %bitcast.9, bf16[256,640]{1,0:T(8,128)(2,1)} %bitcast.11, bf16[256,640]{1,0:T(8,128)(2,1)} %bitcast.13, bf16[256,640]{1,0:T(8,128)(2,1)} %bitcast.15), custom_call_target="tpu_custom_call" | custom-call | tf_op jit(solution)/shard_map/pack_heads/pallas_call | solution.py:344
  11.3 2.9 %collective-permute-start.3 = (bf16[320,256]{1,0:T(8,128)(2,1)}, bf16[320,256]{1,0:T(8,128)(2,1)S(1)}, u32[]{:S(2)}, u32[]{:S(2)}) collective-permute-start(bf16[320,256]{1,0:T(8,128)(2,1)} %get-tuple-element.89), channel_id=1, source_target_pairs={{0,3},{1,2},{2,1},{3,0},{4,7},{5,6},{6,5},{7,4},{8,11},{9,10},{10,... | collective-permute-start | bytes 491528 | tf_op jit(solution)/shard_map/ppermute | solution.py:63
  14.2 0.4 collective-permute-start.4
  14.6 0.0 collective-permute-done.refs_1_
  14.6 0.2 collective-permute-start.5
  14.8 0.9 %collective-permute-done.1.refs_2_ = bf16[320,256]{1,0:T(8,128)(2,1)S(1)} collective-permute-done((bf16[320,256]{1,0:T(8,128)(2,1)}, bf16[320,256]{1,0:T(8,128)(2,1)S(1)}, u32[]{:S(2)}, u32[]{:S(2)}) %collective-permute-start.1) | collective-permute-done | bytes 163872 | tf_op jit(solution)/shard_map/ppermute | solution.py:63
  15.8 0.0 collective-permute-done.2.refs_3_
  15.8 0.0 copy-done.1
  15.8 0.0 copy-start
  15.8 4.9 %attend_head.2 = (bf16[320,256]{1,0:T(8,128)(2,1)S(1)}, bf16[320,256]{1,0:T(8,128)(2,1)S(1)}, bf16[320,256]{1,0:T(8,128)(2,1)S(1)}, bf16[320,256]{1,0:T(8,128)(2,1)S(1)}, f32[8,128]{1,0:T(8,128)S(1)}) custom-call(s32[1,4]{1,0:T(1,128)S(1)} %copy-done.4, s32[4,8]{1,0:T(4,128)S(1)} %copy-done.6, f32[40,1024]{1,0:T(8,128)S(1)} %get-tuple-element.76.cosv, ...), custom_call_target="tpu_custom_call" | custom-call | flops 3221225472 | tf_op jit(solution)/shard_map/attend_head/pallas_call | solution.py:380
  20.7 0.0 collective-permute-done.3.refs_2_
  20.7 1.5 %collective-permute-done.4.refs_3_ = bf16[320,256]{1,0:T(8,128)(2,1)S(1)} collective-permute-done((bf16[320,256]{1,0:T(8,128)(2,1)}, bf16[320,256]{1,0:T(8,128)(2,1)S(1)}, u32[]{:S(2)}, u32[]{:S(2)}) %collective-permute-start.4) | collective-permute-done | bytes 163872 | tf_op jit(solution)/shard_map/ppermute | solution.py:63
  22.2 0.0 collective-permute-done.5.refs_4_
  22.2 2.4 %collective-permute-start.6 = (bf16[320,256]{1,0:T(8,128)(2,1)S(1)}, bf16[320,256]{1,0:T(8,128)(2,1)S(1)}, u32[]{:S(2)}, u32[]{:S(2)}) collective-permute-start(bf16[320,256]{1,0:T(8,128)(2,1)S(1)} %get-tuple-element.98), channel_id=1, source_target_pairs={{3,0},{2,1},{1,2},{0,3},{7,4},{6,5},{5,6},{4,7},{11,8},{10,9},{9,1... | collective-permute-start | bytes 491528 | tf_op jit(solution)/shard_map/ppermute | solution.py:63
  24.6 0.4 collective-permute-start.7
  25.0 0.7 %collective-permute-start.8 = (bf16[320,256]{1,0:T(8,128)(2,1)S(1)}, bf16[320,256]{1,0:T(8,128)(2,1)S(1)}, u32[]{:S(2)}, u32[]{:S(2)}) collective-permute-start(bf16[320,256]{1,0:T(8,128)(2,1)S(1)} %get-tuple-element.100), channel_id=1, source_target_pairs={{1,0},{0,1},{3,2},{2,3},{5,4},{4,5},{7,6},{6,7},{9,8},{8,9},{11,10... | collective-permute-start | bytes 491528 | tf_op jit(solution)/shard_map/ppermute | solution.py:63
  25.7 0.0 copy-done
  25.7 4.9 %attend_head.3 = (bf16[320,256]{1,0:T(8,128)(2,1)S(1)}, bf16[320,256]{1,0:T(8,128)(2,1)S(1)}, bf16[320,256]{1,0:T(8,128)(2,1)S(1)}, bf16[320,256]{1,0:T(8,128)(2,1)S(1)}, f32[8,128]{1,0:T(8,128)S(1)}) custom-call(s32[1,4]{1,0:T(1,128)S(1)} %copy-done.4, s32[4,8]{1,0:T(4,128)S(1)} %copy-done.6, f32[40,1024]{1,0:T(8,128)S(1)} %get-tuple-element.76.cosv, ...), custom_call_target="tpu_custom_call" | custom-call | flops 3221225472 | tf_op jit(solution)/shard_map/attend_head/pallas_call | solution.py:380
  30.6 2.4 %collective-permute-start.9 = (bf16[320,256]{1,0:T(8,128)(2,1)S(1)}, bf16[320,256]{1,0:T(8,128)(2,1)S(1)}, u32[]{:S(2)}, u32[]{:S(2)}) collective-permute-start(bf16[320,256]{1,0:T(8,128)(2,1)S(1)} %get-tuple-element.106), channel_id=1, source_target_pairs={{3,0},{2,1},{1,2},{0,3},{7,4},{6,5},{5,6},{4,7},{11,8},{10,9},{9,1... | collective-permute-start | bytes 491528 | tf_op jit(solution)/shard_map/ppermute | solution.py:63
  33.0 0.4 collective-permute-start.10
  33.4 0.0 collective-permute-done.6.refs_1_
  33.4 0.7 %collective-permute-start.11 = (bf16[320,256]{1,0:T(8,128)(2,1)S(1)}, bf16[320,256]{1,0:T(8,128)(2,1)S(1)}, u32[]{:S(2)}, u32[]{:S(2)}) collective-permute-start(bf16[320,256]{1,0:T(8,128)(2,1)S(1)} %get-tuple-element.108), channel_id=1, source_target_pairs={{1,0},{0,1},{3,2},{2,3},{5,4},{4,5},{7,6},{6,7},{9,8},{8,9},{11,10... | collective-permute-start | bytes 491528 | tf_op jit(solution)/shard_map/ppermute | solution.py:63
  34.1 0.0 collective-permute-done.7.refs_2_
  34.1 0.0 collective-permute-done.8.refs_3_
  34.1 0.7 %broadcast_in_dim.18 = f32[32,8,128]{2,1,0:T(8,128)} broadcast(f32[8,128]{1,0:T(8,128)S(1)} %get-tuple-element.113), dimensions={1,2} | broadcast | bytes 135168 | tf_op jit(solution)/shard_map/broadcast_in_dim | solution.py:404
  34.8 5.7 %all-to-all-start = ((f32[32,8,128]{2,1,0:T(8,128)}), f32[32,8,128]{2,1,0:T(8,128)S(1)}, u32[]{:S(2)}, u32[]{:S(2)}) async-start(f32[32,8,128]{2,1,0:T(8,128)} %broadcast_in_dim.18), calls=%async_computation | async-start | bytes 262144 | tf_op jit(solution)/shard_map/all_to_all | solution.py:405
  40.5 0.0 collective-permute-done.9.refs_5_
  40.5 0.0 collective-permute-done.10.refs_6_
  40.5 0.0 collective-permute-done.11.refs_7_
  40.5 1.9 %unpack_heads.1 = (bf16[256,640]{1,0:T(8,128)(2,1)}, bf16[256,640]{1,0:T(8,128)(2,1)}, bf16[256,640]{1,0:T(8,128)(2,1)}, bf16[256,640]{1,0:T(8,128)(2,1)}) custom-call(s32[1,4]{1,0:T(1,128)S(1)} %copy-done.4, s32[4,8]{1,0:T(4,128)S(1)} %copy-done.6, bf16[320,256]{1,0:T(8,128)(2,1)S(1)} %get-tuple-element.101.refs_0_, ...), custom_call_target="tpu_custom_call" | custom-call | flops 20000000000 | tf_op jit(solution)/shard_map/unpack_heads/pallas_call | solution.py:406
  42.4 5.8 %all-to-all-done.tiles = f32[32,8,128]{2,1,0:T(8,128)S(1)} async-done(((f32[32,8,128]{2,1,0:T(8,128)}), f32[32,8,128]{2,1,0:T(8,128)S(1)}, u32[]{:S(2)}, u32[]{:S(2)}) %all-to-all-start) | async-done | bytes 131104 | tf_op jit(solution)/shard_map/all_to_all | solution.py:405
  48.3 0.7 %bias_sums.1 = f32[3,640]{1,0:T(4,128)} custom-call(f32[32,8,128]{2,1,0:T(8,128)S(1)} %all-to-all-done.tiles), custom_call_target="tpu_custom_call" | custom-call | tf_op jit(solution)/shard_map/bias_sums/pallas_call | solution.py:417
Async XLA Ops:
  0.6 7.0 %copy-start.4 = (s32[1,4]{1,0:T(1,128)S(1)}, s32[1,4]{1,0:T(1,128)}, u32[]{:S(2)}) copy-start(s32[1,4]{1,0:T(1,128)} %lengths.7) | copy-start | bytes 52
  0.6 7.0 %copy-start.5 = (f32[40,128]{1,0:T(8,128)S(1)}, f32[40,128]{1,0:T(8,128)}, u32[]{:S(2)}) copy-start(f32[40,128]{1,0:T(8,128)} %constant.5.clone.inverse) | copy-start | bytes 61444
  0.7 7.0 %copy-start.6 = (s32[4,8]{1,0:T(4,128)S(1)}, s32[4,8]{1,0:T(4,128)}, u32[]{:S(2)}) copy-start(s32[4,8]{1,0:T(4,128)} %constant.4.clone.table) | copy-start | bytes 388
  3.0 4.7 %copy-start.2 = (bf16[3,640]{1,0:T(4,128)(2,1)S(1)}, bf16[3,640]{1,0:T(4,128)(2,1)}, u32[]{:S(2)}) copy-start(bf16[3,640]{1,0:T(4,128)(2,1)} %bias.1) | copy-start | bytes 11524
  3.0 11.6 %collective-permute-start = (bf16[320,256]{1,0:T(8,128)(2,1)}, bf16[320,256]{1,0:T(8,128)(2,1)S(1)}, u32[]{:S(2)}, u32[]{:S(2)}) collective-permute-start(bf16[320,256]{1,0:T(8,128)(2,1)} %get-tuple-element.80), channel_id=1, source_target_pairs={{0,3},{1,2},{2,1},{3,0},{4,7},{5,6},{6,5},{7,4},{8,11},{9,10},{10,... | collective-permute-start | bytes 491528 | tf_op jit(solution)/shard_map/ppermute | solution.py:63
  7.0 0.7 %copy-start.3 = (s32[1,4]{1,0:T(1,128)S(1)}, s32[1,4]{1,0:T(1,128)}, u32[]{:S(2)}) copy-start(s32[1,4]{1,0:T(1,128)} %widths.1) | copy-start | bytes 52
  7.0 8.8 %collective-permute-start.1 = (bf16[320,256]{1,0:T(8,128)(2,1)}, bf16[320,256]{1,0:T(8,128)(2,1)S(1)}, u32[]{:S(2)}, u32[]{:S(2)}) collective-permute-start(bf16[320,256]{1,0:T(8,128)(2,1)} %get-tuple-element.81), channel_id=1, source_target_pairs={{0,2},{1,3},{2,0},{3,1},{4,6},{5,7},{6,4},{7,5},{8,10},{9,11},{10,... | collective-permute-start | bytes 491528 | tf_op jit(solution)/shard_map/ppermute | solution.py:63
  7.4 8.3 %collective-permute-start.2 = (bf16[320,256]{1,0:T(8,128)(2,1)}, bf16[320,256]{1,0:T(8,128)(2,1)S(1)}, u32[]{:S(2)}, u32[]{:S(2)}) collective-permute-start(bf16[320,256]{1,0:T(8,128)(2,1)} %get-tuple-element.82), channel_id=1, source_target_pairs={{0,1},{1,0},{2,3},{3,2},{4,5},{5,4},{6,7},{7,6},{8,9},{9,8},{10,11... | collective-permute-start | bytes 491528 | tf_op jit(solution)/shard_map/ppermute | solution.py:63
  8.9 6.9 %copy-start.1 = (bf16[320,256]{1,0:T(8,128)(2,1)S(1)}, bf16[320,256]{1,0:T(8,128)(2,1)}, u32[]{:S(2)}) copy-start(bf16[320,256]{1,0:T(8,128)(2,1)} %get-tuple-element.79.refs_0_) | copy-start | bytes 491524
  11.3 9.4 %collective-permute-start.3 = (bf16[320,256]{1,0:T(8,128)(2,1)}, bf16[320,256]{1,0:T(8,128)(2,1)S(1)}, u32[]{:S(2)}, u32[]{:S(2)}) collective-permute-start(bf16[320,256]{1,0:T(8,128)(2,1)} %get-tuple-element.89), channel_id=1, source_target_pairs={{0,3},{1,2},{2,1},{3,0},{4,7},{5,6},{6,5},{7,4},{8,11},{9,10},{10,... | collective-permute-start | bytes 491528 | tf_op jit(solution)/shard_map/ppermute | solution.py:63
  14.2 8.0 %collective-permute-start.4 = (bf16[320,256]{1,0:T(8,128)(2,1)}, bf16[320,256]{1,0:T(8,128)(2,1)S(1)}, u32[]{:S(2)}, u32[]{:S(2)}) collective-permute-start(bf16[320,256]{1,0:T(8,128)(2,1)} %get-tuple-element.90), channel_id=1, source_target_pairs={{0,2},{1,3},{2,0},{3,1},{4,6},{5,7},{6,4},{7,5},{8,10},{9,11},{10,... | collective-permute-start | bytes 491528 | tf_op jit(solution)/shard_map/ppermute | solution.py:63
  14.6 7.6 %collective-permute-start.5 = (bf16[320,256]{1,0:T(8,128)(2,1)}, bf16[320,256]{1,0:T(8,128)(2,1)S(1)}, u32[]{:S(2)}, u32[]{:S(2)}) collective-permute-start(bf16[320,256]{1,0:T(8,128)(2,1)} %get-tuple-element.91), channel_id=1, source_target_pairs={{0,1},{1,0},{2,3},{3,2},{4,5},{5,4},{6,7},{7,6},{8,9},{9,8},{10,11... | collective-permute-start | bytes 491528 | tf_op jit(solution)/shard_map/ppermute | solution.py:63
  15.8 9.9 %copy-start = (bf16[320,256]{1,0:T(8,128)(2,1)S(1)}, bf16[320,256]{1,0:T(8,128)(2,1)}, u32[]{:S(2)}) copy-start(bf16[320,256]{1,0:T(8,128)(2,1)} %get-tuple-element.92.refs_1_) | copy-start | bytes 491524
  22.2 11.3 %collective-permute-start.6 = (bf16[320,256]{1,0:T(8,128)(2,1)S(1)}, bf16[320,256]{1,0:T(8,128)(2,1)S(1)}, u32[]{:S(2)}, u32[]{:S(2)}) collective-permute-start(bf16[320,256]{1,0:T(8,128)(2,1)S(1)} %get-tuple-element.98), channel_id=1, source_target_pairs={{3,0},{2,1},{1,2},{0,3},{7,4},{6,5},{5,6},{4,7},{11,8},{10,9},{9,1... | collective-permute-start | bytes 491528 | tf_op jit(solution)/shard_map/ppermute | solution.py:63
  24.6 9.5 %collective-permute-start.7 = (bf16[320,256]{1,0:T(8,128)(2,1)S(1)}, bf16[320,256]{1,0:T(8,128)(2,1)S(1)}, u32[]{:S(2)}, u32[]{:S(2)}) collective-permute-start(bf16[320,256]{1,0:T(8,128)(2,1)S(1)} %get-tuple-element.99), channel_id=1, source_target_pairs={{2,0},{3,1},{0,2},{1,3},{6,4},{7,5},{4,6},{5,7},{10,8},{11,9},{8,1... | collective-permute-start | bytes 491528 | tf_op jit(solution)/shard_map/ppermute | solution.py:63
  25.0 9.1 %collective-permute-start.8 = (bf16[320,256]{1,0:T(8,128)(2,1)S(1)}, bf16[320,256]{1,0:T(8,128)(2,1)S(1)}, u32[]{:S(2)}, u32[]{:S(2)}) collective-permute-start(bf16[320,256]{1,0:T(8,128)(2,1)S(1)} %get-tuple-element.100), channel_id=1, source_target_pairs={{1,0},{0,1},{3,2},{2,3},{5,4},{4,5},{7,6},{6,7},{9,8},{8,9},{11,10... | collective-permute-start | bytes 491528 | tf_op jit(solution)/shard_map/ppermute | solution.py:63
  30.6 9.9 %collective-permute-start.9 = (bf16[320,256]{1,0:T(8,128)(2,1)S(1)}, bf16[320,256]{1,0:T(8,128)(2,1)S(1)}, u32[]{:S(2)}, u32[]{:S(2)}) collective-permute-start(bf16[320,256]{1,0:T(8,128)(2,1)S(1)} %get-tuple-element.106), channel_id=1, source_target_pairs={{3,0},{2,1},{1,2},{0,3},{7,4},{6,5},{5,6},{4,7},{11,8},{10,9},{9,1... | collective-permute-start | bytes 491528 | tf_op jit(solution)/shard_map/ppermute | solution.py:63
  33.0 7.5 %collective-permute-start.10 = (bf16[320,256]{1,0:T(8,128)(2,1)S(1)}, bf16[320,256]{1,0:T(8,128)(2,1)S(1)}, u32[]{:S(2)}, u32[]{:S(2)}) collective-permute-start(bf16[320,256]{1,0:T(8,128)(2,1)S(1)} %get-tuple-element.107), channel_id=1, source_target_pairs={{2,0},{3,1},{0,2},{1,3},{6,4},{7,5},{4,6},{5,7},{10,8},{11,9},{8,1... | collective-permute-start | bytes 491528 | tf_op jit(solution)/shard_map/ppermute | solution.py:63
  33.4 7.1 %collective-permute-start.11 = (bf16[320,256]{1,0:T(8,128)(2,1)S(1)}, bf16[320,256]{1,0:T(8,128)(2,1)S(1)}, u32[]{:S(2)}, u32[]{:S(2)}) collective-permute-start(bf16[320,256]{1,0:T(8,128)(2,1)S(1)} %get-tuple-element.108), channel_id=1, source_target_pairs={{1,0},{0,1},{3,2},{2,3},{5,4},{4,5},{7,6},{6,7},{9,8},{8,9},{11,10... | collective-permute-start | bytes 491528 | tf_op jit(solution)/shard_map/ppermute | solution.py:63
  34.8 13.5 %all-to-all-start = ((f32[32,8,128]{2,1,0:T(8,128)}), f32[32,8,128]{2,1,0:T(8,128)S(1)}, u32[]{:S(2)}, u32[]{:S(2)}) async-start(f32[32,8,128]{2,1,0:T(8,128)} %broadcast_in_dim.18), calls=%async_computation | async-start | bytes 262144 | tf_op jit(solution)/shard_map/all_to_all | solution.py:405

commit v6 on v5

--- a/solution.py
+++ b/solution.py
@@ -18,7 +18,7 @@
 NEG = -1e30
 LANES = 128
 HALF = HEAD_DIM // 2
-PACK_MIB = 60
+PACK_MIB = 52
 UNPACK_FLOPS = 20_000_000_000
 
 rope_base = 10000.0
@@ -55,13 +55,21 @@
     return sources, targets
 
 
-def trade(slices, back=False):
+def trade(slices):
     moved = [slices[0]]
-    for slot, pairs in enumerate(trade_rounds(lax.axis_size("tok")), 1):
-        if back:
-            pairs = [(target, source) for source, target in pairs]
-        moved.append(lax.ppermute(slices[slot], "tok", pairs))
+    for one, pairs in zip(slices[1:], trade_rounds(lax.axis_size("tok"))):
+        moved.append(lax.ppermute(one, "tok", pairs))
     return moved
+
+
+def send_back(result, slot):
+    if slot == 0:
+        return result
+    pairs = trade_rounds(lax.axis_size("tok"))[slot - 1]
+    return lax.ppermute(result, "tok", [(target, source) for source, target in pairs])
+
+
+EARLY = 1
 
 
 def image_of(block, lengths, images):
@@ -96,34 +104,28 @@
     return jnp.concatenate([first * cosv + second * sinv, second * cosv - first * sinv], axis=0)
 
 
-def phase_lanes(phase, model):
-    size = SPAN * HEAD_DIM
-    begin = phase * size // LANES * LANES
-    end = -(-(phase + 1) * size // LANES) * LANES
-    return begin, min(end, model)
-
-
-def pack_kernel(phase, closed, *refs):
+def pack_kernel(closed, *refs):
     inputs, outs, held, turned, sems = refs[:4], refs[4:-3], refs[-3], refs[-2], refs[-1]
-    begin, end = phase_lanes(phase, inputs[0].shape[1])
     copies = [
-        pltpu.make_async_copy(source.at[:, begin:end], held.at[number], sems.at[number])
+        pltpu.make_async_copy(source, held.at[number], sems.at[number])
         for number, source in enumerate(inputs)
     ]
     for copy in copies:
         copy.start()
     me = lax.rem(lax.axis_index("tok"), SPAN)
-    inner = phase * SPAN * HEAD_DIM - begin
     steps = [0] + (
         [*range(SPAN - 1, 0, -1)] if closed else [*range(1, SPAN), *range(SPAN - 1, 0, -1)]
     )
     for number, copy in enumerate(copies):
         copy.wait()
         turned[number] = held[number].T
-        for out, step in zip(outs, steps):
-            residue = me ^ step if closed else lax.rem(me + step, SPAN)
-            rows = pl.ds(pl.multiple_of(inner + residue * HEAD_DIM, 16), HEAD_DIM)
-            out[message_rows(number), :] = turned[number, rows, :]
+        for phase in range(OWN_HEADS):
+            for slot, step in enumerate(steps):
+                residue = me ^ step if closed else lax.rem(me + step, SPAN)
+                begin = pl.multiple_of((phase * SPAN + residue) * HEAD_DIM, 16)
+                outs[phase * len(steps) + slot][message_rows(number), :] = turned[
+                    number, pl.ds(begin, HEAD_DIM), :
+                ]
 
 
 def tables_kernel(images, tokd, lengths, widths, table, inverse, bias, cos_out, sin_out, bias_out):
@@ -149,10 +151,11 @@
 
 
 def attend_kernel(slots, count, images, tokd, head, factor, lengths, table, cosv, sinv, bias, *refs):
+    msgs, refs = refs[:slots], refs[slots:]
     if head > 0:
-        before, refs = refs[0], refs[1:]
-    msgs, outs, sums = refs[:slots], refs[slots : 2 * slots], refs[2 * slots]
-    qt_all, kt_all, vt_all, q_all, k_all, v_all, g_all, s_buf, e_buf, d_buf = refs[2 * slots + 1 :]
+        before, refs = refs[0], refs[slots:]
+    outs, sums = refs[:slots], refs[slots]
+    qt_all, kt_all, vt_all, q_all, k_all, v_all, g_all, s_buf, e_buf, d_buf = refs[slots + 1 :]
     me = lax.axis_index("tok")
     residue = lax.rem(me, SPAN)
     ids = []
@@ -170,6 +173,10 @@
     def block_of(slot):
         return slice(slot * tokd, (slot + 1) * tokd)
 
+    def put(slot, tensor, values):
+        begin = ((0 if slot == EARLY else 4 * head) + tensor) * HEAD_DIM
+        outs[slot][begin : begin + HEAD_DIM, :] = values
+
     def stage(slot):
         at = block_of(slot)
         cos_b, sin_b = cosv[:, at], sinv[:, at]
@@ -205,7 +212,7 @@
         )
         inv = 1.0 / mixed[HEAD_DIM : HEAD_DIM + 1]
         out_b = (mixed[:HEAD_DIM] * inv).astype(jnp.bfloat16)
-        outs[slot][message_rows(0), :] = out_b
+        put(slot, 0, out_b)
         grad = msgs[slot][message_rows(3), :].astype(jnp.float32)
         delta = jnp.sum(grad * out_b.astype(jnp.float32), axis=0, keepdims=True) * inv
         coarse = delta.astype(jnp.bfloat16).astype(jnp.float32)
@@ -224,7 +231,7 @@
         at = block_of(slot)
         dquery = jnp.dot(kt_all[:HEAD_DIM, :], d_buf[:, at], preferred_element_type=jnp.float32)
         dquery = unrotate(dquery * SCALE, cosv[:, at], sinv[:, at])
-        outs[slot][message_rows(1), :] = dquery.astype(jnp.bfloat16)
+        put(slot, 1, dquery.astype(jnp.bfloat16))
         return jnp.where(ids[slot] >= 0, dquery, 0.0)
 
     for slot in range(slots):
@@ -252,10 +259,10 @@
         live = ids[slot] >= 0
         dvalue = jnp.dot(e_buf[at, :], g_all[...], preferred_element_type=jnp.float32)
         dv_total = dv_total + jnp.where(live, jnp.sum(dvalue, axis=0, keepdims=True), 0.0)
-        outs[slot][message_rows(3), :] = dvalue.astype(jnp.bfloat16).T[:HEAD_DIM]
+        put(slot, 3, dvalue.astype(jnp.bfloat16).T[:HEAD_DIM])
         dkey = jnp.dot(d_buf[at, :], q_all[...], preferred_element_type=jnp.float32)
         dkey = unrotate(dkey.T[:HEAD_DIM] * (1.0 / LOG2E), cosv[:, at], sinv[:, at])
-        outs[slot][message_rows(2), :] = dkey.astype(jnp.bfloat16)
+        put(slot, 2, dkey.astype(jnp.bfloat16))
         dk_total = dk_total + jnp.where(live, dkey, 0.0)
     lane = lax.broadcasted_iota(jnp.int32, (HEAD_DIM, LANES), 1)
     columns = jnp.where(
@@ -265,14 +272,25 @@
     )
     columns = jnp.concatenate([columns, jnp.zeros((LANES - HEAD_DIM, LANES), jnp.float32)], axis=0)
     lines = columns.T
-    sums[...] = jnp.zeros_like(sums) if head == 0 else before[...]
+    row = lax.broadcasted_iota(jnp.int32, (8, LANES), 0)
+    tile = jnp.zeros((8, LANES), jnp.float32) if head == 0 else before[...]
     for number, total in enumerate((lines[0:1], lines[1:2], dv_total)):
-        at = number * OWN_HEADS + head
-        sums[at : at + 1, :] = total * factor
+        tile = jnp.where(row == number * OWN_HEADS + head, total * factor, tile)
+    if head + 1 < OWN_HEADS:
+        sums[...] = tile
+    else:
+
+        def spread(device, carry):
+            sums[device] = tile
+            return carry
+
+        lax.fori_loop(0, sums.shape[0], spread, 0, unroll=min(32, sums.shape[0]))
 
 
 def unpack_kernel(slots, count, images, lengths, table, *refs):
-    msgs, outs, held = refs[: OWN_HEADS * slots], refs[OWN_HEADS * slots : -1], refs[-1]
+    msgs, outs, held = refs[: slots + OWN_HEADS - 1], refs[slots + OWN_HEADS - 1 : -1], refs[-1]
+    early, late = msgs[:OWN_HEADS], list(msgs[OWN_HEADS:])
+    late.insert(EARLY, None)
     me = lax.axis_index("tok")
     _, start = image_of(me, lengths, images)
     for slot in range(slots):
@@ -283,9 +301,11 @@
             for phase in range(OWN_HEADS):
                 begin = pl.multiple_of((phase * SPAN + residue) * HEAD_DIM, 16)
                 for number in range(4):
-                    held[number, pl.ds(begin, HEAD_DIM), :] = msgs[phase * slots + slot][
-                        message_rows(number), :
-                    ]
+                    if slot == EARLY:
+                        piece = early[phase][message_rows(number), :]
+                    else:
+                        piece = late[slot][message_rows(4 * phase + number), :]
+                    held[number, pl.ds(begin, HEAD_DIM), :] = piece
 
         if is_closed(count):
             place()
@@ -332,31 +352,29 @@
     vmem = pl.BlockSpec(memory_space=pltpu.VMEM)
     hbm = pl.BlockSpec(memory_space=pltpu.HBM)
     whole = jax.ShapeDtypeStruct((tokd, model), jnp.bfloat16)
-    messages = [jax.ShapeDtypeStruct((4 * HEAD_DIM, tokd), jnp.bfloat16)] * slots
-    sums_shape = jax.ShapeDtypeStruct((8, LANES), jnp.float32)
-    tokens_all = dp_size * count * tokd
+    message = jax.ShapeDtypeStruct((4 * HEAD_DIM, tokd), jnp.bfloat16)
+    joined = jax.ShapeDtypeStruct((OWN_HEADS * 4 * HEAD_DIM, tokd), jnp.bfloat16)
+    devices = dp_size * count
+    tokens_all = devices * tokd
 
     def params(mib):
         return pltpu.CompilerParams(vmem_limit_bytes=mib * 1024 * 1024)
 
-    def pack(phase, inputs):
-        begin, end = phase_lanes(phase, model)
-        return pl.pallas_call(
-            functools.partial(pack_kernel, phase, closed),
-            out_shape=messages,
-            in_specs=[hbm] * 4,
-            out_specs=[vmem] * slots,
-            scratch_shapes=[
-                pltpu.VMEM((4, tokd, end - begin), jnp.bfloat16),
-                pltpu.VMEM((4, end - begin, tokd), jnp.bfloat16),
-                pltpu.SemaphoreType.DMA((4,)),
-            ],
-            compiler_params=params(PACK_MIB),
-            name="pack_heads",
-        )(*inputs)
-
     inputs = (query_in[0], key_in[0], value_in[0], out_grad[0])
-    got = [trade(pack(0, inputs))]
+    sends = pl.pallas_call(
+        functools.partial(pack_kernel, closed),
+        out_shape=[message] * (OWN_HEADS * slots),
+        in_specs=[hbm] * 4,
+        out_specs=[vmem] * (OWN_HEADS * slots),
+        scratch_shapes=[
+            pltpu.VMEM((4, tokd, model), jnp.bfloat16),
+            pltpu.VMEM((4, model, tokd), jnp.bfloat16),
+            pltpu.SemaphoreType.DMA((4,)),
+        ],
+        compiler_params=params(PACK_MIB),
+        name="pack_heads",
+    )(*inputs)
+    got = [trade(sends[:slots])]
     table_shape = jax.ShapeDtypeStruct((HALF, span), jnp.float32)
     tables = pl.pallas_call(
         functools.partial(tables_kernel, images, tokd),
@@ -369,21 +387,29 @@
         ),
         name="rotary_tables",
     )(lengths, widths, table, inverse, bias)
+    tables, sends = lax.optimization_barrier((tables, sends[slots:]))
     for phase in range(1, OWN_HEADS):
-        tables, inputs = lax.optimization_barrier((tables, inputs))
-        packed = pack(phase, inputs)
-        tables, packed = lax.optimization_barrier((tables, packed))
-        got.append(trade(packed))
-    back = []
-    sums = []
+        got.append(trade(sends[(phase - 1) * slots : phase * slots]))
+    early = []
+    carried = []
     for phase in range(OWN_HEADS):
+        last = phase + 1 == OWN_HEADS
+        kept = [slot for slot in range(slots) if slot != EARLY]
+        sums_shape = jax.ShapeDtypeStruct(
+            (devices, 8, LANES) if last else (8, LANES), jnp.float32
+        )
+        first_carried = 5 + slots + 1
         *results, total = pl.pallas_call(
             functools.partial(
                 attend_kernel, slots, count, images, tokd, phase, 1.0 / tokens_all**0.5
             ),
-            out_shape=messages + [sums_shape],
-            in_specs=[smem, smem] + [vmem] * (3 + len(sums) + slots),
+            out_shape=[message if slot == EARLY else joined for slot in range(slots)]
+            + [sums_shape],
+            in_specs=[smem, smem] + [vmem] * (3 + slots + len(carried)),
             out_specs=[vmem] * (slots + 1),
+            input_output_aliases={first_carried + at: slot for at, slot in enumerate(kept)}
+            if carried
+            else {},
             scratch_shapes=[pltpu.VMEM((LANES, span), jnp.bfloat16)] * 3
             + [pltpu.VMEM((span, LANES), jnp.bfloat16)] * 4
             + [pltpu.VMEM((span, tokd), jnp.float32)]
@@ -393,26 +419,22 @@
                 flops=12 * span * span * 256, bytes_accessed=0, transcendentals=0
             ),
             name="attend_head",
-        )(lengths, table, *tables, *sums, *got[phase])
-        sums = [total]
-        if phase + 1 < OWN_HEADS:
-            results, got[phase + 1] = lax.optimization_barrier((results, got[phase + 1]))
-        back.append(trade(results, back=True))
-    total, early = lax.optimization_barrier((sums[0], back[:-1]))
-    back[:-1] = early
-    devices = dp_size * count
-    tiles = jnp.broadcast_to(total[None], (devices,) + total.shape)
-    tiles = lax.all_to_all(tiles, ("dp", "tok"), 0, 0, tiled=True)
+        )(lengths, table, *tables, *got[phase], *carried)
+        early.append(send_back(results[EARLY], EARLY))
+        carried = [total] + [results[slot] for slot in kept]
+    total, early[:-1] = lax.optimization_barrier((total, early[:-1]))
+    tiles = lax.all_to_all(total, ("dp", "tok"), 0, 0, tiled=True)
+    late = [send_back(results[slot], slot) for slot in kept]
     outs = pl.pallas_call(
         functools.partial(unpack_kernel, slots, count, images),
         out_shape=[whole] * 4,
-        in_specs=[smem, smem] + [vmem] * (OWN_HEADS * slots),
+        in_specs=[smem, smem] + [vmem] * (OWN_HEADS + len(late)),
         out_specs=[vmem] * 4,
         scratch_shapes=[pltpu.VMEM((4, model, tokd), jnp.bfloat16)],
         compiler_params=params(16),
         cost_estimate=pl.CostEstimate(flops=UNPACK_FLOPS, bytes_accessed=0, transcendentals=0),
         name="unpack_heads",
-    )(lengths, jnp.asarray(targets), *(result for results in back for result in results))
+    )(lengths, jnp.asarray(targets), *early, *late)
     outs, tiles = lax.optimization_barrier((outs, tiles))
     bias_grad = pl.pallas_call(
         bias_kernel,

time: 49.2 us -> 57.8 us (1.17)
  waiting for transfers between devices: 8.29 us -> 19 us
  Pallas kernels: 18.2 us -> 15.9 us
  local copies, waits for them, and re-layouts: 0.7 us -> 1.96 us
  starting transfers between devices: 21 us -> 20 us
    ppermute x12 -> x10, waiting for transfers between devices: 2.44 us -> 13.1 us  [the longest x4 9.12 us: send_back(): lax.ppermute(result, 'tok', [(target, source) for source, target in pairs])]
    pallas_call x2 -> x1, Pallas kernels: 4.63 us -> 1.54 us  [on_device(): pl.pallas_call(functools.partial(pack_kernel, closed), out_shape=[message...]
    unnamed x14, local copies, waits for them, and re-layouts: 0.04 us -> 1.96 us
    pallas_call x2, Pallas kernels: 9.82 us -> 10.5 us  [on_device(): pl.pallas_call(functools.partial(attend_kernel, slots, count, images, tok...]
    broadcast_in_dim x1 -> x0, local copies, waits for them, and re-layouts: 0.66 us -> none  [on_device(): tiles = jnp.broadcast_to(total[None], (devices,) + total.shape)]
    ppermute x12 -> x10, starting transfers between devices: 15.2 us -> 14.7 us  [the longest x6 9.77 us: trade(): moved.append(lax.ppermute(one, 'tok', pairs))]
  transfers between devices with their start and end apart: 13 -> 11, of which waited for: 3 -> 4; matrix products, arithmetic and copies ran while one was open for 1% -> 0% of each run, Pallas kernels for 31% -> 14%
where the time goes in v6:
time: 57.8 us; the launch traced here: 57.5 us
  starting transfers between devices  20 us (35%)
  waiting for transfers between devices  19 us (33%)
  Pallas kernels  15.9 us (28%)
  local copies, waits for them, and re-layouts  1.96 us (3%)
  between operations  0.74 us (1%)
    pallas_call x2, Pallas kernels, on_device(): pl.pallas_call(functools.partial(attend_kernel, slots, count, images, tok...  10.5 us
    ppermute x6, starting transfers between devices, trade(): moved.append(lax.ppermute(one, 'tok', pairs))  9.77 us
    ppermute x4, waiting for transfers between devices, send_back(): lax.ppermute(result, 'tok', [(target, source) for source, target in pairs])  9.12 us
    all_to_all x1, waiting for transfers between devices, on_device(): tiles = lax.all_to_all(total, ('dp', 'tok'), 0, 0, tiled=True)  5.85 us
    all_to_all x1, starting transfers between devices, on_device(): tiles = lax.all_to_all(total, ('dp', 'tok'), 0, 0, tiled=True)  5.32 us
    ppermute x4, starting transfers between devices, send_back(): lax.ppermute(result, 'tok', [(target, source) for source, target in pairs])  4.91 us
    ppermute x6, waiting for transfers between devices, trade(): moved.append(lax.ppermute(one, 'tok', pairs))  3.98 us
    unnamed x14, local copies, waits for them, and re-layouts  1.96 us
  transfers between devices with their start and end apart: 11, of which 4 were waited for; matrix products, arithmetic and copies ran while one was open for 0% of the time, Pallas kernels for 14%

profile of v6, /device:TPU:0, one launch (start us, length us, event | category | flops | bytes accessed | tf_op | source)
XLA Modules:
  0.0 57.5 jit_solution(18249769955186499531)
XLA Ops:
  0.6 0.0 copy-start
  0.6 1.0 %copy-done = bf16[1,256,640]{2,1,0:T(8,128)(2,1)S(1)} copy-done((bf16[1,256,640]{2,1,0:T(8,128)(2,1)S(1)}, bf16[1,256,640]{2,1,0:T(8,128)(2,1)}, u32[]{:S(2)}) %copy-start) | copy-done | bytes 327704
  1.6 0.0 copy-start.1
  1.6 1.0 %copy-done.1 = bf16[1,256,640]{2,1,0:T(8,128)(2,1)S(1)} copy-done((bf16[1,256,640]{2,1,0:T(8,128)(2,1)S(1)}, bf16[1,256,640]{2,1,0:T(8,128)(2,1)}, u32[]{:S(2)}) %copy-start.1) | copy-done | bytes 327704
  2.6 0.0 copy-start.4
  2.6 0.0 copy-start.5
  2.6 0.0 copy-start.6
  2.6 1.5 %pack_heads.1 = (bf16[320,256]{1,0:T(8,128)(2,1)S(1)}, bf16[320,256]{1,0:T(8,128)(2,1)S(1)}, bf16[320,256]{1,0:T(8,128)(2,1)S(1)}, bf16[320,256]{1,0:T(8,128)(2,...) custom-call(bf16[256,640]{1,0:T(8,128)(2,1)S(1)} %bitcast.8, ...), custom_call_target="tpu_custom_call" | custom-call | tf_op jit(solution)/shard_map/pack_heads/pallas_call | solution.py:364
  4.1 0.0 copy-start.2
  4.1 4.0 %collective-permute-start.3 = (bf16[320,256]{1,0:T(8,128)(2,1)S(1)}, bf16[320,256]{1,0:T(8,128)(2,1)S(1)}, u32[]{:S(2)}, u32[]{:S(2)}) collective-permute-start(bf16[320,256]{1,0:T(8,128)(2,1)S(1)} %get-tuple-element.59), channel_id=1, source_target_pairs={{0,3},{1,2},{2,1},{3,0},{4,7},{5,6},{6,5},{7,4},{8,11},{9,10},{10,... | collective-permute-start | bytes 491528 | tf_op jit(solution)/shard_map/ppermute | solution.py:61
  8.2 0.0 copy-start.3
  8.2 0.4 collective-permute-start.4
  8.6 0.2 collective-permute-start.5
  8.8 0.0 copy-done.4
  8.8 0.0 copy-done.5
  8.8 0.0 copy-done.6
  8.8 0.0 copy-done.2
  8.8 0.0 copy-done.3
  8.9 1.2 %rotary_tables.1 = (f32[40,1024]{1,0:T(8,128)S(1)}, f32[40,1024]{1,0:T(8,128)S(1)}, f32[640,128]{1,0:T(8,128)S(1)}) custom-call(s32[1,4]{1,0:T(1,128)S(1)} %copy-done.4, s32[1,4]{1,0:T(1,128)S(1)} %copy-done.3, s32[4,8]{1,0:T(4,128)S(1)} %copy-done.6, f32[40,128]{1,0:T(8,128)S(1)} %copy-done.5, bf16[3,640]{1,0:T(4,128)(2,1)S(1)} %copy-done.2), custom_call_target="tpu_custom_call" | custom-call | flops 26214400 | tf_op jit(solution)/shard_map/rotary_tables/pallas_call | solution.py:379
  10.1 2.9 %collective-permute-start = (bf16[320,256]{1,0:T(8,128)(2,1)S(1)}, bf16[320,256]{1,0:T(8,128)(2,1)S(1)}, u32[]{:S(2)}, u32[]{:S(2)}) collective-permute-start(bf16[320,256]{1,0:T(8,128)(2,1)S(1)} %get-tuple-element.55), channel_id=1, source_target_pairs={{0,3},{1,2},{2,1},{3,0},{4,7},{5,6},{6,5},{7,4},{8,11},{9,10},{10,... | collective-permute-start | bytes 491528 | tf_op jit(solution)/shard_map/ppermute | solution.py:61
  13.0 0.4 collective-permute-start.1
  13.4 0.0 collective-permute-done.3.refs_1_
  13.4 1.7 %collective-permute-start.2 = (bf16[320,256]{1,0:T(8,128)(2,1)S(1)}, bf16[320,256]{1,0:T(8,128)(2,1)S(1)}, u32[]{:S(2)}, u32[]{:S(2)}) collective-permute-start(bf16[320,256]{1,0:T(8,128)(2,1)S(1)} %get-tuple-element.57), channel_id=1, source_target_pairs={{0,1},{1,0},{2,3},{3,2},{4,5},{5,4},{6,7},{7,6},{8,9},{9,8},{10,11... | collective-permute-start | bytes 491528 | tf_op jit(solution)/shard_map/ppermute | solution.py:61
  15.2 2.0 %collective-permute-done.4.refs_2_ = bf16[320,256]{1,0:T(8,128)(2,1)S(1)} collective-permute-done((bf16[320,256]{1,0:T(8,128)(2,1)S(1)}, bf16[320,256]{1,0:T(8,128)(2,1)S(1)}, u32[]{:S(2)}, u32[]{:S(2)}) %collective-permute-start.4) | collective-permute-done | bytes 163872 | tf_op jit(solution)/shard_map/ppermute | solution.py:61
  17.2 1.9 %collective-permute-done.5.refs_3_ = bf16[320,256]{1,0:T(8,128)(2,1)S(1)} collective-permute-done((bf16[320,256]{1,0:T(8,128)(2,1)S(1)}, bf16[320,256]{1,0:T(8,128)(2,1)S(1)}, u32[]{:S(2)}, u32[]{:S(2)}) %collective-permute-start.5) | collective-permute-done | bytes 163872 | tf_op jit(solution)/shard_map/ppermute | solution.py:61
  19.1 4.9 %attend_head.2 = (bf16[640,256]{1,0:T(8,128)(2,1)S(1)}, bf16[320,256]{1,0:T(8,128)(2,1)S(1)}, bf16[640,256]{1,0:T(8,128)(2,1)S(1)}, bf16[640,256]{1,0:T(8,128)(2,1)S(1)}, f32[8,128]{1,0:T(8,128)S(1)}) custom-call(s32[1,4]{1,0:T(1,128)S(1)} %copy-done.4, s32[4,8]{1,0:T(4,128)S(1)} %copy-done.6, f32[40,1024]{1,0:T(8,128)S(1)} %get-tuple-element.51.cosv, ...), custom_call_target="tpu_custom_call" | custom-call | flops 3221225472 | tf_op jit(solution)/shard_map/attend_head/pallas_call | solution.py:402
  24.1 0.0 collective-permute-done.refs_1_
  24.1 0.0 collective-permute-done.1.refs_2_
  24.1 0.0 collective-permute-done.2.refs_3_
  24.1 5.6 %attend_head.3 = (bf16[640,256]{1,0:T(8,128)(2,1)S(1)}, bf16[320,256]{1,0:T(8,128)(2,1)S(1)}, bf16[640,256]{1,0:T(8,128)(2,1)S(1)}, bf16[640,256]{1,0:T(8,128)(2,1)S(1)}, f32[32,8,128]{2,1,0:T(8,128)}) custom-call(s32[1,4]{1,0:T(1,128)S(1)} %copy-done.4, s32[4,8]{1,0:T(4,128)S(1)} %copy-done.6, ...), custom_call_target="tpu_custom_call", output_to_operand_aliasing={{0}: (10, {}), {2}: (11, {}), {3}: (12, {})} | custom-call | flops 3221225472 | tf_op jit(solution)/shard_map/attend_head/pallas_call | solution.py:402
  29.7 1.7 %collective-permute-start.8 = (bf16[640,256]{1,0:T(8,128)(2,1)S(1)}, bf16[640,256]{1,0:T(8,128)(2,1)S(1)}, u32[]{:S(2)}, u32[]{:S(2)}) collective-permute-start(bf16[640,256]{1,0:T(8,128)(2,1)S(1)} %get-tuple-element.71), channel_id=1, source_target_pairs={{2,0},{3,1},{0,2},{1,3},{6,4},{7,5},{4,6},{5,7},{10,8},{11,9},{8,1... | collective-permute-start | bytes 983048 | tf_op jit(solution)/shard_map/ppermute | solution.py:69
  31.4 0.3 collective-permute-start.9
  31.7 1.5 %collective-permute-start.6 = (bf16[320,256]{1,0:T(8,128)(2,1)S(1)}, bf16[320,256]{1,0:T(8,128)(2,1)S(1)}, u32[]{:S(2)}, u32[]{:S(2)}) collective-permute-start(bf16[320,256]{1,0:T(8,128)(2,1)S(1)} %get-tuple-element.67), channel_id=1, source_target_pairs={{3,0},{2,1},{1,2},{0,3},{7,4},{6,5},{5,6},{4,7},{11,8},{10,9},{9,1... | collective-permute-start | bytes 491528 | tf_op jit(solution)/shard_map/ppermute | solution.py:69
  33.2 1.4 %collective-permute-start.7 = (bf16[320,256]{1,0:T(8,128)(2,1)S(1)}, bf16[320,256]{1,0:T(8,128)(2,1)S(1)}, u32[]{:S(2)}, u32[]{:S(2)}) collective-permute-start(bf16[320,256]{1,0:T(8,128)(2,1)S(1)} %get-tuple-element.69), channel_id=1, source_target_pairs={{3,0},{2,1},{1,2},{0,3},{7,4},{6,5},{5,6},{4,7},{11,8},{10,9},{9,1... | collective-permute-start | bytes 491528 | tf_op jit(solution)/shard_map/ppermute | solution.py:69
  34.6 9.1 %collective-permute-done.6.refs_0_ = bf16[320,256]{1,0:T(8,128)(2,1)S(1)} collective-permute-done((bf16[320,256]{1,0:T(8,128)(2,1)S(1)}, bf16[320,256]{1,0:T(8,128)(2,1)S(1)}, u32[]{:S(2)}, u32[]{:S(2)}) %collective-permute-start.6) | collective-permute-done | bytes 163872 | tf_op jit(solution)/shard_map/ppermute | solution.py:69
  43.8 5.3 %all-to-all-start = ((f32[32,8,128]{2,1,0:T(8,128)}), f32[32,8,128]{2,1,0:T(8,128)S(1)}, u32[]{:S(2)}, u32[]{:S(2)}) async-start(f32[32,8,128]{2,1,0:T(8,128)} %get-tuple-element.77), calls=%async_computation | async-start | bytes 262144 | tf_op jit(solution)/shard_map/all_to_all | solution.py:426
  49.1 0.0 collective-permute-done.7.refs_1_
  49.1 0.0 collective-permute-done.8.refs_3_
  49.1 0.0 collective-permute-done.9.refs_4_
  49.1 1.9 %unpack_heads.1 = (bf16[256,640]{1,0:T(8,128)(2,1)}, bf16[256,640]{1,0:T(8,128)(2,1)}, bf16[256,640]{1,0:T(8,128)(2,1)}, bf16[256,640]{1,0:T(8,128)(2,1)}) custom-call(s32[1,4]{1,0:T(1,128)S(1)} %copy-done.4, s32[4,8]{1,0:T(4,128)S(1)} %copy-done.6, bf16[320,256]{1,0:T(8,128)(2,1)S(1)} %collective-permute-done.6.refs_0_, ...), custom_call_target="tpu_custom_call" | custom-call | flops 20000000000 | tf_op jit(solution)/shard_map/unpack_heads/pallas_call | solution.py:428
  51.0 5.9 %all-to-all-done.tiles = f32[32,8,128]{2,1,0:T(8,128)S(1)} async-done(((f32[32,8,128]{2,1,0:T(8,128)}), f32[32,8,128]{2,1,0:T(8,128)S(1)}, u32[]{:S(2)}, u32[]{:S(2)}) %all-to-all-start) | async-done | bytes 131104 | tf_op jit(solution)/shard_map/all_to_all | solution.py:426
  56.8 0.7 %bias_sums.1 = f32[3,640]{1,0:T(4,128)} custom-call(f32[32,8,128]{2,1,0:T(8,128)S(1)} %all-to-all-done.tiles), custom_call_target="tpu_custom_call" | custom-call | tf_op jit(solution)/shard_map/bias_sums/pallas_call | solution.py:439
Async XLA Ops:
  0.6 1.0 %copy-start = (bf16[1,256,640]{2,1,0:T(8,128)(2,1)S(1)}, bf16[1,256,640]{2,1,0:T(8,128)(2,1)}, u32[]{:S(2)}) copy-start(bf16[1,256,640]{2,1,0:T(8,128)(2,1)} %param.10) | copy-start | bytes 983044
  1.6 1.0 %copy-start.1 = (bf16[1,256,640]{2,1,0:T(8,128)(2,1)S(1)}, bf16[1,256,640]{2,1,0:T(8,128)(2,1)}, u32[]{:S(2)}) copy-start(bf16[1,256,640]{2,1,0:T(8,128)(2,1)} %param.11) | copy-start | bytes 983044
  2.6 6.3 %copy-start.4 = (s32[1,4]{1,0:T(1,128)S(1)}, s32[1,4]{1,0:T(1,128)}, u32[]{:S(2)}) copy-start(s32[1,4]{1,0:T(1,128)} %lengths.7) | copy-start | bytes 52
  2.6 6.3 %copy-start.5 = (f32[40,128]{1,0:T(8,128)S(1)}, f32[40,128]{1,0:T(8,128)}, u32[]{:S(2)}) copy-start(f32[40,128]{1,0:T(8,128)} %constant.5.clone.inverse) | copy-start | bytes 61444
  2.6 6.3 %copy-start.6 = (s32[4,8]{1,0:T(4,128)S(1)}, s32[4,8]{1,0:T(4,128)}, u32[]{:S(2)}) copy-start(s32[4,8]{1,0:T(4,128)} %constant.4.clone.table) | copy-start | bytes 388
  4.1 4.7 %copy-start.2 = (bf16[3,640]{1,0:T(4,128)(2,1)S(1)}, bf16[3,640]{1,0:T(4,128)(2,1)}, u32[]{:S(2)}) copy-start(bf16[3,640]{1,0:T(4,128)(2,1)} %bias.1) | copy-start | bytes 11524
  4.1 9.3 %collective-permute-start.3 = (bf16[320,256]{1,0:T(8,128)(2,1)S(1)}, bf16[320,256]{1,0:T(8,128)(2,1)S(1)}, u32[]{:S(2)}, u32[]{:S(2)}) collective-permute-start(bf16[320,256]{1,0:T(8,128)(2,1)S(1)} %get-tuple-element.59), channel_id=1, source_target_pairs={{0,3},{1,2},{2,1},{3,0},{4,7},{5,6},{6,5},{7,4},{8,11},{9,10},{10,... | collective-permute-start | bytes 491528 | tf_op jit(solution)/shard_map/ppermute | solution.py:61
  8.2 0.7 %copy-start.3 = (s32[1,4]{1,0:T(1,128)S(1)}, s32[1,4]{1,0:T(1,128)}, u32[]{:S(2)}) copy-start(s32[1,4]{1,0:T(1,128)} %widths.1) | copy-start | bytes 52
  8.2 9.1 %collective-permute-start.4 = (bf16[320,256]{1,0:T(8,128)(2,1)S(1)}, bf16[320,256]{1,0:T(8,128)(2,1)S(1)}, u32[]{:S(2)}, u32[]{:S(2)}) collective-permute-start(bf16[320,256]{1,0:T(8,128)(2,1)S(1)} %get-tuple-element.60), channel_id=1, source_target_pairs={{0,2},{1,3},{2,0},{3,1},{4,6},{5,7},{6,4},{7,5},{8,10},{9,11},{10,... | collective-permute-start | bytes 491528 | tf_op jit(solution)/shard_map/ppermute | solution.py:61
  8.6 10.5 %collective-permute-start.5 = (bf16[320,256]{1,0:T(8,128)(2,1)S(1)}, bf16[320,256]{1,0:T(8,128)(2,1)S(1)}, u32[]{:S(2)}, u32[]{:S(2)}) collective-permute-start(bf16[320,256]{1,0:T(8,128)(2,1)S(1)} %get-tuple-element.61), channel_id=1, source_target_pairs={{0,1},{1,0},{2,3},{3,2},{4,5},{5,4},{6,7},{7,6},{8,9},{9,8},{10,11... | collective-permute-start | bytes 491528 | tf_op jit(solution)/shard_map/ppermute | solution.py:61
  10.1 14.0 %collective-permute-start = (bf16[320,256]{1,0:T(8,128)(2,1)S(1)}, bf16[320,256]{1,0:T(8,128)(2,1)S(1)}, u32[]{:S(2)}, u32[]{:S(2)}) collective-permute-start(bf16[320,256]{1,0:T(8,128)(2,1)S(1)} %get-tuple-element.55), channel_id=1, source_target_pairs={{0,3},{1,2},{2,1},{3,0},{4,7},{5,6},{6,5},{7,4},{8,11},{9,10},{10,... | collective-permute-start | bytes 491528 | tf_op jit(solution)/shard_map/ppermute | solution.py:61
  13.0 11.1 %collective-permute-start.1 = (bf16[320,256]{1,0:T(8,128)(2,1)S(1)}, bf16[320,256]{1,0:T(8,128)(2,1)S(1)}, u32[]{:S(2)}, u32[]{:S(2)}) collective-permute-start(bf16[320,256]{1,0:T(8,128)(2,1)S(1)} %get-tuple-element.56), channel_id=1, source_target_pairs={{0,2},{1,3},{2,0},{3,1},{4,6},{5,7},{6,4},{7,5},{8,10},{9,11},{10,... | collective-permute-start | bytes 491528 | tf_op jit(solution)/shard_map/ppermute | solution.py:61
  13.4 10.7 %collective-permute-start.2 = (bf16[320,256]{1,0:T(8,128)(2,1)S(1)}, bf16[320,256]{1,0:T(8,128)(2,1)S(1)}, u32[]{:S(2)}, u32[]{:S(2)}) collective-permute-start(bf16[320,256]{1,0:T(8,128)(2,1)S(1)} %get-tuple-element.57), channel_id=1, source_target_pairs={{0,1},{1,0},{2,3},{3,2},{4,5},{5,4},{6,7},{7,6},{8,9},{9,8},{10,11... | collective-permute-start | bytes 491528 | tf_op jit(solution)/shard_map/ppermute | solution.py:61
  29.7 19.4 %collective-permute-start.8 = (bf16[640,256]{1,0:T(8,128)(2,1)S(1)}, bf16[640,256]{1,0:T(8,128)(2,1)S(1)}, u32[]{:S(2)}, u32[]{:S(2)}) collective-permute-start(bf16[640,256]{1,0:T(8,128)(2,1)S(1)} %get-tuple-element.71), channel_id=1, source_target_pairs={{2,0},{3,1},{0,2},{1,3},{6,4},{7,5},{4,6},{5,7},{10,8},{11,9},{8,1... | collective-permute-start | bytes 983048 | tf_op jit(solution)/shard_map/ppermute | solution.py:69
  31.4 17.7 %collective-permute-start.9 = (bf16[640,256]{1,0:T(8,128)(2,1)S(1)}, bf16[640,256]{1,0:T(8,128)(2,1)S(1)}, u32[]{:S(2)}, u32[]{:S(2)}) collective-permute-start(bf16[640,256]{1,0:T(8,128)(2,1)S(1)} %get-tuple-element.72), channel_id=1, source_target_pairs={{1,0},{0,1},{3,2},{2,3},{5,4},{4,5},{7,6},{6,7},{9,8},{8,9},{11,10... | collective-permute-start | bytes 983048 | tf_op jit(solution)/shard_map/ppermute | solution.py:69
  31.7 12.0 %collective-permute-start.6 = (bf16[320,256]{1,0:T(8,128)(2,1)S(1)}, bf16[320,256]{1,0:T(8,128)(2,1)S(1)}, u32[]{:S(2)}, u32[]{:S(2)}) collective-permute-start(bf16[320,256]{1,0:T(8,128)(2,1)S(1)} %get-tuple-element.67), channel_id=1, source_target_pairs={{3,0},{2,1},{1,2},{0,3},{7,4},{6,5},{5,6},{4,7},{11,8},{10,9},{9,1... | collective-permute-start | bytes 491528 | tf_op jit(solution)/shard_map/ppermute | solution.py:69
  33.2 15.9 %collective-permute-start.7 = (bf16[320,256]{1,0:T(8,128)(2,1)S(1)}, bf16[320,256]{1,0:T(8,128)(2,1)S(1)}, u32[]{:S(2)}, u32[]{:S(2)}) collective-permute-start(bf16[320,256]{1,0:T(8,128)(2,1)S(1)} %get-tuple-element.69), channel_id=1, source_target_pairs={{3,0},{2,1},{1,2},{0,3},{7,4},{6,5},{5,6},{4,7},{11,8},{10,9},{9,1... | collective-permute-start | bytes 491528 | tf_op jit(solution)/shard_map/ppermute | solution.py:69
  43.8 13.1 %all-to-all-start = ((f32[32,8,128]{2,1,0:T(8,128)}), f32[32,8,128]{2,1,0:T(8,128)S(1)}, u32[]{:S(2)}, u32[]{:S(2)}) async-start(f32[32,8,128]{2,1,0:T(8,128)} %get-tuple-element.77), calls=%async_computation | async-start | bytes 262144 | tf_op jit(solution)/shard_map/all_to_all | solution.py:426

commit v7 on v6

--- a/solution.py
+++ b/solution.py
@@ -18,7 +18,7 @@
 NEG = -1e30
 LANES = 128
 HALF = HEAD_DIM // 2
-PACK_MIB = 52
+PACK_KIB = 52 * 1024 + 600
 UNPACK_FLOPS = 20_000_000_000
 
 rope_base = 10000.0
@@ -155,7 +155,7 @@
     if head > 0:
         before, refs = refs[0], refs[slots:]
     outs, sums = refs[:slots], refs[slots]
-    qt_all, kt_all, vt_all, q_all, k_all, v_all, g_all, s_buf, e_buf, d_buf = refs[slots + 1 :]
+    qt_all, kt_all, vt_all, gt_all, k_all, v_all, s_buf, e_buf, d_buf = refs[slots + 1 :]
     me = lax.axis_index("tok")
     residue = lax.rem(me, SPAN)
     ids = []
@@ -170,6 +170,8 @@
     zeros = jnp.zeros((LANES - HEAD_DIM, tokd), jnp.float32)
     ones = jnp.where(rest_row < 2, 1.0, 0.0)
 
+    by_lanes = (((1,), (1,)), ((), ()))
+
     def block_of(slot):
         return slice(slot * tokd, (slot + 1) * tokd)
 
@@ -187,13 +189,14 @@
         )
         query = rotate(query, cos_b, sin_b) * (SCALE * LOG2E)
         for values, rest, turned, plain in (
-            (query, zeros, qt_all, q_all),
+            (query, zeros, qt_all, None),
             (rotate(key, cos_b, sin_b), zeros, kt_all, k_all),
             (value, ones, vt_all, v_all),
         ):
             values = jnp.concatenate([values, rest], axis=0).astype(jnp.bfloat16)
             turned[:, at] = values
-            plain[at, :] = values.T
+            if plain is not None:
+                plain[at, :] = values.T
 
     def scores(slot, other):
         part = jnp.dot(
@@ -218,7 +221,7 @@
         coarse = delta.astype(jnp.bfloat16).astype(jnp.float32)
         rest = jnp.where(rest_row == 0, -coarse, jnp.where(rest_row == 1, coarse - delta, 0.0))
         grad = jnp.concatenate([grad * inv, rest], axis=0).astype(jnp.bfloat16)
-        g_all[block_of(slot), :] = grad.T
+        gt_all[:, block_of(slot)] = grad
         return grad
 
     def dscores(slot, other, grad):
@@ -234,9 +237,20 @@
         put(slot, 1, dquery.astype(jnp.bfloat16))
         return jnp.where(ids[slot] >= 0, dquery, 0.0)
 
+    def value_part(slot):
+        dvalue = lax.dot_general(
+            gt_all[:HEAD_DIM, :],
+            e_buf[block_of(slot), :],
+            by_lanes,
+            preferred_element_type=jnp.float32,
+        )
+        put(slot, 3, dvalue.astype(jnp.bfloat16))
+        return jnp.where(ids[slot] >= 0, dvalue, 0.0)
+
     for slot in range(slots):
         stage(slot)
     dq_total = jnp.zeros((HEAD_DIM, tokd), jnp.float32)
+    dv_total = jnp.zeros((HEAD_DIM, tokd), jnp.float32)
     grad = None
     for slot in range(slots + 1):
         if slot < slots:
@@ -248,43 +262,54 @@
                 dscores(slot - 1, other, grad)
             if slot < slots:
                 exponentials(slot, other, top - offs[other])
+            else:
+                dv_total = dv_total + value_part(other)
         if slot > 0:
             dq_total = dq_total + query_part(slot - 1)
         if slot < slots:
             grad = output(slot)
     dk_total = jnp.zeros((HEAD_DIM, tokd), jnp.float32)
-    dv_total = jnp.zeros((1, LANES), jnp.float32)
     for slot in range(slots):
         at = block_of(slot)
-        live = ids[slot] >= 0
-        dvalue = jnp.dot(e_buf[at, :], g_all[...], preferred_element_type=jnp.float32)
-        dv_total = dv_total + jnp.where(live, jnp.sum(dvalue, axis=0, keepdims=True), 0.0)
-        put(slot, 3, dvalue.astype(jnp.bfloat16).T[:HEAD_DIM])
-        dkey = jnp.dot(d_buf[at, :], q_all[...], preferred_element_type=jnp.float32)
-        dkey = unrotate(dkey.T[:HEAD_DIM] * (1.0 / LOG2E), cosv[:, at], sinv[:, at])
+        dkey = lax.dot_general(
+            qt_all[:HEAD_DIM, :], d_buf[at, :], by_lanes, preferred_element_type=jnp.float32
+        )
+        dkey = unrotate(dkey * (1.0 / LOG2E), cosv[:, at], sinv[:, at])
         put(slot, 2, dkey.astype(jnp.bfloat16))
-        dk_total = dk_total + jnp.where(live, dkey, 0.0)
+        dk_total = dk_total + jnp.where(ids[slot] >= 0, dkey, 0.0)
     lane = lax.broadcasted_iota(jnp.int32, (HEAD_DIM, LANES), 1)
-    columns = jnp.where(
-        lane == 0,
-        jnp.sum(dq_total, axis=1, keepdims=True),
-        jnp.where(lane == 1, jnp.sum(dk_total, axis=1, keepdims=True), 0.0),
-    )
+    columns = jnp.zeros((HEAD_DIM, LANES), jnp.float32)
+    for number, total in enumerate((dq_total, dk_total, dv_total)):
+        total = jnp.sum(total, axis=1, keepdims=True) * factor
+        columns = jnp.where(lane == number, total, columns)
     columns = jnp.concatenate([columns, jnp.zeros((LANES - HEAD_DIM, LANES), jnp.float32)], axis=0)
     lines = columns.T
-    row = lax.broadcasted_iota(jnp.int32, (8, LANES), 0)
-    tile = jnp.zeros((8, LANES), jnp.float32) if head == 0 else before[...]
-    for number, total in enumerate((lines[0:1], lines[1:2], dv_total)):
-        tile = jnp.where(row == number * OWN_HEADS + head, total * factor, tile)
     if head + 1 < OWN_HEADS:
-        sums[...] = tile
+        sums[...] = lines[:8]
     else:
+        tile = join_sums(before[...], lines)
 
         def spread(device, carry):
             sums[device] = tile
             return carry
 
         lax.fori_loop(0, sums.shape[0], spread, 0, unroll=min(32, sums.shape[0]))
+
+
+FIT = LANES - HEAD_DIM
+LEFT = HEAD_DIM - FIT
+
+
+def join_sums(first, second):
+    lane = lax.broadcasted_iota(jnp.int32, (1, LANES), 1)
+    rows = []
+    last = jnp.zeros((1, LANES), jnp.float32)
+    for number in range(3):
+        moved = pltpu.roll(second[number : number + 1], HEAD_DIM, 1)
+        rows.append(jnp.where(lane < HEAD_DIM, first[number : number + 1], moved))
+        rest = jnp.where(lane < LEFT, moved, 0.0)
+        last = last + (pltpu.roll(rest, number * LEFT, 1) if number else rest)
+    return jnp.concatenate(rows + [last], axis=0)
 
 
 def unpack_kernel(slots, count, images, lengths, table, *refs):
@@ -325,13 +350,15 @@
     zero = jnp.zeros(tiles.shape[1:], jnp.float32)
     totals = lax.fori_loop(0, groups, add, (zero,) * SPAN, unroll=groups <= 8)
     for residue, total in enumerate(totals):
-        for phase in range(OWN_HEADS):
-            begin = (phase * SPAN + residue) * HEAD_DIM
-            for tensor in range(3):
-                at = tensor * OWN_HEADS + phase
-                bias_out[tensor : tensor + 1, begin : begin + HEAD_DIM] = total[
-                    at : at + 1, :HEAD_DIM
-                ]
+        first = residue * HEAD_DIM
+        second = (SPAN + residue) * HEAD_DIM
+        for number in range(3):
+            row = slice(number, number + 1)
+            bias_out[row, first : first + HEAD_DIM] = total[row, :HEAD_DIM]
+            bias_out[row, second : second + FIT] = total[row, HEAD_DIM:]
+            bias_out[row, second + FIT : second + HEAD_DIM] = total[
+                3:4, number * LEFT : (number + 1) * LEFT
+            ]
 
 
 def on_device(query_in, key_in, value_in, out_grad, bias, lengths, widths):
@@ -358,7 +385,7 @@
     tokens_all = devices * tokd
 
     def params(mib):
-        return pltpu.CompilerParams(vmem_limit_bytes=mib * 1024 * 1024)
+        return pltpu.CompilerParams(vmem_limit_bytes=int(mib * 1024 * 1024))
 
     inputs = (query_in[0], key_in[0], value_in[0], out_grad[0])
     sends = pl.pallas_call(
@@ -371,7 +398,7 @@
             pltpu.VMEM((4, model, tokd), jnp.bfloat16),
             pltpu.SemaphoreType.DMA((4,)),
         ],
-        compiler_params=params(PACK_MIB),
+        compiler_params=params(PACK_KIB / 1024),
         name="pack_heads",
     )(*inputs)
     got = [trade(sends[:slots])]
@@ -396,7 +423,7 @@
         last = phase + 1 == OWN_HEADS
         kept = [slot for slot in range(slots) if slot != EARLY]
         sums_shape = jax.ShapeDtypeStruct(
-            (devices, 8, LANES) if last else (8, LANES), jnp.float32
+            (devices, 4, LANES) if last else (8, LANES), jnp.float32
         )
         first_carried = 5 + slots + 1
         *results, total = pl.pallas_call(
@@ -410,8 +437,8 @@
             input_output_aliases={first_carried + at: slot for at, slot in enumerate(kept)}
             if carried
             else {},
-            scratch_shapes=[pltpu.VMEM((LANES, span), jnp.bfloat16)] * 3
-            + [pltpu.VMEM((span, LANES), jnp.bfloat16)] * 4
+            scratch_shapes=[pltpu.VMEM((LANES, span), jnp.bfloat16)] * 4
+            + [pltpu.VMEM((span, LANES), jnp.bfloat16)] * 2
             + [pltpu.VMEM((span, tokd), jnp.float32)]
             + [pltpu.VMEM((span, span), jnp.bfloat16)] * 2,
             compiler_params=params(32),
@@ -420,9 +447,9 @@
             ),
             name="attend_head",
         )(lengths, table, *tables, *got[phase], *carried)
+        results, total, early = lax.optimization_barrier((results, total, early))
         early.append(send_back(results[EARLY], EARLY))
         carried = [total] + [results[slot] for slot in kept]
-    total, early[:-1] = lax.optimization_barrier((total, early[:-1]))
     tiles = lax.all_to_all(total, ("dp", "tok"), 0, 0, tiled=True)
     late = [send_back(results[slot], slot) for slot in kept]
     outs = pl.pallas_call(

time: 57.8 us -> 46.5 us (0.80)
  waiting for transfers between devices: 19 us -> 9.4 us
  local copies, waits for them, and re-layouts: 1.96 us -> 0.03 us
    ppermute x4, waiting for transfers between devices: 9.12 us -> 3.46 us  [send_back(): lax.ppermute(result, 'tok', [(target, source) for source, target in pairs])]
    all_to_all x1, waiting for transfers between devices: 5.85 us -> 1.96 us  [on_device(): tiles = lax.all_to_all(total, ('dp', 'tok'), 0, 0, tiled=True)]
    unnamed x14 -> x10, local copies, waits for them, and re-layouts: 1.96 us -> 0.03 us
  transfers between devices with their start and end apart: 11 -> 11, of which waited for: 4 -> 5; matrix products, arithmetic and copies ran while one was open for 0% -> 0% of each run, Pallas kernels for 14% -> 30%
where the time goes in v7:
time: 46.5 us; the launch traced here: 46.3 us
  starting transfers between devices  19.8 us (43%)
  Pallas kernels  16.3 us (35%)
  waiting for transfers between devices  9.4 us (20%)
  between operations  0.72 us (2%)
    pallas_call x2, Pallas kernels, on_device(): pl.pallas_call(functools.partial(attend_kernel, slots, count, images, tok...  10.9 us
    ppermute x6, starting transfers between devices, trade(): moved.append(lax.ppermute(one, 'tok', pairs))  9.76 us
    all_to_all x1, starting transfers between devices, on_device(): tiles = lax.all_to_all(total, ('dp', 'tok'), 0, 0, tiled=True)  5.38 us
    ppermute x4, starting transfers between devices, send_back(): lax.ppermute(result, 'tok', [(target, source) for source, target in pairs])  4.68 us
    ppermute x6, waiting for transfers between devices, trade(): moved.append(lax.ppermute(one, 'tok', pairs))  3.98 us
    ppermute x4, waiting for transfers between devices, send_back(): lax.ppermute(result, 'tok', [(target, source) for source, target in pairs])  3.46 us
    all_to_all x1, waiting for transfers between devices, on_device(): tiles = lax.all_to_all(total, ('dp', 'tok'), 0, 0, tiled=True)  1.96 us
    pallas_call x1, Pallas kernels, on_device(): pl.pallas_call(functools.partial(unpack_kernel, slots, count, images), ou...  1.85 us
  transfers between devices with their start and end apart: 11, of which 5 were waited for; matrix products, arithmetic and copies ran while one was open for 0% of the time, Pallas kernels for 30%

profile of v7, /device:TPU:0, one launch (start us, length us, event | category | flops | bytes accessed | tf_op | source)
XLA Modules:
  0.0 46.3 jit_solution(10911925407842317933)
XLA Ops:
  0.6 0.0 copy-start.2
  0.6 0.0 copy-start.3
  0.7 0.0 copy-start.4
  0.7 1.7 %pack_heads.1 = (bf16[320,256]{1,0:T(8,128)(2,1)S(1)}, bf16[320,256]{1,0:T(8,128)(2,1)S(1)}, bf16[320,256]{1,0:T(8,128)(2,1)S(1)}, bf16[320,256]{1,0:T(8,128)(2,...) custom-call(bf16[256,640]{1,0:T(8,128)(2,1)} %bitcast.8, ...), custom_call_target="tpu_custom_call" | custom-call | tf_op jit(solution)/shard_map/pack_heads/pallas_call | solution.py:391
  2.4 0.0 copy-start
  2.4 4.0 %collective-permute-start.3 = (bf16[320,256]{1,0:T(8,128)(2,1)S(1)}, bf16[320,256]{1,0:T(8,128)(2,1)S(1)}, u32[]{:S(2)}, u32[]{:S(2)}) collective-permute-start(bf16[320,256]{1,0:T(8,128)(2,1)S(1)} %get-tuple-element.63), channel_id=1, source_target_pairs={{0,3},{1,2},{2,1},{3,0},{4,7},{5,6},{6,5},{7,4},{8,11},{9,10},{10,... | collective-permute-start | bytes 491528 | tf_op jit(solution)/shard_map/ppermute | solution.py:61
  6.4 0.0 copy-start.1
  6.4 0.4 collective-permute-start.4
  6.8 0.2 collective-permute-start.5
  7.1 0.0 copy-done.2
  7.1 0.0 copy-done.3
  7.1 0.0 copy-done.4
  7.1 0.0 copy-done
  7.1 0.0 copy-done.1
  7.1 1.2 %rotary_tables.1 = (f32[40,1024]{1,0:T(8,128)S(1)}, f32[40,1024]{1,0:T(8,128)S(1)}, f32[640,128]{1,0:T(8,128)S(1)}) custom-call(s32[1,4]{1,0:T(1,128)S(1)} %copy-done.2, s32[1,4]{1,0:T(1,128)S(1)} %copy-done.1, s32[4,8]{1,0:T(4,128)S(1)} %copy-done.4, f32[40,128]{1,0:T(8,128)S(1)} %copy-done.3, bf16[3,640]{1,0:T(4,128)(2,1)S(1)} %copy-done), custom_call_target="tpu_custom_call" | custom-call | flops 26214400 | tf_op jit(solution)/shard_map/rotary_tables/pallas_call | solution.py:406
  8.3 2.9 %collective-permute-start = (bf16[320,256]{1,0:T(8,128)(2,1)S(1)}, bf16[320,256]{1,0:T(8,128)(2,1)S(1)}, u32[]{:S(2)}, u32[]{:S(2)}) collective-permute-start(bf16[320,256]{1,0:T(8,128)(2,1)S(1)} %get-tuple-element.59), channel_id=1, source_target_pairs={{0,3},{1,2},{2,1},{3,0},{4,7},{5,6},{6,5},{7,4},{8,11},{9,10},{10,... | collective-permute-start | bytes 491528 | tf_op jit(solution)/shard_map/ppermute | solution.py:61
  11.2 0.4 collective-permute-start.1
  11.7 0.0 collective-permute-done.3.refs_1_
  11.7 1.7 %collective-permute-start.2 = (bf16[320,256]{1,0:T(8,128)(2,1)S(1)}, bf16[320,256]{1,0:T(8,128)(2,1)S(1)}, u32[]{:S(2)}, u32[]{:S(2)}) collective-permute-start(bf16[320,256]{1,0:T(8,128)(2,1)S(1)} %get-tuple-element.61), channel_id=1, source_target_pairs={{0,1},{1,0},{2,3},{3,2},{4,5},{5,4},{6,7},{7,6},{8,9},{9,8},{10,11... | collective-permute-start | bytes 491528 | tf_op jit(solution)/shard_map/ppermute | solution.py:61
  13.4 2.0 %collective-permute-done.4.refs_2_ = bf16[320,256]{1,0:T(8,128)(2,1)S(1)} collective-permute-done((bf16[320,256]{1,0:T(8,128)(2,1)S(1)}, bf16[320,256]{1,0:T(8,128)(2,1)S(1)}, u32[]{:S(2)}, u32[]{:S(2)}) %collective-permute-start.4) | collective-permute-done | bytes 163872 | tf_op jit(solution)/shard_map/ppermute | solution.py:61
  15.5 1.9 %collective-permute-done.5.refs_3_ = bf16[320,256]{1,0:T(8,128)(2,1)S(1)} collective-permute-done((bf16[320,256]{1,0:T(8,128)(2,1)S(1)}, bf16[320,256]{1,0:T(8,128)(2,1)S(1)}, u32[]{:S(2)}, u32[]{:S(2)}) %collective-permute-start.5) | collective-permute-done | bytes 163872 | tf_op jit(solution)/shard_map/ppermute | solution.py:61
  17.4 5.0 %attend_head.2 = (bf16[640,256]{1,0:T(8,128)(2,1)S(1)}, bf16[320,256]{1,0:T(8,128)(2,1)S(1)}, bf16[640,256]{1,0:T(8,128)(2,1)S(1)}, bf16[640,256]{1,0:T(8,128)(2,1)S(1)}, f32[8,128]{1,0:T(8,128)S(1)}) custom-call(s32[1,4]{1,0:T(1,128)S(1)} %copy-done.2, s32[4,8]{1,0:T(4,128)S(1)} %copy-done.4, f32[40,1024]{1,0:T(8,128)S(1)} %get-tuple-element.55.cosv, ...), custom_call_target="tpu_custom_call" | custom-call | flops 3221225472 | tf_op jit(solution)/shard_map/attend_head/pallas_call | solution.py:429
  22.4 0.7 %collective-permute-start.6 = (bf16[320,256]{1,0:T(8,128)(2,1)S(1)}, bf16[320,256]{1,0:T(8,128)(2,1)S(1)}, u32[]{:S(2)}, u32[]{:S(2)}) collective-permute-start(bf16[320,256]{1,0:T(8,128)(2,1)S(1)} %get-tuple-element.75), channel_id=1, source_target_pairs={{3,0},{2,1},{1,2},{0,3},{7,4},{6,5},{5,6},{4,7},{11,8},{10,9},{9,1... | collective-permute-start | bytes 491528 | tf_op jit(solution)/shard_map/ppermute | solution.py:69
  23.1 0.0 collective-permute-done.refs_1_
  23.1 0.0 collective-permute-done.1.refs_2_
  23.1 0.0 collective-permute-done.2.refs_3_
  23.1 5.8 %attend_head.3 = (bf16[640,256]{1,0:T(8,128)(2,1)S(1)}, bf16[320,256]{1,0:T(8,128)(2,1)S(1)}, bf16[640,256]{1,0:T(8,128)(2,1)S(1)}, bf16[640,256]{1,0:T(8,128)(2,1)S(1)}, f32[32,4,128]{2,1,0:T(4,128)}) custom-call(s32[1,4]{1,0:T(1,128)S(1)} %copy-done.2, s32[4,8]{1,0:T(4,128)S(1)} %copy-done.4, ...), custom_call_target="tpu_custom_call", output_to_operand_aliasing={{0}: (10, {}), {2}: (11, {}), {3}: (12, {})} | custom-call | flops 3221225472 | tf_op jit(solution)/shard_map/attend_head/pallas_call | solution.py:429
  28.9 0.0 collective-permute-done.6.refs_0_
  28.9 1.4 %collective-permute-start.8 = (bf16[640,256]{1,0:T(8,128)(2,1)S(1)}, bf16[640,256]{1,0:T(8,128)(2,1)S(1)}, u32[]{:S(2)}, u32[]{:S(2)}) collective-permute-start(bf16[640,256]{1,0:T(8,128)(2,1)S(1)} %get-tuple-element.79), channel_id=1, source_target_pairs={{2,0},{3,1},{0,2},{1,3},{6,4},{7,5},{4,6},{5,7},{10,8},{11,9},{8,1... | collective-permute-start | bytes 983048 | tf_op jit(solution)/shard_map/ppermute | solution.py:69
  30.4 1.4 %collective-permute-start.9 = (bf16[640,256]{1,0:T(8,128)(2,1)S(1)}, bf16[640,256]{1,0:T(8,128)(2,1)S(1)}, u32[]{:S(2)}, u32[]{:S(2)}) collective-permute-start(bf16[640,256]{1,0:T(8,128)(2,1)S(1)} %get-tuple-element.80), channel_id=1, source_target_pairs={{1,0},{0,1},{3,2},{2,3},{5,4},{4,5},{7,6},{6,7},{9,8},{8,9},{11,10... | collective-permute-start | bytes 983048 | tf_op jit(solution)/shard_map/ppermute | solution.py:69
  31.8 1.2 %collective-permute-start.7 = (bf16[320,256]{1,0:T(8,128)(2,1)S(1)}, bf16[320,256]{1,0:T(8,128)(2,1)S(1)}, u32[]{:S(2)}, u32[]{:S(2)}) collective-permute-start(bf16[320,256]{1,0:T(8,128)(2,1)S(1)} %get-tuple-element.77), channel_id=1, source_target_pairs={{3,0},{2,1},{1,2},{0,3},{7,4},{6,5},{5,6},{4,7},{11,8},{10,9},{9,1... | collective-permute-start | bytes 491528 | tf_op jit(solution)/shard_map/ppermute | solution.py:69
  32.9 5.4 %all-to-all-start = ((f32[32,4,128]{2,1,0:T(4,128)}), f32[32,4,128]{2,1,0:T(4,128)S(1)}, u32[]{:S(2)}, u32[]{:S(2)}) async-start(f32[32,4,128]{2,1,0:T(4,128)} %get-tuple-element.85), calls=%async_computation | async-start | bytes 131072 | tf_op jit(solution)/shard_map/all_to_all | solution.py:453
  38.3 2.9 %collective-permute-done.7.refs_1_ = bf16[320,256]{1,0:T(8,128)(2,1)S(1)} collective-permute-done((bf16[320,256]{1,0:T(8,128)(2,1)S(1)}, bf16[320,256]{1,0:T(8,128)(2,1)S(1)}, u32[]{:S(2)}, u32[]{:S(2)}) %collective-permute-start.7) | collective-permute-done | bytes 163872 | tf_op jit(solution)/shard_map/ppermute | solution.py:69
  41.3 0.0 collective-permute-done.8.refs_3_
  41.3 0.5 %collective-permute-done.9.refs_4_ = bf16[640,256]{1,0:T(8,128)(2,1)S(1)} collective-permute-done((bf16[640,256]{1,0:T(8,128)(2,1)S(1)}, bf16[640,256]{1,0:T(8,128)(2,1)S(1)}, u32[]{:S(2)}, u32[]{:S(2)}) %collective-permute-start.9) | collective-permute-done | bytes 327712 | tf_op jit(solution)/shard_map/ppermute | solution.py:69
  41.8 1.9 %unpack_heads.1 = (bf16[256,640]{1,0:T(8,128)(2,1)}, bf16[256,640]{1,0:T(8,128)(2,1)}, bf16[256,640]{1,0:T(8,128)(2,1)}, bf16[256,640]{1,0:T(8,128)(2,1)}) custom-call(s32[1,4]{1,0:T(1,128)S(1)} %copy-done.2, s32[4,8]{1,0:T(4,128)S(1)} %copy-done.4, bf16[320,256]{1,0:T(8,128)(2,1)S(1)} %collective-permute-done.6.refs_0_, ...), custom_call_target="tpu_custom_call" | custom-call | flops 20000000000 | tf_op jit(solution)/shard_map/unpack_heads/pallas_call | solution.py:455
  43.6 2.0 %all-to-all-done.tiles = f32[32,4,128]{2,1,0:T(4,128)S(1)} async-done(((f32[32,4,128]{2,1,0:T(4,128)}), f32[32,4,128]{2,1,0:T(4,128)S(1)}, u32[]{:S(2)}, u32[]{:S(2)}) %all-to-all-start) | async-done | bytes 65568 | tf_op jit(solution)/shard_map/all_to_all | solution.py:453
  45.6 0.7 %bias_sums.1 = f32[3,640]{1,0:T(4,128)} custom-call(f32[32,4,128]{2,1,0:T(4,128)S(1)} %all-to-all-done.tiles), custom_call_target="tpu_custom_call" | custom-call | tf_op jit(solution)/shard_map/bias_sums/pallas_call | solution.py:466
Async XLA Ops:
  0.6 6.4 %copy-start.2 = (s32[1,4]{1,0:T(1,128)S(1)}, s32[1,4]{1,0:T(1,128)}, u32[]{:S(2)}) copy-start(s32[1,4]{1,0:T(1,128)} %lengths.7) | copy-start | bytes 52
  0.6 6.4 %copy-start.3 = (f32[40,128]{1,0:T(8,128)S(1)}, f32[40,128]{1,0:T(8,128)}, u32[]{:S(2)}) copy-start(f32[40,128]{1,0:T(8,128)} %constant.5.clone.inverse) | copy-start | bytes 61444
  0.7 6.4 %copy-start.4 = (s32[4,8]{1,0:T(4,128)S(1)}, s32[4,8]{1,0:T(4,128)}, u32[]{:S(2)}) copy-start(s32[4,8]{1,0:T(4,128)} %constant.4.clone.table) | copy-start | bytes 388
  2.4 4.7 %copy-start = (bf16[3,640]{1,0:T(4,128)(2,1)S(1)}, bf16[3,640]{1,0:T(4,128)(2,1)}, u32[]{:S(2)}) copy-start(bf16[3,640]{1,0:T(4,128)(2,1)} %bias.1) | copy-start | bytes 11524
  2.4 9.3 %collective-permute-start.3 = (bf16[320,256]{1,0:T(8,128)(2,1)S(1)}, bf16[320,256]{1,0:T(8,128)(2,1)S(1)}, u32[]{:S(2)}, u32[]{:S(2)}) collective-permute-start(bf16[320,256]{1,0:T(8,128)(2,1)S(1)} %get-tuple-element.63), channel_id=1, source_target_pairs={{0,3},{1,2},{2,1},{3,0},{4,7},{5,6},{6,5},{7,4},{8,11},{9,10},{10,... | collective-permute-start | bytes 491528 | tf_op jit(solution)/shard_map/ppermute | solution.py:61
  6.4 0.7 %copy-start.1 = (s32[1,4]{1,0:T(1,128)S(1)}, s32[1,4]{1,0:T(1,128)}, u32[]{:S(2)}) copy-start(s32[1,4]{1,0:T(1,128)} %widths.1) | copy-start | bytes 52
  6.4 9.0 %collective-permute-start.4 = (bf16[320,256]{1,0:T(8,128)(2,1)S(1)}, bf16[320,256]{1,0:T(8,128)(2,1)S(1)}, u32[]{:S(2)}, u32[]{:S(2)}) collective-permute-start(bf16[320,256]{1,0:T(8,128)(2,1)S(1)} %get-tuple-element.64), channel_id=1, source_target_pairs={{0,2},{1,3},{2,0},{3,1},{4,6},{5,7},{6,4},{7,5},{8,10},{9,11},{10,... | collective-permute-start | bytes 491528 | tf_op jit(solution)/shard_map/ppermute | solution.py:61
  6.8 10.5 %collective-permute-start.5 = (bf16[320,256]{1,0:T(8,128)(2,1)S(1)}, bf16[320,256]{1,0:T(8,128)(2,1)S(1)}, u32[]{:S(2)}, u32[]{:S(2)}) collective-permute-start(bf16[320,256]{1,0:T(8,128)(2,1)S(1)} %get-tuple-element.65), channel_id=1, source_target_pairs={{0,1},{1,0},{2,3},{3,2},{4,5},{5,4},{6,7},{7,6},{8,9},{9,8},{10,11... | collective-permute-start | bytes 491528 | tf_op jit(solution)/shard_map/ppermute | solution.py:61
  8.3 14.8 %collective-permute-start = (bf16[320,256]{1,0:T(8,128)(2,1)S(1)}, bf16[320,256]{1,0:T(8,128)(2,1)S(1)}, u32[]{:S(2)}, u32[]{:S(2)}) collective-permute-start(bf16[320,256]{1,0:T(8,128)(2,1)S(1)} %get-tuple-element.59), channel_id=1, source_target_pairs={{0,3},{1,2},{2,1},{3,0},{4,7},{5,6},{6,5},{7,4},{8,11},{9,10},{10,... | collective-permute-start | bytes 491528 | tf_op jit(solution)/shard_map/ppermute | solution.py:61
  11.2 11.9 %collective-permute-start.1 = (bf16[320,256]{1,0:T(8,128)(2,1)S(1)}, bf16[320,256]{1,0:T(8,128)(2,1)S(1)}, u32[]{:S(2)}, u32[]{:S(2)}) collective-permute-start(bf16[320,256]{1,0:T(8,128)(2,1)S(1)} %get-tuple-element.60), channel_id=1, source_target_pairs={{0,2},{1,3},{2,0},{3,1},{4,6},{5,7},{6,4},{7,5},{8,10},{9,11},{10,... | collective-permute-start | bytes 491528 | tf_op jit(solution)/shard_map/ppermute | solution.py:61
  11.7 11.4 %collective-permute-start.2 = (bf16[320,256]{1,0:T(8,128)(2,1)S(1)}, bf16[320,256]{1,0:T(8,128)(2,1)S(1)}, u32[]{:S(2)}, u32[]{:S(2)}) collective-permute-start(bf16[320,256]{1,0:T(8,128)(2,1)S(1)} %get-tuple-element.61), channel_id=1, source_target_pairs={{0,1},{1,0},{2,3},{3,2},{4,5},{5,4},{6,7},{7,6},{8,9},{9,8},{10,11... | collective-permute-start | bytes 491528 | tf_op jit(solution)/shard_map/ppermute | solution.py:61
  22.4 6.5 %collective-permute-start.6 = (bf16[320,256]{1,0:T(8,128)(2,1)S(1)}, bf16[320,256]{1,0:T(8,128)(2,1)S(1)}, u32[]{:S(2)}, u32[]{:S(2)}) collective-permute-start(bf16[320,256]{1,0:T(8,128)(2,1)S(1)} %get-tuple-element.75), channel_id=1, source_target_pairs={{3,0},{2,1},{1,2},{0,3},{7,4},{6,5},{5,6},{4,7},{11,8},{10,9},{9,1... | collective-permute-start | bytes 491528 | tf_op jit(solution)/shard_map/ppermute | solution.py:69
  28.9 12.3 %collective-permute-start.8 = (bf16[640,256]{1,0:T(8,128)(2,1)S(1)}, bf16[640,256]{1,0:T(8,128)(2,1)S(1)}, u32[]{:S(2)}, u32[]{:S(2)}) collective-permute-start(bf16[640,256]{1,0:T(8,128)(2,1)S(1)} %get-tuple-element.79), channel_id=1, source_target_pairs={{2,0},{3,1},{0,2},{1,3},{6,4},{7,5},{4,6},{5,7},{10,8},{11,9},{8,1... | collective-permute-start | bytes 983048 | tf_op jit(solution)/shard_map/ppermute | solution.py:69
  30.4 11.4 %collective-permute-start.9 = (bf16[640,256]{1,0:T(8,128)(2,1)S(1)}, bf16[640,256]{1,0:T(8,128)(2,1)S(1)}, u32[]{:S(2)}, u32[]{:S(2)}) collective-permute-start(bf16[640,256]{1,0:T(8,128)(2,1)S(1)} %get-tuple-element.80), channel_id=1, source_target_pairs={{1,0},{0,1},{3,2},{2,3},{5,4},{4,5},{7,6},{6,7},{9,8},{8,9},{11,10... | collective-permute-start | bytes 983048 | tf_op jit(solution)/shard_map/ppermute | solution.py:69
  31.8 9.5 %collective-permute-start.7 = (bf16[320,256]{1,0:T(8,128)(2,1)S(1)}, bf16[320,256]{1,0:T(8,128)(2,1)S(1)}, u32[]{:S(2)}, u32[]{:S(2)}) collective-permute-start(bf16[320,256]{1,0:T(8,128)(2,1)S(1)} %get-tuple-element.77), channel_id=1, source_target_pairs={{3,0},{2,1},{1,2},{0,3},{7,4},{6,5},{5,6},{4,7},{11,8},{10,9},{9,1... | collective-permute-start | bytes 491528 | tf_op jit(solution)/shard_map/ppermute | solution.py:69
  32.9 12.7 %all-to-all-start = ((f32[32,4,128]{2,1,0:T(4,128)}), f32[32,4,128]{2,1,0:T(4,128)S(1)}, u32[]{:S(2)}, u32[]{:S(2)}) async-start(f32[32,4,128]{2,1,0:T(4,128)} %get-tuple-element.85), calls=%async_computation | async-start | bytes 131072 | tf_op jit(solution)/shard_map/all_to_all | solution.py:453

commit v8 on v7

--- a/solution.py
+++ b/solution.py
@@ -155,7 +155,7 @@
     if head > 0:
         before, refs = refs[0], refs[slots:]
     outs, sums = refs[:slots], refs[slots]
-    qt_all, kt_all, vt_all, gt_all, k_all, v_all, s_buf, e_buf, d_buf = refs[slots + 1 :]
+    qt_all, kt_all, vt_all, gt_all, k_all, v_all, s_buf, e_buf, d_buf = refs[slots + 1 : slots + 10]
     me = lax.axis_index("tok")
     residue = lax.rem(me, SPAN)
     ids = []
@@ -202,11 +202,11 @@
         part = jnp.dot(
             k_all[block_of(other), :], qt_all[:, block_of(slot)], preferred_element_type=jnp.float32
         )
-        s_buf[block_of(other), :] = part
+        s_buf[slot % 2, block_of(other), :] = part
         return jnp.max(part, axis=0, keepdims=True)
 
     def exponentials(slot, other, top):
-        part = jnp.exp2(s_buf[block_of(other), :] - top)
+        part = jnp.exp2(s_buf[slot % 2, block_of(other), :] - top)
         e_buf[block_of(other), block_of(slot)] = part.astype(jnp.bfloat16)
 
     def output(slot):
@@ -222,7 +222,8 @@
         rest = jnp.where(rest_row == 0, -coarse, jnp.where(rest_row == 1, coarse - delta, 0.0))
         grad = jnp.concatenate([grad * inv, rest], axis=0).astype(jnp.bfloat16)
         gt_all[:, block_of(slot)] = grad
-        return grad
+        spread = grad[:HEAD_DIM].astype(jnp.float32) * mixed[HEAD_DIM : HEAD_DIM + 1]
+        return grad, jnp.where(ids[slot] >= 0, spread, 0.0)
 
     def dscores(slot, other, grad):
         part = jnp.dot(v_all[block_of(other), :], grad, preferred_element_type=jnp.float32)
@@ -245,29 +246,31 @@
             preferred_element_type=jnp.float32,
         )
         put(slot, 3, dvalue.astype(jnp.bfloat16))
-        return jnp.where(ids[slot] >= 0, dvalue, 0.0)
 
     for slot in range(slots):
         stage(slot)
     dq_total = jnp.zeros((HEAD_DIM, tokd), jnp.float32)
     dv_total = jnp.zeros((HEAD_DIM, tokd), jnp.float32)
     grad = None
-    for slot in range(slots + 1):
-        if slot < slots:
+    offs = tops = None
+    for step in range(slots + 2):
+        ahead, slot, behind = step, step - 1, step - 2
+        if 0 <= slot < slots:
             offs = [jnp.where(ids[slot] == ids[other], 0.0, NEG) for other in range(slots)]
-            tops = [scores(slot, other) + offs[other] for other in range(slots)]
-            top = functools.reduce(jnp.maximum, tops)
+            top = functools.reduce(jnp.maximum, [one + off for one, off in zip(tops, offs)])
+        tops = []
         for other in range(slots):
-            if slot > 0:
-                dscores(slot - 1, other, grad)
-            if slot < slots:
+            if ahead < slots:
+                tops.append(scores(ahead, other))
+            if 0 <= behind:
+                dscores(behind, other, grad)
+            if 0 <= slot < slots:
                 exponentials(slot, other, top - offs[other])
-            else:
-                dv_total = dv_total + value_part(other)
-        if slot > 0:
-            dq_total = dq_total + query_part(slot - 1)
-        if slot < slots:
-            grad = output(slot)
+        if 0 <= behind:
+            dq_total = dq_total + query_part(behind)
+        if 0 <= slot < slots:
+            grad, spread = output(slot)
+            dv_total = dv_total + spread
     dk_total = jnp.zeros((HEAD_DIM, tokd), jnp.float32)
     for slot in range(slots):
         at = block_of(slot)
@@ -284,16 +287,24 @@
         columns = jnp.where(lane == number, total, columns)
     columns = jnp.concatenate([columns, jnp.zeros((LANES - HEAD_DIM, LANES), jnp.float32)], axis=0)
     lines = columns.T
+    copy = None
     if head + 1 < OWN_HEADS:
         sums[...] = lines[:8]
     else:
+        tiles, sem = refs[slots + 10 :]
         tile = join_sums(before[...], lines)
 
-        def spread(device, carry):
-            sums[device] = tile
+        def repeat(device, carry):
+            tiles[device] = tile
             return carry
 
-        lax.fori_loop(0, sums.shape[0], spread, 0, unroll=min(32, sums.shape[0]))
+        lax.fori_loop(0, tiles.shape[0], repeat, 0, unroll=min(32, tiles.shape[0]))
+        copy = pltpu.make_async_copy(tiles, sums, sem)
+        copy.start()
+    for slot in range(slots):
+        value_part(slot)
+    if copy is not None:
+        copy.wait()
 
 
 FIT = LANES - HEAD_DIM
@@ -433,14 +444,19 @@
             out_shape=[message if slot == EARLY else joined for slot in range(slots)]
             + [sums_shape],
             in_specs=[smem, smem] + [vmem] * (3 + slots + len(carried)),
-            out_specs=[vmem] * (slots + 1),
+            out_specs=[vmem] * slots + [hbm if last else vmem],
             input_output_aliases={first_carried + at: slot for at, slot in enumerate(kept)}
             if carried
             else {},
             scratch_shapes=[pltpu.VMEM((LANES, span), jnp.bfloat16)] * 4
             + [pltpu.VMEM((span, LANES), jnp.bfloat16)] * 2
-            + [pltpu.VMEM((span, tokd), jnp.float32)]
-            + [pltpu.VMEM((span, span), jnp.bfloat16)] * 2,
+            + [pltpu.VMEM((2, span, tokd), jnp.float32)]
+            + [pltpu.VMEM((span, span), jnp.bfloat16)] * 2
+            + (
+                [pltpu.VMEM(sums_shape.shape, jnp.float32), pltpu.SemaphoreType.DMA(())]
+                if last
+                else []
+            ),
             compiler_params=params(32),
             cost_estimate=pl.CostEstimate(
                 flops=12 * span * span * 256, bytes_accessed=0, transcendentals=0

time: 46.5 us -> 46.3 us (level)
  transfers between devices with their start and end apart: 11 -> 11, of which waited for: 5 -> 5; matrix products, arithmetic and copies ran while one was open for 0% -> 0% of each run, Pallas kernels for 30% -> 29%
where the time goes in v8:
time: 46.3 us; the launch traced here: 46.1 us
  starting transfers between devices  19.9 us (43%)
  Pallas kernels  16 us (35%)
  waiting for transfers between devices  9.44 us (20%)
  between operations  0.73 us (2%)
    pallas_call x2, Pallas kernels, on_device(): pl.pallas_call(functools.partial(attend_kernel, slots, count, images, tok...  10.5 us
    ppermute x6, starting transfers between devices, trade(): moved.append(lax.ppermute(one, 'tok', pairs))  9.76 us
    all_to_all x1, starting transfers between devices, on_device(): tiles = lax.all_to_all(total, ('dp', 'tok'), 0, 0, tiled=True)  5.37 us
    ppermute x4, starting transfers between devices, send_back(): lax.ppermute(result, 'tok', [(target, source) for source, target in pairs])  4.76 us
    ppermute x6, waiting for transfers between devices, trade(): moved.append(lax.ppermute(one, 'tok', pairs))  3.98 us
    ppermute x4, waiting for transfers between devices, send_back(): lax.ppermute(result, 'tok', [(target, source) for source, target in pairs])  3.51 us
    all_to_all x1, waiting for transfers between devices, on_device(): tiles = lax.all_to_all(total, ('dp', 'tok'), 0, 0, tiled=True)  1.95 us
    pallas_call x1, Pallas kernels, on_device(): pl.pallas_call(functools.partial(unpack_kernel, slots, count, images), ou...  1.85 us
  transfers between devices with their start and end apart: 11, of which 5 were waited for; matrix products, arithmetic and copies ran while one was open for 0% of the time, Pallas kernels for 29%

profile of v8, /device:TPU:0, one launch (start us, length us, event | category | flops | bytes accessed | tf_op | source)
XLA Modules:
  0.0 46.1 jit_solution(16814672037660062234)
XLA Ops:
  0.6 0.0 copy-start.2
  0.6 0.0 copy-start.3
  0.7 0.0 copy-start.4
  0.7 1.7 %pack_heads.1 = (bf16[320,256]{1,0:T(8,128)(2,1)S(1)}, bf16[320,256]{1,0:T(8,128)(2,1)S(1)}, bf16[320,256]{1,0:T(8,128)(2,1)S(1)}, bf16[320,256]{1,0:T(8,128)(2,...) custom-call(bf16[256,640]{1,0:T(8,128)(2,1)} %bitcast.8, ...), custom_call_target="tpu_custom_call" | custom-call | tf_op jit(solution)/shard_map/pack_heads/pallas_call | solution.py:402
  2.4 0.0 copy-start
  2.4 4.0 %collective-permute-start.3 = (bf16[320,256]{1,0:T(8,128)(2,1)S(1)}, bf16[320,256]{1,0:T(8,128)(2,1)S(1)}, u32[]{:S(2)}, u32[]{:S(2)}) collective-permute-start(bf16[320,256]{1,0:T(8,128)(2,1)S(1)} %get-tuple-element.63), channel_id=1, source_target_pairs={{0,3},{1,2},{2,1},{3,0},{4,7},{5,6},{6,5},{7,4},{8,11},{9,10},{10,... | collective-permute-start | bytes 491528 | tf_op jit(solution)/shard_map/ppermute | solution.py:61
  6.4 0.0 copy-start.1
  6.4 0.4 collective-permute-start.4
  6.8 0.2 collective-permute-start.5
  7.1 0.0 copy-done.2
  7.1 0.0 copy-done.3
  7.1 0.0 copy-done.4
  7.1 0.0 copy-done
  7.1 0.0 copy-done.1
  7.1 1.2 %rotary_tables.1 = (f32[40,1024]{1,0:T(8,128)S(1)}, f32[40,1024]{1,0:T(8,128)S(1)}, f32[640,128]{1,0:T(8,128)S(1)}) custom-call(s32[1,4]{1,0:T(1,128)S(1)} %copy-done.2, s32[1,4]{1,0:T(1,128)S(1)} %copy-done.1, s32[4,8]{1,0:T(4,128)S(1)} %copy-done.4, f32[40,128]{1,0:T(8,128)S(1)} %copy-done.3, bf16[3,640]{1,0:T(4,128)(2,1)S(1)} %copy-done), custom_call_target="tpu_custom_call" | custom-call | flops 26214400 | tf_op jit(solution)/shard_map/rotary_tables/pallas_call | solution.py:417
  8.3 2.9 %collective-permute-start = (bf16[320,256]{1,0:T(8,128)(2,1)S(1)}, bf16[320,256]{1,0:T(8,128)(2,1)S(1)}, u32[]{:S(2)}, u32[]{:S(2)}) collective-permute-start(bf16[320,256]{1,0:T(8,128)(2,1)S(1)} %get-tuple-element.59), channel_id=1, source_target_pairs={{0,3},{1,2},{2,1},{3,0},{4,7},{5,6},{6,5},{7,4},{8,11},{9,10},{10,... | collective-permute-start | bytes 491528 | tf_op jit(solution)/shard_map/ppermute | solution.py:61
  11.2 0.4 collective-permute-start.1
  11.7 0.0 collective-permute-done.3.refs_1_
  11.7 1.7 %collective-permute-start.2 = (bf16[320,256]{1,0:T(8,128)(2,1)S(1)}, bf16[320,256]{1,0:T(8,128)(2,1)S(1)}, u32[]{:S(2)}, u32[]{:S(2)}) collective-permute-start(bf16[320,256]{1,0:T(8,128)(2,1)S(1)} %get-tuple-element.61), channel_id=1, source_target_pairs={{0,1},{1,0},{2,3},{3,2},{4,5},{5,4},{6,7},{7,6},{8,9},{9,8},{10,11... | collective-permute-start | bytes 491528 | tf_op jit(solution)/shard_map/ppermute | solution.py:61
  13.4 2.0 %collective-permute-done.4.refs_2_ = bf16[320,256]{1,0:T(8,128)(2,1)S(1)} collective-permute-done((bf16[320,256]{1,0:T(8,128)(2,1)S(1)}, bf16[320,256]{1,0:T(8,128)(2,1)S(1)}, u32[]{:S(2)}, u32[]{:S(2)}) %collective-permute-start.4) | collective-permute-done | bytes 163872 | tf_op jit(solution)/shard_map/ppermute | solution.py:61
  15.5 1.9 %collective-permute-done.5.refs_3_ = bf16[320,256]{1,0:T(8,128)(2,1)S(1)} collective-permute-done((bf16[320,256]{1,0:T(8,128)(2,1)S(1)}, bf16[320,256]{1,0:T(8,128)(2,1)S(1)}, u32[]{:S(2)}, u32[]{:S(2)}) %collective-permute-start.5) | collective-permute-done | bytes 163872 | tf_op jit(solution)/shard_map/ppermute | solution.py:61
  17.4 5.0 %attend_head.2 = (bf16[640,256]{1,0:T(8,128)(2,1)S(1)}, bf16[320,256]{1,0:T(8,128)(2,1)S(1)}, bf16[640,256]{1,0:T(8,128)(2,1)S(1)}, bf16[640,256]{1,0:T(8,128)(2,1)S(1)}, f32[8,128]{1,0:T(8,128)S(1)}) custom-call(s32[1,4]{1,0:T(1,128)S(1)} %copy-done.2, s32[4,8]{1,0:T(4,128)S(1)} %copy-done.4, f32[40,1024]{1,0:T(8,128)S(1)} %get-tuple-element.55.cosv, ...), custom_call_target="tpu_custom_call" | custom-call | flops 3221225472 | tf_op jit(solution)/shard_map/attend_head/pallas_call | solution.py:440
  22.4 0.7 %collective-permute-start.6 = (bf16[320,256]{1,0:T(8,128)(2,1)S(1)}, bf16[320,256]{1,0:T(8,128)(2,1)S(1)}, u32[]{:S(2)}, u32[]{:S(2)}) collective-permute-start(bf16[320,256]{1,0:T(8,128)(2,1)S(1)} %get-tuple-element.75), channel_id=1, source_target_pairs={{3,0},{2,1},{1,2},{0,3},{7,4},{6,5},{5,6},{4,7},{11,8},{10,9},{9,1... | collective-permute-start | bytes 491528 | tf_op jit(solution)/shard_map/ppermute | solution.py:69
  23.1 0.0 collective-permute-done.refs_1_
  23.1 0.0 collective-permute-done.1.refs_2_
  23.1 0.0 collective-permute-done.2.refs_3_
  23.1 5.5 %attend_head.3 = (bf16[640,256]{1,0:T(8,128)(2,1)S(1)}, bf16[320,256]{1,0:T(8,128)(2,1)S(1)}, bf16[640,256]{1,0:T(8,128)(2,1)S(1)}, bf16[640,256]{1,0:T(8,128)(2,1)S(1)}, f32[32,4,128]{2,1,0:T(4,128)}) custom-call(s32[1,4]{1,0:T(1,128)S(1)} %copy-done.2, s32[4,8]{1,0:T(4,128)S(1)} %copy-done.4, ...), custom_call_target="tpu_custom_call", output_to_operand_aliasing={{0}: (10, {}), {2}: (11, {}), {3}: (12, {})} | custom-call | flops 3221225472 | tf_op jit(solution)/shard_map/attend_head/pallas_call | solution.py:440
  28.6 0.0 collective-permute-done.6.refs_0_
  28.6 1.7 %collective-permute-start.8 = (bf16[640,256]{1,0:T(8,128)(2,1)S(1)}, bf16[640,256]{1,0:T(8,128)(2,1)S(1)}, u32[]{:S(2)}, u32[]{:S(2)}) collective-permute-start(bf16[640,256]{1,0:T(8,128)(2,1)S(1)} %get-tuple-element.79), channel_id=1, source_target_pairs={{2,0},{3,1},{0,2},{1,3},{6,4},{7,5},{4,6},{5,7},{10,8},{11,9},{8,1... | collective-permute-start | bytes 983048 | tf_op jit(solution)/shard_map/ppermute | solution.py:69
  30.4 1.2 %collective-permute-start.9 = (bf16[640,256]{1,0:T(8,128)(2,1)S(1)}, bf16[640,256]{1,0:T(8,128)(2,1)S(1)}, u32[]{:S(2)}, u32[]{:S(2)}) collective-permute-start(bf16[640,256]{1,0:T(8,128)(2,1)S(1)} %get-tuple-element.80), channel_id=1, source_target_pairs={{1,0},{0,1},{3,2},{2,3},{5,4},{4,5},{7,6},{6,7},{9,8},{8,9},{11,10... | collective-permute-start | bytes 983048 | tf_op jit(solution)/shard_map/ppermute | solution.py:69
  31.5 1.2 %collective-permute-start.7 = (bf16[320,256]{1,0:T(8,128)(2,1)S(1)}, bf16[320,256]{1,0:T(8,128)(2,1)S(1)}, u32[]{:S(2)}, u32[]{:S(2)}) collective-permute-start(bf16[320,256]{1,0:T(8,128)(2,1)S(1)} %get-tuple-element.77), channel_id=1, source_target_pairs={{3,0},{2,1},{1,2},{0,3},{7,4},{6,5},{5,6},{4,7},{11,8},{10,9},{9,1... | collective-permute-start | bytes 491528 | tf_op jit(solution)/shard_map/ppermute | solution.py:69
  32.7 5.4 %all-to-all-start = ((f32[32,4,128]{2,1,0:T(4,128)}), f32[32,4,128]{2,1,0:T(4,128)S(1)}, u32[]{:S(2)}, u32[]{:S(2)}) async-start(f32[32,4,128]{2,1,0:T(4,128)} %get-tuple-element.85), calls=%async_computation | async-start | bytes 131072 | tf_op jit(solution)/shard_map/all_to_all | solution.py:469
  38.1 3.0 %collective-permute-done.7.refs_1_ = bf16[320,256]{1,0:T(8,128)(2,1)S(1)} collective-permute-done((bf16[320,256]{1,0:T(8,128)(2,1)S(1)}, bf16[320,256]{1,0:T(8,128)(2,1)S(1)}, u32[]{:S(2)}, u32[]{:S(2)}) %collective-permute-start.7) | collective-permute-done | bytes 163872 | tf_op jit(solution)/shard_map/ppermute | solution.py:69
  41.0 0.0 collective-permute-done.8.refs_3_
  41.0 0.5 %collective-permute-done.9.refs_4_ = bf16[640,256]{1,0:T(8,128)(2,1)S(1)} collective-permute-done((bf16[640,256]{1,0:T(8,128)(2,1)S(1)}, bf16[640,256]{1,0:T(8,128)(2,1)S(1)}, u32[]{:S(2)}, u32[]{:S(2)}) %collective-permute-start.9) | collective-permute-done | bytes 327712 | tf_op jit(solution)/shard_map/ppermute | solution.py:69
  41.5 1.9 %unpack_heads.1 = (bf16[256,640]{1,0:T(8,128)(2,1)}, bf16[256,640]{1,0:T(8,128)(2,1)}, bf16[256,640]{1,0:T(8,128)(2,1)}, bf16[256,640]{1,0:T(8,128)(2,1)}) custom-call(s32[1,4]{1,0:T(1,128)S(1)} %copy-done.2, s32[4,8]{1,0:T(4,128)S(1)} %copy-done.4, bf16[320,256]{1,0:T(8,128)(2,1)S(1)} %collective-permute-done.6.refs_0_, ...), custom_call_target="tpu_custom_call" | custom-call | flops 20000000000 | tf_op jit(solution)/shard_map/unpack_heads/pallas_call | solution.py:471
  43.4 2.0 %all-to-all-done.tiles = f32[32,4,128]{2,1,0:T(4,128)S(1)} async-done(((f32[32,4,128]{2,1,0:T(4,128)}), f32[32,4,128]{2,1,0:T(4,128)S(1)}, u32[]{:S(2)}, u32[]{:S(2)}) %all-to-all-start) | async-done | bytes 65568 | tf_op jit(solution)/shard_map/all_to_all | solution.py:469
  45.3 0.7 %bias_sums.1 = f32[3,640]{1,0:T(4,128)} custom-call(f32[32,4,128]{2,1,0:T(4,128)S(1)} %all-to-all-done.tiles), custom_call_target="tpu_custom_call" | custom-call | tf_op jit(solution)/shard_map/bias_sums/pallas_call | solution.py:482
Async XLA Ops:
  0.6 6.4 %copy-start.2 = (s32[1,4]{1,0:T(1,128)S(1)}, s32[1,4]{1,0:T(1,128)}, u32[]{:S(2)}) copy-start(s32[1,4]{1,0:T(1,128)} %lengths.7) | copy-start | bytes 52
  0.6 6.4 %copy-start.3 = (f32[40,128]{1,0:T(8,128)S(1)}, f32[40,128]{1,0:T(8,128)}, u32[]{:S(2)}) copy-start(f32[40,128]{1,0:T(8,128)} %constant.5.clone.inverse) | copy-start | bytes 61444
  0.7 6.4 %copy-start.4 = (s32[4,8]{1,0:T(4,128)S(1)}, s32[4,8]{1,0:T(4,128)}, u32[]{:S(2)}) copy-start(s32[4,8]{1,0:T(4,128)} %constant.4.clone.table) | copy-start | bytes 388
  2.4 4.7 %copy-start = (bf16[3,640]{1,0:T(4,128)(2,1)S(1)}, bf16[3,640]{1,0:T(4,128)(2,1)}, u32[]{:S(2)}) copy-start(bf16[3,640]{1,0:T(4,128)(2,1)} %bias.1) | copy-start | bytes 11524
  2.4 9.3 %collective-permute-start.3 = (bf16[320,256]{1,0:T(8,128)(2,1)S(1)}, bf16[320,256]{1,0:T(8,128)(2,1)S(1)}, u32[]{:S(2)}, u32[]{:S(2)}) collective-permute-start(bf16[320,256]{1,0:T(8,128)(2,1)S(1)} %get-tuple-element.63), channel_id=1, source_target_pairs={{0,3},{1,2},{2,1},{3,0},{4,7},{5,6},{6,5},{7,4},{8,11},{9,10},{10,... | collective-permute-start | bytes 491528 | tf_op jit(solution)/shard_map/ppermute | solution.py:61
  6.4 0.7 %copy-start.1 = (s32[1,4]{1,0:T(1,128)S(1)}, s32[1,4]{1,0:T(1,128)}, u32[]{:S(2)}) copy-start(s32[1,4]{1,0:T(1,128)} %widths.1) | copy-start | bytes 52
  6.4 9.0 %collective-permute-start.4 = (bf16[320,256]{1,0:T(8,128)(2,1)S(1)}, bf16[320,256]{1,0:T(8,128)(2,1)S(1)}, u32[]{:S(2)}, u32[]{:S(2)}) collective-permute-start(bf16[320,256]{1,0:T(8,128)(2,1)S(1)} %get-tuple-element.64), channel_id=1, source_target_pairs={{0,2},{1,3},{2,0},{3,1},{4,6},{5,7},{6,4},{7,5},{8,10},{9,11},{10,... | collective-permute-start | bytes 491528 | tf_op jit(solution)/shard_map/ppermute | solution.py:61
  6.8 10.5 %collective-permute-start.5 = (bf16[320,256]{1,0:T(8,128)(2,1)S(1)}, bf16[320,256]{1,0:T(8,128)(2,1)S(1)}, u32[]{:S(2)}, u32[]{:S(2)}) collective-permute-start(bf16[320,256]{1,0:T(8,128)(2,1)S(1)} %get-tuple-element.65), channel_id=1, source_target_pairs={{0,1},{1,0},{2,3},{3,2},{4,5},{5,4},{6,7},{7,6},{8,9},{9,8},{10,11... | collective-permute-start | bytes 491528 | tf_op jit(solution)/shard_map/ppermute | solution.py:61
  8.3 14.7 %collective-permute-start = (bf16[320,256]{1,0:T(8,128)(2,1)S(1)}, bf16[320,256]{1,0:T(8,128)(2,1)S(1)}, u32[]{:S(2)}, u32[]{:S(2)}) collective-permute-start(bf16[320,256]{1,0:T(8,128)(2,1)S(1)} %get-tuple-element.59), channel_id=1, source_target_pairs={{0,3},{1,2},{2,1},{3,0},{4,7},{5,6},{6,5},{7,4},{8,11},{9,10},{10,... | collective-permute-start | bytes 491528 | tf_op jit(solution)/shard_map/ppermute | solution.py:61
  11.2 11.8 %collective-permute-start.1 = (bf16[320,256]{1,0:T(8,128)(2,1)S(1)}, bf16[320,256]{1,0:T(8,128)(2,1)S(1)}, u32[]{:S(2)}, u32[]{:S(2)}) collective-permute-start(bf16[320,256]{1,0:T(8,128)(2,1)S(1)} %get-tuple-element.60), channel_id=1, source_target_pairs={{0,2},{1,3},{2,0},{3,1},{4,6},{5,7},{6,4},{7,5},{8,10},{9,11},{10,... | collective-permute-start | bytes 491528 | tf_op jit(solution)/shard_map/ppermute | solution.py:61
  11.7 11.4 %collective-permute-start.2 = (bf16[320,256]{1,0:T(8,128)(2,1)S(1)}, bf16[320,256]{1,0:T(8,128)(2,1)S(1)}, u32[]{:S(2)}, u32[]{:S(2)}) collective-permute-start(bf16[320,256]{1,0:T(8,128)(2,1)S(1)} %get-tuple-element.61), channel_id=1, source_target_pairs={{0,1},{1,0},{2,3},{3,2},{4,5},{5,4},{6,7},{7,6},{8,9},{9,8},{10,11... | collective-permute-start | bytes 491528 | tf_op jit(solution)/shard_map/ppermute | solution.py:61
  22.4 6.3 %collective-permute-start.6 = (bf16[320,256]{1,0:T(8,128)(2,1)S(1)}, bf16[320,256]{1,0:T(8,128)(2,1)S(1)}, u32[]{:S(2)}, u32[]{:S(2)}) collective-permute-start(bf16[320,256]{1,0:T(8,128)(2,1)S(1)} %get-tuple-element.75), channel_id=1, source_target_pairs={{3,0},{2,1},{1,2},{0,3},{7,4},{6,5},{5,6},{4,7},{11,8},{10,9},{9,1... | collective-permute-start | bytes 491528 | tf_op jit(solution)/shard_map/ppermute | solution.py:69
  28.6 12.4 %collective-permute-start.8 = (bf16[640,256]{1,0:T(8,128)(2,1)S(1)}, bf16[640,256]{1,0:T(8,128)(2,1)S(1)}, u32[]{:S(2)}, u32[]{:S(2)}) collective-permute-start(bf16[640,256]{1,0:T(8,128)(2,1)S(1)} %get-tuple-element.79), channel_id=1, source_target_pairs={{2,0},{3,1},{0,2},{1,3},{6,4},{7,5},{4,6},{5,7},{10,8},{11,9},{8,1... | collective-permute-start | bytes 983048 | tf_op jit(solution)/shard_map/ppermute | solution.py:69
  30.4 11.2 %collective-permute-start.9 = (bf16[640,256]{1,0:T(8,128)(2,1)S(1)}, bf16[640,256]{1,0:T(8,128)(2,1)S(1)}, u32[]{:S(2)}, u32[]{:S(2)}) collective-permute-start(bf16[640,256]{1,0:T(8,128)(2,1)S(1)} %get-tuple-element.80), channel_id=1, source_target_pairs={{1,0},{0,1},{3,2},{2,3},{5,4},{4,5},{7,6},{6,7},{9,8},{8,9},{11,10... | collective-permute-start | bytes 983048 | tf_op jit(solution)/shard_map/ppermute | solution.py:69
  31.5 9.5 %collective-permute-start.7 = (bf16[320,256]{1,0:T(8,128)(2,1)S(1)}, bf16[320,256]{1,0:T(8,128)(2,1)S(1)}, u32[]{:S(2)}, u32[]{:S(2)}) collective-permute-start(bf16[320,256]{1,0:T(8,128)(2,1)S(1)} %get-tuple-element.77), channel_id=1, source_target_pairs={{3,0},{2,1},{1,2},{0,3},{7,4},{6,5},{5,6},{4,7},{11,8},{10,9},{9,1... | collective-permute-start | bytes 491528 | tf_op jit(solution)/shard_map/ppermute | solution.py:69
  32.7 12.7 %all-to-all-start = ((f32[32,4,128]{2,1,0:T(4,128)}), f32[32,4,128]{2,1,0:T(4,128)S(1)}, u32[]{:S(2)}, u32[]{:S(2)}) async-start(f32[32,4,128]{2,1,0:T(4,128)} %get-tuple-element.85), calls=%async_computation | async-start | bytes 131072 | tf_op jit(solution)/shard_map/all_to_all | solution.py:469

commit v9 on v8

--- a/solution.py
+++ b/solution.py
@@ -28,9 +28,15 @@
     return count in (SPAN, 2 * SPAN)
 
 
+def closed_step(slot):
+    return (SPAN - slot) % SPAN
+
+
 def trade_rounds(count):
     if is_closed(count):
-        return [[(one, one ^ step) for one in range(count)] for step in range(SPAN - 1, 0, -1)]
+        return [
+            [(one, one ^ closed_step(slot)) for one in range(count)] for slot in range(1, SPAN)
+        ]
     rounds = []
     for shift in [*range(1, SPAN), *range(-1, -SPAN, -1)]:
         rounds.append(
@@ -113,8 +119,10 @@
     for copy in copies:
         copy.start()
     me = lax.rem(lax.axis_index("tok"), SPAN)
-    steps = [0] + (
-        [*range(SPAN - 1, 0, -1)] if closed else [*range(1, SPAN), *range(SPAN - 1, 0, -1)]
+    steps = (
+        [closed_step(slot) for slot in range(SPAN)]
+        if closed
+        else [0, *range(1, SPAN), *range(SPAN - 1, 0, -1)]
     )
     for number, copy in enumerate(copies):
         copy.wait()
@@ -128,14 +136,19 @@
                 ]
 
 
-def tables_kernel(images, tokd, lengths, widths, table, inverse, bias, cos_out, sin_out, bias_out):
+def tables_kernel(images, count, tokd, lengths, widths, table, inverse, bias, *refs):
+    cos_out, sin_out, mask_out, bias_out, turned = refs
     me = lax.axis_index("tok")
+    residue = lax.rem(me, SPAN)
     slots = table.shape[0]
     spot = lax.broadcasted_iota(jnp.int32, (HALF, tokd), 1)
     by_row = lax.broadcasted_iota(jnp.int32, (HALF, tokd), 0) < HALF // 2
+    ids = []
     for slot in range(slots):
         block = table[slot, me]
         image, start = image_of(block, lengths, images)
+        handled = (block >= 0) & (handler_of(start, residue, count) == me)
+        ids.append(jnp.where(handled, image, -1 - slot))
         width = widths[0, image]
         bits = jnp.where(width == tokd, 0, jnp.where(width * 2 == tokd, 1, 2))
         shift = tokd.bit_length() - 1 - bits
@@ -145,32 +158,44 @@
         angle = jnp.where(by_row, rowpos, colpos).astype(jnp.float32) * inverse[:, 0:1]
         cos_out[:, slot * tokd : (slot + 1) * tokd] = jnp.cos(angle)
         sin_out[:, slot * tokd : (slot + 1) * tokd] = jnp.sin(angle)
+    for slot in range(slots):
+        for other in range(slots):
+            off = jnp.where(ids[slot] == ids[other], 0.0, NEG)
+            row = slot * slots + other
+            mask_out[row : row + 1, :] = jnp.full((1, tokd), off, jnp.float32)
+        row = slots * slots + slot
+        live = jnp.where(ids[slot] >= 0, 1.0, 0.0)
+        mask_out[row : row + 1, :] = jnp.full((1, tokd), live, jnp.float32)
     plain = bias[...].astype(jnp.float32)
     rest = jnp.zeros((LANES - plain.shape[0], plain.shape[1]), jnp.float32)
-    bias_out[...] = jnp.concatenate([plain, rest], axis=0).T
-
-
-def attend_kernel(slots, count, images, tokd, head, factor, lengths, table, cosv, sinv, bias, *refs):
+    turned[...] = jnp.concatenate([plain, rest], axis=0).T
+    for phase in range(OWN_HEADS):
+        begin = pl.multiple_of((phase * SPAN + residue) * HEAD_DIM, 16)
+        bias_out[phase * HEAD_DIM : (phase + 1) * HEAD_DIM, :] = turned[pl.ds(begin, HEAD_DIM), :]
+
+
+def attend_kernel(slots, closed, tokd, head, factor, cosv, sinv, masks, bias, *refs):
     msgs, refs = refs[:slots], refs[slots:]
     if head > 0:
         before, refs = refs[0], refs[slots:]
     outs, sums = refs[:slots], refs[slots]
     qt_all, kt_all, vt_all, gt_all, k_all, v_all, s_buf, e_buf, d_buf = refs[slots + 1 : slots + 10]
-    me = lax.axis_index("tok")
-    residue = lax.rem(me, SPAN)
-    ids = []
-    for slot in range(slots):
-        block = table[slot, me]
-        image, start = image_of(block, lengths, images)
-        handled = (block >= 0) & (handler_of(start, residue, count) == me)
-        ids.append(jnp.where(handled, image, -1 - slot))
-    begin = pl.multiple_of((head * SPAN + residue) * HEAD_DIM, 16)
-    own_bias = bias[pl.ds(begin, HEAD_DIM), :]
+    own_bias = bias[head * HEAD_DIM : (head + 1) * HEAD_DIM, :]
     rest_row = lax.broadcasted_iota(jnp.int32, (LANES - HEAD_DIM, tokd), 0)
     zeros = jnp.zeros((LANES - HEAD_DIM, tokd), jnp.float32)
     ones = jnp.where(rest_row < 2, 1.0, 0.0)
 
     by_lanes = (((1,), (1,)), ((), ()))
+
+    def off_row(slot, other):
+        row = slot * slots + other
+        return masks[row : row + 1, :]
+
+    def live(slot, values):
+        if closed:
+            return values
+        row = slots * slots + slot
+        return values * masks[row : row + 1, :]
 
     def block_of(slot):
         return slice(slot * tokd, (slot + 1) * tokd)
@@ -223,7 +248,7 @@
         grad = jnp.concatenate([grad * inv, rest], axis=0).astype(jnp.bfloat16)
         gt_all[:, block_of(slot)] = grad
         spread = grad[:HEAD_DIM].astype(jnp.float32) * mixed[HEAD_DIM : HEAD_DIM + 1]
-        return grad, jnp.where(ids[slot] >= 0, spread, 0.0)
+        return grad, live(slot, spread)
 
     def dscores(slot, other, grad):
         part = jnp.dot(v_all[block_of(other), :], grad, preferred_element_type=jnp.float32)
@@ -236,7 +261,7 @@
         dquery = jnp.dot(kt_all[:HEAD_DIM, :], d_buf[:, at], preferred_element_type=jnp.float32)
         dquery = unrotate(dquery * SCALE, cosv[:, at], sinv[:, at])
         put(slot, 1, dquery.astype(jnp.bfloat16))
-        return jnp.where(ids[slot] >= 0, dquery, 0.0)
+        return live(slot, dquery)
 
     def value_part(slot):
         dvalue = lax.dot_general(
@@ -256,7 +281,7 @@
     for step in range(slots + 2):
         ahead, slot, behind = step, step - 1, step - 2
         if 0 <= slot < slots:
-            offs = [jnp.where(ids[slot] == ids[other], 0.0, NEG) for other in range(slots)]
+            offs = [off_row(slot, other) for other in range(slots)]
             top = functools.reduce(jnp.maximum, [one + off for one, off in zip(tops, offs)])
         tops = []
         for other in range(slots):
@@ -279,7 +304,7 @@
         )
         dkey = unrotate(dkey * (1.0 / LOG2E), cosv[:, at], sinv[:, at])
         put(slot, 2, dkey.astype(jnp.bfloat16))
-        dk_total = dk_total + jnp.where(ids[slot] >= 0, dkey, 0.0)
+        dk_total = dk_total + live(slot, dkey)
     lane = lax.broadcasted_iota(jnp.int32, (HEAD_DIM, LANES), 1)
     columns = jnp.zeros((HEAD_DIM, LANES), jnp.float32)
     for number, total in enumerate((dq_total, dk_total, dv_total)):
@@ -323,32 +348,42 @@
     return jnp.concatenate(rows + [last], axis=0)
 
 
-def unpack_kernel(slots, count, images, lengths, table, *refs):
-    msgs, outs, held = refs[: slots + OWN_HEADS - 1], refs[slots + OWN_HEADS - 1 : -1], refs[-1]
+def unpack_kernel(slots, count, images, *refs):
+    closed = is_closed(count)
+    if not closed:
+        lengths, table, *refs = refs
+    msgs, refs = refs[: slots + OWN_HEADS - 1], refs[slots + OWN_HEADS - 1 :]
+    outs, held, ready, sems = refs[:4], refs[4], refs[5], refs[6]
     early, late = msgs[:OWN_HEADS], list(msgs[OWN_HEADS:])
     late.insert(EARLY, None)
     me = lax.axis_index("tok")
-    _, start = image_of(me, lengths, images)
+
+    def place(slot, residue):
+        for phase in range(OWN_HEADS):
+            begin = pl.multiple_of((phase * SPAN + residue) * HEAD_DIM, 16)
+            for number in range(4):
+                if slot == EARLY:
+                    piece = early[phase][message_rows(number), :]
+                else:
+                    piece = late[slot][message_rows(4 * phase + number), :]
+                held[number, pl.ds(begin, HEAD_DIM), :] = piece
+
     for slot in range(slots):
-        source = table[slot, me]
-        residue = lax.rem(source + SPAN, SPAN)
-
-        def place(slot=slot, residue=residue):
-            for phase in range(OWN_HEADS):
-                begin = pl.multiple_of((phase * SPAN + residue) * HEAD_DIM, 16)
-                for number in range(4):
-                    if slot == EARLY:
-                        piece = early[phase][message_rows(number), :]
-                    else:
-                        piece = late[slot][message_rows(4 * phase + number), :]
-                    held[number, pl.ds(begin, HEAD_DIM), :] = piece
-
-        if is_closed(count):
-            place()
+        if closed:
+            place(slot, lax.rem(me, SPAN) ^ closed_step(slot))
         else:
-            pl.when((source >= 0) & (source == handler_of(start, residue, count)))(place)
+            _, start = image_of(me, lengths, images)
+            source = table[slot, me]
+            residue = lax.rem(source + SPAN, SPAN)
+            chosen = (source >= 0) & (source == handler_of(start, residue, count))
+            pl.when(chosen)(functools.partial(place, slot, residue))
+    copies = []
     for number, out in enumerate(outs):
-        out[...] = held[number].T
+        ready[number] = held[number].T
+        copies.append(pltpu.make_async_copy(ready.at[number], out, sems.at[number]))
+        copies[-1].start()
+    for copy in copies:
+        copy.wait()
 
 
 def bias_kernel(tiles, bias_out):
@@ -414,11 +449,17 @@
     )(*inputs)
     got = [trade(sends[:slots])]
     table_shape = jax.ShapeDtypeStruct((HALF, span), jnp.float32)
+    mask_rows = -(-slots * (slots + 1) // 8) * 8
     tables = pl.pallas_call(
-        functools.partial(tables_kernel, images, tokd),
-        out_shape=[table_shape] * 2 + [jax.ShapeDtypeStruct((model, LANES), jnp.float32)],
+        functools.partial(tables_kernel, images, count, tokd),
+        out_shape=[table_shape] * 2
+        + [
+            jax.ShapeDtypeStruct((mask_rows, tokd), jnp.float32),
+            jax.ShapeDtypeStruct((OWN_HEADS * HEAD_DIM, LANES), jnp.float32),
+        ],
         in_specs=[smem, smem, smem, vmem, vmem],
-        out_specs=[vmem] * 3,
+        out_specs=[vmem] * 4,
+        scratch_shapes=[pltpu.VMEM((model, LANES), jnp.float32)],
         compiler_params=params(16),
         cost_estimate=pl.CostEstimate(
             flops=span * LANES * 200, bytes_accessed=0, transcendentals=0
@@ -436,14 +477,14 @@
         sums_shape = jax.ShapeDtypeStruct(
             (devices, 4, LANES) if last else (8, LANES), jnp.float32
         )
-        first_carried = 5 + slots + 1
+        first_carried = 4 + slots + 1
         *results, total = pl.pallas_call(
             functools.partial(
-                attend_kernel, slots, count, images, tokd, phase, 1.0 / tokens_all**0.5
+                attend_kernel, slots, closed, tokd, phase, 1.0 / tokens_all**0.5
             ),
             out_shape=[message if slot == EARLY else joined for slot in range(slots)]
             + [sums_shape],
-            in_specs=[smem, smem] + [vmem] * (3 + slots + len(carried)),
+            in_specs=[vmem] * (4 + slots + len(carried)),
             out_specs=[vmem] * slots + [hbm if last else vmem],
             input_output_aliases={first_carried + at: slot for at, slot in enumerate(kept)}
             if carried
@@ -462,22 +503,27 @@
                 flops=12 * span * span * 256, bytes_accessed=0, transcendentals=0
             ),
             name="attend_head",
-        )(lengths, table, *tables, *got[phase], *carried)
+        )(*tables, *got[phase], *carried)
         results, total, early = lax.optimization_barrier((results, total, early))
         early.append(send_back(results[EARLY], EARLY))
         carried = [total] + [results[slot] for slot in kept]
     tiles = lax.all_to_all(total, ("dp", "tok"), 0, 0, tiled=True)
     late = [send_back(results[slot], slot) for slot in kept]
+    places = [] if closed else [lengths, jnp.asarray(targets)]
     outs = pl.pallas_call(
         functools.partial(unpack_kernel, slots, count, images),
         out_shape=[whole] * 4,
-        in_specs=[smem, smem] + [vmem] * (OWN_HEADS + len(late)),
-        out_specs=[vmem] * 4,
-        scratch_shapes=[pltpu.VMEM((4, model, tokd), jnp.bfloat16)],
+        in_specs=[smem] * len(places) + [vmem] * (OWN_HEADS + len(late)),
+        out_specs=[hbm] * 4,
+        scratch_shapes=[
+            pltpu.VMEM((4, model, tokd), jnp.bfloat16),
+            pltpu.VMEM((4, tokd, model), jnp.bfloat16),
+            pltpu.SemaphoreType.DMA((4,)),
+        ],
         compiler_params=params(16),
         cost_estimate=pl.CostEstimate(flops=UNPACK_FLOPS, bytes_accessed=0, transcendentals=0),
         name="unpack_heads",
-    )(lengths, jnp.asarray(targets), *early, *late)
+    )(*places, *early, *late)
     outs, tiles = lax.optimization_barrier((outs, tiles))
     bias_grad = pl.pallas_call(
         bias_kernel,

time: 46.3 us -> 45.1 us (0.974)
  Pallas kernels: 16 us -> 14.3 us
  waiting for transfers between devices: 9.44 us -> 10.5 us
  starting transfers between devices: 19.9 us -> 19.3 us
    pallas_call x3, Pallas kernels: 11.7 us -> 10.6 us  [the longest x2 9.36 us: on_device(): pl.pallas_call(functools.partial(attend_kernel, slots, closed, tokd, phas...]
    ppermute x4, waiting for transfers between devices: 3.51 us -> 4.17 us  [send_back(): lax.ppermute(result, 'tok', [(target, source) for source, target in pairs])]
    ppermute x4, starting transfers between devices: 4.76 us -> 4.2 us  [send_back(): lax.ppermute(result, 'tok', [(target, source) for source, target in pairs])]
    pallas_call x1, Pallas kernels: 1.85 us -> 1.32 us  [on_device(): pl.pallas_call(functools.partial(unpack_kernel, slots, count, images), ou...]
  transfers between devices with their start and end apart: 11 -> 11, of which waited for: 5 -> 5; matrix products, arithmetic and copies ran while one was open for 0% -> 0% of each run, Pallas kernels for 29% -> 27%
where the time goes in v9:
time: 45.1 us; the launch traced here: 44.9 us
  starting transfers between devices  19.3 us (43%)
  Pallas kernels  14.3 us (32%)
  waiting for transfers between devices  10.5 us (23%)
  between operations  0.74 us (2%)
    ppermute x6, starting transfers between devices, trade(): moved.append(lax.ppermute(one, 'tok', pairs))  9.75 us
    pallas_call x2, Pallas kernels, on_device(): pl.pallas_call(functools.partial(attend_kernel, slots, closed, tokd, phas...  9.36 us
    all_to_all x1, starting transfers between devices, on_device(): tiles = lax.all_to_all(total, ('dp', 'tok'), 0, 0, tiled=True)  5.37 us
    ppermute x4, starting transfers between devices, send_back(): lax.ppermute(result, 'tok', [(target, source) for source, target in pairs])  4.2 us
    ppermute x4, waiting for transfers between devices, send_back(): lax.ppermute(result, 'tok', [(target, source) for source, target in pairs])  4.17 us
    ppermute x6, waiting for transfers between devices, trade(): moved.append(lax.ppermute(one, 'tok', pairs))  3.98 us
    all_to_all x1, waiting for transfers between devices, on_device(): tiles = lax.all_to_all(total, ('dp', 'tok'), 0, 0, tiled=True)  2.37 us
    pallas_call x1, Pallas kernels, on_device(): pl.pallas_call(functools.partial(pack_kernel, closed), out_shape=[message...  1.68 us
  transfers between devices with their start and end apart: 11, of which 5 were waited for; matrix products, arithmetic and copies ran while one was open for 0% of the time, Pallas kernels for 27%

profile of v9, /device:TPU:0, one launch (start us, length us, event | category | flops | bytes accessed | tf_op | source)
XLA Modules:
  0.0 44.9 jit_solution(4694636334945585938)
XLA Ops:
  0.6 0.0 copy-start.2
  0.6 0.0 copy-start.3
  0.7 0.0 copy-start.4
  0.7 1.7 %pack_heads.1 = (bf16[320,256]{1,0:T(8,128)(2,1)S(1)}, bf16[320,256]{1,0:T(8,128)(2,1)S(1)}, bf16[320,256]{1,0:T(8,128)(2,1)S(1)}, bf16[320,256]{1,0:T(8,128)(2,...) custom-call(bf16[256,640]{1,0:T(8,128)(2,1)} %bitcast.8, ...), custom_call_target="tpu_custom_call" | custom-call | tf_op jit(solution)/shard_map/pack_heads/pallas_call | solution.py:437
  2.4 0.0 copy-start
  2.4 4.0 %collective-permute-start.3 = (bf16[320,256]{1,0:T(8,128)(2,1)S(1)}, bf16[320,256]{1,0:T(8,128)(2,1)S(1)}, u32[]{:S(2)}, u32[]{:S(2)}) collective-permute-start(bf16[320,256]{1,0:T(8,128)(2,1)S(1)} %get-tuple-element.67), channel_id=1, source_target_pairs={{0,3},{1,2},{2,1},{3,0},{4,7},{5,6},{6,5},{7,4},{8,11},{9,10},{10,... | collective-permute-start | bytes 491528 | tf_op jit(solution)/shard_map/ppermute | solution.py:67
  6.4 0.0 copy-start.1
  6.4 0.4 collective-permute-start.4
  6.8 0.2 collective-permute-start.5
  7.1 0.0 copy-done.2
  7.1 0.0 copy-done.3
  7.1 0.0 copy-done.4
  7.1 0.0 copy-done
  7.1 0.0 copy-done.1
  7.1 1.3 %rotary_tables.1 = (f32[40,1024]{1,0:T(8,128)S(1)}, f32[40,1024]{1,0:T(8,128)S(1)}, f32[24,256]{1,0:T(8,128)S(1)}, f32[160,128]{1,0:T(8,128)S(1)}) custom-call(s32[1,4]{1,0:T(1,128)S(1)} %copy-done.1, s32[1,4]{1,0:T(1,128)S(1)} %copy-done.2, s32[4,8]{1,0:T(4,128)S(1)} %copy-done.4, f32[40,128]{1,0:T(8,128)S(1)} %copy-done.3, bf16[3,640]{1,0:T(4,128)(2,1)S(1)} %copy-done), custom_call_target="tpu_custom_call" | custom-call | flops 26214400 | tf_op jit(solution)/shard_map/rotary_tables/pallas_call | solution.py:453
  8.4 2.9 %collective-permute-start = (bf16[320,256]{1,0:T(8,128)(2,1)S(1)}, bf16[320,256]{1,0:T(8,128)(2,1)S(1)}, u32[]{:S(2)}, u32[]{:S(2)}) collective-permute-start(bf16[320,256]{1,0:T(8,128)(2,1)S(1)} %get-tuple-element.63), channel_id=1, source_target_pairs={{0,3},{1,2},{2,1},{3,0},{4,7},{5,6},{6,5},{7,4},{8,11},{9,10},{10,... | collective-permute-start | bytes 491528 | tf_op jit(solution)/shard_map/ppermute | solution.py:67
  11.3 0.4 collective-permute-start.1
  11.7 0.0 collective-permute-done.3.refs_1_
  11.7 1.7 %collective-permute-start.2 = (bf16[320,256]{1,0:T(8,128)(2,1)S(1)}, bf16[320,256]{1,0:T(8,128)(2,1)S(1)}, u32[]{:S(2)}, u32[]{:S(2)}) collective-permute-start(bf16[320,256]{1,0:T(8,128)(2,1)S(1)} %get-tuple-element.65), channel_id=1, source_target_pairs={{0,1},{1,0},{2,3},{3,2},{4,5},{5,4},{6,7},{7,6},{8,9},{9,8},{10,11... | collective-permute-start | bytes 491528 | tf_op jit(solution)/shard_map/ppermute | solution.py:67
  13.4 2.0 %collective-permute-done.4.refs_2_ = bf16[320,256]{1,0:T(8,128)(2,1)S(1)} collective-permute-done((bf16[320,256]{1,0:T(8,128)(2,1)S(1)}, bf16[320,256]{1,0:T(8,128)(2,1)S(1)}, u32[]{:S(2)}, u32[]{:S(2)}) %collective-permute-start.4) | collective-permute-done | bytes 163872 | tf_op jit(solution)/shard_map/ppermute | solution.py:67
  15.5 1.9 %collective-permute-done.5.refs_3_ = bf16[320,256]{1,0:T(8,128)(2,1)S(1)} collective-permute-done((bf16[320,256]{1,0:T(8,128)(2,1)S(1)}, bf16[320,256]{1,0:T(8,128)(2,1)S(1)}, u32[]{:S(2)}, u32[]{:S(2)}) %collective-permute-start.5) | collective-permute-done | bytes 163872 | tf_op jit(solution)/shard_map/ppermute | solution.py:67
  17.4 4.4 %attend_head.2 = (bf16[640,256]{1,0:T(8,128)(2,1)S(1)}, bf16[320,256]{1,0:T(8,128)(2,1)S(1)}, bf16[640,256]{1,0:T(8,128)(2,1)S(1)}, bf16[640,256]{1,0:T(8,128)(2,1)S(1)}, f32[8,128]{1,0:T(8,128)S(1)}) custom-call(f32[40,1024]{1,0:T(8,128)S(1)} %get-tuple-element.58.cosv, f32[40,1024]{1,0:T(8,128)S(1)} %get-tuple-element.59.sinv, ...), custom_call_target="tpu_custom_call" | custom-call | flops 3221225472 | tf_op jit(solution)/shard_map/attend_head/pallas_call | solution.py:481
  21.8 0.7 %collective-permute-start.6 = (bf16[320,256]{1,0:T(8,128)(2,1)S(1)}, bf16[320,256]{1,0:T(8,128)(2,1)S(1)}, u32[]{:S(2)}, u32[]{:S(2)}) collective-permute-start(bf16[320,256]{1,0:T(8,128)(2,1)S(1)} %get-tuple-element.79), channel_id=1, source_target_pairs={{3,0},{2,1},{1,2},{0,3},{7,4},{6,5},{5,6},{4,7},{11,8},{10,9},{9,1... | collective-permute-start | bytes 491528 | tf_op jit(solution)/shard_map/ppermute | solution.py:75
  22.5 0.0 collective-permute-done.refs_1_
  22.5 0.0 collective-permute-done.1.refs_2_
  22.5 0.0 collective-permute-done.2.refs_3_
  22.5 5.0 %attend_head.3 = (bf16[640,256]{1,0:T(8,128)(2,1)S(1)}, bf16[320,256]{1,0:T(8,128)(2,1)S(1)}, bf16[640,256]{1,0:T(8,128)(2,1)S(1)}, bf16[640,256]{1,0:T(8,128)(2,1)S(1)}, f32[32,4,128]{2,1,0:T(4,128)}) custom-call(f32[40,1024]{1,0:T(8,128)S(1)} %get-tuple-element.58.cosv, ...), custom_call_target="tpu_custom_call", output_to_operand_aliasing={{0}: (9, {}), {2}: (10, {}), {3}: (11, {})} | custom-call | flops 3221225472 | tf_op jit(solution)/shard_map/attend_head/pallas_call | solution.py:481
  27.5 0.6 %collective-permute-done.6.refs_0_ = bf16[320,256]{1,0:T(8,128)(2,1)S(1)} collective-permute-done((bf16[320,256]{1,0:T(8,128)(2,1)S(1)}, bf16[320,256]{1,0:T(8,128)(2,1)S(1)}, u32[]{:S(2)}, u32[]{:S(2)}) %collective-permute-start.6) | collective-permute-done | bytes 163872 | tf_op jit(solution)/shard_map/ppermute | solution.py:75
  28.1 1.7 %collective-permute-start.8 = (bf16[640,256]{1,0:T(8,128)(2,1)S(1)}, bf16[640,256]{1,0:T(8,128)(2,1)S(1)}, u32[]{:S(2)}, u32[]{:S(2)}) collective-permute-start(bf16[640,256]{1,0:T(8,128)(2,1)S(1)} %get-tuple-element.83), channel_id=1, source_target_pairs={{2,0},{3,1},{0,2},{1,3},{6,4},{7,5},{4,6},{5,7},{10,8},{11,9},{8,1... | collective-permute-start | bytes 983048 | tf_op jit(solution)/shard_map/ppermute | solution.py:75
  29.8 0.6 %collective-permute-start.9 = (bf16[640,256]{1,0:T(8,128)(2,1)S(1)}, bf16[640,256]{1,0:T(8,128)(2,1)S(1)}, u32[]{:S(2)}, u32[]{:S(2)}) collective-permute-start(bf16[640,256]{1,0:T(8,128)(2,1)S(1)} %get-tuple-element.84), channel_id=1, source_target_pairs={{1,0},{0,1},{3,2},{2,3},{5,4},{4,5},{7,6},{6,7},{9,8},{8,9},{11,10... | collective-permute-start | bytes 983048 | tf_op jit(solution)/shard_map/ppermute | solution.py:75
  30.4 1.2 %collective-permute-start.7 = (bf16[320,256]{1,0:T(8,128)(2,1)S(1)}, bf16[320,256]{1,0:T(8,128)(2,1)S(1)}, u32[]{:S(2)}, u32[]{:S(2)}) collective-permute-start(bf16[320,256]{1,0:T(8,128)(2,1)S(1)} %get-tuple-element.81), channel_id=1, source_target_pairs={{3,0},{2,1},{1,2},{0,3},{7,4},{6,5},{5,6},{4,7},{11,8},{10,9},{9,1... | collective-permute-start | bytes 491528 | tf_op jit(solution)/shard_map/ppermute | solution.py:75
  31.6 5.4 %all-to-all-start = ((f32[32,4,128]{2,1,0:T(4,128)}), f32[32,4,128]{2,1,0:T(4,128)S(1)}, u32[]{:S(2)}, u32[]{:S(2)}) async-start(f32[32,4,128]{2,1,0:T(4,128)} %get-tuple-element.89), calls=%async_computation | async-start | bytes 131072 | tf_op jit(solution)/shard_map/all_to_all | solution.py:510
  36.9 3.5 %collective-permute-done.7.refs_1_ = bf16[320,256]{1,0:T(8,128)(2,1)S(1)} collective-permute-done((bf16[320,256]{1,0:T(8,128)(2,1)S(1)}, bf16[320,256]{1,0:T(8,128)(2,1)S(1)}, u32[]{:S(2)}, u32[]{:S(2)}) %collective-permute-start.7) | collective-permute-done | bytes 163872 | tf_op jit(solution)/shard_map/ppermute | solution.py:75
  40.5 0.0 collective-permute-done.8.refs_3_
  40.5 0.0 collective-permute-done.9.refs_4_
  40.5 1.3 %unpack_heads.1 = (bf16[256,640]{1,0:T(8,128)(2,1)}, bf16[256,640]{1,0:T(8,128)(2,1)}, bf16[256,640]{1,0:T(8,128)(2,1)}, bf16[256,640]{1,0:T(8,128)(2,1)}) custom-call(bf16[320,256]{1,0:T(8,128)(2,1)S(1)} %collective-permute-done.6.refs_0_, bf16[320,256]{1,0:T(8,128)(2,1)S(1)} %collective-permute-done.7.refs_1_, ...), custom_call_target="tpu_custom_call" | custom-call | flops 20000000000 | tf_op jit(solution)/shard_map/unpack_heads/pallas_call | solution.py:513
  41.8 2.4 %all-to-all-done.tiles = f32[32,4,128]{2,1,0:T(4,128)S(1)} async-done(((f32[32,4,128]{2,1,0:T(4,128)}), f32[32,4,128]{2,1,0:T(4,128)S(1)}, u32[]{:S(2)}, u32[]{:S(2)}) %all-to-all-start) | async-done | bytes 65568 | tf_op jit(solution)/shard_map/all_to_all | solution.py:510
  44.2 0.7 %bias_sums.1 = f32[3,640]{1,0:T(4,128)} custom-call(f32[32,4,128]{2,1,0:T(4,128)S(1)} %all-to-all-done.tiles), custom_call_target="tpu_custom_call" | custom-call | tf_op jit(solution)/shard_map/bias_sums/pallas_call | solution.py:528
Async XLA Ops:
  0.6 6.4 %copy-start.2 = (s32[1,4]{1,0:T(1,128)S(1)}, s32[1,4]{1,0:T(1,128)}, u32[]{:S(2)}) copy-start(s32[1,4]{1,0:T(1,128)} %widths.1) | copy-start | bytes 52
  0.6 6.4 %copy-start.3 = (f32[40,128]{1,0:T(8,128)S(1)}, f32[40,128]{1,0:T(8,128)}, u32[]{:S(2)}) copy-start(f32[40,128]{1,0:T(8,128)} %constant.5.clone.inverse) | copy-start | bytes 61444
  0.7 6.4 %copy-start.4 = (s32[4,8]{1,0:T(4,128)S(1)}, s32[4,8]{1,0:T(4,128)}, u32[]{:S(2)}) copy-start(s32[4,8]{1,0:T(4,128)} %constant.4.clone.table) | copy-start | bytes 388
  2.4 4.7 %copy-start = (bf16[3,640]{1,0:T(4,128)(2,1)S(1)}, bf16[3,640]{1,0:T(4,128)(2,1)}, u32[]{:S(2)}) copy-start(bf16[3,640]{1,0:T(4,128)(2,1)} %bias.1) | copy-start | bytes 11524
  2.4 9.3 %collective-permute-start.3 = (bf16[320,256]{1,0:T(8,128)(2,1)S(1)}, bf16[320,256]{1,0:T(8,128)(2,1)S(1)}, u32[]{:S(2)}, u32[]{:S(2)}) collective-permute-start(bf16[320,256]{1,0:T(8,128)(2,1)S(1)} %get-tuple-element.67), channel_id=1, source_target_pairs={{0,3},{1,2},{2,1},{3,0},{4,7},{5,6},{6,5},{7,4},{8,11},{9,10},{10,... | collective-permute-start | bytes 491528 | tf_op jit(solution)/shard_map/ppermute | solution.py:67
  6.4 0.7 %copy-start.1 = (s32[1,4]{1,0:T(1,128)S(1)}, s32[1,4]{1,0:T(1,128)}, u32[]{:S(2)}) copy-start(s32[1,4]{1,0:T(1,128)} %lengths.1) | copy-start | bytes 52
  6.4 9.0 %collective-permute-start.4 = (bf16[320,256]{1,0:T(8,128)(2,1)S(1)}, bf16[320,256]{1,0:T(8,128)(2,1)S(1)}, u32[]{:S(2)}, u32[]{:S(2)}) collective-permute-start(bf16[320,256]{1,0:T(8,128)(2,1)S(1)} %get-tuple-element.68), channel_id=1, source_target_pairs={{0,2},{1,3},{2,0},{3,1},{4,6},{5,7},{6,4},{7,5},{8,10},{9,11},{10,... | collective-permute-start | bytes 491528 | tf_op jit(solution)/shard_map/ppermute | solution.py:67
  6.8 10.5 %collective-permute-start.5 = (bf16[320,256]{1,0:T(8,128)(2,1)S(1)}, bf16[320,256]{1,0:T(8,128)(2,1)S(1)}, u32[]{:S(2)}, u32[]{:S(2)}) collective-permute-start(bf16[320,256]{1,0:T(8,128)(2,1)S(1)} %get-tuple-element.69), channel_id=1, source_target_pairs={{0,1},{1,0},{2,3},{3,2},{4,5},{5,4},{6,7},{7,6},{8,9},{9,8},{10,11... | collective-permute-start | bytes 491528 | tf_op jit(solution)/shard_map/ppermute | solution.py:67
  8.4 14.1 %collective-permute-start = (bf16[320,256]{1,0:T(8,128)(2,1)S(1)}, bf16[320,256]{1,0:T(8,128)(2,1)S(1)}, u32[]{:S(2)}, u32[]{:S(2)}) collective-permute-start(bf16[320,256]{1,0:T(8,128)(2,1)S(1)} %get-tuple-element.63), channel_id=1, source_target_pairs={{0,3},{1,2},{2,1},{3,0},{4,7},{5,6},{6,5},{7,4},{8,11},{9,10},{10,... | collective-permute-start | bytes 491528 | tf_op jit(solution)/shard_map/ppermute | solution.py:67
  11.3 11.2 %collective-permute-start.1 = (bf16[320,256]{1,0:T(8,128)(2,1)S(1)}, bf16[320,256]{1,0:T(8,128)(2,1)S(1)}, u32[]{:S(2)}, u32[]{:S(2)}) collective-permute-start(bf16[320,256]{1,0:T(8,128)(2,1)S(1)} %get-tuple-element.64), channel_id=1, source_target_pairs={{0,2},{1,3},{2,0},{3,1},{4,6},{5,7},{6,4},{7,5},{8,10},{9,11},{10,... | collective-permute-start | bytes 491528 | tf_op jit(solution)/shard_map/ppermute | solution.py:67
  11.7 10.8 %collective-permute-start.2 = (bf16[320,256]{1,0:T(8,128)(2,1)S(1)}, bf16[320,256]{1,0:T(8,128)(2,1)S(1)}, u32[]{:S(2)}, u32[]{:S(2)}) collective-permute-start(bf16[320,256]{1,0:T(8,128)(2,1)S(1)} %get-tuple-element.65), channel_id=1, source_target_pairs={{0,1},{1,0},{2,3},{3,2},{4,5},{5,4},{6,7},{7,6},{8,9},{9,8},{10,11... | collective-permute-start | bytes 491528 | tf_op jit(solution)/shard_map/ppermute | solution.py:67
  21.8 6.3 %collective-permute-start.6 = (bf16[320,256]{1,0:T(8,128)(2,1)S(1)}, bf16[320,256]{1,0:T(8,128)(2,1)S(1)}, u32[]{:S(2)}, u32[]{:S(2)}) collective-permute-start(bf16[320,256]{1,0:T(8,128)(2,1)S(1)} %get-tuple-element.79), channel_id=1, source_target_pairs={{3,0},{2,1},{1,2},{0,3},{7,4},{6,5},{5,6},{4,7},{11,8},{10,9},{9,1... | collective-permute-start | bytes 491528 | tf_op jit(solution)/shard_map/ppermute | solution.py:75
  28.1 12.4 %collective-permute-start.8 = (bf16[640,256]{1,0:T(8,128)(2,1)S(1)}, bf16[640,256]{1,0:T(8,128)(2,1)S(1)}, u32[]{:S(2)}, u32[]{:S(2)}) collective-permute-start(bf16[640,256]{1,0:T(8,128)(2,1)S(1)} %get-tuple-element.83), channel_id=1, source_target_pairs={{2,0},{3,1},{0,2},{1,3},{6,4},{7,5},{4,6},{5,7},{10,8},{11,9},{8,1... | collective-permute-start | bytes 983048 | tf_op jit(solution)/shard_map/ppermute | solution.py:75
  29.8 10.7 %collective-permute-start.9 = (bf16[640,256]{1,0:T(8,128)(2,1)S(1)}, bf16[640,256]{1,0:T(8,128)(2,1)S(1)}, u32[]{:S(2)}, u32[]{:S(2)}) collective-permute-start(bf16[640,256]{1,0:T(8,128)(2,1)S(1)} %get-tuple-element.84), channel_id=1, source_target_pairs={{1,0},{0,1},{3,2},{2,3},{5,4},{4,5},{7,6},{6,7},{9,8},{8,9},{11,10... | collective-permute-start | bytes 983048 | tf_op jit(solution)/shard_map/ppermute | solution.py:75
  30.4 10.1 %collective-permute-start.7 = (bf16[320,256]{1,0:T(8,128)(2,1)S(1)}, bf16[320,256]{1,0:T(8,128)(2,1)S(1)}, u32[]{:S(2)}, u32[]{:S(2)}) collective-permute-start(bf16[320,256]{1,0:T(8,128)(2,1)S(1)} %get-tuple-element.81), channel_id=1, source_target_pairs={{3,0},{2,1},{1,2},{0,3},{7,4},{6,5},{5,6},{4,7},{11,8},{10,9},{9,1... | collective-permute-start | bytes 491528 | tf_op jit(solution)/shard_map/ppermute | solution.py:75
  31.6 12.7 %all-to-all-start = ((f32[32,4,128]{2,1,0:T(4,128)}), f32[32,4,128]{2,1,0:T(4,128)S(1)}, u32[]{:S(2)}, u32[]{:S(2)}) async-start(f32[32,4,128]{2,1,0:T(4,128)} %get-tuple-element.89), calls=%async_computation | async-start | bytes 131072 | tf_op jit(solution)/shard_map/all_to_all | solution.py:510

commit v10 on v9

--- a/solution.py
+++ b/solution.py
@@ -17,9 +17,9 @@
 LOG2E = 1.4426950408889634
 NEG = -1e30
 LANES = 128
+USED = HEAD_DIM + 16
 HALF = HEAD_DIM // 2
 PACK_KIB = 52 * 1024 + 600
-UNPACK_FLOPS = 20_000_000_000
 
 rope_base = 10000.0
 
@@ -176,9 +176,13 @@
 
 def attend_kernel(slots, closed, tokd, head, factor, cosv, sinv, masks, bias, *refs):
     msgs, refs = refs[:slots], refs[slots:]
+    earlier = ()
     if head > 0:
-        before, refs = refs[0], refs[slots:]
+        before, earlier, refs = refs[0], refs[1:slots], refs[slots:]
     outs, sums = refs[:slots], refs[slots]
+    for result, out in zip(earlier, [out for slot, out in enumerate(outs) if slot != EARLY]):
+        done = head * 4 * HEAD_DIM
+        out[:done, :] = result[:done, :]
     qt_all, kt_all, vt_all, gt_all, k_all, v_all, s_buf, e_buf, d_buf = refs[slots + 1 : slots + 10]
     own_bias = bias[head * HEAD_DIM : (head + 1) * HEAD_DIM, :]
     rest_row = lax.broadcasted_iota(jnp.int32, (LANES - HEAD_DIM, tokd), 0)
@@ -236,7 +240,7 @@
 
     def output(slot):
         mixed = jnp.dot(
-            vt_all[...], e_buf[:, block_of(slot)], preferred_element_type=jnp.float32
+            vt_all[:USED, :], e_buf[:, block_of(slot)], preferred_element_type=jnp.float32
         )
         inv = 1.0 / mixed[HEAD_DIM : HEAD_DIM + 1]
         out_b = (mixed[:HEAD_DIM] * inv).astype(jnp.bfloat16)
@@ -353,7 +357,7 @@
     if not closed:
         lengths, table, *refs = refs
     msgs, refs = refs[: slots + OWN_HEADS - 1], refs[slots + OWN_HEADS - 1 :]
-    outs, held, ready, sems = refs[:4], refs[4], refs[5], refs[6]
+    tiles, *outs, bias_out, held, ready, sems = refs
     early, late = msgs[:OWN_HEADS], list(msgs[OWN_HEADS:])
     late.insert(EARLY, None)
     me = lax.axis_index("tok")
@@ -382,11 +386,12 @@
         ready[number] = held[number].T
         copies.append(pltpu.make_async_copy(ready.at[number], out, sems.at[number]))
         copies[-1].start()
+    sum_tiles(tiles, bias_out)
     for copy in copies:
         copy.wait()
 
 
-def bias_kernel(tiles, bias_out):
+def sum_tiles(tiles, bias_out):
     def add(group, totals):
         return tuple(
             total + tiles[group * SPAN + residue] for residue, total in enumerate(totals)
@@ -477,7 +482,6 @@
         sums_shape = jax.ShapeDtypeStruct(
             (devices, 4, LANES) if last else (8, LANES), jnp.float32
         )
-        first_carried = 4 + slots + 1
         *results, total = pl.pallas_call(
             functools.partial(
                 attend_kernel, slots, closed, tokd, phase, 1.0 / tokens_all**0.5
@@ -486,9 +490,6 @@
             + [sums_shape],
             in_specs=[vmem] * (4 + slots + len(carried)),
             out_specs=[vmem] * slots + [hbm if last else vmem],
-            input_output_aliases={first_carried + at: slot for at, slot in enumerate(kept)}
-            if carried
-            else {},
             scratch_shapes=[pltpu.VMEM((LANES, span), jnp.bfloat16)] * 4
             + [pltpu.VMEM((span, LANES), jnp.bfloat16)] * 2
             + [pltpu.VMEM((2, span, tokd), jnp.float32)]
@@ -510,29 +511,19 @@
     tiles = lax.all_to_all(total, ("dp", "tok"), 0, 0, tiled=True)
     late = [send_back(results[slot], slot) for slot in kept]
     places = [] if closed else [lengths, jnp.asarray(targets)]
-    outs = pl.pallas_call(
+    *outs, bias_grad = pl.pallas_call(
         functools.partial(unpack_kernel, slots, count, images),
-        out_shape=[whole] * 4,
-        in_specs=[smem] * len(places) + [vmem] * (OWN_HEADS + len(late)),
-        out_specs=[hbm] * 4,
+        out_shape=[whole] * 4 + [jax.ShapeDtypeStruct((3, model), jnp.float32)],
+        in_specs=[smem] * len(places) + [vmem] * (OWN_HEADS + len(late) + 1),
+        out_specs=[hbm] * 4 + [vmem],
         scratch_shapes=[
             pltpu.VMEM((4, model, tokd), jnp.bfloat16),
             pltpu.VMEM((4, tokd, model), jnp.bfloat16),
             pltpu.SemaphoreType.DMA((4,)),
         ],
         compiler_params=params(16),
-        cost_estimate=pl.CostEstimate(flops=UNPACK_FLOPS, bytes_accessed=0, transcendentals=0),
         name="unpack_heads",
-    )(*places, *early, *late)
-    outs, tiles = lax.optimization_barrier((outs, tiles))
-    bias_grad = pl.pallas_call(
-        bias_kernel,
-        out_shape=jax.ShapeDtypeStruct((3, model), jnp.float32),
-        in_specs=[vmem],
-        out_specs=vmem,
-        compiler_params=params(16),
-        name="bias_sums",
-    )(tiles)
+    )(*places, *early, *late, tiles)
     return tuple(out[None] for out in outs) + (bias_grad,)
 
 

time: 45.1 us -> 46.3 us (1.027)
  blocking collectives: 0 us -> 12.6 us
  waiting for transfers between devices: 10.5 us -> 4.5 us
  starting transfers between devices: 19.3 us -> 14 us
    all_to_all x0 -> x1, blocking collectives: none -> 12.6 us  [on_device(): tiles = lax.all_to_all(total, ('dp', 'tok'), 0, 0, tiled=True)]
    all_to_all x1 -> x0, starting transfers between devices: 5.37 us -> none  [on_device(): tiles = lax.all_to_all(total, ('dp', 'tok'), 0, 0, tiled=True)]
    ppermute x4, waiting for transfers between devices: 4.17 us -> 0.52 us  [send_back(): lax.ppermute(result, 'tok', [(target, source) for source, target in pairs])]
    all_to_all x1 -> x0, waiting for transfers between devices: 2.37 us -> none  [on_device(): tiles = lax.all_to_all(total, ('dp', 'tok'), 0, 0, tiled=True)]
    pallas_call x1 -> x0, Pallas kernels: 0.71 us -> none  [on_device(): pl.pallas_call(bias_kernel, out_shape=jax.ShapeDtypeStruct((3, model), jn...]
    pallas_call x1, Pallas kernels: 1.32 us -> 1.92 us  [on_device(): pl.pallas_call(functools.partial(unpack_kernel, slots, count, images), ou...]
  transfers between devices with their start and end apart: 11 -> 10, of which waited for: 5 -> 3; matrix products, arithmetic and copies ran while one was open for 0% -> 0% of each run, Pallas kernels for 27% -> 23%
where the time goes in v10:
time: 46.3 us; the launch traced here: 46.1 us
  Pallas kernels  14.3 us (31%)
  starting transfers between devices  14 us (30%)
  blocking collectives  12.6 us (27%)
  waiting for transfers between devices  4.5 us (10%)
  between operations  0.72 us (2%)
    all_to_all x1, blocking collectives, on_device(): tiles = lax.all_to_all(total, ('dp', 'tok'), 0, 0, tiled=True)  12.6 us
    ppermute x6, starting transfers between devices, trade(): moved.append(lax.ppermute(one, 'tok', pairs))  9.75 us
    pallas_call x2, Pallas kernels, on_device(): pl.pallas_call(functools.partial(attend_kernel, slots, closed, tokd, phas...  9.44 us
    ppermute x4, starting transfers between devices, send_back(): lax.ppermute(result, 'tok', [(target, source) for source, target in pairs])  4.28 us
    ppermute x6, waiting for transfers between devices, trade(): moved.append(lax.ppermute(one, 'tok', pairs))  3.98 us
    pallas_call x1, Pallas kernels, on_device(): pl.pallas_call(functools.partial(unpack_kernel, slots, count, images), ou...  1.92 us
    pallas_call x1, Pallas kernels, on_device(): pl.pallas_call(functools.partial(pack_kernel, closed), out_shape=[message...  1.68 us
    pallas_call x1, Pallas kernels, on_device(): pl.pallas_call(functools.partial(tables_kernel, images, count, tokd), out...  1.25 us
  transfers between devices with their start and end apart: 10, of which 3 were waited for; matrix products, arithmetic and copies ran while one was open for 0% of the time, Pallas kernels for 23%

profile of v10, /device:TPU:0, one launch (start us, length us, event | category | flops | bytes accessed | tf_op | source)
XLA Modules:
  0.0 46.1 jit_solution(3992718003391796213)
XLA Ops:
  0.6 0.0 copy-start.2
  0.6 0.0 copy-start.3
  0.7 0.0 copy-start.4
  0.7 1.7 %pack_heads.1 = (bf16[320,256]{1,0:T(8,128)(2,1)S(1)}, bf16[320,256]{1,0:T(8,128)(2,1)S(1)}, bf16[320,256]{1,0:T(8,128)(2,1)S(1)}, bf16[320,256]{1,0:T(8,128)(2,...) custom-call(bf16[256,640]{1,0:T(8,128)(2,1)} %bitcast.8, ...), custom_call_target="tpu_custom_call" | custom-call | tf_op jit(solution)/shard_map/pack_heads/pallas_call | solution.py:442
  2.4 0.0 copy-start
  2.4 4.0 %collective-permute-start.3 = (bf16[320,256]{1,0:T(8,128)(2,1)S(1)}, bf16[320,256]{1,0:T(8,128)(2,1)S(1)}, u32[]{:S(2)}, u32[]{:S(2)}) collective-permute-start(bf16[320,256]{1,0:T(8,128)(2,1)S(1)} %get-tuple-element.63), channel_id=1, source_target_pairs={{0,3},{1,2},{2,1},{3,0},{4,7},{5,6},{6,5},{7,4},{8,11},{9,10},{10,... | collective-permute-start | bytes 491528 | tf_op jit(solution)/shard_map/ppermute | solution.py:67
  6.4 0.0 copy-start.1
  6.4 0.4 collective-permute-start.4
  6.8 0.2 collective-permute-start.5
  7.1 0.0 copy-done.2
  7.1 0.0 copy-done.3
  7.1 0.0 copy-done.4
  7.1 0.0 copy-done
  7.1 0.0 copy-done.1
  7.1 1.3 %rotary_tables.1 = (f32[40,1024]{1,0:T(8,128)S(1)}, f32[40,1024]{1,0:T(8,128)S(1)}, f32[24,256]{1,0:T(8,128)S(1)}, f32[160,128]{1,0:T(8,128)S(1)}) custom-call(s32[1,4]{1,0:T(1,128)S(1)} %copy-done.1, s32[1,4]{1,0:T(1,128)S(1)} %copy-done.2, s32[4,8]{1,0:T(4,128)S(1)} %copy-done.4, f32[40,128]{1,0:T(8,128)S(1)} %copy-done.3, bf16[3,640]{1,0:T(4,128)(2,1)S(1)} %copy-done), custom_call_target="tpu_custom_call" | custom-call | flops 26214400 | tf_op jit(solution)/shard_map/rotary_tables/pallas_call | solution.py:458
  8.4 2.9 %collective-permute-start = (bf16[320,256]{1,0:T(8,128)(2,1)S(1)}, bf16[320,256]{1,0:T(8,128)(2,1)S(1)}, u32[]{:S(2)}, u32[]{:S(2)}) collective-permute-start(bf16[320,256]{1,0:T(8,128)(2,1)S(1)} %get-tuple-element.59), channel_id=1, source_target_pairs={{0,3},{1,2},{2,1},{3,0},{4,7},{5,6},{6,5},{7,4},{8,11},{9,10},{10,... | collective-permute-start | bytes 491528 | tf_op jit(solution)/shard_map/ppermute | solution.py:67
  11.3 0.4 collective-permute-start.1
  11.7 0.0 collective-permute-done.3.refs_1_
  11.7 1.7 %collective-permute-start.2 = (bf16[320,256]{1,0:T(8,128)(2,1)S(1)}, bf16[320,256]{1,0:T(8,128)(2,1)S(1)}, u32[]{:S(2)}, u32[]{:S(2)}) collective-permute-start(bf16[320,256]{1,0:T(8,128)(2,1)S(1)} %get-tuple-element.61), channel_id=1, source_target_pairs={{0,1},{1,0},{2,3},{3,2},{4,5},{5,4},{6,7},{7,6},{8,9},{9,8},{10,11... | collective-permute-start | bytes 491528 | tf_op jit(solution)/shard_map/ppermute | solution.py:67
  13.4 2.0 %collective-permute-done.4.refs_2_ = bf16[320,256]{1,0:T(8,128)(2,1)S(1)} collective-permute-done((bf16[320,256]{1,0:T(8,128)(2,1)S(1)}, bf16[320,256]{1,0:T(8,128)(2,1)S(1)}, u32[]{:S(2)}, u32[]{:S(2)}) %collective-permute-start.4) | collective-permute-done | bytes 163872 | tf_op jit(solution)/shard_map/ppermute | solution.py:67
  15.5 1.9 %collective-permute-done.5.refs_3_ = bf16[320,256]{1,0:T(8,128)(2,1)S(1)} collective-permute-done((bf16[320,256]{1,0:T(8,128)(2,1)S(1)}, bf16[320,256]{1,0:T(8,128)(2,1)S(1)}, u32[]{:S(2)}, u32[]{:S(2)}) %collective-permute-start.5) | collective-permute-done | bytes 163872 | tf_op jit(solution)/shard_map/ppermute | solution.py:67
  17.4 4.4 %attend_head.2 = (bf16[640,256]{1,0:T(8,128)(2,1)S(1)}, bf16[320,256]{1,0:T(8,128)(2,1)S(1)}, bf16[640,256]{1,0:T(8,128)(2,1)S(1)}, bf16[640,256]{1,0:T(8,128)(2,1)S(1)}, f32[8,128]{1,0:T(8,128)S(1)}) custom-call(f32[40,1024]{1,0:T(8,128)S(1)} %get-tuple-element.54.cosv, f32[40,1024]{1,0:T(8,128)S(1)} %get-tuple-element.55.sinv, ...), custom_call_target="tpu_custom_call" | custom-call | flops 3221225472 | tf_op jit(solution)/shard_map/attend_head/pallas_call | solution.py:485
  21.8 0.7 %collective-permute-start.6 = (bf16[320,256]{1,0:T(8,128)(2,1)S(1)}, bf16[320,256]{1,0:T(8,128)(2,1)S(1)}, u32[]{:S(2)}, u32[]{:S(2)}) collective-permute-start(bf16[320,256]{1,0:T(8,128)(2,1)S(1)} %get-tuple-element.75), channel_id=1, source_target_pairs={{3,0},{2,1},{1,2},{0,3},{7,4},{6,5},{5,6},{4,7},{11,8},{10,9},{9,1... | collective-permute-start | bytes 491528 | tf_op jit(solution)/shard_map/ppermute | solution.py:75
  22.5 0.0 collective-permute-done.refs_1_
  22.5 0.0 collective-permute-done.1.refs_2_
  22.5 0.0 collective-permute-done.2.refs_3_
  22.5 5.0 %attend_head.3 = (bf16[640,256]{1,0:T(8,128)(2,1)S(1)}, bf16[320,256]{1,0:T(8,128)(2,1)S(1)}, bf16[640,256]{1,0:T(8,128)(2,1)S(1)}, bf16[640,256]{1,0:T(8,128)(2,1)S(1)}, f32[32,4,128]{2,1,0:T(4,128)S(1)}) custom-call(f32[40,1024]{1,0:T(8,128)S(1)} %get-tuple-element.54.cosv, f32[40,1024]{1,0:T(8,128)S(1)} %get-tuple-element.55.sinv, ...), custom_call_target="tpu_custom_call" | custom-call | flops 3221225472 | tf_op jit(solution)/shard_map/attend_head/pallas_call | solution.py:485
  27.6 0.5 %collective-permute-done.6.refs_0_ = bf16[320,256]{1,0:T(8,128)(2,1)S(1)} collective-permute-done((bf16[320,256]{1,0:T(8,128)(2,1)S(1)}, bf16[320,256]{1,0:T(8,128)(2,1)S(1)}, u32[]{:S(2)}, u32[]{:S(2)}) %collective-permute-start.6) | collective-permute-done | bytes 163872 | tf_op jit(solution)/shard_map/ppermute | solution.py:75
  28.1 1.7 %collective-permute-start.8 = (bf16[640,256]{1,0:T(8,128)(2,1)S(1)}, bf16[640,256]{1,0:T(8,128)(2,1)S(1)}, u32[]{:S(2)}, u32[]{:S(2)}) collective-permute-start(bf16[640,256]{1,0:T(8,128)(2,1)S(1)} %get-tuple-element.79), channel_id=1, source_target_pairs={{2,0},{3,1},{0,2},{1,3},{6,4},{7,5},{4,6},{5,7},{10,8},{11,9},{8,1... | collective-permute-start | bytes 983048 | tf_op jit(solution)/shard_map/ppermute | solution.py:75
  29.8 0.7 %collective-permute-start.9 = (bf16[640,256]{1,0:T(8,128)(2,1)S(1)}, bf16[640,256]{1,0:T(8,128)(2,1)S(1)}, u32[]{:S(2)}, u32[]{:S(2)}) collective-permute-start(bf16[640,256]{1,0:T(8,128)(2,1)S(1)} %get-tuple-element.80), channel_id=1, source_target_pairs={{1,0},{0,1},{3,2},{2,3},{5,4},{4,5},{7,6},{6,7},{9,8},{8,9},{11,10... | collective-permute-start | bytes 983048 | tf_op jit(solution)/shard_map/ppermute | solution.py:75
  30.5 1.2 %collective-permute-start.7 = (bf16[320,256]{1,0:T(8,128)(2,1)S(1)}, bf16[320,256]{1,0:T(8,128)(2,1)S(1)}, u32[]{:S(2)}, u32[]{:S(2)}) collective-permute-start(bf16[320,256]{1,0:T(8,128)(2,1)S(1)} %get-tuple-element.77), channel_id=1, source_target_pairs={{3,0},{2,1},{1,2},{0,3},{7,4},{6,5},{5,6},{4,7},{11,8},{10,9},{9,1... | collective-permute-start | bytes 491528 | tf_op jit(solution)/shard_map/ppermute | solution.py:75
  31.6 12.6 %all_to_all.5.refs_5_ = f32[32,4,128]{2,1,0:T(4,128)S(1)} all-to-all(f32[32,4,128]{2,1,0:T(4,128)S(1)} %get-tuple-element.81), channel_id=1, replica_groups=mesh['dp'=4,'tok'=8] {'dp','tok'}, dimensions={0} | all-to-all | bytes 131072 | tf_op jit(solution)/shard_map/all_to_all | solution.py:511
  44.2 0.0 collective-permute-done.7.refs_1_
  44.2 0.0 collective-permute-done.8.refs_3_
  44.2 0.0 collective-permute-done.9.refs_4_
  44.2 1.9 %unpack_heads.1 = (bf16[256,640]{1,0:T(8,128)(2,1)}, bf16[256,640]{1,0:T(8,128)(2,1)}, bf16[256,640]{1,0:T(8,128)(2,1)}, bf16[256,640]{1,0:T(8,128)(2,1)}, f32[3,640]{1,0:T(4,128)}) custom-call(bf16[320,256]{1,0:T(8,128)(2,1)S(1)} %collective-permute-done.6.refs_0_, bf16[320,256]{1,0:T(8,128)(2,1)S(1)} %collective-permute-done.7.refs_1_, ...), custom_call_target="tpu_custom_call" | custom-call | tf_op jit(solution)/shard_map/unpack_heads/pallas_call | solution.py:514
Async XLA Ops:
  0.6 6.4 %copy-start.2 = (s32[1,4]{1,0:T(1,128)S(1)}, s32[1,4]{1,0:T(1,128)}, u32[]{:S(2)}) copy-start(s32[1,4]{1,0:T(1,128)} %widths.1) | copy-start | bytes 52
  0.6 6.4 %copy-start.3 = (f32[40,128]{1,0:T(8,128)S(1)}, f32[40,128]{1,0:T(8,128)}, u32[]{:S(2)}) copy-start(f32[40,128]{1,0:T(8,128)} %constant.5.clone.inverse) | copy-start | bytes 61444
  0.7 6.4 %copy-start.4 = (s32[4,8]{1,0:T(4,128)S(1)}, s32[4,8]{1,0:T(4,128)}, u32[]{:S(2)}) copy-start(s32[4,8]{1,0:T(4,128)} %constant.4.clone.table) | copy-start | bytes 388
  2.4 4.7 %copy-start = (bf16[3,640]{1,0:T(4,128)(2,1)S(1)}, bf16[3,640]{1,0:T(4,128)(2,1)}, u32[]{:S(2)}) copy-start(bf16[3,640]{1,0:T(4,128)(2,1)} %bias.1) | copy-start | bytes 11524
  2.4 9.3 %collective-permute-start.3 = (bf16[320,256]{1,0:T(8,128)(2,1)S(1)}, bf16[320,256]{1,0:T(8,128)(2,1)S(1)}, u32[]{:S(2)}, u32[]{:S(2)}) collective-permute-start(bf16[320,256]{1,0:T(8,128)(2,1)S(1)} %get-tuple-element.63), channel_id=1, source_target_pairs={{0,3},{1,2},{2,1},{3,0},{4,7},{5,6},{6,5},{7,4},{8,11},{9,10},{10,... | collective-permute-start | bytes 491528 | tf_op jit(solution)/shard_map/ppermute | solution.py:67
  6.4 0.7 %copy-start.1 = (s32[1,4]{1,0:T(1,128)S(1)}, s32[1,4]{1,0:T(1,128)}, u32[]{:S(2)}) copy-start(s32[1,4]{1,0:T(1,128)} %lengths.1) | copy-start | bytes 52
  6.4 9.0 %collective-permute-start.4 = (bf16[320,256]{1,0:T(8,128)(2,1)S(1)}, bf16[320,256]{1,0:T(8,128)(2,1)S(1)}, u32[]{:S(2)}, u32[]{:S(2)}) collective-permute-start(bf16[320,256]{1,0:T(8,128)(2,1)S(1)} %get-tuple-element.64), channel_id=1, source_target_pairs={{0,2},{1,3},{2,0},{3,1},{4,6},{5,7},{6,4},{7,5},{8,10},{9,11},{10,... | collective-permute-start | bytes 491528 | tf_op jit(solution)/shard_map/ppermute | solution.py:67
  6.8 10.5 %collective-permute-start.5 = (bf16[320,256]{1,0:T(8,128)(2,1)S(1)}, bf16[320,256]{1,0:T(8,128)(2,1)S(1)}, u32[]{:S(2)}, u32[]{:S(2)}) collective-permute-start(bf16[320,256]{1,0:T(8,128)(2,1)S(1)} %get-tuple-element.65), channel_id=1, source_target_pairs={{0,1},{1,0},{2,3},{3,2},{4,5},{5,4},{6,7},{7,6},{8,9},{9,8},{10,11... | collective-permute-start | bytes 491528 | tf_op jit(solution)/shard_map/ppermute | solution.py:67
  8.4 14.1 %collective-permute-start = (bf16[320,256]{1,0:T(8,128)(2,1)S(1)}, bf16[320,256]{1,0:T(8,128)(2,1)S(1)}, u32[]{:S(2)}, u32[]{:S(2)}) collective-permute-start(bf16[320,256]{1,0:T(8,128)(2,1)S(1)} %get-tuple-element.59), channel_id=1, source_target_pairs={{0,3},{1,2},{2,1},{3,0},{4,7},{5,6},{6,5},{7,4},{8,11},{9,10},{10,... | collective-permute-start | bytes 491528 | tf_op jit(solution)/shard_map/ppermute | solution.py:67
  11.3 11.2 %collective-permute-start.1 = (bf16[320,256]{1,0:T(8,128)(2,1)S(1)}, bf16[320,256]{1,0:T(8,128)(2,1)S(1)}, u32[]{:S(2)}, u32[]{:S(2)}) collective-permute-start(bf16[320,256]{1,0:T(8,128)(2,1)S(1)} %get-tuple-element.60), channel_id=1, source_target_pairs={{0,2},{1,3},{2,0},{3,1},{4,6},{5,7},{6,4},{7,5},{8,10},{9,11},{10,... | collective-permute-start | bytes 491528 | tf_op jit(solution)/shard_map/ppermute | solution.py:67
  11.7 10.8 %collective-permute-start.2 = (bf16[320,256]{1,0:T(8,128)(2,1)S(1)}, bf16[320,256]{1,0:T(8,128)(2,1)S(1)}, u32[]{:S(2)}, u32[]{:S(2)}) collective-permute-start(bf16[320,256]{1,0:T(8,128)(2,1)S(1)} %get-tuple-element.61), channel_id=1, source_target_pairs={{0,1},{1,0},{2,3},{3,2},{4,5},{5,4},{6,7},{7,6},{8,9},{9,8},{10,11... | collective-permute-start | bytes 491528 | tf_op jit(solution)/shard_map/ppermute | solution.py:67
  21.8 6.3 %collective-permute-start.6 = (bf16[320,256]{1,0:T(8,128)(2,1)S(1)}, bf16[320,256]{1,0:T(8,128)(2,1)S(1)}, u32[]{:S(2)}, u32[]{:S(2)}) collective-permute-start(bf16[320,256]{1,0:T(8,128)(2,1)S(1)} %get-tuple-element.75), channel_id=1, source_target_pairs={{3,0},{2,1},{1,2},{0,3},{7,4},{6,5},{5,6},{4,7},{11,8},{10,9},{9,1... | collective-permute-start | bytes 491528 | tf_op jit(solution)/shard_map/ppermute | solution.py:75
  28.1 16.2 %collective-permute-start.8 = (bf16[640,256]{1,0:T(8,128)(2,1)S(1)}, bf16[640,256]{1,0:T(8,128)(2,1)S(1)}, u32[]{:S(2)}, u32[]{:S(2)}) collective-permute-start(bf16[640,256]{1,0:T(8,128)(2,1)S(1)} %get-tuple-element.79), channel_id=1, source_target_pairs={{2,0},{3,1},{0,2},{1,3},{6,4},{7,5},{4,6},{5,7},{10,8},{11,9},{8,1... | collective-permute-start | bytes 983048 | tf_op jit(solution)/shard_map/ppermute | solution.py:75
  29.8 14.4 %collective-permute-start.9 = (bf16[640,256]{1,0:T(8,128)(2,1)S(1)}, bf16[640,256]{1,0:T(8,128)(2,1)S(1)}, u32[]{:S(2)}, u32[]{:S(2)}) collective-permute-start(bf16[640,256]{1,0:T(8,128)(2,1)S(1)} %get-tuple-element.80), channel_id=1, source_target_pairs={{1,0},{0,1},{3,2},{2,3},{5,4},{4,5},{7,6},{6,7},{9,8},{8,9},{11,10... | collective-permute-start | bytes 983048 | tf_op jit(solution)/shard_map/ppermute | solution.py:75
  30.5 13.7 %collective-permute-start.7 = (bf16[320,256]{1,0:T(8,128)(2,1)S(1)}, bf16[320,256]{1,0:T(8,128)(2,1)S(1)}, u32[]{:S(2)}, u32[]{:S(2)}) collective-permute-start(bf16[320,256]{1,0:T(8,128)(2,1)S(1)} %get-tuple-element.77), channel_id=1, source_target_pairs={{3,0},{2,1},{1,2},{0,3},{7,4},{6,5},{5,6},{4,7},{11,8},{10,9},{9,1... | collective-permute-start | bytes 491528 | tf_op jit(solution)/shard_map/ppermute | solution.py:75

commit v11 on v9

--- a/solution.py
+++ b/solution.py
@@ -17,9 +17,9 @@
 LOG2E = 1.4426950408889634
 NEG = -1e30
 LANES = 128
+USED = HEAD_DIM + 16
 HALF = HEAD_DIM // 2
 PACK_KIB = 52 * 1024 + 600
-UNPACK_FLOPS = 20_000_000_000
 
 rope_base = 10000.0
 
@@ -59,13 +59,6 @@
             sources[slot, target] = source
             targets[slot, source] = target
     return sources, targets
-
-
-def trade(slices):
-    moved = [slices[0]]
-    for one, pairs in zip(slices[1:], trade_rounds(lax.axis_size("tok"))):
-        moved.append(lax.ppermute(one, "tok", pairs))
-    return moved
 
 
 def send_back(result, slot):
@@ -174,16 +167,52 @@
         bias_out[phase * HEAD_DIM : (phase + 1) * HEAD_DIM, :] = turned[pl.ds(begin, HEAD_DIM), :]
 
 
-def attend_kernel(slots, closed, tokd, head, factor, cosv, sinv, masks, bias, *refs):
+def stage(slot, tokd, message, cosv, sinv, bias):
+    at = slice(slot * tokd, (slot + 1) * tokd)
+    cos_b, sin_b = cosv[:, at], sinv[:, at]
+    query, key, value = (
+        message[message_rows(tensor), :].astype(jnp.float32) + bias[:, tensor : tensor + 1]
+        for tensor in range(3)
+    )
+    rest_row = lax.broadcasted_iota(jnp.int32, (LANES - HEAD_DIM, tokd), 0)
+    zeros = jnp.zeros((LANES - HEAD_DIM, tokd), jnp.float32)
+    ones = jnp.where(rest_row < 2, 1.0, 0.0)
+    return [
+        jnp.concatenate(pair, axis=0).astype(jnp.bfloat16)
+        for pair in (
+            (rotate(query, cos_b, sin_b) * (SCALE * LOG2E), zeros),
+            (rotate(key, cos_b, sin_b), zeros),
+            (value, ones),
+        )
+    ]
+
+
+def stage_kernel(slot, phases, tokd, cosv, sinv, bias, *refs):
+    count = len(phases)
+    msgs, turned, plain = refs[:count], refs[count : 2 * count], refs[2 * count :]
+    for number, phase in enumerate(phases):
+        own_bias = bias[phase * HEAD_DIM : (phase + 1) * HEAD_DIM, :]
+        values = stage(slot, tokd, msgs[number], cosv, sinv, own_bias)
+        for tensor, value in enumerate(values):
+            turned[number][tensor] = value
+            if tensor > 0:
+                plain[number][tensor - 1] = value.T
+
+
+def attend_kernel(slots, staged, closed, tokd, head, factor, cosv, sinv, masks, bias, *refs):
     msgs, refs = refs[:slots], refs[slots:]
+    ready = {slot: refs[2 * at : 2 * at + 2] for at, slot in enumerate(staged)}
+    refs = refs[2 * len(staged) :]
+    earlier = ()
     if head > 0:
-        before, refs = refs[0], refs[slots:]
+        before, earlier, refs = refs[0], refs[1:slots], refs[slots:]
     outs, sums = refs[:slots], refs[slots]
+    for result, out in zip(earlier, [out for slot, out in enumerate(outs) if slot != EARLY]):
+        done = head * 4 * HEAD_DIM
+        out[:done, :] = result[:done, :]
     qt_all, kt_all, vt_all, gt_all, k_all, v_all, s_buf, e_buf, d_buf = refs[slots + 1 : slots + 10]
     own_bias = bias[head * HEAD_DIM : (head + 1) * HEAD_DIM, :]
     rest_row = lax.broadcasted_iota(jnp.int32, (LANES - HEAD_DIM, tokd), 0)
-    zeros = jnp.zeros((LANES - HEAD_DIM, tokd), jnp.float32)
-    ones = jnp.where(rest_row < 2, 1.0, 0.0)
 
     by_lanes = (((1,), (1,)), ((), ()))
 
@@ -204,25 +233,6 @@
         begin = ((0 if slot == EARLY else 4 * head) + tensor) * HEAD_DIM
         outs[slot][begin : begin + HEAD_DIM, :] = values
 
-    def stage(slot):
-        at = block_of(slot)
-        cos_b, sin_b = cosv[:, at], sinv[:, at]
-        query, key, value = (
-            msgs[slot][message_rows(tensor), :].astype(jnp.float32)
-            + own_bias[:, tensor : tensor + 1]
-            for tensor in range(3)
-        )
-        query = rotate(query, cos_b, sin_b) * (SCALE * LOG2E)
-        for values, rest, turned, plain in (
-            (query, zeros, qt_all, None),
-            (rotate(key, cos_b, sin_b), zeros, kt_all, k_all),
-            (value, ones, vt_all, v_all),
-        ):
-            values = jnp.concatenate([values, rest], axis=0).astype(jnp.bfloat16)
-            turned[:, at] = values
-            if plain is not None:
-                plain[at, :] = values.T
-
     def scores(slot, other):
         part = jnp.dot(
             k_all[block_of(other), :], qt_all[:, block_of(slot)], preferred_element_type=jnp.float32
@@ -236,7 +246,7 @@
 
     def output(slot):
         mixed = jnp.dot(
-            vt_all[...], e_buf[:, block_of(slot)], preferred_element_type=jnp.float32
+            vt_all[:USED, :], e_buf[:, block_of(slot)], preferred_element_type=jnp.float32
         )
         inv = 1.0 / mixed[HEAD_DIM : HEAD_DIM + 1]
         out_b = (mixed[:HEAD_DIM] * inv).astype(jnp.bfloat16)
@@ -273,7 +283,15 @@
         put(slot, 3, dvalue.astype(jnp.bfloat16))
 
     for slot in range(slots):
-        stage(slot)
+        at = block_of(slot)
+        if slot in ready:
+            turned, plain = ready[slot]
+            values, natural = [turned[number] for number in range(3)], [plain[0], plain[1]]
+        else:
+            values = stage(slot, tokd, msgs[slot], cosv, sinv, own_bias)
+            natural = [value.T for value in values[1:]]
+        qt_all[:, at], kt_all[:, at], vt_all[:, at] = values
+        k_all[at, :], v_all[at, :] = natural
     dq_total = jnp.zeros((HEAD_DIM, tokd), jnp.float32)
     dv_total = jnp.zeros((HEAD_DIM, tokd), jnp.float32)
     grad = None
@@ -345,7 +363,7 @@
         rows.append(jnp.where(lane < HEAD_DIM, first[number : number + 1], moved))
         rest = jnp.where(lane < LEFT, moved, 0.0)
         last = last + (pltpu.roll(rest, number * LEFT, 1) if number else rest)
-    return jnp.concatenate(rows + [last], axis=0)
+    return jnp.concatenate(rows + [last, jnp.zeros((4, LANES), jnp.float32)], axis=0)
 
 
 def unpack_kernel(slots, count, images, *refs):
@@ -353,7 +371,7 @@
     if not closed:
         lengths, table, *refs = refs
     msgs, refs = refs[: slots + OWN_HEADS - 1], refs[slots + OWN_HEADS - 1 :]
-    outs, held, ready, sems = refs[:4], refs[4], refs[5], refs[6]
+    *outs, held, ready, sems = refs
     early, late = msgs[:OWN_HEADS], list(msgs[OWN_HEADS:])
     late.insert(EARLY, None)
     me = lax.axis_index("tok")
@@ -447,7 +465,10 @@
         compiler_params=params(PACK_KIB / 1024),
         name="pack_heads",
     )(*inputs)
-    got = [trade(sends[:slots])]
+    rounds = trade_rounds(count)
+    first = [sends[0]] + [
+        lax.ppermute(send, "tok", pairs) for send, pairs in zip(sends[1:slots], rounds)
+    ]
     table_shape = jax.ShapeDtypeStruct((HALF, span), jnp.float32)
     mask_rows = -(-slots * (slots + 1) // 8) * 8
     tables = pl.pallas_call(
@@ -466,29 +487,60 @@
         ),
         name="rotary_tables",
     )(lengths, widths, table, inverse, bias)
-    tables, sends = lax.optimization_barrier((tables, sends[slots:]))
-    for phase in range(1, OWN_HEADS):
-        got.append(trade(sends[(phase - 1) * slots : phase * slots]))
+
+    def stage_ahead(slot, phases, messages):
+        number = len(phases)
+        results = pl.pallas_call(
+            functools.partial(stage_kernel, slot, phases, tokd),
+            out_shape=[jax.ShapeDtypeStruct((3, LANES, tokd), jnp.bfloat16)] * number
+            + [jax.ShapeDtypeStruct((2, tokd, LANES), jnp.bfloat16)] * number,
+            in_specs=[vmem] * (3 + number),
+            out_specs=[vmem] * (2 * number),
+            compiler_params=params(16),
+            cost_estimate=pl.CostEstimate(
+                flops=1_000_000 * number, bytes_accessed=0, transcendentals=0
+            ),
+            name="stage_slot",
+        )(tables[0], tables[1], tables[3], *messages)
+        return [list(pair) for pair in zip(results[:number], results[number:])]
+
+    phases = tuple(range(OWN_HEADS))
+    own = stage_ahead(0, phases, [sends[phase * slots] for phase in phases])
+    staged = [{0: pair} for pair in own]
+    got = [first] + [[sends[phase * slots]] for phase in phases[1:]]
+    latest = own
+    for slot in range(1, slots):
+        for phase in phases[1:]:
+            send, latest = lax.optimization_barrier((sends[phase * slots + slot], latest))
+            got[phase].append(lax.ppermute(send, "tok", rounds[slot - 1]))
+        if slot == 1:
+            staged[0][0], staged[1][0] = latest
+        else:
+            staged[0][slot - 1] = latest[0]
+        if slot + 1 < slots:
+            latest = stage_ahead(slot, (0,), [first[slot]])
     early = []
     carried = []
     for phase in range(OWN_HEADS):
         last = phase + 1 == OWN_HEADS
         kept = [slot for slot in range(slots) if slot != EARLY]
         sums_shape = jax.ShapeDtypeStruct(
-            (devices, 4, LANES) if last else (8, LANES), jnp.float32
-        )
-        first_carried = 4 + slots + 1
+            (devices, 8, LANES) if last else (8, LANES), jnp.float32
+        )
         *results, total = pl.pallas_call(
             functools.partial(
-                attend_kernel, slots, closed, tokd, phase, 1.0 / tokens_all**0.5
+                attend_kernel,
+                slots,
+                tuple(staged[phase]),
+                closed,
+                tokd,
+                phase,
+                1.0 / tokens_all**0.5,
             ),
             out_shape=[message if slot == EARLY else joined for slot in range(slots)]
             + [sums_shape],
-            in_specs=[vmem] * (4 + slots + len(carried)),
+            in_specs=[vmem] * (4 + slots + 2 * len(staged[phase]) + len(carried)),
             out_specs=[vmem] * slots + [hbm if last else vmem],
-            input_output_aliases={first_carried + at: slot for at, slot in enumerate(kept)}
-            if carried
-            else {},
             scratch_shapes=[pltpu.VMEM((LANES, span), jnp.bfloat16)] * 4
             + [pltpu.VMEM((span, LANES), jnp.bfloat16)] * 2
             + [pltpu.VMEM((2, span, tokd), jnp.float32)]
@@ -503,7 +555,7 @@
                 flops=12 * span * span * 256, bytes_accessed=0, transcendentals=0
             ),
             name="attend_head",
-        )(*tables, *got[phase], *carried)
+        )(*tables, *got[phase], *(one for pair in staged[phase].values() for one in pair), *carried)
         results, total, early = lax.optimization_barrier((results, total, early))
         early.append(send_back(results[EARLY], EARLY))
         carried = [total] + [results[slot] for slot in kept]
@@ -521,7 +573,6 @@
             pltpu.SemaphoreType.DMA((4,)),
         ],
         compiler_params=params(16),
-        cost_estimate=pl.CostEstimate(flops=UNPACK_FLOPS, bytes_accessed=0, transcendentals=0),
         name="unpack_heads",
     )(*places, *early, *late)
     outs, tiles = lax.optimization_barrier((outs, tiles))

time: 45.1 us -> 46.5 us (1.031)
  starting transfers between devices: 19.3 us -> 22.4 us
  waiting for transfers between devices: 10.5 us -> 8.41 us
    ppermute x4, starting transfers between devices: 4.2 us -> 7.68 us  [send_back(): lax.ppermute(result, 'tok', [(target, source) for source, target in pairs])]
    ppermute x4, waiting for transfers between devices: 4.17 us -> 6.65 us  [send_back(): lax.ppermute(result, 'tok', [(target, source) for source, target in pairs])]
    all_to_all x1, waiting for transfers between devices: 2.37 us -> 0.01 us  [on_device(): tiles = lax.all_to_all(total, ('dp', 'tok'), 0, 0, tiled=True)]
    ppermute x6, waiting for transfers between devices: 3.98 us -> 1.75 us  [the longest x3 1.75 us: on_device(): lax.ppermute(send, 'tok', pairs)]
    pallas_call x2 -> x5, Pallas kernels: 9.36 us -> 9.73 us  [the longest x2 9.12 us: on_device(): pl.pallas_call(functools.partial(attend_kernel, slots, tuple(staged[phase...]
  transfers between devices with their start and end apart: 11 -> 11, of which waited for: 5 -> 2; matrix products, arithmetic and copies ran while one was open for 0% -> 0% of each run, Pallas kernels for 27% -> 27%
where the time goes in v11:
time: 46.5 us; the launch traced here: 46.3 us
  starting transfers between devices  22.4 us (48%)
  Pallas kernels  14.7 us (32%)
  waiting for transfers between devices  8.41 us (18%)
  between operations  0.77 us (2%)
    pallas_call x2, Pallas kernels, on_device(): pl.pallas_call(functools.partial(attend_kernel, slots, tuple(staged[phase...  9.12 us
    ppermute x4, starting transfers between devices, send_back(): lax.ppermute(result, 'tok', [(target, source) for source, target in pairs])  7.68 us
    ppermute x4, waiting for transfers between devices, send_back(): lax.ppermute(result, 'tok', [(target, source) for source, target in pairs])  6.65 us
    ppermute x3, starting transfers between devices, on_device(): got[phase].append(lax.ppermute(send, 'tok', rounds[slot - 1]))  5.05 us
    all_to_all x1, starting transfers between devices, on_device(): tiles = lax.all_to_all(total, ('dp', 'tok'), 0, 0, tiled=True)  5.01 us
    ppermute x3, starting transfers between devices, on_device(): lax.ppermute(send, 'tok', pairs)  4.7 us
    ppermute x3, waiting for transfers between devices, on_device(): lax.ppermute(send, 'tok', pairs)  1.75 us
    pallas_call x1, Pallas kernels, on_device(): pl.pallas_call(functools.partial(pack_kernel, closed), out_shape=[message...  1.68 us
  transfers between devices with their start and end apart: 11, of which 2 were waited for; matrix products, arithmetic and copies ran while one was open for 0% of the time, Pallas kernels for 27%

profile of v11, /device:TPU:0, one launch (start us, length us, event | category | flops | bytes accessed | tf_op | source)
XLA Modules:
  0.0 46.3 jit_solution(14924178403036571093)
XLA Ops:
  0.6 0.0 copy-start.2
  0.6 0.0 copy-start.3
  0.7 0.0 copy-start.4
  0.7 1.7 %pack_heads.1 = (bf16[320,256]{1,0:T(8,128)(2,1)S(1)}, bf16[320,256]{1,0:T(8,128)(2,1)S(1)}, bf16[320,256]{1,0:T(8,128)(2,1)S(1)}, bf16[320,256]{1,0:T(8,128)(2,...) custom-call(bf16[256,640]{1,0:T(8,128)(2,1)} %bitcast.8, ...), custom_call_target="tpu_custom_call" | custom-call | tf_op jit(solution)/shard_map/pack_heads/pallas_call | solution.py:455
  2.4 0.0 copy-start
  2.4 4.0 %collective-permute-start.1 = (bf16[320,256]{1,0:T(8,128)(2,1)S(1)}, bf16[320,256]{1,0:T(8,128)(2,1)S(1)}, u32[]{:S(2)}, u32[]{:S(2)}) collective-permute-start(bf16[320,256]{1,0:T(8,128)(2,1)S(1)} %get-tuple-element.74), channel_id=1, source_target_pairs={{0,3},{1,2},{2,1},{3,0},{4,7},{5,6},{6,5},{7,4},{8,11},{9,10},{10,... | collective-permute-start | bytes 491528 | tf_op jit(solution)/shard_map/ppermute | solution.py:470
  6.4 0.0 copy-start.1
  6.4 0.4 collective-permute-start.3
  6.8 0.2 collective-permute-start.5
  7.1 0.0 copy-done.2
  7.1 0.0 copy-done.3
  7.1 0.0 copy-done.4
  7.1 0.0 copy-done
  7.1 0.0 copy-done.1
  7.1 1.3 %rotary_tables.1 = (f32[40,1024]{1,0:T(8,128)S(1)}, f32[40,1024]{1,0:T(8,128)S(1)}, f32[24,256]{1,0:T(8,128)S(1)}, f32[160,128]{1,0:T(8,128)S(1)}) custom-call(s32[1,4]{1,0:T(1,128)S(1)} %copy-done.1, s32[1,4]{1,0:T(1,128)S(1)} %copy-done.2, s32[4,8]{1,0:T(4,128)S(1)} %copy-done.4, f32[40,128]{1,0:T(8,128)S(1)} %copy-done.3, bf16[3,640]{1,0:T(4,128)(2,1)S(1)} %copy-done), custom_call_target="tpu_custom_call" | custom-call | flops 26214400 | tf_op jit(solution)/shard_map/rotary_tables/pallas_call | solution.py:474
  8.4 0.2 stage_slot.3
  8.6 2.9 %collective-permute-start = (bf16[320,256]{1,0:T(8,128)(2,1)S(1)}, bf16[320,256]{1,0:T(8,128)(2,1)S(1)}, u32[]{:S(2)}, u32[]{:S(2)}) collective-permute-start(bf16[320,256]{1,0:T(8,128)(2,1)S(1)} %get-tuple-element.72), channel_id=1, source_target_pairs={{0,3},{1,2},{2,1},{3,0},{4,7},{5,6},{6,5},{7,4},{8,11},{9,10},{10,... | collective-permute-start | bytes 491528 | tf_op jit(solution)/shard_map/ppermute | solution.py:515
  11.5 0.0 collective-permute-done.1.refs_0_.refs_1_
  11.5 0.2 stage_slot.4
  11.7 2.0 %collective-permute-start.2 = (bf16[320,256]{1,0:T(8,128)(2,1)S(1)}, bf16[320,256]{1,0:T(8,128)(2,1)S(1)}, u32[]{:S(2)}, u32[]{:S(2)}) collective-permute-start(bf16[320,256]{1,0:T(8,128)(2,1)S(1)} %get-tuple-element.77), channel_id=1, source_target_pairs={{0,2},{1,3},{2,0},{3,1},{4,6},{5,7},{6,4},{7,5},{8,10},{9,11},{10,... | collective-permute-start | bytes 491528 | tf_op jit(solution)/shard_map/ppermute | solution.py:515
  13.7 1.7 %collective-permute-done.3.refs_0_.refs_2_ = bf16[320,256]{1,0:T(8,128)(2,1)S(1)} collective-permute-done((bf16[320,256]{1,0:T(8,128)(2,1)S(1)}, bf16[320,256]{1,0:T(8,128)(2,1)S(1)}, u32[]{:S(2)}, u32[]{:S(2)}) %collective-permute-start.3) | collective-permute-done | bytes 163872 | tf_op jit(solution)/shard_map/ppermute | solution.py:470
  15.5 0.2 stage_slot.5
  15.6 0.1 collective-permute-start.4
  15.8 0.0 collective-permute-done.5.refs_3_
  15.8 4.3 %attend_head.2 = (bf16[640,256]{1,0:T(8,128)(2,1)S(1)}, bf16[320,256]{1,0:T(8,128)(2,1)S(1)}, bf16[640,256]{1,0:T(8,128)(2,1)S(1)}, bf16[640,256]{1,0:T(8,128)(2,1)S(1)}, f32[8,128]{1,0:T(8,128)S(1)}) custom-call(f32[40,1024]{1,0:T(8,128)S(1)} %get-tuple-element.61.cosv, f32[40,1024]{1,0:T(8,128)S(1)} %get-tuple-element.62.sinv, ...), custom_call_target="tpu_custom_call" | custom-call | flops 3221225472 | tf_op jit(solution)/shard_map/attend_head/pallas_call | solution.py:530
  20.0 3.1 %collective-permute-start.6 = (bf16[320,256]{1,0:T(8,128)(2,1)S(1)}, bf16[320,256]{1,0:T(8,128)(2,1)S(1)}, u32[]{:S(2)}, u32[]{:S(2)}) collective-permute-start(bf16[320,256]{1,0:T(8,128)(2,1)S(1)} %get-tuple-element.101), channel_id=1, source_target_pairs={{3,0},{2,1},{1,2},{0,3},{7,4},{6,5},{5,6},{4,7},{11,8},{10,9},{9,1... | collective-permute-start | bytes 491528 | tf_op jit(solution)/shard_map/ppermute | solution.py:68
  23.1 0.0 collective-permute-done.refs_1_
  23.1 0.0 collective-permute-done.2.refs_2_
  23.1 0.0 collective-permute-done.4.refs_3_
  23.1 4.9 %attend_head.3 = (bf16[640,256]{1,0:T(8,128)(2,1)S(1)}, bf16[320,256]{1,0:T(8,128)(2,1)S(1)}, bf16[640,256]{1,0:T(8,128)(2,1)S(1)}, bf16[640,256]{1,0:T(8,128)(2,1)S(1)}, f32[32,8,128]{2,1,0:T(8,128)}) custom-call(f32[40,1024]{1,0:T(8,128)S(1)} %get-tuple-element.61.cosv, f32[40,1024]{1,0:T(8,128)S(1)} %get-tuple-element.62.sinv, ...), custom_call_target="tpu_custom_call" | custom-call | flops 3221225472 | tf_op jit(solution)/shard_map/attend_head/pallas_call | solution.py:530
  28.0 0.0 collective-permute-done.6.refs_0_
  28.0 0.5 %collective-permute-start.8 = (bf16[640,256]{1,0:T(8,128)(2,1)S(1)}, bf16[640,256]{1,0:T(8,128)(2,1)S(1)}, u32[]{:S(2)}, u32[]{:S(2)}) collective-permute-start(bf16[640,256]{1,0:T(8,128)(2,1)S(1)} %get-tuple-element.105), channel_id=1, source_target_pairs={{2,0},{3,1},{0,2},{1,3},{6,4},{7,5},{4,6},{5,7},{10,8},{11,9},{8,1... | collective-permute-start | bytes 983048 | tf_op jit(solution)/shard_map/ppermute | solution.py:68
  28.5 1.4 %collective-permute-start.9 = (bf16[640,256]{1,0:T(8,128)(2,1)S(1)}, bf16[640,256]{1,0:T(8,128)(2,1)S(1)}, u32[]{:S(2)}, u32[]{:S(2)}) collective-permute-start(bf16[640,256]{1,0:T(8,128)(2,1)S(1)} %get-tuple-element.106), channel_id=1, source_target_pairs={{1,0},{0,1},{3,2},{2,3},{5,4},{4,5},{7,6},{6,7},{9,8},{8,9},{11,10... | collective-permute-start | bytes 983048 | tf_op jit(solution)/shard_map/ppermute | solution.py:68
  29.9 5.0 %all-to-all-start = ((f32[32,8,128]{2,1,0:T(8,128)}), f32[32,8,128]{2,1,0:T(8,128)S(1)}, u32[]{:S(2)}, u32[]{:S(2)}) async-start(f32[32,8,128]{2,1,0:T(8,128)} %get-tuple-element.111), calls=%async_computation | async-start | bytes 262144 | tf_op jit(solution)/shard_map/all_to_all | solution.py:562
  34.9 2.7 %collective-permute-start.7 = (bf16[320,256]{1,0:T(8,128)(2,1)S(1)}, bf16[320,256]{1,0:T(8,128)(2,1)S(1)}, u32[]{:S(2)}, u32[]{:S(2)}) collective-permute-start(bf16[320,256]{1,0:T(8,128)(2,1)S(1)} %get-tuple-element.103), channel_id=1, source_target_pairs={{3,0},{2,1},{1,2},{0,3},{7,4},{6,5},{5,6},{4,7},{11,8},{10,9},{9,1... | collective-permute-start | bytes 491528 | tf_op jit(solution)/shard_map/ppermute | solution.py:68
  37.6 6.6 %collective-permute-done.7.refs_1_ = bf16[320,256]{1,0:T(8,128)(2,1)S(1)} collective-permute-done((bf16[320,256]{1,0:T(8,128)(2,1)S(1)}, bf16[320,256]{1,0:T(8,128)(2,1)S(1)}, u32[]{:S(2)}, u32[]{:S(2)}) %collective-permute-start.7) | collective-permute-done | bytes 163872 | tf_op jit(solution)/shard_map/ppermute | solution.py:68
  44.3 0.0 collective-permute-done.8.refs_3_
  44.3 0.0 collective-permute-done.9.refs_4_
  44.3 1.3 %unpack_heads.1 = (bf16[256,640]{1,0:T(8,128)(2,1)}, bf16[256,640]{1,0:T(8,128)(2,1)}, bf16[256,640]{1,0:T(8,128)(2,1)}, bf16[256,640]{1,0:T(8,128)(2,1)}) custom-call(bf16[320,256]{1,0:T(8,128)(2,1)S(1)} %collective-permute-done.6.refs_0_, bf16[320,256]{1,0:T(8,128)(2,1)S(1)} %collective-permute-done.7.refs_1_, ...), custom_call_target="tpu_custom_call" | custom-call | tf_op jit(solution)/shard_map/unpack_heads/pallas_call | solution.py:565
  45.6 0.0 all-to-all-done.tiles
  45.6 0.7 %bias_sums.1 = f32[3,640]{1,0:T(4,128)} custom-call(f32[32,8,128]{2,1,0:T(8,128)S(1)} %all-to-all-done.tiles), custom_call_target="tpu_custom_call" | custom-call | tf_op jit(solution)/shard_map/bias_sums/pallas_call | solution.py:579
Async XLA Ops:
  0.6 6.4 %copy-start.2 = (s32[1,4]{1,0:T(1,128)S(1)}, s32[1,4]{1,0:T(1,128)}, u32[]{:S(2)}) copy-start(s32[1,4]{1,0:T(1,128)} %widths.1) | copy-start | bytes 52
  0.6 6.4 %copy-start.3 = (f32[40,128]{1,0:T(8,128)S(1)}, f32[40,128]{1,0:T(8,128)}, u32[]{:S(2)}) copy-start(f32[40,128]{1,0:T(8,128)} %constant.5.clone.inverse) | copy-start | bytes 61444
  0.7 6.4 %copy-start.4 = (s32[4,8]{1,0:T(4,128)S(1)}, s32[4,8]{1,0:T(4,128)}, u32[]{:S(2)}) copy-start(s32[4,8]{1,0:T(4,128)} %constant.4.clone.table) | copy-start | bytes 388
  2.4 4.7 %copy-start = (bf16[3,640]{1,0:T(4,128)(2,1)S(1)}, bf16[3,640]{1,0:T(4,128)(2,1)}, u32[]{:S(2)}) copy-start(bf16[3,640]{1,0:T(4,128)(2,1)} %bias.1) | copy-start | bytes 11524
  2.4 9.1 %collective-permute-start.1 = (bf16[320,256]{1,0:T(8,128)(2,1)S(1)}, bf16[320,256]{1,0:T(8,128)(2,1)S(1)}, u32[]{:S(2)}, u32[]{:S(2)}) collective-permute-start(bf16[320,256]{1,0:T(8,128)(2,1)S(1)} %get-tuple-element.74), channel_id=1, source_target_pairs={{0,3},{1,2},{2,1},{3,0},{4,7},{5,6},{6,5},{7,4},{8,11},{9,10},{10,... | collective-permute-start | bytes 491528 | tf_op jit(solution)/shard_map/ppermute | solution.py:470
  6.4 0.7 %copy-start.1 = (s32[1,4]{1,0:T(1,128)S(1)}, s32[1,4]{1,0:T(1,128)}, u32[]{:S(2)}) copy-start(s32[1,4]{1,0:T(1,128)} %lengths.1) | copy-start | bytes 52
  6.4 9.0 %collective-permute-start.3 = (bf16[320,256]{1,0:T(8,128)(2,1)S(1)}, bf16[320,256]{1,0:T(8,128)(2,1)S(1)}, u32[]{:S(2)}, u32[]{:S(2)}) collective-permute-start(bf16[320,256]{1,0:T(8,128)(2,1)S(1)} %get-tuple-element.79), channel_id=1, source_target_pairs={{0,2},{1,3},{2,0},{3,1},{4,6},{5,7},{6,4},{7,5},{8,10},{9,11},{10,... | collective-permute-start | bytes 491528 | tf_op jit(solution)/shard_map/ppermute | solution.py:470
  6.8 8.9 %collective-permute-start.5 = (bf16[320,256]{1,0:T(8,128)(2,1)S(1)}, bf16[320,256]{1,0:T(8,128)(2,1)S(1)}, u32[]{:S(2)}, u32[]{:S(2)}) collective-permute-start(bf16[320,256]{1,0:T(8,128)(2,1)S(1)} %get-tuple-element.85), channel_id=1, source_target_pairs={{0,1},{1,0},{2,3},{3,2},{4,5},{5,4},{6,7},{7,6},{8,9},{9,8},{10,11... | collective-permute-start | bytes 491528 | tf_op jit(solution)/shard_map/ppermute | solution.py:470
  8.6 14.5 %collective-permute-start = (bf16[320,256]{1,0:T(8,128)(2,1)S(1)}, bf16[320,256]{1,0:T(8,128)(2,1)S(1)}, u32[]{:S(2)}, u32[]{:S(2)}) collective-permute-start(bf16[320,256]{1,0:T(8,128)(2,1)S(1)} %get-tuple-element.72), channel_id=1, source_target_pairs={{0,3},{1,2},{2,1},{3,0},{4,7},{5,6},{6,5},{7,4},{8,11},{9,10},{10,... | collective-permute-start | bytes 491528 | tf_op jit(solution)/shard_map/ppermute | solution.py:515
  11.7 11.4 %collective-permute-start.2 = (bf16[320,256]{1,0:T(8,128)(2,1)S(1)}, bf16[320,256]{1,0:T(8,128)(2,1)S(1)}, u32[]{:S(2)}, u32[]{:S(2)}) collective-permute-start(bf16[320,256]{1,0:T(8,128)(2,1)S(1)} %get-tuple-element.77), channel_id=1, source_target_pairs={{0,2},{1,3},{2,0},{3,1},{4,6},{5,7},{6,4},{7,5},{8,10},{9,11},{10,... | collective-permute-start | bytes 491528 | tf_op jit(solution)/shard_map/ppermute | solution.py:515
  15.6 7.5 %collective-permute-start.4 = (bf16[320,256]{1,0:T(8,128)(2,1)S(1)}, bf16[320,256]{1,0:T(8,128)(2,1)S(1)}, u32[]{:S(2)}, u32[]{:S(2)}) collective-permute-start(bf16[320,256]{1,0:T(8,128)(2,1)S(1)} %get-tuple-element.82), channel_id=1, source_target_pairs={{0,1},{1,0},{2,3},{3,2},{4,5},{5,4},{6,7},{7,6},{8,9},{9,8},{10,11... | collective-permute-start | bytes 491528 | tf_op jit(solution)/shard_map/ppermute | solution.py:515
  20.0 7.9 %collective-permute-start.6 = (bf16[320,256]{1,0:T(8,128)(2,1)S(1)}, bf16[320,256]{1,0:T(8,128)(2,1)S(1)}, u32[]{:S(2)}, u32[]{:S(2)}) collective-permute-start(bf16[320,256]{1,0:T(8,128)(2,1)S(1)} %get-tuple-element.101), channel_id=1, source_target_pairs={{3,0},{2,1},{1,2},{0,3},{7,4},{6,5},{5,6},{4,7},{11,8},{10,9},{9,1... | collective-permute-start | bytes 491528 | tf_op jit(solution)/shard_map/ppermute | solution.py:68
  28.0 16.3 %collective-permute-start.8 = (bf16[640,256]{1,0:T(8,128)(2,1)S(1)}, bf16[640,256]{1,0:T(8,128)(2,1)S(1)}, u32[]{:S(2)}, u32[]{:S(2)}) collective-permute-start(bf16[640,256]{1,0:T(8,128)(2,1)S(1)} %get-tuple-element.105), channel_id=1, source_target_pairs={{2,0},{3,1},{0,2},{1,3},{6,4},{7,5},{4,6},{5,7},{10,8},{11,9},{8,1... | collective-permute-start | bytes 983048 | tf_op jit(solution)/shard_map/ppermute | solution.py:68
  28.5 15.8 %collective-permute-start.9 = (bf16[640,256]{1,0:T(8,128)(2,1)S(1)}, bf16[640,256]{1,0:T(8,128)(2,1)S(1)}, u32[]{:S(2)}, u32[]{:S(2)}) collective-permute-start(bf16[640,256]{1,0:T(8,128)(2,1)S(1)} %get-tuple-element.106), channel_id=1, source_target_pairs={{1,0},{0,1},{3,2},{2,3},{5,4},{4,5},{7,6},{6,7},{9,8},{8,9},{11,10... | collective-permute-start | bytes 983048 | tf_op jit(solution)/shard_map/ppermute | solution.py:68
  29.9 15.7 %all-to-all-start = ((f32[32,8,128]{2,1,0:T(8,128)}), f32[32,8,128]{2,1,0:T(8,128)S(1)}, u32[]{:S(2)}, u32[]{:S(2)}) async-start(f32[32,8,128]{2,1,0:T(8,128)} %get-tuple-element.111), calls=%async_computation | async-start | bytes 262144 | tf_op jit(solution)/shard_map/all_to_all | solution.py:562
  34.9 9.4 %collective-permute-start.7 = (bf16[320,256]{1,0:T(8,128)(2,1)S(1)}, bf16[320,256]{1,0:T(8,128)(2,1)S(1)}, u32[]{:S(2)}, u32[]{:S(2)}) collective-permute-start(bf16[320,256]{1,0:T(8,128)(2,1)S(1)} %get-tuple-element.103), channel_id=1, source_target_pairs={{3,0},{2,1},{1,2},{0,3},{7,4},{6,5},{5,6},{4,7},{11,8},{10,9},{9,1... | collective-permute-start | bytes 491528 | tf_op jit(solution)/shard_map/ppermute | solution.py:68

commit v12 on v11

--- a/solution.py
+++ b/solution.py
@@ -20,6 +20,7 @@
 USED = HEAD_DIM + 16
 HALF = HEAD_DIM // 2
 PACK_KIB = 52 * 1024 + 600
+UNPACK_FLOPS = 20_000_000_000
 
 rope_base = 10000.0
 
@@ -363,7 +364,7 @@
         rows.append(jnp.where(lane < HEAD_DIM, first[number : number + 1], moved))
         rest = jnp.where(lane < LEFT, moved, 0.0)
         last = last + (pltpu.roll(rest, number * LEFT, 1) if number else rest)
-    return jnp.concatenate(rows + [last, jnp.zeros((4, LANES), jnp.float32)], axis=0)
+    return jnp.concatenate(rows + [last], axis=0)
 
 
 def unpack_kernel(slots, count, images, *refs):
@@ -525,7 +526,7 @@
         last = phase + 1 == OWN_HEADS
         kept = [slot for slot in range(slots) if slot != EARLY]
         sums_shape = jax.ShapeDtypeStruct(
-            (devices, 8, LANES) if last else (8, LANES), jnp.float32
+            (devices, 4, LANES) if last else (8, LANES), jnp.float32
         )
         *results, total = pl.pallas_call(
             functools.partial(
@@ -573,6 +574,7 @@
             pltpu.SemaphoreType.DMA((4,)),
         ],
         compiler_params=params(16),
+        cost_estimate=pl.CostEstimate(flops=UNPACK_FLOPS, bytes_accessed=0, transcendentals=0),
         name="unpack_heads",
     )(*places, *early, *late)
     outs, tiles = lax.optimization_barrier((outs, tiles))

time: 46.5 us -> 44.7 us (0.961)
  starting transfers between devices: 22.4 us -> 21 us
    ppermute x4, waiting for transfers between devices: 6.65 us -> 4.06 us  [send_back(): lax.ppermute(result, 'tok', [(target, source) for source, target in pairs])]
    all_to_all x1, waiting for transfers between devices: 0.01 us -> 2.2 us  [on_device(): tiles = lax.all_to_all(total, ('dp', 'tok'), 0, 0, tiled=True)]
    ppermute x4, starting transfers between devices: 7.68 us -> 6.61 us  [send_back(): lax.ppermute(result, 'tok', [(target, source) for source, target in pairs])]
  transfers between devices with their start and end apart: 11 -> 11, of which waited for: 2 -> 4; matrix products, arithmetic and copies ran while one was open for 0% -> 0% of each run, Pallas kernels for 27% -> 28%
where the time goes in v12:
time: 44.7 us; the launch traced here: 44.5 us
  starting transfers between devices  21 us (47%)
  Pallas kernels  14.7 us (33%)
  waiting for transfers between devices  8.02 us (18%)
  between operations  0.76 us (2%)
    pallas_call x2, Pallas kernels, on_device(): pl.pallas_call(functools.partial(attend_kernel, slots, tuple(staged[phase...  9.1 us
    ppermute x4, starting transfers between devices, send_back(): lax.ppermute(result, 'tok', [(target, source) for source, target in pairs])  6.61 us
    ppermute x3, starting transfers between devices, on_device(): got[phase].append(lax.ppermute(send, 'tok', rounds[slot - 1]))  5.05 us
    ppermute x3, starting transfers between devices, on_device(): lax.ppermute(send, 'tok', pairs)  4.7 us
    all_to_all x1, starting transfers between devices, on_device(): tiles = lax.all_to_all(total, ('dp', 'tok'), 0, 0, tiled=True)  4.63 us
    ppermute x4, waiting for transfers between devices, send_back(): lax.ppermute(result, 'tok', [(target, source) for source, target in pairs])  4.06 us
    all_to_all x1, waiting for transfers between devices, on_device(): tiles = lax.all_to_all(total, ('dp', 'tok'), 0, 0, tiled=True)  2.2 us
    ppermute x3, waiting for transfers between devices, on_device(): lax.ppermute(send, 'tok', pairs)  1.75 us
  transfers between devices with their start and end apart: 11, of which 4 were waited for; matrix products, arithmetic and copies ran while one was open for 0% of the time, Pallas kernels for 28%

profile of v12, /device:TPU:0, one launch (start us, length us, event | category | flops | bytes accessed | tf_op | source)
XLA Modules:
  0.0 44.5 jit_solution(17538591578427523210)
XLA Ops:
  0.6 0.0 copy-start.2
  0.6 0.0 copy-start.3
  0.7 0.0 copy-start.4
  0.7 1.7 %pack_heads.1 = (bf16[320,256]{1,0:T(8,128)(2,1)S(1)}, bf16[320,256]{1,0:T(8,128)(2,1)S(1)}, bf16[320,256]{1,0:T(8,128)(2,1)S(1)}, bf16[320,256]{1,0:T(8,128)(2,...) custom-call(bf16[256,640]{1,0:T(8,128)(2,1)} %bitcast.8, ...), custom_call_target="tpu_custom_call" | custom-call | tf_op jit(solution)/shard_map/pack_heads/pallas_call | solution.py:456
  2.4 0.0 copy-start
  2.4 4.0 %collective-permute-start.1 = (bf16[320,256]{1,0:T(8,128)(2,1)S(1)}, bf16[320,256]{1,0:T(8,128)(2,1)S(1)}, u32[]{:S(2)}, u32[]{:S(2)}) collective-permute-start(bf16[320,256]{1,0:T(8,128)(2,1)S(1)} %get-tuple-element.74), channel_id=1, source_target_pairs={{0,3},{1,2},{2,1},{3,0},{4,7},{5,6},{6,5},{7,4},{8,11},{9,10},{10,... | collective-permute-start | bytes 491528 | tf_op jit(solution)/shard_map/ppermute | solution.py:471
  6.4 0.0 copy-start.1
  6.4 0.4 collective-permute-start.3
  6.8 0.2 collective-permute-start.5
  7.1 0.0 copy-done.2
  7.1 0.0 copy-done.3
  7.1 0.0 copy-done.4
  7.1 0.0 copy-done
  7.1 0.0 copy-done.1
  7.1 1.3 %rotary_tables.1 = (f32[40,1024]{1,0:T(8,128)S(1)}, f32[40,1024]{1,0:T(8,128)S(1)}, f32[24,256]{1,0:T(8,128)S(1)}, f32[160,128]{1,0:T(8,128)S(1)}) custom-call(s32[1,4]{1,0:T(1,128)S(1)} %copy-done.1, s32[1,4]{1,0:T(1,128)S(1)} %copy-done.2, s32[4,8]{1,0:T(4,128)S(1)} %copy-done.4, f32[40,128]{1,0:T(8,128)S(1)} %copy-done.3, bf16[3,640]{1,0:T(4,128)(2,1)S(1)} %copy-done), custom_call_target="tpu_custom_call" | custom-call | flops 26214400 | tf_op jit(solution)/shard_map/rotary_tables/pallas_call | solution.py:475
  8.4 0.2 stage_slot.3
  8.6 2.9 %collective-permute-start = (bf16[320,256]{1,0:T(8,128)(2,1)S(1)}, bf16[320,256]{1,0:T(8,128)(2,1)S(1)}, u32[]{:S(2)}, u32[]{:S(2)}) collective-permute-start(bf16[320,256]{1,0:T(8,128)(2,1)S(1)} %get-tuple-element.72), channel_id=1, source_target_pairs={{0,3},{1,2},{2,1},{3,0},{4,7},{5,6},{6,5},{7,4},{8,11},{9,10},{10,... | collective-permute-start | bytes 491528 | tf_op jit(solution)/shard_map/ppermute | solution.py:516
  11.5 0.0 collective-permute-done.1.refs_0_.refs_1_
  11.5 0.2 stage_slot.4
  11.7 2.0 %collective-permute-start.2 = (bf16[320,256]{1,0:T(8,128)(2,1)S(1)}, bf16[320,256]{1,0:T(8,128)(2,1)S(1)}, u32[]{:S(2)}, u32[]{:S(2)}) collective-permute-start(bf16[320,256]{1,0:T(8,128)(2,1)S(1)} %get-tuple-element.77), channel_id=1, source_target_pairs={{0,2},{1,3},{2,0},{3,1},{4,6},{5,7},{6,4},{7,5},{8,10},{9,11},{10,... | collective-permute-start | bytes 491528 | tf_op jit(solution)/shard_map/ppermute | solution.py:516
  13.7 1.7 %collective-permute-done.3.refs_0_.refs_2_ = bf16[320,256]{1,0:T(8,128)(2,1)S(1)} collective-permute-done((bf16[320,256]{1,0:T(8,128)(2,1)S(1)}, bf16[320,256]{1,0:T(8,128)(2,1)S(1)}, u32[]{:S(2)}, u32[]{:S(2)}) %collective-permute-start.3) | collective-permute-done | bytes 163872 | tf_op jit(solution)/shard_map/ppermute | solution.py:471
  15.5 0.2 stage_slot.5
  15.6 0.1 collective-permute-start.4
  15.8 0.0 collective-permute-done.5.refs_3_
  15.8 4.3 %attend_head.2 = (bf16[640,256]{1,0:T(8,128)(2,1)S(1)}, bf16[320,256]{1,0:T(8,128)(2,1)S(1)}, bf16[640,256]{1,0:T(8,128)(2,1)S(1)}, bf16[640,256]{1,0:T(8,128)(2,1)S(1)}, f32[8,128]{1,0:T(8,128)S(1)}) custom-call(f32[40,1024]{1,0:T(8,128)S(1)} %get-tuple-element.61.cosv, f32[40,1024]{1,0:T(8,128)S(1)} %get-tuple-element.62.sinv, ...), custom_call_target="tpu_custom_call" | custom-call | flops 3221225472 | tf_op jit(solution)/shard_map/attend_head/pallas_call | solution.py:531
  20.0 3.1 %collective-permute-start.6 = (bf16[320,256]{1,0:T(8,128)(2,1)S(1)}, bf16[320,256]{1,0:T(8,128)(2,1)S(1)}, u32[]{:S(2)}, u32[]{:S(2)}) collective-permute-start(bf16[320,256]{1,0:T(8,128)(2,1)S(1)} %get-tuple-element.101), channel_id=1, source_target_pairs={{3,0},{2,1},{1,2},{0,3},{7,4},{6,5},{5,6},{4,7},{11,8},{10,9},{9,1... | collective-permute-start | bytes 491528 | tf_op jit(solution)/shard_map/ppermute | solution.py:69
  23.1 0.0 collective-permute-done.refs_1_
  23.1 0.0 collective-permute-done.2.refs_2_
  23.1 0.0 collective-permute-done.4.refs_3_
  23.1 4.8 %attend_head.3 = (bf16[640,256]{1,0:T(8,128)(2,1)S(1)}, bf16[320,256]{1,0:T(8,128)(2,1)S(1)}, bf16[640,256]{1,0:T(8,128)(2,1)S(1)}, bf16[640,256]{1,0:T(8,128)(2,1)S(1)}, f32[32,4,128]{2,1,0:T(4,128)}) custom-call(f32[40,1024]{1,0:T(8,128)S(1)} %get-tuple-element.61.cosv, f32[40,1024]{1,0:T(8,128)S(1)} %get-tuple-element.62.sinv, ...), custom_call_target="tpu_custom_call" | custom-call | flops 3221225472 | tf_op jit(solution)/shard_map/attend_head/pallas_call | solution.py:531
  28.0 0.0 collective-permute-done.6.refs_0_
  28.0 0.5 %collective-permute-start.8 = (bf16[640,256]{1,0:T(8,128)(2,1)S(1)}, bf16[640,256]{1,0:T(8,128)(2,1)S(1)}, u32[]{:S(2)}, u32[]{:S(2)}) collective-permute-start(bf16[640,256]{1,0:T(8,128)(2,1)S(1)} %get-tuple-element.105), channel_id=1, source_target_pairs={{2,0},{3,1},{0,2},{1,3},{6,4},{7,5},{4,6},{5,7},{10,8},{11,9},{8,1... | collective-permute-start | bytes 983048 | tf_op jit(solution)/shard_map/ppermute | solution.py:69
  28.5 1.4 %collective-permute-start.9 = (bf16[640,256]{1,0:T(8,128)(2,1)S(1)}, bf16[640,256]{1,0:T(8,128)(2,1)S(1)}, u32[]{:S(2)}, u32[]{:S(2)}) collective-permute-start(bf16[640,256]{1,0:T(8,128)(2,1)S(1)} %get-tuple-element.106), channel_id=1, source_target_pairs={{1,0},{0,1},{3,2},{2,3},{5,4},{4,5},{7,6},{6,7},{9,8},{8,9},{11,10... | collective-permute-start | bytes 983048 | tf_op jit(solution)/shard_map/ppermute | solution.py:69
  29.9 1.6 %collective-permute-start.7 = (bf16[320,256]{1,0:T(8,128)(2,1)S(1)}, bf16[320,256]{1,0:T(8,128)(2,1)S(1)}, u32[]{:S(2)}, u32[]{:S(2)}) collective-permute-start(bf16[320,256]{1,0:T(8,128)(2,1)S(1)} %get-tuple-element.103), channel_id=1, source_target_pairs={{3,0},{2,1},{1,2},{0,3},{7,4},{6,5},{5,6},{4,7},{11,8},{10,9},{9,1... | collective-permute-start | bytes 491528 | tf_op jit(solution)/shard_map/ppermute | solution.py:69
  31.5 4.6 %all-to-all-start = ((f32[32,4,128]{2,1,0:T(4,128)}), f32[32,4,128]{2,1,0:T(4,128)S(1)}, u32[]{:S(2)}, u32[]{:S(2)}) async-start(f32[32,4,128]{2,1,0:T(4,128)} %get-tuple-element.111), calls=%async_computation | async-start | bytes 131072 | tf_op jit(solution)/shard_map/all_to_all | solution.py:563
  36.2 3.5 %collective-permute-done.7.refs_1_ = bf16[320,256]{1,0:T(8,128)(2,1)S(1)} collective-permute-done((bf16[320,256]{1,0:T(8,128)(2,1)S(1)}, bf16[320,256]{1,0:T(8,128)(2,1)S(1)}, u32[]{:S(2)}, u32[]{:S(2)}) %collective-permute-start.7) | collective-permute-done | bytes 163872 | tf_op jit(solution)/shard_map/ppermute | solution.py:69
  39.7 0.0 collective-permute-done.8.refs_3_
  39.7 0.5 %collective-permute-done.9.refs_4_ = bf16[640,256]{1,0:T(8,128)(2,1)S(1)} collective-permute-done((bf16[640,256]{1,0:T(8,128)(2,1)S(1)}, bf16[640,256]{1,0:T(8,128)(2,1)S(1)}, u32[]{:S(2)}, u32[]{:S(2)}) %collective-permute-start.9) | collective-permute-done | bytes 327712 | tf_op jit(solution)/shard_map/ppermute | solution.py:69
  40.2 1.3 %unpack_heads.1 = (bf16[256,640]{1,0:T(8,128)(2,1)}, bf16[256,640]{1,0:T(8,128)(2,1)}, bf16[256,640]{1,0:T(8,128)(2,1)}, bf16[256,640]{1,0:T(8,128)(2,1)}) custom-call(bf16[320,256]{1,0:T(8,128)(2,1)S(1)} %collective-permute-done.6.refs_0_, bf16[320,256]{1,0:T(8,128)(2,1)S(1)} %collective-permute-done.7.refs_1_, ...), custom_call_target="tpu_custom_call" | custom-call | flops 20000000000 | tf_op jit(solution)/shard_map/unpack_heads/pallas_call | solution.py:566
  41.6 2.2 %all-to-all-done.tiles = f32[32,4,128]{2,1,0:T(4,128)S(1)} async-done(((f32[32,4,128]{2,1,0:T(4,128)}), f32[32,4,128]{2,1,0:T(4,128)S(1)}, u32[]{:S(2)}, u32[]{:S(2)}) %all-to-all-start) | async-done | bytes 65568 | tf_op jit(solution)/shard_map/all_to_all | solution.py:563
  43.8 0.7 %bias_sums.1 = f32[3,640]{1,0:T(4,128)} custom-call(f32[32,4,128]{2,1,0:T(4,128)S(1)} %all-to-all-done.tiles), custom_call_target="tpu_custom_call" | custom-call | tf_op jit(solution)/shard_map/bias_sums/pallas_call | solution.py:581
Async XLA Ops:
  0.6 6.4 %copy-start.2 = (s32[1,4]{1,0:T(1,128)S(1)}, s32[1,4]{1,0:T(1,128)}, u32[]{:S(2)}) copy-start(s32[1,4]{1,0:T(1,128)} %widths.1) | copy-start | bytes 52
  0.6 6.4 %copy-start.3 = (f32[40,128]{1,0:T(8,128)S(1)}, f32[40,128]{1,0:T(8,128)}, u32[]{:S(2)}) copy-start(f32[40,128]{1,0:T(8,128)} %constant.5.clone.inverse) | copy-start | bytes 61444
  0.7 6.4 %copy-start.4 = (s32[4,8]{1,0:T(4,128)S(1)}, s32[4,8]{1,0:T(4,128)}, u32[]{:S(2)}) copy-start(s32[4,8]{1,0:T(4,128)} %constant.4.clone.table) | copy-start | bytes 388
  2.4 4.7 %copy-start = (bf16[3,640]{1,0:T(4,128)(2,1)S(1)}, bf16[3,640]{1,0:T(4,128)(2,1)}, u32[]{:S(2)}) copy-start(bf16[3,640]{1,0:T(4,128)(2,1)} %bias.1) | copy-start | bytes 11524
  2.4 9.1 %collective-permute-start.1 = (bf16[320,256]{1,0:T(8,128)(2,1)S(1)}, bf16[320,256]{1,0:T(8,128)(2,1)S(1)}, u32[]{:S(2)}, u32[]{:S(2)}) collective-permute-start(bf16[320,256]{1,0:T(8,128)(2,1)S(1)} %get-tuple-element.74), channel_id=1, source_target_pairs={{0,3},{1,2},{2,1},{3,0},{4,7},{5,6},{6,5},{7,4},{8,11},{9,10},{10,... | collective-permute-start | bytes 491528 | tf_op jit(solution)/shard_map/ppermute | solution.py:471
  6.4 0.7 %copy-start.1 = (s32[1,4]{1,0:T(1,128)S(1)}, s32[1,4]{1,0:T(1,128)}, u32[]{:S(2)}) copy-start(s32[1,4]{1,0:T(1,128)} %lengths.1) | copy-start | bytes 52
  6.4 9.0 %collective-permute-start.3 = (bf16[320,256]{1,0:T(8,128)(2,1)S(1)}, bf16[320,256]{1,0:T(8,128)(2,1)S(1)}, u32[]{:S(2)}, u32[]{:S(2)}) collective-permute-start(bf16[320,256]{1,0:T(8,128)(2,1)S(1)} %get-tuple-element.79), channel_id=1, source_target_pairs={{0,2},{1,3},{2,0},{3,1},{4,6},{5,7},{6,4},{7,5},{8,10},{9,11},{10,... | collective-permute-start | bytes 491528 | tf_op jit(solution)/shard_map/ppermute | solution.py:471
  6.8 8.9 %collective-permute-start.5 = (bf16[320,256]{1,0:T(8,128)(2,1)S(1)}, bf16[320,256]{1,0:T(8,128)(2,1)S(1)}, u32[]{:S(2)}, u32[]{:S(2)}) collective-permute-start(bf16[320,256]{1,0:T(8,128)(2,1)S(1)} %get-tuple-element.85), channel_id=1, source_target_pairs={{0,1},{1,0},{2,3},{3,2},{4,5},{5,4},{6,7},{7,6},{8,9},{9,8},{10,11... | collective-permute-start | bytes 491528 | tf_op jit(solution)/shard_map/ppermute | solution.py:471
  8.6 14.5 %collective-permute-start = (bf16[320,256]{1,0:T(8,128)(2,1)S(1)}, bf16[320,256]{1,0:T(8,128)(2,1)S(1)}, u32[]{:S(2)}, u32[]{:S(2)}) collective-permute-start(bf16[320,256]{1,0:T(8,128)(2,1)S(1)} %get-tuple-element.72), channel_id=1, source_target_pairs={{0,3},{1,2},{2,1},{3,0},{4,7},{5,6},{6,5},{7,4},{8,11},{9,10},{10,... | collective-permute-start | bytes 491528 | tf_op jit(solution)/shard_map/ppermute | solution.py:516
  11.7 11.4 %collective-permute-start.2 = (bf16[320,256]{1,0:T(8,128)(2,1)S(1)}, bf16[320,256]{1,0:T(8,128)(2,1)S(1)}, u32[]{:S(2)}, u32[]{:S(2)}) collective-permute-start(bf16[320,256]{1,0:T(8,128)(2,1)S(1)} %get-tuple-element.77), channel_id=1, source_target_pairs={{0,2},{1,3},{2,0},{3,1},{4,6},{5,7},{6,4},{7,5},{8,10},{9,11},{10,... | collective-permute-start | bytes 491528 | tf_op jit(solution)/shard_map/ppermute | solution.py:516
  15.6 7.5 %collective-permute-start.4 = (bf16[320,256]{1,0:T(8,128)(2,1)S(1)}, bf16[320,256]{1,0:T(8,128)(2,1)S(1)}, u32[]{:S(2)}, u32[]{:S(2)}) collective-permute-start(bf16[320,256]{1,0:T(8,128)(2,1)S(1)} %get-tuple-element.82), channel_id=1, source_target_pairs={{0,1},{1,0},{2,3},{3,2},{4,5},{5,4},{6,7},{7,6},{8,9},{9,8},{10,11... | collective-permute-start | bytes 491528 | tf_op jit(solution)/shard_map/ppermute | solution.py:516
  20.0 7.9 %collective-permute-start.6 = (bf16[320,256]{1,0:T(8,128)(2,1)S(1)}, bf16[320,256]{1,0:T(8,128)(2,1)S(1)}, u32[]{:S(2)}, u32[]{:S(2)}) collective-permute-start(bf16[320,256]{1,0:T(8,128)(2,1)S(1)} %get-tuple-element.101), channel_id=1, source_target_pairs={{3,0},{2,1},{1,2},{0,3},{7,4},{6,5},{5,6},{4,7},{11,8},{10,9},{9,1... | collective-permute-start | bytes 491528 | tf_op jit(solution)/shard_map/ppermute | solution.py:69
  28.0 11.7 %collective-permute-start.8 = (bf16[640,256]{1,0:T(8,128)(2,1)S(1)}, bf16[640,256]{1,0:T(8,128)(2,1)S(1)}, u32[]{:S(2)}, u32[]{:S(2)}) collective-permute-start(bf16[640,256]{1,0:T(8,128)(2,1)S(1)} %get-tuple-element.105), channel_id=1, source_target_pairs={{2,0},{3,1},{0,2},{1,3},{6,4},{7,5},{4,6},{5,7},{10,8},{11,9},{8,1... | collective-permute-start | bytes 983048 | tf_op jit(solution)/shard_map/ppermute | solution.py:69
  28.5 11.8 %collective-permute-start.9 = (bf16[640,256]{1,0:T(8,128)(2,1)S(1)}, bf16[640,256]{1,0:T(8,128)(2,1)S(1)}, u32[]{:S(2)}, u32[]{:S(2)}) collective-permute-start(bf16[640,256]{1,0:T(8,128)(2,1)S(1)} %get-tuple-element.106), channel_id=1, source_target_pairs={{1,0},{0,1},{3,2},{2,3},{5,4},{4,5},{7,6},{6,7},{9,8},{8,9},{11,10... | collective-permute-start | bytes 983048 | tf_op jit(solution)/shard_map/ppermute | solution.py:69
  29.9 9.8 %collective-permute-start.7 = (bf16[320,256]{1,0:T(8,128)(2,1)S(1)}, bf16[320,256]{1,0:T(8,128)(2,1)S(1)}, u32[]{:S(2)}, u32[]{:S(2)}) collective-permute-start(bf16[320,256]{1,0:T(8,128)(2,1)S(1)} %get-tuple-element.103), channel_id=1, source_target_pairs={{3,0},{2,1},{1,2},{0,3},{7,4},{6,5},{5,6},{4,7},{11,8},{10,9},{9,1... | collective-permute-start | bytes 491528 | tf_op jit(solution)/shard_map/ppermute | solution.py:69
  31.5 12.2 %all-to-all-start = ((f32[32,4,128]{2,1,0:T(4,128)}), f32[32,4,128]{2,1,0:T(4,128)S(1)}, u32[]{:S(2)}, u32[]{:S(2)}) async-start(f32[32,4,128]{2,1,0:T(4,128)} %get-tuple-element.111), calls=%async_computation | async-start | bytes 131072 | tf_op jit(solution)/shard_map/all_to_all | solution.py:563

commit v13 on v12

--- a/solution.py
+++ b/solution.py
@@ -234,12 +234,12 @@
         begin = ((0 if slot == EARLY else 4 * head) + tensor) * HEAD_DIM
         outs[slot][begin : begin + HEAD_DIM, :] = values
 
-    def scores(slot, other):
+    def scores(slot):
         part = jnp.dot(
-            k_all[block_of(other), :], qt_all[:, block_of(slot)], preferred_element_type=jnp.float32
-        )
-        s_buf[slot % 2, block_of(other), :] = part
-        return jnp.max(part, axis=0, keepdims=True)
+            k_all[...], qt_all[:, block_of(slot)], preferred_element_type=jnp.float32
+        )
+        s_buf[slot % 2] = part
+        return [jnp.max(part[block_of(other)], axis=0, keepdims=True) for other in range(slots)]
 
     def exponentials(slot, other, top):
         part = jnp.exp2(s_buf[slot % 2, block_of(other), :] - top)
@@ -261,11 +261,9 @@
         spread = grad[:HEAD_DIM].astype(jnp.float32) * mixed[HEAD_DIM : HEAD_DIM + 1]
         return grad, live(slot, spread)
 
-    def dscores(slot, other, grad):
-        part = jnp.dot(v_all[block_of(other), :], grad, preferred_element_type=jnp.float32)
-        d_buf[block_of(other), block_of(slot)] = (
-            e_buf[block_of(other), block_of(slot)] * part.astype(jnp.bfloat16)
-        )
+    def dscores(slot, grad):
+        part = jnp.dot(v_all[...], grad, preferred_element_type=jnp.float32)
+        d_buf[:, block_of(slot)] = e_buf[:, block_of(slot)] * part.astype(jnp.bfloat16)
 
     def query_part(slot):
         at = block_of(slot)
@@ -302,13 +300,12 @@
         if 0 <= slot < slots:
             offs = [off_row(slot, other) for other in range(slots)]
             top = functools.reduce(jnp.maximum, [one + off for one, off in zip(tops, offs)])
-        tops = []
-        for other in range(slots):
-            if ahead < slots:
-                tops.append(scores(ahead, other))
-            if 0 <= behind:
-                dscores(behind, other, grad)
-            if 0 <= slot < slots:
+        if ahead < slots:
+            tops = scores(ahead)
+        if 0 <= behind:
+            dscores(behind, grad)
+        if 0 <= slot < slots:
+            for other in range(slots):
                 exponentials(slot, other, top - offs[other])
         if 0 <= behind:
             dq_total = dq_total + query_part(behind)
@@ -316,6 +313,8 @@
             grad, spread = output(slot)
             dv_total = dv_total + spread
     dk_total = jnp.zeros((HEAD_DIM, tokd), jnp.float32)
+    for slot in range(slots // 2):
+        value_part(slot)
     for slot in range(slots):
         at = block_of(slot)
         dkey = lax.dot_general(
@@ -345,7 +344,7 @@
         lax.fori_loop(0, tiles.shape[0], repeat, 0, unroll=min(32, tiles.shape[0]))
         copy = pltpu.make_async_copy(tiles, sums, sem)
         copy.start()
-    for slot in range(slots):
+    for slot in range(slots // 2, slots):
         value_part(slot)
     if copy is not None:
         copy.wait()

time: 44.7 us -> 45.3 us (1.013)
  Pallas kernels: 14.7 us -> 15.3 us
    pallas_call x2, Pallas kernels: 9.1 us -> 9.73 us  [on_device(): pl.pallas_call(functools.partial(attend_kernel, slots, tuple(staged[phase...]
  transfers between devices with their start and end apart: 11 -> 11, of which waited for: 4 -> 4; matrix products, arithmetic and copies ran while one was open for 0% -> 0% of each run, Pallas kernels for 28% -> 29%
where the time goes in v13:
time: 45.3 us; the launch traced here: 45.1 us
  starting transfers between devices  20.6 us (45%)
  Pallas kernels  15.3 us (34%)
  waiting for transfers between devices  8.39 us (19%)
  between operations  0.76 us (2%)
    pallas_call x2, Pallas kernels, on_device(): pl.pallas_call(functools.partial(attend_kernel, slots, tuple(staged[phase...  9.73 us
    ppermute x4, starting transfers between devices, send_back(): lax.ppermute(result, 'tok', [(target, source) for source, target in pairs])  6.61 us
    ppermute x3, starting transfers between devices, on_device(): got[phase].append(lax.ppermute(send, 'tok', rounds[slot - 1]))  5.05 us
    ppermute x3, starting transfers between devices, on_device(): lax.ppermute(send, 'tok', pairs)  4.7 us
    ppermute x4, waiting for transfers between devices, send_back(): lax.ppermute(result, 'tok', [(target, source) for source, target in pairs])  4.51 us
    all_to_all x1, starting transfers between devices, on_device(): tiles = lax.all_to_all(total, ('dp', 'tok'), 0, 0, tiled=True)  4.27 us
    all_to_all x1, waiting for transfers between devices, on_device(): tiles = lax.all_to_all(total, ('dp', 'tok'), 0, 0, tiled=True)  2.13 us
    ppermute x3, waiting for transfers between devices, on_device(): lax.ppermute(send, 'tok', pairs)  1.75 us
  transfers between devices with their start and end apart: 11, of which 4 were waited for; matrix products, arithmetic and copies ran while one was open for 0% of the time, Pallas kernels for 29%

profile of v13, /device:TPU:0, one launch (start us, length us, event | category | flops | bytes accessed | tf_op | source)
XLA Modules:
  0.0 45.1 jit_solution(11091336092966837498)
XLA Ops:
  0.6 0.0 copy-start.2
  0.6 0.0 copy-start.3
  0.7 0.0 copy-start.4
  0.7 1.7 %pack_heads.1 = (bf16[320,256]{1,0:T(8,128)(2,1)S(1)}, bf16[320,256]{1,0:T(8,128)(2,1)S(1)}, bf16[320,256]{1,0:T(8,128)(2,1)S(1)}, bf16[320,256]{1,0:T(8,128)(2,...) custom-call(bf16[256,640]{1,0:T(8,128)(2,1)} %bitcast.8, ...), custom_call_target="tpu_custom_call" | custom-call | tf_op jit(solution)/shard_map/pack_heads/pallas_call | solution.py:455
  2.4 0.0 copy-start
  2.4 4.0 %collective-permute-start.1 = (bf16[320,256]{1,0:T(8,128)(2,1)S(1)}, bf16[320,256]{1,0:T(8,128)(2,1)S(1)}, u32[]{:S(2)}, u32[]{:S(2)}) collective-permute-start(bf16[320,256]{1,0:T(8,128)(2,1)S(1)} %get-tuple-element.74), channel_id=1, source_target_pairs={{0,3},{1,2},{2,1},{3,0},{4,7},{5,6},{6,5},{7,4},{8,11},{9,10},{10,... | collective-permute-start | bytes 491528 | tf_op jit(solution)/shard_map/ppermute | solution.py:470
  6.4 0.0 copy-start.1
  6.4 0.4 collective-permute-start.3
  6.8 0.2 collective-permute-start.5
  7.1 0.0 copy-done.2
  7.1 0.0 copy-done.3
  7.1 0.0 copy-done.4
  7.1 0.0 copy-done
  7.1 0.0 copy-done.1
  7.1 1.3 %rotary_tables.1 = (f32[40,1024]{1,0:T(8,128)S(1)}, f32[40,1024]{1,0:T(8,128)S(1)}, f32[24,256]{1,0:T(8,128)S(1)}, f32[160,128]{1,0:T(8,128)S(1)}) custom-call(s32[1,4]{1,0:T(1,128)S(1)} %copy-done.1, s32[1,4]{1,0:T(1,128)S(1)} %copy-done.2, s32[4,8]{1,0:T(4,128)S(1)} %copy-done.4, f32[40,128]{1,0:T(8,128)S(1)} %copy-done.3, bf16[3,640]{1,0:T(4,128)(2,1)S(1)} %copy-done), custom_call_target="tpu_custom_call" | custom-call | flops 26214400 | tf_op jit(solution)/shard_map/rotary_tables/pallas_call | solution.py:474
  8.4 0.2 stage_slot.3
  8.6 2.9 %collective-permute-start = (bf16[320,256]{1,0:T(8,128)(2,1)S(1)}, bf16[320,256]{1,0:T(8,128)(2,1)S(1)}, u32[]{:S(2)}, u32[]{:S(2)}) collective-permute-start(bf16[320,256]{1,0:T(8,128)(2,1)S(1)} %get-tuple-element.72), channel_id=1, source_target_pairs={{0,3},{1,2},{2,1},{3,0},{4,7},{5,6},{6,5},{7,4},{8,11},{9,10},{10,... | collective-permute-start | bytes 491528 | tf_op jit(solution)/shard_map/ppermute | solution.py:515
  11.5 0.0 collective-permute-done.1.refs_0_.refs_1_
  11.5 0.2 stage_slot.4
  11.7 2.0 %collective-permute-start.2 = (bf16[320,256]{1,0:T(8,128)(2,1)S(1)}, bf16[320,256]{1,0:T(8,128)(2,1)S(1)}, u32[]{:S(2)}, u32[]{:S(2)}) collective-permute-start(bf16[320,256]{1,0:T(8,128)(2,1)S(1)} %get-tuple-element.77), channel_id=1, source_target_pairs={{0,2},{1,3},{2,0},{3,1},{4,6},{5,7},{6,4},{7,5},{8,10},{9,11},{10,... | collective-permute-start | bytes 491528 | tf_op jit(solution)/shard_map/ppermute | solution.py:515
  13.7 1.7 %collective-permute-done.3.refs_0_.refs_2_ = bf16[320,256]{1,0:T(8,128)(2,1)S(1)} collective-permute-done((bf16[320,256]{1,0:T(8,128)(2,1)S(1)}, bf16[320,256]{1,0:T(8,128)(2,1)S(1)}, u32[]{:S(2)}, u32[]{:S(2)}) %collective-permute-start.3) | collective-permute-done | bytes 163872 | tf_op jit(solution)/shard_map/ppermute | solution.py:470
  15.5 0.2 stage_slot.5
  15.6 0.1 collective-permute-start.4
  15.8 0.0 collective-permute-done.5.refs_3_
  15.8 4.5 %attend_head.2 = (bf16[640,256]{1,0:T(8,128)(2,1)S(1)}, bf16[320,256]{1,0:T(8,128)(2,1)S(1)}, bf16[640,256]{1,0:T(8,128)(2,1)S(1)}, bf16[640,256]{1,0:T(8,128)(2,1)S(1)}, f32[8,128]{1,0:T(8,128)S(1)}) custom-call(f32[40,1024]{1,0:T(8,128)S(1)} %get-tuple-element.61.cosv, f32[40,1024]{1,0:T(8,128)S(1)} %get-tuple-element.62.sinv, ...), custom_call_target="tpu_custom_call" | custom-call | flops 3221225472 | tf_op jit(solution)/shard_map/attend_head/pallas_call | solution.py:530
  20.3 3.1 %collective-permute-start.6 = (bf16[320,256]{1,0:T(8,128)(2,1)S(1)}, bf16[320,256]{1,0:T(8,128)(2,1)S(1)}, u32[]{:S(2)}, u32[]{:S(2)}) collective-permute-start(bf16[320,256]{1,0:T(8,128)(2,1)S(1)} %get-tuple-element.101), channel_id=1, source_target_pairs={{3,0},{2,1},{1,2},{0,3},{7,4},{6,5},{5,6},{4,7},{11,8},{10,9},{9,1... | collective-permute-start | bytes 491528 | tf_op jit(solution)/shard_map/ppermute | solution.py:69
  23.4 0.0 collective-permute-done.refs_1_
  23.4 0.0 collective-permute-done.2.refs_2_
  23.4 0.0 collective-permute-done.4.refs_3_
  23.4 5.2 %attend_head.3 = (bf16[640,256]{1,0:T(8,128)(2,1)S(1)}, bf16[320,256]{1,0:T(8,128)(2,1)S(1)}, bf16[640,256]{1,0:T(8,128)(2,1)S(1)}, bf16[640,256]{1,0:T(8,128)(2,1)S(1)}, f32[32,4,128]{2,1,0:T(4,128)}) custom-call(f32[40,1024]{1,0:T(8,128)S(1)} %get-tuple-element.61.cosv, f32[40,1024]{1,0:T(8,128)S(1)} %get-tuple-element.62.sinv, ...), custom_call_target="tpu_custom_call" | custom-call | flops 3221225472 | tf_op jit(solution)/shard_map/attend_head/pallas_call | solution.py:530
  28.6 0.0 collective-permute-done.6.refs_0_
  28.6 0.5 %collective-permute-start.8 = (bf16[640,256]{1,0:T(8,128)(2,1)S(1)}, bf16[640,256]{1,0:T(8,128)(2,1)S(1)}, u32[]{:S(2)}, u32[]{:S(2)}) collective-permute-start(bf16[640,256]{1,0:T(8,128)(2,1)S(1)} %get-tuple-element.105), channel_id=1, source_target_pairs={{2,0},{3,1},{0,2},{1,3},{6,4},{7,5},{4,6},{5,7},{10,8},{11,9},{8,1... | collective-permute-start | bytes 983048 | tf_op jit(solution)/shard_map/ppermute | solution.py:69
  29.1 1.1 %collective-permute-start.9 = (bf16[640,256]{1,0:T(8,128)(2,1)S(1)}, bf16[640,256]{1,0:T(8,128)(2,1)S(1)}, u32[]{:S(2)}, u32[]{:S(2)}) collective-permute-start(bf16[640,256]{1,0:T(8,128)(2,1)S(1)} %get-tuple-element.106), channel_id=1, source_target_pairs={{1,0},{0,1},{3,2},{2,3},{5,4},{4,5},{7,6},{6,7},{9,8},{8,9},{11,10... | collective-permute-start | bytes 983048 | tf_op jit(solution)/shard_map/ppermute | solution.py:69
  30.1 2.0 %collective-permute-start.7 = (bf16[320,256]{1,0:T(8,128)(2,1)S(1)}, bf16[320,256]{1,0:T(8,128)(2,1)S(1)}, u32[]{:S(2)}, u32[]{:S(2)}) collective-permute-start(bf16[320,256]{1,0:T(8,128)(2,1)S(1)} %get-tuple-element.103), channel_id=1, source_target_pairs={{3,0},{2,1},{1,2},{0,3},{7,4},{6,5},{5,6},{4,7},{11,8},{10,9},{9,1... | collective-permute-start | bytes 491528 | tf_op jit(solution)/shard_map/ppermute | solution.py:69
  32.2 4.3 %all-to-all-start = ((f32[32,4,128]{2,1,0:T(4,128)}), f32[32,4,128]{2,1,0:T(4,128)S(1)}, u32[]{:S(2)}, u32[]{:S(2)}) async-start(f32[32,4,128]{2,1,0:T(4,128)} %get-tuple-element.111), calls=%async_computation | async-start | bytes 131072 | tf_op jit(solution)/shard_map/all_to_all | solution.py:562
  36.4 3.7 %collective-permute-done.7.refs_1_ = bf16[320,256]{1,0:T(8,128)(2,1)S(1)} collective-permute-done((bf16[320,256]{1,0:T(8,128)(2,1)S(1)}, bf16[320,256]{1,0:T(8,128)(2,1)S(1)}, u32[]{:S(2)}, u32[]{:S(2)}) %collective-permute-start.7) | collective-permute-done | bytes 163872 | tf_op jit(solution)/shard_map/ppermute | solution.py:69
  40.1 0.0 collective-permute-done.8.refs_3_
  40.1 0.9 %collective-permute-done.9.refs_4_ = bf16[640,256]{1,0:T(8,128)(2,1)S(1)} collective-permute-done((bf16[640,256]{1,0:T(8,128)(2,1)S(1)}, bf16[640,256]{1,0:T(8,128)(2,1)S(1)}, u32[]{:S(2)}, u32[]{:S(2)}) %collective-permute-start.9) | collective-permute-done | bytes 327712 | tf_op jit(solution)/shard_map/ppermute | solution.py:69
  40.9 1.3 %unpack_heads.1 = (bf16[256,640]{1,0:T(8,128)(2,1)}, bf16[256,640]{1,0:T(8,128)(2,1)}, bf16[256,640]{1,0:T(8,128)(2,1)}, bf16[256,640]{1,0:T(8,128)(2,1)}) custom-call(bf16[320,256]{1,0:T(8,128)(2,1)S(1)} %collective-permute-done.6.refs_0_, bf16[320,256]{1,0:T(8,128)(2,1)S(1)} %collective-permute-done.7.refs_1_, ...), custom_call_target="tpu_custom_call" | custom-call | flops 20000000000 | tf_op jit(solution)/shard_map/unpack_heads/pallas_call | solution.py:565
  42.3 2.1 %all-to-all-done.tiles = f32[32,4,128]{2,1,0:T(4,128)S(1)} async-done(((f32[32,4,128]{2,1,0:T(4,128)}), f32[32,4,128]{2,1,0:T(4,128)S(1)}, u32[]{:S(2)}, u32[]{:S(2)}) %all-to-all-start) | async-done | bytes 65568 | tf_op jit(solution)/shard_map/all_to_all | solution.py:562
  44.4 0.7 %bias_sums.1 = f32[3,640]{1,0:T(4,128)} custom-call(f32[32,4,128]{2,1,0:T(4,128)S(1)} %all-to-all-done.tiles), custom_call_target="tpu_custom_call" | custom-call | tf_op jit(solution)/shard_map/bias_sums/pallas_call | solution.py:580
Async XLA Ops:
  0.6 6.4 %copy-start.2 = (s32[1,4]{1,0:T(1,128)S(1)}, s32[1,4]{1,0:T(1,128)}, u32[]{:S(2)}) copy-start(s32[1,4]{1,0:T(1,128)} %widths.1) | copy-start | bytes 52
  0.6 6.4 %copy-start.3 = (f32[40,128]{1,0:T(8,128)S(1)}, f32[40,128]{1,0:T(8,128)}, u32[]{:S(2)}) copy-start(f32[40,128]{1,0:T(8,128)} %constant.5.clone.inverse) | copy-start | bytes 61444
  0.7 6.4 %copy-start.4 = (s32[4,8]{1,0:T(4,128)S(1)}, s32[4,8]{1,0:T(4,128)}, u32[]{:S(2)}) copy-start(s32[4,8]{1,0:T(4,128)} %constant.4.clone.table) | copy-start | bytes 388
  2.4 4.7 %copy-start = (bf16[3,640]{1,0:T(4,128)(2,1)S(1)}, bf16[3,640]{1,0:T(4,128)(2,1)}, u32[]{:S(2)}) copy-start(bf16[3,640]{1,0:T(4,128)(2,1)} %bias.1) | copy-start | bytes 11524
  2.4 9.1 %collective-permute-start.1 = (bf16[320,256]{1,0:T(8,128)(2,1)S(1)}, bf16[320,256]{1,0:T(8,128)(2,1)S(1)}, u32[]{:S(2)}, u32[]{:S(2)}) collective-permute-start(bf16[320,256]{1,0:T(8,128)(2,1)S(1)} %get-tuple-element.74), channel_id=1, source_target_pairs={{0,3},{1,2},{2,1},{3,0},{4,7},{5,6},{6,5},{7,4},{8,11},{9,10},{10,... | collective-permute-start | bytes 491528 | tf_op jit(solution)/shard_map/ppermute | solution.py:470
  6.4 0.7 %copy-start.1 = (s32[1,4]{1,0:T(1,128)S(1)}, s32[1,4]{1,0:T(1,128)}, u32[]{:S(2)}) copy-start(s32[1,4]{1,0:T(1,128)} %lengths.1) | copy-start | bytes 52
  6.4 9.0 %collective-permute-start.3 = (bf16[320,256]{1,0:T(8,128)(2,1)S(1)}, bf16[320,256]{1,0:T(8,128)(2,1)S(1)}, u32[]{:S(2)}, u32[]{:S(2)}) collective-permute-start(bf16[320,256]{1,0:T(8,128)(2,1)S(1)} %get-tuple-element.79), channel_id=1, source_target_pairs={{0,2},{1,3},{2,0},{3,1},{4,6},{5,7},{6,4},{7,5},{8,10},{9,11},{10,... | collective-permute-start | bytes 491528 | tf_op jit(solution)/shard_map/ppermute | solution.py:470
  6.8 8.9 %collective-permute-start.5 = (bf16[320,256]{1,0:T(8,128)(2,1)S(1)}, bf16[320,256]{1,0:T(8,128)(2,1)S(1)}, u32[]{:S(2)}, u32[]{:S(2)}) collective-permute-start(bf16[320,256]{1,0:T(8,128)(2,1)S(1)} %get-tuple-element.85), channel_id=1, source_target_pairs={{0,1},{1,0},{2,3},{3,2},{4,5},{5,4},{6,7},{7,6},{8,9},{9,8},{10,11... | collective-permute-start | bytes 491528 | tf_op jit(solution)/shard_map/ppermute | solution.py:470
  8.6 14.8 %collective-permute-start = (bf16[320,256]{1,0:T(8,128)(2,1)S(1)}, bf16[320,256]{1,0:T(8,128)(2,1)S(1)}, u32[]{:S(2)}, u32[]{:S(2)}) collective-permute-start(bf16[320,256]{1,0:T(8,128)(2,1)S(1)} %get-tuple-element.72), channel_id=1, source_target_pairs={{0,3},{1,2},{2,1},{3,0},{4,7},{5,6},{6,5},{7,4},{8,11},{9,10},{10,... | collective-permute-start | bytes 491528 | tf_op jit(solution)/shard_map/ppermute | solution.py:515
  11.7 11.7 %collective-permute-start.2 = (bf16[320,256]{1,0:T(8,128)(2,1)S(1)}, bf16[320,256]{1,0:T(8,128)(2,1)S(1)}, u32[]{:S(2)}, u32[]{:S(2)}) collective-permute-start(bf16[320,256]{1,0:T(8,128)(2,1)S(1)} %get-tuple-element.77), channel_id=1, source_target_pairs={{0,2},{1,3},{2,0},{3,1},{4,6},{5,7},{6,4},{7,5},{8,10},{9,11},{10,... | collective-permute-start | bytes 491528 | tf_op jit(solution)/shard_map/ppermute | solution.py:515
  15.6 7.7 %collective-permute-start.4 = (bf16[320,256]{1,0:T(8,128)(2,1)S(1)}, bf16[320,256]{1,0:T(8,128)(2,1)S(1)}, u32[]{:S(2)}, u32[]{:S(2)}) collective-permute-start(bf16[320,256]{1,0:T(8,128)(2,1)S(1)} %get-tuple-element.82), channel_id=1, source_target_pairs={{0,1},{1,0},{2,3},{3,2},{4,5},{5,4},{6,7},{7,6},{8,9},{9,8},{10,11... | collective-permute-start | bytes 491528 | tf_op jit(solution)/shard_map/ppermute | solution.py:515
  20.3 8.3 %collective-permute-start.6 = (bf16[320,256]{1,0:T(8,128)(2,1)S(1)}, bf16[320,256]{1,0:T(8,128)(2,1)S(1)}, u32[]{:S(2)}, u32[]{:S(2)}) collective-permute-start(bf16[320,256]{1,0:T(8,128)(2,1)S(1)} %get-tuple-element.101), channel_id=1, source_target_pairs={{3,0},{2,1},{1,2},{0,3},{7,4},{6,5},{5,6},{4,7},{11,8},{10,9},{9,1... | collective-permute-start | bytes 491528 | tf_op jit(solution)/shard_map/ppermute | solution.py:69
  28.6 11.5 %collective-permute-start.8 = (bf16[640,256]{1,0:T(8,128)(2,1)S(1)}, bf16[640,256]{1,0:T(8,128)(2,1)S(1)}, u32[]{:S(2)}, u32[]{:S(2)}) collective-permute-start(bf16[640,256]{1,0:T(8,128)(2,1)S(1)} %get-tuple-element.105), channel_id=1, source_target_pairs={{2,0},{3,1},{0,2},{1,3},{6,4},{7,5},{4,6},{5,7},{10,8},{11,9},{8,1... | collective-permute-start | bytes 983048 | tf_op jit(solution)/shard_map/ppermute | solution.py:69
  29.1 11.8 %collective-permute-start.9 = (bf16[640,256]{1,0:T(8,128)(2,1)S(1)}, bf16[640,256]{1,0:T(8,128)(2,1)S(1)}, u32[]{:S(2)}, u32[]{:S(2)}) collective-permute-start(bf16[640,256]{1,0:T(8,128)(2,1)S(1)} %get-tuple-element.106), channel_id=1, source_target_pairs={{1,0},{0,1},{3,2},{2,3},{5,4},{4,5},{7,6},{6,7},{9,8},{8,9},{11,10... | collective-permute-start | bytes 983048 | tf_op jit(solution)/shard_map/ppermute | solution.py:69
  30.1 9.9 %collective-permute-start.7 = (bf16[320,256]{1,0:T(8,128)(2,1)S(1)}, bf16[320,256]{1,0:T(8,128)(2,1)S(1)}, u32[]{:S(2)}, u32[]{:S(2)}) collective-permute-start(bf16[320,256]{1,0:T(8,128)(2,1)S(1)} %get-tuple-element.103), channel_id=1, source_target_pairs={{3,0},{2,1},{1,2},{0,3},{7,4},{6,5},{5,6},{4,7},{11,8},{10,9},{9,1... | collective-permute-start | bytes 491528 | tf_op jit(solution)/shard_map/ppermute | solution.py:69
  32.2 12.2 %all-to-all-start = ((f32[32,4,128]{2,1,0:T(4,128)}), f32[32,4,128]{2,1,0:T(4,128)S(1)}, u32[]{:S(2)}, u32[]{:S(2)}) async-start(f32[32,4,128]{2,1,0:T(4,128)} %get-tuple-element.111), calls=%async_computation | async-start | bytes 131072 | tf_op jit(solution)/shard_map/all_to_all | solution.py:562

commit v14 on v12

--- a/solution.py
+++ b/solution.py
@@ -19,6 +19,7 @@
 LANES = 128
 USED = HEAD_DIM + 16
 HALF = HEAD_DIM // 2
+PIECES = 2
 PACK_KIB = 52 * 1024 + 600
 UNPACK_FLOPS = 20_000_000_000
 
@@ -234,16 +235,23 @@
         begin = ((0 if slot == EARLY else 4 * head) + tensor) * HEAD_DIM
         outs[slot][begin : begin + HEAD_DIM, :] = values
 
-    def scores(slot, other):
+    def pieces_of(other):
+        step = tokd // PIECES
+        return [
+            slice(other * tokd + number * step, other * tokd + (number + 1) * step)
+            for number in range(PIECES)
+        ]
+
+    def scores(slot, keys):
         part = jnp.dot(
-            k_all[block_of(other), :], qt_all[:, block_of(slot)], preferred_element_type=jnp.float32
-        )
-        s_buf[slot % 2, block_of(other), :] = part
+            k_all[keys, :], qt_all[:, block_of(slot)], preferred_element_type=jnp.float32
+        )
+        s_buf[slot % 2, keys, :] = part
         return jnp.max(part, axis=0, keepdims=True)
 
-    def exponentials(slot, other, top):
-        part = jnp.exp2(s_buf[slot % 2, block_of(other), :] - top)
-        e_buf[block_of(other), block_of(slot)] = part.astype(jnp.bfloat16)
+    def exponentials(slot, keys, top):
+        part = jnp.exp2(s_buf[slot % 2, keys, :] - top)
+        e_buf[keys, block_of(slot)] = part.astype(jnp.bfloat16)
 
     def output(slot):
         mixed = jnp.dot(
@@ -261,11 +269,9 @@
         spread = grad[:HEAD_DIM].astype(jnp.float32) * mixed[HEAD_DIM : HEAD_DIM + 1]
         return grad, live(slot, spread)
 
-    def dscores(slot, other, grad):
-        part = jnp.dot(v_all[block_of(other), :], grad, preferred_element_type=jnp.float32)
-        d_buf[block_of(other), block_of(slot)] = (
-            e_buf[block_of(other), block_of(slot)] * part.astype(jnp.bfloat16)
-        )
+    def dscores(slot, keys, grad):
+        part = jnp.dot(v_all[keys, :], grad, preferred_element_type=jnp.float32)
+        d_buf[keys, block_of(slot)] = e_buf[keys, block_of(slot)] * part.astype(jnp.bfloat16)
 
     def query_part(slot):
         at = block_of(slot)
@@ -304,12 +310,16 @@
             top = functools.reduce(jnp.maximum, [one + off for one, off in zip(tops, offs)])
         tops = []
         for other in range(slots):
-            if ahead < slots:
-                tops.append(scores(ahead, other))
-            if 0 <= behind:
-                dscores(behind, other, grad)
-            if 0 <= slot < slots:
-                exponentials(slot, other, top - offs[other])
+            found = []
+            for keys in pieces_of(other):
+                if ahead < slots:
+                    found.append(scores(ahead, keys))
+                if 0 <= behind:
+                    dscores(behind, keys, grad)
+                if 0 <= slot < slots:
+                    exponentials(slot, keys, top - offs[other])
+            if found:
+                tops.append(functools.reduce(jnp.maximum, found))
         if 0 <= behind:
             dq_total = dq_total + query_part(behind)
         if 0 <= slot < slots:

time: 44.7 us -> 44.5 us (level)
  transfers between devices with their start and end apart: 11 -> 11, of which waited for: 4 -> 4; matrix products, arithmetic and copies ran while one was open for 0% -> 0% of each run, Pallas kernels for 28% -> 27%
where the time goes in v14:
time: 44.5 us; the launch traced here: 44.3 us
  starting transfers between devices  21.1 us (47%)
  Pallas kernels  14.5 us (33%)
  waiting for transfers between devices  7.88 us (18%)
  between operations  0.76 us (2%)
    pallas_call x2, Pallas kernels, on_device(): pl.pallas_call(functools.partial(attend_kernel, slots, tuple(staged[phase...  8.93 us
    ppermute x4, starting transfers between devices, send_back(): lax.ppermute(result, 'tok', [(target, source) for source, target in pairs])  6.6 us
    ppermute x3, starting transfers between devices, on_device(): got[phase].append(lax.ppermute(send, 'tok', rounds[slot - 1]))  5.05 us
    all_to_all x1, starting transfers between devices, on_device(): tiles = lax.all_to_all(total, ('dp', 'tok'), 0, 0, tiled=True)  4.77 us
    ppermute x3, starting transfers between devices, on_device(): lax.ppermute(send, 'tok', pairs)  4.7 us
    ppermute x4, waiting for transfers between devices, send_back(): lax.ppermute(result, 'tok', [(target, source) for source, target in pairs])  3.87 us
    all_to_all x1, waiting for transfers between devices, on_device(): tiles = lax.all_to_all(total, ('dp', 'tok'), 0, 0, tiled=True)  2.26 us
    ppermute x3, waiting for transfers between devices, on_device(): lax.ppermute(send, 'tok', pairs)  1.75 us
  transfers between devices with their start and end apart: 11, of which 4 were waited for; matrix products, arithmetic and copies ran while one was open for 0% of the time, Pallas kernels for 27%

profile of v14, /device:TPU:0, one launch (start us, length us, event | category | flops | bytes accessed | tf_op | source)
XLA Modules:
  0.0 44.3 jit_solution(10838312860417815210)
XLA Ops:
  0.6 0.0 copy-start.2
  0.6 0.0 copy-start.3
  0.7 0.0 copy-start.4
  0.7 1.7 %pack_heads.1 = (bf16[320,256]{1,0:T(8,128)(2,1)S(1)}, bf16[320,256]{1,0:T(8,128)(2,1)S(1)}, bf16[320,256]{1,0:T(8,128)(2,1)S(1)}, bf16[320,256]{1,0:T(8,128)(2,...) custom-call(bf16[256,640]{1,0:T(8,128)(2,1)} %bitcast.8, ...), custom_call_target="tpu_custom_call" | custom-call | tf_op jit(solution)/shard_map/pack_heads/pallas_call | solution.py:466
  2.4 0.0 copy-start
  2.4 4.0 %collective-permute-start.1 = (bf16[320,256]{1,0:T(8,128)(2,1)S(1)}, bf16[320,256]{1,0:T(8,128)(2,1)S(1)}, u32[]{:S(2)}, u32[]{:S(2)}) collective-permute-start(bf16[320,256]{1,0:T(8,128)(2,1)S(1)} %get-tuple-element.74), channel_id=1, source_target_pairs={{0,3},{1,2},{2,1},{3,0},{4,7},{5,6},{6,5},{7,4},{8,11},{9,10},{10,... | collective-permute-start | bytes 491528 | tf_op jit(solution)/shard_map/ppermute | solution.py:481
  6.4 0.0 copy-start.1
  6.4 0.4 collective-permute-start.3
  6.8 0.2 collective-permute-start.5
  7.1 0.0 copy-done.2
  7.1 0.0 copy-done.3
  7.1 0.0 copy-done.4
  7.1 0.0 copy-done
  7.1 0.0 copy-done.1
  7.1 1.3 %rotary_tables.1 = (f32[40,1024]{1,0:T(8,128)S(1)}, f32[40,1024]{1,0:T(8,128)S(1)}, f32[24,256]{1,0:T(8,128)S(1)}, f32[160,128]{1,0:T(8,128)S(1)}) custom-call(s32[1,4]{1,0:T(1,128)S(1)} %copy-done.1, s32[1,4]{1,0:T(1,128)S(1)} %copy-done.2, s32[4,8]{1,0:T(4,128)S(1)} %copy-done.4, f32[40,128]{1,0:T(8,128)S(1)} %copy-done.3, bf16[3,640]{1,0:T(4,128)(2,1)S(1)} %copy-done), custom_call_target="tpu_custom_call" | custom-call | flops 26214400 | tf_op jit(solution)/shard_map/rotary_tables/pallas_call | solution.py:485
  8.4 0.2 stage_slot.3
  8.6 2.9 %collective-permute-start = (bf16[320,256]{1,0:T(8,128)(2,1)S(1)}, bf16[320,256]{1,0:T(8,128)(2,1)S(1)}, u32[]{:S(2)}, u32[]{:S(2)}) collective-permute-start(bf16[320,256]{1,0:T(8,128)(2,1)S(1)} %get-tuple-element.72), channel_id=1, source_target_pairs={{0,3},{1,2},{2,1},{3,0},{4,7},{5,6},{6,5},{7,4},{8,11},{9,10},{10,... | collective-permute-start | bytes 491528 | tf_op jit(solution)/shard_map/ppermute | solution.py:526
  11.5 0.0 collective-permute-done.1.refs_0_.refs_1_
  11.5 0.2 stage_slot.4
  11.7 2.0 %collective-permute-start.2 = (bf16[320,256]{1,0:T(8,128)(2,1)S(1)}, bf16[320,256]{1,0:T(8,128)(2,1)S(1)}, u32[]{:S(2)}, u32[]{:S(2)}) collective-permute-start(bf16[320,256]{1,0:T(8,128)(2,1)S(1)} %get-tuple-element.77), channel_id=1, source_target_pairs={{0,2},{1,3},{2,0},{3,1},{4,6},{5,7},{6,4},{7,5},{8,10},{9,11},{10,... | collective-permute-start | bytes 491528 | tf_op jit(solution)/shard_map/ppermute | solution.py:526
  13.7 1.7 %collective-permute-done.3.refs_0_.refs_2_ = bf16[320,256]{1,0:T(8,128)(2,1)S(1)} collective-permute-done((bf16[320,256]{1,0:T(8,128)(2,1)S(1)}, bf16[320,256]{1,0:T(8,128)(2,1)S(1)}, u32[]{:S(2)}, u32[]{:S(2)}) %collective-permute-start.3) | collective-permute-done | bytes 163872 | tf_op jit(solution)/shard_map/ppermute | solution.py:481
  15.5 0.2 stage_slot.5
  15.6 0.1 collective-permute-start.4
  15.8 0.0 collective-permute-done.5.refs_3_
  15.8 4.2 %attend_head.2 = (bf16[640,256]{1,0:T(8,128)(2,1)S(1)}, bf16[320,256]{1,0:T(8,128)(2,1)S(1)}, bf16[640,256]{1,0:T(8,128)(2,1)S(1)}, bf16[640,256]{1,0:T(8,128)(2,1)S(1)}, f32[8,128]{1,0:T(8,128)S(1)}) custom-call(f32[40,1024]{1,0:T(8,128)S(1)} %get-tuple-element.61.cosv, f32[40,1024]{1,0:T(8,128)S(1)} %get-tuple-element.62.sinv, ...), custom_call_target="tpu_custom_call" | custom-call | flops 3221225472 | tf_op jit(solution)/shard_map/attend_head/pallas_call | solution.py:541
  20.0 3.0 %collective-permute-start.6 = (bf16[320,256]{1,0:T(8,128)(2,1)S(1)}, bf16[320,256]{1,0:T(8,128)(2,1)S(1)}, u32[]{:S(2)}, u32[]{:S(2)}) collective-permute-start(bf16[320,256]{1,0:T(8,128)(2,1)S(1)} %get-tuple-element.101), channel_id=1, source_target_pairs={{3,0},{2,1},{1,2},{0,3},{7,4},{6,5},{5,6},{4,7},{11,8},{10,9},{9,1... | collective-permute-start | bytes 491528 | tf_op jit(solution)/shard_map/ppermute | solution.py:70
  23.1 0.0 collective-permute-done.refs_1_
  23.1 0.0 collective-permute-done.2.refs_2_
  23.1 0.0 collective-permute-done.4.refs_3_
  23.1 4.7 %attend_head.3 = (bf16[640,256]{1,0:T(8,128)(2,1)S(1)}, bf16[320,256]{1,0:T(8,128)(2,1)S(1)}, bf16[640,256]{1,0:T(8,128)(2,1)S(1)}, bf16[640,256]{1,0:T(8,128)(2,1)S(1)}, f32[32,4,128]{2,1,0:T(4,128)}) custom-call(f32[40,1024]{1,0:T(8,128)S(1)} %get-tuple-element.61.cosv, f32[40,1024]{1,0:T(8,128)S(1)} %get-tuple-element.62.sinv, ...), custom_call_target="tpu_custom_call" | custom-call | flops 3221225472 | tf_op jit(solution)/shard_map/attend_head/pallas_call | solution.py:541
  27.8 0.0 collective-permute-done.6.refs_0_
  27.8 0.5 %collective-permute-start.8 = (bf16[640,256]{1,0:T(8,128)(2,1)S(1)}, bf16[640,256]{1,0:T(8,128)(2,1)S(1)}, u32[]{:S(2)}, u32[]{:S(2)}) collective-permute-start(bf16[640,256]{1,0:T(8,128)(2,1)S(1)} %get-tuple-element.105), channel_id=1, source_target_pairs={{2,0},{3,1},{0,2},{1,3},{6,4},{7,5},{4,6},{5,7},{10,8},{11,9},{8,1... | collective-permute-start | bytes 983048 | tf_op jit(solution)/shard_map/ppermute | solution.py:70
  28.3 1.5 %collective-permute-start.9 = (bf16[640,256]{1,0:T(8,128)(2,1)S(1)}, bf16[640,256]{1,0:T(8,128)(2,1)S(1)}, u32[]{:S(2)}, u32[]{:S(2)}) collective-permute-start(bf16[640,256]{1,0:T(8,128)(2,1)S(1)} %get-tuple-element.106), channel_id=1, source_target_pairs={{1,0},{0,1},{3,2},{2,3},{5,4},{4,5},{7,6},{6,7},{9,8},{8,9},{11,10... | collective-permute-start | bytes 983048 | tf_op jit(solution)/shard_map/ppermute | solution.py:70
  29.8 1.5 %collective-permute-start.7 = (bf16[320,256]{1,0:T(8,128)(2,1)S(1)}, bf16[320,256]{1,0:T(8,128)(2,1)S(1)}, u32[]{:S(2)}, u32[]{:S(2)}) collective-permute-start(bf16[320,256]{1,0:T(8,128)(2,1)S(1)} %get-tuple-element.103), channel_id=1, source_target_pairs={{3,0},{2,1},{1,2},{0,3},{7,4},{6,5},{5,6},{4,7},{11,8},{10,9},{9,1... | collective-permute-start | bytes 491528 | tf_op jit(solution)/shard_map/ppermute | solution.py:70
  31.3 4.8 %all-to-all-start = ((f32[32,4,128]{2,1,0:T(4,128)}), f32[32,4,128]{2,1,0:T(4,128)S(1)}, u32[]{:S(2)}, u32[]{:S(2)}) async-start(f32[32,4,128]{2,1,0:T(4,128)} %get-tuple-element.111), calls=%async_computation | async-start | bytes 131072 | tf_op jit(solution)/shard_map/all_to_all | solution.py:573
  36.1 3.5 %collective-permute-done.7.refs_1_ = bf16[320,256]{1,0:T(8,128)(2,1)S(1)} collective-permute-done((bf16[320,256]{1,0:T(8,128)(2,1)S(1)}, bf16[320,256]{1,0:T(8,128)(2,1)S(1)}, u32[]{:S(2)}, u32[]{:S(2)}) %collective-permute-start.7) | collective-permute-done | bytes 163872 | tf_op jit(solution)/shard_map/ppermute | solution.py:70
  39.6 0.0 collective-permute-done.8.refs_3_
  39.6 0.4 collective-permute-done.9.refs_4_
  40.0 1.3 %unpack_heads.1 = (bf16[256,640]{1,0:T(8,128)(2,1)}, bf16[256,640]{1,0:T(8,128)(2,1)}, bf16[256,640]{1,0:T(8,128)(2,1)}, bf16[256,640]{1,0:T(8,128)(2,1)}) custom-call(bf16[320,256]{1,0:T(8,128)(2,1)S(1)} %collective-permute-done.6.refs_0_, bf16[320,256]{1,0:T(8,128)(2,1)S(1)} %collective-permute-done.7.refs_1_, ...), custom_call_target="tpu_custom_call" | custom-call | flops 20000000000 | tf_op jit(solution)/shard_map/unpack_heads/pallas_call | solution.py:576
  41.3 2.3 %all-to-all-done.tiles = f32[32,4,128]{2,1,0:T(4,128)S(1)} async-done(((f32[32,4,128]{2,1,0:T(4,128)}), f32[32,4,128]{2,1,0:T(4,128)S(1)}, u32[]{:S(2)}, u32[]{:S(2)}) %all-to-all-start) | async-done | bytes 65568 | tf_op jit(solution)/shard_map/all_to_all | solution.py:573
  43.6 0.7 %bias_sums.1 = f32[3,640]{1,0:T(4,128)} custom-call(f32[32,4,128]{2,1,0:T(4,128)S(1)} %all-to-all-done.tiles), custom_call_target="tpu_custom_call" | custom-call | tf_op jit(solution)/shard_map/bias_sums/pallas_call | solution.py:591
Async XLA Ops:
  0.6 6.4 %copy-start.2 = (s32[1,4]{1,0:T(1,128)S(1)}, s32[1,4]{1,0:T(1,128)}, u32[]{:S(2)}) copy-start(s32[1,4]{1,0:T(1,128)} %widths.1) | copy-start | bytes 52
  0.6 6.4 %copy-start.3 = (f32[40,128]{1,0:T(8,128)S(1)}, f32[40,128]{1,0:T(8,128)}, u32[]{:S(2)}) copy-start(f32[40,128]{1,0:T(8,128)} %constant.5.clone.inverse) | copy-start | bytes 61444
  0.7 6.4 %copy-start.4 = (s32[4,8]{1,0:T(4,128)S(1)}, s32[4,8]{1,0:T(4,128)}, u32[]{:S(2)}) copy-start(s32[4,8]{1,0:T(4,128)} %constant.4.clone.table) | copy-start | bytes 388
  2.4 4.7 %copy-start = (bf16[3,640]{1,0:T(4,128)(2,1)S(1)}, bf16[3,640]{1,0:T(4,128)(2,1)}, u32[]{:S(2)}) copy-start(bf16[3,640]{1,0:T(4,128)(2,1)} %bias.1) | copy-start | bytes 11524
  2.4 9.1 %collective-permute-start.1 = (bf16[320,256]{1,0:T(8,128)(2,1)S(1)}, bf16[320,256]{1,0:T(8,128)(2,1)S(1)}, u32[]{:S(2)}, u32[]{:S(2)}) collective-permute-start(bf16[320,256]{1,0:T(8,128)(2,1)S(1)} %get-tuple-element.74), channel_id=1, source_target_pairs={{0,3},{1,2},{2,1},{3,0},{4,7},{5,6},{6,5},{7,4},{8,11},{9,10},{10,... | collective-permute-start | bytes 491528 | tf_op jit(solution)/shard_map/ppermute | solution.py:481
  6.4 0.7 %copy-start.1 = (s32[1,4]{1,0:T(1,128)S(1)}, s32[1,4]{1,0:T(1,128)}, u32[]{:S(2)}) copy-start(s32[1,4]{1,0:T(1,128)} %lengths.1) | copy-start | bytes 52
  6.4 9.0 %collective-permute-start.3 = (bf16[320,256]{1,0:T(8,128)(2,1)S(1)}, bf16[320,256]{1,0:T(8,128)(2,1)S(1)}, u32[]{:S(2)}, u32[]{:S(2)}) collective-permute-start(bf16[320,256]{1,0:T(8,128)(2,1)S(1)} %get-tuple-element.79), channel_id=1, source_target_pairs={{0,2},{1,3},{2,0},{3,1},{4,6},{5,7},{6,4},{7,5},{8,10},{9,11},{10,... | collective-permute-start | bytes 491528 | tf_op jit(solution)/shard_map/ppermute | solution.py:481
  6.8 8.9 %collective-permute-start.5 = (bf16[320,256]{1,0:T(8,128)(2,1)S(1)}, bf16[320,256]{1,0:T(8,128)(2,1)S(1)}, u32[]{:S(2)}, u32[]{:S(2)}) collective-permute-start(bf16[320,256]{1,0:T(8,128)(2,1)S(1)} %get-tuple-element.85), channel_id=1, source_target_pairs={{0,1},{1,0},{2,3},{3,2},{4,5},{5,4},{6,7},{7,6},{8,9},{9,8},{10,11... | collective-permute-start | bytes 491528 | tf_op jit(solution)/shard_map/ppermute | solution.py:481
  8.6 14.5 %collective-permute-start = (bf16[320,256]{1,0:T(8,128)(2,1)S(1)}, bf16[320,256]{1,0:T(8,128)(2,1)S(1)}, u32[]{:S(2)}, u32[]{:S(2)}) collective-permute-start(bf16[320,256]{1,0:T(8,128)(2,1)S(1)} %get-tuple-element.72), channel_id=1, source_target_pairs={{0,3},{1,2},{2,1},{3,0},{4,7},{5,6},{6,5},{7,4},{8,11},{9,10},{10,... | collective-permute-start | bytes 491528 | tf_op jit(solution)/shard_map/ppermute | solution.py:526
  11.7 11.4 %collective-permute-start.2 = (bf16[320,256]{1,0:T(8,128)(2,1)S(1)}, bf16[320,256]{1,0:T(8,128)(2,1)S(1)}, u32[]{:S(2)}, u32[]{:S(2)}) collective-permute-start(bf16[320,256]{1,0:T(8,128)(2,1)S(1)} %get-tuple-element.77), channel_id=1, source_target_pairs={{0,2},{1,3},{2,0},{3,1},{4,6},{5,7},{6,4},{7,5},{8,10},{9,11},{10,... | collective-permute-start | bytes 491528 | tf_op jit(solution)/shard_map/ppermute | solution.py:526
  15.6 7.4 %collective-permute-start.4 = (bf16[320,256]{1,0:T(8,128)(2,1)S(1)}, bf16[320,256]{1,0:T(8,128)(2,1)S(1)}, u32[]{:S(2)}, u32[]{:S(2)}) collective-permute-start(bf16[320,256]{1,0:T(8,128)(2,1)S(1)} %get-tuple-element.82), channel_id=1, source_target_pairs={{0,1},{1,0},{2,3},{3,2},{4,5},{5,4},{6,7},{7,6},{8,9},{9,8},{10,11... | collective-permute-start | bytes 491528 | tf_op jit(solution)/shard_map/ppermute | solution.py:526
  20.0 7.8 %collective-permute-start.6 = (bf16[320,256]{1,0:T(8,128)(2,1)S(1)}, bf16[320,256]{1,0:T(8,128)(2,1)S(1)}, u32[]{:S(2)}, u32[]{:S(2)}) collective-permute-start(bf16[320,256]{1,0:T(8,128)(2,1)S(1)} %get-tuple-element.101), channel_id=1, source_target_pairs={{3,0},{2,1},{1,2},{0,3},{7,4},{6,5},{5,6},{4,7},{11,8},{10,9},{9,1... | collective-permute-start | bytes 491528 | tf_op jit(solution)/shard_map/ppermute | solution.py:70
  27.8 11.8 %collective-permute-start.8 = (bf16[640,256]{1,0:T(8,128)(2,1)S(1)}, bf16[640,256]{1,0:T(8,128)(2,1)S(1)}, u32[]{:S(2)}, u32[]{:S(2)}) collective-permute-start(bf16[640,256]{1,0:T(8,128)(2,1)S(1)} %get-tuple-element.105), channel_id=1, source_target_pairs={{2,0},{3,1},{0,2},{1,3},{6,4},{7,5},{4,6},{5,7},{10,8},{11,9},{8,1... | collective-permute-start | bytes 983048 | tf_op jit(solution)/shard_map/ppermute | solution.py:70
  28.3 11.7 %collective-permute-start.9 = (bf16[640,256]{1,0:T(8,128)(2,1)S(1)}, bf16[640,256]{1,0:T(8,128)(2,1)S(1)}, u32[]{:S(2)}, u32[]{:S(2)}) collective-permute-start(bf16[640,256]{1,0:T(8,128)(2,1)S(1)} %get-tuple-element.106), channel_id=1, source_target_pairs={{1,0},{0,1},{3,2},{2,3},{5,4},{4,5},{7,6},{6,7},{9,8},{8,9},{11,10... | collective-permute-start | bytes 983048 | tf_op jit(solution)/shard_map/ppermute | solution.py:70
  29.8 9.7 %collective-permute-start.7 = (bf16[320,256]{1,0:T(8,128)(2,1)S(1)}, bf16[320,256]{1,0:T(8,128)(2,1)S(1)}, u32[]{:S(2)}, u32[]{:S(2)}) collective-permute-start(bf16[320,256]{1,0:T(8,128)(2,1)S(1)} %get-tuple-element.103), channel_id=1, source_target_pairs={{3,0},{2,1},{1,2},{0,3},{7,4},{6,5},{5,6},{4,7},{11,8},{10,9},{9,1... | collective-permute-start | bytes 491528 | tf_op jit(solution)/shard_map/ppermute | solution.py:70
  31.3 12.2 %all-to-all-start = ((f32[32,4,128]{2,1,0:T(4,128)}), f32[32,4,128]{2,1,0:T(4,128)S(1)}, u32[]{:S(2)}, u32[]{:S(2)}) async-start(f32[32,4,128]{2,1,0:T(4,128)} %get-tuple-element.111), calls=%async_computation | async-start | bytes 131072 | tf_op jit(solution)/shard_map/all_to_all | solution.py:573

commit v15 on v14

--- a/solution.py
+++ b/solution.py
@@ -212,7 +212,7 @@
     for result, out in zip(earlier, [out for slot, out in enumerate(outs) if slot != EARLY]):
         done = head * 4 * HEAD_DIM
         out[:done, :] = result[:done, :]
-    qt_all, kt_all, vt_all, gt_all, k_all, v_all, s_buf, e_buf, d_buf = refs[slots + 1 : slots + 10]
+    qt_all, kt_all, vt_all, g_all, k_all, v_all, s_buf, e_buf, d_buf = refs[slots + 1 : slots + 10]
     own_bias = bias[head * HEAD_DIM : (head + 1) * HEAD_DIM, :]
     rest_row = lax.broadcasted_iota(jnp.int32, (LANES - HEAD_DIM, tokd), 0)
 
@@ -265,7 +265,7 @@
         coarse = delta.astype(jnp.bfloat16).astype(jnp.float32)
         rest = jnp.where(rest_row == 0, -coarse, jnp.where(rest_row == 1, coarse - delta, 0.0))
         grad = jnp.concatenate([grad * inv, rest], axis=0).astype(jnp.bfloat16)
-        gt_all[:, block_of(slot)] = grad
+        g_all[block_of(slot), :] = grad.T
         spread = grad[:HEAD_DIM].astype(jnp.float32) * mixed[HEAD_DIM : HEAD_DIM + 1]
         return grad, live(slot, spread)
 
@@ -281,13 +281,10 @@
         return live(slot, dquery)
 
     def value_part(slot):
-        dvalue = lax.dot_general(
-            gt_all[:HEAD_DIM, :],
-            e_buf[block_of(slot), :],
-            by_lanes,
-            preferred_element_type=jnp.float32,
-        )
-        put(slot, 3, dvalue.astype(jnp.bfloat16))
+        dvalue = jnp.dot(
+            e_buf[block_of(slot), :], g_all[...], preferred_element_type=jnp.float32
+        )
+        put(slot, 3, dvalue.astype(jnp.bfloat16).T[:HEAD_DIM])
 
     for slot in range(slots):
         at = block_of(slot)
@@ -552,8 +549,8 @@
             + [sums_shape],
             in_specs=[vmem] * (4 + slots + 2 * len(staged[phase]) + len(carried)),
             out_specs=[vmem] * slots + [hbm if last else vmem],
-            scratch_shapes=[pltpu.VMEM((LANES, span), jnp.bfloat16)] * 4
-            + [pltpu.VMEM((span, LANES), jnp.bfloat16)] * 2
+            scratch_shapes=[pltpu.VMEM((LANES, span), jnp.bfloat16)] * 3
+            + [pltpu.VMEM((span, LANES), jnp.bfloat16)] * 3
             + [pltpu.VMEM((2, span, tokd), jnp.float32)]
             + [pltpu.VMEM((span, span), jnp.bfloat16)] * 2
             + (
@@ -567,7 +564,7 @@
             ),
             name="attend_head",
         )(*tables, *got[phase], *(one for pair in staged[phase].values() for one in pair), *carried)
-        results, total, early = lax.optimization_barrier((results, total, early))
+        results[EARLY], early = lax.optimization_barrier((results[EARLY], early))
         early.append(send_back(results[EARLY], EARLY))
         carried = [total] + [results[slot] for slot in kept]
     tiles = lax.all_to_all(total, ("dp", "tok"), 0, 0, tiled=True)

time: 44.5 us -> 44.6 us (level)
  starting transfers between devices: 21.1 us -> 20.3 us
  waiting for transfers between devices: 7.88 us -> 8.65 us
    ppermute x4, waiting for transfers between devices: 3.87 us -> 4.85 us  [send_back(): lax.ppermute(result, 'tok', [(target, source) for source, target in pairs])]
    all_to_all x1, starting transfers between devices: 4.77 us -> 4.01 us  [on_device(): tiles = lax.all_to_all(total, ('dp', 'tok'), 0, 0, tiled=True)]
  transfers between devices with their start and end apart: 11 -> 11, of which waited for: 4 -> 4; matrix products, arithmetic and copies ran while one was open for 0% -> 0% of each run, Pallas kernels for 27% -> 28%
where the time goes in v15:
time: 44.6 us; the launch traced here: 44.5 us
  starting transfers between devices  20.3 us (46%)
  Pallas kernels  14.7 us (33%)
  waiting for transfers between devices  8.65 us (19%)
  between operations  0.75 us (2%)
    pallas_call x2, Pallas kernels, on_device(): pl.pallas_call(functools.partial(attend_kernel, slots, tuple(staged[phase...  9.13 us
    ppermute x4, starting transfers between devices, send_back(): lax.ppermute(result, 'tok', [(target, source) for source, target in pairs])  6.59 us
    ppermute x3, starting transfers between devices, on_device(): got[phase].append(lax.ppermute(send, 'tok', rounds[slot - 1]))  5.05 us
    ppermute x4, waiting for transfers between devices, send_back(): lax.ppermute(result, 'tok', [(target, source) for source, target in pairs])  4.85 us
    ppermute x3, starting transfers between devices, on_device(): lax.ppermute(send, 'tok', pairs)  4.7 us
    all_to_all x1, starting transfers between devices, on_device(): tiles = lax.all_to_all(total, ('dp', 'tok'), 0, 0, tiled=True)  4.01 us
    all_to_all x1, waiting for transfers between devices, on_device(): tiles = lax.all_to_all(total, ('dp', 'tok'), 0, 0, tiled=True)  2.05 us
    ppermute x3, waiting for transfers between devices, on_device(): lax.ppermute(send, 'tok', pairs)  1.75 us
  transfers between devices with their start and end apart: 11, of which 4 were waited for; matrix products, arithmetic and copies ran while one was open for 0% of the time, Pallas kernels for 28%

profile of v15, /device:TPU:0, one launch (start us, length us, event | category | flops | bytes accessed | tf_op | source)
XLA Modules:
  0.0 44.5 jit_solution(1146375408043649775)
XLA Ops:
  0.6 0.0 copy-start.2
  0.6 0.0 copy-start.3
  0.7 0.0 copy-start.4
  0.7 1.7 %pack_heads.1 = (bf16[320,256]{1,0:T(8,128)(2,1)S(1)}, bf16[320,256]{1,0:T(8,128)(2,1)S(1)}, bf16[320,256]{1,0:T(8,128)(2,1)S(1)}, bf16[320,256]{1,0:T(8,128)(2,...) custom-call(bf16[256,640]{1,0:T(8,128)(2,1)} %bitcast.8, ...), custom_call_target="tpu_custom_call" | custom-call | tf_op jit(solution)/shard_map/pack_heads/pallas_call | solution.py:463
  2.4 0.0 copy-start
  2.4 4.0 %collective-permute-start.1 = (bf16[320,256]{1,0:T(8,128)(2,1)S(1)}, bf16[320,256]{1,0:T(8,128)(2,1)S(1)}, u32[]{:S(2)}, u32[]{:S(2)}) collective-permute-start(bf16[320,256]{1,0:T(8,128)(2,1)S(1)} %get-tuple-element.70), channel_id=1, source_target_pairs={{0,3},{1,2},{2,1},{3,0},{4,7},{5,6},{6,5},{7,4},{8,11},{9,10},{10,... | collective-permute-start | bytes 491528 | tf_op jit(solution)/shard_map/ppermute | solution.py:478
  6.4 0.0 copy-start.1
  6.4 0.4 collective-permute-start.3
  6.8 0.2 collective-permute-start.5
  7.1 0.0 copy-done.2
  7.1 0.0 copy-done.3
  7.1 0.0 copy-done.4
  7.1 0.0 copy-done
  7.1 0.0 copy-done.1
  7.1 1.3 %rotary_tables.1 = (f32[40,1024]{1,0:T(8,128)S(1)}, f32[40,1024]{1,0:T(8,128)S(1)}, f32[24,256]{1,0:T(8,128)S(1)}, f32[160,128]{1,0:T(8,128)S(1)}) custom-call(s32[1,4]{1,0:T(1,128)S(1)} %copy-done.1, s32[1,4]{1,0:T(1,128)S(1)} %copy-done.2, s32[4,8]{1,0:T(4,128)S(1)} %copy-done.4, f32[40,128]{1,0:T(8,128)S(1)} %copy-done.3, bf16[3,640]{1,0:T(4,128)(2,1)S(1)} %copy-done), custom_call_target="tpu_custom_call" | custom-call | flops 26214400 | tf_op jit(solution)/shard_map/rotary_tables/pallas_call | solution.py:482
  8.4 0.2 stage_slot.3
  8.6 2.9 %collective-permute-start = (bf16[320,256]{1,0:T(8,128)(2,1)S(1)}, bf16[320,256]{1,0:T(8,128)(2,1)S(1)}, u32[]{:S(2)}, u32[]{:S(2)}) collective-permute-start(bf16[320,256]{1,0:T(8,128)(2,1)S(1)} %get-tuple-element.68), channel_id=1, source_target_pairs={{0,3},{1,2},{2,1},{3,0},{4,7},{5,6},{6,5},{7,4},{8,11},{9,10},{10,... | collective-permute-start | bytes 491528 | tf_op jit(solution)/shard_map/ppermute | solution.py:523
  11.5 0.0 collective-permute-done.1.refs_0_.refs_1_
  11.5 0.2 stage_slot.4
  11.7 2.0 %collective-permute-start.2 = (bf16[320,256]{1,0:T(8,128)(2,1)S(1)}, bf16[320,256]{1,0:T(8,128)(2,1)S(1)}, u32[]{:S(2)}, u32[]{:S(2)}) collective-permute-start(bf16[320,256]{1,0:T(8,128)(2,1)S(1)} %get-tuple-element.73), channel_id=1, source_target_pairs={{0,2},{1,3},{2,0},{3,1},{4,6},{5,7},{6,4},{7,5},{8,10},{9,11},{10,... | collective-permute-start | bytes 491528 | tf_op jit(solution)/shard_map/ppermute | solution.py:523
  13.7 1.7 %collective-permute-done.3.refs_0_.refs_2_ = bf16[320,256]{1,0:T(8,128)(2,1)S(1)} collective-permute-done((bf16[320,256]{1,0:T(8,128)(2,1)S(1)}, bf16[320,256]{1,0:T(8,128)(2,1)S(1)}, u32[]{:S(2)}, u32[]{:S(2)}) %collective-permute-start.3) | collective-permute-done | bytes 163872 | tf_op jit(solution)/shard_map/ppermute | solution.py:478
  15.5 0.2 stage_slot.5
  15.6 0.1 collective-permute-start.4
  15.8 0.0 collective-permute-done.5.refs_3_
  15.8 4.3 %attend_head.2 = (bf16[640,256]{1,0:T(8,128)(2,1)S(1)}, bf16[320,256]{1,0:T(8,128)(2,1)S(1)}, bf16[640,256]{1,0:T(8,128)(2,1)S(1)}, bf16[640,256]{1,0:T(8,128)(2,1)S(1)}, f32[8,128]{1,0:T(8,128)S(1)}) custom-call(f32[40,1024]{1,0:T(8,128)S(1)} %get-tuple-element.57.cosv, f32[40,1024]{1,0:T(8,128)S(1)} %get-tuple-element.58.sinv, ...), custom_call_target="tpu_custom_call" | custom-call | flops 3221225472 | tf_op jit(solution)/shard_map/attend_head/pallas_call | solution.py:538
  20.1 3.0 %collective-permute-start.6 = (bf16[320,256]{1,0:T(8,128)(2,1)S(1)}, bf16[320,256]{1,0:T(8,128)(2,1)S(1)}, u32[]{:S(2)}, u32[]{:S(2)}) collective-permute-start(bf16[320,256]{1,0:T(8,128)(2,1)S(1)} %get-tuple-element.93), channel_id=1, source_target_pairs={{3,0},{2,1},{1,2},{0,3},{7,4},{6,5},{5,6},{4,7},{11,8},{10,9},{9,1... | collective-permute-start | bytes 491528 | tf_op jit(solution)/shard_map/ppermute | solution.py:70
  23.1 0.0 collective-permute-done.refs_1_
  23.1 0.0 collective-permute-done.2.refs_2_
  23.1 0.0 collective-permute-done.4.refs_3_
  23.1 4.8 %attend_head.3 = (bf16[640,256]{1,0:T(8,128)(2,1)S(1)}, bf16[320,256]{1,0:T(8,128)(2,1)S(1)}, bf16[640,256]{1,0:T(8,128)(2,1)S(1)}, bf16[640,256]{1,0:T(8,128)(2,1)S(1)}, f32[32,4,128]{2,1,0:T(4,128)}) custom-call(f32[40,1024]{1,0:T(8,128)S(1)} %get-tuple-element.57.cosv, f32[40,1024]{1,0:T(8,128)S(1)} %get-tuple-element.58.sinv, ...), custom_call_target="tpu_custom_call" | custom-call | flops 3221225472 | tf_op jit(solution)/shard_map/attend_head/pallas_call | solution.py:538
  28.0 0.5 %collective-permute-start.8 = (bf16[640,256]{1,0:T(8,128)(2,1)S(1)}, bf16[640,256]{1,0:T(8,128)(2,1)S(1)}, u32[]{:S(2)}, u32[]{:S(2)}) collective-permute-start(bf16[640,256]{1,0:T(8,128)(2,1)S(1)} %get-tuple-element.97), channel_id=1, source_target_pairs={{2,0},{3,1},{0,2},{1,3},{6,4},{7,5},{4,6},{5,7},{10,8},{11,9},{8,1... | collective-permute-start | bytes 983048 | tf_op jit(solution)/shard_map/ppermute | solution.py:70
  28.5 0.8 %collective-permute-start.9 = (bf16[640,256]{1,0:T(8,128)(2,1)S(1)}, bf16[640,256]{1,0:T(8,128)(2,1)S(1)}, u32[]{:S(2)}, u32[]{:S(2)}) collective-permute-start(bf16[640,256]{1,0:T(8,128)(2,1)S(1)} %get-tuple-element.98), channel_id=1, source_target_pairs={{1,0},{0,1},{3,2},{2,3},{5,4},{4,5},{7,6},{6,7},{9,8},{8,9},{11,10... | collective-permute-start | bytes 983048 | tf_op jit(solution)/shard_map/ppermute | solution.py:70
  29.3 0.0 collective-permute-done.6.refs_0_
  29.3 2.3 %collective-permute-start.7 = (bf16[320,256]{1,0:T(8,128)(2,1)S(1)}, bf16[320,256]{1,0:T(8,128)(2,1)S(1)}, u32[]{:S(2)}, u32[]{:S(2)}) collective-permute-start(bf16[320,256]{1,0:T(8,128)(2,1)S(1)} %get-tuple-element.95), channel_id=1, source_target_pairs={{3,0},{2,1},{1,2},{0,3},{7,4},{6,5},{5,6},{4,7},{11,8},{10,9},{9,1... | collective-permute-start | bytes 491528 | tf_op jit(solution)/shard_map/ppermute | solution.py:70
  31.5 4.0 %all-to-all-start = ((f32[32,4,128]{2,1,0:T(4,128)}), f32[32,4,128]{2,1,0:T(4,128)S(1)}, u32[]{:S(2)}, u32[]{:S(2)}) async-start(f32[32,4,128]{2,1,0:T(4,128)} %get-tuple-element.103), calls=%async_computation | async-start | bytes 131072 | tf_op jit(solution)/shard_map/all_to_all | solution.py:570
  35.5 4.3 %collective-permute-done.7.refs_1_ = bf16[320,256]{1,0:T(8,128)(2,1)S(1)} collective-permute-done((bf16[320,256]{1,0:T(8,128)(2,1)S(1)}, bf16[320,256]{1,0:T(8,128)(2,1)S(1)}, u32[]{:S(2)}, u32[]{:S(2)}) %collective-permute-start.7) | collective-permute-done | bytes 163872 | tf_op jit(solution)/shard_map/ppermute | solution.py:70
  39.8 0.0 collective-permute-done.8.refs_3_
  39.8 0.6 %collective-permute-done.9.refs_4_ = bf16[640,256]{1,0:T(8,128)(2,1)S(1)} collective-permute-done((bf16[640,256]{1,0:T(8,128)(2,1)S(1)}, bf16[640,256]{1,0:T(8,128)(2,1)S(1)}, u32[]{:S(2)}, u32[]{:S(2)}) %collective-permute-start.9) | collective-permute-done | bytes 327712 | tf_op jit(solution)/shard_map/ppermute | solution.py:70
  40.4 1.3 %unpack_heads.1 = (bf16[256,640]{1,0:T(8,128)(2,1)}, bf16[256,640]{1,0:T(8,128)(2,1)}, bf16[256,640]{1,0:T(8,128)(2,1)}, bf16[256,640]{1,0:T(8,128)(2,1)}) custom-call(bf16[320,256]{1,0:T(8,128)(2,1)S(1)} %collective-permute-done.6.refs_0_, bf16[320,256]{1,0:T(8,128)(2,1)S(1)} %collective-permute-done.7.refs_1_, ...), custom_call_target="tpu_custom_call" | custom-call | flops 20000000000 | tf_op jit(solution)/shard_map/unpack_heads/pallas_call | solution.py:573
  41.7 2.0 %all-to-all-done.tiles = f32[32,4,128]{2,1,0:T(4,128)S(1)} async-done(((f32[32,4,128]{2,1,0:T(4,128)}), f32[32,4,128]{2,1,0:T(4,128)S(1)}, u32[]{:S(2)}, u32[]{:S(2)}) %all-to-all-start) | async-done | bytes 65568 | tf_op jit(solution)/shard_map/all_to_all | solution.py:570
  43.8 0.7 %bias_sums.1 = f32[3,640]{1,0:T(4,128)} custom-call(f32[32,4,128]{2,1,0:T(4,128)S(1)} %all-to-all-done.tiles), custom_call_target="tpu_custom_call" | custom-call | tf_op jit(solution)/shard_map/bias_sums/pallas_call | solution.py:588
Async XLA Ops:
  0.6 6.4 %copy-start.2 = (s32[1,4]{1,0:T(1,128)S(1)}, s32[1,4]{1,0:T(1,128)}, u32[]{:S(2)}) copy-start(s32[1,4]{1,0:T(1,128)} %widths.1) | copy-start | bytes 52
  0.6 6.4 %copy-start.3 = (f32[40,128]{1,0:T(8,128)S(1)}, f32[40,128]{1,0:T(8,128)}, u32[]{:S(2)}) copy-start(f32[40,128]{1,0:T(8,128)} %constant.5.clone.inverse) | copy-start | bytes 61444
  0.7 6.4 %copy-start.4 = (s32[4,8]{1,0:T(4,128)S(1)}, s32[4,8]{1,0:T(4,128)}, u32[]{:S(2)}) copy-start(s32[4,8]{1,0:T(4,128)} %constant.4.clone.table) | copy-start | bytes 388
  2.4 4.7 %copy-start = (bf16[3,640]{1,0:T(4,128)(2,1)S(1)}, bf16[3,640]{1,0:T(4,128)(2,1)}, u32[]{:S(2)}) copy-start(bf16[3,640]{1,0:T(4,128)(2,1)} %bias.1) | copy-start | bytes 11524
  2.4 9.1 %collective-permute-start.1 = (bf16[320,256]{1,0:T(8,128)(2,1)S(1)}, bf16[320,256]{1,0:T(8,128)(2,1)S(1)}, u32[]{:S(2)}, u32[]{:S(2)}) collective-permute-start(bf16[320,256]{1,0:T(8,128)(2,1)S(1)} %get-tuple-element.70), channel_id=1, source_target_pairs={{0,3},{1,2},{2,1},{3,0},{4,7},{5,6},{6,5},{7,4},{8,11},{9,10},{10,... | collective-permute-start | bytes 491528 | tf_op jit(solution)/shard_map/ppermute | solution.py:478
  6.4 0.7 %copy-start.1 = (s32[1,4]{1,0:T(1,128)S(1)}, s32[1,4]{1,0:T(1,128)}, u32[]{:S(2)}) copy-start(s32[1,4]{1,0:T(1,128)} %lengths.1) | copy-start | bytes 52
  6.4 9.0 %collective-permute-start.3 = (bf16[320,256]{1,0:T(8,128)(2,1)S(1)}, bf16[320,256]{1,0:T(8,128)(2,1)S(1)}, u32[]{:S(2)}, u32[]{:S(2)}) collective-permute-start(bf16[320,256]{1,0:T(8,128)(2,1)S(1)} %get-tuple-element.75), channel_id=1, source_target_pairs={{0,2},{1,3},{2,0},{3,1},{4,6},{5,7},{6,4},{7,5},{8,10},{9,11},{10,... | collective-permute-start | bytes 491528 | tf_op jit(solution)/shard_map/ppermute | solution.py:478
  6.8 8.9 %collective-permute-start.5 = (bf16[320,256]{1,0:T(8,128)(2,1)S(1)}, bf16[320,256]{1,0:T(8,128)(2,1)S(1)}, u32[]{:S(2)}, u32[]{:S(2)}) collective-permute-start(bf16[320,256]{1,0:T(8,128)(2,1)S(1)} %get-tuple-element.81), channel_id=1, source_target_pairs={{0,1},{1,0},{2,3},{3,2},{4,5},{5,4},{6,7},{7,6},{8,9},{9,8},{10,11... | collective-permute-start | bytes 491528 | tf_op jit(solution)/shard_map/ppermute | solution.py:478
  8.6 14.5 %collective-permute-start = (bf16[320,256]{1,0:T(8,128)(2,1)S(1)}, bf16[320,256]{1,0:T(8,128)(2,1)S(1)}, u32[]{:S(2)}, u32[]{:S(2)}) collective-permute-start(bf16[320,256]{1,0:T(8,128)(2,1)S(1)} %get-tuple-element.68), channel_id=1, source_target_pairs={{0,3},{1,2},{2,1},{3,0},{4,7},{5,6},{6,5},{7,4},{8,11},{9,10},{10,... | collective-permute-start | bytes 491528 | tf_op jit(solution)/shard_map/ppermute | solution.py:523
  11.7 11.4 %collective-permute-start.2 = (bf16[320,256]{1,0:T(8,128)(2,1)S(1)}, bf16[320,256]{1,0:T(8,128)(2,1)S(1)}, u32[]{:S(2)}, u32[]{:S(2)}) collective-permute-start(bf16[320,256]{1,0:T(8,128)(2,1)S(1)} %get-tuple-element.73), channel_id=1, source_target_pairs={{0,2},{1,3},{2,0},{3,1},{4,6},{5,7},{6,4},{7,5},{8,10},{9,11},{10,... | collective-permute-start | bytes 491528 | tf_op jit(solution)/shard_map/ppermute | solution.py:523
  15.6 7.5 %collective-permute-start.4 = (bf16[320,256]{1,0:T(8,128)(2,1)S(1)}, bf16[320,256]{1,0:T(8,128)(2,1)S(1)}, u32[]{:S(2)}, u32[]{:S(2)}) collective-permute-start(bf16[320,256]{1,0:T(8,128)(2,1)S(1)} %get-tuple-element.78), channel_id=1, source_target_pairs={{0,1},{1,0},{2,3},{3,2},{4,5},{5,4},{6,7},{7,6},{8,9},{9,8},{10,11... | collective-permute-start | bytes 491528 | tf_op jit(solution)/shard_map/ppermute | solution.py:523
  20.1 9.2 %collective-permute-start.6 = (bf16[320,256]{1,0:T(8,128)(2,1)S(1)}, bf16[320,256]{1,0:T(8,128)(2,1)S(1)}, u32[]{:S(2)}, u32[]{:S(2)}) collective-permute-start(bf16[320,256]{1,0:T(8,128)(2,1)S(1)} %get-tuple-element.93), channel_id=1, source_target_pairs={{3,0},{2,1},{1,2},{0,3},{7,4},{6,5},{5,6},{4,7},{11,8},{10,9},{9,1... | collective-permute-start | bytes 491528 | tf_op jit(solution)/shard_map/ppermute | solution.py:70
  28.0 11.9 %collective-permute-start.8 = (bf16[640,256]{1,0:T(8,128)(2,1)S(1)}, bf16[640,256]{1,0:T(8,128)(2,1)S(1)}, u32[]{:S(2)}, u32[]{:S(2)}) collective-permute-start(bf16[640,256]{1,0:T(8,128)(2,1)S(1)} %get-tuple-element.97), channel_id=1, source_target_pairs={{2,0},{3,1},{0,2},{1,3},{6,4},{7,5},{4,6},{5,7},{10,8},{11,9},{8,1... | collective-permute-start | bytes 983048 | tf_op jit(solution)/shard_map/ppermute | solution.py:70
  28.5 11.9 %collective-permute-start.9 = (bf16[640,256]{1,0:T(8,128)(2,1)S(1)}, bf16[640,256]{1,0:T(8,128)(2,1)S(1)}, u32[]{:S(2)}, u32[]{:S(2)}) collective-permute-start(bf16[640,256]{1,0:T(8,128)(2,1)S(1)} %get-tuple-element.98), channel_id=1, source_target_pairs={{1,0},{0,1},{3,2},{2,3},{5,4},{4,5},{7,6},{6,7},{9,8},{8,9},{11,10... | collective-permute-start | bytes 983048 | tf_op jit(solution)/shard_map/ppermute | solution.py:70
  29.3 10.6 %collective-permute-start.7 = (bf16[320,256]{1,0:T(8,128)(2,1)S(1)}, bf16[320,256]{1,0:T(8,128)(2,1)S(1)}, u32[]{:S(2)}, u32[]{:S(2)}) collective-permute-start(bf16[320,256]{1,0:T(8,128)(2,1)S(1)} %get-tuple-element.95), channel_id=1, source_target_pairs={{3,0},{2,1},{1,2},{0,3},{7,4},{6,5},{5,6},{4,7},{11,8},{10,9},{9,1... | collective-permute-start | bytes 491528 | tf_op jit(solution)/shard_map/ppermute | solution.py:70
  31.5 12.2 %all-to-all-start = ((f32[32,4,128]{2,1,0:T(4,128)}), f32[32,4,128]{2,1,0:T(4,128)S(1)}, u32[]{:S(2)}, u32[]{:S(2)}) async-start(f32[32,4,128]{2,1,0:T(4,128)} %get-tuple-element.103), calls=%async_computation | async-start | bytes 131072 | tf_op jit(solution)/shard_map/all_to_all | solution.py:570

commit v16 on v14

--- a/solution.py
+++ b/solution.py
@@ -377,25 +377,28 @@
     return jnp.concatenate(rows + [last], axis=0)
 
 
+def join_kernel(*refs):
+    msgs, out = refs[:-1], refs[-1]
+    rows = msgs[0].shape[0]
+    for phase, message in enumerate(msgs):
+        out[phase * rows : (phase + 1) * rows, :] = message[...]
+
+
 def unpack_kernel(slots, count, images, *refs):
     closed = is_closed(count)
     if not closed:
         lengths, table, *refs = refs
-    msgs, refs = refs[: slots + OWN_HEADS - 1], refs[slots + OWN_HEADS - 1 :]
+    msgs, refs = refs[:slots], refs[slots:]
     *outs, held, ready, sems = refs
-    early, late = msgs[:OWN_HEADS], list(msgs[OWN_HEADS:])
-    late.insert(EARLY, None)
     me = lax.axis_index("tok")
 
     def place(slot, residue):
         for phase in range(OWN_HEADS):
             begin = pl.multiple_of((phase * SPAN + residue) * HEAD_DIM, 16)
             for number in range(4):
-                if slot == EARLY:
-                    piece = early[phase][message_rows(number), :]
-                else:
-                    piece = late[slot][message_rows(4 * phase + number), :]
-                held[number, pl.ds(begin, HEAD_DIM), :] = piece
+                held[number, pl.ds(begin, HEAD_DIM), :] = msgs[slot][
+                    message_rows(4 * phase + number), :
+                ]
 
     for slot in range(slots):
         if closed:
@@ -567,16 +570,26 @@
             ),
             name="attend_head",
         )(*tables, *got[phase], *(one for pair in staged[phase].values() for one in pair), *carried)
-        results, total, early = lax.optimization_barrier((results, total, early))
+        results[-1], early = lax.optimization_barrier((results[-1], early))
         early.append(send_back(results[EARLY], EARLY))
         carried = [total] + [results[slot] for slot in kept]
     tiles = lax.all_to_all(total, ("dp", "tok"), 0, 0, tiled=True)
     late = [send_back(results[slot], slot) for slot in kept]
+    both = pl.pallas_call(
+        join_kernel,
+        out_shape=joined,
+        in_specs=[vmem] * OWN_HEADS,
+        out_specs=vmem,
+        compiler_params=params(16),
+        cost_estimate=pl.CostEstimate(flops=UNPACK_FLOPS, bytes_accessed=0, transcendentals=0),
+        name="join_phases",
+    )(*early)
+    late.insert(EARLY, both)
     places = [] if closed else [lengths, jnp.asarray(targets)]
     outs = pl.pallas_call(
         functools.partial(unpack_kernel, slots, count, images),
         out_shape=[whole] * 4,
-        in_specs=[smem] * len(places) + [vmem] * (OWN_HEADS + len(late)),
+        in_specs=[smem] * len(places) + [vmem] * slots,
         out_specs=[hbm] * 4,
         scratch_shapes=[
             pltpu.VMEM((4, model, tokd), jnp.bfloat16),
@@ -586,7 +599,7 @@
         compiler_params=params(16),
         cost_estimate=pl.CostEstimate(flops=UNPACK_FLOPS, bytes_accessed=0, transcendentals=0),
         name="unpack_heads",
-    )(*places, *early, *late)
+    )(*places, *late)
     outs, tiles = lax.optimization_barrier((outs, tiles))
     bias_grad = pl.pallas_call(
         bias_kernel,

time: 44.5 us -> 45.2 us (1.016)
  waiting for transfers between devices: 7.88 us -> 9.3 us
  starting transfers between devices: 21.1 us -> 20.4 us
    ppermute x4, waiting for transfers between devices: 3.87 us -> 5.52 us  [send_back(): lax.ppermute(result, 'tok', [(target, source) for source, target in pairs])]
    all_to_all x1, starting transfers between devices: 4.77 us -> 4.05 us  [on_device(): tiles = lax.all_to_all(total, ('dp', 'tok'), 0, 0, tiled=True)]
  transfers between devices with their start and end apart: 11 -> 11, of which waited for: 4 -> 5; matrix products, arithmetic and copies ran while one was open for 0% -> 0% of each run, Pallas kernels for 27% -> 27%
where the time goes in v16:
time: 45.2 us; the launch traced here: 45 us
  starting transfers between devices  20.4 us (45%)
  Pallas kernels  14.5 us (32%)
  waiting for transfers between devices  9.3 us (21%)
  between operations  0.76 us (2%)
    pallas_call x2, Pallas kernels, on_device(): pl.pallas_call(functools.partial(attend_kernel, slots, tuple(staged[phase...  8.93 us
    ppermute x4, starting transfers between devices, send_back(): lax.ppermute(result, 'tok', [(target, source) for source, target in pairs])  6.6 us
    ppermute x4, waiting for transfers between devices, send_back(): lax.ppermute(result, 'tok', [(target, source) for source, target in pairs])  5.52 us
    ppermute x3, starting transfers between devices, on_device(): got[phase].append(lax.ppermute(send, 'tok', rounds[slot - 1]))  5.05 us
    ppermute x3, starting transfers between devices, on_device(): lax.ppermute(send, 'tok', pairs)  4.7 us
    all_to_all x1, starting transfers between devices, on_device(): tiles = lax.all_to_all(total, ('dp', 'tok'), 0, 0, tiled=True)  4.05 us
    all_to_all x1, waiting for transfers between devices, on_device(): tiles = lax.all_to_all(total, ('dp', 'tok'), 0, 0, tiled=True)  2.03 us
    ppermute x3, waiting for transfers between devices, on_device(): lax.ppermute(send, 'tok', pairs)  1.75 us
  transfers between devices with their start and end apart: 11, of which 5 were waited for; matrix products, arithmetic and copies ran while one was open for 0% of the time, Pallas kernels for 27%

profile of v16, /device:TPU:0, one launch (start us, length us, event | category | flops | bytes accessed | tf_op | source)
XLA Modules:
  0.0 45.0 jit_solution(355389284717446565)
XLA Ops:
  0.6 0.0 copy-start.2
  0.6 0.0 copy-start.3
  0.7 0.0 copy-start.4
  0.7 1.7 %pack_heads.1 = (bf16[320,256]{1,0:T(8,128)(2,1)S(1)}, bf16[320,256]{1,0:T(8,128)(2,1)S(1)}, bf16[320,256]{1,0:T(8,128)(2,1)S(1)}, bf16[320,256]{1,0:T(8,128)(2,...) custom-call(bf16[256,640]{1,0:T(8,128)(2,1)} %bitcast.8, ...), custom_call_target="tpu_custom_call" | custom-call | tf_op jit(solution)/shard_map/pack_heads/pallas_call | solution.py:469
  2.4 0.0 copy-start
  2.4 4.0 %collective-permute-start.1 = (bf16[320,256]{1,0:T(8,128)(2,1)S(1)}, bf16[320,256]{1,0:T(8,128)(2,1)S(1)}, u32[]{:S(2)}, u32[]{:S(2)}) collective-permute-start(bf16[320,256]{1,0:T(8,128)(2,1)S(1)} %get-tuple-element.70), channel_id=1, source_target_pairs={{0,3},{1,2},{2,1},{3,0},{4,7},{5,6},{6,5},{7,4},{8,11},{9,10},{10,... | collective-permute-start | bytes 491528 | tf_op jit(solution)/shard_map/ppermute | solution.py:484
  6.4 0.0 copy-start.1
  6.4 0.4 collective-permute-start.3
  6.8 0.2 collective-permute-start.5
  7.1 0.0 copy-done.2
  7.1 0.0 copy-done.3
  7.1 0.0 copy-done.4
  7.1 0.0 copy-done
  7.1 0.0 copy-done.1
  7.1 1.3 %rotary_tables.1 = (f32[40,1024]{1,0:T(8,128)S(1)}, f32[40,1024]{1,0:T(8,128)S(1)}, f32[24,256]{1,0:T(8,128)S(1)}, f32[160,128]{1,0:T(8,128)S(1)}) custom-call(s32[1,4]{1,0:T(1,128)S(1)} %copy-done.1, s32[1,4]{1,0:T(1,128)S(1)} %copy-done.2, s32[4,8]{1,0:T(4,128)S(1)} %copy-done.4, f32[40,128]{1,0:T(8,128)S(1)} %copy-done.3, bf16[3,640]{1,0:T(4,128)(2,1)S(1)} %copy-done), custom_call_target="tpu_custom_call" | custom-call | flops 26214400 | tf_op jit(solution)/shard_map/rotary_tables/pallas_call | solution.py:488
  8.4 0.2 stage_slot.3
  8.6 2.9 %collective-permute-start = (bf16[320,256]{1,0:T(8,128)(2,1)S(1)}, bf16[320,256]{1,0:T(8,128)(2,1)S(1)}, u32[]{:S(2)}, u32[]{:S(2)}) collective-permute-start(bf16[320,256]{1,0:T(8,128)(2,1)S(1)} %get-tuple-element.68), channel_id=1, source_target_pairs={{0,3},{1,2},{2,1},{3,0},{4,7},{5,6},{6,5},{7,4},{8,11},{9,10},{10,... | collective-permute-start | bytes 491528 | tf_op jit(solution)/shard_map/ppermute | solution.py:529
  11.5 0.0 collective-permute-done.1.refs_0_.refs_1_
  11.5 0.2 stage_slot.4
  11.7 2.0 %collective-permute-start.2 = (bf16[320,256]{1,0:T(8,128)(2,1)S(1)}, bf16[320,256]{1,0:T(8,128)(2,1)S(1)}, u32[]{:S(2)}, u32[]{:S(2)}) collective-permute-start(bf16[320,256]{1,0:T(8,128)(2,1)S(1)} %get-tuple-element.73), channel_id=1, source_target_pairs={{0,2},{1,3},{2,0},{3,1},{4,6},{5,7},{6,4},{7,5},{8,10},{9,11},{10,... | collective-permute-start | bytes 491528 | tf_op jit(solution)/shard_map/ppermute | solution.py:529
  13.7 1.7 %collective-permute-done.3.refs_0_.refs_2_ = bf16[320,256]{1,0:T(8,128)(2,1)S(1)} collective-permute-done((bf16[320,256]{1,0:T(8,128)(2,1)S(1)}, bf16[320,256]{1,0:T(8,128)(2,1)S(1)}, u32[]{:S(2)}, u32[]{:S(2)}) %collective-permute-start.3) | collective-permute-done | bytes 163872 | tf_op jit(solution)/shard_map/ppermute | solution.py:484
  15.5 0.2 stage_slot.5
  15.6 0.1 collective-permute-start.4
  15.8 0.0 collective-permute-done.5.refs_3_
  15.8 4.2 %attend_head.2 = (bf16[640,256]{1,0:T(8,128)(2,1)S(1)}, bf16[320,256]{1,0:T(8,128)(2,1)S(1)}, bf16[640,256]{1,0:T(8,128)(2,1)S(1)}, bf16[640,256]{1,0:T(8,128)(2,1)S(1)}, f32[8,128]{1,0:T(8,128)S(1)}) custom-call(f32[40,1024]{1,0:T(8,128)S(1)} %get-tuple-element.57.cosv, f32[40,1024]{1,0:T(8,128)S(1)} %get-tuple-element.58.sinv, ...), custom_call_target="tpu_custom_call" | custom-call | flops 3221225472 | tf_op jit(solution)/shard_map/attend_head/pallas_call | solution.py:544
  20.0 3.0 %collective-permute-start.6 = (bf16[320,256]{1,0:T(8,128)(2,1)S(1)}, bf16[320,256]{1,0:T(8,128)(2,1)S(1)}, u32[]{:S(2)}, u32[]{:S(2)}) collective-permute-start(bf16[320,256]{1,0:T(8,128)(2,1)S(1)} %get-tuple-element.94), channel_id=1, source_target_pairs={{3,0},{2,1},{1,2},{0,3},{7,4},{6,5},{5,6},{4,7},{11,8},{10,9},{9,1... | collective-permute-start | bytes 491528 | tf_op jit(solution)/shard_map/ppermute | solution.py:70
  23.1 0.0 collective-permute-done.refs_1_
  23.1 0.0 collective-permute-done.2.refs_2_
  23.1 0.0 collective-permute-done.4.refs_3_
  23.1 4.7 %attend_head.3 = (bf16[640,256]{1,0:T(8,128)(2,1)S(1)}, bf16[320,256]{1,0:T(8,128)(2,1)S(1)}, bf16[640,256]{1,0:T(8,128)(2,1)S(1)}, bf16[640,256]{1,0:T(8,128)(2,1)S(1)}, f32[32,4,128]{2,1,0:T(4,128)}) custom-call(f32[40,1024]{1,0:T(8,128)S(1)} %get-tuple-element.57.cosv, f32[40,1024]{1,0:T(8,128)S(1)} %get-tuple-element.58.sinv, ...), custom_call_target="tpu_custom_call" | custom-call | flops 3221225472 | tf_op jit(solution)/shard_map/attend_head/pallas_call | solution.py:544
  27.8 0.8 %collective-permute-start.7 = (bf16[320,256]{1,0:T(8,128)(2,1)S(1)}, bf16[320,256]{1,0:T(8,128)(2,1)S(1)}, u32[]{:S(2)}, u32[]{:S(2)}) collective-permute-start(bf16[320,256]{1,0:T(8,128)(2,1)S(1)} %get-tuple-element.96), channel_id=1, source_target_pairs={{3,0},{2,1},{1,2},{0,3},{7,4},{6,5},{5,6},{4,7},{11,8},{10,9},{9,1... | collective-permute-start | bytes 491528 | tf_op jit(solution)/shard_map/ppermute | solution.py:70
  28.6 0.0 collective-permute-done.6.refs_0_
  28.6 1.2 %collective-permute-start.8 = (bf16[640,256]{1,0:T(8,128)(2,1)S(1)}, bf16[640,256]{1,0:T(8,128)(2,1)S(1)}, u32[]{:S(2)}, u32[]{:S(2)}) collective-permute-start(bf16[640,256]{1,0:T(8,128)(2,1)S(1)} %get-tuple-element.97), channel_id=1, source_target_pairs={{2,0},{3,1},{0,2},{1,3},{6,4},{7,5},{4,6},{5,7},{10,8},{11,9},{8,1... | collective-permute-start | bytes 983048 | tf_op jit(solution)/shard_map/ppermute | solution.py:70
  29.8 1.5 %collective-permute-start.9 = (bf16[640,256]{1,0:T(8,128)(2,1)S(1)}, bf16[640,256]{1,0:T(8,128)(2,1)S(1)}, u32[]{:S(2)}, u32[]{:S(2)}) collective-permute-start(bf16[640,256]{1,0:T(8,128)(2,1)S(1)} %get-tuple-element.98), channel_id=1, source_target_pairs={{1,0},{0,1},{3,2},{2,3},{5,4},{4,5},{7,6},{6,7},{9,8},{8,9},{11,10... | collective-permute-start | bytes 983048 | tf_op jit(solution)/shard_map/ppermute | solution.py:70
  31.3 4.0 %all-to-all-start = ((f32[32,4,128]{2,1,0:T(4,128)}), f32[32,4,128]{2,1,0:T(4,128)S(1)}, u32[]{:S(2)}, u32[]{:S(2)}) async-start(f32[32,4,128]{2,1,0:T(4,128)} %get-tuple-element.103), calls=%async_computation | async-start | bytes 131072 | tf_op jit(solution)/shard_map/all_to_all | solution.py:576
  35.4 0.5 %collective-permute-done.7.refs_1_ = bf16[320,256]{1,0:T(8,128)(2,1)S(1)} collective-permute-done((bf16[320,256]{1,0:T(8,128)(2,1)S(1)}, bf16[320,256]{1,0:T(8,128)(2,1)S(1)}, u32[]{:S(2)}, u32[]{:S(2)}) %collective-permute-start.7) | collective-permute-done | bytes 163872 | tf_op jit(solution)/shard_map/ppermute | solution.py:70
  35.9 4.0 %collective-permute-done.8.refs_2_ = bf16[640,256]{1,0:T(8,128)(2,1)S(1)} collective-permute-done((bf16[640,256]{1,0:T(8,128)(2,1)S(1)}, bf16[640,256]{1,0:T(8,128)(2,1)S(1)}, u32[]{:S(2)}, u32[]{:S(2)}) %collective-permute-start.8) | collective-permute-done | bytes 327712 | tf_op jit(solution)/shard_map/ppermute | solution.py:70
  39.9 1.0 %collective-permute-done.9.refs_3_ = bf16[640,256]{1,0:T(8,128)(2,1)S(1)} collective-permute-done((bf16[640,256]{1,0:T(8,128)(2,1)S(1)}, bf16[640,256]{1,0:T(8,128)(2,1)S(1)}, u32[]{:S(2)}, u32[]{:S(2)}) %collective-permute-start.9) | collective-permute-done | bytes 327712 | tf_op jit(solution)/shard_map/ppermute | solution.py:70
  40.9 1.3 %unpack_heads.1 = (bf16[256,640]{1,0:T(8,128)(2,1)}, bf16[256,640]{1,0:T(8,128)(2,1)}, bf16[256,640]{1,0:T(8,128)(2,1)}, bf16[256,640]{1,0:T(8,128)(2,1)}) custom-call(bf16[640,256]{1,0:T(8,128)(2,1)S(1)} %get-tuple-element.92.refs_0_, bf16[640,256]{1,0:T(8,128)(2,1)S(1)} %join_phases.1.refs_1_, bf16[640,256]{1,0:T(8,128)(2,1)S(1)} %collective-permute-done.8.refs_2_, ...), custom_call_target="tpu_custom_call" | custom-call | flops 20000000000 | tf_op jit(solution)/shard_map/unpack_heads/pallas_call | solution.py:589
  42.3 2.0 %all-to-all-done.tiles = f32[32,4,128]{2,1,0:T(4,128)S(1)} async-done(((f32[32,4,128]{2,1,0:T(4,128)}), f32[32,4,128]{2,1,0:T(4,128)S(1)}, u32[]{:S(2)}, u32[]{:S(2)}) %all-to-all-start) | async-done | bytes 65568 | tf_op jit(solution)/shard_map/all_to_all | solution.py:576
  44.3 0.7 %bias_sums.1 = f32[3,640]{1,0:T(4,128)} custom-call(f32[32,4,128]{2,1,0:T(4,128)S(1)} %all-to-all-done.tiles), custom_call_target="tpu_custom_call" | custom-call | tf_op jit(solution)/shard_map/bias_sums/pallas_call | solution.py:604
  (1 shorter events, 0.0 us)
Async XLA Ops:
  0.6 6.4 %copy-start.2 = (s32[1,4]{1,0:T(1,128)S(1)}, s32[1,4]{1,0:T(1,128)}, u32[]{:S(2)}) copy-start(s32[1,4]{1,0:T(1,128)} %widths.1) | copy-start | bytes 52
  0.6 6.4 %copy-start.3 = (f32[40,128]{1,0:T(8,128)S(1)}, f32[40,128]{1,0:T(8,128)}, u32[]{:S(2)}) copy-start(f32[40,128]{1,0:T(8,128)} %constant.5.clone.inverse) | copy-start | bytes 61444
  0.7 6.4 %copy-start.4 = (s32[4,8]{1,0:T(4,128)S(1)}, s32[4,8]{1,0:T(4,128)}, u32[]{:S(2)}) copy-start(s32[4,8]{1,0:T(4,128)} %constant.4.clone.table) | copy-start | bytes 388
  2.4 4.7 %copy-start = (bf16[3,640]{1,0:T(4,128)(2,1)S(1)}, bf16[3,640]{1,0:T(4,128)(2,1)}, u32[]{:S(2)}) copy-start(bf16[3,640]{1,0:T(4,128)(2,1)} %bias.1) | copy-start | bytes 11524
  2.4 9.1 %collective-permute-start.1 = (bf16[320,256]{1,0:T(8,128)(2,1)S(1)}, bf16[320,256]{1,0:T(8,128)(2,1)S(1)}, u32[]{:S(2)}, u32[]{:S(2)}) collective-permute-start(bf16[320,256]{1,0:T(8,128)(2,1)S(1)} %get-tuple-element.70), channel_id=1, source_target_pairs={{0,3},{1,2},{2,1},{3,0},{4,7},{5,6},{6,5},{7,4},{8,11},{9,10},{10,... | collective-permute-start | bytes 491528 | tf_op jit(solution)/shard_map/ppermute | solution.py:484
  6.4 0.7 %copy-start.1 = (s32[1,4]{1,0:T(1,128)S(1)}, s32[1,4]{1,0:T(1,128)}, u32[]{:S(2)}) copy-start(s32[1,4]{1,0:T(1,128)} %lengths.1) | copy-start | bytes 52
  6.4 9.0 %collective-permute-start.3 = (bf16[320,256]{1,0:T(8,128)(2,1)S(1)}, bf16[320,256]{1,0:T(8,128)(2,1)S(1)}, u32[]{:S(2)}, u32[]{:S(2)}) collective-permute-start(bf16[320,256]{1,0:T(8,128)(2,1)S(1)} %get-tuple-element.75), channel_id=1, source_target_pairs={{0,2},{1,3},{2,0},{3,1},{4,6},{5,7},{6,4},{7,5},{8,10},{9,11},{10,... | collective-permute-start | bytes 491528 | tf_op jit(solution)/shard_map/ppermute | solution.py:484
  6.8 8.9 %collective-permute-start.5 = (bf16[320,256]{1,0:T(8,128)(2,1)S(1)}, bf16[320,256]{1,0:T(8,128)(2,1)S(1)}, u32[]{:S(2)}, u32[]{:S(2)}) collective-permute-start(bf16[320,256]{1,0:T(8,128)(2,1)S(1)} %get-tuple-element.81), channel_id=1, source_target_pairs={{0,1},{1,0},{2,3},{3,2},{4,5},{5,4},{6,7},{7,6},{8,9},{9,8},{10,11... | collective-permute-start | bytes 491528 | tf_op jit(solution)/shard_map/ppermute | solution.py:484
  8.6 14.5 %collective-permute-start = (bf16[320,256]{1,0:T(8,128)(2,1)S(1)}, bf16[320,256]{1,0:T(8,128)(2,1)S(1)}, u32[]{:S(2)}, u32[]{:S(2)}) collective-permute-start(bf16[320,256]{1,0:T(8,128)(2,1)S(1)} %get-tuple-element.68), channel_id=1, source_target_pairs={{0,3},{1,2},{2,1},{3,0},{4,7},{5,6},{6,5},{7,4},{8,11},{9,10},{10,... | collective-permute-start | bytes 491528 | tf_op jit(solution)/shard_map/ppermute | solution.py:529
  11.7 11.4 %collective-permute-start.2 = (bf16[320,256]{1,0:T(8,128)(2,1)S(1)}, bf16[320,256]{1,0:T(8,128)(2,1)S(1)}, u32[]{:S(2)}, u32[]{:S(2)}) collective-permute-start(bf16[320,256]{1,0:T(8,128)(2,1)S(1)} %get-tuple-element.73), channel_id=1, source_target_pairs={{0,2},{1,3},{2,0},{3,1},{4,6},{5,7},{6,4},{7,5},{8,10},{9,11},{10,... | collective-permute-start | bytes 491528 | tf_op jit(solution)/shard_map/ppermute | solution.py:529
  15.6 7.4 %collective-permute-start.4 = (bf16[320,256]{1,0:T(8,128)(2,1)S(1)}, bf16[320,256]{1,0:T(8,128)(2,1)S(1)}, u32[]{:S(2)}, u32[]{:S(2)}) collective-permute-start(bf16[320,256]{1,0:T(8,128)(2,1)S(1)} %get-tuple-element.78), channel_id=1, source_target_pairs={{0,1},{1,0},{2,3},{3,2},{4,5},{5,4},{6,7},{7,6},{8,9},{9,8},{10,11... | collective-permute-start | bytes 491528 | tf_op jit(solution)/shard_map/ppermute | solution.py:529
  20.0 8.5 %collective-permute-start.6 = (bf16[320,256]{1,0:T(8,128)(2,1)S(1)}, bf16[320,256]{1,0:T(8,128)(2,1)S(1)}, u32[]{:S(2)}, u32[]{:S(2)}) collective-permute-start(bf16[320,256]{1,0:T(8,128)(2,1)S(1)} %get-tuple-element.94), channel_id=1, source_target_pairs={{3,0},{2,1},{1,2},{0,3},{7,4},{6,5},{5,6},{4,7},{11,8},{10,9},{9,1... | collective-permute-start | bytes 491528 | tf_op jit(solution)/shard_map/ppermute | solution.py:70
  27.8 8.1 %collective-permute-start.7 = (bf16[320,256]{1,0:T(8,128)(2,1)S(1)}, bf16[320,256]{1,0:T(8,128)(2,1)S(1)}, u32[]{:S(2)}, u32[]{:S(2)}) collective-permute-start(bf16[320,256]{1,0:T(8,128)(2,1)S(1)} %get-tuple-element.96), channel_id=1, source_target_pairs={{3,0},{2,1},{1,2},{0,3},{7,4},{6,5},{5,6},{4,7},{11,8},{10,9},{9,1... | collective-permute-start | bytes 491528 | tf_op jit(solution)/shard_map/ppermute | solution.py:70
  28.6 11.3 %collective-permute-start.8 = (bf16[640,256]{1,0:T(8,128)(2,1)S(1)}, bf16[640,256]{1,0:T(8,128)(2,1)S(1)}, u32[]{:S(2)}, u32[]{:S(2)}) collective-permute-start(bf16[640,256]{1,0:T(8,128)(2,1)S(1)} %get-tuple-element.97), channel_id=1, source_target_pairs={{2,0},{3,1},{0,2},{1,3},{6,4},{7,5},{4,6},{5,7},{10,8},{11,9},{8,1... | collective-permute-start | bytes 983048 | tf_op jit(solution)/shard_map/ppermute | solution.py:70
  29.8 11.1 %collective-permute-start.9 = (bf16[640,256]{1,0:T(8,128)(2,1)S(1)}, bf16[640,256]{1,0:T(8,128)(2,1)S(1)}, u32[]{:S(2)}, u32[]{:S(2)}) collective-permute-start(bf16[640,256]{1,0:T(8,128)(2,1)S(1)} %get-tuple-element.98), channel_id=1, source_target_pairs={{1,0},{0,1},{3,2},{2,3},{5,4},{4,5},{7,6},{6,7},{9,8},{8,9},{11,10... | collective-permute-start | bytes 983048 | tf_op jit(solution)/shard_map/ppermute | solution.py:70
  31.3 12.9 %all-to-all-start = ((f32[32,4,128]{2,1,0:T(4,128)}), f32[32,4,128]{2,1,0:T(4,128)S(1)}, u32[]{:S(2)}, u32[]{:S(2)}) async-start(f32[32,4,128]{2,1,0:T(4,128)} %get-tuple-element.103), calls=%async_computation | async-start | bytes 131072 | tf_op jit(solution)/shard_map/all_to_all | solution.py:576

commit v17 on v14

--- a/solution.py
+++ b/solution.py
@@ -20,7 +20,8 @@
 USED = HEAD_DIM + 16
 HALF = HEAD_DIM // 2
 PIECES = 2
-PACK_KIB = 52 * 1024 + 600
+FIRST_PACK_KIB = 52 * 1024 + 1260
+PACK_KIB = 52 * 1024 - 400
 UNPACK_FLOPS = 20_000_000_000
 
 rope_base = 10000.0
@@ -105,15 +106,24 @@
     return jnp.concatenate([first * cosv + second * sinv, second * cosv - first * sinv], axis=0)
 
 
-def pack_kernel(closed, *refs):
+def phase_lanes(phase, model):
+    size = SPAN * HEAD_DIM
+    begin = phase * size // LANES * LANES
+    end = -(-(phase + 1) * size // LANES) * LANES
+    return begin, min(end, model)
+
+
+def pack_kernel(phase, closed, *refs):
     inputs, outs, held, turned, sems = refs[:4], refs[4:-3], refs[-3], refs[-2], refs[-1]
+    begin, end = phase_lanes(phase, inputs[0].shape[1])
     copies = [
-        pltpu.make_async_copy(source, held.at[number], sems.at[number])
+        pltpu.make_async_copy(source.at[:, begin:end], held.at[number], sems.at[number])
         for number, source in enumerate(inputs)
     ]
     for copy in copies:
         copy.start()
     me = lax.rem(lax.axis_index("tok"), SPAN)
+    inner = phase * SPAN * HEAD_DIM - begin
     steps = (
         [closed_step(slot) for slot in range(SPAN)]
         if closed
@@ -122,13 +132,10 @@
     for number, copy in enumerate(copies):
         copy.wait()
         turned[number] = held[number].T
-        for phase in range(OWN_HEADS):
-            for slot, step in enumerate(steps):
-                residue = me ^ step if closed else lax.rem(me + step, SPAN)
-                begin = pl.multiple_of((phase * SPAN + residue) * HEAD_DIM, 16)
-                outs[phase * len(steps) + slot][message_rows(number), :] = turned[
-                    number, pl.ds(begin, HEAD_DIM), :
-                ]
+        for out, step in zip(outs, steps):
+            residue = me ^ step if closed else lax.rem(me + step, SPAN)
+            rows = pl.ds(pl.multiple_of(inner + residue * HEAD_DIM, 16), HEAD_DIM)
+            out[message_rows(number), :] = turned[number, rows, :]
 
 
 def tables_kernel(images, count, tokd, lengths, widths, table, inverse, bias, *refs):
@@ -463,22 +470,27 @@
         return pltpu.CompilerParams(vmem_limit_bytes=int(mib * 1024 * 1024))
 
     inputs = (query_in[0], key_in[0], value_in[0], out_grad[0])
-    sends = pl.pallas_call(
-        functools.partial(pack_kernel, closed),
-        out_shape=[message] * (OWN_HEADS * slots),
-        in_specs=[hbm] * 4,
-        out_specs=[vmem] * (OWN_HEADS * slots),
-        scratch_shapes=[
-            pltpu.VMEM((4, tokd, model), jnp.bfloat16),
-            pltpu.VMEM((4, model, tokd), jnp.bfloat16),
-            pltpu.SemaphoreType.DMA((4,)),
-        ],
-        compiler_params=params(PACK_KIB / 1024),
-        name="pack_heads",
-    )(*inputs)
+    def pack(phase, kib, inputs):
+        begin, end = phase_lanes(phase, model)
+        return pl.pallas_call(
+            functools.partial(pack_kernel, phase, closed),
+            out_shape=[message] * slots,
+            in_specs=[hbm] * 4,
+            out_specs=[vmem] * slots,
+            scratch_shapes=[
+                pltpu.VMEM((4, tokd, end - begin), jnp.bfloat16),
+                pltpu.VMEM((4, end - begin, tokd), jnp.bfloat16),
+                pltpu.SemaphoreType.DMA((4,)),
+            ],
+            compiler_params=params(kib / 1024),
+            cost_estimate=pl.CostEstimate(flops=1_000_000, bytes_accessed=0, transcendentals=0),
+            name="pack_heads",
+        )(*inputs)
+
+    sends = [pack(0, FIRST_PACK_KIB, inputs)]
     rounds = trade_rounds(count)
-    first = [sends[0]] + [
-        lax.ppermute(send, "tok", pairs) for send, pairs in zip(sends[1:slots], rounds)
+    first = [sends[0][0]] + [
+        lax.ppermute(send, "tok", pairs) for send, pairs in zip(sends[0][1:], rounds)
     ]
     table_shape = jax.ShapeDtypeStruct((HALF, span), jnp.float32)
     mask_rows = -(-slots * (slots + 1) // 8) * 8
@@ -516,13 +528,16 @@
         return [list(pair) for pair in zip(results[:number], results[number:])]
 
     phases = tuple(range(OWN_HEADS))
-    own = stage_ahead(0, phases, [sends[phase * slots] for phase in phases])
+    tables, inputs = lax.optimization_barrier((tables, inputs))
+    for phase in phases[1:]:
+        sends.append(pack(phase, PACK_KIB, inputs))
+    own = stage_ahead(0, phases, [sent[0] for sent in sends])
     staged = [{0: pair} for pair in own]
-    got = [first] + [[sends[phase * slots]] for phase in phases[1:]]
+    got = [first] + [[sent[0]] for sent in sends[1:]]
     latest = own
     for slot in range(1, slots):
         for phase in phases[1:]:
-            send, latest = lax.optimization_barrier((sends[phase * slots + slot], latest))
+            send, latest = lax.optimization_barrier((sends[phase][slot], latest))
             got[phase].append(lax.ppermute(send, "tok", rounds[slot - 1]))
         if slot == 1:
             staged[0][0], staged[1][0] = latest
@@ -567,7 +582,7 @@
             ),
             name="attend_head",
         )(*tables, *got[phase], *(one for pair in staged[phase].values() for one in pair), *carried)
-        results, total, early = lax.optimization_barrier((results, total, early))
+        results[EARLY], early = lax.optimization_barrier((results[EARLY], early))
         early.append(send_back(results[EARLY], EARLY))
         carried = [total] + [results[slot] for slot in kept]
     tiles = lax.all_to_all(total, ("dp", "tok"), 0, 0, tiled=True)

time: 44.5 us -> 43.7 us (0.982)
  local copies, waits for them, and re-layouts: 0.03 us -> 2.09 us
  waiting for transfers between devices: 7.88 us -> 6.14 us
  starting transfers between devices: 21.1 us -> 19.5 us
    unnamed x10 -> x18, local copies, waits for them, and re-layouts: 0.03 us -> 2.09 us
    ppermute x3, waiting for transfers between devices: 1.75 us -> 0.01 us  [on_device(): lax.ppermute(send, 'tok', pairs)]
    ppermute x3, starting transfers between devices: 5.05 us -> 3.83 us  [on_device(): got[phase].append(lax.ppermute(send, 'tok', rounds[slot - 1]))]
    pallas_call x1 -> x2, Pallas kernels: 1.68 us -> 2.15 us  [pack(): pl.pallas_call(functools.partial(pack_kernel, phase, closed), out_shape=[...]
  transfers between devices with their start and end apart: 11 -> 11, of which waited for: 4 -> 2; matrix products, arithmetic and copies ran while one was open for 0% -> 0% of each run, Pallas kernels for 27% -> 29%
where the time goes in v17:
time: 43.7 us; the launch traced here: 43.4 us
  starting transfers between devices  19.5 us (45%)
  Pallas kernels  14.9 us (34%)
  waiting for transfers between devices  6.14 us (14%)
  local copies, waits for them, and re-layouts  2.09 us (5%)
  between operations  0.79 us (2%)
    pallas_call x2, Pallas kernels, on_device(): pl.pallas_call(functools.partial(attend_kernel, slots, tuple(staged[phase...  8.88 us
    ppermute x4, starting transfers between devices, send_back(): lax.ppermute(result, 'tok', [(target, source) for source, target in pairs])  6.32 us
    ppermute x3, starting transfers between devices, on_device(): lax.ppermute(send, 'tok', pairs)  4.67 us
    all_to_all x1, starting transfers between devices, on_device(): tiles = lax.all_to_all(total, ('dp', 'tok'), 0, 0, tiled=True)  4.67 us
    ppermute x4, waiting for transfers between devices, send_back(): lax.ppermute(result, 'tok', [(target, source) for source, target in pairs])  4.06 us
    ppermute x3, starting transfers between devices, on_device(): got[phase].append(lax.ppermute(send, 'tok', rounds[slot - 1]))  3.83 us
    pallas_call x2, Pallas kernels, pack(): pl.pallas_call(functools.partial(pack_kernel, phase, closed), out_shape=[...  2.15 us
    unnamed x18, local copies, waits for them, and re-layouts  2.09 us
  transfers between devices with their start and end apart: 11, of which 2 were waited for; matrix products, arithmetic and copies ran while one was open for 0% of the time, Pallas kernels for 29%

profile of v17, /device:TPU:0, one launch (start us, length us, event | category | flops | bytes accessed | tf_op | source)
XLA Modules:
  0.0 43.4 jit_solution(17370891369011291520)
XLA Ops:
  0.6 0.0 copy-start
  0.6 0.0 copy-start.1
  0.7 0.0 copy-start.2
  0.7 0.0 copy-start.3
  0.7 1.5 %pack_heads.3 = (bf16[320,256]{1,0:T(8,128)(2,1)S(1)}, bf16[320,256]{1,0:T(8,128)(2,1)S(1)}, bf16[320,256]{1,0:T(8,128)(2,1)S(1)}, bf16[320,256]{1,0:T(8,128)(2,1)S(1)}) custom-call(bf16[256,640]{1,0:T(8,128)(2,1)} %bitcast.8, bf16[256,640]{1,0:T(8,128)(2,1)} %bitcast.10, bf16[256,640]{1,0:T(8,128)(2,1)} %bitcast.12, bf16[256,640]{1,0:T(8,128)(2,1)} %bitcast.14), custom_call_target="tpu_custom_call" | custom-call | flops 1000000 | tf_op jit(solution)/shard_map/pack_heads/pallas_call | solution.py:475
  2.2 0.0 copy-start.4
  2.2 4.0 %collective-permute-start.1 = (bf16[320,256]{1,0:T(8,128)(2,1)S(1)}, bf16[320,256]{1,0:T(8,128)(2,1)S(1)}, u32[]{:S(2)}, u32[]{:S(2)}) collective-permute-start(bf16[320,256]{1,0:T(8,128)(2,1)S(1)} %get-tuple-element.86), channel_id=1, source_target_pairs={{0,3},{1,2},{2,1},{3,0},{4,7},{5,6},{6,5},{7,4},{8,11},{9,10},{10,... | collective-permute-start | bytes 491528 | tf_op jit(solution)/shard_map/ppermute | solution.py:493
  6.3 0.0 copy-start.5
  6.3 0.4 %collective-permute-start.3 = (bf16[320,256]{1,0:T(8,128)(2,1)S(1)}, bf16[320,256]{1,0:T(8,128)(2,1)S(1)}, u32[]{:S(2)}, u32[]{:S(2)}) collective-permute-start(bf16[320,256]{1,0:T(8,128)(2,1)S(1)} %get-tuple-element.91), channel_id=1, source_target_pairs={{0,2},{1,3},{2,0},{3,1},{4,6},{5,7},{6,4},{7,5},{8,10},{9,11},{10,... | collective-permute-start | bytes 491528 | tf_op jit(solution)/shard_map/ppermute | solution.py:493
  6.7 0.2 collective-permute-start.5
  6.9 0.0 copy-done.4
  6.9 0.0 copy-done.5
  6.9 0.7 %copy-done.6 = s32[1,4]{1,0:T(1,128)S(1)} copy-done((s32[1,4]{1,0:T(1,128)S(1)}, s32[1,4]{1,0:T(1,128)}, u32[]{:S(2)}) %copy-start.6) | copy-done | bytes 40
  7.6 0.0 copy-start.7
  7.6 0.7 %copy-done.7 = f32[40,128]{1,0:T(8,128)S(1)} copy-done((f32[40,128]{1,0:T(8,128)S(1)}, f32[40,128]{1,0:T(8,128)}, u32[]{:S(2)}) %copy-start.7) | copy-done | bytes 20504
  8.3 0.7 %copy-done.8 = s32[4,8]{1,0:T(4,128)S(1)} copy-done((s32[4,8]{1,0:T(4,128)S(1)}, s32[4,8]{1,0:T(4,128)}, u32[]{:S(2)}) %copy-start.8) | copy-done | bytes 152
  9.0 1.2 %rotary_tables.1 = (f32[40,1024]{1,0:T(8,128)S(1)}, f32[40,1024]{1,0:T(8,128)S(1)}, f32[24,256]{1,0:T(8,128)S(1)}, f32[160,128]{1,0:T(8,128)S(1)}) custom-call(s32[1,4]{1,0:T(1,128)S(1)} %copy-done.5, s32[1,4]{1,0:T(1,128)S(1)} %copy-done.6, s32[4,8]{1,0:T(4,128)S(1)} %copy-done.8, f32[40,128]{1,0:T(8,128)S(1)} %copy-done.7, bf16[3,640]{1,0:T(4,128)(2,1)S(1)} %copy-done.4), custom_call_target="tpu_custom_call" | custom-call | flops 26214400 | tf_op jit(solution)/shard_map/rotary_tables/pallas_call | solution.py:497
  10.2 0.0 copy-done
  10.3 0.0 copy-done.1
  10.3 0.0 copy-done.2
  10.3 0.0 copy-done.3
  10.3 0.6 %pack_heads.2 = (bf16[320,256]{1,0:T(8,128)(2,1)S(1)}, bf16[320,256]{1,0:T(8,128)(2,1)S(1)}, bf16[320,256]{1,0:T(8,128)(2,1)S(1)}, bf16[320,256]{1,0:T(8,128)(2,1)S(1)}) custom-call(bf16[256,640]{1,0:T(8,128)(2,1)S(1)} %bitcast.9, bf16[256,640]{1,0:T(8,128)(2,1)S(1)} %bitcast.11, bf16[256,640]{1,0:T(8,128)(2,1)S(1)} %bitcast.13, bf16[256,640]{1,0:T(8,128)(2,1)S(1)} %bitcast.15), custom_call_target="tpu_custom_call" | custom-call | flops 1000000 | tf_op jit(solution)/shard_map/pack_heads/pallas_call | solution.py:475
  10.9 0.2 stage_slot.3
  11.1 2.9 %collective-permute-start = (bf16[320,256]{1,0:T(8,128)(2,1)S(1)}, bf16[320,256]{1,0:T(8,128)(2,1)S(1)}, u32[]{:S(2)}, u32[]{:S(2)}) collective-permute-start(bf16[320,256]{1,0:T(8,128)(2,1)S(1)} %get-tuple-element.84), channel_id=1, source_target_pairs={{0,3},{1,2},{2,1},{3,0},{4,7},{5,6},{6,5},{7,4},{8,11},{9,10},{10,... | collective-permute-start | bytes 491528 | tf_op jit(solution)/shard_map/ppermute | solution.py:541
  14.1 0.0 collective-permute-done.1.refs_0_.refs_1_
  14.1 0.2 stage_slot.4
  14.3 0.5 %collective-permute-start.2 = (bf16[320,256]{1,0:T(8,128)(2,1)S(1)}, bf16[320,256]{1,0:T(8,128)(2,1)S(1)}, u32[]{:S(2)}, u32[]{:S(2)}) collective-permute-start(bf16[320,256]{1,0:T(8,128)(2,1)S(1)} %get-tuple-element.89), channel_id=1, source_target_pairs={{0,2},{1,3},{2,0},{3,1},{4,6},{5,7},{6,4},{7,5},{8,10},{9,11},{10,... | collective-permute-start | bytes 491528 | tf_op jit(solution)/shard_map/ppermute | solution.py:541
  14.7 0.0 collective-permute-done.3.refs_0_.refs_2_
  14.8 0.2 stage_slot.5
  14.9 0.4 collective-permute-start.4
  15.4 0.0 collective-permute-done.5.refs_3_
  15.4 4.2 %attend_head.2 = (bf16[640,256]{1,0:T(8,128)(2,1)S(1)}, bf16[320,256]{1,0:T(8,128)(2,1)S(1)}, bf16[640,256]{1,0:T(8,128)(2,1)S(1)}, bf16[640,256]{1,0:T(8,128)(2,1)S(1)}, f32[8,128]{1,0:T(8,128)S(1)}) custom-call(f32[40,1024]{1,0:T(8,128)S(1)} %get-tuple-element.69.cosv, f32[40,1024]{1,0:T(8,128)S(1)} %get-tuple-element.70.sinv, ...), custom_call_target="tpu_custom_call" | custom-call | flops 3221225472 | tf_op jit(solution)/shard_map/attend_head/pallas_call | solution.py:556
  19.6 2.8 %collective-permute-start.6 = (bf16[320,256]{1,0:T(8,128)(2,1)S(1)}, bf16[320,256]{1,0:T(8,128)(2,1)S(1)}, u32[]{:S(2)}, u32[]{:S(2)}) collective-permute-start(bf16[320,256]{1,0:T(8,128)(2,1)S(1)} %get-tuple-element.109), channel_id=1, source_target_pairs={{3,0},{2,1},{1,2},{0,3},{7,4},{6,5},{5,6},{4,7},{11,8},{10,9},{9,1... | collective-permute-start | bytes 491528 | tf_op jit(solution)/shard_map/ppermute | solution.py:71
  22.3 0.0 collective-permute-done.refs_1_
  22.3 0.0 collective-permute-done.2.refs_2_
  22.3 0.0 collective-permute-done.4.refs_3_
  22.3 4.7 %attend_head.3 = (bf16[640,256]{1,0:T(8,128)(2,1)S(1)}, bf16[320,256]{1,0:T(8,128)(2,1)S(1)}, bf16[640,256]{1,0:T(8,128)(2,1)S(1)}, bf16[640,256]{1,0:T(8,128)(2,1)S(1)}, f32[32,4,128]{2,1,0:T(4,128)}) custom-call(f32[40,1024]{1,0:T(8,128)S(1)} %get-tuple-element.69.cosv, f32[40,1024]{1,0:T(8,128)S(1)} %get-tuple-element.70.sinv, ...), custom_call_target="tpu_custom_call" | custom-call | flops 3221225472 | tf_op jit(solution)/shard_map/attend_head/pallas_call | solution.py:556
  27.0 0.6 %collective-permute-start.8 = (bf16[640,256]{1,0:T(8,128)(2,1)S(1)}, bf16[640,256]{1,0:T(8,128)(2,1)S(1)}, u32[]{:S(2)}, u32[]{:S(2)}) collective-permute-start(bf16[640,256]{1,0:T(8,128)(2,1)S(1)} %get-tuple-element.113), channel_id=1, source_target_pairs={{2,0},{3,1},{0,2},{1,3},{6,4},{7,5},{4,6},{5,7},{10,8},{11,9},{8,1... | collective-permute-start | bytes 983048 | tf_op jit(solution)/shard_map/ppermute | solution.py:71
  27.7 1.3 %collective-permute-start.9 = (bf16[640,256]{1,0:T(8,128)(2,1)S(1)}, bf16[640,256]{1,0:T(8,128)(2,1)S(1)}, u32[]{:S(2)}, u32[]{:S(2)}) collective-permute-start(bf16[640,256]{1,0:T(8,128)(2,1)S(1)} %get-tuple-element.114), channel_id=1, source_target_pairs={{1,0},{0,1},{3,2},{2,3},{5,4},{4,5},{7,6},{6,7},{9,8},{8,9},{11,10... | collective-permute-start | bytes 983048 | tf_op jit(solution)/shard_map/ppermute | solution.py:71
  29.0 0.0 collective-permute-done.6.refs_0_
  29.0 1.6 %collective-permute-start.7 = (bf16[320,256]{1,0:T(8,128)(2,1)S(1)}, bf16[320,256]{1,0:T(8,128)(2,1)S(1)}, u32[]{:S(2)}, u32[]{:S(2)}) collective-permute-start(bf16[320,256]{1,0:T(8,128)(2,1)S(1)} %get-tuple-element.111), channel_id=1, source_target_pairs={{3,0},{2,1},{1,2},{0,3},{7,4},{6,5},{5,6},{4,7},{11,8},{10,9},{9,1... | collective-permute-start | bytes 491528 | tf_op jit(solution)/shard_map/ppermute | solution.py:71
  30.6 4.7 %all-to-all-start = ((f32[32,4,128]{2,1,0:T(4,128)}), f32[32,4,128]{2,1,0:T(4,128)S(1)}, u32[]{:S(2)}, u32[]{:S(2)}) async-start(f32[32,4,128]{2,1,0:T(4,128)} %get-tuple-element.119), calls=%async_computation | async-start | bytes 131072 | tf_op jit(solution)/shard_map/all_to_all | solution.py:588
  35.3 4.1 %collective-permute-done.7.refs_1_ = bf16[320,256]{1,0:T(8,128)(2,1)S(1)} collective-permute-done((bf16[320,256]{1,0:T(8,128)(2,1)S(1)}, bf16[320,256]{1,0:T(8,128)(2,1)S(1)}, u32[]{:S(2)}, u32[]{:S(2)}) %collective-permute-start.7) | collective-permute-done | bytes 163872 | tf_op jit(solution)/shard_map/ppermute | solution.py:71
  39.3 0.0 collective-permute-done.8.refs_3_
  39.3 0.0 collective-permute-done.9.refs_4_
  39.3 1.3 %unpack_heads.1 = (bf16[256,640]{1,0:T(8,128)(2,1)}, bf16[256,640]{1,0:T(8,128)(2,1)}, bf16[256,640]{1,0:T(8,128)(2,1)}, bf16[256,640]{1,0:T(8,128)(2,1)}) custom-call(bf16[320,256]{1,0:T(8,128)(2,1)S(1)} %collective-permute-done.6.refs_0_, bf16[320,256]{1,0:T(8,128)(2,1)S(1)} %collective-permute-done.7.refs_1_, ...), custom_call_target="tpu_custom_call" | custom-call | flops 20000000000 | tf_op jit(solution)/shard_map/unpack_heads/pallas_call | solution.py:591
  40.7 2.1 %all-to-all-done.tiles = f32[32,4,128]{2,1,0:T(4,128)S(1)} async-done(((f32[32,4,128]{2,1,0:T(4,128)}), f32[32,4,128]{2,1,0:T(4,128)S(1)}, u32[]{:S(2)}, u32[]{:S(2)}) %all-to-all-start) | async-done | bytes 65568 | tf_op jit(solution)/shard_map/all_to_all | solution.py:588
  42.7 0.7 %bias_sums.1 = f32[3,640]{1,0:T(4,128)} custom-call(f32[32,4,128]{2,1,0:T(4,128)S(1)} %all-to-all-done.tiles), custom_call_target="tpu_custom_call" | custom-call | tf_op jit(solution)/shard_map/bias_sums/pallas_call | solution.py:606
  (2 shorter events, 0.0 us)
Async XLA Ops:
  0.6 9.6 %copy-start = (bf16[1,256,640]{2,1,0:T(8,128)(2,1)S(1)}, bf16[1,256,640]{2,1,0:T(8,128)(2,1)}, u32[]{:S(2)}) copy-start(bf16[1,256,640]{2,1,0:T(8,128)(2,1)} %param.9) | copy-start | bytes 983044
  0.6 9.6 %copy-start.1 = (bf16[1,256,640]{2,1,0:T(8,128)(2,1)S(1)}, bf16[1,256,640]{2,1,0:T(8,128)(2,1)}, u32[]{:S(2)}) copy-start(bf16[1,256,640]{2,1,0:T(8,128)(2,1)} %param.10) | copy-start | bytes 983044
  0.7 9.6 %copy-start.2 = (bf16[1,256,640]{2,1,0:T(8,128)(2,1)S(1)}, bf16[1,256,640]{2,1,0:T(8,128)(2,1)}, u32[]{:S(2)}) copy-start(bf16[1,256,640]{2,1,0:T(8,128)(2,1)} %param.11) | copy-start | bytes 983044
  0.7 9.6 %copy-start.3 = (bf16[1,256,640]{2,1,0:T(8,128)(2,1)S(1)}, bf16[1,256,640]{2,1,0:T(8,128)(2,1)}, u32[]{:S(2)}) copy-start(bf16[1,256,640]{2,1,0:T(8,128)(2,1)} %param.12) | copy-start | bytes 983044
  2.2 4.7 %copy-start.4 = (bf16[3,640]{1,0:T(4,128)(2,1)S(1)}, bf16[3,640]{1,0:T(4,128)(2,1)}, u32[]{:S(2)}) copy-start(bf16[3,640]{1,0:T(4,128)(2,1)} %bias.1) | copy-start | bytes 11524
  2.2 11.8 %collective-permute-start.1 = (bf16[320,256]{1,0:T(8,128)(2,1)S(1)}, bf16[320,256]{1,0:T(8,128)(2,1)S(1)}, u32[]{:S(2)}, u32[]{:S(2)}) collective-permute-start(bf16[320,256]{1,0:T(8,128)(2,1)S(1)} %get-tuple-element.86), channel_id=1, source_target_pairs={{0,3},{1,2},{2,1},{3,0},{4,7},{5,6},{6,5},{7,4},{8,11},{9,10},{10,... | collective-permute-start | bytes 491528 | tf_op jit(solution)/shard_map/ppermute | solution.py:493
  6.3 0.7 %copy-start.5 = (s32[1,4]{1,0:T(1,128)S(1)}, s32[1,4]{1,0:T(1,128)}, u32[]{:S(2)}) copy-start(s32[1,4]{1,0:T(1,128)} %lengths.1) | copy-start | bytes 52
  6.3 8.5 %collective-permute-start.3 = (bf16[320,256]{1,0:T(8,128)(2,1)S(1)}, bf16[320,256]{1,0:T(8,128)(2,1)S(1)}, u32[]{:S(2)}, u32[]{:S(2)}) collective-permute-start(bf16[320,256]{1,0:T(8,128)(2,1)S(1)} %get-tuple-element.91), channel_id=1, source_target_pairs={{0,2},{1,3},{2,0},{3,1},{4,6},{5,7},{6,4},{7,5},{8,10},{9,11},{10,... | collective-permute-start | bytes 491528 | tf_op jit(solution)/shard_map/ppermute | solution.py:493
  6.7 8.7 %collective-permute-start.5 = (bf16[320,256]{1,0:T(8,128)(2,1)S(1)}, bf16[320,256]{1,0:T(8,128)(2,1)S(1)}, u32[]{:S(2)}, u32[]{:S(2)}) collective-permute-start(bf16[320,256]{1,0:T(8,128)(2,1)S(1)} %get-tuple-element.97), channel_id=1, source_target_pairs={{0,1},{1,0},{2,3},{3,2},{4,5},{5,4},{6,7},{7,6},{8,9},{9,8},{10,11... | collective-permute-start | bytes 491528 | tf_op jit(solution)/shard_map/ppermute | solution.py:493
  6.9 0.7 %copy-start.6 = (s32[1,4]{1,0:T(1,128)S(1)}, s32[1,4]{1,0:T(1,128)}, u32[]{:S(2)}) copy-start(s32[1,4]{1,0:T(1,128)} %widths.1) | copy-start | bytes 52
  7.6 0.7 %copy-start.7 = (f32[40,128]{1,0:T(8,128)S(1)}, f32[40,128]{1,0:T(8,128)}, u32[]{:S(2)}) copy-start(f32[40,128]{1,0:T(8,128)} %constant.5.clone.inverse) | copy-start | bytes 61444
  8.3 0.7 %copy-start.8 = (s32[4,8]{1,0:T(4,128)S(1)}, s32[4,8]{1,0:T(4,128)}, u32[]{:S(2)}) copy-start(s32[4,8]{1,0:T(4,128)} %constant.4.clone.table) | copy-start | bytes 388
  11.1 11.2 %collective-permute-start = (bf16[320,256]{1,0:T(8,128)(2,1)S(1)}, bf16[320,256]{1,0:T(8,128)(2,1)S(1)}, u32[]{:S(2)}, u32[]{:S(2)}) collective-permute-start(bf16[320,256]{1,0:T(8,128)(2,1)S(1)} %get-tuple-element.84), channel_id=1, source_target_pairs={{0,3},{1,2},{2,1},{3,0},{4,7},{5,6},{6,5},{7,4},{8,11},{9,10},{10,... | collective-permute-start | bytes 491528 | tf_op jit(solution)/shard_map/ppermute | solution.py:541
  14.3 8.1 %collective-permute-start.2 = (bf16[320,256]{1,0:T(8,128)(2,1)S(1)}, bf16[320,256]{1,0:T(8,128)(2,1)S(1)}, u32[]{:S(2)}, u32[]{:S(2)}) collective-permute-start(bf16[320,256]{1,0:T(8,128)(2,1)S(1)} %get-tuple-element.89), channel_id=1, source_target_pairs={{0,2},{1,3},{2,0},{3,1},{4,6},{5,7},{6,4},{7,5},{8,10},{9,11},{10,... | collective-permute-start | bytes 491528 | tf_op jit(solution)/shard_map/ppermute | solution.py:541
  14.9 7.4 %collective-permute-start.4 = (bf16[320,256]{1,0:T(8,128)(2,1)S(1)}, bf16[320,256]{1,0:T(8,128)(2,1)S(1)}, u32[]{:S(2)}, u32[]{:S(2)}) collective-permute-start(bf16[320,256]{1,0:T(8,128)(2,1)S(1)} %get-tuple-element.94), channel_id=1, source_target_pairs={{0,1},{1,0},{2,3},{3,2},{4,5},{5,4},{6,7},{7,6},{8,9},{9,8},{10,11... | collective-permute-start | bytes 491528 | tf_op jit(solution)/shard_map/ppermute | solution.py:541
  19.6 9.4 %collective-permute-start.6 = (bf16[320,256]{1,0:T(8,128)(2,1)S(1)}, bf16[320,256]{1,0:T(8,128)(2,1)S(1)}, u32[]{:S(2)}, u32[]{:S(2)}) collective-permute-start(bf16[320,256]{1,0:T(8,128)(2,1)S(1)} %get-tuple-element.109), channel_id=1, source_target_pairs={{3,0},{2,1},{1,2},{0,3},{7,4},{6,5},{5,6},{4,7},{11,8},{10,9},{9,1... | collective-permute-start | bytes 491528 | tf_op jit(solution)/shard_map/ppermute | solution.py:71
  27.0 12.3 %collective-permute-start.8 = (bf16[640,256]{1,0:T(8,128)(2,1)S(1)}, bf16[640,256]{1,0:T(8,128)(2,1)S(1)}, u32[]{:S(2)}, u32[]{:S(2)}) collective-permute-start(bf16[640,256]{1,0:T(8,128)(2,1)S(1)} %get-tuple-element.113), channel_id=1, source_target_pairs={{2,0},{3,1},{0,2},{1,3},{6,4},{7,5},{4,6},{5,7},{10,8},{11,9},{8,1... | collective-permute-start | bytes 983048 | tf_op jit(solution)/shard_map/ppermute | solution.py:71
  27.7 11.7 %collective-permute-start.9 = (bf16[640,256]{1,0:T(8,128)(2,1)S(1)}, bf16[640,256]{1,0:T(8,128)(2,1)S(1)}, u32[]{:S(2)}, u32[]{:S(2)}) collective-permute-start(bf16[640,256]{1,0:T(8,128)(2,1)S(1)} %get-tuple-element.114), channel_id=1, source_target_pairs={{1,0},{0,1},{3,2},{2,3},{5,4},{4,5},{7,6},{6,7},{9,8},{8,9},{11,10... | collective-permute-start | bytes 983048 | tf_op jit(solution)/shard_map/ppermute | solution.py:71
  29.0 10.3 %collective-permute-start.7 = (bf16[320,256]{1,0:T(8,128)(2,1)S(1)}, bf16[320,256]{1,0:T(8,128)(2,1)S(1)}, u32[]{:S(2)}, u32[]{:S(2)}) collective-permute-start(bf16[320,256]{1,0:T(8,128)(2,1)S(1)} %get-tuple-element.111), channel_id=1, source_target_pairs={{3,0},{2,1},{1,2},{0,3},{7,4},{6,5},{5,6},{4,7},{11,8},{10,9},{9,1... | collective-permute-start | bytes 491528 | tf_op jit(solution)/shard_map/ppermute | solution.py:71
  30.6 12.1 %all-to-all-start = ((f32[32,4,128]{2,1,0:T(4,128)}), f32[32,4,128]{2,1,0:T(4,128)S(1)}, u32[]{:S(2)}, u32[]{:S(2)}) async-start(f32[32,4,128]{2,1,0:T(4,128)} %get-tuple-element.119), calls=%async_computation | async-start | bytes 131072 | tf_op jit(solution)/shard_map/all_to_all | solution.py:588

commit v18 on v17

--- a/solution.py
+++ b/solution.py
@@ -1,4 +1,5 @@
 import functools
+import math
 
 import jax
 import jax.numpy as jnp
@@ -21,7 +22,7 @@
 HALF = HEAD_DIM // 2
 PIECES = 2
 FIRST_PACK_KIB = 52 * 1024 + 1260
-PACK_KIB = 52 * 1024 - 400
+PREPARE_KIB = 52 * 1024 + 300
 UNPACK_FLOPS = 20_000_000_000
 
 rope_base = 10000.0
@@ -113,8 +114,7 @@
     return begin, min(end, model)
 
 
-def pack_kernel(phase, closed, *refs):
-    inputs, outs, held, turned, sems = refs[:4], refs[4:-3], refs[-3], refs[-2], refs[-1]
+def fetch(phase, inputs, held, sems):
     begin, end = phase_lanes(phase, inputs[0].shape[1])
     copies = [
         pltpu.make_async_copy(source.at[:, begin:end], held.at[number], sems.at[number])
@@ -122,8 +122,12 @@
     ]
     for copy in copies:
         copy.start()
+    return copies
+
+
+def pack(phase, closed, copies, outs, held, turned):
     me = lax.rem(lax.axis_index("tok"), SPAN)
-    inner = phase * SPAN * HEAD_DIM - begin
+    inner = phase * SPAN * HEAD_DIM % LANES
     steps = (
         [closed_step(slot) for slot in range(SPAN)]
         if closed
@@ -138,16 +142,34 @@
             out[message_rows(number), :] = turned[number, rows, :]
 
 
-def tables_kernel(images, count, tokd, lengths, widths, table, inverse, bias, *refs):
-    cos_out, sin_out, mask_out, bias_out, turned = refs
+def pack_kernel(closed, *refs):
+    inputs, outs, (held, turned, sems) = refs[:4], refs[4:-3], refs[-3:]
+    pack(0, closed, fetch(0, inputs, held, sems), outs, held, turned)
+
+
+def prepare_kernel(slots, images, count, tokd, lengths, widths, *refs):
+    closed = is_closed(count)
+    if not closed:
+        table, *refs = refs
+    later = OWN_HEADS - 1
+    bias, *inputs, own = refs[:6]
+    cos_out, sin_out, mask_out, bias_out, *refs = refs[6:]
+    messages, refs = refs[: later * slots], refs[later * slots :]
+    turned_out, plain_out = refs[:OWN_HEADS], refs[OWN_HEADS : 2 * OWN_HEADS]
+    held, turned, sems, columns = refs[2 * OWN_HEADS :]
+    copies = [
+        fetch(phase + 1, inputs, held.at[phase], sems.at[phase]) for phase in range(later)
+    ]
     me = lax.axis_index("tok")
     residue = lax.rem(me, SPAN)
-    slots = table.shape[0]
     spot = lax.broadcasted_iota(jnp.int32, (HALF, tokd), 1)
-    by_row = lax.broadcasted_iota(jnp.int32, (HALF, tokd), 0) < HALF // 2
+    feature = lax.broadcasted_iota(jnp.int32, (HALF, tokd), 0)
+    by_row = feature < HALF // 2
+    feature = jnp.where(by_row, feature, feature - HALF // 2).astype(jnp.float32)
+    inverse = jnp.exp(feature * (-math.log(rope_base) / (HALF // 2)))
     ids = []
     for slot in range(slots):
-        block = table[slot, me]
+        block = me - residue + (residue ^ closed_step(slot)) if closed else table[slot, me]
         image, start = image_of(block, lengths, images)
         handled = (block >= 0) & (handler_of(start, residue, count) == me)
         ids.append(jnp.where(handled, image, -1 - slot))
@@ -157,7 +179,7 @@
         local = spot + (block - start) * tokd
         rowpos = lax.shift_right_logical(local, jnp.broadcast_to(shift, local.shape))
         colpos = local & (width - 1)
-        angle = jnp.where(by_row, rowpos, colpos).astype(jnp.float32) * inverse[:, 0:1]
+        angle = jnp.where(by_row, rowpos, colpos).astype(jnp.float32) * inverse
         cos_out[:, slot * tokd : (slot + 1) * tokd] = jnp.cos(angle)
         sin_out[:, slot * tokd : (slot + 1) * tokd] = jnp.sin(angle)
     for slot in range(slots):
@@ -170,10 +192,15 @@
         mask_out[row : row + 1, :] = jnp.full((1, tokd), live, jnp.float32)
     plain = bias[...].astype(jnp.float32)
     rest = jnp.zeros((LANES - plain.shape[0], plain.shape[1]), jnp.float32)
-    turned[...] = jnp.concatenate([plain, rest], axis=0).T
+    columns[...] = jnp.concatenate([plain, rest], axis=0).T
     for phase in range(OWN_HEADS):
         begin = pl.multiple_of((phase * SPAN + residue) * HEAD_DIM, 16)
-        bias_out[phase * HEAD_DIM : (phase + 1) * HEAD_DIM, :] = turned[pl.ds(begin, HEAD_DIM), :]
+        bias_out[phase * HEAD_DIM : (phase + 1) * HEAD_DIM, :] = columns[pl.ds(begin, HEAD_DIM), :]
+    for phase in range(later):
+        outs = messages[phase * slots : (phase + 1) * slots]
+        pack(phase + 1, closed, copies[phase], outs, held.at[phase], turned.at[phase])
+    owns = [own] + [messages[phase * slots] for phase in range(later)]
+    stage_all(0, range(OWN_HEADS), tokd, cos_out, sin_out, bias_out, owns, turned_out, plain_out)
 
 
 def stage(slot, tokd, message, cosv, sinv, bias):
@@ -196,9 +223,7 @@
     ]
 
 
-def stage_kernel(slot, phases, tokd, cosv, sinv, bias, *refs):
-    count = len(phases)
-    msgs, turned, plain = refs[:count], refs[count : 2 * count], refs[2 * count :]
+def stage_all(slot, phases, tokd, cosv, sinv, bias, msgs, turned, plain):
     for number, phase in enumerate(phases):
         own_bias = bias[phase * HEAD_DIM : (phase + 1) * HEAD_DIM, :]
         values = stage(slot, tokd, msgs[number], cosv, sinv, own_bias)
@@ -206,6 +231,12 @@
             turned[number][tensor] = value
             if tensor > 0:
                 plain[number][tensor - 1] = value.T
+
+
+def stage_kernel(slot, phases, tokd, cosv, sinv, bias, *refs):
+    count = len(phases)
+    msgs, turned, plain = refs[:count], refs[count : 2 * count], refs[2 * count :]
+    stage_all(slot, phases, tokd, cosv, sinv, bias, msgs, turned, plain)
 
 
 def attend_kernel(slots, staged, closed, tokd, head, factor, cosv, sinv, masks, bias, *refs):
@@ -453,10 +484,6 @@
     sources, targets = trade_tables(count)
     slots = sources.shape[0]
     span = slots * tokd
-    table = jnp.asarray(sources)
-    quarter = HEAD_DIM // 4
-    inverse = rope_base ** (-np.arange(quarter, dtype=np.float64) / quarter)
-    inverse = jnp.asarray(np.tile(np.tile(inverse, 2)[:, None], (1, LANES)), jnp.float32)
     smem = pl.BlockSpec(memory_space=pltpu.SMEM)
     vmem = pl.BlockSpec(memory_space=pltpu.VMEM)
     hbm = pl.BlockSpec(memory_space=pltpu.HBM)
@@ -470,53 +497,66 @@
         return pltpu.CompilerParams(vmem_limit_bytes=int(mib * 1024 * 1024))
 
     inputs = (query_in[0], key_in[0], value_in[0], out_grad[0])
-    def pack(phase, kib, inputs):
-        begin, end = phase_lanes(phase, model)
-        return pl.pallas_call(
-            functools.partial(pack_kernel, phase, closed),
-            out_shape=[message] * slots,
-            in_specs=[hbm] * 4,
-            out_specs=[vmem] * slots,
-            scratch_shapes=[
-                pltpu.VMEM((4, tokd, end - begin), jnp.bfloat16),
-                pltpu.VMEM((4, end - begin, tokd), jnp.bfloat16),
-                pltpu.SemaphoreType.DMA((4,)),
-            ],
-            compiler_params=params(kib / 1024),
-            cost_estimate=pl.CostEstimate(flops=1_000_000, bytes_accessed=0, transcendentals=0),
-            name="pack_heads",
-        )(*inputs)
-
-    sends = [pack(0, FIRST_PACK_KIB, inputs)]
+    later = OWN_HEADS - 1
+    lanes = max(end - begin for begin, end in (phase_lanes(p, model) for p in range(OWN_HEADS)))
+    own_sends = pl.pallas_call(
+        functools.partial(pack_kernel, closed),
+        out_shape=[message] * slots,
+        in_specs=[hbm] * 4,
+        out_specs=[vmem] * slots,
+        scratch_shapes=[
+            pltpu.VMEM((4, tokd, lanes), jnp.bfloat16),
+            pltpu.VMEM((4, lanes, tokd), jnp.bfloat16),
+            pltpu.SemaphoreType.DMA((4,)),
+        ],
+        compiler_params=params(FIRST_PACK_KIB / 1024),
+        name="pack_heads",
+    )(*inputs)
+    sends = [own_sends]
     rounds = trade_rounds(count)
     first = [sends[0][0]] + [
         lax.ppermute(send, "tok", pairs) for send, pairs in zip(sends[0][1:], rounds)
     ]
     table_shape = jax.ShapeDtypeStruct((HALF, span), jnp.float32)
     mask_rows = -(-slots * (slots + 1) // 8) * 8
-    tables = pl.pallas_call(
-        functools.partial(tables_kernel, images, count, tokd),
-        out_shape=[table_shape] * 2
+    turned_shape = jax.ShapeDtypeStruct((3, LANES, tokd), jnp.bfloat16)
+    plain_shape = jax.ShapeDtypeStruct((2, tokd, LANES), jnp.bfloat16)
+    places = [] if closed else [jnp.asarray(sources)]
+    out_shape = (
+        [table_shape] * 2
         + [
             jax.ShapeDtypeStruct((mask_rows, tokd), jnp.float32),
             jax.ShapeDtypeStruct((OWN_HEADS * HEAD_DIM, LANES), jnp.float32),
+        ]
+        + [message] * (later * slots)
+        + [turned_shape] * OWN_HEADS
+        + [plain_shape] * OWN_HEADS
+    )
+    prepared = pl.pallas_call(
+        functools.partial(prepare_kernel, slots, images, count, tokd),
+        out_shape=out_shape,
+        in_specs=[smem] * (2 + len(places)) + [vmem] + [hbm] * 4 + [vmem],
+        out_specs=[vmem] * len(out_shape),
+        scratch_shapes=[
+            pltpu.VMEM((later, 4, tokd, lanes), jnp.bfloat16),
+            pltpu.VMEM((later, 4, lanes, tokd), jnp.bfloat16),
+            pltpu.SemaphoreType.DMA((later, 4)),
+            pltpu.VMEM((model, LANES), jnp.float32),
         ],
-        in_specs=[smem, smem, smem, vmem, vmem],
-        out_specs=[vmem] * 4,
-        scratch_shapes=[pltpu.VMEM((model, LANES), jnp.float32)],
-        compiler_params=params(16),
-        cost_estimate=pl.CostEstimate(
-            flops=span * LANES * 200, bytes_accessed=0, transcendentals=0
-        ),
-        name="rotary_tables",
-    )(lengths, widths, table, inverse, bias)
+        compiler_params=params(PREPARE_KIB / 1024),
+        cost_estimate=pl.CostEstimate(flops=1_000_000, bytes_accessed=0, transcendentals=0),
+        name="prepare",
+    )(lengths, widths, *places, bias, *inputs, sends[0][0])
+    tables, prepared = prepared[:4], prepared[4:]
+    for phase in range(later):
+        sends.append(prepared[phase * slots : (phase + 1) * slots])
+    prepared = prepared[later * slots :]
 
     def stage_ahead(slot, phases, messages):
         number = len(phases)
         results = pl.pallas_call(
             functools.partial(stage_kernel, slot, phases, tokd),
-            out_shape=[jax.ShapeDtypeStruct((3, LANES, tokd), jnp.bfloat16)] * number
-            + [jax.ShapeDtypeStruct((2, tokd, LANES), jnp.bfloat16)] * number,
+            out_shape=[turned_shape] * number + [plain_shape] * number,
             in_specs=[vmem] * (3 + number),
             out_specs=[vmem] * (2 * number),
             compiler_params=params(16),
@@ -528,10 +568,7 @@
         return [list(pair) for pair in zip(results[:number], results[number:])]
 
     phases = tuple(range(OWN_HEADS))
-    tables, inputs = lax.optimization_barrier((tables, inputs))
-    for phase in phases[1:]:
-        sends.append(pack(phase, PACK_KIB, inputs))
-    own = stage_ahead(0, phases, [sent[0] for sent in sends])
+    own = [[prepared[phase], prepared[OWN_HEADS + phase]] for phase in phases]
     staged = [{0: pair} for pair in own]
     got = [first] + [[sent[0]] for sent in sends[1:]]
     latest = own

time: 43.7 us -> 44.2 us (1.011)
  waiting for transfers between devices: 6.14 us -> 8.59 us
  local copies, waits for them, and re-layouts: 2.09 us -> 0.48 us
  starting transfers between devices: 19.5 us -> 18.6 us
  Pallas kernels: 14.9 us -> 15.6 us
    ppermute x3, waiting for transfers between devices: 0.01 us -> 1.74 us  [on_device(): lax.ppermute(send, 'tok', pairs)]
    unnamed x18 -> x10, local copies, waits for them, and re-layouts: 2.09 us -> 0.48 us
    pallas_call x3 -> x2, Pallas kernels: 3.4 us -> 4.3 us  [the longest x1 2.84 us: on_device(): pl.pallas_call(functools.partial(prepare_kernel, slots, images, count, to...]
    ppermute x4, waiting for transfers between devices: 4.06 us -> 4.77 us  [send_back(): lax.ppermute(result, 'tok', [(target, source) for source, target in pairs])]
    all_to_all x1, starting transfers between devices: 4.67 us -> 4.06 us  [on_device(): tiles = lax.all_to_all(total, ('dp', 'tok'), 0, 0, tiled=True)]
    ppermute x3, starting transfers between devices: 3.83 us -> 3.26 us  [on_device(): got[phase].append(lax.ppermute(send, 'tok', rounds[slot - 1]))]
  transfers between devices with their start and end apart: 11 -> 11, of which waited for: 2 -> 4; matrix products, arithmetic and copies ran while one was open for 0% -> 0% of each run, Pallas kernels for 29% -> 31%
where the time goes in v18:
time: 44.2 us; the launch traced here: 44 us
  starting transfers between devices  18.6 us (42%)
  Pallas kernels  15.6 us (35%)
  waiting for transfers between devices  8.59 us (19%)
  between operations  0.73 us (2%)
  local copies, waits for them, and re-layouts  0.48 us (1%)
    pallas_call x2, Pallas kernels, on_device(): pl.pallas_call(functools.partial(attend_kernel, slots, tuple(staged[phase...  8.9 us
    ppermute x4, starting transfers between devices, send_back(): lax.ppermute(result, 'tok', [(target, source) for source, target in pairs])  6.61 us
    ppermute x4, waiting for transfers between devices, send_back(): lax.ppermute(result, 'tok', [(target, source) for source, target in pairs])  4.77 us
    ppermute x3, starting transfers between devices, on_device(): lax.ppermute(send, 'tok', pairs)  4.66 us
    all_to_all x1, starting transfers between devices, on_device(): tiles = lax.all_to_all(total, ('dp', 'tok'), 0, 0, tiled=True)  4.06 us
    ppermute x3, starting transfers between devices, on_device(): got[phase].append(lax.ppermute(send, 'tok', rounds[slot - 1]))  3.26 us
    pallas_call x1, Pallas kernels, on_device(): pl.pallas_call(functools.partial(prepare_kernel, slots, images, count, to...  2.84 us
    all_to_all x1, waiting for transfers between devices, on_device(): tiles = lax.all_to_all(total, ('dp', 'tok'), 0, 0, tiled=True)  2.07 us
  transfers between devices with their start and end apart: 11, of which 4 were waited for; matrix products, arithmetic and copies ran while one was open for 0% of the time, Pallas kernels for 31%

profile of v18, /device:TPU:0, one launch (start us, length us, event | category | flops | bytes accessed | tf_op | source)
XLA Modules:
  0.0 44.0 jit_solution(12529379186420385302)
XLA Ops:
  0.6 1.5 %pack_heads.1 = (bf16[320,256]{1,0:T(8,128)(2,1)S(1)}, bf16[320,256]{1,0:T(8,128)(2,1)S(1)}, bf16[320,256]{1,0:T(8,128)(2,1)S(1)}, bf16[320,256]{1,0:T(8,128)(2,1)S(1)}) custom-call(bf16[256,640]{1,0:T(8,128)(2,1)} %bitcast.8, bf16[256,640]{1,0:T(8,128)(2,1)} %bitcast.10, bf16[256,640]{1,0:T(8,128)(2,1)} %bitcast.12, bf16[256,640]{1,0:T(8,128)(2,1)} %bitcast.14), custom_call_target="tpu_custom_call" | custom-call | tf_op jit(solution)/shard_map/pack_heads/pallas_call | solution.py:502
  2.1 0.0 copy-start
  2.1 4.0 %collective-permute-start.1 = (bf16[320,256]{1,0:T(8,128)(2,1)S(1)}, bf16[320,256]{1,0:T(8,128)(2,1)S(1)}, u32[]{:S(2)}, u32[]{:S(2)}) collective-permute-start(bf16[320,256]{1,0:T(8,128)(2,1)S(1)} %get-tuple-element.70), channel_id=1, source_target_pairs={{0,3},{1,2},{2,1},{3,0},{4,7},{5,6},{6,5},{7,4},{8,11},{9,10},{10,... | collective-permute-start | bytes 491528 | tf_op jit(solution)/shard_map/ppermute | solution.py:518
  6.1 0.4 %collective-permute-start.3 = (bf16[320,256]{1,0:T(8,128)(2,1)S(1)}, bf16[320,256]{1,0:T(8,128)(2,1)S(1)}, u32[]{:S(2)}, u32[]{:S(2)}) collective-permute-start(bf16[320,256]{1,0:T(8,128)(2,1)S(1)} %get-tuple-element.75), channel_id=1, source_target_pairs={{0,2},{1,3},{2,0},{3,1},{4,6},{5,7},{6,4},{7,5},{8,10},{9,11},{10,... | collective-permute-start | bytes 491528 | tf_op jit(solution)/shard_map/ppermute | solution.py:518
  6.6 0.0 copy-start.1
  6.6 0.0 copy-start.2
  6.6 0.2 collective-permute-start.5
  6.8 0.0 copy-done
  6.8 0.4 %copy-done.1 = s32[1,4]{1,0:T(1,128)S(1)} copy-done((s32[1,4]{1,0:T(1,128)S(1)}, s32[1,4]{1,0:T(1,128)}, u32[]{:S(2)}) %copy-start.1) | copy-done | bytes 40
  7.2 0.0 copy-done.2
  7.2 2.8 %prepare.1 = (f32[40,1024]{1,0:T(8,128)S(1)}, f32[40,1024]{1,0:T(8,128)S(1)}, f32[24,256]{1,0:T(8,128)S(1)}, f32[160,128]{1,0:T(8,128)S(1)}, bf16[320,256]{1,0:T...) custom-call(s32[1,4]{1,0:T(1,128)S(1)} %copy-done.1, ...), custom_call_target="tpu_custom_call" | custom-call | flops 1000000 | tf_op jit(solution)/shard_map/prepare/pallas_call | solution.py:535
  10.1 2.5 %collective-permute-start = (bf16[320,256]{1,0:T(8,128)(2,1)S(1)}, bf16[320,256]{1,0:T(8,128)(2,1)S(1)}, u32[]{:S(2)}, u32[]{:S(2)}) collective-permute-start(bf16[320,256]{1,0:T(8,128)(2,1)S(1)} %get-tuple-element.68), channel_id=1, source_target_pairs={{0,3},{1,2},{2,1},{3,0},{4,7},{5,6},{6,5},{7,4},{8,11},{9,10},{10,... | collective-permute-start | bytes 491528 | tf_op jit(solution)/shard_map/ppermute | solution.py:578
  12.6 0.0 collective-permute-done.1.refs_0_.refs_1_
  12.6 0.2 stage_slot.2
  12.8 0.0 copy-start.4
  12.8 0.7 %collective-permute-start.2 = (bf16[320,256]{1,0:T(8,128)(2,1)S(1)}, bf16[320,256]{1,0:T(8,128)(2,1)S(1)}, u32[]{:S(2)}, u32[]{:S(2)}) collective-permute-start(bf16[320,256]{1,0:T(8,128)(2,1)S(1)} %get-tuple-element.73), channel_id=1, source_target_pairs={{0,2},{1,3},{2,0},{3,1},{4,6},{5,7},{6,4},{7,5},{8,10},{9,11},{10,... | collective-permute-start | bytes 491528 | tf_op jit(solution)/shard_map/ppermute | solution.py:578
  13.4 1.7 %collective-permute-done.3.refs_0_.refs_2_ = bf16[320,256]{1,0:T(8,128)(2,1)S(1)} collective-permute-done((bf16[320,256]{1,0:T(8,128)(2,1)S(1)}, bf16[320,256]{1,0:T(8,128)(2,1)S(1)}, u32[]{:S(2)}, u32[]{:S(2)}) %collective-permute-start.3) | collective-permute-done | bytes 163872 | tf_op jit(solution)/shard_map/ppermute | solution.py:518
  15.2 0.2 stage_slot.3
  15.4 0.1 collective-permute-start.4
  15.5 0.0 collective-permute-done.5.refs_3_
  15.5 0.0 copy-done.4
  15.5 0.0 copy-start.3
  15.5 4.2 %attend_head.2 = (bf16[640,256]{1,0:T(8,128)(2,1)S(1)}, bf16[320,256]{1,0:T(8,128)(2,1)S(1)}, bf16[640,256]{1,0:T(8,128)(2,1)S(1)}, bf16[640,256]{1,0:T(8,128)(2,1)S(1)}, f32[8,128]{1,0:T(8,128)S(1)}) custom-call(f32[40,1024]{1,0:T(8,128)S(1)} %get-tuple-element.58.cosv, f32[40,1024]{1,0:T(8,128)S(1)} %get-tuple-element.59.sinv, ...), custom_call_target="tpu_custom_call" | custom-call | flops 3221225472 | tf_op jit(solution)/shard_map/attend_head/pallas_call | solution.py:593
  19.7 3.1 %collective-permute-start.6 = (bf16[320,256]{1,0:T(8,128)(2,1)S(1)}, bf16[320,256]{1,0:T(8,128)(2,1)S(1)}, u32[]{:S(2)}, u32[]{:S(2)}) collective-permute-start(bf16[320,256]{1,0:T(8,128)(2,1)S(1)} %get-tuple-element.93), channel_id=1, source_target_pairs={{3,0},{2,1},{1,2},{0,3},{7,4},{6,5},{5,6},{4,7},{11,8},{10,9},{9,1... | collective-permute-start | bytes 491528 | tf_op jit(solution)/shard_map/ppermute | solution.py:72
  22.8 0.0 collective-permute-done.refs_1_
  22.8 0.0 collective-permute-done.2.refs_2_
  22.8 0.0 collective-permute-done.4.refs_3_
  22.8 0.0 copy-done.3
  22.8 4.7 %attend_head.3 = (bf16[640,256]{1,0:T(8,128)(2,1)S(1)}, bf16[320,256]{1,0:T(8,128)(2,1)S(1)}, bf16[640,256]{1,0:T(8,128)(2,1)S(1)}, bf16[640,256]{1,0:T(8,128)(2,1)S(1)}, f32[32,4,128]{2,1,0:T(4,128)}) custom-call(f32[40,1024]{1,0:T(8,128)S(1)} %get-tuple-element.58.cosv, f32[40,1024]{1,0:T(8,128)S(1)} %get-tuple-element.59.sinv, ...), custom_call_target="tpu_custom_call" | custom-call | flops 3221225472 | tf_op jit(solution)/shard_map/attend_head/pallas_call | solution.py:593
  27.5 0.5 %collective-permute-start.8 = (bf16[640,256]{1,0:T(8,128)(2,1)S(1)}, bf16[640,256]{1,0:T(8,128)(2,1)S(1)}, u32[]{:S(2)}, u32[]{:S(2)}) collective-permute-start(bf16[640,256]{1,0:T(8,128)(2,1)S(1)} %get-tuple-element.97), channel_id=1, source_target_pairs={{2,0},{3,1},{0,2},{1,3},{6,4},{7,5},{4,6},{5,7},{10,8},{11,9},{8,1... | collective-permute-start | bytes 983048 | tf_op jit(solution)/shard_map/ppermute | solution.py:72
  28.0 0.8 %collective-permute-start.9 = (bf16[640,256]{1,0:T(8,128)(2,1)S(1)}, bf16[640,256]{1,0:T(8,128)(2,1)S(1)}, u32[]{:S(2)}, u32[]{:S(2)}) collective-permute-start(bf16[640,256]{1,0:T(8,128)(2,1)S(1)} %get-tuple-element.98), channel_id=1, source_target_pairs={{1,0},{0,1},{3,2},{2,3},{5,4},{4,5},{7,6},{6,7},{9,8},{8,9},{11,10... | collective-permute-start | bytes 983048 | tf_op jit(solution)/shard_map/ppermute | solution.py:72
  28.8 0.0 collective-permute-done.6.refs_0_
  28.8 2.2 %collective-permute-start.7 = (bf16[320,256]{1,0:T(8,128)(2,1)S(1)}, bf16[320,256]{1,0:T(8,128)(2,1)S(1)}, u32[]{:S(2)}, u32[]{:S(2)}) collective-permute-start(bf16[320,256]{1,0:T(8,128)(2,1)S(1)} %get-tuple-element.95), channel_id=1, source_target_pairs={{3,0},{2,1},{1,2},{0,3},{7,4},{6,5},{5,6},{4,7},{11,8},{10,9},{9,1... | collective-permute-start | bytes 491528 | tf_op jit(solution)/shard_map/ppermute | solution.py:72
  31.0 4.1 %all-to-all-start = ((f32[32,4,128]{2,1,0:T(4,128)}), f32[32,4,128]{2,1,0:T(4,128)S(1)}, u32[]{:S(2)}, u32[]{:S(2)}) async-start(f32[32,4,128]{2,1,0:T(4,128)} %get-tuple-element.103), calls=%async_computation | async-start | bytes 131072 | tf_op jit(solution)/shard_map/all_to_all | solution.py:625
  35.1 4.3 %collective-permute-done.7.refs_1_ = bf16[320,256]{1,0:T(8,128)(2,1)S(1)} collective-permute-done((bf16[320,256]{1,0:T(8,128)(2,1)S(1)}, bf16[320,256]{1,0:T(8,128)(2,1)S(1)}, u32[]{:S(2)}, u32[]{:S(2)}) %collective-permute-start.7) | collective-permute-done | bytes 163872 | tf_op jit(solution)/shard_map/ppermute | solution.py:72
  39.4 0.0 collective-permute-done.8.refs_3_
  39.4 0.5 %collective-permute-done.9.refs_4_ = bf16[640,256]{1,0:T(8,128)(2,1)S(1)} collective-permute-done((bf16[640,256]{1,0:T(8,128)(2,1)S(1)}, bf16[640,256]{1,0:T(8,128)(2,1)S(1)}, u32[]{:S(2)}, u32[]{:S(2)}) %collective-permute-start.9) | collective-permute-done | bytes 327712 | tf_op jit(solution)/shard_map/ppermute | solution.py:72
  39.9 1.3 %unpack_heads.1 = (bf16[256,640]{1,0:T(8,128)(2,1)}, bf16[256,640]{1,0:T(8,128)(2,1)}, bf16[256,640]{1,0:T(8,128)(2,1)}, bf16[256,640]{1,0:T(8,128)(2,1)}) custom-call(bf16[320,256]{1,0:T(8,128)(2,1)S(1)} %collective-permute-done.6.refs_0_, bf16[320,256]{1,0:T(8,128)(2,1)S(1)} %collective-permute-done.7.refs_1_, ...), custom_call_target="tpu_custom_call" | custom-call | flops 20000000000 | tf_op jit(solution)/shard_map/unpack_heads/pallas_call | solution.py:628
  41.2 2.1 %all-to-all-done.tiles = f32[32,4,128]{2,1,0:T(4,128)S(1)} async-done(((f32[32,4,128]{2,1,0:T(4,128)}), f32[32,4,128]{2,1,0:T(4,128)S(1)}, u32[]{:S(2)}, u32[]{:S(2)}) %all-to-all-start) | async-done | bytes 65568 | tf_op jit(solution)/shard_map/all_to_all | solution.py:625
  43.3 0.7 %bias_sums.1 = f32[3,640]{1,0:T(4,128)} custom-call(f32[32,4,128]{2,1,0:T(4,128)S(1)} %all-to-all-done.tiles), custom_call_target="tpu_custom_call" | custom-call | tf_op jit(solution)/shard_map/bias_sums/pallas_call | solution.py:643
Async XLA Ops:
  2.1 4.7 %copy-start = (bf16[3,640]{1,0:T(4,128)(2,1)S(1)}, bf16[3,640]{1,0:T(4,128)(2,1)}, u32[]{:S(2)}) copy-start(bf16[3,640]{1,0:T(4,128)(2,1)} %refs_0_.1) | copy-start | bytes 11524
  2.1 10.5 %collective-permute-start.1 = (bf16[320,256]{1,0:T(8,128)(2,1)S(1)}, bf16[320,256]{1,0:T(8,128)(2,1)S(1)}, u32[]{:S(2)}, u32[]{:S(2)}) collective-permute-start(bf16[320,256]{1,0:T(8,128)(2,1)S(1)} %get-tuple-element.70), channel_id=1, source_target_pairs={{0,3},{1,2},{2,1},{3,0},{4,7},{5,6},{6,5},{7,4},{8,11},{9,10},{10,... | collective-permute-start | bytes 491528 | tf_op jit(solution)/shard_map/ppermute | solution.py:518
  6.1 9.1 %collective-permute-start.3 = (bf16[320,256]{1,0:T(8,128)(2,1)S(1)}, bf16[320,256]{1,0:T(8,128)(2,1)S(1)}, u32[]{:S(2)}, u32[]{:S(2)}) collective-permute-start(bf16[320,256]{1,0:T(8,128)(2,1)S(1)} %get-tuple-element.75), channel_id=1, source_target_pairs={{0,2},{1,3},{2,0},{3,1},{4,6},{5,7},{6,4},{7,5},{8,10},{9,11},{10,... | collective-permute-start | bytes 491528 | tf_op jit(solution)/shard_map/ppermute | solution.py:518
  6.6 0.7 %copy-start.1 = (s32[1,4]{1,0:T(1,128)S(1)}, s32[1,4]{1,0:T(1,128)}, u32[]{:S(2)}) copy-start(s32[1,4]{1,0:T(1,128)} %lengths.1) | copy-start | bytes 52
  6.6 0.7 %copy-start.2 = (s32[1,4]{1,0:T(1,128)S(1)}, s32[1,4]{1,0:T(1,128)}, u32[]{:S(2)}) copy-start(s32[1,4]{1,0:T(1,128)} %widths.1) | copy-start | bytes 52
  6.6 8.9 %collective-permute-start.5 = (bf16[320,256]{1,0:T(8,128)(2,1)S(1)}, bf16[320,256]{1,0:T(8,128)(2,1)S(1)}, u32[]{:S(2)}, u32[]{:S(2)}) collective-permute-start(bf16[320,256]{1,0:T(8,128)(2,1)S(1)} %get-tuple-element.81), channel_id=1, source_target_pairs={{0,1},{1,0},{2,3},{3,2},{4,5},{5,4},{6,7},{7,6},{8,9},{9,8},{10,11... | collective-permute-start | bytes 491528 | tf_op jit(solution)/shard_map/ppermute | solution.py:518
  10.1 12.7 %collective-permute-start = (bf16[320,256]{1,0:T(8,128)(2,1)S(1)}, bf16[320,256]{1,0:T(8,128)(2,1)S(1)}, u32[]{:S(2)}, u32[]{:S(2)}) collective-permute-start(bf16[320,256]{1,0:T(8,128)(2,1)S(1)} %get-tuple-element.68), channel_id=1, source_target_pairs={{0,3},{1,2},{2,1},{3,0},{4,7},{5,6},{6,5},{7,4},{8,11},{9,10},{10,... | collective-permute-start | bytes 491528 | tf_op jit(solution)/shard_map/ppermute | solution.py:578
  12.8 2.7 %copy-start.4 = (bf16[3,128,256]{2,1,0:T(8,128)(2,1)S(1)}, bf16[3,128,256]{2,1,0:T(8,128)(2,1)}, u32[]{:S(2)}) copy-start(bf16[3,128,256]{2,1,0:T(8,128)(2,1)} %get-tuple-element.82.refs_4_) | copy-start | bytes 589828
  12.8 10.0 %collective-permute-start.2 = (bf16[320,256]{1,0:T(8,128)(2,1)S(1)}, bf16[320,256]{1,0:T(8,128)(2,1)S(1)}, u32[]{:S(2)}, u32[]{:S(2)}) collective-permute-start(bf16[320,256]{1,0:T(8,128)(2,1)S(1)} %get-tuple-element.73), channel_id=1, source_target_pairs={{0,2},{1,3},{2,0},{3,1},{4,6},{5,7},{6,4},{7,5},{8,10},{9,11},{10,... | collective-permute-start | bytes 491528 | tf_op jit(solution)/shard_map/ppermute | solution.py:578
  15.4 7.4 %collective-permute-start.4 = (bf16[320,256]{1,0:T(8,128)(2,1)S(1)}, bf16[320,256]{1,0:T(8,128)(2,1)S(1)}, u32[]{:S(2)}, u32[]{:S(2)}) collective-permute-start(bf16[320,256]{1,0:T(8,128)(2,1)S(1)} %get-tuple-element.78), channel_id=1, source_target_pairs={{0,1},{1,0},{2,3},{3,2},{4,5},{5,4},{6,7},{7,6},{8,9},{9,8},{10,11... | collective-permute-start | bytes 491528 | tf_op jit(solution)/shard_map/ppermute | solution.py:578
  15.5 7.3 %copy-start.3 = (bf16[3,128,256]{2,1,0:T(8,128)(2,1)S(1)}, bf16[3,128,256]{2,1,0:T(8,128)(2,1)}, u32[]{:S(2)}) copy-start(bf16[3,128,256]{2,1,0:T(8,128)(2,1)} %get-tuple-element.79.refs_4_) | copy-start | bytes 589828
  19.7 9.1 %collective-permute-start.6 = (bf16[320,256]{1,0:T(8,128)(2,1)S(1)}, bf16[320,256]{1,0:T(8,128)(2,1)S(1)}, u32[]{:S(2)}, u32[]{:S(2)}) collective-permute-start(bf16[320,256]{1,0:T(8,128)(2,1)S(1)} %get-tuple-element.93), channel_id=1, source_target_pairs={{3,0},{2,1},{1,2},{0,3},{7,4},{6,5},{5,6},{4,7},{11,8},{10,9},{9,1... | collective-permute-start | bytes 491528 | tf_op jit(solution)/shard_map/ppermute | solution.py:72
  27.5 11.9 %collective-permute-start.8 = (bf16[640,256]{1,0:T(8,128)(2,1)S(1)}, bf16[640,256]{1,0:T(8,128)(2,1)S(1)}, u32[]{:S(2)}, u32[]{:S(2)}) collective-permute-start(bf16[640,256]{1,0:T(8,128)(2,1)S(1)} %get-tuple-element.97), channel_id=1, source_target_pairs={{2,0},{3,1},{0,2},{1,3},{6,4},{7,5},{4,6},{5,7},{10,8},{11,9},{8,1... | collective-permute-start | bytes 983048 | tf_op jit(solution)/shard_map/ppermute | solution.py:72
  28.0 11.9 %collective-permute-start.9 = (bf16[640,256]{1,0:T(8,128)(2,1)S(1)}, bf16[640,256]{1,0:T(8,128)(2,1)S(1)}, u32[]{:S(2)}, u32[]{:S(2)}) collective-permute-start(bf16[640,256]{1,0:T(8,128)(2,1)S(1)} %get-tuple-element.98), channel_id=1, source_target_pairs={{1,0},{0,1},{3,2},{2,3},{5,4},{4,5},{7,6},{6,7},{9,8},{8,9},{11,10... | collective-permute-start | bytes 983048 | tf_op jit(solution)/shard_map/ppermute | solution.py:72
  28.8 10.6 %collective-permute-start.7 = (bf16[320,256]{1,0:T(8,128)(2,1)S(1)}, bf16[320,256]{1,0:T(8,128)(2,1)S(1)}, u32[]{:S(2)}, u32[]{:S(2)}) collective-permute-start(bf16[320,256]{1,0:T(8,128)(2,1)S(1)} %get-tuple-element.95), channel_id=1, source_target_pairs={{3,0},{2,1},{1,2},{0,3},{7,4},{6,5},{5,6},{4,7},{11,8},{10,9},{9,1... | collective-permute-start | bytes 491528 | tf_op jit(solution)/shard_map/ppermute | solution.py:72
  31.0 12.2 %all-to-all-start = ((f32[32,4,128]{2,1,0:T(4,128)}), f32[32,4,128]{2,1,0:T(4,128)S(1)}, u32[]{:S(2)}, u32[]{:S(2)}) async-start(f32[32,4,128]{2,1,0:T(4,128)} %get-tuple-element.103), calls=%async_computation | async-start | bytes 131072 | tf_op jit(solution)/shard_map/all_to_all | solution.py:625

commit v19 on v18

--- a/solution.py
+++ b/solution.py
@@ -571,17 +571,13 @@
     own = [[prepared[phase], prepared[OWN_HEADS + phase]] for phase in phases]
     staged = [{0: pair} for pair in own]
     got = [first] + [[sent[0]] for sent in sends[1:]]
-    latest = own
-    for slot in range(1, slots):
+    for slot in range(1, slots - 1):
+        latest = stage_ahead(slot, (0,), [first[slot]])
         for phase in phases[1:]:
-            send, latest = lax.optimization_barrier((sends[phase][slot], latest))
-            got[phase].append(lax.ppermute(send, "tok", rounds[slot - 1]))
-        if slot == 1:
-            staged[0][0], staged[1][0] = latest
-        else:
-            staged[0][slot - 1] = latest[0]
-        if slot + 1 < slots:
-            latest = stage_ahead(slot, (0,), [first[slot]])
+            for leaving in (1, 2) if slot == 1 else (slot + 1,):
+                send, latest = lax.optimization_barrier((sends[phase][leaving], latest))
+                got[phase].append(lax.ppermute(send, "tok", rounds[leaving - 1]))
+        staged[0][slot] = latest[0]
     early = []
     carried = []
     for phase in range(OWN_HEADS):

time: 44.2 us -> 43.8 us (level)
  waiting for transfers between devices: 8.59 us -> 7.47 us
  starting transfers between devices: 18.6 us -> 19.3 us
    ppermute x3, waiting for transfers between devices: 1.74 us -> 1.07 us  [on_device(): lax.ppermute(send, 'tok', pairs)]
    ppermute x4, waiting for transfers between devices: 4.77 us -> 4.19 us  [send_back(): lax.ppermute(result, 'tok', [(target, source) for source, target in pairs])]
    ppermute x3, starting transfers between devices: 3.26 us -> 3.78 us  [on_device(): got[phase].append(lax.ppermute(send, 'tok', rounds[leaving - 1]))]
where the time goes in v19:
time: 43.8 us; the launch traced here: 43.6 us
  starting transfers between devices  19.3 us (44%)
  Pallas kernels  15.6 us (36%)
  waiting for transfers between devices  7.47 us (17%)
  between operations  0.73 us (2%)
  local copies, waits for them, and re-layouts  0.49 us (1%)
    pallas_call x2, Pallas kernels, on_device(): pl.pallas_call(functools.partial(attend_kernel, slots, tuple(staged[phase...  8.9 us
    ppermute x4, starting transfers between devices, send_back(): lax.ppermute(result, 'tok', [(target, source) for source, target in pairs])  6.45 us
    ppermute x3, starting transfers between devices, on_device(): lax.ppermute(send, 'tok', pairs)  4.66 us
    all_to_all x1, starting transfers between devices, on_device(): tiles = lax.all_to_all(total, ('dp', 'tok'), 0, 0, tiled=True)  4.41 us
    ppermute x4, waiting for transfers between devices, send_back(): lax.ppermute(result, 'tok', [(target, source) for source, target in pairs])  4.19 us
    ppermute x3, starting transfers between devices, on_device(): got[phase].append(lax.ppermute(send, 'tok', rounds[leaving - 1]))  3.78 us
    pallas_call x1, Pallas kernels, on_device(): pl.pallas_call(functools.partial(prepare_kernel, slots, images, count, to...  2.84 us
    all_to_all x1, waiting for transfers between devices, on_device(): tiles = lax.all_to_all(total, ('dp', 'tok'), 0, 0, tiled=True)  2.2 us
  transfers between devices with their start and end apart: 11, of which 4 were waited for; matrix products, arithmetic and copies ran while one was open for 0% of the time, Pallas kernels for 31%

profile of v19, /device:TPU:0, one launch (start us, length us, event | category | flops | bytes accessed | tf_op | source)
XLA Modules:
  0.0 43.6 jit_solution(319624071638017048)
XLA Ops:
  0.6 1.5 %pack_heads.1 = (bf16[320,256]{1,0:T(8,128)(2,1)S(1)}, bf16[320,256]{1,0:T(8,128)(2,1)S(1)}, bf16[320,256]{1,0:T(8,128)(2,1)S(1)}, bf16[320,256]{1,0:T(8,128)(2,1)S(1)}) custom-call(bf16[256,640]{1,0:T(8,128)(2,1)} %bitcast.8, bf16[256,640]{1,0:T(8,128)(2,1)} %bitcast.10, bf16[256,640]{1,0:T(8,128)(2,1)} %bitcast.12, bf16[256,640]{1,0:T(8,128)(2,1)} %bitcast.14), custom_call_target="tpu_custom_call" | custom-call | tf_op jit(solution)/shard_map/pack_heads/pallas_call | solution.py:502
  2.1 0.0 copy-start
  2.1 4.0 %collective-permute-start = (bf16[320,256]{1,0:T(8,128)(2,1)S(1)}, bf16[320,256]{1,0:T(8,128)(2,1)S(1)}, u32[]{:S(2)}, u32[]{:S(2)}) collective-permute-start(bf16[320,256]{1,0:T(8,128)(2,1)S(1)} %get-tuple-element.62), channel_id=1, source_target_pairs={{0,3},{1,2},{2,1},{3,0},{4,7},{5,6},{6,5},{7,4},{8,11},{9,10},{10,... | collective-permute-start | bytes 491528 | tf_op jit(solution)/shard_map/ppermute | solution.py:518
  6.1 0.4 %collective-permute-start.3 = (bf16[320,256]{1,0:T(8,128)(2,1)S(1)}, bf16[320,256]{1,0:T(8,128)(2,1)S(1)}, u32[]{:S(2)}, u32[]{:S(2)}) collective-permute-start(bf16[320,256]{1,0:T(8,128)(2,1)S(1)} %get-tuple-element.71), channel_id=1, source_target_pairs={{0,2},{1,3},{2,0},{3,1},{4,6},{5,7},{6,4},{7,5},{8,10},{9,11},{10,... | collective-permute-start | bytes 491528 | tf_op jit(solution)/shard_map/ppermute | solution.py:518
  6.6 0.0 copy-start.1
  6.6 0.0 copy-start.2
  6.6 0.2 collective-permute-start.5
  6.8 0.0 copy-done
  6.8 0.4 %copy-done.1 = s32[1,4]{1,0:T(1,128)S(1)} copy-done((s32[1,4]{1,0:T(1,128)S(1)}, s32[1,4]{1,0:T(1,128)}, u32[]{:S(2)}) %copy-start.1) | copy-done | bytes 40
  7.2 0.0 copy-done.2
  7.2 2.8 %prepare.1 = (f32[40,1024]{1,0:T(8,128)S(1)}, f32[40,1024]{1,0:T(8,128)S(1)}, f32[24,256]{1,0:T(8,128)S(1)}, f32[160,128]{1,0:T(8,128)S(1)}, bf16[320,256]{1,0:T...) custom-call(s32[1,4]{1,0:T(1,128)S(1)} %copy-done.1, ...), custom_call_target="tpu_custom_call" | custom-call | flops 1000000 | tf_op jit(solution)/shard_map/prepare/pallas_call | solution.py:535
  10.1 1.1 %collective-permute-done.refs_0_.refs_1_ = bf16[320,256]{1,0:T(8,128)(2,1)S(1)} collective-permute-done((bf16[320,256]{1,0:T(8,128)(2,1)S(1)}, bf16[320,256]{1,0:T(8,128)(2,1)S(1)}, u32[]{:S(2)}, u32[]{:S(2)}) %collective-permute-start) | collective-permute-done | bytes 163872 | tf_op jit(solution)/shard_map/ppermute | solution.py:518
  11.2 0.2 stage_slot.2
  11.3 3.1 %collective-permute-start.1 = (bf16[320,256]{1,0:T(8,128)(2,1)S(1)}, bf16[320,256]{1,0:T(8,128)(2,1)S(1)}, u32[]{:S(2)}, u32[]{:S(2)}) collective-permute-start(bf16[320,256]{1,0:T(8,128)(2,1)S(1)} %get-tuple-element.65), channel_id=1, source_target_pairs={{0,3},{1,2},{2,1},{3,0},{4,7},{5,6},{6,5},{7,4},{8,11},{9,10},{10,... | collective-permute-start | bytes 491528 | tf_op jit(solution)/shard_map/ppermute | solution.py:579
  14.4 0.0 copy-start.4
  14.4 0.4 %collective-permute-start.2 = (bf16[320,256]{1,0:T(8,128)(2,1)S(1)}, bf16[320,256]{1,0:T(8,128)(2,1)S(1)}, u32[]{:S(2)}, u32[]{:S(2)}) collective-permute-start(bf16[320,256]{1,0:T(8,128)(2,1)S(1)} %get-tuple-element.69), channel_id=1, source_target_pairs={{0,2},{1,3},{2,0},{3,1},{4,6},{5,7},{6,4},{7,5},{8,10},{9,11},{10,... | collective-permute-start | bytes 491528 | tf_op jit(solution)/shard_map/ppermute | solution.py:579
  14.9 0.0 collective-permute-done.3.refs_0_.refs_2_
  14.9 0.2 stage_slot.3
  15.0 0.3 collective-permute-start.4
  15.3 0.0 collective-permute-done.5.refs_3_
  15.3 0.0 copy-done.4
  15.3 0.0 copy-start.3
  15.3 4.2 %attend_head.2 = (bf16[640,256]{1,0:T(8,128)(2,1)S(1)}, bf16[320,256]{1,0:T(8,128)(2,1)S(1)}, bf16[640,256]{1,0:T(8,128)(2,1)S(1)}, bf16[640,256]{1,0:T(8,128)(2,1)S(1)}, f32[8,128]{1,0:T(8,128)S(1)}) custom-call(f32[40,1024]{1,0:T(8,128)S(1)} %get-tuple-element.56.cosv, f32[40,1024]{1,0:T(8,128)S(1)} %get-tuple-element.57.sinv, ...), custom_call_target="tpu_custom_call" | custom-call | flops 3221225472 | tf_op jit(solution)/shard_map/attend_head/pallas_call | solution.py:589
  19.5 2.9 %collective-permute-start.6 = (bf16[320,256]{1,0:T(8,128)(2,1)S(1)}, bf16[320,256]{1,0:T(8,128)(2,1)S(1)}, u32[]{:S(2)}, u32[]{:S(2)}) collective-permute-start(bf16[320,256]{1,0:T(8,128)(2,1)S(1)} %get-tuple-element.89), channel_id=1, source_target_pairs={{3,0},{2,1},{1,2},{0,3},{7,4},{6,5},{5,6},{4,7},{11,8},{10,9},{9,1... | collective-permute-start | bytes 491528 | tf_op jit(solution)/shard_map/ppermute | solution.py:72
  22.4 0.0 collective-permute-done.1.refs_1_
  22.4 0.0 collective-permute-done.2.refs_2_
  22.4 0.0 collective-permute-done.4.refs_3_
  22.5 0.0 copy-done.3
  22.5 4.7 %attend_head.3 = (bf16[640,256]{1,0:T(8,128)(2,1)S(1)}, bf16[320,256]{1,0:T(8,128)(2,1)S(1)}, bf16[640,256]{1,0:T(8,128)(2,1)S(1)}, bf16[640,256]{1,0:T(8,128)(2,1)S(1)}, f32[32,4,128]{2,1,0:T(4,128)}) custom-call(f32[40,1024]{1,0:T(8,128)S(1)} %get-tuple-element.56.cosv, f32[40,1024]{1,0:T(8,128)S(1)} %get-tuple-element.57.sinv, ...), custom_call_target="tpu_custom_call" | custom-call | flops 3221225472 | tf_op jit(solution)/shard_map/attend_head/pallas_call | solution.py:589
  27.2 0.5 %collective-permute-start.8 = (bf16[640,256]{1,0:T(8,128)(2,1)S(1)}, bf16[640,256]{1,0:T(8,128)(2,1)S(1)}, u32[]{:S(2)}, u32[]{:S(2)}) collective-permute-start(bf16[640,256]{1,0:T(8,128)(2,1)S(1)} %get-tuple-element.93), channel_id=1, source_target_pairs={{2,0},{3,1},{0,2},{1,3},{6,4},{7,5},{4,6},{5,7},{10,8},{11,9},{8,1... | collective-permute-start | bytes 983048 | tf_op jit(solution)/shard_map/ppermute | solution.py:72
  27.7 1.2 %collective-permute-start.9 = (bf16[640,256]{1,0:T(8,128)(2,1)S(1)}, bf16[640,256]{1,0:T(8,128)(2,1)S(1)}, u32[]{:S(2)}, u32[]{:S(2)}) collective-permute-start(bf16[640,256]{1,0:T(8,128)(2,1)S(1)} %get-tuple-element.94), channel_id=1, source_target_pairs={{1,0},{0,1},{3,2},{2,3},{5,4},{4,5},{7,6},{6,7},{9,8},{8,9},{11,10... | collective-permute-start | bytes 983048 | tf_op jit(solution)/shard_map/ppermute | solution.py:72
  28.9 0.0 collective-permute-done.6.refs_0_
  28.9 1.9 %collective-permute-start.7 = (bf16[320,256]{1,0:T(8,128)(2,1)S(1)}, bf16[320,256]{1,0:T(8,128)(2,1)S(1)}, u32[]{:S(2)}, u32[]{:S(2)}) collective-permute-start(bf16[320,256]{1,0:T(8,128)(2,1)S(1)} %get-tuple-element.91), channel_id=1, source_target_pairs={{3,0},{2,1},{1,2},{0,3},{7,4},{6,5},{5,6},{4,7},{11,8},{10,9},{9,1... | collective-permute-start | bytes 491528 | tf_op jit(solution)/shard_map/ppermute | solution.py:72
  30.7 4.4 %all-to-all-start = ((f32[32,4,128]{2,1,0:T(4,128)}), f32[32,4,128]{2,1,0:T(4,128)S(1)}, u32[]{:S(2)}, u32[]{:S(2)}) async-start(f32[32,4,128]{2,1,0:T(4,128)} %get-tuple-element.99), calls=%async_computation | async-start | bytes 131072 | tf_op jit(solution)/shard_map/all_to_all | solution.py:621
  35.1 3.7 %collective-permute-done.7.refs_1_ = bf16[320,256]{1,0:T(8,128)(2,1)S(1)} collective-permute-done((bf16[320,256]{1,0:T(8,128)(2,1)S(1)}, bf16[320,256]{1,0:T(8,128)(2,1)S(1)}, u32[]{:S(2)}, u32[]{:S(2)}) %collective-permute-start.7) | collective-permute-done | bytes 163872 | tf_op jit(solution)/shard_map/ppermute | solution.py:72
  38.8 0.0 collective-permute-done.8.refs_3_
  38.8 0.5 %collective-permute-done.9.refs_4_ = bf16[640,256]{1,0:T(8,128)(2,1)S(1)} collective-permute-done((bf16[640,256]{1,0:T(8,128)(2,1)S(1)}, bf16[640,256]{1,0:T(8,128)(2,1)S(1)}, u32[]{:S(2)}, u32[]{:S(2)}) %collective-permute-start.9) | collective-permute-done | bytes 327712 | tf_op jit(solution)/shard_map/ppermute | solution.py:72
  39.3 1.3 %unpack_heads.1 = (bf16[256,640]{1,0:T(8,128)(2,1)}, bf16[256,640]{1,0:T(8,128)(2,1)}, bf16[256,640]{1,0:T(8,128)(2,1)}, bf16[256,640]{1,0:T(8,128)(2,1)}) custom-call(bf16[320,256]{1,0:T(8,128)(2,1)S(1)} %collective-permute-done.6.refs_0_, bf16[320,256]{1,0:T(8,128)(2,1)S(1)} %collective-permute-done.7.refs_1_, ...), custom_call_target="tpu_custom_call" | custom-call | flops 20000000000 | tf_op jit(solution)/shard_map/unpack_heads/pallas_call | solution.py:624
  40.7 2.2 %all-to-all-done.tiles = f32[32,4,128]{2,1,0:T(4,128)S(1)} async-done(((f32[32,4,128]{2,1,0:T(4,128)}), f32[32,4,128]{2,1,0:T(4,128)S(1)}, u32[]{:S(2)}, u32[]{:S(2)}) %all-to-all-start) | async-done | bytes 65568 | tf_op jit(solution)/shard_map/all_to_all | solution.py:621
  42.9 0.7 %bias_sums.1 = f32[3,640]{1,0:T(4,128)} custom-call(f32[32,4,128]{2,1,0:T(4,128)S(1)} %all-to-all-done.tiles), custom_call_target="tpu_custom_call" | custom-call | tf_op jit(solution)/shard_map/bias_sums/pallas_call | solution.py:639
Async XLA Ops:
  2.1 4.7 %copy-start = (bf16[3,640]{1,0:T(4,128)(2,1)S(1)}, bf16[3,640]{1,0:T(4,128)(2,1)}, u32[]{:S(2)}) copy-start(bf16[3,640]{1,0:T(4,128)(2,1)} %refs_0_.1) | copy-start | bytes 11524
  2.1 9.0 %collective-permute-start = (bf16[320,256]{1,0:T(8,128)(2,1)S(1)}, bf16[320,256]{1,0:T(8,128)(2,1)S(1)}, u32[]{:S(2)}, u32[]{:S(2)}) collective-permute-start(bf16[320,256]{1,0:T(8,128)(2,1)S(1)} %get-tuple-element.62), channel_id=1, source_target_pairs={{0,3},{1,2},{2,1},{3,0},{4,7},{5,6},{6,5},{7,4},{8,11},{9,10},{10,... | collective-permute-start | bytes 491528 | tf_op jit(solution)/shard_map/ppermute | solution.py:518
  6.1 8.7 %collective-permute-start.3 = (bf16[320,256]{1,0:T(8,128)(2,1)S(1)}, bf16[320,256]{1,0:T(8,128)(2,1)S(1)}, u32[]{:S(2)}, u32[]{:S(2)}) collective-permute-start(bf16[320,256]{1,0:T(8,128)(2,1)S(1)} %get-tuple-element.71), channel_id=1, source_target_pairs={{0,2},{1,3},{2,0},{3,1},{4,6},{5,7},{6,4},{7,5},{8,10},{9,11},{10,... | collective-permute-start | bytes 491528 | tf_op jit(solution)/shard_map/ppermute | solution.py:518
  6.6 0.7 %copy-start.1 = (s32[1,4]{1,0:T(1,128)S(1)}, s32[1,4]{1,0:T(1,128)}, u32[]{:S(2)}) copy-start(s32[1,4]{1,0:T(1,128)} %lengths.1) | copy-start | bytes 52
  6.6 0.7 %copy-start.2 = (s32[1,4]{1,0:T(1,128)S(1)}, s32[1,4]{1,0:T(1,128)}, u32[]{:S(2)}) copy-start(s32[1,4]{1,0:T(1,128)} %widths.1) | copy-start | bytes 52
  6.6 8.7 %collective-permute-start.5 = (bf16[320,256]{1,0:T(8,128)(2,1)S(1)}, bf16[320,256]{1,0:T(8,128)(2,1)S(1)}, u32[]{:S(2)}, u32[]{:S(2)}) collective-permute-start(bf16[320,256]{1,0:T(8,128)(2,1)S(1)} %get-tuple-element.77), channel_id=1, source_target_pairs={{0,1},{1,0},{2,3},{3,2},{4,5},{5,4},{6,7},{7,6},{8,9},{9,8},{10,11... | collective-permute-start | bytes 491528 | tf_op jit(solution)/shard_map/ppermute | solution.py:518
  11.3 11.1 %collective-permute-start.1 = (bf16[320,256]{1,0:T(8,128)(2,1)S(1)}, bf16[320,256]{1,0:T(8,128)(2,1)S(1)}, u32[]{:S(2)}, u32[]{:S(2)}) collective-permute-start(bf16[320,256]{1,0:T(8,128)(2,1)S(1)} %get-tuple-element.65), channel_id=1, source_target_pairs={{0,3},{1,2},{2,1},{3,0},{4,7},{5,6},{6,5},{7,4},{8,11},{9,10},{10,... | collective-permute-start | bytes 491528 | tf_op jit(solution)/shard_map/ppermute | solution.py:579
  14.4 0.9 %copy-start.4 = (bf16[3,128,256]{2,1,0:T(8,128)(2,1)S(1)}, bf16[3,128,256]{2,1,0:T(8,128)(2,1)}, u32[]{:S(2)}) copy-start(bf16[3,128,256]{2,1,0:T(8,128)(2,1)} %get-tuple-element.78.refs_4_) | copy-start | bytes 589828
  14.4 8.0 %collective-permute-start.2 = (bf16[320,256]{1,0:T(8,128)(2,1)S(1)}, bf16[320,256]{1,0:T(8,128)(2,1)S(1)}, u32[]{:S(2)}, u32[]{:S(2)}) collective-permute-start(bf16[320,256]{1,0:T(8,128)(2,1)S(1)} %get-tuple-element.69), channel_id=1, source_target_pairs={{0,2},{1,3},{2,0},{3,1},{4,6},{5,7},{6,4},{7,5},{8,10},{9,11},{10,... | collective-permute-start | bytes 491528 | tf_op jit(solution)/shard_map/ppermute | solution.py:579
  15.0 7.4 %collective-permute-start.4 = (bf16[320,256]{1,0:T(8,128)(2,1)S(1)}, bf16[320,256]{1,0:T(8,128)(2,1)S(1)}, u32[]{:S(2)}, u32[]{:S(2)}) collective-permute-start(bf16[320,256]{1,0:T(8,128)(2,1)S(1)} %get-tuple-element.74), channel_id=1, source_target_pairs={{0,1},{1,0},{2,3},{3,2},{4,5},{5,4},{6,7},{7,6},{8,9},{9,8},{10,11... | collective-permute-start | bytes 491528 | tf_op jit(solution)/shard_map/ppermute | solution.py:579
  15.3 7.1 %copy-start.3 = (bf16[3,128,256]{2,1,0:T(8,128)(2,1)S(1)}, bf16[3,128,256]{2,1,0:T(8,128)(2,1)}, u32[]{:S(2)}) copy-start(bf16[3,128,256]{2,1,0:T(8,128)(2,1)} %get-tuple-element.75.refs_4_) | copy-start | bytes 589828
  19.5 9.3 %collective-permute-start.6 = (bf16[320,256]{1,0:T(8,128)(2,1)S(1)}, bf16[320,256]{1,0:T(8,128)(2,1)S(1)}, u32[]{:S(2)}, u32[]{:S(2)}) collective-permute-start(bf16[320,256]{1,0:T(8,128)(2,1)S(1)} %get-tuple-element.89), channel_id=1, source_target_pairs={{3,0},{2,1},{1,2},{0,3},{7,4},{6,5},{5,6},{4,7},{11,8},{10,9},{9,1... | collective-permute-start | bytes 491528 | tf_op jit(solution)/shard_map/ppermute | solution.py:72
  27.2 11.7 %collective-permute-start.8 = (bf16[640,256]{1,0:T(8,128)(2,1)S(1)}, bf16[640,256]{1,0:T(8,128)(2,1)S(1)}, u32[]{:S(2)}, u32[]{:S(2)}) collective-permute-start(bf16[640,256]{1,0:T(8,128)(2,1)S(1)} %get-tuple-element.93), channel_id=1, source_target_pairs={{2,0},{3,1},{0,2},{1,3},{6,4},{7,5},{4,6},{5,7},{10,8},{11,9},{8,1... | collective-permute-start | bytes 983048 | tf_op jit(solution)/shard_map/ppermute | solution.py:72
  27.7 11.7 %collective-permute-start.9 = (bf16[640,256]{1,0:T(8,128)(2,1)S(1)}, bf16[640,256]{1,0:T(8,128)(2,1)S(1)}, u32[]{:S(2)}, u32[]{:S(2)}) collective-permute-start(bf16[640,256]{1,0:T(8,128)(2,1)S(1)} %get-tuple-element.94), channel_id=1, source_target_pairs={{1,0},{0,1},{3,2},{2,3},{5,4},{4,5},{7,6},{6,7},{9,8},{8,9},{11,10... | collective-permute-start | bytes 983048 | tf_op jit(solution)/shard_map/ppermute | solution.py:72
  28.9 10.0 %collective-permute-start.7 = (bf16[320,256]{1,0:T(8,128)(2,1)S(1)}, bf16[320,256]{1,0:T(8,128)(2,1)S(1)}, u32[]{:S(2)}, u32[]{:S(2)}) collective-permute-start(bf16[320,256]{1,0:T(8,128)(2,1)S(1)} %get-tuple-element.91), channel_id=1, source_target_pairs={{3,0},{2,1},{1,2},{0,3},{7,4},{6,5},{5,6},{4,7},{11,8},{10,9},{9,1... | collective-permute-start | bytes 491528 | tf_op jit(solution)/shard_map/ppermute | solution.py:72
  30.7 12.1 %all-to-all-start = ((f32[32,4,128]{2,1,0:T(4,128)}), f32[32,4,128]{2,1,0:T(4,128)S(1)}, u32[]{:S(2)}, u32[]{:S(2)}) async-start(f32[32,4,128]{2,1,0:T(4,128)} %get-tuple-element.99), calls=%async_computation | async-start | bytes 131072 | tf_op jit(solution)/shard_map/all_to_all | solution.py:621

commit v20 on v19

--- a/solution.py
+++ b/solution.py
@@ -20,7 +20,7 @@
 LANES = 128
 USED = HEAD_DIM + 16
 HALF = HEAD_DIM // 2
-PIECES = 2
+PIECES = 4
 FIRST_PACK_KIB = 52 * 1024 + 1260
 PREPARE_KIB = 52 * 1024 + 300
 UNPACK_FLOPS = 20_000_000_000
@@ -372,6 +372,8 @@
         dkey = unrotate(dkey * (1.0 / LOG2E), cosv[:, at], sinv[:, at])
         put(slot, 2, dkey.astype(jnp.bfloat16))
         dk_total = dk_total + live(slot, dkey)
+    for slot in range(slots // 2):
+        value_part(slot)
     lane = lax.broadcasted_iota(jnp.int32, (HEAD_DIM, LANES), 1)
     columns = jnp.zeros((HEAD_DIM, LANES), jnp.float32)
     for number, total in enumerate((dq_total, dk_total, dv_total)):
@@ -393,7 +395,7 @@
         lax.fori_loop(0, tiles.shape[0], repeat, 0, unroll=min(32, tiles.shape[0]))
         copy = pltpu.make_async_copy(tiles, sums, sem)
         copy.start()
-    for slot in range(slots):
+    for slot in range(slots // 2, slots):
         value_part(slot)
     if copy is not None:
         copy.wait()

time: 43.8 us -> 44.1 us (level)
  no operation moved by 1% of the time
where the time goes in v20:
time: 44.1 us; the launch traced here: 43.8 us
  starting transfers between devices  19.2 us (44%)
  Pallas kernels  15.9 us (36%)
  waiting for transfers between devices  7.58 us (17%)
  between operations  0.72 us (2%)
  local copies, waits for them, and re-layouts  0.49 us (1%)
    pallas_call x2, Pallas kernels, on_device(): pl.pallas_call(functools.partial(attend_kernel, slots, tuple(staged[phase...  9.16 us
    ppermute x4, starting transfers between devices, send_back(): lax.ppermute(result, 'tok', [(target, source) for source, target in pairs])  6.46 us
    ppermute x3, starting transfers between devices, on_device(): lax.ppermute(send, 'tok', pairs)  4.66 us
    ppermute x4, waiting for transfers between devices, send_back(): lax.ppermute(result, 'tok', [(target, source) for source, target in pairs])  4.3 us
    all_to_all x1, starting transfers between devices, on_device(): tiles = lax.all_to_all(total, ('dp', 'tok'), 0, 0, tiled=True)  4.29 us
    ppermute x3, starting transfers between devices, on_device(): got[phase].append(lax.ppermute(send, 'tok', rounds[leaving - 1]))  3.78 us
    pallas_call x1, Pallas kernels, on_device(): pl.pallas_call(functools.partial(prepare_kernel, slots, images, count, to...  2.84 us
    all_to_all x1, waiting for transfers between devices, on_device(): tiles = lax.all_to_all(total, ('dp', 'tok'), 0, 0, tiled=True)  2.2 us
  transfers between devices with their start and end apart: 11, of which 4 were waited for; matrix products, arithmetic and copies ran while one was open for 0% of the time, Pallas kernels for 31%

profile of v20, /device:TPU:0, one launch (start us, length us, event | category | flops | bytes accessed | tf_op | source)
XLA Modules:
  0.0 43.8 jit_solution(17117279638899043678)
XLA Ops:
  0.6 1.5 %pack_heads.1 = (bf16[320,256]{1,0:T(8,128)(2,1)S(1)}, bf16[320,256]{1,0:T(8,128)(2,1)S(1)}, bf16[320,256]{1,0:T(8,128)(2,1)S(1)}, bf16[320,256]{1,0:T(8,128)(2,1)S(1)}) custom-call(bf16[256,640]{1,0:T(8,128)(2,1)} %bitcast.8, bf16[256,640]{1,0:T(8,128)(2,1)} %bitcast.10, bf16[256,640]{1,0:T(8,128)(2,1)} %bitcast.12, bf16[256,640]{1,0:T(8,128)(2,1)} %bitcast.14), custom_call_target="tpu_custom_call" | custom-call | tf_op jit(solution)/shard_map/pack_heads/pallas_call | solution.py:504
  2.1 0.0 copy-start
  2.1 4.0 %collective-permute-start = (bf16[320,256]{1,0:T(8,128)(2,1)S(1)}, bf16[320,256]{1,0:T(8,128)(2,1)S(1)}, u32[]{:S(2)}, u32[]{:S(2)}) collective-permute-start(bf16[320,256]{1,0:T(8,128)(2,1)S(1)} %get-tuple-element.62), channel_id=1, source_target_pairs={{0,3},{1,2},{2,1},{3,0},{4,7},{5,6},{6,5},{7,4},{8,11},{9,10},{10,... | collective-permute-start | bytes 491528 | tf_op jit(solution)/shard_map/ppermute | solution.py:520
  6.1 0.4 %collective-permute-start.3 = (bf16[320,256]{1,0:T(8,128)(2,1)S(1)}, bf16[320,256]{1,0:T(8,128)(2,1)S(1)}, u32[]{:S(2)}, u32[]{:S(2)}) collective-permute-start(bf16[320,256]{1,0:T(8,128)(2,1)S(1)} %get-tuple-element.71), channel_id=1, source_target_pairs={{0,2},{1,3},{2,0},{3,1},{4,6},{5,7},{6,4},{7,5},{8,10},{9,11},{10,... | collective-permute-start | bytes 491528 | tf_op jit(solution)/shard_map/ppermute | solution.py:520
  6.6 0.0 copy-start.1
  6.6 0.0 copy-start.2
  6.6 0.2 collective-permute-start.5
  6.8 0.0 copy-done
  6.8 0.4 %copy-done.1 = s32[1,4]{1,0:T(1,128)S(1)} copy-done((s32[1,4]{1,0:T(1,128)S(1)}, s32[1,4]{1,0:T(1,128)}, u32[]{:S(2)}) %copy-start.1) | copy-done | bytes 40
  7.2 0.0 copy-done.2
  7.2 2.8 %prepare.1 = (f32[40,1024]{1,0:T(8,128)S(1)}, f32[40,1024]{1,0:T(8,128)S(1)}, f32[24,256]{1,0:T(8,128)S(1)}, f32[160,128]{1,0:T(8,128)S(1)}, bf16[320,256]{1,0:T...) custom-call(s32[1,4]{1,0:T(1,128)S(1)} %copy-done.1, ...), custom_call_target="tpu_custom_call" | custom-call | flops 1000000 | tf_op jit(solution)/shard_map/prepare/pallas_call | solution.py:537
  10.1 1.1 %collective-permute-done.refs_0_.refs_1_ = bf16[320,256]{1,0:T(8,128)(2,1)S(1)} collective-permute-done((bf16[320,256]{1,0:T(8,128)(2,1)S(1)}, bf16[320,256]{1,0:T(8,128)(2,1)S(1)}, u32[]{:S(2)}, u32[]{:S(2)}) %collective-permute-start) | collective-permute-done | bytes 163872 | tf_op jit(solution)/shard_map/ppermute | solution.py:520
  11.2 0.2 stage_slot.2
  11.3 3.1 %collective-permute-start.1 = (bf16[320,256]{1,0:T(8,128)(2,1)S(1)}, bf16[320,256]{1,0:T(8,128)(2,1)S(1)}, u32[]{:S(2)}, u32[]{:S(2)}) collective-permute-start(bf16[320,256]{1,0:T(8,128)(2,1)S(1)} %get-tuple-element.65), channel_id=1, source_target_pairs={{0,3},{1,2},{2,1},{3,0},{4,7},{5,6},{6,5},{7,4},{8,11},{9,10},{10,... | collective-permute-start | bytes 491528 | tf_op jit(solution)/shard_map/ppermute | solution.py:581
  14.4 0.0 copy-start.4
  14.4 0.4 %collective-permute-start.2 = (bf16[320,256]{1,0:T(8,128)(2,1)S(1)}, bf16[320,256]{1,0:T(8,128)(2,1)S(1)}, u32[]{:S(2)}, u32[]{:S(2)}) collective-permute-start(bf16[320,256]{1,0:T(8,128)(2,1)S(1)} %get-tuple-element.69), channel_id=1, source_target_pairs={{0,2},{1,3},{2,0},{3,1},{4,6},{5,7},{6,4},{7,5},{8,10},{9,11},{10,... | collective-permute-start | bytes 491528 | tf_op jit(solution)/shard_map/ppermute | solution.py:581
  14.9 0.0 collective-permute-done.3.refs_0_.refs_2_
  14.9 0.2 stage_slot.3
  15.0 0.3 collective-permute-start.4
  15.3 0.0 collective-permute-done.5.refs_3_
  15.3 0.0 copy-done.4
  15.3 0.0 copy-start.3
  15.3 4.3 %attend_head.2 = (bf16[640,256]{1,0:T(8,128)(2,1)S(1)}, bf16[320,256]{1,0:T(8,128)(2,1)S(1)}, bf16[640,256]{1,0:T(8,128)(2,1)S(1)}, bf16[640,256]{1,0:T(8,128)(2,1)S(1)}, f32[8,128]{1,0:T(8,128)S(1)}) custom-call(f32[40,1024]{1,0:T(8,128)S(1)} %get-tuple-element.56.cosv, f32[40,1024]{1,0:T(8,128)S(1)} %get-tuple-element.57.sinv, ...), custom_call_target="tpu_custom_call" | custom-call | flops 3221225472 | tf_op jit(solution)/shard_map/attend_head/pallas_call | solution.py:591
  19.7 2.9 %collective-permute-start.6 = (bf16[320,256]{1,0:T(8,128)(2,1)S(1)}, bf16[320,256]{1,0:T(8,128)(2,1)S(1)}, u32[]{:S(2)}, u32[]{:S(2)}) collective-permute-start(bf16[320,256]{1,0:T(8,128)(2,1)S(1)} %get-tuple-element.89), channel_id=1, source_target_pairs={{3,0},{2,1},{1,2},{0,3},{7,4},{6,5},{5,6},{4,7},{11,8},{10,9},{9,1... | collective-permute-start | bytes 491528 | tf_op jit(solution)/shard_map/ppermute | solution.py:72
  22.6 0.0 collective-permute-done.1.refs_1_
  22.6 0.0 collective-permute-done.2.refs_2_
  22.6 0.0 collective-permute-done.4.refs_3_
  22.6 0.0 copy-done.3
  22.6 4.8 %attend_head.3 = (bf16[640,256]{1,0:T(8,128)(2,1)S(1)}, bf16[320,256]{1,0:T(8,128)(2,1)S(1)}, bf16[640,256]{1,0:T(8,128)(2,1)S(1)}, bf16[640,256]{1,0:T(8,128)(2,1)S(1)}, f32[32,4,128]{2,1,0:T(4,128)}) custom-call(f32[40,1024]{1,0:T(8,128)S(1)} %get-tuple-element.56.cosv, f32[40,1024]{1,0:T(8,128)S(1)} %get-tuple-element.57.sinv, ...), custom_call_target="tpu_custom_call" | custom-call | flops 3221225472 | tf_op jit(solution)/shard_map/attend_head/pallas_call | solution.py:591
  27.4 0.5 %collective-permute-start.8 = (bf16[640,256]{1,0:T(8,128)(2,1)S(1)}, bf16[640,256]{1,0:T(8,128)(2,1)S(1)}, u32[]{:S(2)}, u32[]{:S(2)}) collective-permute-start(bf16[640,256]{1,0:T(8,128)(2,1)S(1)} %get-tuple-element.93), channel_id=1, source_target_pairs={{2,0},{3,1},{0,2},{1,3},{6,4},{7,5},{4,6},{5,7},{10,8},{11,9},{8,1... | collective-permute-start | bytes 983048 | tf_op jit(solution)/shard_map/ppermute | solution.py:72
  28.0 1.1 %collective-permute-start.9 = (bf16[640,256]{1,0:T(8,128)(2,1)S(1)}, bf16[640,256]{1,0:T(8,128)(2,1)S(1)}, u32[]{:S(2)}, u32[]{:S(2)}) collective-permute-start(bf16[640,256]{1,0:T(8,128)(2,1)S(1)} %get-tuple-element.94), channel_id=1, source_target_pairs={{1,0},{0,1},{3,2},{2,3},{5,4},{4,5},{7,6},{6,7},{9,8},{8,9},{11,10... | collective-permute-start | bytes 983048 | tf_op jit(solution)/shard_map/ppermute | solution.py:72
  29.0 0.0 collective-permute-done.6.refs_0_
  29.0 2.0 %collective-permute-start.7 = (bf16[320,256]{1,0:T(8,128)(2,1)S(1)}, bf16[320,256]{1,0:T(8,128)(2,1)S(1)}, u32[]{:S(2)}, u32[]{:S(2)}) collective-permute-start(bf16[320,256]{1,0:T(8,128)(2,1)S(1)} %get-tuple-element.91), channel_id=1, source_target_pairs={{3,0},{2,1},{1,2},{0,3},{7,4},{6,5},{5,6},{4,7},{11,8},{10,9},{9,1... | collective-permute-start | bytes 491528 | tf_op jit(solution)/shard_map/ppermute | solution.py:72
  31.0 4.3 %all-to-all-start = ((f32[32,4,128]{2,1,0:T(4,128)}), f32[32,4,128]{2,1,0:T(4,128)S(1)}, u32[]{:S(2)}, u32[]{:S(2)}) async-start(f32[32,4,128]{2,1,0:T(4,128)} %get-tuple-element.99), calls=%async_computation | async-start | bytes 131072 | tf_op jit(solution)/shard_map/all_to_all | solution.py:623
  35.3 3.7 %collective-permute-done.7.refs_1_ = bf16[320,256]{1,0:T(8,128)(2,1)S(1)} collective-permute-done((bf16[320,256]{1,0:T(8,128)(2,1)S(1)}, bf16[320,256]{1,0:T(8,128)(2,1)S(1)}, u32[]{:S(2)}, u32[]{:S(2)}) %collective-permute-start.7) | collective-permute-done | bytes 163872 | tf_op jit(solution)/shard_map/ppermute | solution.py:72
  39.0 0.0 collective-permute-done.8.refs_3_
  39.0 0.6 %collective-permute-done.9.refs_4_ = bf16[640,256]{1,0:T(8,128)(2,1)S(1)} collective-permute-done((bf16[640,256]{1,0:T(8,128)(2,1)S(1)}, bf16[640,256]{1,0:T(8,128)(2,1)S(1)}, u32[]{:S(2)}, u32[]{:S(2)}) %collective-permute-start.9) | collective-permute-done | bytes 327712 | tf_op jit(solution)/shard_map/ppermute | solution.py:72
  39.6 1.3 %unpack_heads.1 = (bf16[256,640]{1,0:T(8,128)(2,1)}, bf16[256,640]{1,0:T(8,128)(2,1)}, bf16[256,640]{1,0:T(8,128)(2,1)}, bf16[256,640]{1,0:T(8,128)(2,1)}) custom-call(bf16[320,256]{1,0:T(8,128)(2,1)S(1)} %collective-permute-done.6.refs_0_, bf16[320,256]{1,0:T(8,128)(2,1)S(1)} %collective-permute-done.7.refs_1_, ...), custom_call_target="tpu_custom_call" | custom-call | flops 20000000000 | tf_op jit(solution)/shard_map/unpack_heads/pallas_call | solution.py:626
  40.9 2.2 %all-to-all-done.tiles = f32[32,4,128]{2,1,0:T(4,128)S(1)} async-done(((f32[32,4,128]{2,1,0:T(4,128)}), f32[32,4,128]{2,1,0:T(4,128)S(1)}, u32[]{:S(2)}, u32[]{:S(2)}) %all-to-all-start) | async-done | bytes 65568 | tf_op jit(solution)/shard_map/all_to_all | solution.py:623
  43.1 0.7 %bias_sums.1 = f32[3,640]{1,0:T(4,128)} custom-call(f32[32,4,128]{2,1,0:T(4,128)S(1)} %all-to-all-done.tiles), custom_call_target="tpu_custom_call" | custom-call | tf_op jit(solution)/shard_map/bias_sums/pallas_call | solution.py:641
Async XLA Ops:
  2.1 4.7 %copy-start = (bf16[3,640]{1,0:T(4,128)(2,1)S(1)}, bf16[3,640]{1,0:T(4,128)(2,1)}, u32[]{:S(2)}) copy-start(bf16[3,640]{1,0:T(4,128)(2,1)} %refs_0_.1) | copy-start | bytes 11524
  2.1 9.0 %collective-permute-start = (bf16[320,256]{1,0:T(8,128)(2,1)S(1)}, bf16[320,256]{1,0:T(8,128)(2,1)S(1)}, u32[]{:S(2)}, u32[]{:S(2)}) collective-permute-start(bf16[320,256]{1,0:T(8,128)(2,1)S(1)} %get-tuple-element.62), channel_id=1, source_target_pairs={{0,3},{1,2},{2,1},{3,0},{4,7},{5,6},{6,5},{7,4},{8,11},{9,10},{10,... | collective-permute-start | bytes 491528 | tf_op jit(solution)/shard_map/ppermute | solution.py:520
  6.1 8.7 %collective-permute-start.3 = (bf16[320,256]{1,0:T(8,128)(2,1)S(1)}, bf16[320,256]{1,0:T(8,128)(2,1)S(1)}, u32[]{:S(2)}, u32[]{:S(2)}) collective-permute-start(bf16[320,256]{1,0:T(8,128)(2,1)S(1)} %get-tuple-element.71), channel_id=1, source_target_pairs={{0,2},{1,3},{2,0},{3,1},{4,6},{5,7},{6,4},{7,5},{8,10},{9,11},{10,... | collective-permute-start | bytes 491528 | tf_op jit(solution)/shard_map/ppermute | solution.py:520
  6.6 0.7 %copy-start.1 = (s32[1,4]{1,0:T(1,128)S(1)}, s32[1,4]{1,0:T(1,128)}, u32[]{:S(2)}) copy-start(s32[1,4]{1,0:T(1,128)} %lengths.1) | copy-start | bytes 52
  6.6 0.7 %copy-start.2 = (s32[1,4]{1,0:T(1,128)S(1)}, s32[1,4]{1,0:T(1,128)}, u32[]{:S(2)}) copy-start(s32[1,4]{1,0:T(1,128)} %widths.1) | copy-start | bytes 52
  6.6 8.7 %collective-permute-start.5 = (bf16[320,256]{1,0:T(8,128)(2,1)S(1)}, bf16[320,256]{1,0:T(8,128)(2,1)S(1)}, u32[]{:S(2)}, u32[]{:S(2)}) collective-permute-start(bf16[320,256]{1,0:T(8,128)(2,1)S(1)} %get-tuple-element.77), channel_id=1, source_target_pairs={{0,1},{1,0},{2,3},{3,2},{4,5},{5,4},{6,7},{7,6},{8,9},{9,8},{10,11... | collective-permute-start | bytes 491528 | tf_op jit(solution)/shard_map/ppermute | solution.py:520
  11.3 11.2 %collective-permute-start.1 = (bf16[320,256]{1,0:T(8,128)(2,1)S(1)}, bf16[320,256]{1,0:T(8,128)(2,1)S(1)}, u32[]{:S(2)}, u32[]{:S(2)}) collective-permute-start(bf16[320,256]{1,0:T(8,128)(2,1)S(1)} %get-tuple-element.65), channel_id=1, source_target_pairs={{0,3},{1,2},{2,1},{3,0},{4,7},{5,6},{6,5},{7,4},{8,11},{9,10},{10,... | collective-permute-start | bytes 491528 | tf_op jit(solution)/shard_map/ppermute | solution.py:581
  14.4 0.9 %copy-start.4 = (bf16[3,128,256]{2,1,0:T(8,128)(2,1)S(1)}, bf16[3,128,256]{2,1,0:T(8,128)(2,1)}, u32[]{:S(2)}) copy-start(bf16[3,128,256]{2,1,0:T(8,128)(2,1)} %get-tuple-element.78.refs_4_) | copy-start | bytes 589828
  14.4 8.2 %collective-permute-start.2 = (bf16[320,256]{1,0:T(8,128)(2,1)S(1)}, bf16[320,256]{1,0:T(8,128)(2,1)S(1)}, u32[]{:S(2)}, u32[]{:S(2)}) collective-permute-start(bf16[320,256]{1,0:T(8,128)(2,1)S(1)} %get-tuple-element.69), channel_id=1, source_target_pairs={{0,2},{1,3},{2,0},{3,1},{4,6},{5,7},{6,4},{7,5},{8,10},{9,11},{10,... | collective-permute-start | bytes 491528 | tf_op jit(solution)/shard_map/ppermute | solution.py:581
  15.0 7.5 %collective-permute-start.4 = (bf16[320,256]{1,0:T(8,128)(2,1)S(1)}, bf16[320,256]{1,0:T(8,128)(2,1)S(1)}, u32[]{:S(2)}, u32[]{:S(2)}) collective-permute-start(bf16[320,256]{1,0:T(8,128)(2,1)S(1)} %get-tuple-element.74), channel_id=1, source_target_pairs={{0,1},{1,0},{2,3},{3,2},{4,5},{5,4},{6,7},{7,6},{8,9},{9,8},{10,11... | collective-permute-start | bytes 491528 | tf_op jit(solution)/shard_map/ppermute | solution.py:581
  15.3 7.3 %copy-start.3 = (bf16[3,128,256]{2,1,0:T(8,128)(2,1)S(1)}, bf16[3,128,256]{2,1,0:T(8,128)(2,1)}, u32[]{:S(2)}) copy-start(bf16[3,128,256]{2,1,0:T(8,128)(2,1)} %get-tuple-element.75.refs_4_) | copy-start | bytes 589828
  19.7 9.3 %collective-permute-start.6 = (bf16[320,256]{1,0:T(8,128)(2,1)S(1)}, bf16[320,256]{1,0:T(8,128)(2,1)S(1)}, u32[]{:S(2)}, u32[]{:S(2)}) collective-permute-start(bf16[320,256]{1,0:T(8,128)(2,1)S(1)} %get-tuple-element.89), channel_id=1, source_target_pairs={{3,0},{2,1},{1,2},{0,3},{7,4},{6,5},{5,6},{4,7},{11,8},{10,9},{9,1... | collective-permute-start | bytes 491528 | tf_op jit(solution)/shard_map/ppermute | solution.py:72
  27.4 11.6 %collective-permute-start.8 = (bf16[640,256]{1,0:T(8,128)(2,1)S(1)}, bf16[640,256]{1,0:T(8,128)(2,1)S(1)}, u32[]{:S(2)}, u32[]{:S(2)}) collective-permute-start(bf16[640,256]{1,0:T(8,128)(2,1)S(1)} %get-tuple-element.93), channel_id=1, source_target_pairs={{2,0},{3,1},{0,2},{1,3},{6,4},{7,5},{4,6},{5,7},{10,8},{11,9},{8,1... | collective-permute-start | bytes 983048 | tf_op jit(solution)/shard_map/ppermute | solution.py:72
  28.0 11.6 %collective-permute-start.9 = (bf16[640,256]{1,0:T(8,128)(2,1)S(1)}, bf16[640,256]{1,0:T(8,128)(2,1)S(1)}, u32[]{:S(2)}, u32[]{:S(2)}) collective-permute-start(bf16[640,256]{1,0:T(8,128)(2,1)S(1)} %get-tuple-element.94), channel_id=1, source_target_pairs={{1,0},{0,1},{3,2},{2,3},{5,4},{4,5},{7,6},{6,7},{9,8},{8,9},{11,10... | collective-permute-start | bytes 983048 | tf_op jit(solution)/shard_map/ppermute | solution.py:72
  29.0 10.0 %collective-permute-start.7 = (bf16[320,256]{1,0:T(8,128)(2,1)S(1)}, bf16[320,256]{1,0:T(8,128)(2,1)S(1)}, u32[]{:S(2)}, u32[]{:S(2)}) collective-permute-start(bf16[320,256]{1,0:T(8,128)(2,1)S(1)} %get-tuple-element.91), channel_id=1, source_target_pairs={{3,0},{2,1},{1,2},{0,3},{7,4},{6,5},{5,6},{4,7},{11,8},{10,9},{9,1... | collective-permute-start | bytes 491528 | tf_op jit(solution)/shard_map/ppermute | solution.py:72
  31.0 12.1 %all-to-all-start = ((f32[32,4,128]{2,1,0:T(4,128)}), f32[32,4,128]{2,1,0:T(4,128)S(1)}, u32[]{:S(2)}, u32[]{:S(2)}) async-start(f32[32,4,128]{2,1,0:T(4,128)} %get-tuple-element.99), calls=%async_computation | async-start | bytes 131072 | tf_op jit(solution)/shard_map/all_to_all | solution.py:623

commit v21 on v19

--- a/solution.py
+++ b/solution.py
@@ -571,12 +571,14 @@
     own = [[prepared[phase], prepared[OWN_HEADS + phase]] for phase in phases]
     staged = [{0: pair} for pair in own]
     got = [first] + [[sent[0]] for sent in sends[1:]]
+    for phase in phases[1:]:
+        got[phase] += [None] * (slots - 2)
+        got[phase].append(lax.ppermute(sends[phase][-1], "tok", rounds[-1]))
     for slot in range(1, slots - 1):
         latest = stage_ahead(slot, (0,), [first[slot]])
         for phase in phases[1:]:
-            for leaving in (1, 2) if slot == 1 else (slot + 1,):
-                send, latest = lax.optimization_barrier((sends[phase][leaving], latest))
-                got[phase].append(lax.ppermute(send, "tok", rounds[leaving - 1]))
+            send, latest = lax.optimization_barrier((sends[phase][slot], latest))
+            got[phase][slot] = lax.ppermute(send, "tok", rounds[slot - 1])
         staged[0][slot] = latest[0]
     early = []
     carried = []

time: 43.8 us -> 44.4 us (1.014)
  starting transfers between devices: 19.3 us -> 20.3 us
    ppermute x3, starting transfers between devices: 3.78 us -> 5.75 us  [the longest x2 4.3 us: on_device(): got[phase][slot] = lax.ppermute(send, 'tok', rounds[slot - 1])]
    ppermute x4, starting transfers between devices: 6.45 us -> 4.5 us  [send_back(): lax.ppermute(result, 'tok', [(target, source) for source, target in pairs])]
    all_to_all x1, starting transfers between devices: 4.41 us -> 5.4 us  [on_device(): tiles = lax.all_to_all(total, ('dp', 'tok'), 0, 0, tiled=True)]
    ppermute x3, waiting for transfers between devices: 1.07 us -> 0.11 us  [on_device(): lax.ppermute(send, 'tok', pairs)]
    ppermute x4, waiting for transfers between devices: 4.19 us -> 5.05 us  [send_back(): lax.ppermute(result, 'tok', [(target, source) for source, target in pairs])]
  transfers between devices with their start and end apart: 11 -> 11, of which waited for: 4 -> 3; matrix products, arithmetic and copies ran while one was open for 0% -> 0% of each run, Pallas kernels for 31% -> 30%
where the time goes in v21:
time: 44.4 us; the launch traced here: 44.2 us
  starting transfers between devices  20.3 us (46%)
  Pallas kernels  15.6 us (35%)
  waiting for transfers between devices  7.11 us (16%)
  between operations  0.73 us (2%)
  local copies, waits for them, and re-layouts  0.48 us (1%)
    pallas_call x2, Pallas kernels, on_device(): pl.pallas_call(functools.partial(attend_kernel, slots, tuple(staged[phase...  8.88 us
    all_to_all x1, starting transfers between devices, on_device(): tiles = lax.all_to_all(total, ('dp', 'tok'), 0, 0, tiled=True)  5.4 us
    ppermute x4, waiting for transfers between devices, send_back(): lax.ppermute(result, 'tok', [(target, source) for source, target in pairs])  5.05 us
    ppermute x3, starting transfers between devices, on_device(): lax.ppermute(send, 'tok', pairs)  4.66 us
    ppermute x4, starting transfers between devices, send_back(): lax.ppermute(result, 'tok', [(target, source) for source, target in pairs])  4.5 us
    ppermute x2, starting transfers between devices, on_device(): got[phase][slot] = lax.ppermute(send, 'tok', rounds[slot - 1])  4.3 us
    pallas_call x1, Pallas kernels, on_device(): pl.pallas_call(functools.partial(prepare_kernel, slots, images, count, to...  2.84 us
    all_to_all x1, waiting for transfers between devices, on_device(): tiles = lax.all_to_all(total, ('dp', 'tok'), 0, 0, tiled=True)  1.95 us
  transfers between devices with their start and end apart: 11, of which 3 were waited for; matrix products, arithmetic and copies ran while one was open for 0% of the time, Pallas kernels for 30%

profile of v21, /device:TPU:0, one launch (start us, length us, event | category | flops | bytes accessed | tf_op | source)
XLA Modules:
  0.0 44.2 jit_solution(8145231666461415722)
XLA Ops:
  0.6 1.5 %pack_heads.1 = (bf16[320,256]{1,0:T(8,128)(2,1)S(1)}, bf16[320,256]{1,0:T(8,128)(2,1)S(1)}, bf16[320,256]{1,0:T(8,128)(2,1)S(1)}, bf16[320,256]{1,0:T(8,128)(2,1)S(1)}) custom-call(bf16[256,640]{1,0:T(8,128)(2,1)} %bitcast.8, bf16[256,640]{1,0:T(8,128)(2,1)} %bitcast.10, bf16[256,640]{1,0:T(8,128)(2,1)} %bitcast.12, bf16[256,640]{1,0:T(8,128)(2,1)} %bitcast.14), custom_call_target="tpu_custom_call" | custom-call | tf_op jit(solution)/shard_map/pack_heads/pallas_call | solution.py:502
  2.1 0.0 copy-start
  2.1 4.0 %collective-permute-start = (bf16[320,256]{1,0:T(8,128)(2,1)S(1)}, bf16[320,256]{1,0:T(8,128)(2,1)S(1)}, u32[]{:S(2)}, u32[]{:S(2)}) collective-permute-start(bf16[320,256]{1,0:T(8,128)(2,1)S(1)} %get-tuple-element.59), channel_id=1, source_target_pairs={{0,3},{1,2},{2,1},{3,0},{4,7},{5,6},{6,5},{7,4},{8,11},{9,10},{10,... | collective-permute-start | bytes 491528 | tf_op jit(solution)/shard_map/ppermute | solution.py:518
  6.1 0.4 collective-permute-start.2
  6.6 0.0 copy-start.1
  6.6 0.0 copy-start.2
  6.6 0.2 collective-permute-start.5
  6.8 0.0 copy-done
  6.8 0.4 %copy-done.1 = s32[1,4]{1,0:T(1,128)S(1)} copy-done((s32[1,4]{1,0:T(1,128)S(1)}, s32[1,4]{1,0:T(1,128)}, u32[]{:S(2)}) %copy-start.1) | copy-done | bytes 40
  7.2 0.0 copy-done.2
  7.2 2.8 %prepare.1 = (f32[40,1024]{1,0:T(8,128)S(1)}, f32[40,1024]{1,0:T(8,128)S(1)}, f32[24,256]{1,0:T(8,128)S(1)}, f32[160,128]{1,0:T(8,128)S(1)}, bf16[320,256]{1,0:T...) custom-call(s32[1,4]{1,0:T(1,128)S(1)} %copy-done.1, ...), custom_call_target="tpu_custom_call" | custom-call | flops 1000000 | tf_op jit(solution)/shard_map/prepare/pallas_call | solution.py:535
  10.1 1.5 %collective-permute-start.4 = (bf16[320,256]{1,0:T(8,128)(2,1)S(1)}, bf16[320,256]{1,0:T(8,128)(2,1)S(1)}, u32[]{:S(2)}, u32[]{:S(2)}) collective-permute-start(bf16[320,256]{1,0:T(8,128)(2,1)S(1)} %get-tuple-element.68), channel_id=1, source_target_pairs={{0,1},{1,0},{2,3},{3,2},{4,5},{5,4},{6,7},{7,6},{8,9},{9,8},{10,11... | collective-permute-start | bytes 491528 | tf_op jit(solution)/shard_map/ppermute | solution.py:576
  11.5 0.0 collective-permute-done.refs_0_.refs_1_
  11.5 0.2 stage_slot.2
  11.7 0.0 copy-start.4
  11.7 2.7 %collective-permute-start.1 = (bf16[320,256]{1,0:T(8,128)(2,1)S(1)}, bf16[320,256]{1,0:T(8,128)(2,1)S(1)}, u32[]{:S(2)}, u32[]{:S(2)}) collective-permute-start(bf16[320,256]{1,0:T(8,128)(2,1)S(1)} %get-tuple-element.62), channel_id=1, source_target_pairs={{0,3},{1,2},{2,1},{3,0},{4,7},{5,6},{6,5},{7,4},{8,11},{9,10},{10,... | collective-permute-start | bytes 491528 | tf_op jit(solution)/shard_map/ppermute | solution.py:581
  14.4 0.1 collective-permute-done.2.refs_0_.refs_2_
  14.5 0.2 stage_slot.3
  14.7 1.6 %collective-permute-start.3 = (bf16[320,256]{1,0:T(8,128)(2,1)S(1)}, bf16[320,256]{1,0:T(8,128)(2,1)S(1)}, u32[]{:S(2)}, u32[]{:S(2)}) collective-permute-start(bf16[320,256]{1,0:T(8,128)(2,1)S(1)} %get-tuple-element.67), channel_id=1, source_target_pairs={{0,2},{1,3},{2,0},{3,1},{4,6},{5,7},{6,4},{7,5},{8,10},{9,11},{10,... | collective-permute-start | bytes 491528 | tf_op jit(solution)/shard_map/ppermute | solution.py:581
  16.3 0.0 collective-permute-done.5.refs_3_
  16.3 0.0 copy-done.4
  16.3 0.0 copy-start.3
  16.3 4.2 %attend_head.2 = (bf16[640,256]{1,0:T(8,128)(2,1)S(1)}, bf16[320,256]{1,0:T(8,128)(2,1)S(1)}, bf16[640,256]{1,0:T(8,128)(2,1)S(1)}, bf16[640,256]{1,0:T(8,128)(2,1)S(1)}, f32[8,128]{1,0:T(8,128)S(1)}) custom-call(f32[40,1024]{1,0:T(8,128)S(1)} %get-tuple-element.53.cosv, f32[40,1024]{1,0:T(8,128)S(1)} %get-tuple-element.54.sinv, ...), custom_call_target="tpu_custom_call" | custom-call | flops 3221225472 | tf_op jit(solution)/shard_map/attend_head/pallas_call | solution.py:591
  20.6 0.8 %collective-permute-start.6 = (bf16[320,256]{1,0:T(8,128)(2,1)S(1)}, bf16[320,256]{1,0:T(8,128)(2,1)S(1)}, u32[]{:S(2)}, u32[]{:S(2)}) collective-permute-start(bf16[320,256]{1,0:T(8,128)(2,1)S(1)} %get-tuple-element.83), channel_id=1, source_target_pairs={{3,0},{2,1},{1,2},{0,3},{7,4},{6,5},{5,6},{4,7},{11,8},{10,9},{9,1... | collective-permute-start | bytes 491528 | tf_op jit(solution)/shard_map/ppermute | solution.py:72
  21.3 0.0 collective-permute-done.4.refs_3_
  21.3 0.0 collective-permute-done.1.refs_1_
  21.3 0.0 collective-permute-done.3.refs_2_
  21.4 0.0 copy-done.3
  21.4 4.7 %attend_head.3 = (bf16[640,256]{1,0:T(8,128)(2,1)S(1)}, bf16[320,256]{1,0:T(8,128)(2,1)S(1)}, bf16[640,256]{1,0:T(8,128)(2,1)S(1)}, bf16[640,256]{1,0:T(8,128)(2,1)S(1)}, f32[32,4,128]{2,1,0:T(4,128)}) custom-call(f32[40,1024]{1,0:T(8,128)S(1)} %get-tuple-element.53.cosv, f32[40,1024]{1,0:T(8,128)S(1)} %get-tuple-element.54.sinv, ...), custom_call_target="tpu_custom_call" | custom-call | flops 3221225472 | tf_op jit(solution)/shard_map/attend_head/pallas_call | solution.py:591
  26.1 1.4 %collective-permute-start.8 = (bf16[640,256]{1,0:T(8,128)(2,1)S(1)}, bf16[640,256]{1,0:T(8,128)(2,1)S(1)}, u32[]{:S(2)}, u32[]{:S(2)}) collective-permute-start(bf16[640,256]{1,0:T(8,128)(2,1)S(1)} %get-tuple-element.87), channel_id=1, source_target_pairs={{2,0},{3,1},{0,2},{1,3},{6,4},{7,5},{4,6},{5,7},{10,8},{11,9},{8,1... | collective-permute-start | bytes 983048 | tf_op jit(solution)/shard_map/ppermute | solution.py:72
  27.5 1.4 %collective-permute-start.9 = (bf16[640,256]{1,0:T(8,128)(2,1)S(1)}, bf16[640,256]{1,0:T(8,128)(2,1)S(1)}, u32[]{:S(2)}, u32[]{:S(2)}) collective-permute-start(bf16[640,256]{1,0:T(8,128)(2,1)S(1)} %get-tuple-element.88), channel_id=1, source_target_pairs={{1,0},{0,1},{3,2},{2,3},{5,4},{4,5},{7,6},{6,7},{9,8},{8,9},{11,10... | collective-permute-start | bytes 983048 | tf_op jit(solution)/shard_map/ppermute | solution.py:72
  28.9 0.0 collective-permute-done.6.refs_0_
  28.9 0.9 %collective-permute-start.7 = (bf16[320,256]{1,0:T(8,128)(2,1)S(1)}, bf16[320,256]{1,0:T(8,128)(2,1)S(1)}, u32[]{:S(2)}, u32[]{:S(2)}) collective-permute-start(bf16[320,256]{1,0:T(8,128)(2,1)S(1)} %get-tuple-element.85), channel_id=1, source_target_pairs={{3,0},{2,1},{1,2},{0,3},{7,4},{6,5},{5,6},{4,7},{11,8},{10,9},{9,1... | collective-permute-start | bytes 491528 | tf_op jit(solution)/shard_map/ppermute | solution.py:72
  29.8 5.4 %all-to-all-start = ((f32[32,4,128]{2,1,0:T(4,128)}), f32[32,4,128]{2,1,0:T(4,128)S(1)}, u32[]{:S(2)}, u32[]{:S(2)}) async-start(f32[32,4,128]{2,1,0:T(4,128)} %get-tuple-element.93), calls=%async_computation | async-start | bytes 131072 | tf_op jit(solution)/shard_map/all_to_all | solution.py:623
  35.2 5.0 %collective-permute-done.7.refs_1_ = bf16[320,256]{1,0:T(8,128)(2,1)S(1)} collective-permute-done((bf16[320,256]{1,0:T(8,128)(2,1)S(1)}, bf16[320,256]{1,0:T(8,128)(2,1)S(1)}, u32[]{:S(2)}, u32[]{:S(2)}) %collective-permute-start.7) | collective-permute-done | bytes 163872 | tf_op jit(solution)/shard_map/ppermute | solution.py:72
  40.2 0.0 collective-permute-done.8.refs_3_
  40.2 0.0 collective-permute-done.9.refs_4_
  40.2 1.3 %unpack_heads.1 = (bf16[256,640]{1,0:T(8,128)(2,1)}, bf16[256,640]{1,0:T(8,128)(2,1)}, bf16[256,640]{1,0:T(8,128)(2,1)}, bf16[256,640]{1,0:T(8,128)(2,1)}) custom-call(bf16[320,256]{1,0:T(8,128)(2,1)S(1)} %collective-permute-done.6.refs_0_, bf16[320,256]{1,0:T(8,128)(2,1)S(1)} %collective-permute-done.7.refs_1_, ...), custom_call_target="tpu_custom_call" | custom-call | flops 20000000000 | tf_op jit(solution)/shard_map/unpack_heads/pallas_call | solution.py:626
  41.6 1.9 %all-to-all-done.tiles = f32[32,4,128]{2,1,0:T(4,128)S(1)} async-done(((f32[32,4,128]{2,1,0:T(4,128)}), f32[32,4,128]{2,1,0:T(4,128)S(1)}, u32[]{:S(2)}, u32[]{:S(2)}) %all-to-all-start) | async-done | bytes 65568 | tf_op jit(solution)/shard_map/all_to_all | solution.py:623
  43.5 0.7 %bias_sums.1 = f32[3,640]{1,0:T(4,128)} custom-call(f32[32,4,128]{2,1,0:T(4,128)S(1)} %all-to-all-done.tiles), custom_call_target="tpu_custom_call" | custom-call | tf_op jit(solution)/shard_map/bias_sums/pallas_call | solution.py:641
Async XLA Ops:
  2.1 4.7 %copy-start = (bf16[3,640]{1,0:T(4,128)(2,1)S(1)}, bf16[3,640]{1,0:T(4,128)(2,1)}, u32[]{:S(2)}) copy-start(bf16[3,640]{1,0:T(4,128)(2,1)} %refs_0_.1) | copy-start | bytes 11524
  2.1 9.4 %collective-permute-start = (bf16[320,256]{1,0:T(8,128)(2,1)S(1)}, bf16[320,256]{1,0:T(8,128)(2,1)S(1)}, u32[]{:S(2)}, u32[]{:S(2)}) collective-permute-start(bf16[320,256]{1,0:T(8,128)(2,1)S(1)} %get-tuple-element.59), channel_id=1, source_target_pairs={{0,3},{1,2},{2,1},{3,0},{4,7},{5,6},{6,5},{7,4},{8,11},{9,10},{10,... | collective-permute-start | bytes 491528 | tf_op jit(solution)/shard_map/ppermute | solution.py:518
  6.1 8.4 %collective-permute-start.2 = (bf16[320,256]{1,0:T(8,128)(2,1)S(1)}, bf16[320,256]{1,0:T(8,128)(2,1)S(1)}, u32[]{:S(2)}, u32[]{:S(2)}) collective-permute-start(bf16[320,256]{1,0:T(8,128)(2,1)S(1)} %get-tuple-element.64), channel_id=1, source_target_pairs={{0,2},{1,3},{2,0},{3,1},{4,6},{5,7},{6,4},{7,5},{8,10},{9,11},{10,... | collective-permute-start | bytes 491528 | tf_op jit(solution)/shard_map/ppermute | solution.py:518
  6.6 0.7 %copy-start.1 = (s32[1,4]{1,0:T(1,128)S(1)}, s32[1,4]{1,0:T(1,128)}, u32[]{:S(2)}) copy-start(s32[1,4]{1,0:T(1,128)} %lengths.1) | copy-start | bytes 52
  6.6 0.7 %copy-start.2 = (s32[1,4]{1,0:T(1,128)S(1)}, s32[1,4]{1,0:T(1,128)}, u32[]{:S(2)}) copy-start(s32[1,4]{1,0:T(1,128)} %widths.1) | copy-start | bytes 52
  6.6 9.8 %collective-permute-start.5 = (bf16[320,256]{1,0:T(8,128)(2,1)S(1)}, bf16[320,256]{1,0:T(8,128)(2,1)S(1)}, u32[]{:S(2)}, u32[]{:S(2)}) collective-permute-start(bf16[320,256]{1,0:T(8,128)(2,1)S(1)} %get-tuple-element.71), channel_id=1, source_target_pairs={{0,1},{1,0},{2,3},{3,2},{4,5},{5,4},{6,7},{7,6},{8,9},{9,8},{10,11... | collective-permute-start | bytes 491528 | tf_op jit(solution)/shard_map/ppermute | solution.py:518
  10.1 11.3 %collective-permute-start.4 = (bf16[320,256]{1,0:T(8,128)(2,1)S(1)}, bf16[320,256]{1,0:T(8,128)(2,1)S(1)}, u32[]{:S(2)}, u32[]{:S(2)}) collective-permute-start(bf16[320,256]{1,0:T(8,128)(2,1)S(1)} %get-tuple-element.68), channel_id=1, source_target_pairs={{0,1},{1,0},{2,3},{3,2},{4,5},{5,4},{6,7},{7,6},{8,9},{9,8},{10,11... | collective-permute-start | bytes 491528 | tf_op jit(solution)/shard_map/ppermute | solution.py:576
  11.7 4.6 %copy-start.4 = (bf16[3,128,256]{2,1,0:T(8,128)(2,1)S(1)}, bf16[3,128,256]{2,1,0:T(8,128)(2,1)}, u32[]{:S(2)}) copy-start(bf16[3,128,256]{2,1,0:T(8,128)(2,1)} %get-tuple-element.72.refs_4_) | copy-start | bytes 589828
  11.7 9.6 %collective-permute-start.1 = (bf16[320,256]{1,0:T(8,128)(2,1)S(1)}, bf16[320,256]{1,0:T(8,128)(2,1)S(1)}, u32[]{:S(2)}, u32[]{:S(2)}) collective-permute-start(bf16[320,256]{1,0:T(8,128)(2,1)S(1)} %get-tuple-element.62), channel_id=1, source_target_pairs={{0,3},{1,2},{2,1},{3,0},{4,7},{5,6},{6,5},{7,4},{8,11},{9,10},{10,... | collective-permute-start | bytes 491528 | tf_op jit(solution)/shard_map/ppermute | solution.py:581
  14.7 6.6 %collective-permute-start.3 = (bf16[320,256]{1,0:T(8,128)(2,1)S(1)}, bf16[320,256]{1,0:T(8,128)(2,1)S(1)}, u32[]{:S(2)}, u32[]{:S(2)}) collective-permute-start(bf16[320,256]{1,0:T(8,128)(2,1)S(1)} %get-tuple-element.67), channel_id=1, source_target_pairs={{0,2},{1,3},{2,0},{3,1},{4,6},{5,7},{6,4},{7,5},{8,10},{9,11},{10,... | collective-permute-start | bytes 491528 | tf_op jit(solution)/shard_map/ppermute | solution.py:581
  16.3 5.0 %copy-start.3 = (bf16[3,128,256]{2,1,0:T(8,128)(2,1)S(1)}, bf16[3,128,256]{2,1,0:T(8,128)(2,1)}, u32[]{:S(2)}) copy-start(bf16[3,128,256]{2,1,0:T(8,128)(2,1)} %get-tuple-element.69.refs_4_) | copy-start | bytes 589828
  20.6 8.3 %collective-permute-start.6 = (bf16[320,256]{1,0:T(8,128)(2,1)S(1)}, bf16[320,256]{1,0:T(8,128)(2,1)S(1)}, u32[]{:S(2)}, u32[]{:S(2)}) collective-permute-start(bf16[320,256]{1,0:T(8,128)(2,1)S(1)} %get-tuple-element.83), channel_id=1, source_target_pairs={{3,0},{2,1},{1,2},{0,3},{7,4},{6,5},{5,6},{4,7},{11,8},{10,9},{9,1... | collective-permute-start | bytes 491528 | tf_op jit(solution)/shard_map/ppermute | solution.py:72
  26.1 14.2 %collective-permute-start.8 = (bf16[640,256]{1,0:T(8,128)(2,1)S(1)}, bf16[640,256]{1,0:T(8,128)(2,1)S(1)}, u32[]{:S(2)}, u32[]{:S(2)}) collective-permute-start(bf16[640,256]{1,0:T(8,128)(2,1)S(1)} %get-tuple-element.87), channel_id=1, source_target_pairs={{2,0},{3,1},{0,2},{1,3},{6,4},{7,5},{4,6},{5,7},{10,8},{11,9},{8,1... | collective-permute-start | bytes 983048 | tf_op jit(solution)/shard_map/ppermute | solution.py:72
  27.5 12.8 %collective-permute-start.9 = (bf16[640,256]{1,0:T(8,128)(2,1)S(1)}, bf16[640,256]{1,0:T(8,128)(2,1)S(1)}, u32[]{:S(2)}, u32[]{:S(2)}) collective-permute-start(bf16[640,256]{1,0:T(8,128)(2,1)S(1)} %get-tuple-element.88), channel_id=1, source_target_pairs={{1,0},{0,1},{3,2},{2,3},{5,4},{4,5},{7,6},{6,7},{9,8},{8,9},{11,10... | collective-permute-start | bytes 983048 | tf_op jit(solution)/shard_map/ppermute | solution.py:72
  28.9 11.3 %collective-permute-start.7 = (bf16[320,256]{1,0:T(8,128)(2,1)S(1)}, bf16[320,256]{1,0:T(8,128)(2,1)S(1)}, u32[]{:S(2)}, u32[]{:S(2)}) collective-permute-start(bf16[320,256]{1,0:T(8,128)(2,1)S(1)} %get-tuple-element.85), channel_id=1, source_target_pairs={{3,0},{2,1},{1,2},{0,3},{7,4},{6,5},{5,6},{4,7},{11,8},{10,9},{9,1... | collective-permute-start | bytes 491528 | tf_op jit(solution)/shard_map/ppermute | solution.py:72
  29.8 13.7 %all-to-all-start = ((f32[32,4,128]{2,1,0:T(4,128)}), f32[32,4,128]{2,1,0:T(4,128)S(1)}, u32[]{:S(2)}, u32[]{:S(2)}) async-start(f32[32,4,128]{2,1,0:T(4,128)} %get-tuple-element.93), calls=%async_computation | async-start | bytes 131072 | tf_op jit(solution)/shard_map/all_to_all | solution.py:623

commit v22 on v19

--- a/solution.py
+++ b/solution.py
@@ -288,8 +288,8 @@
         return jnp.max(part, axis=0, keepdims=True)
 
     def exponentials(slot, keys, top):
-        part = jnp.exp2(s_buf[slot % 2, keys, :] - top)
-        e_buf[keys, block_of(slot)] = part.astype(jnp.bfloat16)
+        part = (s_buf[slot % 2, keys, :] - top).astype(jnp.bfloat16)
+        e_buf[keys, block_of(slot)] = jnp.exp2(part)
 
     def output(slot):
         mixed = jnp.dot(

time: 43.8 us -> 43.9 us (level)
  no operation moved by 1% of the time
where the time goes in v22:
time: 43.9 us; the launch traced here: 43.7 us
  starting transfers between devices  19.3 us (44%)
  Pallas kernels  15.7 us (36%)
  waiting for transfers between devices  7.44 us (17%)
  between operations  0.73 us (2%)
  local copies, waits for them, and re-layouts  0.49 us (1%)
    pallas_call x2, Pallas kernels, on_device(): pl.pallas_call(functools.partial(attend_kernel, slots, tuple(staged[phase...  8.98 us
    ppermute x4, starting transfers between devices, send_back(): lax.ppermute(result, 'tok', [(target, source) for source, target in pairs])  6.46 us
    ppermute x3, starting transfers between devices, on_device(): lax.ppermute(send, 'tok', pairs)  4.66 us
    all_to_all x1, starting transfers between devices, on_device(): tiles = lax.all_to_all(total, ('dp', 'tok'), 0, 0, tiled=True)  4.44 us
    ppermute x4, waiting for transfers between devices, send_back(): lax.ppermute(result, 'tok', [(target, source) for source, target in pairs])  4.15 us
    ppermute x3, starting transfers between devices, on_device(): got[phase].append(lax.ppermute(send, 'tok', rounds[leaving - 1]))  3.78 us
    pallas_call x1, Pallas kernels, on_device(): pl.pallas_call(functools.partial(prepare_kernel, slots, images, count, to...  2.84 us
    all_to_all x1, waiting for transfers between devices, on_device(): tiles = lax.all_to_all(total, ('dp', 'tok'), 0, 0, tiled=True)  2.21 us
  transfers between devices with their start and end apart: 11, of which 4 were waited for; matrix products, arithmetic and copies ran while one was open for 0% of the time, Pallas kernels for 31%

profile of v22, /device:TPU:0, one launch (start us, length us, event | category | flops | bytes accessed | tf_op | source)
XLA Modules:
  0.0 43.7 jit_solution(15183688573002044676)
XLA Ops:
  0.6 1.5 %pack_heads.1 = (bf16[320,256]{1,0:T(8,128)(2,1)S(1)}, bf16[320,256]{1,0:T(8,128)(2,1)S(1)}, bf16[320,256]{1,0:T(8,128)(2,1)S(1)}, bf16[320,256]{1,0:T(8,128)(2,1)S(1)}) custom-call(bf16[256,640]{1,0:T(8,128)(2,1)} %bitcast.8, bf16[256,640]{1,0:T(8,128)(2,1)} %bitcast.10, bf16[256,640]{1,0:T(8,128)(2,1)} %bitcast.12, bf16[256,640]{1,0:T(8,128)(2,1)} %bitcast.14), custom_call_target="tpu_custom_call" | custom-call | tf_op jit(solution)/shard_map/pack_heads/pallas_call | solution.py:502
  2.1 0.0 copy-start
  2.1 4.0 %collective-permute-start = (bf16[320,256]{1,0:T(8,128)(2,1)S(1)}, bf16[320,256]{1,0:T(8,128)(2,1)S(1)}, u32[]{:S(2)}, u32[]{:S(2)}) collective-permute-start(bf16[320,256]{1,0:T(8,128)(2,1)S(1)} %get-tuple-element.62), channel_id=1, source_target_pairs={{0,3},{1,2},{2,1},{3,0},{4,7},{5,6},{6,5},{7,4},{8,11},{9,10},{10,... | collective-permute-start | bytes 491528 | tf_op jit(solution)/shard_map/ppermute | solution.py:518
  6.1 0.4 %collective-permute-start.3 = (bf16[320,256]{1,0:T(8,128)(2,1)S(1)}, bf16[320,256]{1,0:T(8,128)(2,1)S(1)}, u32[]{:S(2)}, u32[]{:S(2)}) collective-permute-start(bf16[320,256]{1,0:T(8,128)(2,1)S(1)} %get-tuple-element.71), channel_id=1, source_target_pairs={{0,2},{1,3},{2,0},{3,1},{4,6},{5,7},{6,4},{7,5},{8,10},{9,11},{10,... | collective-permute-start | bytes 491528 | tf_op jit(solution)/shard_map/ppermute | solution.py:518
  6.6 0.0 copy-start.1
  6.6 0.0 copy-start.2
  6.6 0.2 collective-permute-start.5
  6.8 0.0 copy-done
  6.8 0.4 %copy-done.1 = s32[1,4]{1,0:T(1,128)S(1)} copy-done((s32[1,4]{1,0:T(1,128)S(1)}, s32[1,4]{1,0:T(1,128)}, u32[]{:S(2)}) %copy-start.1) | copy-done | bytes 40
  7.2 0.0 copy-done.2
  7.2 2.8 %prepare.1 = (f32[40,1024]{1,0:T(8,128)S(1)}, f32[40,1024]{1,0:T(8,128)S(1)}, f32[24,256]{1,0:T(8,128)S(1)}, f32[160,128]{1,0:T(8,128)S(1)}, bf16[320,256]{1,0:T...) custom-call(s32[1,4]{1,0:T(1,128)S(1)} %copy-done.1, ...), custom_call_target="tpu_custom_call" | custom-call | flops 1000000 | tf_op jit(solution)/shard_map/prepare/pallas_call | solution.py:535
  10.1 1.1 %collective-permute-done.refs_0_.refs_1_ = bf16[320,256]{1,0:T(8,128)(2,1)S(1)} collective-permute-done((bf16[320,256]{1,0:T(8,128)(2,1)S(1)}, bf16[320,256]{1,0:T(8,128)(2,1)S(1)}, u32[]{:S(2)}, u32[]{:S(2)}) %collective-permute-start) | collective-permute-done | bytes 163872 | tf_op jit(solution)/shard_map/ppermute | solution.py:518
  11.2 0.2 stage_slot.2
  11.3 3.1 %collective-permute-start.1 = (bf16[320,256]{1,0:T(8,128)(2,1)S(1)}, bf16[320,256]{1,0:T(8,128)(2,1)S(1)}, u32[]{:S(2)}, u32[]{:S(2)}) collective-permute-start(bf16[320,256]{1,0:T(8,128)(2,1)S(1)} %get-tuple-element.65), channel_id=1, source_target_pairs={{0,3},{1,2},{2,1},{3,0},{4,7},{5,6},{6,5},{7,4},{8,11},{9,10},{10,... | collective-permute-start | bytes 491528 | tf_op jit(solution)/shard_map/ppermute | solution.py:579
  14.4 0.0 copy-start.4
  14.4 0.4 %collective-permute-start.2 = (bf16[320,256]{1,0:T(8,128)(2,1)S(1)}, bf16[320,256]{1,0:T(8,128)(2,1)S(1)}, u32[]{:S(2)}, u32[]{:S(2)}) collective-permute-start(bf16[320,256]{1,0:T(8,128)(2,1)S(1)} %get-tuple-element.69), channel_id=1, source_target_pairs={{0,2},{1,3},{2,0},{3,1},{4,6},{5,7},{6,4},{7,5},{8,10},{9,11},{10,... | collective-permute-start | bytes 491528 | tf_op jit(solution)/shard_map/ppermute | solution.py:579
  14.9 0.0 collective-permute-done.3.refs_0_.refs_2_
  14.9 0.2 stage_slot.3
  15.0 0.3 collective-permute-start.4
  15.3 0.0 collective-permute-done.5.refs_3_
  15.3 0.0 copy-done.4
  15.3 0.0 copy-start.3
  15.3 4.2 %attend_head.2 = (bf16[640,256]{1,0:T(8,128)(2,1)S(1)}, bf16[320,256]{1,0:T(8,128)(2,1)S(1)}, bf16[640,256]{1,0:T(8,128)(2,1)S(1)}, bf16[640,256]{1,0:T(8,128)(2,1)S(1)}, f32[8,128]{1,0:T(8,128)S(1)}) custom-call(f32[40,1024]{1,0:T(8,128)S(1)} %get-tuple-element.56.cosv, f32[40,1024]{1,0:T(8,128)S(1)} %get-tuple-element.57.sinv, ...), custom_call_target="tpu_custom_call" | custom-call | flops 3221225472 | tf_op jit(solution)/shard_map/attend_head/pallas_call | solution.py:589
  19.5 2.9 %collective-permute-start.6 = (bf16[320,256]{1,0:T(8,128)(2,1)S(1)}, bf16[320,256]{1,0:T(8,128)(2,1)S(1)}, u32[]{:S(2)}, u32[]{:S(2)}) collective-permute-start(bf16[320,256]{1,0:T(8,128)(2,1)S(1)} %get-tuple-element.89), channel_id=1, source_target_pairs={{3,0},{2,1},{1,2},{0,3},{7,4},{6,5},{5,6},{4,7},{11,8},{10,9},{9,1... | collective-permute-start | bytes 491528 | tf_op jit(solution)/shard_map/ppermute | solution.py:72
  22.4 0.0 collective-permute-done.1.refs_1_
  22.4 0.0 collective-permute-done.2.refs_2_
  22.4 0.0 collective-permute-done.4.refs_3_
  22.4 0.0 copy-done.3
  22.4 4.8 %attend_head.3 = (bf16[640,256]{1,0:T(8,128)(2,1)S(1)}, bf16[320,256]{1,0:T(8,128)(2,1)S(1)}, bf16[640,256]{1,0:T(8,128)(2,1)S(1)}, bf16[640,256]{1,0:T(8,128)(2,1)S(1)}, f32[32,4,128]{2,1,0:T(4,128)}) custom-call(f32[40,1024]{1,0:T(8,128)S(1)} %get-tuple-element.56.cosv, f32[40,1024]{1,0:T(8,128)S(1)} %get-tuple-element.57.sinv, ...), custom_call_target="tpu_custom_call" | custom-call | flops 3221225472 | tf_op jit(solution)/shard_map/attend_head/pallas_call | solution.py:589
  27.3 0.5 %collective-permute-start.8 = (bf16[640,256]{1,0:T(8,128)(2,1)S(1)}, bf16[640,256]{1,0:T(8,128)(2,1)S(1)}, u32[]{:S(2)}, u32[]{:S(2)}) collective-permute-start(bf16[640,256]{1,0:T(8,128)(2,1)S(1)} %get-tuple-element.93), channel_id=1, source_target_pairs={{2,0},{3,1},{0,2},{1,3},{6,4},{7,5},{4,6},{5,7},{10,8},{11,9},{8,1... | collective-permute-start | bytes 983048 | tf_op jit(solution)/shard_map/ppermute | solution.py:72
  27.8 1.2 %collective-permute-start.9 = (bf16[640,256]{1,0:T(8,128)(2,1)S(1)}, bf16[640,256]{1,0:T(8,128)(2,1)S(1)}, u32[]{:S(2)}, u32[]{:S(2)}) collective-permute-start(bf16[640,256]{1,0:T(8,128)(2,1)S(1)} %get-tuple-element.94), channel_id=1, source_target_pairs={{1,0},{0,1},{3,2},{2,3},{5,4},{4,5},{7,6},{6,7},{9,8},{8,9},{11,10... | collective-permute-start | bytes 983048 | tf_op jit(solution)/shard_map/ppermute | solution.py:72
  29.0 0.0 collective-permute-done.6.refs_0_
  29.0 1.8 %collective-permute-start.7 = (bf16[320,256]{1,0:T(8,128)(2,1)S(1)}, bf16[320,256]{1,0:T(8,128)(2,1)S(1)}, u32[]{:S(2)}, u32[]{:S(2)}) collective-permute-start(bf16[320,256]{1,0:T(8,128)(2,1)S(1)} %get-tuple-element.91), channel_id=1, source_target_pairs={{3,0},{2,1},{1,2},{0,3},{7,4},{6,5},{5,6},{4,7},{11,8},{10,9},{9,1... | collective-permute-start | bytes 491528 | tf_op jit(solution)/shard_map/ppermute | solution.py:72
  30.8 4.4 %all-to-all-start = ((f32[32,4,128]{2,1,0:T(4,128)}), f32[32,4,128]{2,1,0:T(4,128)S(1)}, u32[]{:S(2)}, u32[]{:S(2)}) async-start(f32[32,4,128]{2,1,0:T(4,128)} %get-tuple-element.99), calls=%async_computation | async-start | bytes 131072 | tf_op jit(solution)/shard_map/all_to_all | solution.py:621
  35.3 3.7 %collective-permute-done.7.refs_1_ = bf16[320,256]{1,0:T(8,128)(2,1)S(1)} collective-permute-done((bf16[320,256]{1,0:T(8,128)(2,1)S(1)}, bf16[320,256]{1,0:T(8,128)(2,1)S(1)}, u32[]{:S(2)}, u32[]{:S(2)}) %collective-permute-start.7) | collective-permute-done | bytes 163872 | tf_op jit(solution)/shard_map/ppermute | solution.py:72
  39.0 0.0 collective-permute-done.8.refs_3_
  39.0 0.5 %collective-permute-done.9.refs_4_ = bf16[640,256]{1,0:T(8,128)(2,1)S(1)} collective-permute-done((bf16[640,256]{1,0:T(8,128)(2,1)S(1)}, bf16[640,256]{1,0:T(8,128)(2,1)S(1)}, u32[]{:S(2)}, u32[]{:S(2)}) %collective-permute-start.9) | collective-permute-done | bytes 327712 | tf_op jit(solution)/shard_map/ppermute | solution.py:72
  39.4 1.3 %unpack_heads.1 = (bf16[256,640]{1,0:T(8,128)(2,1)}, bf16[256,640]{1,0:T(8,128)(2,1)}, bf16[256,640]{1,0:T(8,128)(2,1)}, bf16[256,640]{1,0:T(8,128)(2,1)}) custom-call(bf16[320,256]{1,0:T(8,128)(2,1)S(1)} %collective-permute-done.6.refs_0_, bf16[320,256]{1,0:T(8,128)(2,1)S(1)} %collective-permute-done.7.refs_1_, ...), custom_call_target="tpu_custom_call" | custom-call | flops 20000000000 | tf_op jit(solution)/shard_map/unpack_heads/pallas_call | solution.py:624
  40.7 2.2 %all-to-all-done.tiles = f32[32,4,128]{2,1,0:T(4,128)S(1)} async-done(((f32[32,4,128]{2,1,0:T(4,128)}), f32[32,4,128]{2,1,0:T(4,128)S(1)}, u32[]{:S(2)}, u32[]{:S(2)}) %all-to-all-start) | async-done | bytes 65568 | tf_op jit(solution)/shard_map/all_to_all | solution.py:621
  43.0 0.7 %bias_sums.1 = f32[3,640]{1,0:T(4,128)} custom-call(f32[32,4,128]{2,1,0:T(4,128)S(1)} %all-to-all-done.tiles), custom_call_target="tpu_custom_call" | custom-call | tf_op jit(solution)/shard_map/bias_sums/pallas_call | solution.py:639
Async XLA Ops:
  2.1 4.7 %copy-start = (bf16[3,640]{1,0:T(4,128)(2,1)S(1)}, bf16[3,640]{1,0:T(4,128)(2,1)}, u32[]{:S(2)}) copy-start(bf16[3,640]{1,0:T(4,128)(2,1)} %refs_0_.1) | copy-start | bytes 11524
  2.1 9.0 %collective-permute-start = (bf16[320,256]{1,0:T(8,128)(2,1)S(1)}, bf16[320,256]{1,0:T(8,128)(2,1)S(1)}, u32[]{:S(2)}, u32[]{:S(2)}) collective-permute-start(bf16[320,256]{1,0:T(8,128)(2,1)S(1)} %get-tuple-element.62), channel_id=1, source_target_pairs={{0,3},{1,2},{2,1},{3,0},{4,7},{5,6},{6,5},{7,4},{8,11},{9,10},{10,... | collective-permute-start | bytes 491528 | tf_op jit(solution)/shard_map/ppermute | solution.py:518
  6.1 8.7 %collective-permute-start.3 = (bf16[320,256]{1,0:T(8,128)(2,1)S(1)}, bf16[320,256]{1,0:T(8,128)(2,1)S(1)}, u32[]{:S(2)}, u32[]{:S(2)}) collective-permute-start(bf16[320,256]{1,0:T(8,128)(2,1)S(1)} %get-tuple-element.71), channel_id=1, source_target_pairs={{0,2},{1,3},{2,0},{3,1},{4,6},{5,7},{6,4},{7,5},{8,10},{9,11},{10,... | collective-permute-start | bytes 491528 | tf_op jit(solution)/shard_map/ppermute | solution.py:518
  6.6 0.7 %copy-start.1 = (s32[1,4]{1,0:T(1,128)S(1)}, s32[1,4]{1,0:T(1,128)}, u32[]{:S(2)}) copy-start(s32[1,4]{1,0:T(1,128)} %lengths.1) | copy-start | bytes 52
  6.6 0.7 %copy-start.2 = (s32[1,4]{1,0:T(1,128)S(1)}, s32[1,4]{1,0:T(1,128)}, u32[]{:S(2)}) copy-start(s32[1,4]{1,0:T(1,128)} %widths.1) | copy-start | bytes 52
  6.6 8.7 %collective-permute-start.5 = (bf16[320,256]{1,0:T(8,128)(2,1)S(1)}, bf16[320,256]{1,0:T(8,128)(2,1)S(1)}, u32[]{:S(2)}, u32[]{:S(2)}) collective-permute-start(bf16[320,256]{1,0:T(8,128)(2,1)S(1)} %get-tuple-element.77), channel_id=1, source_target_pairs={{0,1},{1,0},{2,3},{3,2},{4,5},{5,4},{6,7},{7,6},{8,9},{9,8},{10,11... | collective-permute-start | bytes 491528 | tf_op jit(solution)/shard_map/ppermute | solution.py:518
  11.3 11.1 %collective-permute-start.1 = (bf16[320,256]{1,0:T(8,128)(2,1)S(1)}, bf16[320,256]{1,0:T(8,128)(2,1)S(1)}, u32[]{:S(2)}, u32[]{:S(2)}) collective-permute-start(bf16[320,256]{1,0:T(8,128)(2,1)S(1)} %get-tuple-element.65), channel_id=1, source_target_pairs={{0,3},{1,2},{2,1},{3,0},{4,7},{5,6},{6,5},{7,4},{8,11},{9,10},{10,... | collective-permute-start | bytes 491528 | tf_op jit(solution)/shard_map/ppermute | solution.py:579
  14.4 0.9 %copy-start.4 = (bf16[3,128,256]{2,1,0:T(8,128)(2,1)S(1)}, bf16[3,128,256]{2,1,0:T(8,128)(2,1)}, u32[]{:S(2)}) copy-start(bf16[3,128,256]{2,1,0:T(8,128)(2,1)} %get-tuple-element.78.refs_4_) | copy-start | bytes 589828
  14.4 8.0 %collective-permute-start.2 = (bf16[320,256]{1,0:T(8,128)(2,1)S(1)}, bf16[320,256]{1,0:T(8,128)(2,1)S(1)}, u32[]{:S(2)}, u32[]{:S(2)}) collective-permute-start(bf16[320,256]{1,0:T(8,128)(2,1)S(1)} %get-tuple-element.69), channel_id=1, source_target_pairs={{0,2},{1,3},{2,0},{3,1},{4,6},{5,7},{6,4},{7,5},{8,10},{9,11},{10,... | collective-permute-start | bytes 491528 | tf_op jit(solution)/shard_map/ppermute | solution.py:579
  15.0 7.4 %collective-permute-start.4 = (bf16[320,256]{1,0:T(8,128)(2,1)S(1)}, bf16[320,256]{1,0:T(8,128)(2,1)S(1)}, u32[]{:S(2)}, u32[]{:S(2)}) collective-permute-start(bf16[320,256]{1,0:T(8,128)(2,1)S(1)} %get-tuple-element.74), channel_id=1, source_target_pairs={{0,1},{1,0},{2,3},{3,2},{4,5},{5,4},{6,7},{7,6},{8,9},{9,8},{10,11... | collective-permute-start | bytes 491528 | tf_op jit(solution)/shard_map/ppermute | solution.py:579
  15.3 7.1 %copy-start.3 = (bf16[3,128,256]{2,1,0:T(8,128)(2,1)S(1)}, bf16[3,128,256]{2,1,0:T(8,128)(2,1)}, u32[]{:S(2)}) copy-start(bf16[3,128,256]{2,1,0:T(8,128)(2,1)} %get-tuple-element.75.refs_4_) | copy-start | bytes 589828
  19.5 9.5 %collective-permute-start.6 = (bf16[320,256]{1,0:T(8,128)(2,1)S(1)}, bf16[320,256]{1,0:T(8,128)(2,1)S(1)}, u32[]{:S(2)}, u32[]{:S(2)}) collective-permute-start(bf16[320,256]{1,0:T(8,128)(2,1)S(1)} %get-tuple-element.89), channel_id=1, source_target_pairs={{3,0},{2,1},{1,2},{0,3},{7,4},{6,5},{5,6},{4,7},{11,8},{10,9},{9,1... | collective-permute-start | bytes 491528 | tf_op jit(solution)/shard_map/ppermute | solution.py:72
  27.3 11.7 %collective-permute-start.8 = (bf16[640,256]{1,0:T(8,128)(2,1)S(1)}, bf16[640,256]{1,0:T(8,128)(2,1)S(1)}, u32[]{:S(2)}, u32[]{:S(2)}) collective-permute-start(bf16[640,256]{1,0:T(8,128)(2,1)S(1)} %get-tuple-element.93), channel_id=1, source_target_pairs={{2,0},{3,1},{0,2},{1,3},{6,4},{7,5},{4,6},{5,7},{10,8},{11,9},{8,1... | collective-permute-start | bytes 983048 | tf_op jit(solution)/shard_map/ppermute | solution.py:72
  27.8 11.7 %collective-permute-start.9 = (bf16[640,256]{1,0:T(8,128)(2,1)S(1)}, bf16[640,256]{1,0:T(8,128)(2,1)S(1)}, u32[]{:S(2)}, u32[]{:S(2)}) collective-permute-start(bf16[640,256]{1,0:T(8,128)(2,1)S(1)} %get-tuple-element.94), channel_id=1, source_target_pairs={{1,0},{0,1},{3,2},{2,3},{5,4},{4,5},{7,6},{6,7},{9,8},{8,9},{11,10... | collective-permute-start | bytes 983048 | tf_op jit(solution)/shard_map/ppermute | solution.py:72
  29.0 10.0 %collective-permute-start.7 = (bf16[320,256]{1,0:T(8,128)(2,1)S(1)}, bf16[320,256]{1,0:T(8,128)(2,1)S(1)}, u32[]{:S(2)}, u32[]{:S(2)}) collective-permute-start(bf16[320,256]{1,0:T(8,128)(2,1)S(1)} %get-tuple-element.91), channel_id=1, source_target_pairs={{3,0},{2,1},{1,2},{0,3},{7,4},{6,5},{5,6},{4,7},{11,8},{10,9},{9,1... | collective-permute-start | bytes 491528 | tf_op jit(solution)/shard_map/ppermute | solution.py:72
  30.8 12.1 %all-to-all-start = ((f32[32,4,128]{2,1,0:T(4,128)}), f32[32,4,128]{2,1,0:T(4,128)S(1)}, u32[]{:S(2)}, u32[]{:S(2)}) async-start(f32[32,4,128]{2,1,0:T(4,128)} %get-tuple-element.99), calls=%async_computation | async-start | bytes 131072 | tf_op jit(solution)/shard_map/all_to_all | solution.py:621

commit v23 on v19

--- a/solution.py
+++ b/solution.py
@@ -420,7 +420,7 @@
     if not closed:
         lengths, table, *refs = refs
     msgs, refs = refs[: slots + OWN_HEADS - 1], refs[slots + OWN_HEADS - 1 :]
-    *outs, held, ready, sems = refs
+    *outs, held = refs
     early, late = msgs[:OWN_HEADS], list(msgs[OWN_HEADS:])
     late.insert(EARLY, None)
     me = lax.axis_index("tok")
@@ -444,16 +444,26 @@
             residue = lax.rem(source + SPAN, SPAN)
             chosen = (source >= 0) & (source == handler_of(start, residue, count))
             pl.when(chosen)(functools.partial(place, slot, residue))
-    copies = []
     for number, out in enumerate(outs):
-        ready[number] = held[number].T
-        copies.append(pltpu.make_async_copy(ready.at[number], out, sems.at[number]))
-        copies[-1].start()
+        out[...] = held[number].T
+
+
+def finish_kernel(*refs):
+    results, tiles, outs, bias_out, (total, sems) = refs[:4], refs[4], refs[5:9], refs[9], refs[10:]
+    copies = [
+        pltpu.make_async_copy(result, out, sems.at[number])
+        for number, (result, out) in enumerate(zip(results, outs))
+    ]
+    for copy in copies:
+        copy.start()
+    add_tiles(tiles, total)
+    copies.append(pltpu.make_async_copy(total, bias_out, sems.at[4]))
+    copies[-1].start()
     for copy in copies:
         copy.wait()
 
 
-def bias_kernel(tiles, bias_out):
+def add_tiles(tiles, bias_out):
     def add(group, totals):
         return tuple(
             total + tiles[group * SPAN + residue] for residue, total in enumerate(totals)
@@ -621,29 +631,29 @@
     tiles = lax.all_to_all(total, ("dp", "tok"), 0, 0, tiled=True)
     late = [send_back(results[slot], slot) for slot in kept]
     places = [] if closed else [lengths, jnp.asarray(targets)]
-    outs = pl.pallas_call(
+    ready = pl.pallas_call(
         functools.partial(unpack_kernel, slots, count, images),
         out_shape=[whole] * 4,
         in_specs=[smem] * len(places) + [vmem] * (OWN_HEADS + len(late)),
-        out_specs=[hbm] * 4,
-        scratch_shapes=[
-            pltpu.VMEM((4, model, tokd), jnp.bfloat16),
-            pltpu.VMEM((4, tokd, model), jnp.bfloat16),
-            pltpu.SemaphoreType.DMA((4,)),
-        ],
+        out_specs=[vmem] * 4,
+        scratch_shapes=[pltpu.VMEM((4, model, tokd), jnp.bfloat16)],
         compiler_params=params(16),
         cost_estimate=pl.CostEstimate(flops=UNPACK_FLOPS, bytes_accessed=0, transcendentals=0),
         name="unpack_heads",
     )(*places, *early, *late)
-    outs, tiles = lax.optimization_barrier((outs, tiles))
-    bias_grad = pl.pallas_call(
-        bias_kernel,
-        out_shape=jax.ShapeDtypeStruct((3, model), jnp.float32),
-        in_specs=[vmem],
-        out_specs=vmem,
+    bias_shape = jax.ShapeDtypeStruct((3, model), jnp.float32)
+    *outs, bias_grad = pl.pallas_call(
+        finish_kernel,
+        out_shape=[whole] * 4 + [bias_shape],
+        in_specs=[vmem] * 5,
+        out_specs=[hbm] * 5,
+        scratch_shapes=[
+            pltpu.VMEM(bias_shape.shape, jnp.float32),
+            pltpu.SemaphoreType.DMA((5,)),
+        ],
         compiler_params=params(16),
-        name="bias_sums",
-    )(tiles)
+        name="finish",
+    )(*ready, tiles)
     return tuple(out[None] for out in outs) + (bias_grad,)
 
 

time: 43.8 us -> 44.2 us (level)
  waiting for transfers between devices: 7.47 us -> 8.3 us
    pallas_call x1, Pallas kernels: 1.32 us -> 0.48 us  [on_device(): pl.pallas_call(functools.partial(unpack_kernel, slots, count, images), ou...]
    all_to_all x1, waiting for transfers between devices: 2.2 us -> 3.03 us  [on_device(): tiles = lax.all_to_all(total, ('dp', 'tok'), 0, 0, tiled=True)]
  transfers between devices with their start and end apart: 11 -> 11, of which waited for: 4 -> 4; matrix products, arithmetic and copies ran while one was open for 0% -> 0% of each run, Pallas kernels for 31% -> 29%
where the time goes in v23:
time: 44.2 us; the launch traced here: 44 us
  starting transfers between devices  19.3 us (44%)
  Pallas kernels  15.2 us (34%)
  waiting for transfers between devices  8.3 us (19%)
  between operations  0.73 us (2%)
  local copies, waits for them, and re-layouts  0.49 us (1%)
    pallas_call x2, Pallas kernels, on_device(): pl.pallas_call(functools.partial(attend_kernel, slots, tuple(staged[phase...  8.91 us
    ppermute x4, starting transfers between devices, send_back(): lax.ppermute(result, 'tok', [(target, source) for source, target in pairs])  6.45 us
    ppermute x3, starting transfers between devices, on_device(): lax.ppermute(send, 'tok', pairs)  4.66 us
    all_to_all x1, starting transfers between devices, on_device(): tiles = lax.all_to_all(total, ('dp', 'tok'), 0, 0, tiled=True)  4.41 us
    ppermute x4, waiting for transfers between devices, send_back(): lax.ppermute(result, 'tok', [(target, source) for source, target in pairs])  4.19 us
    ppermute x3, starting transfers between devices, on_device(): got[phase].append(lax.ppermute(send, 'tok', rounds[leaving - 1]))  3.78 us
    all_to_all x1, waiting for transfers between devices, on_device(): tiles = lax.all_to_all(total, ('dp', 'tok'), 0, 0, tiled=True)  3.03 us
    pallas_call x1, Pallas kernels, on_device(): pl.pallas_call(functools.partial(prepare_kernel, slots, images, count, to...  2.84 us
  transfers between devices with their start and end apart: 11, of which 4 were waited for; matrix products, arithmetic and copies ran while one was open for 0% of the time, Pallas kernels for 29%

profile of v23, /device:TPU:0, one launch (start us, length us, event | category | flops | bytes accessed | tf_op | source)
XLA Modules:
  0.0 44.0 jit_solution(14552927801402130744)
XLA Ops:
  0.6 1.5 %pack_heads.1 = (bf16[320,256]{1,0:T(8,128)(2,1)S(1)}, bf16[320,256]{1,0:T(8,128)(2,1)S(1)}, bf16[320,256]{1,0:T(8,128)(2,1)S(1)}, bf16[320,256]{1,0:T(8,128)(2,1)S(1)}) custom-call(bf16[256,640]{1,0:T(8,128)(2,1)} %bitcast.8, bf16[256,640]{1,0:T(8,128)(2,1)} %bitcast.10, bf16[256,640]{1,0:T(8,128)(2,1)} %bitcast.12, bf16[256,640]{1,0:T(8,128)(2,1)} %bitcast.14), custom_call_target="tpu_custom_call" | custom-call | tf_op jit(solution)/shard_map/pack_heads/pallas_call | solution.py:512
  2.1 0.0 copy-start
  2.1 4.0 %collective-permute-start = (bf16[320,256]{1,0:T(8,128)(2,1)S(1)}, bf16[320,256]{1,0:T(8,128)(2,1)S(1)}, u32[]{:S(2)}, u32[]{:S(2)}) collective-permute-start(bf16[320,256]{1,0:T(8,128)(2,1)S(1)} %get-tuple-element.62), channel_id=1, source_target_pairs={{0,3},{1,2},{2,1},{3,0},{4,7},{5,6},{6,5},{7,4},{8,11},{9,10},{10,... | collective-permute-start | bytes 491528 | tf_op jit(solution)/shard_map/ppermute | solution.py:528
  6.1 0.4 %collective-permute-start.3 = (bf16[320,256]{1,0:T(8,128)(2,1)S(1)}, bf16[320,256]{1,0:T(8,128)(2,1)S(1)}, u32[]{:S(2)}, u32[]{:S(2)}) collective-permute-start(bf16[320,256]{1,0:T(8,128)(2,1)S(1)} %get-tuple-element.71), channel_id=1, source_target_pairs={{0,2},{1,3},{2,0},{3,1},{4,6},{5,7},{6,4},{7,5},{8,10},{9,11},{10,... | collective-permute-start | bytes 491528 | tf_op jit(solution)/shard_map/ppermute | solution.py:528
  6.6 0.0 copy-start.1
  6.6 0.0 copy-start.2
  6.6 0.2 collective-permute-start.5
  6.8 0.0 copy-done
  6.8 0.4 %copy-done.1 = s32[1,4]{1,0:T(1,128)S(1)} copy-done((s32[1,4]{1,0:T(1,128)S(1)}, s32[1,4]{1,0:T(1,128)}, u32[]{:S(2)}) %copy-start.1) | copy-done | bytes 40
  7.2 0.0 copy-done.2
  7.2 2.8 %prepare.1 = (f32[40,1024]{1,0:T(8,128)S(1)}, f32[40,1024]{1,0:T(8,128)S(1)}, f32[24,256]{1,0:T(8,128)S(1)}, f32[160,128]{1,0:T(8,128)S(1)}, bf16[320,256]{1,0:T...) custom-call(s32[1,4]{1,0:T(1,128)S(1)} %copy-done.1, ...), custom_call_target="tpu_custom_call" | custom-call | flops 1000000 | tf_op jit(solution)/shard_map/prepare/pallas_call | solution.py:545
  10.1 1.1 %collective-permute-done.refs_0_.refs_1_ = bf16[320,256]{1,0:T(8,128)(2,1)S(1)} collective-permute-done((bf16[320,256]{1,0:T(8,128)(2,1)S(1)}, bf16[320,256]{1,0:T(8,128)(2,1)S(1)}, u32[]{:S(2)}, u32[]{:S(2)}) %collective-permute-start) | collective-permute-done | bytes 163872 | tf_op jit(solution)/shard_map/ppermute | solution.py:528
  11.2 0.2 stage_slot.2
  11.3 3.1 %collective-permute-start.1 = (bf16[320,256]{1,0:T(8,128)(2,1)S(1)}, bf16[320,256]{1,0:T(8,128)(2,1)S(1)}, u32[]{:S(2)}, u32[]{:S(2)}) collective-permute-start(bf16[320,256]{1,0:T(8,128)(2,1)S(1)} %get-tuple-element.65), channel_id=1, source_target_pairs={{0,3},{1,2},{2,1},{3,0},{4,7},{5,6},{6,5},{7,4},{8,11},{9,10},{10,... | collective-permute-start | bytes 491528 | tf_op jit(solution)/shard_map/ppermute | solution.py:589
  14.4 0.0 copy-start.4
  14.4 0.4 %collective-permute-start.2 = (bf16[320,256]{1,0:T(8,128)(2,1)S(1)}, bf16[320,256]{1,0:T(8,128)(2,1)S(1)}, u32[]{:S(2)}, u32[]{:S(2)}) collective-permute-start(bf16[320,256]{1,0:T(8,128)(2,1)S(1)} %get-tuple-element.69), channel_id=1, source_target_pairs={{0,2},{1,3},{2,0},{3,1},{4,6},{5,7},{6,4},{7,5},{8,10},{9,11},{10,... | collective-permute-start | bytes 491528 | tf_op jit(solution)/shard_map/ppermute | solution.py:589
  14.9 0.0 collective-permute-done.3.refs_0_.refs_2_
  14.9 0.2 stage_slot.3
  15.0 0.3 collective-permute-start.4
  15.3 0.0 collective-permute-done.5.refs_3_
  15.3 0.0 copy-done.4
  15.3 0.0 copy-start.3
  15.3 4.2 %attend_head.2 = (bf16[640,256]{1,0:T(8,128)(2,1)S(1)}, bf16[320,256]{1,0:T(8,128)(2,1)S(1)}, bf16[640,256]{1,0:T(8,128)(2,1)S(1)}, bf16[640,256]{1,0:T(8,128)(2,1)S(1)}, f32[8,128]{1,0:T(8,128)S(1)}) custom-call(f32[40,1024]{1,0:T(8,128)S(1)} %get-tuple-element.56.cosv, f32[40,1024]{1,0:T(8,128)S(1)} %get-tuple-element.57.sinv, ...), custom_call_target="tpu_custom_call" | custom-call | flops 3221225472 | tf_op jit(solution)/shard_map/attend_head/pallas_call | solution.py:599
  19.5 2.9 %collective-permute-start.6 = (bf16[320,256]{1,0:T(8,128)(2,1)S(1)}, bf16[320,256]{1,0:T(8,128)(2,1)S(1)}, u32[]{:S(2)}, u32[]{:S(2)}) collective-permute-start(bf16[320,256]{1,0:T(8,128)(2,1)S(1)} %get-tuple-element.89), channel_id=1, source_target_pairs={{3,0},{2,1},{1,2},{0,3},{7,4},{6,5},{5,6},{4,7},{11,8},{10,9},{9,1... | collective-permute-start | bytes 491528 | tf_op jit(solution)/shard_map/ppermute | solution.py:72
  22.4 0.0 collective-permute-done.1.refs_1_
  22.4 0.0 collective-permute-done.2.refs_2_
  22.4 0.0 collective-permute-done.4.refs_3_
  22.5 0.0 copy-done.3
  22.5 4.7 %attend_head.3 = (bf16[640,256]{1,0:T(8,128)(2,1)S(1)}, bf16[320,256]{1,0:T(8,128)(2,1)S(1)}, bf16[640,256]{1,0:T(8,128)(2,1)S(1)}, bf16[640,256]{1,0:T(8,128)(2,1)S(1)}, f32[32,4,128]{2,1,0:T(4,128)}) custom-call(f32[40,1024]{1,0:T(8,128)S(1)} %get-tuple-element.56.cosv, f32[40,1024]{1,0:T(8,128)S(1)} %get-tuple-element.57.sinv, ...), custom_call_target="tpu_custom_call" | custom-call | flops 3221225472 | tf_op jit(solution)/shard_map/attend_head/pallas_call | solution.py:599
  27.2 0.5 %collective-permute-start.8 = (bf16[640,256]{1,0:T(8,128)(2,1)S(1)}, bf16[640,256]{1,0:T(8,128)(2,1)S(1)}, u32[]{:S(2)}, u32[]{:S(2)}) collective-permute-start(bf16[640,256]{1,0:T(8,128)(2,1)S(1)} %get-tuple-element.93), channel_id=1, source_target_pairs={{2,0},{3,1},{0,2},{1,3},{6,4},{7,5},{4,6},{5,7},{10,8},{11,9},{8,1... | collective-permute-start | bytes 983048 | tf_op jit(solution)/shard_map/ppermute | solution.py:72
  27.7 1.2 %collective-permute-start.9 = (bf16[640,256]{1,0:T(8,128)(2,1)S(1)}, bf16[640,256]{1,0:T(8,128)(2,1)S(1)}, u32[]{:S(2)}, u32[]{:S(2)}) collective-permute-start(bf16[640,256]{1,0:T(8,128)(2,1)S(1)} %get-tuple-element.94), channel_id=1, source_target_pairs={{1,0},{0,1},{3,2},{2,3},{5,4},{4,5},{7,6},{6,7},{9,8},{8,9},{11,10... | collective-permute-start | bytes 983048 | tf_op jit(solution)/shard_map/ppermute | solution.py:72
  28.9 0.0 collective-permute-done.6.refs_0_
  28.9 1.9 %collective-permute-start.7 = (bf16[320,256]{1,0:T(8,128)(2,1)S(1)}, bf16[320,256]{1,0:T(8,128)(2,1)S(1)}, u32[]{:S(2)}, u32[]{:S(2)}) collective-permute-start(bf16[320,256]{1,0:T(8,128)(2,1)S(1)} %get-tuple-element.91), channel_id=1, source_target_pairs={{3,0},{2,1},{1,2},{0,3},{7,4},{6,5},{5,6},{4,7},{11,8},{10,9},{9,1... | collective-permute-start | bytes 491528 | tf_op jit(solution)/shard_map/ppermute | solution.py:72
  30.7 4.4 %all-to-all-start = ((f32[32,4,128]{2,1,0:T(4,128)}), f32[32,4,128]{2,1,0:T(4,128)S(1)}, u32[]{:S(2)}, u32[]{:S(2)}) async-start(f32[32,4,128]{2,1,0:T(4,128)} %get-tuple-element.99), calls=%async_computation | async-start | bytes 131072 | tf_op jit(solution)/shard_map/all_to_all | solution.py:631
  35.2 3.7 %collective-permute-done.7.refs_1_ = bf16[320,256]{1,0:T(8,128)(2,1)S(1)} collective-permute-done((bf16[320,256]{1,0:T(8,128)(2,1)S(1)}, bf16[320,256]{1,0:T(8,128)(2,1)S(1)}, u32[]{:S(2)}, u32[]{:S(2)}) %collective-permute-start.7) | collective-permute-done | bytes 163872 | tf_op jit(solution)/shard_map/ppermute | solution.py:72
  38.9 0.0 collective-permute-done.8.refs_3_
  38.9 0.5 %collective-permute-done.9.refs_4_ = bf16[640,256]{1,0:T(8,128)(2,1)S(1)} collective-permute-done((bf16[640,256]{1,0:T(8,128)(2,1)S(1)}, bf16[640,256]{1,0:T(8,128)(2,1)S(1)}, u32[]{:S(2)}, u32[]{:S(2)}) %collective-permute-start.9) | collective-permute-done | bytes 327712 | tf_op jit(solution)/shard_map/ppermute | solution.py:72
  39.3 0.5 %unpack_heads.1 = (bf16[256,640]{1,0:T(8,128)(2,1)S(1)}, bf16[256,640]{1,0:T(8,128)(2,1)S(1)}, bf16[256,640]{1,0:T(8,128)(2,1)S(1)}, bf16[256,640]{1,0:T(8,128)(2,1)S(1)}) custom-call(bf16[320,256]{1,0:T(8,128)(2,1)S(1)} %collective-permute-done.6.refs_0_, bf16[320,256]{1,0:T(8,128)(2,1)S(1)} %collective-permute-done.7.refs_1_, ...), custom_call_target="tpu_custom_call" | custom-call | flops 20000000000 | tf_op jit(solution)/shard_map/unpack_heads/pallas_call | solution.py:634
  39.8 3.0 %all-to-all-done.refs_4_ = f32[32,4,128]{2,1,0:T(4,128)S(1)} async-done(((f32[32,4,128]{2,1,0:T(4,128)}), f32[32,4,128]{2,1,0:T(4,128)S(1)}, u32[]{:S(2)}, u32[]{:S(2)}) %all-to-all-start) | async-done | bytes 65568 | tf_op jit(solution)/shard_map/all_to_all | solution.py:631
  42.9 1.1 %finish.1 = (bf16[256,640]{1,0:T(8,128)(2,1)}, bf16[256,640]{1,0:T(8,128)(2,1)}, bf16[256,640]{1,0:T(8,128)(2,1)}, bf16[256,640]{1,0:T(8,128)(2,1)}, f32[3,640]{1,0:T(4,128)}) custom-call(bf16[256,640]{1,0:T(8,128)(2,1)S(1)} %get-tuple-element.95.refs_0_, bf16[256,640]{1,0:T(8,128)(2,1)S(1)} %get-tuple-element.96.refs_1_, ...), custom_call_target="tpu_custom_call" | custom-call | tf_op jit(solution)/shard_map/finish/pallas_call | solution.py:645
Async XLA Ops:
  2.1 4.7 %copy-start = (bf16[3,640]{1,0:T(4,128)(2,1)S(1)}, bf16[3,640]{1,0:T(4,128)(2,1)}, u32[]{:S(2)}) copy-start(bf16[3,640]{1,0:T(4,128)(2,1)} %refs_0_.1) | copy-start | bytes 11524
  2.1 9.0 %collective-permute-start = (bf16[320,256]{1,0:T(8,128)(2,1)S(1)}, bf16[320,256]{1,0:T(8,128)(2,1)S(1)}, u32[]{:S(2)}, u32[]{:S(2)}) collective-permute-start(bf16[320,256]{1,0:T(8,128)(2,1)S(1)} %get-tuple-element.62), channel_id=1, source_target_pairs={{0,3},{1,2},{2,1},{3,0},{4,7},{5,6},{6,5},{7,4},{8,11},{9,10},{10,... | collective-permute-start | bytes 491528 | tf_op jit(solution)/shard_map/ppermute | solution.py:528
  6.1 8.7 %collective-permute-start.3 = (bf16[320,256]{1,0:T(8,128)(2,1)S(1)}, bf16[320,256]{1,0:T(8,128)(2,1)S(1)}, u32[]{:S(2)}, u32[]{:S(2)}) collective-permute-start(bf16[320,256]{1,0:T(8,128)(2,1)S(1)} %get-tuple-element.71), channel_id=1, source_target_pairs={{0,2},{1,3},{2,0},{3,1},{4,6},{5,7},{6,4},{7,5},{8,10},{9,11},{10,... | collective-permute-start | bytes 491528 | tf_op jit(solution)/shard_map/ppermute | solution.py:528
  6.6 0.7 %copy-start.1 = (s32[1,4]{1,0:T(1,128)S(1)}, s32[1,4]{1,0:T(1,128)}, u32[]{:S(2)}) copy-start(s32[1,4]{1,0:T(1,128)} %lengths.1) | copy-start | bytes 52
  6.6 0.7 %copy-start.2 = (s32[1,4]{1,0:T(1,128)S(1)}, s32[1,4]{1,0:T(1,128)}, u32[]{:S(2)}) copy-start(s32[1,4]{1,0:T(1,128)} %widths.1) | copy-start | bytes 52
  6.6 8.7 %collective-permute-start.5 = (bf16[320,256]{1,0:T(8,128)(2,1)S(1)}, bf16[320,256]{1,0:T(8,128)(2,1)S(1)}, u32[]{:S(2)}, u32[]{:S(2)}) collective-permute-start(bf16[320,256]{1,0:T(8,128)(2,1)S(1)} %get-tuple-element.77), channel_id=1, source_target_pairs={{0,1},{1,0},{2,3},{3,2},{4,5},{5,4},{6,7},{7,6},{8,9},{9,8},{10,11... | collective-permute-start | bytes 491528 | tf_op jit(solution)/shard_map/ppermute | solution.py:528
  11.3 11.1 %collective-permute-start.1 = (bf16[320,256]{1,0:T(8,128)(2,1)S(1)}, bf16[320,256]{1,0:T(8,128)(2,1)S(1)}, u32[]{:S(2)}, u32[]{:S(2)}) collective-permute-start(bf16[320,256]{1,0:T(8,128)(2,1)S(1)} %get-tuple-element.65), channel_id=1, source_target_pairs={{0,3},{1,2},{2,1},{3,0},{4,7},{5,6},{6,5},{7,4},{8,11},{9,10},{10,... | collective-permute-start | bytes 491528 | tf_op jit(solution)/shard_map/ppermute | solution.py:589
  14.4 0.9 %copy-start.4 = (bf16[3,128,256]{2,1,0:T(8,128)(2,1)S(1)}, bf16[3,128,256]{2,1,0:T(8,128)(2,1)}, u32[]{:S(2)}) copy-start(bf16[3,128,256]{2,1,0:T(8,128)(2,1)} %get-tuple-element.78.refs_4_) | copy-start | bytes 589828
  14.4 8.0 %collective-permute-start.2 = (bf16[320,256]{1,0:T(8,128)(2,1)S(1)}, bf16[320,256]{1,0:T(8,128)(2,1)S(1)}, u32[]{:S(2)}, u32[]{:S(2)}) collective-permute-start(bf16[320,256]{1,0:T(8,128)(2,1)S(1)} %get-tuple-element.69), channel_id=1, source_target_pairs={{0,2},{1,3},{2,0},{3,1},{4,6},{5,7},{6,4},{7,5},{8,10},{9,11},{10,... | collective-permute-start | bytes 491528 | tf_op jit(solution)/shard_map/ppermute | solution.py:589
  15.0 7.4 %collective-permute-start.4 = (bf16[320,256]{1,0:T(8,128)(2,1)S(1)}, bf16[320,256]{1,0:T(8,128)(2,1)S(1)}, u32[]{:S(2)}, u32[]{:S(2)}) collective-permute-start(bf16[320,256]{1,0:T(8,128)(2,1)S(1)} %get-tuple-element.74), channel_id=1, source_target_pairs={{0,1},{1,0},{2,3},{3,2},{4,5},{5,4},{6,7},{7,6},{8,9},{9,8},{10,11... | collective-permute-start | bytes 491528 | tf_op jit(solution)/shard_map/ppermute | solution.py:589
  15.3 7.1 %copy-start.3 = (bf16[3,128,256]{2,1,0:T(8,128)(2,1)S(1)}, bf16[3,128,256]{2,1,0:T(8,128)(2,1)}, u32[]{:S(2)}) copy-start(bf16[3,128,256]{2,1,0:T(8,128)(2,1)} %get-tuple-element.75.refs_4_) | copy-start | bytes 589828
  19.5 9.3 %collective-permute-start.6 = (bf16[320,256]{1,0:T(8,128)(2,1)S(1)}, bf16[320,256]{1,0:T(8,128)(2,1)S(1)}, u32[]{:S(2)}, u32[]{:S(2)}) collective-permute-start(bf16[320,256]{1,0:T(8,128)(2,1)S(1)} %get-tuple-element.89), channel_id=1, source_target_pairs={{3,0},{2,1},{1,2},{0,3},{7,4},{6,5},{5,6},{4,7},{11,8},{10,9},{9,1... | collective-permute-start | bytes 491528 | tf_op jit(solution)/shard_map/ppermute | solution.py:72
  27.2 11.7 %collective-permute-start.8 = (bf16[640,256]{1,0:T(8,128)(2,1)S(1)}, bf16[640,256]{1,0:T(8,128)(2,1)S(1)}, u32[]{:S(2)}, u32[]{:S(2)}) collective-permute-start(bf16[640,256]{1,0:T(8,128)(2,1)S(1)} %get-tuple-element.93), channel_id=1, source_target_pairs={{2,0},{3,1},{0,2},{1,3},{6,4},{7,5},{4,6},{5,7},{10,8},{11,9},{8,1... | collective-permute-start | bytes 983048 | tf_op jit(solution)/shard_map/ppermute | solution.py:72
  27.7 11.7 %collective-permute-start.9 = (bf16[640,256]{1,0:T(8,128)(2,1)S(1)}, bf16[640,256]{1,0:T(8,128)(2,1)S(1)}, u32[]{:S(2)}, u32[]{:S(2)}) collective-permute-start(bf16[640,256]{1,0:T(8,128)(2,1)S(1)} %get-tuple-element.94), channel_id=1, source_target_pairs={{1,0},{0,1},{3,2},{2,3},{5,4},{4,5},{7,6},{6,7},{9,8},{8,9},{11,10... | collective-permute-start | bytes 983048 | tf_op jit(solution)/shard_map/ppermute | solution.py:72
  28.9 10.0 %collective-permute-start.7 = (bf16[320,256]{1,0:T(8,128)(2,1)S(1)}, bf16[320,256]{1,0:T(8,128)(2,1)S(1)}, u32[]{:S(2)}, u32[]{:S(2)}) collective-permute-start(bf16[320,256]{1,0:T(8,128)(2,1)S(1)} %get-tuple-element.91), channel_id=1, source_target_pairs={{3,0},{2,1},{1,2},{0,3},{7,4},{6,5},{5,6},{4,7},{11,8},{10,9},{9,1... | collective-permute-start | bytes 491528 | tf_op jit(solution)/shard_map/ppermute | solution.py:72
  30.7 12.1 %all-to-all-start = ((f32[32,4,128]{2,1,0:T(4,128)}), f32[32,4,128]{2,1,0:T(4,128)S(1)}, u32[]{:S(2)}, u32[]{:S(2)}) async-start(f32[32,4,128]{2,1,0:T(4,128)} %get-tuple-element.99), calls=%async_computation | async-start | bytes 131072 | tf_op jit(solution)/shard_map/all_to_all | solution.py:631

commit v24 on v19

--- a/solution.py
+++ b/solution.py
@@ -133,9 +133,22 @@
         if closed
         else [0, *range(1, SPAN), *range(SPAN - 1, 0, -1)]
     )
+    row = lax.broadcasted_iota(jnp.int32, (LANES, LANES), 0)
+    lane = lax.broadcasted_iota(jnp.int32, (LANES, LANES), 1)
+    ones = jnp.where(row == lane, 1.0, 0.0).astype(jnp.bfloat16)
     for number, copy in enumerate(copies):
         copy.wait()
-        turned[number] = held[number].T
+        if number % 2 == 0:
+            turned[number] = held[number].T
+        else:
+            for begin in range(0, held.shape[2], LANES):
+                block = lax.dot_general(
+                    ones,
+                    held[number, :, begin : begin + LANES],
+                    (((1,), (1,)), ((), ())),
+                    preferred_element_type=jnp.float32,
+                )
+                turned[number, begin : begin + LANES, :] = block.astype(jnp.bfloat16)
         for out, step in zip(outs, steps):
             residue = me ^ step if closed else lax.rem(me + step, SPAN)
             rows = pl.ds(pl.multiple_of(inner + residue * HEAD_DIM, 16), HEAD_DIM)

time: 43.8 us -> 44.1 us (level)
  no operation moved by 1% of the time
where the time goes in v24:
time: 44.1 us; the launch traced here: 43.8 us
  starting transfers between devices  19.3 us (44%)
  Pallas kernels  15.9 us (36%)
  waiting for transfers between devices  7.39 us (17%)
  between operations  0.73 us (2%)
  local copies, waits for them, and re-layouts  0.48 us (1%)
    pallas_call x2, Pallas kernels, on_device(): pl.pallas_call(functools.partial(attend_kernel, slots, tuple(staged[phase...  8.89 us
    ppermute x4, starting transfers between devices, send_back(): lax.ppermute(result, 'tok', [(target, source) for source, target in pairs])  6.45 us
    ppermute x3, starting transfers between devices, on_device(): lax.ppermute(send, 'tok', pairs)  4.67 us
    all_to_all x1, starting transfers between devices, on_device(): tiles = lax.all_to_all(total, ('dp', 'tok'), 0, 0, tiled=True)  4.43 us
    ppermute x4, waiting for transfers between devices, send_back(): lax.ppermute(result, 'tok', [(target, source) for source, target in pairs])  4.18 us
    ppermute x3, starting transfers between devices, on_device(): got[phase].append(lax.ppermute(send, 'tok', rounds[leaving - 1]))  3.78 us
    pallas_call x1, Pallas kernels, on_device(): pl.pallas_call(functools.partial(prepare_kernel, slots, images, count, to...  2.93 us
    all_to_all x1, waiting for transfers between devices, on_device(): tiles = lax.all_to_all(total, ('dp', 'tok'), 0, 0, tiled=True)  2.22 us
  transfers between devices with their start and end apart: 11, of which 4 were waited for; matrix products, arithmetic and copies ran while one was open for 0% of the time, Pallas kernels for 31%

profile of v24, /device:TPU:0, one launch (start us, length us, event | category | flops | bytes accessed | tf_op | source)
XLA Modules:
  0.0 43.8 jit_solution(5149865870132494712)
XLA Ops:
  0.6 1.7 %pack_heads.1 = (bf16[320,256]{1,0:T(8,128)(2,1)S(1)}, bf16[320,256]{1,0:T(8,128)(2,1)S(1)}, bf16[320,256]{1,0:T(8,128)(2,1)S(1)}, bf16[320,256]{1,0:T(8,128)(2,1)S(1)}) custom-call(bf16[256,640]{1,0:T(8,128)(2,1)} %bitcast.8, bf16[256,640]{1,0:T(8,128)(2,1)} %bitcast.10, bf16[256,640]{1,0:T(8,128)(2,1)} %bitcast.12, bf16[256,640]{1,0:T(8,128)(2,1)} %bitcast.14), custom_call_target="tpu_custom_call" | custom-call | tf_op jit(solution)/shard_map/pack_heads/pallas_call | solution.py:515
  2.3 0.0 copy-start
  2.3 4.0 %collective-permute-start = (bf16[320,256]{1,0:T(8,128)(2,1)S(1)}, bf16[320,256]{1,0:T(8,128)(2,1)S(1)}, u32[]{:S(2)}, u32[]{:S(2)}) collective-permute-start(bf16[320,256]{1,0:T(8,128)(2,1)S(1)} %get-tuple-element.62), channel_id=1, source_target_pairs={{0,3},{1,2},{2,1},{3,0},{4,7},{5,6},{6,5},{7,4},{8,11},{9,10},{10,... | collective-permute-start | bytes 491528 | tf_op jit(solution)/shard_map/ppermute | solution.py:531
  6.4 0.4 collective-permute-start.3
  6.8 0.0 copy-start.1
  6.8 0.0 copy-start.2
  6.8 0.2 collective-permute-start.5
  7.0 0.0 copy-done
  7.0 0.4 %copy-done.1 = s32[1,4]{1,0:T(1,128)S(1)} copy-done((s32[1,4]{1,0:T(1,128)S(1)}, s32[1,4]{1,0:T(1,128)}, u32[]{:S(2)}) %copy-start.1) | copy-done | bytes 40
  7.5 0.0 copy-done.2
  7.5 2.9 %prepare.1 = (f32[40,1024]{1,0:T(8,128)S(1)}, f32[40,1024]{1,0:T(8,128)S(1)}, f32[24,256]{1,0:T(8,128)S(1)}, f32[160,128]{1,0:T(8,128)S(1)}, bf16[320,256]{1,0:T...) custom-call(s32[1,4]{1,0:T(1,128)S(1)} %copy-done.1, ...), custom_call_target="tpu_custom_call" | custom-call | flops 1000000 | tf_op jit(solution)/shard_map/prepare/pallas_call | solution.py:548
  10.4 1.0 %collective-permute-done.refs_0_.refs_1_ = bf16[320,256]{1,0:T(8,128)(2,1)S(1)} collective-permute-done((bf16[320,256]{1,0:T(8,128)(2,1)S(1)}, bf16[320,256]{1,0:T(8,128)(2,1)S(1)}, u32[]{:S(2)}, u32[]{:S(2)}) %collective-permute-start) | collective-permute-done | bytes 163872 | tf_op jit(solution)/shard_map/ppermute | solution.py:531
  11.4 0.2 stage_slot.2
  11.6 3.1 %collective-permute-start.1 = (bf16[320,256]{1,0:T(8,128)(2,1)S(1)}, bf16[320,256]{1,0:T(8,128)(2,1)S(1)}, u32[]{:S(2)}, u32[]{:S(2)}) collective-permute-start(bf16[320,256]{1,0:T(8,128)(2,1)S(1)} %get-tuple-element.65), channel_id=1, source_target_pairs={{0,3},{1,2},{2,1},{3,0},{4,7},{5,6},{6,5},{7,4},{8,11},{9,10},{10,... | collective-permute-start | bytes 491528 | tf_op jit(solution)/shard_map/ppermute | solution.py:592
  14.6 0.0 copy-start.4
  14.7 0.4 %collective-permute-start.2 = (bf16[320,256]{1,0:T(8,128)(2,1)S(1)}, bf16[320,256]{1,0:T(8,128)(2,1)S(1)}, u32[]{:S(2)}, u32[]{:S(2)}) collective-permute-start(bf16[320,256]{1,0:T(8,128)(2,1)S(1)} %get-tuple-element.69), channel_id=1, source_target_pairs={{0,2},{1,3},{2,0},{3,1},{4,6},{5,7},{6,4},{7,5},{8,10},{9,11},{10,... | collective-permute-start | bytes 491528 | tf_op jit(solution)/shard_map/ppermute | solution.py:592
  15.1 0.0 collective-permute-done.3.refs_0_.refs_2_
  15.1 0.2 stage_slot.3
  15.3 0.3 collective-permute-start.4
  15.6 0.0 collective-permute-done.5.refs_3_
  15.6 0.0 copy-done.4
  15.6 0.0 copy-start.3
  15.6 4.2 %attend_head.2 = (bf16[640,256]{1,0:T(8,128)(2,1)S(1)}, bf16[320,256]{1,0:T(8,128)(2,1)S(1)}, bf16[640,256]{1,0:T(8,128)(2,1)S(1)}, bf16[640,256]{1,0:T(8,128)(2,1)S(1)}, f32[8,128]{1,0:T(8,128)S(1)}) custom-call(f32[40,1024]{1,0:T(8,128)S(1)} %get-tuple-element.56.cosv, f32[40,1024]{1,0:T(8,128)S(1)} %get-tuple-element.57.sinv, ...), custom_call_target="tpu_custom_call" | custom-call | flops 3221225472 | tf_op jit(solution)/shard_map/attend_head/pallas_call | solution.py:602
  19.8 2.9 %collective-permute-start.6 = (bf16[320,256]{1,0:T(8,128)(2,1)S(1)}, bf16[320,256]{1,0:T(8,128)(2,1)S(1)}, u32[]{:S(2)}, u32[]{:S(2)}) collective-permute-start(bf16[320,256]{1,0:T(8,128)(2,1)S(1)} %get-tuple-element.89), channel_id=1, source_target_pairs={{3,0},{2,1},{1,2},{0,3},{7,4},{6,5},{5,6},{4,7},{11,8},{10,9},{9,1... | collective-permute-start | bytes 491528 | tf_op jit(solution)/shard_map/ppermute | solution.py:72
  22.7 0.0 collective-permute-done.1.refs_1_
  22.7 0.0 collective-permute-done.2.refs_2_
  22.7 0.0 collective-permute-done.4.refs_3_
  22.7 0.0 copy-done.3
  22.7 4.7 %attend_head.3 = (bf16[640,256]{1,0:T(8,128)(2,1)S(1)}, bf16[320,256]{1,0:T(8,128)(2,1)S(1)}, bf16[640,256]{1,0:T(8,128)(2,1)S(1)}, bf16[640,256]{1,0:T(8,128)(2,1)S(1)}, f32[32,4,128]{2,1,0:T(4,128)}) custom-call(f32[40,1024]{1,0:T(8,128)S(1)} %get-tuple-element.56.cosv, f32[40,1024]{1,0:T(8,128)S(1)} %get-tuple-element.57.sinv, ...), custom_call_target="tpu_custom_call" | custom-call | flops 3221225472 | tf_op jit(solution)/shard_map/attend_head/pallas_call | solution.py:602
  27.4 0.5 %collective-permute-start.8 = (bf16[640,256]{1,0:T(8,128)(2,1)S(1)}, bf16[640,256]{1,0:T(8,128)(2,1)S(1)}, u32[]{:S(2)}, u32[]{:S(2)}) collective-permute-start(bf16[640,256]{1,0:T(8,128)(2,1)S(1)} %get-tuple-element.93), channel_id=1, source_target_pairs={{2,0},{3,1},{0,2},{1,3},{6,4},{7,5},{4,6},{5,7},{10,8},{11,9},{8,1... | collective-permute-start | bytes 983048 | tf_op jit(solution)/shard_map/ppermute | solution.py:72
  27.9 1.2 %collective-permute-start.9 = (bf16[640,256]{1,0:T(8,128)(2,1)S(1)}, bf16[640,256]{1,0:T(8,128)(2,1)S(1)}, u32[]{:S(2)}, u32[]{:S(2)}) collective-permute-start(bf16[640,256]{1,0:T(8,128)(2,1)S(1)} %get-tuple-element.94), channel_id=1, source_target_pairs={{1,0},{0,1},{3,2},{2,3},{5,4},{4,5},{7,6},{6,7},{9,8},{8,9},{11,10... | collective-permute-start | bytes 983048 | tf_op jit(solution)/shard_map/ppermute | solution.py:72
  29.1 0.0 collective-permute-done.6.refs_0_
  29.1 1.8 %collective-permute-start.7 = (bf16[320,256]{1,0:T(8,128)(2,1)S(1)}, bf16[320,256]{1,0:T(8,128)(2,1)S(1)}, u32[]{:S(2)}, u32[]{:S(2)}) collective-permute-start(bf16[320,256]{1,0:T(8,128)(2,1)S(1)} %get-tuple-element.91), channel_id=1, source_target_pairs={{3,0},{2,1},{1,2},{0,3},{7,4},{6,5},{5,6},{4,7},{11,8},{10,9},{9,1... | collective-permute-start | bytes 491528 | tf_op jit(solution)/shard_map/ppermute | solution.py:72
  31.0 4.4 %all-to-all-start = ((f32[32,4,128]{2,1,0:T(4,128)}), f32[32,4,128]{2,1,0:T(4,128)S(1)}, u32[]{:S(2)}, u32[]{:S(2)}) async-start(f32[32,4,128]{2,1,0:T(4,128)} %get-tuple-element.99), calls=%async_computation | async-start | bytes 131072 | tf_op jit(solution)/shard_map/all_to_all | solution.py:634
  35.4 3.7 %collective-permute-done.7.refs_1_ = bf16[320,256]{1,0:T(8,128)(2,1)S(1)} collective-permute-done((bf16[320,256]{1,0:T(8,128)(2,1)S(1)}, bf16[320,256]{1,0:T(8,128)(2,1)S(1)}, u32[]{:S(2)}, u32[]{:S(2)}) %collective-permute-start.7) | collective-permute-done | bytes 163872 | tf_op jit(solution)/shard_map/ppermute | solution.py:72
  39.1 0.0 collective-permute-done.8.refs_3_
  39.1 0.5 %collective-permute-done.9.refs_4_ = bf16[640,256]{1,0:T(8,128)(2,1)S(1)} collective-permute-done((bf16[640,256]{1,0:T(8,128)(2,1)S(1)}, bf16[640,256]{1,0:T(8,128)(2,1)S(1)}, u32[]{:S(2)}, u32[]{:S(2)}) %collective-permute-start.9) | collective-permute-done | bytes 327712 | tf_op jit(solution)/shard_map/ppermute | solution.py:72
  39.6 1.3 %unpack_heads.1 = (bf16[256,640]{1,0:T(8,128)(2,1)}, bf16[256,640]{1,0:T(8,128)(2,1)}, bf16[256,640]{1,0:T(8,128)(2,1)}, bf16[256,640]{1,0:T(8,128)(2,1)}) custom-call(bf16[320,256]{1,0:T(8,128)(2,1)S(1)} %collective-permute-done.6.refs_0_, bf16[320,256]{1,0:T(8,128)(2,1)S(1)} %collective-permute-done.7.refs_1_, ...), custom_call_target="tpu_custom_call" | custom-call | flops 20000000000 | tf_op jit(solution)/shard_map/unpack_heads/pallas_call | solution.py:637
  40.9 2.2 %all-to-all-done.tiles = f32[32,4,128]{2,1,0:T(4,128)S(1)} async-done(((f32[32,4,128]{2,1,0:T(4,128)}), f32[32,4,128]{2,1,0:T(4,128)S(1)}, u32[]{:S(2)}, u32[]{:S(2)}) %all-to-all-start) | async-done | bytes 65568 | tf_op jit(solution)/shard_map/all_to_all | solution.py:634
  43.1 0.7 %bias_sums.1 = f32[3,640]{1,0:T(4,128)} custom-call(f32[32,4,128]{2,1,0:T(4,128)S(1)} %all-to-all-done.tiles), custom_call_target="tpu_custom_call" | custom-call | tf_op jit(solution)/shard_map/bias_sums/pallas_call | solution.py:652
Async XLA Ops:
  2.3 4.7 %copy-start = (bf16[3,640]{1,0:T(4,128)(2,1)S(1)}, bf16[3,640]{1,0:T(4,128)(2,1)}, u32[]{:S(2)}) copy-start(bf16[3,640]{1,0:T(4,128)(2,1)} %refs_0_.1) | copy-start | bytes 11524
  2.3 9.1 %collective-permute-start = (bf16[320,256]{1,0:T(8,128)(2,1)S(1)}, bf16[320,256]{1,0:T(8,128)(2,1)S(1)}, u32[]{:S(2)}, u32[]{:S(2)}) collective-permute-start(bf16[320,256]{1,0:T(8,128)(2,1)S(1)} %get-tuple-element.62), channel_id=1, source_target_pairs={{0,3},{1,2},{2,1},{3,0},{4,7},{5,6},{6,5},{7,4},{8,11},{9,10},{10,... | collective-permute-start | bytes 491528 | tf_op jit(solution)/shard_map/ppermute | solution.py:531
  6.4 8.7 %collective-permute-start.3 = (bf16[320,256]{1,0:T(8,128)(2,1)S(1)}, bf16[320,256]{1,0:T(8,128)(2,1)S(1)}, u32[]{:S(2)}, u32[]{:S(2)}) collective-permute-start(bf16[320,256]{1,0:T(8,128)(2,1)S(1)} %get-tuple-element.71), channel_id=1, source_target_pairs={{0,2},{1,3},{2,0},{3,1},{4,6},{5,7},{6,4},{7,5},{8,10},{9,11},{10,... | collective-permute-start | bytes 491528 | tf_op jit(solution)/shard_map/ppermute | solution.py:531
  6.8 0.7 %copy-start.1 = (s32[1,4]{1,0:T(1,128)S(1)}, s32[1,4]{1,0:T(1,128)}, u32[]{:S(2)}) copy-start(s32[1,4]{1,0:T(1,128)} %lengths.1) | copy-start | bytes 52
  6.8 0.7 %copy-start.2 = (s32[1,4]{1,0:T(1,128)S(1)}, s32[1,4]{1,0:T(1,128)}, u32[]{:S(2)}) copy-start(s32[1,4]{1,0:T(1,128)} %widths.1) | copy-start | bytes 52
  6.8 8.8 %collective-permute-start.5 = (bf16[320,256]{1,0:T(8,128)(2,1)S(1)}, bf16[320,256]{1,0:T(8,128)(2,1)S(1)}, u32[]{:S(2)}, u32[]{:S(2)}) collective-permute-start(bf16[320,256]{1,0:T(8,128)(2,1)S(1)} %get-tuple-element.77), channel_id=1, source_target_pairs={{0,1},{1,0},{2,3},{3,2},{4,5},{5,4},{6,7},{7,6},{8,9},{9,8},{10,11... | collective-permute-start | bytes 491528 | tf_op jit(solution)/shard_map/ppermute | solution.py:531
  11.6 11.1 %collective-permute-start.1 = (bf16[320,256]{1,0:T(8,128)(2,1)S(1)}, bf16[320,256]{1,0:T(8,128)(2,1)S(1)}, u32[]{:S(2)}, u32[]{:S(2)}) collective-permute-start(bf16[320,256]{1,0:T(8,128)(2,1)S(1)} %get-tuple-element.65), channel_id=1, source_target_pairs={{0,3},{1,2},{2,1},{3,0},{4,7},{5,6},{6,5},{7,4},{8,11},{9,10},{10,... | collective-permute-start | bytes 491528 | tf_op jit(solution)/shard_map/ppermute | solution.py:592
  14.6 0.9 %copy-start.4 = (bf16[3,128,256]{2,1,0:T(8,128)(2,1)S(1)}, bf16[3,128,256]{2,1,0:T(8,128)(2,1)}, u32[]{:S(2)}) copy-start(bf16[3,128,256]{2,1,0:T(8,128)(2,1)} %get-tuple-element.78.refs_4_) | copy-start | bytes 589828
  14.7 8.0 %collective-permute-start.2 = (bf16[320,256]{1,0:T(8,128)(2,1)S(1)}, bf16[320,256]{1,0:T(8,128)(2,1)S(1)}, u32[]{:S(2)}, u32[]{:S(2)}) collective-permute-start(bf16[320,256]{1,0:T(8,128)(2,1)S(1)} %get-tuple-element.69), channel_id=1, source_target_pairs={{0,2},{1,3},{2,0},{3,1},{4,6},{5,7},{6,4},{7,5},{8,10},{9,11},{10,... | collective-permute-start | bytes 491528 | tf_op jit(solution)/shard_map/ppermute | solution.py:592
  15.3 7.4 %collective-permute-start.4 = (bf16[320,256]{1,0:T(8,128)(2,1)S(1)}, bf16[320,256]{1,0:T(8,128)(2,1)S(1)}, u32[]{:S(2)}, u32[]{:S(2)}) collective-permute-start(bf16[320,256]{1,0:T(8,128)(2,1)S(1)} %get-tuple-element.74), channel_id=1, source_target_pairs={{0,1},{1,0},{2,3},{3,2},{4,5},{5,4},{6,7},{7,6},{8,9},{9,8},{10,11... | collective-permute-start | bytes 491528 | tf_op jit(solution)/shard_map/ppermute | solution.py:592
  15.6 7.1 %copy-start.3 = (bf16[3,128,256]{2,1,0:T(8,128)(2,1)S(1)}, bf16[3,128,256]{2,1,0:T(8,128)(2,1)}, u32[]{:S(2)}) copy-start(bf16[3,128,256]{2,1,0:T(8,128)(2,1)} %get-tuple-element.75.refs_4_) | copy-start | bytes 589828
  19.8 9.3 %collective-permute-start.6 = (bf16[320,256]{1,0:T(8,128)(2,1)S(1)}, bf16[320,256]{1,0:T(8,128)(2,1)S(1)}, u32[]{:S(2)}, u32[]{:S(2)}) collective-permute-start(bf16[320,256]{1,0:T(8,128)(2,1)S(1)} %get-tuple-element.89), channel_id=1, source_target_pairs={{3,0},{2,1},{1,2},{0,3},{7,4},{6,5},{5,6},{4,7},{11,8},{10,9},{9,1... | collective-permute-start | bytes 491528 | tf_op jit(solution)/shard_map/ppermute | solution.py:72
  27.4 11.7 %collective-permute-start.8 = (bf16[640,256]{1,0:T(8,128)(2,1)S(1)}, bf16[640,256]{1,0:T(8,128)(2,1)S(1)}, u32[]{:S(2)}, u32[]{:S(2)}) collective-permute-start(bf16[640,256]{1,0:T(8,128)(2,1)S(1)} %get-tuple-element.93), channel_id=1, source_target_pairs={{2,0},{3,1},{0,2},{1,3},{6,4},{7,5},{4,6},{5,7},{10,8},{11,9},{8,1... | collective-permute-start | bytes 983048 | tf_op jit(solution)/shard_map/ppermute | solution.py:72
  27.9 11.7 %collective-permute-start.9 = (bf16[640,256]{1,0:T(8,128)(2,1)S(1)}, bf16[640,256]{1,0:T(8,128)(2,1)S(1)}, u32[]{:S(2)}, u32[]{:S(2)}) collective-permute-start(bf16[640,256]{1,0:T(8,128)(2,1)S(1)} %get-tuple-element.94), channel_id=1, source_target_pairs={{1,0},{0,1},{3,2},{2,3},{5,4},{4,5},{7,6},{6,7},{9,8},{8,9},{11,10... | collective-permute-start | bytes 983048 | tf_op jit(solution)/shard_map/ppermute | solution.py:72
  29.1 10.0 %collective-permute-start.7 = (bf16[320,256]{1,0:T(8,128)(2,1)S(1)}, bf16[320,256]{1,0:T(8,128)(2,1)S(1)}, u32[]{:S(2)}, u32[]{:S(2)}) collective-permute-start(bf16[320,256]{1,0:T(8,128)(2,1)S(1)} %get-tuple-element.91), channel_id=1, source_target_pairs={{3,0},{2,1},{1,2},{0,3},{7,4},{6,5},{5,6},{4,7},{11,8},{10,9},{9,1... | collective-permute-start | bytes 491528 | tf_op jit(solution)/shard_map/ppermute | solution.py:72
  31.0 12.2 %all-to-all-start = ((f32[32,4,128]{2,1,0:T(4,128)}), f32[32,4,128]{2,1,0:T(4,128)S(1)}, u32[]{:S(2)}, u32[]{:S(2)}) async-start(f32[32,4,128]{2,1,0:T(4,128)} %get-tuple-element.99), calls=%async_computation | async-start | bytes 131072 | tf_op jit(solution)/shard_map/all_to_all | solution.py:634

commit v25 on v19

--- a/solution.py
+++ b/solution.py
@@ -216,7 +216,7 @@
     return [
         jnp.concatenate(pair, axis=0).astype(jnp.bfloat16)
         for pair in (
-            (rotate(query, cos_b, sin_b) * (SCALE * LOG2E), zeros),
+            (rotate(query, cos_b, sin_b), zeros),
             (rotate(key, cos_b, sin_b), zeros),
             (value, ones),
         )
@@ -288,7 +288,7 @@
         return jnp.max(part, axis=0, keepdims=True)
 
     def exponentials(slot, keys, top):
-        part = jnp.exp2(s_buf[slot % 2, keys, :] - top)
+        part = jnp.exp2((s_buf[slot % 2, keys, :] - top) * (SCALE * LOG2E))
         e_buf[keys, block_of(slot)] = part.astype(jnp.bfloat16)
 
     def output(slot):
@@ -369,7 +369,7 @@
         dkey = lax.dot_general(
             qt_all[:HEAD_DIM, :], d_buf[at, :], by_lanes, preferred_element_type=jnp.float32
         )
-        dkey = unrotate(dkey * (1.0 / LOG2E), cosv[:, at], sinv[:, at])
+        dkey = unrotate(dkey * SCALE, cosv[:, at], sinv[:, at])
         put(slot, 2, dkey.astype(jnp.bfloat16))
         dk_total = dk_total + live(slot, dkey)
     lane = lax.broadcasted_iota(jnp.int32, (HEAD_DIM, LANES), 1)

time: 43.8 us -> 43.9 us (level)
  no operation moved by 1% of the time
where the time goes in v25:
time: 43.9 us; the launch traced here: 43.7 us
  starting transfers between devices  19.3 us (44%)
  Pallas kernels  15.7 us (36%)
  waiting for transfers between devices  7.51 us (17%)
  between operations  0.73 us (2%)
  local copies, waits for them, and re-layouts  0.49 us (1%)
    pallas_call x2, Pallas kernels, on_device(): pl.pallas_call(functools.partial(attend_kernel, slots, tuple(staged[phase...  8.98 us
    ppermute x4, starting transfers between devices, send_back(): lax.ppermute(result, 'tok', [(target, source) for source, target in pairs])  6.45 us
    ppermute x3, starting transfers between devices, on_device(): lax.ppermute(send, 'tok', pairs)  4.66 us
    all_to_all x1, starting transfers between devices, on_device(): tiles = lax.all_to_all(total, ('dp', 'tok'), 0, 0, tiled=True)  4.39 us
    ppermute x4, waiting for transfers between devices, send_back(): lax.ppermute(result, 'tok', [(target, source) for source, target in pairs])  4.24 us
    ppermute x3, starting transfers between devices, on_device(): got[phase].append(lax.ppermute(send, 'tok', rounds[leaving - 1]))  3.78 us
    pallas_call x1, Pallas kernels, on_device(): pl.pallas_call(functools.partial(prepare_kernel, slots, images, count, to...  2.84 us
    all_to_all x1, waiting for transfers between devices, on_device(): tiles = lax.all_to_all(total, ('dp', 'tok'), 0, 0, tiled=True)  2.19 us
  transfers between devices with their start and end apart: 11, of which 4 were waited for; matrix products, arithmetic and copies ran while one was open for 0% of the time, Pallas kernels for 31%

profile of v25, /device:TPU:0, one launch (start us, length us, event | category | flops | bytes accessed | tf_op | source)
XLA Modules:
  0.0 43.7 jit_solution(16390706202439745214)
XLA Ops:
  0.6 1.5 %pack_heads.1 = (bf16[320,256]{1,0:T(8,128)(2,1)S(1)}, bf16[320,256]{1,0:T(8,128)(2,1)S(1)}, bf16[320,256]{1,0:T(8,128)(2,1)S(1)}, bf16[320,256]{1,0:T(8,128)(2,1)S(1)}) custom-call(bf16[256,640]{1,0:T(8,128)(2,1)} %bitcast.8, bf16[256,640]{1,0:T(8,128)(2,1)} %bitcast.10, bf16[256,640]{1,0:T(8,128)(2,1)} %bitcast.12, bf16[256,640]{1,0:T(8,128)(2,1)} %bitcast.14), custom_call_target="tpu_custom_call" | custom-call | tf_op jit(solution)/shard_map/pack_heads/pallas_call | solution.py:502
  2.1 0.0 copy-start
  2.1 4.0 %collective-permute-start = (bf16[320,256]{1,0:T(8,128)(2,1)S(1)}, bf16[320,256]{1,0:T(8,128)(2,1)S(1)}, u32[]{:S(2)}, u32[]{:S(2)}) collective-permute-start(bf16[320,256]{1,0:T(8,128)(2,1)S(1)} %get-tuple-element.62), channel_id=1, source_target_pairs={{0,3},{1,2},{2,1},{3,0},{4,7},{5,6},{6,5},{7,4},{8,11},{9,10},{10,... | collective-permute-start | bytes 491528 | tf_op jit(solution)/shard_map/ppermute | solution.py:518
  6.1 0.4 %collective-permute-start.3 = (bf16[320,256]{1,0:T(8,128)(2,1)S(1)}, bf16[320,256]{1,0:T(8,128)(2,1)S(1)}, u32[]{:S(2)}, u32[]{:S(2)}) collective-permute-start(bf16[320,256]{1,0:T(8,128)(2,1)S(1)} %get-tuple-element.71), channel_id=1, source_target_pairs={{0,2},{1,3},{2,0},{3,1},{4,6},{5,7},{6,4},{7,5},{8,10},{9,11},{10,... | collective-permute-start | bytes 491528 | tf_op jit(solution)/shard_map/ppermute | solution.py:518
  6.6 0.0 copy-start.1
  6.6 0.0 copy-start.2
  6.6 0.2 collective-permute-start.5
  6.8 0.0 copy-done
  6.8 0.4 %copy-done.1 = s32[1,4]{1,0:T(1,128)S(1)} copy-done((s32[1,4]{1,0:T(1,128)S(1)}, s32[1,4]{1,0:T(1,128)}, u32[]{:S(2)}) %copy-start.1) | copy-done | bytes 40
  7.2 0.0 copy-done.2
  7.2 2.8 %prepare.1 = (f32[40,1024]{1,0:T(8,128)S(1)}, f32[40,1024]{1,0:T(8,128)S(1)}, f32[24,256]{1,0:T(8,128)S(1)}, f32[160,128]{1,0:T(8,128)S(1)}, bf16[320,256]{1,0:T...) custom-call(s32[1,4]{1,0:T(1,128)S(1)} %copy-done.1, ...), custom_call_target="tpu_custom_call" | custom-call | flops 1000000 | tf_op jit(solution)/shard_map/prepare/pallas_call | solution.py:535
  10.1 1.1 %collective-permute-done.refs_0_.refs_1_ = bf16[320,256]{1,0:T(8,128)(2,1)S(1)} collective-permute-done((bf16[320,256]{1,0:T(8,128)(2,1)S(1)}, bf16[320,256]{1,0:T(8,128)(2,1)S(1)}, u32[]{:S(2)}, u32[]{:S(2)}) %collective-permute-start) | collective-permute-done | bytes 163872 | tf_op jit(solution)/shard_map/ppermute | solution.py:518
  11.2 0.2 stage_slot.2
  11.3 3.1 %collective-permute-start.1 = (bf16[320,256]{1,0:T(8,128)(2,1)S(1)}, bf16[320,256]{1,0:T(8,128)(2,1)S(1)}, u32[]{:S(2)}, u32[]{:S(2)}) collective-permute-start(bf16[320,256]{1,0:T(8,128)(2,1)S(1)} %get-tuple-element.65), channel_id=1, source_target_pairs={{0,3},{1,2},{2,1},{3,0},{4,7},{5,6},{6,5},{7,4},{8,11},{9,10},{10,... | collective-permute-start | bytes 491528 | tf_op jit(solution)/shard_map/ppermute | solution.py:579
  14.4 0.0 copy-start.4
  14.4 0.4 %collective-permute-start.2 = (bf16[320,256]{1,0:T(8,128)(2,1)S(1)}, bf16[320,256]{1,0:T(8,128)(2,1)S(1)}, u32[]{:S(2)}, u32[]{:S(2)}) collective-permute-start(bf16[320,256]{1,0:T(8,128)(2,1)S(1)} %get-tuple-element.69), channel_id=1, source_target_pairs={{0,2},{1,3},{2,0},{3,1},{4,6},{5,7},{6,4},{7,5},{8,10},{9,11},{10,... | collective-permute-start | bytes 491528 | tf_op jit(solution)/shard_map/ppermute | solution.py:579
  14.8 0.0 collective-permute-done.3.refs_0_.refs_2_
  14.9 0.2 stage_slot.3
  15.0 0.3 collective-permute-start.4
  15.3 0.0 collective-permute-done.5.refs_3_
  15.3 0.0 copy-done.4
  15.3 0.0 copy-start.3
  15.3 4.2 %attend_head.2 = (bf16[640,256]{1,0:T(8,128)(2,1)S(1)}, bf16[320,256]{1,0:T(8,128)(2,1)S(1)}, bf16[640,256]{1,0:T(8,128)(2,1)S(1)}, bf16[640,256]{1,0:T(8,128)(2,1)S(1)}, f32[8,128]{1,0:T(8,128)S(1)}) custom-call(f32[40,1024]{1,0:T(8,128)S(1)} %get-tuple-element.56.cosv, f32[40,1024]{1,0:T(8,128)S(1)} %get-tuple-element.57.sinv, ...), custom_call_target="tpu_custom_call" | custom-call | flops 3221225472 | tf_op jit(solution)/shard_map/attend_head/pallas_call | solution.py:589
  19.6 2.9 %collective-permute-start.6 = (bf16[320,256]{1,0:T(8,128)(2,1)S(1)}, bf16[320,256]{1,0:T(8,128)(2,1)S(1)}, u32[]{:S(2)}, u32[]{:S(2)}) collective-permute-start(bf16[320,256]{1,0:T(8,128)(2,1)S(1)} %get-tuple-element.89), channel_id=1, source_target_pairs={{3,0},{2,1},{1,2},{0,3},{7,4},{6,5},{5,6},{4,7},{11,8},{10,9},{9,1... | collective-permute-start | bytes 491528 | tf_op jit(solution)/shard_map/ppermute | solution.py:72
  22.5 0.0 collective-permute-done.1.refs_1_
  22.5 0.0 collective-permute-done.2.refs_2_
  22.5 0.0 collective-permute-done.4.refs_3_
  22.5 0.0 copy-done.3
  22.5 4.7 %attend_head.3 = (bf16[640,256]{1,0:T(8,128)(2,1)S(1)}, bf16[320,256]{1,0:T(8,128)(2,1)S(1)}, bf16[640,256]{1,0:T(8,128)(2,1)S(1)}, bf16[640,256]{1,0:T(8,128)(2,1)S(1)}, f32[32,4,128]{2,1,0:T(4,128)}) custom-call(f32[40,1024]{1,0:T(8,128)S(1)} %get-tuple-element.56.cosv, f32[40,1024]{1,0:T(8,128)S(1)} %get-tuple-element.57.sinv, ...), custom_call_target="tpu_custom_call" | custom-call | flops 3221225472 | tf_op jit(solution)/shard_map/attend_head/pallas_call | solution.py:589
  27.2 0.5 %collective-permute-start.8 = (bf16[640,256]{1,0:T(8,128)(2,1)S(1)}, bf16[640,256]{1,0:T(8,128)(2,1)S(1)}, u32[]{:S(2)}, u32[]{:S(2)}) collective-permute-start(bf16[640,256]{1,0:T(8,128)(2,1)S(1)} %get-tuple-element.93), channel_id=1, source_target_pairs={{2,0},{3,1},{0,2},{1,3},{6,4},{7,5},{4,6},{5,7},{10,8},{11,9},{8,1... | collective-permute-start | bytes 983048 | tf_op jit(solution)/shard_map/ppermute | solution.py:72
  27.8 1.2 %collective-permute-start.9 = (bf16[640,256]{1,0:T(8,128)(2,1)S(1)}, bf16[640,256]{1,0:T(8,128)(2,1)S(1)}, u32[]{:S(2)}, u32[]{:S(2)}) collective-permute-start(bf16[640,256]{1,0:T(8,128)(2,1)S(1)} %get-tuple-element.94), channel_id=1, source_target_pairs={{1,0},{0,1},{3,2},{2,3},{5,4},{4,5},{7,6},{6,7},{9,8},{8,9},{11,10... | collective-permute-start | bytes 983048 | tf_op jit(solution)/shard_map/ppermute | solution.py:72
  28.9 0.0 collective-permute-done.6.refs_0_
  28.9 1.9 %collective-permute-start.7 = (bf16[320,256]{1,0:T(8,128)(2,1)S(1)}, bf16[320,256]{1,0:T(8,128)(2,1)S(1)}, u32[]{:S(2)}, u32[]{:S(2)}) collective-permute-start(bf16[320,256]{1,0:T(8,128)(2,1)S(1)} %get-tuple-element.91), channel_id=1, source_target_pairs={{3,0},{2,1},{1,2},{0,3},{7,4},{6,5},{5,6},{4,7},{11,8},{10,9},{9,1... | collective-permute-start | bytes 491528 | tf_op jit(solution)/shard_map/ppermute | solution.py:72
  30.8 4.4 %all-to-all-start = ((f32[32,4,128]{2,1,0:T(4,128)}), f32[32,4,128]{2,1,0:T(4,128)S(1)}, u32[]{:S(2)}, u32[]{:S(2)}) async-start(f32[32,4,128]{2,1,0:T(4,128)} %get-tuple-element.99), calls=%async_computation | async-start | bytes 131072 | tf_op jit(solution)/shard_map/all_to_all | solution.py:621
  35.2 3.7 %collective-permute-done.7.refs_1_ = bf16[320,256]{1,0:T(8,128)(2,1)S(1)} collective-permute-done((bf16[320,256]{1,0:T(8,128)(2,1)S(1)}, bf16[320,256]{1,0:T(8,128)(2,1)S(1)}, u32[]{:S(2)}, u32[]{:S(2)}) %collective-permute-start.7) | collective-permute-done | bytes 163872 | tf_op jit(solution)/shard_map/ppermute | solution.py:72
  38.9 0.0 collective-permute-done.8.refs_3_
  38.9 0.5 %collective-permute-done.9.refs_4_ = bf16[640,256]{1,0:T(8,128)(2,1)S(1)} collective-permute-done((bf16[640,256]{1,0:T(8,128)(2,1)S(1)}, bf16[640,256]{1,0:T(8,128)(2,1)S(1)}, u32[]{:S(2)}, u32[]{:S(2)}) %collective-permute-start.9) | collective-permute-done | bytes 327712 | tf_op jit(solution)/shard_map/ppermute | solution.py:72
  39.4 1.3 %unpack_heads.1 = (bf16[256,640]{1,0:T(8,128)(2,1)}, bf16[256,640]{1,0:T(8,128)(2,1)}, bf16[256,640]{1,0:T(8,128)(2,1)}, bf16[256,640]{1,0:T(8,128)(2,1)}) custom-call(bf16[320,256]{1,0:T(8,128)(2,1)S(1)} %collective-permute-done.6.refs_0_, bf16[320,256]{1,0:T(8,128)(2,1)S(1)} %collective-permute-done.7.refs_1_, ...), custom_call_target="tpu_custom_call" | custom-call | flops 20000000000 | tf_op jit(solution)/shard_map/unpack_heads/pallas_call | solution.py:624
  40.8 2.2 %all-to-all-done.tiles = f32[32,4,128]{2,1,0:T(4,128)S(1)} async-done(((f32[32,4,128]{2,1,0:T(4,128)}), f32[32,4,128]{2,1,0:T(4,128)S(1)}, u32[]{:S(2)}, u32[]{:S(2)}) %all-to-all-start) | async-done | bytes 65568 | tf_op jit(solution)/shard_map/all_to_all | solution.py:621
  43.0 0.7 %bias_sums.1 = f32[3,640]{1,0:T(4,128)} custom-call(f32[32,4,128]{2,1,0:T(4,128)S(1)} %all-to-all-done.tiles), custom_call_target="tpu_custom_call" | custom-call | tf_op jit(solution)/shard_map/bias_sums/pallas_call | solution.py:639
Async XLA Ops:
  2.1 4.7 %copy-start = (bf16[3,640]{1,0:T(4,128)(2,1)S(1)}, bf16[3,640]{1,0:T(4,128)(2,1)}, u32[]{:S(2)}) copy-start(bf16[3,640]{1,0:T(4,128)(2,1)} %refs_0_.1) | copy-start | bytes 11524
  2.1 9.0 %collective-permute-start = (bf16[320,256]{1,0:T(8,128)(2,1)S(1)}, bf16[320,256]{1,0:T(8,128)(2,1)S(1)}, u32[]{:S(2)}, u32[]{:S(2)}) collective-permute-start(bf16[320,256]{1,0:T(8,128)(2,1)S(1)} %get-tuple-element.62), channel_id=1, source_target_pairs={{0,3},{1,2},{2,1},{3,0},{4,7},{5,6},{6,5},{7,4},{8,11},{9,10},{10,... | collective-permute-start | bytes 491528 | tf_op jit(solution)/shard_map/ppermute | solution.py:518
  6.1 8.7 %collective-permute-start.3 = (bf16[320,256]{1,0:T(8,128)(2,1)S(1)}, bf16[320,256]{1,0:T(8,128)(2,1)S(1)}, u32[]{:S(2)}, u32[]{:S(2)}) collective-permute-start(bf16[320,256]{1,0:T(8,128)(2,1)S(1)} %get-tuple-element.71), channel_id=1, source_target_pairs={{0,2},{1,3},{2,0},{3,1},{4,6},{5,7},{6,4},{7,5},{8,10},{9,11},{10,... | collective-permute-start | bytes 491528 | tf_op jit(solution)/shard_map/ppermute | solution.py:518
  6.6 0.7 %copy-start.1 = (s32[1,4]{1,0:T(1,128)S(1)}, s32[1,4]{1,0:T(1,128)}, u32[]{:S(2)}) copy-start(s32[1,4]{1,0:T(1,128)} %lengths.1) | copy-start | bytes 52
  6.6 0.7 %copy-start.2 = (s32[1,4]{1,0:T(1,128)S(1)}, s32[1,4]{1,0:T(1,128)}, u32[]{:S(2)}) copy-start(s32[1,4]{1,0:T(1,128)} %widths.1) | copy-start | bytes 52
  6.6 8.7 %collective-permute-start.5 = (bf16[320,256]{1,0:T(8,128)(2,1)S(1)}, bf16[320,256]{1,0:T(8,128)(2,1)S(1)}, u32[]{:S(2)}, u32[]{:S(2)}) collective-permute-start(bf16[320,256]{1,0:T(8,128)(2,1)S(1)} %get-tuple-element.77), channel_id=1, source_target_pairs={{0,1},{1,0},{2,3},{3,2},{4,5},{5,4},{6,7},{7,6},{8,9},{9,8},{10,11... | collective-permute-start | bytes 491528 | tf_op jit(solution)/shard_map/ppermute | solution.py:518
  11.3 11.1 %collective-permute-start.1 = (bf16[320,256]{1,0:T(8,128)(2,1)S(1)}, bf16[320,256]{1,0:T(8,128)(2,1)S(1)}, u32[]{:S(2)}, u32[]{:S(2)}) collective-permute-start(bf16[320,256]{1,0:T(8,128)(2,1)S(1)} %get-tuple-element.65), channel_id=1, source_target_pairs={{0,3},{1,2},{2,1},{3,0},{4,7},{5,6},{6,5},{7,4},{8,11},{9,10},{10,... | collective-permute-start | bytes 491528 | tf_op jit(solution)/shard_map/ppermute | solution.py:579
  14.4 0.9 %copy-start.4 = (bf16[3,128,256]{2,1,0:T(8,128)(2,1)S(1)}, bf16[3,128,256]{2,1,0:T(8,128)(2,1)}, u32[]{:S(2)}) copy-start(bf16[3,128,256]{2,1,0:T(8,128)(2,1)} %get-tuple-element.78.refs_4_) | copy-start | bytes 589828
  14.4 8.1 %collective-permute-start.2 = (bf16[320,256]{1,0:T(8,128)(2,1)S(1)}, bf16[320,256]{1,0:T(8,128)(2,1)S(1)}, u32[]{:S(2)}, u32[]{:S(2)}) collective-permute-start(bf16[320,256]{1,0:T(8,128)(2,1)S(1)} %get-tuple-element.69), channel_id=1, source_target_pairs={{0,2},{1,3},{2,0},{3,1},{4,6},{5,7},{6,4},{7,5},{8,10},{9,11},{10,... | collective-permute-start | bytes 491528 | tf_op jit(solution)/shard_map/ppermute | solution.py:579
  15.0 7.4 %collective-permute-start.4 = (bf16[320,256]{1,0:T(8,128)(2,1)S(1)}, bf16[320,256]{1,0:T(8,128)(2,1)S(1)}, u32[]{:S(2)}, u32[]{:S(2)}) collective-permute-start(bf16[320,256]{1,0:T(8,128)(2,1)S(1)} %get-tuple-element.74), channel_id=1, source_target_pairs={{0,1},{1,0},{2,3},{3,2},{4,5},{5,4},{6,7},{7,6},{8,9},{9,8},{10,11... | collective-permute-start | bytes 491528 | tf_op jit(solution)/shard_map/ppermute | solution.py:579
  15.3 7.2 %copy-start.3 = (bf16[3,128,256]{2,1,0:T(8,128)(2,1)S(1)}, bf16[3,128,256]{2,1,0:T(8,128)(2,1)}, u32[]{:S(2)}) copy-start(bf16[3,128,256]{2,1,0:T(8,128)(2,1)} %get-tuple-element.75.refs_4_) | copy-start | bytes 589828
  19.6 9.4 %collective-permute-start.6 = (bf16[320,256]{1,0:T(8,128)(2,1)S(1)}, bf16[320,256]{1,0:T(8,128)(2,1)S(1)}, u32[]{:S(2)}, u32[]{:S(2)}) collective-permute-start(bf16[320,256]{1,0:T(8,128)(2,1)S(1)} %get-tuple-element.89), channel_id=1, source_target_pairs={{3,0},{2,1},{1,2},{0,3},{7,4},{6,5},{5,6},{4,7},{11,8},{10,9},{9,1... | collective-permute-start | bytes 491528 | tf_op jit(solution)/shard_map/ppermute | solution.py:72
  27.2 11.7 %collective-permute-start.8 = (bf16[640,256]{1,0:T(8,128)(2,1)S(1)}, bf16[640,256]{1,0:T(8,128)(2,1)S(1)}, u32[]{:S(2)}, u32[]{:S(2)}) collective-permute-start(bf16[640,256]{1,0:T(8,128)(2,1)S(1)} %get-tuple-element.93), channel_id=1, source_target_pairs={{2,0},{3,1},{0,2},{1,3},{6,4},{7,5},{4,6},{5,7},{10,8},{11,9},{8,1... | collective-permute-start | bytes 983048 | tf_op jit(solution)/shard_map/ppermute | solution.py:72
  27.8 11.7 %collective-permute-start.9 = (bf16[640,256]{1,0:T(8,128)(2,1)S(1)}, bf16[640,256]{1,0:T(8,128)(2,1)S(1)}, u32[]{:S(2)}, u32[]{:S(2)}) collective-permute-start(bf16[640,256]{1,0:T(8,128)(2,1)S(1)} %get-tuple-element.94), channel_id=1, source_target_pairs={{1,0},{0,1},{3,2},{2,3},{5,4},{4,5},{7,6},{6,7},{9,8},{8,9},{11,10... | collective-permute-start | bytes 983048 | tf_op jit(solution)/shard_map/ppermute | solution.py:72
  28.9 10.0 %collective-permute-start.7 = (bf16[320,256]{1,0:T(8,128)(2,1)S(1)}, bf16[320,256]{1,0:T(8,128)(2,1)S(1)}, u32[]{:S(2)}, u32[]{:S(2)}) collective-permute-start(bf16[320,256]{1,0:T(8,128)(2,1)S(1)} %get-tuple-element.91), channel_id=1, source_target_pairs={{3,0},{2,1},{1,2},{0,3},{7,4},{6,5},{5,6},{4,7},{11,8},{10,9},{9,1... | collective-permute-start | bytes 491528 | tf_op jit(solution)/shard_map/ppermute | solution.py:72
  30.8 12.2 %all-to-all-start = ((f32[32,4,128]{2,1,0:T(4,128)}), f32[32,4,128]{2,1,0:T(4,128)S(1)}, u32[]{:S(2)}, u32[]{:S(2)}) async-start(f32[32,4,128]{2,1,0:T(4,128)} %get-tuple-element.99), calls=%async_computation | async-start | bytes 131072 | tf_op jit(solution)/shard_map/all_to_all | solution.py:621

commit v26 on v25

--- a/solution.py
+++ b/solution.py
@@ -33,7 +33,7 @@
 
 
 def closed_step(slot):
-    return (SPAN - slot) % SPAN
+    return (0, 3, 1, 2)[slot]
 
 
 def trade_rounds(count):

time: 43.9 us -> 45.3 us (1.032)
  waiting for transfers between devices: 7.51 us -> 8.42 us
    ppermute x4, waiting for transfers between devices: 4.24 us -> 5.62 us  [send_back(): lax.ppermute(result, 'tok', [(target, source) for source, target in pairs])]
    ppermute x4, starting transfers between devices: 6.45 us -> 5.08 us  [send_back(): lax.ppermute(result, 'tok', [(target, source) for source, target in pairs])]
    ppermute x3, starting transfers between devices: 3.78 us -> 5.11 us  [on_device(): got[phase].append(lax.ppermute(send, 'tok', rounds[leaving - 1]))]
  transfers between devices with their start and end apart: 11 -> 11, of which waited for: 4 -> 3; matrix products, arithmetic and copies ran while one was open for 0% -> 0% of each run, Pallas kernels for 31% -> 30%
where the time goes in v26:
time: 45.3 us; the launch traced here: 45.1 us
  starting transfers between devices  19.7 us (43%)
  Pallas kernels  15.7 us (35%)
  waiting for transfers between devices  8.42 us (19%)
  between operations  0.73 us (2%)
  local copies, waits for them, and re-layouts  0.58 us (1%)
    pallas_call x2, Pallas kernels, on_device(): pl.pallas_call(functools.partial(attend_kernel, slots, tuple(staged[phase...  8.99 us
    ppermute x4, waiting for transfers between devices, send_back(): lax.ppermute(result, 'tok', [(target, source) for source, target in pairs])  5.62 us
    ppermute x3, starting transfers between devices, on_device(): got[phase].append(lax.ppermute(send, 'tok', rounds[leaving - 1]))  5.11 us
    ppermute x4, starting transfers between devices, send_back(): lax.ppermute(result, 'tok', [(target, source) for source, target in pairs])  5.08 us
    all_to_all x1, starting transfers between devices, on_device(): tiles = lax.all_to_all(total, ('dp', 'tok'), 0, 0, tiled=True)  4.82 us
    ppermute x3, starting transfers between devices, on_device(): lax.ppermute(send, 'tok', pairs)  4.66 us
    pallas_call x1, Pallas kernels, on_device(): pl.pallas_call(functools.partial(prepare_kernel, slots, images, count, to...  2.84 us
    all_to_all x1, waiting for transfers between devices, on_device(): tiles = lax.all_to_all(total, ('dp', 'tok'), 0, 0, tiled=True)  1.82 us
  transfers between devices with their start and end apart: 11, of which 3 were waited for; matrix products, arithmetic and copies ran while one was open for 0% of the time, Pallas kernels for 30%

profile of v26, /device:TPU:0, one launch (start us, length us, event | category | flops | bytes accessed | tf_op | source)
XLA Modules:
  0.0 45.1 jit_solution(13080240043241614138)
XLA Ops:
  0.6 1.5 %pack_heads.1 = (bf16[320,256]{1,0:T(8,128)(2,1)S(1)}, bf16[320,256]{1,0:T(8,128)(2,1)S(1)}, bf16[320,256]{1,0:T(8,128)(2,1)S(1)}, bf16[320,256]{1,0:T(8,128)(2,1)S(1)}) custom-call(bf16[256,640]{1,0:T(8,128)(2,1)} %bitcast.8, bf16[256,640]{1,0:T(8,128)(2,1)} %bitcast.10, bf16[256,640]{1,0:T(8,128)(2,1)} %bitcast.12, bf16[256,640]{1,0:T(8,128)(2,1)} %bitcast.14), custom_call_target="tpu_custom_call" | custom-call | tf_op jit(solution)/shard_map/pack_heads/pallas_call | solution.py:502
  2.1 0.0 copy-start
  2.1 4.0 %collective-permute-start = (bf16[320,256]{1,0:T(8,128)(2,1)S(1)}, bf16[320,256]{1,0:T(8,128)(2,1)S(1)}, u32[]{:S(2)}, u32[]{:S(2)}) collective-permute-start(bf16[320,256]{1,0:T(8,128)(2,1)S(1)} %get-tuple-element.62), channel_id=1, source_target_pairs={{0,3},{1,2},{2,1},{3,0},{4,7},{5,6},{6,5},{7,4},{8,11},{9,10},{10,... | collective-permute-start | bytes 491528 | tf_op jit(solution)/shard_map/ppermute | solution.py:518
  6.1 0.5 %collective-permute-start.3 = (bf16[320,256]{1,0:T(8,128)(2,1)S(1)}, bf16[320,256]{1,0:T(8,128)(2,1)S(1)}, u32[]{:S(2)}, u32[]{:S(2)}) collective-permute-start(bf16[320,256]{1,0:T(8,128)(2,1)S(1)} %get-tuple-element.71), channel_id=1, source_target_pairs={{0,1},{1,0},{2,3},{3,2},{4,5},{5,4},{6,7},{7,6},{8,9},{9,8},{10,11... | collective-permute-start | bytes 491528 | tf_op jit(solution)/shard_map/ppermute | solution.py:518
  6.7 0.0 copy-start.1
  6.7 0.0 copy-start.2
  6.7 0.1 collective-permute-start.5
  6.8 0.0 copy-done
  6.8 0.5 %copy-done.1 = s32[1,4]{1,0:T(1,128)S(1)} copy-done((s32[1,4]{1,0:T(1,128)S(1)}, s32[1,4]{1,0:T(1,128)}, u32[]{:S(2)}) %copy-start.1) | copy-done | bytes 40
  7.3 0.0 copy-done.2
  7.3 2.8 %prepare.1 = (f32[40,1024]{1,0:T(8,128)S(1)}, f32[40,1024]{1,0:T(8,128)S(1)}, f32[24,256]{1,0:T(8,128)S(1)}, f32[160,128]{1,0:T(8,128)S(1)}, bf16[320,256]{1,0:T...) custom-call(s32[1,4]{1,0:T(1,128)S(1)} %copy-done.1, ...), custom_call_target="tpu_custom_call" | custom-call | flops 1000000 | tf_op jit(solution)/shard_map/prepare/pallas_call | solution.py:535
  10.2 1.0 %collective-permute-done.refs_0_.refs_1_ = bf16[320,256]{1,0:T(8,128)(2,1)S(1)} collective-permute-done((bf16[320,256]{1,0:T(8,128)(2,1)S(1)}, bf16[320,256]{1,0:T(8,128)(2,1)S(1)}, u32[]{:S(2)}, u32[]{:S(2)}) %collective-permute-start) | collective-permute-done | bytes 163872 | tf_op jit(solution)/shard_map/ppermute | solution.py:518
  11.2 0.2 stage_slot.2
  11.3 3.0 %collective-permute-start.1 = (bf16[320,256]{1,0:T(8,128)(2,1)S(1)}, bf16[320,256]{1,0:T(8,128)(2,1)S(1)}, u32[]{:S(2)}, u32[]{:S(2)}) collective-permute-start(bf16[320,256]{1,0:T(8,128)(2,1)S(1)} %get-tuple-element.65), channel_id=1, source_target_pairs={{0,3},{1,2},{2,1},{3,0},{4,7},{5,6},{6,5},{7,4},{8,11},{9,10},{10,... | collective-permute-start | bytes 491528 | tf_op jit(solution)/shard_map/ppermute | solution.py:579
  14.4 0.0 copy-start.4
  14.4 0.6 %collective-permute-start.2 = (bf16[320,256]{1,0:T(8,128)(2,1)S(1)}, bf16[320,256]{1,0:T(8,128)(2,1)S(1)}, u32[]{:S(2)}, u32[]{:S(2)}) collective-permute-start(bf16[320,256]{1,0:T(8,128)(2,1)S(1)} %get-tuple-element.69), channel_id=1, source_target_pairs={{0,1},{1,0},{2,3},{3,2},{4,5},{5,4},{6,7},{7,6},{8,9},{9,8},{10,11... | collective-permute-start | bytes 491528 | tf_op jit(solution)/shard_map/ppermute | solution.py:579
  14.9 0.0 collective-permute-done.3.refs_0_.refs_2_
  14.9 0.2 stage_slot.3
  15.1 1.5 %collective-permute-start.4 = (bf16[320,256]{1,0:T(8,128)(2,1)S(1)}, bf16[320,256]{1,0:T(8,128)(2,1)S(1)}, u32[]{:S(2)}, u32[]{:S(2)}) collective-permute-start(bf16[320,256]{1,0:T(8,128)(2,1)S(1)} %get-tuple-element.74), channel_id=1, source_target_pairs={{0,2},{1,3},{2,0},{3,1},{4,6},{5,7},{6,4},{7,5},{8,10},{9,11},{10,... | collective-permute-start | bytes 491528 | tf_op jit(solution)/shard_map/ppermute | solution.py:579
  16.6 0.0 collective-permute-done.5.refs_3_
  16.6 0.0 copy-done.4
  16.6 0.0 copy-start.3
  16.6 4.2 %attend_head.2 = (bf16[640,256]{1,0:T(8,128)(2,1)S(1)}, bf16[320,256]{1,0:T(8,128)(2,1)S(1)}, bf16[640,256]{1,0:T(8,128)(2,1)S(1)}, bf16[640,256]{1,0:T(8,128)(2,1)S(1)}, f32[8,128]{1,0:T(8,128)S(1)}) custom-call(f32[40,1024]{1,0:T(8,128)S(1)} %get-tuple-element.56.cosv, f32[40,1024]{1,0:T(8,128)S(1)} %get-tuple-element.57.sinv, ...), custom_call_target="tpu_custom_call" | custom-call | flops 3221225472 | tf_op jit(solution)/shard_map/attend_head/pallas_call | solution.py:589
  20.9 1.5 %collective-permute-start.6 = (bf16[320,256]{1,0:T(8,128)(2,1)S(1)}, bf16[320,256]{1,0:T(8,128)(2,1)S(1)}, u32[]{:S(2)}, u32[]{:S(2)}) collective-permute-start(bf16[320,256]{1,0:T(8,128)(2,1)S(1)} %get-tuple-element.89), channel_id=1, source_target_pairs={{3,0},{2,1},{1,2},{0,3},{7,4},{6,5},{5,6},{4,7},{11,8},{10,9},{9,1... | collective-permute-start | bytes 491528 | tf_op jit(solution)/shard_map/ppermute | solution.py:72
  22.4 0.0 collective-permute-done.1.refs_1_
  22.4 0.0 collective-permute-done.2.refs_2_
  22.4 0.0 collective-permute-done.4.refs_3_
  22.4 0.0 copy-done.3
  22.5 4.7 %attend_head.3 = (bf16[640,256]{1,0:T(8,128)(2,1)S(1)}, bf16[320,256]{1,0:T(8,128)(2,1)S(1)}, bf16[640,256]{1,0:T(8,128)(2,1)S(1)}, bf16[640,256]{1,0:T(8,128)(2,1)S(1)}, f32[32,4,128]{2,1,0:T(4,128)}) custom-call(f32[40,1024]{1,0:T(8,128)S(1)} %get-tuple-element.56.cosv, f32[40,1024]{1,0:T(8,128)S(1)} %get-tuple-element.57.sinv, ...), custom_call_target="tpu_custom_call" | custom-call | flops 3221225472 | tf_op jit(solution)/shard_map/attend_head/pallas_call | solution.py:589
  27.2 0.6 %collective-permute-start.8 = (bf16[640,256]{1,0:T(8,128)(2,1)S(1)}, bf16[640,256]{1,0:T(8,128)(2,1)S(1)}, u32[]{:S(2)}, u32[]{:S(2)}) collective-permute-start(bf16[640,256]{1,0:T(8,128)(2,1)S(1)} %get-tuple-element.93), channel_id=1, source_target_pairs={{1,0},{0,1},{3,2},{2,3},{5,4},{4,5},{7,6},{6,7},{9,8},{8,9},{11,10... | collective-permute-start | bytes 983048 | tf_op jit(solution)/shard_map/ppermute | solution.py:72
  27.8 1.5 %collective-permute-start.9 = (bf16[640,256]{1,0:T(8,128)(2,1)S(1)}, bf16[640,256]{1,0:T(8,128)(2,1)S(1)}, u32[]{:S(2)}, u32[]{:S(2)}) collective-permute-start(bf16[640,256]{1,0:T(8,128)(2,1)S(1)} %get-tuple-element.94), channel_id=1, source_target_pairs={{2,0},{3,1},{0,2},{1,3},{6,4},{7,5},{4,6},{5,7},{10,8},{11,9},{8,1... | collective-permute-start | bytes 983048 | tf_op jit(solution)/shard_map/ppermute | solution.py:72
  29.3 0.0 collective-permute-done.6.refs_0_
  29.3 1.4 %collective-permute-start.7 = (bf16[320,256]{1,0:T(8,128)(2,1)S(1)}, bf16[320,256]{1,0:T(8,128)(2,1)S(1)}, u32[]{:S(2)}, u32[]{:S(2)}) collective-permute-start(bf16[320,256]{1,0:T(8,128)(2,1)S(1)} %get-tuple-element.91), channel_id=1, source_target_pairs={{3,0},{2,1},{1,2},{0,3},{7,4},{6,5},{5,6},{4,7},{11,8},{10,9},{9,1... | collective-permute-start | bytes 491528 | tf_op jit(solution)/shard_map/ppermute | solution.py:72
  30.8 4.8 %all-to-all-start = ((f32[32,4,128]{2,1,0:T(4,128)}), f32[32,4,128]{2,1,0:T(4,128)S(1)}, u32[]{:S(2)}, u32[]{:S(2)}) async-start(f32[32,4,128]{2,1,0:T(4,128)} %get-tuple-element.99), calls=%async_computation | async-start | bytes 131072 | tf_op jit(solution)/shard_map/all_to_all | solution.py:621
  35.6 5.6 %collective-permute-done.7.refs_1_ = bf16[320,256]{1,0:T(8,128)(2,1)S(1)} collective-permute-done((bf16[320,256]{1,0:T(8,128)(2,1)S(1)}, bf16[320,256]{1,0:T(8,128)(2,1)S(1)}, u32[]{:S(2)}, u32[]{:S(2)}) %collective-permute-start.7) | collective-permute-done | bytes 163872 | tf_op jit(solution)/shard_map/ppermute | solution.py:72
  41.2 0.0 collective-permute-done.8.refs_3_
  41.2 0.0 collective-permute-done.9.refs_4_
  41.2 1.3 %unpack_heads.1 = (bf16[256,640]{1,0:T(8,128)(2,1)}, bf16[256,640]{1,0:T(8,128)(2,1)}, bf16[256,640]{1,0:T(8,128)(2,1)}, bf16[256,640]{1,0:T(8,128)(2,1)}) custom-call(bf16[320,256]{1,0:T(8,128)(2,1)S(1)} %collective-permute-done.6.refs_0_, bf16[320,256]{1,0:T(8,128)(2,1)S(1)} %collective-permute-done.7.refs_1_, ...), custom_call_target="tpu_custom_call" | custom-call | flops 20000000000 | tf_op jit(solution)/shard_map/unpack_heads/pallas_call | solution.py:624
  42.5 1.8 %all-to-all-done.tiles = f32[32,4,128]{2,1,0:T(4,128)S(1)} async-done(((f32[32,4,128]{2,1,0:T(4,128)}), f32[32,4,128]{2,1,0:T(4,128)S(1)}, u32[]{:S(2)}, u32[]{:S(2)}) %all-to-all-start) | async-done | bytes 65568 | tf_op jit(solution)/shard_map/all_to_all | solution.py:621
  44.4 0.7 %bias_sums.1 = f32[3,640]{1,0:T(4,128)} custom-call(f32[32,4,128]{2,1,0:T(4,128)S(1)} %all-to-all-done.tiles), custom_call_target="tpu_custom_call" | custom-call | tf_op jit(solution)/shard_map/bias_sums/pallas_call | solution.py:639
Async XLA Ops:
  2.1 4.7 %copy-start = (bf16[3,640]{1,0:T(4,128)(2,1)S(1)}, bf16[3,640]{1,0:T(4,128)(2,1)}, u32[]{:S(2)}) copy-start(bf16[3,640]{1,0:T(4,128)(2,1)} %refs_0_.1) | copy-start | bytes 11524
  2.1 9.0 %collective-permute-start = (bf16[320,256]{1,0:T(8,128)(2,1)S(1)}, bf16[320,256]{1,0:T(8,128)(2,1)S(1)}, u32[]{:S(2)}, u32[]{:S(2)}) collective-permute-start(bf16[320,256]{1,0:T(8,128)(2,1)S(1)} %get-tuple-element.62), channel_id=1, source_target_pairs={{0,3},{1,2},{2,1},{3,0},{4,7},{5,6},{6,5},{7,4},{8,11},{9,10},{10,... | collective-permute-start | bytes 491528 | tf_op jit(solution)/shard_map/ppermute | solution.py:518
  6.1 8.8 %collective-permute-start.3 = (bf16[320,256]{1,0:T(8,128)(2,1)S(1)}, bf16[320,256]{1,0:T(8,128)(2,1)S(1)}, u32[]{:S(2)}, u32[]{:S(2)}) collective-permute-start(bf16[320,256]{1,0:T(8,128)(2,1)S(1)} %get-tuple-element.71), channel_id=1, source_target_pairs={{0,1},{1,0},{2,3},{3,2},{4,5},{5,4},{6,7},{7,6},{8,9},{9,8},{10,11... | collective-permute-start | bytes 491528 | tf_op jit(solution)/shard_map/ppermute | solution.py:518
  6.7 0.7 %copy-start.1 = (s32[1,4]{1,0:T(1,128)S(1)}, s32[1,4]{1,0:T(1,128)}, u32[]{:S(2)}) copy-start(s32[1,4]{1,0:T(1,128)} %lengths.1) | copy-start | bytes 52
  6.7 0.7 %copy-start.2 = (s32[1,4]{1,0:T(1,128)S(1)}, s32[1,4]{1,0:T(1,128)}, u32[]{:S(2)}) copy-start(s32[1,4]{1,0:T(1,128)} %widths.1) | copy-start | bytes 52
  6.7 10.0 %collective-permute-start.5 = (bf16[320,256]{1,0:T(8,128)(2,1)S(1)}, bf16[320,256]{1,0:T(8,128)(2,1)S(1)}, u32[]{:S(2)}, u32[]{:S(2)}) collective-permute-start(bf16[320,256]{1,0:T(8,128)(2,1)S(1)} %get-tuple-element.77), channel_id=1, source_target_pairs={{0,2},{1,3},{2,0},{3,1},{4,6},{5,7},{6,4},{7,5},{8,10},{9,11},{10,... | collective-permute-start | bytes 491528 | tf_op jit(solution)/shard_map/ppermute | solution.py:518
  11.3 11.1 %collective-permute-start.1 = (bf16[320,256]{1,0:T(8,128)(2,1)S(1)}, bf16[320,256]{1,0:T(8,128)(2,1)S(1)}, u32[]{:S(2)}, u32[]{:S(2)}) collective-permute-start(bf16[320,256]{1,0:T(8,128)(2,1)S(1)} %get-tuple-element.65), channel_id=1, source_target_pairs={{0,3},{1,2},{2,1},{3,0},{4,7},{5,6},{6,5},{7,4},{8,11},{9,10},{10,... | collective-permute-start | bytes 491528 | tf_op jit(solution)/shard_map/ppermute | solution.py:579
  14.4 2.3 %copy-start.4 = (bf16[3,128,256]{2,1,0:T(8,128)(2,1)S(1)}, bf16[3,128,256]{2,1,0:T(8,128)(2,1)}, u32[]{:S(2)}) copy-start(bf16[3,128,256]{2,1,0:T(8,128)(2,1)} %get-tuple-element.78.refs_4_) | copy-start | bytes 589828
  14.4 8.1 %collective-permute-start.2 = (bf16[320,256]{1,0:T(8,128)(2,1)S(1)}, bf16[320,256]{1,0:T(8,128)(2,1)S(1)}, u32[]{:S(2)}, u32[]{:S(2)}) collective-permute-start(bf16[320,256]{1,0:T(8,128)(2,1)S(1)} %get-tuple-element.69), channel_id=1, source_target_pairs={{0,1},{1,0},{2,3},{3,2},{4,5},{5,4},{6,7},{7,6},{8,9},{9,8},{10,11... | collective-permute-start | bytes 491528 | tf_op jit(solution)/shard_map/ppermute | solution.py:579
  15.1 7.3 %collective-permute-start.4 = (bf16[320,256]{1,0:T(8,128)(2,1)S(1)}, bf16[320,256]{1,0:T(8,128)(2,1)S(1)}, u32[]{:S(2)}, u32[]{:S(2)}) collective-permute-start(bf16[320,256]{1,0:T(8,128)(2,1)S(1)} %get-tuple-element.74), channel_id=1, source_target_pairs={{0,2},{1,3},{2,0},{3,1},{4,6},{5,7},{6,4},{7,5},{8,10},{9,11},{10,... | collective-permute-start | bytes 491528 | tf_op jit(solution)/shard_map/ppermute | solution.py:579
  16.6 5.8 %copy-start.3 = (bf16[3,128,256]{2,1,0:T(8,128)(2,1)S(1)}, bf16[3,128,256]{2,1,0:T(8,128)(2,1)}, u32[]{:S(2)}) copy-start(bf16[3,128,256]{2,1,0:T(8,128)(2,1)} %get-tuple-element.75.refs_4_) | copy-start | bytes 589828
  20.9 8.4 %collective-permute-start.6 = (bf16[320,256]{1,0:T(8,128)(2,1)S(1)}, bf16[320,256]{1,0:T(8,128)(2,1)S(1)}, u32[]{:S(2)}, u32[]{:S(2)}) collective-permute-start(bf16[320,256]{1,0:T(8,128)(2,1)S(1)} %get-tuple-element.89), channel_id=1, source_target_pairs={{3,0},{2,1},{1,2},{0,3},{7,4},{6,5},{5,6},{4,7},{11,8},{10,9},{9,1... | collective-permute-start | bytes 491528 | tf_op jit(solution)/shard_map/ppermute | solution.py:72
  27.2 14.0 %collective-permute-start.8 = (bf16[640,256]{1,0:T(8,128)(2,1)S(1)}, bf16[640,256]{1,0:T(8,128)(2,1)S(1)}, u32[]{:S(2)}, u32[]{:S(2)}) collective-permute-start(bf16[640,256]{1,0:T(8,128)(2,1)S(1)} %get-tuple-element.93), channel_id=1, source_target_pairs={{1,0},{0,1},{3,2},{2,3},{5,4},{4,5},{7,6},{6,7},{9,8},{8,9},{11,10... | collective-permute-start | bytes 983048 | tf_op jit(solution)/shard_map/ppermute | solution.py:72
  27.8 13.4 %collective-permute-start.9 = (bf16[640,256]{1,0:T(8,128)(2,1)S(1)}, bf16[640,256]{1,0:T(8,128)(2,1)S(1)}, u32[]{:S(2)}, u32[]{:S(2)}) collective-permute-start(bf16[640,256]{1,0:T(8,128)(2,1)S(1)} %get-tuple-element.94), channel_id=1, source_target_pairs={{2,0},{3,1},{0,2},{1,3},{6,4},{7,5},{4,6},{5,7},{10,8},{11,9},{8,1... | collective-permute-start | bytes 983048 | tf_op jit(solution)/shard_map/ppermute | solution.py:72
  29.3 11.9 %collective-permute-start.7 = (bf16[320,256]{1,0:T(8,128)(2,1)S(1)}, bf16[320,256]{1,0:T(8,128)(2,1)S(1)}, u32[]{:S(2)}, u32[]{:S(2)}) collective-permute-start(bf16[320,256]{1,0:T(8,128)(2,1)S(1)} %get-tuple-element.91), channel_id=1, source_target_pairs={{3,0},{2,1},{1,2},{0,3},{7,4},{6,5},{5,6},{4,7},{11,8},{10,9},{9,1... | collective-permute-start | bytes 491528 | tf_op jit(solution)/shard_map/ppermute | solution.py:72
  30.8 13.6 %all-to-all-start = ((f32[32,4,128]{2,1,0:T(4,128)}), f32[32,4,128]{2,1,0:T(4,128)S(1)}, u32[]{:S(2)}, u32[]{:S(2)}) async-start(f32[32,4,128]{2,1,0:T(4,128)} %get-tuple-element.99), calls=%async_computation | async-start | bytes 131072 | tf_op jit(solution)/shard_map/all_to_all | solution.py:621
